TPU v7x, 32 devices: a whole 2x2x4 slice. The times are simulated.
32 devices in a mesh: groups: 2 (over y), dp: 4 (over z), tile: 4 (over x, core).
Axes of the slice: x: 2, y: 2, z: 4, core: 2. Of those that a mesh axis runs over, the one named last changes fastest.
Arguments:
- left_outputs: bfloat16 [4096, 2048], P(('groups', 'dp'), 'tile'), parts along dimension 0, may hold values from -48 to 48, as said below
- right_outputs: bfloat16 [4096, 2048], P(('groups', 'dp'), 'tile'), parts along dimension 0, may hold values from -48 to 48, as said below
Outputs:
- left_gradient: bfloat16 [4096, 2048], P(('groups', 'dp'), 'tile'), parts along dimension 0
- right_gradient: bfloat16 [4096, 2048], P(('groups', 'dp'), 'tile'), parts along dimension 0
- corr_tiles: float32 [8, 1024, 1024], P(('groups', 'tile'), 'dp'), parts along dimension 0
- loss: float32 [2], P('groups'), parts along dimension 0
There are 2 independent parts, one for each index of `groups`. A program takes and returns all parts, laid end to end along the dimension named above; each array names one. Nothing has to cross between parts.
Inputs may be any that keep to these rules, and one draw needn't show every extreme that they name: `left_outputs`: projector outputs; each feature has its own offset and scale, and the two views share a part. `right_outputs`: projector outputs; each feature has its own offset and scale, and the two views share a part.
All inputs are finite; a program needn't handle non-finite values.
Results may differ from a plain program's by a relative error of at most 0.0061.
Values may be sent and summed in bfloat16 or wider, within the bound.
No kernel may reach another device: no remote copies, remote signals or barrier semaphores. Data moves between devices by JAX's collectives and lax.ppermute only.
A program may use at most 64 MiB of HBM per device.

v0:
```python
import jax
import jax.numpy as jnp
from jax import lax
from jax.sharding import PartitionSpec as P

off_weight = 0.0051


def swapped(block, axis, bit):
    count = lax.axis_size(axis)
    route = []
    for low in range(count):
        high = low | 1 << bit
        if high != low and high < count:
            route += [(low, high), (high, low)]
    return lax.ppermute(block, axis, route)


def pair_views(first_moment, second_moment, row_halves, column_halves):
    other_a = swapped(first_moment, "tile", 0)
    other_b = swapped(second_moment, "tile", 1)
    joined_a = jnp.where(
        column_halves == 0,
        jnp.concatenate([first_moment, other_a], axis=1),
        jnp.concatenate([other_a, first_moment], axis=1),
    )
    joined_b = jnp.where(
        row_halves == 0,
        jnp.concatenate([second_moment, other_b], axis=1),
        jnp.concatenate([other_b, second_moment], axis=1),
    )
    return (joined_a, joined_b)


def moment_pair(total, squares, batch_images):
    column_mean = total / batch_images
    var = squares / batch_images - column_mean * column_mean
    return (column_mean, lax.rsqrt(var + 1e-05))


def col_sums(values):
    as_float = values.astype(jnp.float32)
    return (jnp.sum(as_float, axis=0), jnp.sum(as_float * as_float, axis=0))


def per_device(left_outputs, right_outputs):
    rows, quart = left_outputs.shape
    half = 2 * quart
    feats = 4 * quart
    dp_count = lax.axis_size("dp")
    batch_images = rows * dp_count
    tpos = lax.axis_index("tile")
    row_halves = tpos // 2
    column_halves = tpos % 2
    sum_a, sq_a = col_sums(left_outputs)
    sum_b, sq_b = col_sums(right_outputs)
    sum_a, sq_a, sum_b, sq_b = lax.psum((sum_a, sq_a, sum_b, sq_b), "dp")
    left_mean, left_inverse_deviation = moment_pair(sum_a, sq_a, batch_images)
    right_mean, right_inverse_deviation = moment_pair(sum_b, sq_b, batch_images)
    standardized_left = (left_outputs.astype(jnp.float32) - left_mean) * left_inverse_deviation
    standardized_right = (right_outputs.astype(jnp.float32) - right_mean) * right_inverse_deviation
    half_a, cols_b = pair_views(
        standardized_left.astype(jnp.bfloat16),
        standardized_right.astype(jnp.bfloat16),
        row_halves,
        column_halves,
    )
    col_local = jnp.arange(half, dtype=jnp.int32)
    col_ids = quart * column_halves + col_local + jnp.where(col_local >= quart, quart, 0)
    owned = half // dp_count
    picked = half_a
    corr_rows = (
        lax.psum_scatter(
            lax.dot_general(
                picked, cols_b, (((0,), (0,)), ((), ())), preferred_element_type=jnp.float32
            ),
            "dp",
            scatter_dimension=0,
            tiled=True,
        )
        / batch_images
    )
    row_ids = half * row_halves + lax.axis_index("dp") * owned + jnp.arange(owned, dtype=jnp.int32)
    diagonal = row_ids[:, None] == col_ids[None, :]
    part_loss = jnp.sum(
        jnp.where(diagonal, (1.0 - corr_rows) ** 2, off_weight * corr_rows * corr_rows)
    )
    loss = lax.psum(part_loss, ("dp", "tile")) / feats
    dcorr_part = jnp.where(diagonal, corr_rows - 1.0, off_weight * corr_rows).astype(jnp.bfloat16)
    piece = lax.all_gather(dcorr_part, "dp", axis=0, tiled=True)
    block_a = lax.dot_general(
        cols_b, piece, (((1,), (1,)), ((), ())), preferred_element_type=jnp.float32
    )
    picked = half_a
    into_b = jnp.dot(picked, piece, preferred_element_type=jnp.float32)
    other_a = swapped(block_a.astype(jnp.bfloat16), "tile", 0).astype(block_a.dtype)
    other_b = swapped(into_b.astype(jnp.bfloat16), "tile", 1).astype(into_b.dtype)
    normed_grad_left = lax.dynamic_slice_in_dim(block_a + other_a, column_halves * quart, quart, 1)
    normed_grad_right = lax.dynamic_slice_in_dim(into_b + other_b, row_halves * quart, quart, 1)
    first_moment_left, second_moment_left, first_moment_right, second_moment_right = lax.psum(
        (
            jnp.sum(normed_grad_left, axis=0),
            jnp.sum(normed_grad_left * standardized_left, axis=0),
            jnp.sum(normed_grad_right, axis=0),
            jnp.sum(normed_grad_right * standardized_right, axis=0),
        ),
        "dp",
    )
    left_gradient = (
        left_inverse_deviation
        * (
            normed_grad_left
            - first_moment_left / batch_images
            - standardized_left * (second_moment_left / batch_images)
        )
    ).astype(jnp.bfloat16)
    right_gradient = (
        right_inverse_deviation
        * (
            normed_grad_right
            - first_moment_right / batch_images
            - standardized_right * (second_moment_right / batch_images)
        )
    ).astype(jnp.bfloat16)
    return (left_gradient, right_gradient, corr_rows[None, :, :], jnp.reshape(loss, (1,)))


def solution(mesh):
    return jax.shard_map(
        per_device,
        mesh=mesh,
        in_specs=(P(("groups", "dp"), "tile"), P(("groups", "dp"), "tile")),
        out_specs=(
            P(("groups", "dp"), "tile"),
            P(("groups", "dp"), "tile"),
            P(("groups", "tile"), "dp", None),
            P("groups"),
        ),
        check_vma=False,
    )
```

profile of v0, /device:TPU:0, one launch (start us, length us, event | category | flops | bytes accessed | tf_op | source)
XLA Modules:
  0.0 243.7 jit_solution(14832561769078030465)
XLA Ops:
  7.2 0.0 copy-start.1
  7.2 0.0 reduce-scatter.2.cloned.1.call-start
  7.2 1.5 convert_reduce_fusion
  8.8 13.7 %all-reduce.1 = (f32[512]{0:T(512)S(1)}, f32[512]{0:T(512)S(1)}, f32[512]{0:T(512)S(1)}, f32[512]{0:T(512)S(1)}) all-reduce(f32[512]{0:T(512)S(1)} %get-tuple-element.31, f32[512]{0:T(512)S(1)} %get-tuple-element.32, f32[512]{0:T(512)S(1)} %get-tuple-element.9, ...), channel_id=1, replica_groups=mesh['groups'=2,'dp'=4,'tile'=4] {'dp'}, use_global_device_ids=true, to_apply=%region_3.4 | all-reduce | flops 2048 | bytes 16384 | tf_op jit(solution)/shard_map/psum | solution.py:57
  22.5 1.2 fusion.6
  23.6 0.1 collective-permute-start.1
  23.7 0.0 copy-done.1
  23.7 0.1 fusion.14
  23.9 0.0 copy-start.2
  23.9 1.6 collective-permute-start
  25.4 0.2 collective-permute-done.1
  25.6 12.6 %collective-permute-done = bf16[512,512]{1,0:T(8,128)(2,1)S(1)} collective-permute-done((bf16[512,512]{1,0:T(8,128)(2,1)S(1)}, bf16[512,512]{1,0:T(8,128)(2,1)S(1)}, u32[]{:S(2)}, u32[]{:S(2)}) %collective-permute-start) | collective-permute-done | bytes 524320 | tf_op jit(solution)/shard_map/ppermute | solution.py:16
  38.3 3.2 %fusion.21 = f32[1024,1024]{1,0:T(8,128)} fusion(bf16[512,512]{1,0:T(8,128)(2,1)S(1)} %collective-permute-done.1, bf16[512,512]{1,0:T(8,128)(2,1)S(1)} %fusion.6, pred[]{:T(512)S(6)} %eq.25, bf16[512,512]{1,0:T(8,128)(2,1)S(1)} %collective-permute-done, bf16[512,512]{1,0:T(8,128)(2,1)S(1)} %fusion.14, pred[]{:T(512)S(6)} %eq.21), kind=kOutput, calls=%fused_computation.34 | convolution fusion | flops 1083179008 | bytes 6291458 | tf_op jit(solution)/shard_map/dot_general | solution.py:74
  41.5 0.0 copy-done.6
  41.5 0.0 reduce-scatter.2.cloned.1.call-update
  41.6 0.0 all-gather.2.cloned.1.call-start
  41.6 75.0 %reduce-scatter.2.cloned.1.call-done = f32[256,1024]{1,0:T(8,128)} async-done(((f32[1024,1024]{1,0:T(8,128)}), f32[256,1024]{1,0:T(8,128)}) %reduce-scatter.2.cloned.1.call-update) | async-done | bytes 1048592 | tf_op jit(solution)/shard_map/reduce_scatter | solution.py:73
  116.7 3.4 %fusion.1 = (f32[]{:T(128)}, bf16[256,1024]{1,0:T(8,128)(2,1)}, f32[1,256,1024]{2,1,0:T(8,128)}) fusion(f32[256,1024]{1,0:T(8,128)} %reduce-scatter.2.cloned.1.call-done, s32[1024]{0:T(1024)S(1)} %select_add_fusion, s32[256]{0:T(256)S(1)} %iota_add_fusion), kind=kLoop, calls=%fused_computation.9 | loop fusion | flops 2883583 | bytes 2626564 | tf_op jit(solution)/shard_map/reduce_sum | solution.py:85
  120.1 0.0 all-gather.2.cloned.1.call-update
  120.1 46.6 %all-gather.2.cloned.1.call-done = bf16[1024,1024]{1,0:T(8,128)(2,1)} async-done(((bf16[256,1024]{1,0:T(8,128)(2,1)}), bf16[1024,1024]{1,0:T(8,128)(2,1)}) %all-gather.2.cloned.1.call-update) | async-done | bytes 2097168 | tf_op jit(solution)/shard_map/all_gather | solution.py:90
  166.7 4.3 %fusion.29 = (bf16[512,1024]{1,0:T(8,128)(2,1)}, f32[512,1024]{1,0:T(8,128)S(1)}) fusion(bf16[1024,1024]{1,0:T(8,128)(2,1)} %all-gather.2.cloned.1.call-done, bf16[512,512]{1,0:T(8,128)(2,1)} %copy-done.5, bf16[512,512]{1,0:T(8,128)(2,1)S(1)} %fusion.6, pred[]{:T(512)S(6)} %eq.25), kind=kOutput, calls=%fused_computation.53 | convolution fusion | flops 1078984704 | bytes 6291457 | tf_op jit(solution)/shard_map/dot_general | solution.py:95
  171.0 1.5 collective-permute-start.3
  172.5 3.0 %fusion.28 = (bf16[512,1024]{1,0:T(8,128)(2,1)}, f32[512,1024]{1,0:T(8,128)}) fusion(bf16[1024,1024]{1,0:T(8,128)(2,1)S(1)} %copy-done.4, bf16[512,512]{1,0:T(8,128)(2,1)S(1)} %copy-done.7, bf16[512,512]{1,0:T(8,128)(2,1)S(1)} %copy-done.3, pred[]{:T(512)S(6)} %eq.21), kind=kOutput, calls=%fused_computation.52 | convolution fusion | flops 1078984704 | bytes 6291457 | tf_op jit(solution)/shard_map/dot_general | solution.py:91
  175.5 0.0 collective-permute-start.2
  175.5 43.2 %psum.71 = f32[]{:T(128)} all-reduce(f32[]{:T(128)} %get-tuple-element.20), channel_id=1, replica_groups=mesh['groups'=2,'dp'=4,'tile'=4] {'dp','tile'}, use_global_device_ids=true, to_apply=%region_18.19 | all-reduce | flops 1 | bytes 8 | tf_op jit(solution)/shard_map/psum | solution.py:88
  219.4 0.0 collective-permute-done.3
  219.4 1.3 fusion.24
  220.8 0.0 collective-permute-done.2
  220.8 1.7 fusion.23
  222.5 8.5 %all-reduce = (f32[512]{0:T(512)S(1)}, f32[512]{0:T(512)S(1)}, f32[512]{0:T(512)S(1)}, f32[512]{0:T(512)S(1)}) all-reduce(f32[512]{0:T(512)S(1)} %get-tuple-element.7, f32[512]{0:T(512)S(1)} %get-tuple-element.6, f32[512]{0:T(512)S(1)} %get-tuple-element.5, ...), channel_id=1, replica_groups=mesh['groups'=2,'dp'=4,'tile'=4] {'dp'}, use_global_device_ids=true, to_apply=%region_12.13 | all-reduce | flops 2048 | bytes 16384 | tf_op jit(solution)/shard_map/psum | solution.py:100
  231.0 2.5 %fusion.10 = bf16[512,512]{1,0:T(8,128)(2,1)} fusion(bf16[512,512]{1,0:T(8,128)(2,1)S(1)} %copy-done, f32[512]{0:T(512)S(1)} %broadcast_multiply_fusion.2, f32[512]{0:T(512)S(1)} %broadcast_multiply_fusion.3, f32[512]{0:T(512)S(1)} %get-tuple-element.26, f32[512]{0:T(512)S(1)} %get-tuple-element.25, bf16[512,1024]{1,0:T(8,128)(2,1)} %collective-permute-done.2, ...), kind=kLoop, calls=%fused_computation.18 | loop fusion | flops 2621440 | bytes 2629636 | tf_op jit(solution)/shard_map/convert_element_type | solution.py:116
  233.6 2.2 fusion.18
  (20 shorter events, 0.1 us)
Async XLA Ops:
  7.2 16.6 %copy-start.1 = (bf16[512,512]{1,0:T(8,128)(2,1)S(1)}, bf16[512,512]{1,0:T(8,128)(2,1)}, u32[]{:S(2)}) copy-start(bf16[512,512]{1,0:T(8,128)(2,1)} %param.3) | copy-start | bytes 1572868
  7.2 109.5 %reduce-scatter.2.cloned.1.call-start = ((), (), s32[]{:S(2)}) async-start(), calls=%async_computation.1 | async-start | bytes 5242880 | tf_op jit(solution)/shard_map/reduce_scatter | solution.py:73
  23.6 2.0 collective-permute-start.1
  23.9 17.6 %copy-start.2 = (bf16[512,512]{1,0:T(8,128)(2,1)}, bf16[512,512]{1,0:T(8,128)(2,1)S(1)}, u32[]{:S(2)}) copy-start(bf16[512,512]{1,0:T(8,128)(2,1)S(1)} %fusion.14) | copy-start | bytes 1572868
  23.9 14.4 %collective-permute-start = (bf16[512,512]{1,0:T(8,128)(2,1)S(1)}, bf16[512,512]{1,0:T(8,128)(2,1)S(1)}, u32[]{:S(2)}, u32[]{:S(2)}) collective-permute-start(bf16[512,512]{1,0:T(8,128)(2,1)S(1)} %fusion.14), channel_id=1, source_target_pairs={{0,2},{2,0},{1,3},{3,1},{4,6},{6,4},{5,7},{7,5},{8,10},{10,8},{9,1... | collective-permute-start | bytes 1572872 | tf_op jit(solution)/shard_map/ppermute | solution.py:16
  25.6 15.9 %copy-start.5 = (bf16[512,512]{1,0:T(8,128)(2,1)}, bf16[512,512]{1,0:T(8,128)(2,1)S(1)}, u32[]{:S(2)}) copy-start(bf16[512,512]{1,0:T(8,128)(2,1)S(1)} %collective-permute-done.1) | copy-start | bytes 1572868
  38.3 3.3 %copy-start.6 = (bf16[512,512]{1,0:T(8,128)(2,1)}, bf16[512,512]{1,0:T(8,128)(2,1)S(1)}, u32[]{:S(2)}) copy-start(bf16[512,512]{1,0:T(8,128)(2,1)S(1)} %collective-permute-done) | copy-start | bytes 1572868
  41.6 125.2 %all-gather.2.cloned.1.call-start = ((), (), s32[]{:S(2)}) async-start(), calls=%async_computation.2 | async-start | bytes 2621440 | tf_op jit(solution)/shard_map/all_gather | solution.py:90
  166.7 5.8 %copy-start.3 = (bf16[512,512]{1,0:T(8,128)(2,1)S(1)}, bf16[512,512]{1,0:T(8,128)(2,1)}, u32[]{:S(2)}) copy-start(bf16[512,512]{1,0:T(8,128)(2,1)} %copy-done.2) | copy-start | bytes 1572868
  166.7 5.8 %copy-start.4 = (bf16[1024,1024]{1,0:T(8,128)(2,1)S(1)}, bf16[1024,1024]{1,0:T(8,128)(2,1)}, u32[]{:S(2)}) copy-start(bf16[1024,1024]{1,0:T(8,128)(2,1)} %all-gather.2.cloned.1.call-done) | copy-start | bytes 6291460
  166.7 5.8 %copy-start.7 = (bf16[512,512]{1,0:T(8,128)(2,1)S(1)}, bf16[512,512]{1,0:T(8,128)(2,1)}, u32[]{:S(2)}) copy-start(bf16[512,512]{1,0:T(8,128)(2,1)} %copy-done.6) | copy-start | bytes 1572868
  171.0 48.4 %collective-permute-start.3 = (bf16[512,1024]{1,0:T(8,128)(2,1)}, bf16[512,1024]{1,0:T(8,128)(2,1)}, u32[]{:S(2)}, u32[]{:S(2)}) collective-permute-start(bf16[512,1024]{1,0:T(8,128)(2,1)} %get-tuple-element.29), channel_id=1, source_target_pairs={{0,2},{2,0},{1,3},{3,1},{4,6},{6,4},{5,7},{7,5},{8,10},{10,8},{9,1... | collective-permute-start | bytes 3145736 | tf_op jit(solution)/shard_map/ppermute | solution.py:16
  175.5 45.3 %copy-start = (bf16[512,512]{1,0:T(8,128)(2,1)S(1)}, bf16[512,512]{1,0:T(8,128)(2,1)}, u32[]{:S(2)}) copy-start(bf16[512,512]{1,0:T(8,128)(2,1)} %param.2) | copy-start | bytes 1572868
  175.5 45.3 %collective-permute-start.2 = (bf16[512,1024]{1,0:T(8,128)(2,1)}, bf16[512,1024]{1,0:T(8,128)(2,1)}, u32[]{:S(2)}, u32[]{:S(2)}) collective-permute-start(bf16[512,1024]{1,0:T(8,128)(2,1)} %get-tuple-element.27), channel_id=1, source_target_pairs={{0,1},{1,0},{2,3},{3,2},{4,5},{5,4},{6,7},{7,6},{8,9},{9,8},{10,11... | collective-permute-start | bytes 3145736 | tf_op jit(solution)/shard_map/ppermute | solution.py:16
Sparse Core Ops, SparseCore 0:
  41.7 74.9 reduce-scatter.1
  120.2 46.4 all-gather.1
where the time goes:
time: 244 us
  waiting for transfers between devices  135 us (55%)
  blocking collectives  65.4 us (27%)
  between operations  16 us (7%)
  other arithmetic  14 us (6%)
  matrix products  10.5 us (4%)
  starting transfers between devices  3.18 us (1%)
    reduce_scatter x1, waiting for transfers between devices, per_device(): lax.psum_scatter(lax.dot_general(picked, cols_b, (((0,), (0,)), ((), ()))...  75 us
    all_gather x1, waiting for transfers between devices, per_device(): piece = lax.all_gather(dcorr_part, 'dp', axis=0, tiled=True)  46.6 us
    psum x1, blocking collectives, per_device(): loss = lax.psum(part_loss, ('dp', 'tile')) / feats  43.2 us
    psum x1, blocking collectives, per_device(): sum_a, sq_a, sum_b, sq_b = lax.psum((sum_a, sq_a, sum_b, sq_b), 'dp')  13.7 us
    ppermute x4, waiting for transfers between devices, swapped(): return lax.ppermute(block, axis, route)  12.8 us
    psum x1, blocking collectives, per_device(): lax.psum((jnp.sum(normed_grad_left, axis=0), jnp.sum(normed_grad_left * s...  8.49 us
  transfers between devices with their start and end apart: 6, of which 4 were waited for; matrix products, arithmetic and copies ran while one was open for 2% of the time, Pallas kernels for 0%

commit v1 on v0

--- a/solution.py
+++ b/solution.py
@@ -43,7 +43,7 @@
     return (jnp.sum(as_float, axis=0), jnp.sum(as_float * as_float, axis=0))
 
 
-def per_device(left_outputs, right_outputs):
+def reduced_device(left_outputs, right_outputs):
     rows, quart = left_outputs.shape
     half = 2 * quart
     feats = 4 * quart
@@ -125,7 +125,108 @@
     return (left_gradient, right_gradient, corr_rows[None, :, :], jnp.reshape(loss, (1,)))
 
 
+def gathered_device(left_outputs, right_outputs):
+    rows, quart = left_outputs.shape
+    half = 2 * quart
+    feats = 4 * quart
+    batch_images = rows * 4
+    tpos = lax.axis_index("tile")
+    dpos = lax.axis_index("dp")
+    row_halves = tpos // 2
+    column_halves = tpos % 2
+    at_end = (dpos == 0) | (dpos == 3)
+
+    pairs = [(0, 1), (1, 0), (2, 3), (3, 2)]
+    middle = [(1, 2), (2, 1)]
+    outward = [(1, 0), (2, 3)]
+
+    def chain(block):
+        first = lax.ppermute(block, "dp", pairs)
+        second_inner = lax.ppermute(block, "dp", middle)
+        second_outer = lax.ppermute(second_inner, "dp", outward)
+        third_inner = lax.ppermute(first, "dp", middle)
+        third_outer = lax.ppermute(third_inner, "dp", outward)
+        return [
+            block,
+            first,
+            jnp.where(at_end, second_outer, second_inner),
+            jnp.where(at_end, third_outer, third_inner),
+        ]
+
+    own_b = chain(right_outputs)
+    own_a = chain(left_outputs)
+
+    sum_a, sq_a = col_sums(left_outputs)
+    sum_b, sq_b = col_sums(right_outputs)
+    sum_a, sq_a, sum_b, sq_b = lax.psum((sum_a, sq_a, sum_b, sq_b), "dp")
+    mean_a, rstd_a = moment_pair(sum_a, sq_a, batch_images)
+    mean_b, rstd_b = moment_pair(sum_b, sq_b, batch_images)
+    stats_a = jnp.stack([mean_a, rstd_a])
+    stats_b = jnp.stack([mean_b, rstd_b])
+    stats_a = jnp.concatenate([stats_a, swapped(stats_a, "tile", 0)], axis=1)
+    stats_b = jnp.concatenate([stats_b, swapped(stats_b, "tile", 1)], axis=1)
+
+    def normalized(own, bit, stats):
+        pair = jnp.concatenate([own, swapped(own, "tile", bit)], axis=1)
+        return (pair.astype(jnp.float32) - stats[0]) * stats[1]
+
+    total = None
+    colsum_a = colsum_b = 0.0
+    for step in range(4):
+        x_a = normalized(own_a[step], 0, stats_a)
+        x_b = normalized(own_b[step], 1, stats_b)
+        n_a = x_a.astype(jnp.bfloat16)
+        n_b = x_b.astype(jnp.bfloat16)
+        if step == 0:
+            xhat_a, xhat_b, norm_a, norm_b = x_a, x_b, n_a, n_b
+        part = lax.dot_general(
+            n_a, n_b, (((0,), (0,)), ((), ())), preferred_element_type=jnp.float32
+        )
+        total = part if total is None else total + part
+        colsum_a = colsum_a + jnp.sum(n_a.astype(jnp.float32), axis=0)
+        colsum_b = colsum_b + jnp.sum(n_b.astype(jnp.float32), axis=0)
+    corr = total / batch_images
+
+    local = jnp.arange(half, dtype=jnp.int32)
+    diagonal = (local[:, None] == local[None, :]) & (local < quart)[:, None]
+    part_loss = jnp.sum(jnp.where(diagonal, (1.0 - corr) ** 2, off_weight * corr * corr))
+    part_loss = part_loss + swapped(part_loss, "tile", 0)
+    part_loss = part_loss + swapped(part_loss, "tile", 1)
+    loss = part_loss / feats
+    dcorr = jnp.where(diagonal, corr - 1.0, off_weight * corr).astype(jnp.bfloat16)
+
+    wide = dcorr.astype(jnp.float32)
+    first_a = jnp.sum(wide * (colsum_b / batch_images)[None, :], axis=1)
+    first_b = jnp.sum(wide * (colsum_a / batch_images)[:, None], axis=0)
+    product = wide * corr
+    second_a = jnp.sum(product, axis=1)
+    second_b = jnp.sum(product, axis=0)
+    grad_a = lax.dot_general(
+        norm_b, dcorr, (((1,), (1,)), ((), ())), preferred_element_type=jnp.float32
+    )
+    grad_b = jnp.dot(norm_a, dcorr, preferred_element_type=jnp.float32)
+    grad_a = grad_a - first_a - xhat_a * second_a
+    grad_b = grad_b - first_b - xhat_b * second_b
+    other_b = swapped(grad_b[:, quart:].astype(jnp.bfloat16), "tile", 1)
+    other_a = swapped(grad_a[:, quart:].astype(jnp.bfloat16), "tile", 0)
+    left_gradient = (rstd_a * (grad_a[:, :quart] + other_a.astype(jnp.float32))).astype(
+        jnp.bfloat16
+    )
+    right_gradient = (rstd_b * (grad_b[:, :quart] + other_b.astype(jnp.float32))).astype(
+        jnp.bfloat16
+    )
+
+    owned = half // 4
+    row_quarter = jnp.where(dpos // 2 == column_halves, 0, quart)
+    mine = lax.dynamic_slice_in_dim(corr, row_quarter + (dpos % 2) * owned, owned, 0)
+    mine = jnp.where(
+        row_halves == 0, mine, jnp.concatenate([mine[:, quart:], mine[:, :quart]], axis=1)
+    )
+    return (left_gradient, right_gradient, mine[None, :, :], jnp.reshape(loss, (1,)))
+
+
 def solution(mesh):
+    per_device = gathered_device if mesh.shape["dp"] == 4 else reduced_device
     return jax.shard_map(
         per_device,
         mesh=mesh,

time: 244 us -> 141 us (0.58)
  waiting for transfers between devices: 135 us -> 59.2 us
  blocking collectives: 65.4 us -> 14.5 us
  starting transfers between devices: 3.18 us -> 37.8 us
  between operations: 16 us -> 3.94 us
  other arithmetic: 14 us -> 9.48 us
  local copies, waits for them, and re-layouts: 0.03 us -> 3.48 us
    reduce_scatter x1 -> x0, waiting for transfers between devices: 75 us -> none  [per_device(): lax.psum_scatter(lax.dot_general(picked, cols_b, (((0,), (0,)), ((), ()))...]
    psum x3 -> x1, blocking collectives: 65.4 us -> 14.5 us  [gathered_device(): sum_a, sq_a, sum_b, sq_b = lax.psum((sum_a, sq_a, sum_b, sq_b), 'dp')]
    all_gather x1 -> x0, waiting for transfers between devices: 46.6 us -> none  [per_device(): piece = lax.all_gather(dcorr_part, 'dp', axis=0, tiled=True)]
    ppermute x0 -> x10, waiting for transfers between devices: none -> 45.5 us  [the longest x2 21.5 us: chain(): third_outer = lax.ppermute(third_inner, 'dp', outward)]
    ppermute x0 -> x10, starting transfers between devices: none -> 21.7 us  [the longest x2 13.6 us: chain(): first = lax.ppermute(block, 'dp', pairs)]
    ppermute x4 -> x14, starting transfers between devices: 3.1 us -> 16.1 us  [swapped(): return lax.ppermute(block, axis, route)]
    reduce_sum x3 -> x2, other arithmetic: 6.45 us -> 2.33 us  [the longest x1 1.17 us: gathered_device(): colsum_a = colsum_a + jnp.sum(n_a.astype(jnp.float32), axis=0)]
    dot_general x3 -> x6, matrix products: 10.5 us -> 12.6 us  [the longest x4 9.77 us: gathered_device(): lax.dot_general(n_a, n_b, (((0,), (0,)), ((), ())), preferred_element_typ...]
  transfers between devices with their start and end apart: 6 -> 24, of which waited for: 4 -> 9; matrix products, arithmetic and copies ran while one was open for 2% -> 13% of each run, Pallas kernels for 0% -> 0%
where the time goes in v1:
time: 141 us
  waiting for transfers between devices  59.2 us (42%)
  starting transfers between devices  37.8 us (27%)
  blocking collectives  14.5 us (10%)
  matrix products  12.6 us (9%)
  other arithmetic  9.48 us (7%)
  between operations  3.94 us (3%)
  local copies, waits for them, and re-layouts  3.48 us (2%)
    ppermute x2, waiting for transfers between devices, chain(): third_outer = lax.ppermute(third_inner, 'dp', outward)  21.5 us
    ppermute x14, starting transfers between devices, swapped(): return lax.ppermute(block, axis, route)  16.1 us
    ppermute x2, waiting for transfers between devices, chain(): second_outer = lax.ppermute(second_inner, 'dp', outward)  14.6 us
    psum x1, blocking collectives, gathered_device(): sum_a, sq_a, sum_b, sq_b = lax.psum((sum_a, sq_a, sum_b, sq_b), 'dp')  14.5 us
    ppermute x14, waiting for transfers between devices, swapped(): return lax.ppermute(block, axis, route)  13.7 us
    ppermute x2, starting transfers between devices, chain(): first = lax.ppermute(block, 'dp', pairs)  13.6 us
    dot_general x4, matrix products, gathered_device(): lax.dot_general(n_a, n_b, (((0,), (0,)), ((), ())), preferred_element_typ...  9.77 us
    ppermute x2, waiting for transfers between devices, chain(): first = lax.ppermute(block, 'dp', pairs)  9.39 us
  transfers between devices with their start and end apart: 24, of which 9 were waited for; matrix products, arithmetic and copies ran while one was open for 13% of the time, Pallas kernels for 0%

profile of v1, /device:TPU:0, one launch (start us, length us, event | category | flops | bytes accessed | tf_op | source)
XLA Modules:
  0.0 141.0 jit_solution(12507869797054721205)
XLA Ops:
  1.3 5.9 %collective-permute-start.4 = (bf16[512,512]{1,0:T(8,128)(2,1)}, bf16[512,512]{1,0:T(8,128)(2,1)S(1)}, u32[]{:S(2)}, u32[]{:S(2)}) collective-permute-start(bf16[512,512]{1,0:T(8,128)(2,1)} %param.2), channel_id=1, source_target_pairs={{0,4},{4,0},{8,12},{12,8},{1,5},{5,1},{9,13},{13,9},{2,6},{6,2},{1... | collective-permute-start | bytes 1572872 | tf_op jit(solution)/shard_map/ppermute | solution.py:144
  7.9 1.2 convert_reduce_fusion.8
  9.1 1.2 convert_reduce_fusion.9
  10.3 14.5 %all-reduce = (f32[512]{0:T(512)S(1)}, f32[512]{0:T(512)S(1)}, f32[512]{0:T(512)S(1)}, f32[512]{0:T(512)S(1)}) all-reduce(f32[512]{0:T(512)S(1)} %get-tuple-element.16, f32[512]{0:T(512)S(1)} %get-tuple-element.15, f32[512]{0:T(512)S(1)} %get-tuple-element.14, ...), channel_id=1, replica_groups=mesh['groups'=2,'dp'=4,'tile'=4] {'dp'}, use_global_device_ids=true, to_apply=%region_1.2 | all-reduce | flops 2048 | bytes 16384 | tf_op jit(solution)/shard_map/psum | solution.py:161
  26.1 1.5 %collective-permute-start.1 = (f32[2,512]{1,0:T(2,128)S(1)}, f32[2,512]{1,0:T(2,128)S(1)}, u32[]{:S(2)}, u32[]{:S(2)}) collective-permute-start(f32[2,512]{1,0:T(2,128)S(1)} %pad_maximum_fusion.4), channel_id=1, source_target_pairs={{0,2},{2,0},{1,3},{3,1},{4,6},{6,4},{5,7},{7,5},{8,10},{10,8},{9,1... | collective-permute-start | bytes 12296 | tf_op jit(solution)/shard_map/ppermute | solution.py:16
  27.6 2.1 %collective-permute-done.1 = f32[2,512]{1,0:T(2,128)S(1)} collective-permute-done((f32[2,512]{1,0:T(2,128)S(1)}, f32[2,512]{1,0:T(2,128)S(1)}, u32[]{:S(2)}, u32[]{:S(2)}) %collective-permute-start.1) | collective-permute-done | bytes 4128 | tf_op jit(solution)/shard_map/ppermute | solution.py:16
  29.7 7.7 %collective-permute-start.6 = (bf16[512,512]{1,0:T(8,128)(2,1)}, bf16[512,512]{1,0:T(8,128)(2,1)S(1)}, u32[]{:S(2)}, u32[]{:S(2)}) collective-permute-start(bf16[512,512]{1,0:T(8,128)(2,1)} %param.3), channel_id=1, source_target_pairs={{0,4},{4,0},{8,12},{12,8},{1,5},{5,1},{9,13},{13,9},{2,6},{6,2},{1... | collective-permute-start | bytes 1572872 | tf_op jit(solution)/shard_map/ppermute | solution.py:144
  37.5 1.5 %collective-permute-start = (bf16[512,512]{1,0:T(8,128)(2,1)}, bf16[512,512]{1,0:T(8,128)(2,1)S(1)}, u32[]{:S(2)}, u32[]{:S(2)}) collective-permute-start(bf16[512,512]{1,0:T(8,128)(2,1)} %param.3), channel_id=1, source_target_pairs={{0,2},{2,0},{1,3},{3,1},{4,6},{6,4},{5,7},{7,5},{8,10},{10,8},{9,1... | collective-permute-start | bytes 1572872 | tf_op jit(solution)/shard_map/ppermute | solution.py:16
  39.0 1.3 collective-permute-start.9
  41.1 9.4 %collective-permute-done.6 = bf16[512,512]{1,0:T(8,128)(2,1)S(1)} collective-permute-done((bf16[512,512]{1,0:T(8,128)(2,1)}, bf16[512,512]{1,0:T(8,128)(2,1)S(1)}, u32[]{:S(2)}, u32[]{:S(2)}) %collective-permute-start.6) | collective-permute-done | bytes 524320 | tf_op jit(solution)/shard_map/ppermute | solution.py:144
  50.5 1.3 collective-permute-start.12
  51.8 1.6 %collective-permute-start.7 = (bf16[512,512]{1,0:T(8,128)(2,1)S(1)}, bf16[512,512]{1,0:T(8,128)(2,1)S(1)}, u32[]{:S(2)}, u32[]{:S(2)}) collective-permute-start(bf16[512,512]{1,0:T(8,128)(2,1)S(1)} %collective-permute-done.6), channel_id=1, source_target_pairs={{0,2},{2,0},{1,3},{3,1},{4,6},{6,4},{5,7},{7,5},{8,10},{10,8},{9,1... | collective-permute-start | bytes 1572872 | tf_op jit(solution)/shard_map/ppermute | solution.py:16
  53.4 2.5 %fusion.20 = f32[1024,1024]{0,1:T(8,128)S(1)} fusion(f32[1024]{0:T(1024)S(1)} %bitcast.40, f32[1024]{0:T(1024)S(1)} %bitcast.33, bf16[512,512]{1,0:T(8,128)(2,1)S(1)} %collective-permute-done, bf16[512,512]{1,0:T(8,128)(2,1)} %param.3, f32[1024]{0:T(1024)S(1)} %bitcast.26, f32[1024]{0:T(1024)S(1)} %bitcast.19, ...), kind=kOutput, calls=%fused_computation.72 | convolution fusion | flops 1081081856 | bytes 6307840 | tf_op jit(solution)/shard_map/dot_general | solution.py:182
  55.9 5.8 %collective-permute-done.9 = bf16[512,512]{1,0:T(8,128)(2,1)S(1)} collective-permute-done((bf16[512,512]{1,0:T(8,128)(2,1)S(1)}, bf16[512,512]{1,0:T(8,128)(2,1)S(1)}, u32[]{:S(2)}, u32[]{:S(2)}) %collective-permute-start.9) | collective-permute-done | bytes 524320 | tf_op jit(solution)/shard_map/ppermute | solution.py:146
  62.5 8.7 %collective-permute-done.12 = bf16[512,512]{1,0:T(8,128)(2,1)S(1)} collective-permute-done((bf16[512,512]{1,0:T(8,128)(2,1)S(1)}, bf16[512,512]{1,0:T(8,128)(2,1)S(1)}, u32[]{:S(2)}, u32[]{:S(2)}) %collective-permute-start.12) | collective-permute-done | bytes 524320 | tf_op jit(solution)/shard_map/ppermute | solution.py:146
  71.2 1.3 collective-permute-start.15
  72.6 1.6 %collective-permute-start.13 = (bf16[512,512]{1,0:T(8,128)(2,1)S(1)}, bf16[512,512]{1,0:T(8,128)(2,1)S(1)}, u32[]{:S(2)}, u32[]{:S(2)}) collective-permute-start(bf16[512,512]{1,0:T(8,128)(2,1)S(1)} %broadcast_select_fusion.2), channel_id=1, source_target_pairs={{0,2},{2,0},{1,3},{3,1},{4,6},{6,4},{5,7},{7,5},{8,10},{10,8},{9,1... | collective-permute-start | bytes 1572872 | tf_op jit(solution)/shard_map/ppermute | solution.py:16
  74.2 1.5 %collective-permute-start.18 = (bf16[512,512]{1,0:T(8,128)(2,1)S(1)}, bf16[512,512]{1,0:T(8,128)(2,1)S(1)}, u32[]{:S(2)}, u32[]{:S(2)}) collective-permute-start(bf16[512,512]{1,0:T(8,128)(2,1)S(1)} %collective-permute-done.17), channel_id=1, source_target_pairs={{4,0},{8,12},{5,1},{9,13},{6,2},{10,14},{7,3},{11,15},{20,16},{24,... | collective-permute-start | bytes 1572872 | tf_op jit(solution)/shard_map/ppermute | solution.py:148
  75.7 1.4 fusion.14
  77.0 10.8 %collective-permute-done.15 = bf16[512,512]{1,0:T(8,128)(2,1)S(1)} collective-permute-done((bf16[512,512]{1,0:T(8,128)(2,1)S(1)}, bf16[512,512]{1,0:T(8,128)(2,1)S(1)}, u32[]{:S(2)}, u32[]{:S(2)}) %collective-permute-start.15) | collective-permute-done | bytes 524320 | tf_op jit(solution)/shard_map/ppermute | solution.py:148
  88.0 10.7 %collective-permute-done.18 = bf16[512,512]{1,0:T(8,128)(2,1)S(1)} collective-permute-done((bf16[512,512]{1,0:T(8,128)(2,1)S(1)}, bf16[512,512]{1,0:T(8,128)(2,1)S(1)}, u32[]{:S(2)}, u32[]{:S(2)}) %collective-permute-start.18) | collective-permute-done | bytes 524320 | tf_op jit(solution)/shard_map/ppermute | solution.py:148
  98.8 1.6 %collective-permute-start.19 = (bf16[512,512]{1,0:T(8,128)(2,1)S(1)}, bf16[512,512]{1,0:T(8,128)(2,1)S(1)}, u32[]{:S(2)}, u32[]{:S(2)}) collective-permute-start(bf16[512,512]{1,0:T(8,128)(2,1)S(1)} %broadcast_select_fusion), channel_id=1, source_target_pairs={{0,2},{2,0},{1,3},{3,1},{4,6},{6,4},{5,7},{7,5},{8,10},{10,8},{9,1... | collective-permute-start | bytes 1572872 | tf_op jit(solution)/shard_map/ppermute | solution.py:16
  100.3 1.4 fusion.15
  102.9 9.5 %collective-permute-done.19 = bf16[512,512]{1,0:T(8,128)(2,1)S(1)} collective-permute-done((bf16[512,512]{1,0:T(8,128)(2,1)S(1)}, bf16[512,512]{1,0:T(8,128)(2,1)S(1)}, u32[]{:S(2)}, u32[]{:S(2)}) %collective-permute-start.19) | collective-permute-done | bytes 524320 | tf_op jit(solution)/shard_map/ppermute | solution.py:16
  113.6 4.5 %select_reduce_fusion = (f32[]{:T(128)}, f32[1024]{0:T(1024)S(1)}, f32[1024]{0:T(1024)S(1)}, f32[1024]{0:T(1024)S(1)}, f32[1024]{0:T(1024)S(1)}, /*index=5*/f32[1024,1024]{0,1:T(8,128)S(1)}, f32[1024,1024]{0,1:T(8,128)S(1)}) fusion(pred[1024]{0:T(1024)(128)(4,1)S(1)} %iota_compare_fusion.1, f32[1024]{0:T(1024)S(1)} %add_multiply_fusion.1, ...), kind=kOutput, calls=%fused_computation.5 | convolution fusion | flops 1105195008 | bytes 23110660 | tf_op jit(solution)/shard_map/dot_general | solution.py:182
  118.1 1.4 multiply_subtract_fusion
  120.4 1.5 %collective-permute-start.21 = (bf16[512,512]{1,0:T(8,128)(2,1)}, bf16[512,512]{1,0:T(8,128)(2,1)}, u32[]{:S(2)}, u32[]{:S(2)}) collective-permute-start(bf16[512,512]{1,0:T(8,128)(2,1)} %slice.74), channel_id=1, source_target_pairs={{0,2},{2,0},{1,3},{3,1},{4,6},{6,4},{5,7},{7,5},{8,10},{10,8},{9,1... | collective-permute-start | bytes 1572872 | tf_op jit(solution)/shard_map/ppermute | solution.py:16
  121.9 1.4 multiply_subtract_fusion.1
  125.0 1.3 copy.6
  127.5 6.5 %collective-permute-start.23 = (f32[]{:T(128)}, f32[]{:T(128)}, u32[]{:S(2)}, u32[]{:S(2)}) collective-permute-start(f32[]{:T(128)} %add.110), channel_id=1, source_target_pairs={{0,2},{2,0},{1,3},{3,1},{4,6},{6,4},{5,7},{7,5},{8,10},{10,8},{9,1... | collective-permute-start | bytes 20 | tf_op jit(solution)/shard_map/ppermute | solution.py:16
  135.7 2.2 %fusion.10 = bf16[512,512]{1,0:T(8,128)(2,1)} fusion(f32[512,1024]{1,0:T(8,128)S(1)} %multiply_subtract_fusion, bf16[512,512]{1,0:T(8,128)(2,1)} %collective-permute-done.21, f32[512]{0:T(512)S(1)} %get-tuple-element.37), kind=kLoop, calls=%fused_computation.42 | loop fusion | flops 1048576 | bytes 2099200 | tf_op jit(solution)/shard_map/convert_element_type | solution.py:215
  137.8 2.0 %fusion.12 = bf16[512,512]{1,0:T(8,128)(2,1)} fusion(f32[512,1024]{1,0:T(8,128)S(1)} %copy-done.3, bf16[512,512]{1,0:T(8,128)(2,1)} %collective-permute-done.20, f32[512]{0:T(512)S(1)} %get-tuple-element.41), kind=kLoop, calls=%fused_computation.46 | loop fusion | flops 1048576 | bytes 2099200 | tf_op jit(solution)/shard_map/convert_element_type | solution.py:212
  (60 shorter events, 10.4 us)
Async XLA Ops:
  0.6 36.8 %collective-permute-start.8 = (bf16[512,512]{1,0:T(8,128)(2,1)}, bf16[512,512]{1,0:T(8,128)(2,1)S(1)}, u32[]{:S(2)}, u32[]{:S(2)}) collective-permute-start(bf16[512,512]{1,0:T(8,128)(2,1)} %param.2), channel_id=1, source_target_pairs={{4,8},{8,4},{5,9},{9,5},{6,10},{10,6},{7,11},{11,7},{20,24},{24,20... | collective-permute-start | bytes 1572872 | tf_op jit(solution)/shard_map/ppermute | solution.py:145
  1.3 39.0 %collective-permute-start.4 = (bf16[512,512]{1,0:T(8,128)(2,1)}, bf16[512,512]{1,0:T(8,128)(2,1)S(1)}, u32[]{:S(2)}, u32[]{:S(2)}) collective-permute-start(bf16[512,512]{1,0:T(8,128)(2,1)} %param.2), channel_id=1, source_target_pairs={{0,4},{4,0},{8,12},{12,8},{1,5},{5,1},{9,13},{13,9},{2,6},{6,2},{1... | collective-permute-start | bytes 1572872 | tf_op jit(solution)/shard_map/ppermute | solution.py:144
  7.2 33.8 %collective-permute-start.2 = (bf16[512,512]{1,0:T(8,128)(2,1)}, bf16[512,512]{1,0:T(8,128)(2,1)S(1)}, u32[]{:S(2)}, u32[]{:S(2)}) collective-permute-start(bf16[512,512]{1,0:T(8,128)(2,1)} %param.2), channel_id=1, source_target_pairs={{0,1},{1,0},{2,3},{3,2},{4,5},{5,4},{6,7},{7,6},{8,9},{9,8},{10,11... | collective-permute-start | bytes 1572872 | tf_op jit(solution)/shard_map/ppermute | solution.py:16
  7.2 31.8 %collective-permute-start.11 = (bf16[512,512]{1,0:T(8,128)(2,1)}, bf16[512,512]{1,0:T(8,128)(2,1)S(1)}, u32[]{:S(2)}, u32[]{:S(2)}) collective-permute-start(bf16[512,512]{1,0:T(8,128)(2,1)} %param.3), channel_id=1, source_target_pairs={{4,8},{8,4},{5,9},{9,5},{6,10},{10,6},{7,11},{11,7},{20,24},{24,20... | collective-permute-start | bytes 1572872 | tf_op jit(solution)/shard_map/ppermute | solution.py:145
  24.9 1.2 collective-permute-start.3
  26.1 3.6 %collective-permute-start.1 = (f32[2,512]{1,0:T(2,128)S(1)}, f32[2,512]{1,0:T(2,128)S(1)}, u32[]{:S(2)}, u32[]{:S(2)}) collective-permute-start(f32[2,512]{1,0:T(2,128)S(1)} %pad_maximum_fusion.4), channel_id=1, source_target_pairs={{0,2},{2,0},{1,3},{3,1},{4,6},{6,4},{5,7},{7,5},{8,10},{10,8},{9,1... | collective-permute-start | bytes 12296 | tf_op jit(solution)/shard_map/ppermute | solution.py:16
  29.7 20.8 %collective-permute-start.6 = (bf16[512,512]{1,0:T(8,128)(2,1)}, bf16[512,512]{1,0:T(8,128)(2,1)S(1)}, u32[]{:S(2)}, u32[]{:S(2)}) collective-permute-start(bf16[512,512]{1,0:T(8,128)(2,1)} %param.3), channel_id=1, source_target_pairs={{0,4},{4,0},{8,12},{12,8},{1,5},{5,1},{9,13},{13,9},{2,6},{6,2},{1... | collective-permute-start | bytes 1572872 | tf_op jit(solution)/shard_map/ppermute | solution.py:144
  37.5 14.3 %collective-permute-start = (bf16[512,512]{1,0:T(8,128)(2,1)}, bf16[512,512]{1,0:T(8,128)(2,1)S(1)}, u32[]{:S(2)}, u32[]{:S(2)}) collective-permute-start(bf16[512,512]{1,0:T(8,128)(2,1)} %param.3), channel_id=1, source_target_pairs={{0,2},{2,0},{1,3},{3,1},{4,6},{6,4},{5,7},{7,5},{8,10},{10,8},{9,1... | collective-permute-start | bytes 1572872 | tf_op jit(solution)/shard_map/ppermute | solution.py:16
  39.0 22.7 %collective-permute-start.9 = (bf16[512,512]{1,0:T(8,128)(2,1)S(1)}, bf16[512,512]{1,0:T(8,128)(2,1)S(1)}, u32[]{:S(2)}, u32[]{:S(2)}) collective-permute-start(bf16[512,512]{1,0:T(8,128)(2,1)S(1)} %collective-permute-done.8), channel_id=1, source_target_pairs={{4,0},{8,12},{5,1},{9,13},{6,2},{10,14},{7,3},{11,15},{20,16},{24,... | collective-permute-start | bytes 1572872 | tf_op jit(solution)/shard_map/ppermute | solution.py:146
  40.3 30.9 %collective-permute-start.14 = (bf16[512,512]{1,0:T(8,128)(2,1)S(1)}, bf16[512,512]{1,0:T(8,128)(2,1)S(1)}, u32[]{:S(2)}, u32[]{:S(2)}) collective-permute-start(bf16[512,512]{1,0:T(8,128)(2,1)S(1)} %collective-permute-done.4), channel_id=1, source_target_pairs={{4,8},{8,4},{5,9},{9,5},{6,10},{10,6},{7,11},{11,7},{20,24},{24,20... | collective-permute-start | bytes 1572872 | tf_op jit(solution)/shard_map/ppermute | solution.py:147
  41.0 60.7 %copy-start.4 = (bf16[512,512]{1,0:T(8,128)(2,1)}, bf16[512,512]{1,0:T(8,128)(2,1)S(1)}, u32[]{:S(2)}) copy-start(bf16[512,512]{1,0:T(8,128)(2,1)S(1)} %collective-permute-done.2) | copy-start | bytes 1572868
  41.0 31.6 %collective-permute-start.5 = (bf16[512,512]{1,0:T(8,128)(2,1)S(1)}, bf16[512,512]{1,0:T(8,128)(2,1)S(1)}, u32[]{:S(2)}, u32[]{:S(2)}) collective-permute-start(bf16[512,512]{1,0:T(8,128)(2,1)S(1)} %collective-permute-done.4), channel_id=1, source_target_pairs={{0,1},{1,0},{2,3},{3,2},{4,5},{5,4},{6,7},{7,6},{8,9},{9,8},{10,11... | collective-permute-start | bytes 1572872 | tf_op jit(solution)/shard_map/ppermute | solution.py:16
  50.5 20.7 %collective-permute-start.12 = (bf16[512,512]{1,0:T(8,128)(2,1)S(1)}, bf16[512,512]{1,0:T(8,128)(2,1)S(1)}, u32[]{:S(2)}, u32[]{:S(2)}) collective-permute-start(bf16[512,512]{1,0:T(8,128)(2,1)S(1)} %collective-permute-done.11), channel_id=1, source_target_pairs={{4,0},{8,12},{5,1},{9,13},{6,2},{10,14},{7,3},{11,15},{20,16},{24,... | collective-permute-start | bytes 1572872 | tf_op jit(solution)/shard_map/ppermute | solution.py:146
  51.8 23.8 %collective-permute-start.7 = (bf16[512,512]{1,0:T(8,128)(2,1)S(1)}, bf16[512,512]{1,0:T(8,128)(2,1)S(1)}, u32[]{:S(2)}, u32[]{:S(2)}) collective-permute-start(bf16[512,512]{1,0:T(8,128)(2,1)S(1)} %collective-permute-done.6), channel_id=1, source_target_pairs={{0,2},{2,0},{1,3},{3,1},{4,6},{6,4},{5,7},{7,5},{8,10},{10,8},{9,1... | collective-permute-start | bytes 1572872 | tf_op jit(solution)/shard_map/ppermute | solution.py:16
  61.7 12.4 %collective-permute-start.17 = (bf16[512,512]{1,0:T(8,128)(2,1)S(1)}, bf16[512,512]{1,0:T(8,128)(2,1)S(1)}, u32[]{:S(2)}, u32[]{:S(2)}) collective-permute-start(bf16[512,512]{1,0:T(8,128)(2,1)S(1)} %collective-permute-done.6), channel_id=1, source_target_pairs={{4,8},{8,4},{5,9},{9,5},{6,10},{10,6},{7,11},{11,7},{20,24},{24,20... | collective-permute-start | bytes 1572872 | tf_op jit(solution)/shard_map/ppermute | solution.py:147
  71.2 29.1 %collective-permute-start.10 = (bf16[512,512]{1,0:T(8,128)(2,1)S(1)}, bf16[512,512]{1,0:T(8,128)(2,1)S(1)}, u32[]{:S(2)}, u32[]{:S(2)}) collective-permute-start(bf16[512,512]{1,0:T(8,128)(2,1)S(1)} %broadcast_select_fusion.3), channel_id=1, source_target_pairs={{0,1},{1,0},{2,3},{3,2},{4,5},{5,4},{6,7},{7,6},{8,9},{9,8},{10,11... | collective-permute-start | bytes 1572872 | tf_op jit(solution)/shard_map/ppermute | solution.py:16
  71.2 16.6 %collective-permute-start.15 = (bf16[512,512]{1,0:T(8,128)(2,1)S(1)}, bf16[512,512]{1,0:T(8,128)(2,1)S(1)}, u32[]{:S(2)}, u32[]{:S(2)}) collective-permute-start(bf16[512,512]{1,0:T(8,128)(2,1)S(1)} %collective-permute-done.14), channel_id=1, source_target_pairs={{4,0},{8,12},{5,1},{9,13},{6,2},{10,14},{7,3},{11,15},{20,16},{24,... | collective-permute-start | bytes 1572872 | tf_op jit(solution)/shard_map/ppermute | solution.py:148
  72.6 27.7 %collective-permute-start.13 = (bf16[512,512]{1,0:T(8,128)(2,1)S(1)}, bf16[512,512]{1,0:T(8,128)(2,1)S(1)}, u32[]{:S(2)}, u32[]{:S(2)}) collective-permute-start(bf16[512,512]{1,0:T(8,128)(2,1)S(1)} %broadcast_select_fusion.2), channel_id=1, source_target_pairs={{0,2},{2,0},{1,3},{3,1},{4,6},{6,4},{5,7},{7,5},{8,10},{10,8},{9,1... | collective-permute-start | bytes 1572872 | tf_op jit(solution)/shard_map/ppermute | solution.py:16
  74.2 24.5 %collective-permute-start.18 = (bf16[512,512]{1,0:T(8,128)(2,1)S(1)}, bf16[512,512]{1,0:T(8,128)(2,1)S(1)}, u32[]{:S(2)}, u32[]{:S(2)}) collective-permute-start(bf16[512,512]{1,0:T(8,128)(2,1)S(1)} %collective-permute-done.17), channel_id=1, source_target_pairs={{4,0},{8,12},{5,1},{9,13},{6,2},{10,14},{7,3},{11,15},{20,16},{24,... | collective-permute-start | bytes 1572872 | tf_op jit(solution)/shard_map/ppermute | solution.py:148
  87.9 13.8 %collective-permute-start.16 = (bf16[512,512]{1,0:T(8,128)(2,1)S(1)}, bf16[512,512]{1,0:T(8,128)(2,1)S(1)}, u32[]{:S(2)}, u32[]{:S(2)}) collective-permute-start(bf16[512,512]{1,0:T(8,128)(2,1)S(1)} %broadcast_select_fusion.1), channel_id=1, source_target_pairs={{0,1},{1,0},{2,3},{3,2},{4,5},{5,4},{6,7},{7,6},{8,9},{9,8},{10,11... | collective-permute-start | bytes 1572872 | tf_op jit(solution)/shard_map/ppermute | solution.py:16
  98.8 3.0 %copy-start = (bf16[512,512]{1,0:T(8,128)(2,1)S(1)}, bf16[512,512]{1,0:T(8,128)(2,1)}, u32[]{:S(2)}) copy-start(bf16[512,512]{1,0:T(8,128)(2,1)} %param.2) | copy-start | bytes 1572868
  98.8 13.6 %collective-permute-start.19 = (bf16[512,512]{1,0:T(8,128)(2,1)S(1)}, bf16[512,512]{1,0:T(8,128)(2,1)S(1)}, u32[]{:S(2)}, u32[]{:S(2)}) collective-permute-start(bf16[512,512]{1,0:T(8,128)(2,1)S(1)} %broadcast_select_fusion), channel_id=1, source_target_pairs={{0,2},{2,0},{1,3},{3,1},{4,6},{6,4},{5,7},{7,5},{8,10},{10,8},{9,1... | collective-permute-start | bytes 1572872 | tf_op jit(solution)/shard_map/ppermute | solution.py:16
  101.7 10.7 %copy-start.1 = (bf16[512,512]{1,0:T(8,128)(2,1)S(1)}, bf16[512,512]{1,0:T(8,128)(2,1)}, u32[]{:S(2)}) copy-start(bf16[512,512]{1,0:T(8,128)(2,1)} %param.3) | copy-start | bytes 1572868
  113.6 4.5 %copy-start.5 = (bf16[512,512]{1,0:T(8,128)(2,1)S(1)}, bf16[512,512]{1,0:T(8,128)(2,1)}, u32[]{:S(2)}) copy-start(bf16[512,512]{1,0:T(8,128)(2,1)} %copy-done.4) | copy-start | bytes 1572868
  118.1 8.2 %collective-permute-start.22 = (f32[]{:T(128)}, f32[]{:T(128)}, u32[]{:S(2)}, u32[]{:S(2)}) collective-permute-start(f32[]{:T(128)} %get-tuple-element.8), channel_id=1, source_target_pairs={{0,1},{1,0},{2,3},{3,2},{4,5},{5,4},{6,7},{7,6},{8,9},{9,8},{10,11... | collective-permute-start | bytes 20 | tf_op jit(solution)/shard_map/ppermute | solution.py:16
  120.4 15.3 %collective-permute-start.21 = (bf16[512,512]{1,0:T(8,128)(2,1)}, bf16[512,512]{1,0:T(8,128)(2,1)}, u32[]{:S(2)}, u32[]{:S(2)}) collective-permute-start(bf16[512,512]{1,0:T(8,128)(2,1)} %slice.74), channel_id=1, source_target_pairs={{0,2},{2,0},{1,3},{3,1},{4,6},{6,4},{5,7},{7,5},{8,10},{10,8},{9,1... | collective-permute-start | bytes 1572872 | tf_op jit(solution)/shard_map/ppermute | solution.py:16
  123.3 1.5 %copy-start.2 = (f32[512,1024]{1,0:T(8,128)}, f32[512,1024]{1,0:T(8,128)S(1)}, u32[]{:S(2)}) copy-start(f32[512,1024]{1,0:T(8,128)S(1)} %multiply_subtract_fusion.1) | copy-start | bytes 6291460
  124.2 13.6 %collective-permute-start.20 = (bf16[512,512]{1,0:T(8,128)(2,1)}, bf16[512,512]{1,0:T(8,128)(2,1)}, u32[]{:S(2)}, u32[]{:S(2)}) collective-permute-start(bf16[512,512]{1,0:T(8,128)(2,1)} %slice.75), channel_id=1, source_target_pairs={{0,1},{1,0},{2,3},{3,2},{4,5},{5,4},{6,7},{7,6},{8,9},{9,8},{10,11... | collective-permute-start | bytes 1572872 | tf_op jit(solution)/shard_map/ppermute | solution.py:16
  127.5 7.6 %collective-permute-start.23 = (f32[]{:T(128)}, f32[]{:T(128)}, u32[]{:S(2)}, u32[]{:S(2)}) collective-permute-start(f32[]{:T(128)} %add.110), channel_id=1, source_target_pairs={{0,2},{2,0},{1,3},{3,1},{4,6},{6,4},{5,7},{7,5},{8,10},{10,8},{9,1... | collective-permute-start | bytes 20 | tf_op jit(solution)/shard_map/ppermute | solution.py:16
  135.7 2.2 %copy-start.3 = (f32[512,1024]{1,0:T(8,128)S(1)}, f32[512,1024]{1,0:T(8,128)}, u32[]{:S(2)}) copy-start(f32[512,1024]{1,0:T(8,128)} %copy-done.2) | copy-start | bytes 6291460

commit v2 on v1

--- a/solution.py
+++ b/solution.py
@@ -140,12 +140,15 @@
     middle = [(1, 2), (2, 1)]
     outward = [(1, 0), (2, 3)]
 
+    def along(block, route):
+        return lax.ppermute(block, "dp", route)
+
     def chain(block):
-        first = lax.ppermute(block, "dp", pairs)
-        second_inner = lax.ppermute(block, "dp", middle)
-        second_outer = lax.ppermute(second_inner, "dp", outward)
-        third_inner = lax.ppermute(first, "dp", middle)
-        third_outer = lax.ppermute(third_inner, "dp", outward)
+        first = along(block, pairs)
+        second_inner = along(block, middle)
+        second_outer = along(second_inner, outward)
+        third_inner = along(first, middle)
+        third_outer = along(third_inner, outward)
         return [
             block,
             first,
@@ -153,39 +156,54 @@
             jnp.where(at_end, third_outer, third_inner),
         ]
 
+    def paired(own, bit):
+        return jnp.concatenate([own, swapped(own, "tile", bit)], axis=1).astype(jnp.float32)
+
+    partner_a = swapped(left_outputs, "tile", 0)
+    left_behind, partner_a = lax.optimization_barrier((left_outputs, partner_a))
     own_b = chain(right_outputs)
-    own_a = chain(left_outputs)
-
-    sum_a, sq_a = col_sums(left_outputs)
-    sum_b, sq_b = col_sums(right_outputs)
-    sum_a, sq_a, sum_b, sq_b = lax.psum((sum_a, sq_a, sum_b, sq_b), "dp")
-    mean_a, rstd_a = moment_pair(sum_a, sq_a, batch_images)
-    mean_b, rstd_b = moment_pair(sum_b, sq_b, batch_images)
-    stats_a = jnp.stack([mean_a, rstd_a])
-    stats_b = jnp.stack([mean_b, rstd_b])
-    stats_a = jnp.concatenate([stats_a, swapped(stats_a, "tile", 0)], axis=1)
-    stats_b = jnp.concatenate([stats_b, swapped(stats_b, "tile", 1)], axis=1)
-
-    def normalized(own, bit, stats):
-        pair = jnp.concatenate([own, swapped(own, "tile", bit)], axis=1)
-        return (pair.astype(jnp.float32) - stats[0]) * stats[1]
-
-    total = None
-    colsum_a = colsum_b = 0.0
+    own_a = chain(left_behind)
+    raw_a = jnp.concatenate([left_outputs, partner_a], axis=1).astype(jnp.float32)
+    raw_b = paired(own_b[0], 1)
+    shift_a = jnp.sum(raw_a, axis=0) / rows
+    shift_b = jnp.sum(raw_b, axis=0) / rows
+
+    products = None
+    sums_a = sums_b = (0.0, 0.0, 0.0)
+
+    def add_sums(sums, centred, rounded):
+        return (
+            sums[0] + jnp.sum(centred, axis=0),
+            sums[1] + jnp.sum(centred * centred, axis=0),
+            sums[2] + jnp.sum(rounded.astype(jnp.float32), axis=0),
+        )
+
     for step in range(4):
-        x_a = normalized(own_a[step], 0, stats_a)
-        x_b = normalized(own_b[step], 1, stats_b)
-        n_a = x_a.astype(jnp.bfloat16)
-        n_b = x_b.astype(jnp.bfloat16)
-        if step == 0:
-            xhat_a, xhat_b, norm_a, norm_b = x_a, x_b, n_a, n_b
+        c_a = (raw_a if step == 0 else paired(own_a[step], 0)) - shift_a
+        c_b = (raw_b if step == 0 else paired(own_b[step], 1)) - shift_b
+        u_a = c_a.astype(jnp.bfloat16)
+        u_b = c_b.astype(jnp.bfloat16)
         part = lax.dot_general(
-            n_a, n_b, (((0,), (0,)), ((), ())), preferred_element_type=jnp.float32
-        )
-        total = part if total is None else total + part
-        colsum_a = colsum_a + jnp.sum(n_a.astype(jnp.float32), axis=0)
-        colsum_b = colsum_b + jnp.sum(n_b.astype(jnp.float32), axis=0)
-    corr = total / batch_images
+            u_a, u_b, (((0,), (0,)), ((), ())), preferred_element_type=jnp.float32
+        )
+        products = part if products is None else products + part
+        sums_a = add_sums(sums_a, c_a, u_a)
+        sums_b = add_sums(sums_b, c_b, u_b)
+
+    def moments(sums):
+        delta = sums[0] / batch_images
+        rstd = lax.rsqrt(sums[1] / batch_images - delta * delta + 1e-05)
+        return delta, rstd, (sums[2] / batch_images - delta) * rstd
+
+    delta_a, rstd_a, rest_a = moments(sums_a)
+    delta_b, rstd_b, rest_b = moments(sums_b)
+    corr = (products / batch_images - delta_a[:, None] * delta_b[None, :]) * (
+        rstd_a[:, None] * rstd_b[None, :]
+    )
+    xhat_a = (raw_a - shift_a - delta_a) * rstd_a
+    xhat_b = (raw_b - shift_b - delta_b) * rstd_b
+    norm_a = xhat_a.astype(jnp.bfloat16)
+    norm_b = xhat_b.astype(jnp.bfloat16)
 
     local = jnp.arange(half, dtype=jnp.int32)
     diagonal = (local[:, None] == local[None, :]) & (local < quart)[:, None]
@@ -196,8 +214,8 @@
     dcorr = jnp.where(diagonal, corr - 1.0, off_weight * corr).astype(jnp.bfloat16)
 
     wide = dcorr.astype(jnp.float32)
-    first_a = jnp.sum(wide * (colsum_b / batch_images)[None, :], axis=1)
-    first_b = jnp.sum(wide * (colsum_a / batch_images)[:, None], axis=0)
+    first_a = jnp.sum(wide * rest_b[None, :], axis=1)
+    first_b = jnp.sum(wide * rest_a[:, None], axis=0)
     product = wide * corr
     second_a = jnp.sum(product, axis=1)
     second_b = jnp.sum(product, axis=0)
@@ -209,12 +227,12 @@
     grad_b = grad_b - first_b - xhat_b * second_b
     other_b = swapped(grad_b[:, quart:].astype(jnp.bfloat16), "tile", 1)
     other_a = swapped(grad_a[:, quart:].astype(jnp.bfloat16), "tile", 0)
-    left_gradient = (rstd_a * (grad_a[:, :quart] + other_a.astype(jnp.float32))).astype(
-        jnp.bfloat16
-    )
-    right_gradient = (rstd_b * (grad_b[:, :quart] + other_b.astype(jnp.float32))).astype(
-        jnp.bfloat16
-    )
+    left_gradient = (
+        rstd_a[:quart] * (grad_a[:, :quart] + other_a.astype(jnp.float32))
+    ).astype(jnp.bfloat16)
+    right_gradient = (
+        rstd_b[:quart] * (grad_b[:, :quart] + other_b.astype(jnp.float32))
+    ).astype(jnp.bfloat16)
 
     owned = half // 4
     row_quarter = jnp.where(dpos // 2 == column_halves, 0, quart)

time: 141 us -> 112 us (0.79)
  blocking collectives: 14.5 us -> 0 us
  waiting for transfers between devices: 59.2 us -> 48.8 us
  starting transfers between devices: 37.8 us -> 32.3 us
    psum x1 -> x0, blocking collectives: 14.5 us -> none  [gathered_device(): sum_a, sq_a, sum_b, sq_b = lax.psum((sum_a, sq_a, sum_b, sq_b), 'dp')]
    ppermute x14 -> x12, waiting for transfers between devices: 13.7 us -> 1.02 us  [swapped(): return lax.ppermute(block, axis, route)]
    ppermute x10, starting transfers between devices: 21.7 us -> 16.2 us  [along(): return lax.ppermute(block, 'dp', route)]
    ppermute x10, waiting for transfers between devices: 45.5 us -> 47.8 us  [along(): return lax.ppermute(block, 'dp', route)]
    ppermute x14 -> x12, starting transfers between devices: 16.1 us -> 16.1 us  [swapped(): return lax.ppermute(block, axis, route)]
  transfers between devices with their start and end apart: 24 -> 22, of which waited for: 9 -> 7; matrix products, arithmetic and copies ran while one was open for 13% -> 14% of each run, Pallas kernels for 0% -> 0%
where the time goes in v2:
time: 112 us
  waiting for transfers between devices  48.8 us (44%)
  starting transfers between devices  32.3 us (29%)
  matrix products  12.3 us (11%)
  other arithmetic  10.3 us (9%)
  between operations  4.21 us (4%)
  local copies, waits for them, and re-layouts  3.7 us (3%)
    ppermute x10, waiting for transfers between devices, along(): return lax.ppermute(block, 'dp', route)  47.8 us
    ppermute x10, starting transfers between devices, along(): return lax.ppermute(block, 'dp', route)  16.2 us
    ppermute x12, starting transfers between devices, swapped(): return lax.ppermute(block, axis, route)  16.1 us
    dot_general x4, matrix products, gathered_device(): lax.dot_general(u_a, u_b, (((0,), (0,)), ((), ())), preferred_element_typ...  9.39 us
    reduce_sum x2, other arithmetic, add_sums(): jnp.sum(rounded.astype(jnp.float32), axis=0)  3.2 us
  transfers between devices with their start and end apart: 22, of which 7 were waited for; matrix products, arithmetic and copies ran while one was open for 14% of the time, Pallas kernels for 0%

profile of v2, /device:TPU:0, one launch (start us, length us, event | category | flops | bytes accessed | tf_op | source)
XLA Modules:
  0.0 111.7 jit_solution(17494151637358619104)
XLA Ops:
  1.1 2.7 %collective-permute-start.10 = (bf16[512,512]{1,0:T(8,128)(2,1)}, bf16[512,512]{1,0:T(8,128)(2,1)S(1)}, u32[]{:S(2)}, u32[]{:S(2)}) collective-permute-start(bf16[512,512]{1,0:T(8,128)(2,1)} %param.3), channel_id=1, source_target_pairs={{0,4},{4,0},{8,12},{12,8},{1,5},{5,1},{9,13},{13,9},{2,6},{6,2},{1... | collective-permute-start | bytes 1572872 | tf_op jit(solution)/shard_map/ppermute | solution.py:144
  4.5 1.6 %collective-permute-start.9 = (bf16[512,512]{1,0:T(8,128)(2,1)}, bf16[512,512]{1,0:T(8,128)(2,1)S(1)}, u32[]{:S(2)}, u32[]{:S(2)}) collective-permute-start(bf16[512,512]{1,0:T(8,128)(2,1)} %param.3), channel_id=1, source_target_pairs={{0,2},{2,0},{1,3},{3,1},{4,6},{6,4},{5,7},{7,5},{8,10},{10,8},{9,1... | collective-permute-start | bytes 1572872 | tf_op jit(solution)/shard_map/ppermute | solution.py:16
  6.8 5.7 %collective-permute-start.1 = (bf16[512,512]{1,0:T(8,128)(2,1)}, bf16[512,512]{1,0:T(8,128)(2,1)S(1)}, u32[]{:S(2)}, u32[]{:S(2)}) collective-permute-start(bf16[512,512]{1,0:T(8,128)(2,1)} %param.2), channel_id=1, source_target_pairs={{0,4},{4,0},{8,12},{12,8},{1,5},{5,1},{9,13},{13,9},{2,6},{6,2},{1... | collective-permute-start | bytes 1572872 | tf_op jit(solution)/shard_map/ppermute | solution.py:144
  12.5 4.3 %collective-permute-done.10 = bf16[512,512]{1,0:T(8,128)(2,1)S(1)} collective-permute-done((bf16[512,512]{1,0:T(8,128)(2,1)}, bf16[512,512]{1,0:T(8,128)(2,1)S(1)}, u32[]{:S(2)}, u32[]{:S(2)}) %collective-permute-start.10) | collective-permute-done | bytes 524320 | tf_op jit(solution)/shard_map/ppermute | solution.py:144
  17.5 1.3 %collective-permute-start.13 = (bf16[512,512]{1,0:T(8,128)(2,1)S(1)}, bf16[512,512]{1,0:T(8,128)(2,1)S(1)}, u32[]{:S(2)}, u32[]{:S(2)}) collective-permute-start(bf16[512,512]{1,0:T(8,128)(2,1)S(1)} %collective-permute-done.12), channel_id=1, source_target_pairs={{4,0},{8,12},{5,1},{9,13},{6,2},{10,14},{7,3},{11,15},{20,16},{24,... | collective-permute-start | bytes 1572872 | tf_op jit(solution)/shard_map/ppermute | solution.py:144
  18.8 1.2 %convert_reduce_fusion.1 = f32[1024]{0:T(1024)S(1)} fusion(bf16[512,512]{1,0:T(8,128)(2,1)S(1)} %collective-permute-done, bf16[512,512]{1,0:T(8,128)(2,1)} %param.2), kind=kLoop, calls=%fused_computation.22 | loop fusion | flops 2620416 | bytes 1052672 | tf_op jit(solution)/shard_map/reduce_sum | solution.py:168
  20.0 1.9 %collective-permute-start.11 = (bf16[512,512]{1,0:T(8,128)(2,1)S(1)}, bf16[512,512]{1,0:T(8,128)(2,1)S(1)}, u32[]{:S(2)}, u32[]{:S(2)}) collective-permute-start(bf16[512,512]{1,0:T(8,128)(2,1)S(1)} %collective-permute-done.10), channel_id=1, source_target_pairs={{0,2},{2,0},{1,3},{3,1},{4,6},{6,4},{5,7},{7,5},{8,10},{10,8},{9,1... | collective-permute-start | bytes 1572872 | tf_op jit(solution)/shard_map/ppermute | solution.py:16
  22.0 1.3 %collective-permute-start.4 = (bf16[512,512]{1,0:T(8,128)(2,1)S(1)}, bf16[512,512]{1,0:T(8,128)(2,1)S(1)}, u32[]{:S(2)}, u32[]{:S(2)}) collective-permute-start(bf16[512,512]{1,0:T(8,128)(2,1)S(1)} %collective-permute-done.3), channel_id=1, source_target_pairs={{4,0},{8,12},{5,1},{9,13},{6,2},{10,14},{7,3},{11,15},{20,16},{24,... | collective-permute-start | bytes 1572872 | tf_op jit(solution)/shard_map/ppermute | solution.py:144
  23.2 1.2 %convert_reduce_fusion = f32[1024]{0:T(1024)S(1)} fusion(bf16[512,512]{1,0:T(8,128)(2,1)S(1)} %collective-permute-done.9, bf16[512,512]{1,0:T(8,128)(2,1)} %param.3), kind=kLoop, calls=%fused_computation.16 | loop fusion | flops 2620416 | bytes 1052672 | tf_op jit(solution)/shard_map/reduce_sum | solution.py:169
  24.5 3.5 %collective-permute-done.1 = bf16[512,512]{1,0:T(8,128)(2,1)S(1)} collective-permute-done((bf16[512,512]{1,0:T(8,128)(2,1)}, bf16[512,512]{1,0:T(8,128)(2,1)S(1)}, u32[]{:S(2)}, u32[]{:S(2)}) %collective-permute-start.1) | collective-permute-done | bytes 524320 | tf_op jit(solution)/shard_map/ppermute | solution.py:144
  28.7 1.3 %collective-permute-start.16 = (bf16[512,512]{1,0:T(8,128)(2,1)S(1)}, bf16[512,512]{1,0:T(8,128)(2,1)S(1)}, u32[]{:S(2)}, u32[]{:S(2)}) collective-permute-start(bf16[512,512]{1,0:T(8,128)(2,1)S(1)} %collective-permute-done.15), channel_id=1, source_target_pairs={{4,0},{8,12},{5,1},{9,13},{6,2},{10,14},{7,3},{11,15},{20,16},{24,... | collective-permute-start | bytes 1572872 | tf_op jit(solution)/shard_map/ppermute | solution.py:144
  30.0 9.2 %collective-permute-done.13 = bf16[512,512]{1,0:T(8,128)(2,1)S(1)} collective-permute-done((bf16[512,512]{1,0:T(8,128)(2,1)S(1)}, bf16[512,512]{1,0:T(8,128)(2,1)S(1)}, u32[]{:S(2)}, u32[]{:S(2)}) %collective-permute-start.13) | collective-permute-done | bytes 524320 | tf_op jit(solution)/shard_map/ppermute | solution.py:144
  39.3 1.9 %collective-permute-start.14 = (bf16[512,512]{1,0:T(8,128)(2,1)S(1)}, bf16[512,512]{1,0:T(8,128)(2,1)S(1)}, u32[]{:S(2)}, u32[]{:S(2)}) collective-permute-start(bf16[512,512]{1,0:T(8,128)(2,1)S(1)} %broadcast_select_fusion.1), channel_id=1, source_target_pairs={{0,2},{2,0},{1,3},{3,1},{4,6},{6,4},{5,7},{7,5},{8,10},{10,8},{9,1... | collective-permute-start | bytes 1572872 | tf_op jit(solution)/shard_map/ppermute | solution.py:16
  41.3 9.2 %collective-permute-done.4 = bf16[512,512]{1,0:T(8,128)(2,1)S(1)} collective-permute-done((bf16[512,512]{1,0:T(8,128)(2,1)S(1)}, bf16[512,512]{1,0:T(8,128)(2,1)S(1)}, u32[]{:S(2)}, u32[]{:S(2)}) %collective-permute-start.4) | collective-permute-done | bytes 524320 | tf_op jit(solution)/shard_map/ppermute | solution.py:144
  51.2 10.3 %collective-permute-done.16 = bf16[512,512]{1,0:T(8,128)(2,1)S(1)} collective-permute-done((bf16[512,512]{1,0:T(8,128)(2,1)S(1)}, bf16[512,512]{1,0:T(8,128)(2,1)S(1)}, u32[]{:S(2)}, u32[]{:S(2)}) %collective-permute-start.16) | collective-permute-done | bytes 524320 | tf_op jit(solution)/shard_map/ppermute | solution.py:144
  61.5 1.3 %collective-permute-start.7 = (bf16[512,512]{1,0:T(8,128)(2,1)S(1)}, bf16[512,512]{1,0:T(8,128)(2,1)S(1)}, u32[]{:S(2)}, u32[]{:S(2)}) collective-permute-start(bf16[512,512]{1,0:T(8,128)(2,1)S(1)} %collective-permute-done.6), channel_id=1, source_target_pairs={{4,0},{8,12},{5,1},{9,13},{6,2},{10,14},{7,3},{11,15},{20,16},{24,... | collective-permute-start | bytes 1572872 | tf_op jit(solution)/shard_map/ppermute | solution.py:144
  62.8 1.7 %collective-permute-start.17 = (bf16[512,512]{1,0:T(8,128)(2,1)S(1)}, bf16[512,512]{1,0:T(8,128)(2,1)S(1)}, u32[]{:S(2)}, u32[]{:S(2)}) collective-permute-start(bf16[512,512]{1,0:T(8,128)(2,1)S(1)} %broadcast_select_fusion), channel_id=1, source_target_pairs={{0,2},{2,0},{1,3},{3,1},{4,6},{6,4},{5,7},{7,5},{8,10},{10,8},{9,1... | collective-permute-start | bytes 1572872 | tf_op jit(solution)/shard_map/ppermute | solution.py:16
  64.6 1.3 %fusion.51 = f32[1024,1024]{0,1:T(8,128)S(1)} fusion(f32[1024]{0:T(1024)S(1)} %broadcast_multiply_fusion.1, f32[1024]{0:T(1024)S(1)} %broadcast_multiply_fusion, bf16[512,512]{1,0:T(8,128)(2,1)S(1)} %collective-permute-done.11, bf16[512,512]{1,0:T(8,128)(2,1)S(1)} %collective-permute-done.10, bf16[512,512]{1,0:T(8,128)(2,1)S(1)} %collective-permute-done.2, ...), kind=kOutput, calls=%fused_computation.93 | convolution fusion | flops 1080033280 | bytes 6299648 | tf_op jit(solution)/shard_map/dot_general | solution.py:186
  65.9 11.1 %collective-permute-done.7 = bf16[512,512]{1,0:T(8,128)(2,1)S(1)} collective-permute-done((bf16[512,512]{1,0:T(8,128)(2,1)S(1)}, bf16[512,512]{1,0:T(8,128)(2,1)S(1)}, u32[]{:S(2)}, u32[]{:S(2)}) %collective-permute-start.7) | collective-permute-done | bytes 524320 | tf_op jit(solution)/shard_map/ppermute | solution.py:144
  77.2 1.5 %convert_reduce_fusion.7 = (f32[1024]{0:T(1024)S(1)}, f32[1024]{0:T(1024)S(1)}, f32[1024]{0:T(1024)S(1)}, f32[1024]{0:T(1024)S(1)}, f32[1024]{0:T(1024)S(1)}, /*...) fusion(f32[1024]{0:T(1024)S(1)} %broadcast_multiply_fusion, ...), kind=kLoop, calls=%fused_computation.42 | loop fusion | flops 23056384 | bytes 4247552 | tf_op jit(solution)/shard_map/reduce_sum | solution.py:178
  78.8 1.3 %fusion.53 = f32[1024,1024]{0,1:T(8,128)S(1)} fusion(f32[1024]{0:T(1024)S(1)} %broadcast_multiply_fusion.1, f32[1024]{0:T(1024)S(1)} %broadcast_multiply_fusion, bf16[512,512]{1,0:T(8,128)(2,1)S(1)} %collective-permute-done.14, bf16[512,512]{1,0:T(8,128)(2,1)S(1)} %broadcast_select_fusion.1, bf16[512,512]{1,0:T(8,128)(2,1)S(1)} %collective-permute-done.5, ...), kind=kOutput, calls=%fused_computation.94 | convolution fusion | flops 1080033280 | bytes 6299648 | tf_op jit(solution)/shard_map/dot_general | solution.py:186
  80.1 1.7 %convert_reduce_fusion.3 = (f32[1024]{0:T(1024)S(1)}, f32[1024]{0:T(1024)S(1)}, f32[1024]{0:T(1024)S(1)}, f32[1024]{0:T(1024)S(1)}, f32[1024]{0:T(1024)S(1)}, /*...) fusion(f32[1024]{0:T(1024)S(1)} %broadcast_multiply_fusion.1, ...), kind=kLoop, calls=%fused_computation.38 | loop fusion | flops 23056384 | bytes 4247552 | tf_op jit(solution)/shard_map/reduce_sum | solution.py:178
  81.9 1.3 %fusion.55 = f32[1024,1024]{0,1:T(8,128)S(1)} fusion(f32[1024]{0:T(1024)S(1)} %broadcast_multiply_fusion.1, f32[1024]{0:T(1024)S(1)} %broadcast_multiply_fusion, bf16[512,512]{1,0:T(8,128)(2,1)S(1)} %collective-permute-done.17, bf16[512,512]{1,0:T(8,128)(2,1)S(1)} %broadcast_select_fusion, bf16[512,512]{1,0:T(8,128)(2,1)S(1)} %collective-permute-done.8, ...), kind=kOutput, calls=%fused_computation.95 | convolution fusion | flops 1080033280 | bytes 6299648 | tf_op jit(solution)/shard_map/dot_general | solution.py:186
  83.2 5.4 %fusion.2 = (f32[]{:T(128)}, f32[1024]{0:T(1024)S(1)}, f32[1024]{0:T(1024)S(1)}, f32[1024]{0:T(1024)S(1)}, f32[1024]{0:T(1024)S(1)}, /*index=5*/f32[1024,1024]{0,1:T(8,128)S(1)}) fusion(pred[1024]{0:T(1024)(128)(4,1)S(1)} %iota_compare_fusion.1, f32[1024]{0:T(1024)S(1)} %get-tuple-element.56, f32[1024]{0:T(1024)S(1)} %get-tuple-element.53, ...), kind=kOutput, calls=%fused_computation.7 | convolution fusion | flops 1108340736 | bytes 18924548 | tf_op jit(solution)/shard_map/dot_general | solution.py:186
  89.1 1.5 %fusion.24 = f32[512,1024]{1,0:T(8,128)S(1)} fusion(f32[1024]{0:T(1024)S(1)} %get-tuple-element.15, f32[1024]{0:T(1024)S(1)} %get-tuple-element.14, f32[1024]{0:T(1024)S(1)} %add_rsqrt_fusion.1, f32[1024]{0:T(1024)S(1)} %get-tuple-element.54, f32[1024]{0:T(1024)S(1)} %add_rsqrt_fusion, f32[1024]{0:T(1024)S(1)} %get-tuple-element.57, ...), kind=kOutput, calls=%fused_computation.35 | convolution fusion | flops 1089470464 | bytes 8422400 | tf_op jit(solution)/shard_map/dot_general | solution.py:225
  91.5 1.5 %collective-permute-start.19 = (bf16[512,512]{1,0:T(8,128)(2,1)}, bf16[512,512]{1,0:T(8,128)(2,1)}, u32[]{:S(2)}, u32[]{:S(2)}) collective-permute-start(bf16[512,512]{1,0:T(8,128)(2,1)} %slice.50), channel_id=1, source_target_pairs={{0,2},{2,0},{1,3},{3,1},{4,6},{6,4},{5,7},{7,5},{8,10},{10,8},{9,1... | collective-permute-start | bytes 1572872 | tf_op jit(solution)/shard_map/ppermute | solution.py:16
  93.0 1.5 %fusion.20 = f32[512,1024]{1,0:T(8,128)S(1)} fusion(f32[1024]{0:T(1024)S(1)} %get-tuple-element.16, f32[1024]{0:T(1024)S(1)} %add_rsqrt_fusion.1, f32[1024]{0:T(1024)S(1)} %get-tuple-element.54, f32[1024]{0:T(1024)S(1)} %get-tuple-element.13, f32[1024]{0:T(1024)S(1)} %add_rsqrt_fusion, f32[1024]{0:T(1024)S(1)} %get-tuple-element.57, ...), kind=kOutput, calls=%fused_computation.31 | convolution fusion | flops 1089470464 | bytes 8422400 | tf_op jit(solution)/shard_map/dot_general | solution.py:222
  96.1 1.3 %copy.6 = f32[1,256,1024]{2,1,0:T(8,128)} copy(f32[1,256,1024]{1,2,0:T(8,128)S(1)} %fusion.44) | data formatting | bytes 2097152
  98.8 5.9 %collective-permute-start.21 = (f32[]{:T(128)}, f32[]{:T(128)}, u32[]{:S(2)}, u32[]{:S(2)}) collective-permute-start(f32[]{:T(128)} %add.303), channel_id=1, source_target_pairs={{0,2},{2,0},{1,3},{3,1},{4,6},{6,4},{5,7},{7,5},{8,10},{10,8},{9,1... | collective-permute-start | bytes 20 | tf_op jit(solution)/shard_map/ppermute | solution.py:16
  104.7 1.0 collective-permute-done.21
  106.4 2.1 %fusion.41 = bf16[512,512]{1,0:T(8,128)(2,1)} fusion(f32[512,1024]{1,0:T(8,128)S(1)} %fusion.24, bf16[512,512]{1,0:T(8,128)(2,1)} %collective-permute-done.19, f32[512]{0:T(512)S(1)} %slice-done), kind=kLoop, calls=%fused_computation.72 | loop fusion | flops 1048576 | bytes 2099200 | tf_op jit(solution)/shard_map/convert_element_type | solution.py:235
  108.5 2.0 %fusion.43 = bf16[512,512]{1,0:T(8,128)(2,1)} fusion(f32[512,1024]{1,0:T(8,128)S(1)} %copy-done.3, bf16[512,512]{1,0:T(8,128)(2,1)} %collective-permute-done.18, f32[512]{0:T(512)S(1)} %slice-done.1), kind=kLoop, calls=%fused_computation.76 | loop fusion | flops 1048576 | bytes 2099200 | tf_op jit(solution)/shard_map/convert_element_type | solution.py:232
  (56 shorter events, 7.3 us)
Async XLA Ops:
  0.6 5.4 %collective-permute-start = (bf16[512,512]{1,0:T(8,128)(2,1)}, bf16[512,512]{1,0:T(8,128)(2,1)S(1)}, u32[]{:S(2)}, u32[]{:S(2)}) collective-permute-start(bf16[512,512]{1,0:T(8,128)(2,1)} %param.2), channel_id=1, source_target_pairs={{0,1},{1,0},{2,3},{3,2},{4,5},{5,4},{6,7},{7,6},{8,9},{9,8},{10,11... | collective-permute-start | bytes 1572872 | tf_op jit(solution)/shard_map/ppermute | solution.py:16
  1.1 15.6 %collective-permute-start.10 = (bf16[512,512]{1,0:T(8,128)(2,1)}, bf16[512,512]{1,0:T(8,128)(2,1)S(1)}, u32[]{:S(2)}, u32[]{:S(2)}) collective-permute-start(bf16[512,512]{1,0:T(8,128)(2,1)} %param.3), channel_id=1, source_target_pairs={{0,4},{4,0},{8,12},{12,8},{1,5},{5,1},{9,13},{13,9},{2,6},{6,2},{1... | collective-permute-start | bytes 1572872 | tf_op jit(solution)/shard_map/ppermute | solution.py:144
  3.8 13.7 %collective-permute-start.12 = (bf16[512,512]{1,0:T(8,128)(2,1)}, bf16[512,512]{1,0:T(8,128)(2,1)S(1)}, u32[]{:S(2)}, u32[]{:S(2)}) collective-permute-start(bf16[512,512]{1,0:T(8,128)(2,1)} %param.3), channel_id=1, source_target_pairs={{4,8},{8,4},{5,9},{9,5},{6,10},{10,6},{7,11},{11,7},{20,24},{24,20... | collective-permute-start | bytes 1572872 | tf_op jit(solution)/shard_map/ppermute | solution.py:144
  4.5 15.5 %collective-permute-start.9 = (bf16[512,512]{1,0:T(8,128)(2,1)}, bf16[512,512]{1,0:T(8,128)(2,1)S(1)}, u32[]{:S(2)}, u32[]{:S(2)}) collective-permute-start(bf16[512,512]{1,0:T(8,128)(2,1)} %param.3), channel_id=1, source_target_pairs={{0,2},{2,0},{1,3},{3,1},{4,6},{6,4},{5,7},{7,5},{8,10},{10,8},{9,1... | collective-permute-start | bytes 1572872 | tf_op jit(solution)/shard_map/ppermute | solution.py:16
  6.0 15.9 %collective-permute-start.3 = (bf16[512,512]{1,0:T(8,128)(2,1)}, bf16[512,512]{1,0:T(8,128)(2,1)S(1)}, u32[]{:S(2)}, u32[]{:S(2)}) collective-permute-start(bf16[512,512]{1,0:T(8,128)(2,1)} %param.2), channel_id=1, source_target_pairs={{4,8},{8,4},{5,9},{9,5},{6,10},{10,6},{7,11},{11,7},{20,24},{24,20... | collective-permute-start | bytes 1572872 | tf_op jit(solution)/shard_map/ppermute | solution.py:144
  6.8 21.2 %collective-permute-start.1 = (bf16[512,512]{1,0:T(8,128)(2,1)}, bf16[512,512]{1,0:T(8,128)(2,1)S(1)}, u32[]{:S(2)}, u32[]{:S(2)}) collective-permute-start(bf16[512,512]{1,0:T(8,128)(2,1)} %param.2), channel_id=1, source_target_pairs={{0,4},{4,0},{8,12},{12,8},{1,5},{5,1},{9,13},{13,9},{2,6},{6,2},{1... | collective-permute-start | bytes 1572872 | tf_op jit(solution)/shard_map/ppermute | solution.py:144
  16.8 11.9 %collective-permute-start.15 = (bf16[512,512]{1,0:T(8,128)(2,1)S(1)}, bf16[512,512]{1,0:T(8,128)(2,1)S(1)}, u32[]{:S(2)}, u32[]{:S(2)}) collective-permute-start(bf16[512,512]{1,0:T(8,128)(2,1)S(1)} %collective-permute-done.10), channel_id=1, source_target_pairs={{4,8},{8,4},{5,9},{9,5},{6,10},{10,6},{7,11},{11,7},{20,24},{24,20... | collective-permute-start | bytes 1572872 | tf_op jit(solution)/shard_map/ppermute | solution.py:144
  17.5 21.8 %collective-permute-start.13 = (bf16[512,512]{1,0:T(8,128)(2,1)S(1)}, bf16[512,512]{1,0:T(8,128)(2,1)S(1)}, u32[]{:S(2)}, u32[]{:S(2)}) collective-permute-start(bf16[512,512]{1,0:T(8,128)(2,1)S(1)} %collective-permute-done.12), channel_id=1, source_target_pairs={{4,0},{8,12},{5,1},{9,13},{6,2},{10,14},{7,3},{11,15},{20,16},{24,... | collective-permute-start | bytes 1572872 | tf_op jit(solution)/shard_map/ppermute | solution.py:144
  20.0 42.8 %collective-permute-start.11 = (bf16[512,512]{1,0:T(8,128)(2,1)S(1)}, bf16[512,512]{1,0:T(8,128)(2,1)S(1)}, u32[]{:S(2)}, u32[]{:S(2)}) collective-permute-start(bf16[512,512]{1,0:T(8,128)(2,1)S(1)} %collective-permute-done.10), channel_id=1, source_target_pairs={{0,2},{2,0},{1,3},{3,1},{4,6},{6,4},{5,7},{7,5},{8,10},{10,8},{9,1... | collective-permute-start | bytes 1572872 | tf_op jit(solution)/shard_map/ppermute | solution.py:16
  22.0 28.5 %collective-permute-start.4 = (bf16[512,512]{1,0:T(8,128)(2,1)S(1)}, bf16[512,512]{1,0:T(8,128)(2,1)S(1)}, u32[]{:S(2)}, u32[]{:S(2)}) collective-permute-start(bf16[512,512]{1,0:T(8,128)(2,1)S(1)} %collective-permute-done.3), channel_id=1, source_target_pairs={{4,0},{8,12},{5,1},{9,13},{6,2},{10,14},{7,3},{11,15},{20,16},{24,... | collective-permute-start | bytes 1572872 | tf_op jit(solution)/shard_map/ppermute | solution.py:144
  28.0 22.5 %collective-permute-start.6 = (bf16[512,512]{1,0:T(8,128)(2,1)S(1)}, bf16[512,512]{1,0:T(8,128)(2,1)S(1)}, u32[]{:S(2)}, u32[]{:S(2)}) collective-permute-start(bf16[512,512]{1,0:T(8,128)(2,1)S(1)} %collective-permute-done.1), channel_id=1, source_target_pairs={{4,8},{8,4},{5,9},{9,5},{6,10},{10,6},{7,11},{11,7},{20,24},{24,20... | collective-permute-start | bytes 1572872 | tf_op jit(solution)/shard_map/ppermute | solution.py:144
  28.7 32.7 %collective-permute-start.16 = (bf16[512,512]{1,0:T(8,128)(2,1)S(1)}, bf16[512,512]{1,0:T(8,128)(2,1)S(1)}, u32[]{:S(2)}, u32[]{:S(2)}) collective-permute-start(bf16[512,512]{1,0:T(8,128)(2,1)S(1)} %collective-permute-done.15), channel_id=1, source_target_pairs={{4,0},{8,12},{5,1},{9,13},{6,2},{10,14},{7,3},{11,15},{20,16},{24,... | collective-permute-start | bytes 1572872 | tf_op jit(solution)/shard_map/ppermute | solution.py:144
  39.3 37.8 %collective-permute-start.14 = (bf16[512,512]{1,0:T(8,128)(2,1)S(1)}, bf16[512,512]{1,0:T(8,128)(2,1)S(1)}, u32[]{:S(2)}, u32[]{:S(2)}) collective-permute-start(bf16[512,512]{1,0:T(8,128)(2,1)S(1)} %broadcast_select_fusion.1), channel_id=1, source_target_pairs={{0,2},{2,0},{1,3},{3,1},{4,6},{6,4},{5,7},{7,5},{8,10},{10,8},{9,1... | collective-permute-start | bytes 1572872 | tf_op jit(solution)/shard_map/ppermute | solution.py:16
  50.5 14.1 %collective-permute-start.2 = (bf16[512,512]{1,0:T(8,128)(2,1)S(1)}, bf16[512,512]{1,0:T(8,128)(2,1)S(1)}, u32[]{:S(2)}, u32[]{:S(2)}) collective-permute-start(bf16[512,512]{1,0:T(8,128)(2,1)S(1)} %collective-permute-done.1), channel_id=1, source_target_pairs={{0,1},{1,0},{2,3},{3,2},{4,5},{5,4},{6,7},{7,6},{8,9},{9,8},{10,11... | collective-permute-start | bytes 1572872 | tf_op jit(solution)/shard_map/ppermute | solution.py:16
  50.6 28.2 %collective-permute-start.5 = (bf16[512,512]{1,0:T(8,128)(2,1)S(1)}, bf16[512,512]{1,0:T(8,128)(2,1)S(1)}, u32[]{:S(2)}, u32[]{:S(2)}) collective-permute-start(bf16[512,512]{1,0:T(8,128)(2,1)S(1)} %broadcast_select_fusion.3), channel_id=1, source_target_pairs={{0,1},{1,0},{2,3},{3,2},{4,5},{5,4},{6,7},{7,6},{8,9},{9,8},{10,11... | collective-permute-start | bytes 1572872 | tf_op jit(solution)/shard_map/ppermute | solution.py:16
  61.5 15.6 %collective-permute-start.7 = (bf16[512,512]{1,0:T(8,128)(2,1)S(1)}, bf16[512,512]{1,0:T(8,128)(2,1)S(1)}, u32[]{:S(2)}, u32[]{:S(2)}) collective-permute-start(bf16[512,512]{1,0:T(8,128)(2,1)S(1)} %collective-permute-done.6), channel_id=1, source_target_pairs={{4,0},{8,12},{5,1},{9,13},{6,2},{10,14},{7,3},{11,15},{20,16},{24,... | collective-permute-start | bytes 1572872 | tf_op jit(solution)/shard_map/ppermute | solution.py:144
  62.8 14.4 %copy-start = (bf16[512,512]{1,0:T(8,128)(2,1)S(1)}, bf16[512,512]{1,0:T(8,128)(2,1)}, u32[]{:S(2)}) copy-start(bf16[512,512]{1,0:T(8,128)(2,1)} %param.3) | copy-start | bytes 1572868
  62.8 14.3 %collective-permute-start.17 = (bf16[512,512]{1,0:T(8,128)(2,1)S(1)}, bf16[512,512]{1,0:T(8,128)(2,1)S(1)}, u32[]{:S(2)}, u32[]{:S(2)}) collective-permute-start(bf16[512,512]{1,0:T(8,128)(2,1)S(1)} %broadcast_select_fusion), channel_id=1, source_target_pairs={{0,2},{2,0},{1,3},{3,1},{4,6},{6,4},{5,7},{7,5},{8,10},{10,8},{9,1... | collective-permute-start | bytes 1572872 | tf_op jit(solution)/shard_map/ppermute | solution.py:16
  77.1 3.0 %collective-permute-start.8 = (bf16[512,512]{1,0:T(8,128)(2,1)S(1)}, bf16[512,512]{1,0:T(8,128)(2,1)S(1)}, u32[]{:S(2)}, u32[]{:S(2)}) collective-permute-start(bf16[512,512]{1,0:T(8,128)(2,1)S(1)} %broadcast_select_fusion.2), channel_id=1, source_target_pairs={{0,1},{1,0},{2,3},{3,2},{4,5},{5,4},{6,7},{7,6},{8,9},{9,8},{10,11... | collective-permute-start | bytes 1572872 | tf_op jit(solution)/shard_map/ppermute | solution.py:16
  78.8 14.2 %copy-start.4 = (f32[1024]{0:T(1024)}, f32[1024]{0:T(1024)S(1)}, u32[]{:S(2)}) copy-start(f32[1024]{0:T(1024)S(1)} %add_rsqrt_fusion) | copy-start | bytes 12292
  78.8 1.4 %copy-start.1 = (bf16[512,512]{1,0:T(8,128)(2,1)S(1)}, bf16[512,512]{1,0:T(8,128)(2,1)}, u32[]{:S(2)}) copy-start(bf16[512,512]{1,0:T(8,128)(2,1)} %param.2) | copy-start | bytes 1572868
  81.9 11.1 %copy-start.5 = (f32[1024]{0:T(1024)}, f32[1024]{0:T(1024)S(1)}, u32[]{:S(2)}) copy-start(f32[1024]{0:T(1024)S(1)} %add_rsqrt_fusion.1) | copy-start | bytes 12292
  88.6 8.8 %collective-permute-start.20 = (f32[]{:T(128)}, f32[]{:T(128)}, u32[]{:S(2)}, u32[]{:S(2)}) collective-permute-start(f32[]{:T(128)} %get-tuple-element.12), channel_id=1, source_target_pairs={{0,1},{1,0},{2,3},{3,2},{4,5},{5,4},{6,7},{7,6},{8,9},{9,8},{10,11... | collective-permute-start | bytes 20 | tf_op jit(solution)/shard_map/ppermute | solution.py:16
  91.5 14.9 %collective-permute-start.19 = (bf16[512,512]{1,0:T(8,128)(2,1)}, bf16[512,512]{1,0:T(8,128)(2,1)}, u32[]{:S(2)}, u32[]{:S(2)}) collective-permute-start(bf16[512,512]{1,0:T(8,128)(2,1)} %slice.50), channel_id=1, source_target_pairs={{0,2},{2,0},{1,3},{3,1},{4,6},{6,4},{5,7},{7,5},{8,10},{10,8},{9,1... | collective-permute-start | bytes 1572872 | tf_op jit(solution)/shard_map/ppermute | solution.py:16
  94.4 1.5 %copy-start.2 = (f32[512,1024]{1,0:T(8,128)}, f32[512,1024]{1,0:T(8,128)S(1)}, u32[]{:S(2)}) copy-start(f32[512,1024]{1,0:T(8,128)S(1)} %fusion.20) | copy-start | bytes 6291460
  95.4 13.1 %collective-permute-start.18 = (bf16[512,512]{1,0:T(8,128)(2,1)}, bf16[512,512]{1,0:T(8,128)(2,1)}, u32[]{:S(2)}, u32[]{:S(2)}) collective-permute-start(bf16[512,512]{1,0:T(8,128)(2,1)} %slice.51), channel_id=1, source_target_pairs={{0,1},{1,0},{2,3},{3,2},{4,5},{5,4},{6,7},{7,6},{8,9},{9,8},{10,11... | collective-permute-start | bytes 1572872 | tf_op jit(solution)/shard_map/ppermute | solution.py:16
  95.9 10.4 %slice-start = ((f32[1024]{0:T(1024)}), f32[512]{0:T(512)S(1)}, s32[]{:S(2)}) async-start(f32[1024]{0:T(1024)} %copy-done.4), calls=%async_computation | async-start | bytes 4096 | tf_op jit(solution)/shard_map/slice | solution.py:234
  96.1 12.4 %slice-start.1 = ((f32[1024]{0:T(1024)}), f32[512]{0:T(512)S(1)}, s32[]{:S(2)}) async-start(f32[1024]{0:T(1024)} %copy-done.5), calls=%async_computation.1 | async-start | bytes 4096 | tf_op jit(solution)/shard_map/slice | solution.py:231
  98.8 6.9 %collective-permute-start.21 = (f32[]{:T(128)}, f32[]{:T(128)}, u32[]{:S(2)}, u32[]{:S(2)}) collective-permute-start(f32[]{:T(128)} %add.303), channel_id=1, source_target_pairs={{0,2},{2,0},{1,3},{3,1},{4,6},{6,4},{5,7},{7,5},{8,10},{10,8},{9,1... | collective-permute-start | bytes 20 | tf_op jit(solution)/shard_map/ppermute | solution.py:16
  106.4 2.2 %copy-start.3 = (f32[512,1024]{1,0:T(8,128)S(1)}, f32[512,1024]{1,0:T(8,128)}, u32[]{:S(2)}) copy-start(f32[512,1024]{1,0:T(8,128)} %copy-done.2) | copy-start | bytes 6291460

commit v3 on v0

--- a/solution.py
+++ b/solution.py
@@ -1,6 +1,9 @@
+import functools
 import jax
 import jax.numpy as jnp
 from jax import lax
+from jax.experimental import pallas as pl
+from jax.experimental.pallas import tpu as pltpu
 from jax.sharding import PartitionSpec as P
 
 off_weight = 0.0051
@@ -43,7 +46,7 @@
     return (jnp.sum(as_float, axis=0), jnp.sum(as_float * as_float, axis=0))
 
 
-def per_device(left_outputs, right_outputs):
+def reduced_device(left_outputs, right_outputs):
     rows, quart = left_outputs.shape
     half = 2 * quart
     feats = 4 * quart
@@ -125,7 +128,463 @@
     return (left_gradient, right_gradient, corr_rows[None, :, :], jnp.reshape(loss, (1,)))
 
 
+def tile_scaled(sums, delta_col, rstd_col, delta_row, rstd_row, inverse_images):
+    return (sums * inverse_images - delta_col * delta_row) * rstd_col * rstd_row
+
+
+def centre_rows(source, shift, target, lanes, chunk):
+    rows, width = source.shape
+    zero = jnp.zeros((8, width), jnp.float32)
+
+    def body(step, carry):
+        total, squares, rounded = carry
+        at = pl.ds(pl.multiple_of(step * chunk, chunk), chunk)
+        centred = source[at, :].astype(jnp.float32) - shift
+        low = centred.astype(jnp.bfloat16)
+        target[at, lanes] = low
+        fold = lambda v: jnp.sum(v.reshape(chunk // 8, 8, width), axis=0)
+        return (
+            total + fold(centred),
+            squares + fold(centred * centred),
+            rounded + fold(low.astype(jnp.float32)),
+        )
+
+    sums = lax.fori_loop(0, rows // chunk, body, (zero, zero, zero), unroll=True)
+    return [jnp.sum(s, axis=0, keepdims=True) for s in sums]
+
+
+def normalise_rows(source, offset, rstd, target, lanes, chunk):
+    rows = source.shape[0]
+
+    def body(step, carry):
+        at = pl.ds(pl.multiple_of(step * chunk, chunk), chunk)
+        target[at, lanes] = ((source[at, :].astype(jnp.float32) - offset) * rstd).astype(
+            jnp.bfloat16
+        )
+        return carry
+
+    lax.fori_loop(0, rows // chunk, body, 0, unroll=True)
+
+
+def lanes_to_row(partial):
+    ones = jnp.ones((16, partial.shape[1]), jnp.bfloat16)
+    high = partial.astype(jnp.bfloat16)
+    low = (partial - high.astype(jnp.float32)).astype(jnp.bfloat16)
+    contract = (((1,), (1,)), ((), ()))
+    row = lax.dot_general(ones, high, contract, preferred_element_type=jnp.float32)
+    row = row + lax.dot_general(ones, low, contract, preferred_element_type=jnp.float32)
+    return row[:1, :]
+
+
+def fold_lanes(values):
+    width = values.shape[1]
+    return sum(values[:, at : at + 128] for at in range(0, width, 128))
+
+
+def partner_kernel(
+    images,
+    own_tile,
+    late_a,
+    late_other,
+    first_a,
+    first_other,
+    row_a,
+    prev,
+    late_b,
+    col_b,
+    norm_b,
+    partial_out,
+    dcorr_out,
+    mine_out,
+    vec_out,
+    centred,
+    norms,
+):
+    rows, quart = late_a.shape
+    half = 2 * quart
+    inverse = 1.0 / images
+    shift = row_a[0:1, :]
+    own = centre_rows(late_a, shift[:, :quart], centred, slice(0, quart), 64)
+    other = centre_rows(late_other, shift[:, quart:], centred, slice(quart, half), 64)
+    total, squares, rounded = [
+        row_a[i + 1 : i + 2, :] + jnp.concatenate([own[i], other[i]], axis=1) for i in range(3)
+    ]
+    delta = total * inverse
+    rstd = lax.rsqrt(squares * inverse - delta * delta + 1e-05)
+    rest = (rounded * inverse - delta) * rstd
+    offset = shift + delta
+    normalise_rows(first_a, offset[:, :quart], rstd[:, :quart], norms, slice(0, quart), 64)
+    normalise_rows(first_other, offset[:, quart:], rstd[:, quart:], norms, slice(quart, half), 64)
+    norms[rows : rows + 16, :] = jnp.broadcast_to(rest, (16, half)).astype(jnp.bfloat16)
+
+    delta_col = col_b[:, 0:1]
+    rstd_col = col_b[:, 1:2]
+    width = half // 4
+    across = jnp.zeros((quart, 128), jnp.float32)
+    down = []
+    for tile in range(4):
+        at = slice(tile * width, (tile + 1) * width)
+        sums = prev[:, at] + jnp.dot(
+            late_b[...], centred[:, at], preferred_element_type=jnp.float32
+        )
+        corr = tile_scaled(sums, delta_col, rstd_col, delta[:, at], rstd[:, at], inverse)
+        dcorr = off_weight * corr
+        dcorr_out[:, at] = dcorr.astype(jnp.bfloat16)
+        product = dcorr * corr
+        across = across + fold_lanes(product)
+        down.append(jnp.sum(product, axis=0, keepdims=True))
+
+        @pl.when(own_tile[0] == tile)
+        def _():
+            mine_out[...] = corr
+
+    vec_out[0:1, :] = delta
+    vec_out[1:2, :] = rstd
+    vec_out[2:3, :] = rest
+    vec_out[3:4, :] = jnp.concatenate(down, axis=1)
+    vec_out[4:8, :] = jnp.zeros((4, half), jnp.float32)
+    second = lanes_to_row(across)
+    contract = (((1,), (1,)), ((), ()))
+    for tile in range(2):
+        at = slice(tile * width, (tile + 1) * width)
+        terms = lax.dot_general(
+            norms[...], dcorr_out[at, :], contract, preferred_element_type=jnp.float32
+        )
+        partial_out[:, at] = (
+            terms[:rows]
+            - terms[rows : rows + 1]
+            - norm_b[:, at].astype(jnp.float32) * second[:, at]
+        ).astype(jnp.bfloat16)
+
+
+def own_kernel(
+    images,
+    own_tile,
+    late_a,
+    late_other,
+    first_a,
+    first_other,
+    row_a,
+    prev,
+    late_b,
+    col_b,
+    norm_b,
+    first_b,
+    row_b,
+    partner_dcorr,
+    partner_mine,
+    vec_a,
+    right_out,
+    left_out,
+    left_partial_out,
+    mine_out,
+    loss_out,
+    centred,
+    norms,
+    dcorr_own,
+    mine_own,
+):
+    rows, quart = late_a.shape
+    half = 2 * quart
+    inverse = 1.0 / images
+    shift = row_a[0:1, :]
+    delta = vec_a[0:1, :]
+    rstd = vec_a[1:2, :]
+    rest = vec_a[2:3, :]
+    offset = shift + delta
+    for source, lanes in ((late_a, slice(0, quart)), (late_other, slice(quart, half))):
+        normalise_rows(source, shift[:, lanes], 1.0, centred, lanes, 64)
+    for source, lanes in ((first_a, slice(0, quart)), (first_other, slice(quart, half))):
+        normalise_rows(source, offset[:, lanes], rstd[:, lanes], norms, lanes, 64)
+    norms[rows : rows + 16, :] = jnp.broadcast_to(rest, (16, half)).astype(jnp.bfloat16)
+
+    delta_col = col_b[:, 0:1]
+    rstd_col = col_b[:, 1:2]
+    width = half // 4
+    across = jnp.zeros((quart, 128), jnp.float32)
+    losses = jnp.zeros((8, 128), jnp.float32)
+    down = []
+    for tile in range(4):
+        at = slice(tile * width, (tile + 1) * width)
+        sums = prev[:, at] + jnp.dot(
+            late_b[...], centred[:, at], preferred_element_type=jnp.float32
+        )
+        corr = tile_scaled(sums, delta_col, rstd_col, delta[:, at], rstd[:, at], inverse)
+        dcorr = off_weight * corr
+        product = dcorr * corr
+        loss = product
+        if tile < 2:
+            feature = lax.broadcasted_iota(jnp.int32, (quart, width), 0)
+            lane = lax.broadcasted_iota(jnp.int32, (quart, width), 1) + tile * width
+            diagonal = feature == lane
+            dcorr = jnp.where(diagonal, corr - 1.0, dcorr)
+            product = dcorr * corr
+            loss = jnp.where(diagonal, dcorr * dcorr, product)
+        dcorr_own[:, at] = dcorr.astype(jnp.bfloat16)
+        across = across + fold_lanes(product)
+        folded = fold_lanes(loss)
+        losses = losses + jnp.sum(folded.reshape(quart // 8, 8, 128), axis=0)
+        down.append(jnp.sum(product, axis=0, keepdims=True))
+
+        @pl.when(own_tile[0] == tile)
+        def _():
+            mine_own[...] = corr
+
+    second_a = vec_a[3:4, :] + jnp.concatenate(down, axis=1)
+    second_b = lanes_to_row(across)
+    total_loss = jnp.sum(losses, keepdims=True) + jnp.sum(vec_a[3:4, :], keepdims=True)
+    loss_out[...] = jnp.broadcast_to(total_loss, (8, 128))
+
+    for tile in (2, 3, 0, 1):
+        at = slice(tile * width, (tile + 1) * width)
+        terms = jnp.dot(
+            norm_b[:, :quart], dcorr_own[:, at], preferred_element_type=jnp.float32
+        ) + jnp.dot(norm_b[:, quart:], partner_dcorr[:, at], preferred_element_type=jnp.float32)
+        source = first_a if tile < 2 else first_other
+        inner = slice((tile % 2) * width, (tile % 2 + 1) * width)
+        xhat = (source[:, inner].astype(jnp.float32) - offset[:, at]) * rstd[:, at]
+        value = terms[:rows] - terms[rows : rows + 1] - xhat * second_a[:, at]
+        if tile < 2:
+            left_out[:, inner] = value
+        else:
+            left_partial_out[:, inner] = value.astype(jnp.bfloat16)
+
+    contract = (((1,), (1,)), ((), ()))
+    for tile in range(2):
+        at = slice(tile * width, (tile + 1) * width)
+        terms = lax.dot_general(
+            norms[...], dcorr_own[at, :], contract, preferred_element_type=jnp.float32
+        )
+        xhat = (first_b[:, at].astype(jnp.float32) - row_b[0:1, at]) * row_b[1:2, at]
+        right_out[:, at] = terms[:rows] - terms[rows : rows + 1] - xhat * second_b[:, at]
+
+    own_columns = jnp.transpose(mine_own[...])
+    partner_columns = jnp.transpose(partner_mine[...])
+
+    @pl.when(own_tile[1] == 0)
+    def _():
+        mine_out[:, :quart] = own_columns
+        mine_out[:, quart:] = partner_columns
+
+    @pl.when(own_tile[1] != 0)
+    def _():
+        mine_out[:, :quart] = partner_columns
+        mine_out[:, quart:] = own_columns
+
+
+vmem = pl.BlockSpec(memory_space=pltpu.VMEM)
+smem = pl.BlockSpec(memory_space=pltpu.SMEM)
+
+
+def local_call(kernel, scalars, operands, outs, scratch, flops):
+    moved = sum(x.size * x.dtype.itemsize for x in (*operands, *outs))
+    return pl.pallas_call(
+        kernel,
+        out_shape=outs,
+        in_specs=[smem] + [vmem] * len(operands),
+        out_specs=[vmem] * len(outs),
+        scratch_shapes=scratch,
+        compiler_params=pltpu.CompilerParams(vmem_limit_bytes=28 * 2**20),
+        cost_estimate=pl.CostEstimate(flops=flops, bytes_accessed=moved, transcendentals=0),
+    )(scalars, *operands)
+
+
+def gathered_device(left_outputs, right_outputs):
+    rows, quart = left_outputs.shape
+    half = 2 * quart
+    feats = 4 * quart
+    batch_images = rows * 4
+    tpos = lax.axis_index("tile")
+    dpos = lax.axis_index("dp")
+    row_halves = tpos // 2
+    column_halves = tpos % 2
+    at_end = (dpos == 0) | (dpos == 3)
+
+    pairs = [(0, 1), (1, 0), (2, 3), (3, 2)]
+    middle = [(1, 2), (2, 1)]
+    outward = [(1, 0), (2, 3)]
+
+    def along(block, route):
+        return lax.ppermute(block, "dp", route)
+
+    def core_swap(block):
+        return swapped(block, "tile", 0)
+
+    def x_swap(block):
+        return swapped(block, "tile", 1)
+
+    other_a0 = core_swap(left_outputs)
+    left_behind, other_a0 = lax.optimization_barrier((left_outputs, other_a0))
+
+    first_b = along(right_outputs, pairs)
+    inner_b = along(right_outputs, middle)
+    other_b0 = x_swap(right_outputs)
+    first_a = along(left_behind, pairs)
+    inner_a = along(left_behind, middle)
+
+    outer_b = along(inner_b, outward)
+    third_b = along(first_b, middle)
+    other_b1 = x_swap(first_b)
+    outer_a = along(inner_a, outward)
+    third_a = along(first_a, middle)
+    other_a1 = core_swap(first_a)
+
+    last_b = along(third_b, outward)
+    second_b = jnp.where(at_end, outer_b, inner_b)
+    other_b2 = x_swap(second_b)
+    third_a, other_b1, other_a1 = lax.optimization_barrier((third_a, other_b1, other_a1))
+    last_a = along(third_a, outward)
+    second_a = jnp.where(at_end, outer_a, inner_a)
+    other_a2 = core_swap(second_a)
+    late_b = jnp.where(at_end, last_b, third_b)
+    other_b3 = x_swap(late_b)
+
+    def paired(own, other):
+        return jnp.concatenate([own, other], axis=1).astype(jnp.float32)
+
+    raw_a = [paired(*p) for p in ((left_outputs, other_a0), (first_a, other_a1), (second_a, other_a2))]
+    raw_b = [
+        paired(*p)
+        for p in (
+            (right_outputs, other_b0),
+            (first_b, other_b1),
+            (second_b, other_b2),
+            (late_b, other_b3),
+        )
+    ]
+    shift_a = jnp.sum(raw_a[0], axis=0) / rows
+    shift_b = jnp.sum(raw_b[0], axis=0) / rows
+    centred_a = [x - shift_a for x in raw_a]
+    centred_b = [x - shift_b for x in raw_b]
+    low_a = [x.astype(jnp.bfloat16) for x in centred_a]
+    low_b = [x.astype(jnp.bfloat16) for x in centred_b]
+
+    def three_sums(centred, low):
+        return (
+            sum(jnp.sum(x, axis=0) for x in centred),
+            sum(jnp.sum(x * x, axis=0) for x in centred),
+            sum(jnp.sum(x.astype(jnp.float32), axis=0) for x in low),
+        )
+
+    prev = sum(
+        lax.dot_general(y, x, (((0,), (0,)), ((), ())), preferred_element_type=jnp.float32)
+        for x, y in zip(low_a, low_b)
+    )
+    sums_a = three_sums(centred_a, low_a)
+    sums_b = three_sums(centred_b, low_b)
+    delta_b = sums_b[0] / batch_images
+    rstd_b = lax.rsqrt(sums_b[1] / batch_images - delta_b * delta_b + 1e-05)
+    rest_b = (sums_b[2] / batch_images - delta_b) * rstd_b
+    norm_b = ((centred_b[0] - delta_b) * rstd_b).astype(jnp.bfloat16)
+    norm_b = jnp.concatenate(
+        [norm_b, jnp.broadcast_to(rest_b.astype(jnp.bfloat16), (16, half))], axis=0
+    )
+    late_low_b = low_b[3].T
+    col_b = jnp.stack([delta_b, rstd_b], axis=1)
+    row_b = jnp.stack([shift_b + delta_b, rstd_b] + [rest_b] * 6)
+    row_a = jnp.stack([shift_a, *sums_a] + [shift_a] * 4)
+
+    late_a = jnp.where(at_end, last_a, third_a)
+    (late_a, prev_own, prev_other, late_low_own, late_low_other, col_own, col_other, norm_b, norm_b_other, row_a, row_b) = (
+        lax.optimization_barrier(
+            (
+                late_a,
+                prev[:quart],
+                prev[quart:],
+                late_low_b[:quart],
+                late_low_b[quart:],
+                col_b[:quart],
+                col_b[quart:],
+                norm_b,
+                norm_b[:rows, quart:],
+                row_a,
+                row_b,
+            )
+        )
+    )
+    other_a3 = core_swap(late_a)
+
+    owned_tile = jnp.where(dpos // 2 == column_halves, 0, 2) + dpos % 2
+    scalars = jnp.stack([owned_tile, row_halves]).astype(jnp.int32)
+    quarter_f32 = jax.ShapeDtypeStruct((rows, quart), jnp.float32)
+    quarter_bf16 = jax.ShapeDtypeStruct((rows, quart), jnp.bfloat16)
+    width = half // 4
+    wide_low = pltpu.VMEM((rows, half), jnp.bfloat16)
+    wide_ext = pltpu.VMEM((rows + 16, half), jnp.bfloat16)
+    gemm = 2 * rows * half * quart
+    partial_right, dcorr_other, mine_other, vec_a = local_call(
+        functools.partial(partner_kernel, batch_images),
+        scalars,
+        (
+            late_a,
+            other_a3,
+            left_outputs,
+            other_a0,
+            row_a,
+            prev_other,
+            late_low_other,
+            col_other,
+            norm_b_other,
+        ),
+        (
+            quarter_bf16,
+            jax.ShapeDtypeStruct((quart, half), jnp.bfloat16),
+            jax.ShapeDtypeStruct((quart, width), jnp.float32),
+            jax.ShapeDtypeStruct((8, half), jnp.float32),
+        ),
+        [wide_low, wide_ext],
+        2 * gemm,
+    )
+    from_x = x_swap(partial_right)
+    right_own, left_own, partial_left, mine, part_loss = local_call(
+        functools.partial(own_kernel, batch_images),
+        scalars,
+        (
+            late_a,
+            other_a3,
+            left_outputs,
+            other_a0,
+            row_a,
+            prev_own,
+            late_low_own,
+            col_own,
+            norm_b,
+            right_outputs,
+            row_b,
+            dcorr_other,
+            mine_other,
+            vec_a,
+        ),
+        (
+            quarter_f32,
+            quarter_f32,
+            quarter_bf16,
+            jax.ShapeDtypeStruct((width, half), jnp.float32),
+            jax.ShapeDtypeStruct((8, 128), jnp.float32),
+        ),
+        [
+            wide_low,
+            wide_ext,
+            pltpu.VMEM((quart, half), jnp.bfloat16),
+            pltpu.VMEM((quart, width), jnp.float32),
+        ],
+        4 * gemm,
+    )
+    from_core = core_swap(partial_left)
+    loss = part_loss + core_swap(part_loss)
+    left_gradient = (vec_a[1, :quart] * (left_own + from_core.astype(jnp.float32))).astype(
+        jnp.bfloat16
+    )
+    loss, left_gradient, from_x = lax.optimization_barrier((loss, left_gradient, from_x))
+    loss = loss + x_swap(loss)
+    right_gradient = (row_b[1, :quart] * (right_own + from_x.astype(jnp.float32))).astype(
+        jnp.bfloat16
+    )
+    return (left_gradient, right_gradient, mine[None, :, :], loss[0, :1] / feats)
+
+
 def solution(mesh):
+    per_device = gathered_device if mesh.shape["dp"] == 4 else reduced_device
     return jax.shard_map(
         per_device,
         mesh=mesh,

time: 244 us -> 133 us (0.55)
  waiting for transfers between devices: 135 us -> 60.8 us
  blocking collectives: 65.4 us -> 0 us
  starting transfers between devices: 3.18 us -> 23.5 us
  local copies, waits for them, and re-layouts: 0.03 us -> 17.1 us
  between operations: 16 us -> 2.71 us
  Pallas kernels: 0 us -> 12.3 us
  matrix products: 10.5 us -> 5.86 us
  other arithmetic: 14 us -> 10.2 us
    reduce_scatter x1 -> x0, waiting for transfers between devices: 75 us -> none  [per_device(): lax.psum_scatter(lax.dot_general(picked, cols_b, (((0,), (0,)), ((), ()))...]
    psum x3 -> x0, blocking collectives: 65.4 us -> none  [the longest x1 43.2 us: per_device(): loss = lax.psum(part_loss, ('dp', 'tile')) / feats]
    all_gather x1 -> x0, waiting for transfers between devices: 46.6 us -> none  [per_device(): piece = lax.all_gather(dcorr_part, 'dp', axis=0, tiled=True)]
    ppermute x0 -> x10, waiting for transfers between devices: none -> 45.6 us  [along(): return lax.ppermute(block, 'dp', route)]
    ppermute x0 -> x10, starting transfers between devices: none -> 15.8 us  [along(): return lax.ppermute(block, 'dp', route)]
    pallas_call x0 -> x2, Pallas kernels: none -> 12.3 us  [local_call(): pl.pallas_call(kernel, out_shape=outs, in_specs=[smem] + [vmem] * len(ope...]
    slice x0 -> x6, local copies, waits for them, and re-layouts: none -> 7.19 us  [the longest x1 4.8 us: gathered_device(): prev[quart:]]
    optimization_barrier x0 -> x4, local copies, waits for them, and re-layouts: none -> 5.11 us  [gathered_device(): lax.optimization_barrier((late_a, prev[:quart], prev[quart:], late_low_b[...]
  transfers between devices with their start and end apart: 6 -> 22, of which waited for: 4 -> 9; matrix products, arithmetic and copies ran while one was open for 2% -> 20% of each run, Pallas kernels for 0% -> 0%
where the time goes in v3:
time: 133 us
  waiting for transfers between devices  60.8 us (46%)
  starting transfers between devices  23.5 us (18%)
  local copies, waits for them, and re-layouts  17.1 us (13%)
  Pallas kernels  12.3 us (9%)
  other arithmetic  10.2 us (8%)
  matrix products  5.86 us (4%)
  between operations  2.71 us (2%)
    ppermute x10, waiting for transfers between devices, along(): return lax.ppermute(block, 'dp', route)  45.6 us
    ppermute x10, starting transfers between devices, along(): return lax.ppermute(block, 'dp', route)  15.8 us
    ppermute x12, waiting for transfers between devices, swapped(): return lax.ppermute(block, axis, route)  15.3 us
    pallas_call x2, Pallas kernels, local_call(): pl.pallas_call(kernel, out_shape=outs, in_specs=[smem] + [vmem] * len(ope...  12.3 us
    ppermute x12, starting transfers between devices, swapped(): return lax.ppermute(block, axis, route)  7.76 us
    dot_general x3, matrix products, gathered_device(): lax.dot_general(y, x, (((0,), (0,)), ((), ())), preferred_element_type=jn...  5.86 us
    optimization_barrier x4, local copies, waits for them, and re-layouts, gathered_device(): lax.optimization_barrier((late_a, prev[:quart], prev[quart:], late_low_b[...  5.11 us
    slice x1, local copies, waits for them, and re-layouts, gathered_device(): prev[quart:]  4.8 us
  transfers between devices with their start and end apart: 22, of which 9 were waited for; matrix products, arithmetic and copies ran while one was open for 20% of the time, Pallas kernels for 0%

profile of v3, /device:TPU:0, one launch (start us, length us, event | category | flops | bytes accessed | tf_op | source)
XLA Modules:
  0.0 132.6 jit_solution(5746755441573550917)
XLA Ops:
  1.1 2.7 %collective-permute-start.3 = (bf16[512,512]{1,0:T(8,128)(2,1)}, bf16[512,512]{1,0:T(8,128)(2,1)S(1)}, u32[]{:S(2)}, u32[]{:S(2)}) collective-permute-start(bf16[512,512]{1,0:T(8,128)(2,1)} %first_b.1), channel_id=1, source_target_pairs={{0,4},{4,0},{8,12},{12,8},{1,5},{5,1},{9,13},{13,9},{2,6},{6,2},{1... | collective-permute-start | bytes 1572872 | tf_op jit(solution)/shard_map/ppermute | solution.py:408
  3.8 1.5 %collective-permute-start.7 = (bf16[512,512]{1,0:T(8,128)(2,1)}, bf16[512,512]{1,0:T(8,128)(2,1)S(1)}, u32[]{:S(2)}, u32[]{:S(2)}) collective-permute-start(bf16[512,512]{1,0:T(8,128)(2,1)} %first_b.1), channel_id=1, source_target_pairs={{0,2},{2,0},{1,3},{3,1},{4,6},{6,4},{5,7},{7,5},{8,10},{10,8},{9,1... | collective-permute-start | bytes 1572872 | tf_op jit(solution)/shard_map/ppermute | solution.py:19
  5.3 1.4 %collective-permute-start.8 = (bf16[512,512]{1,0:T(8,128)(2,1)}, bf16[512,512]{1,0:T(8,128)(2,1)}, u32[]{:S(2)}, u32[]{:S(2)}) collective-permute-start(bf16[512,512]{1,0:T(8,128)(2,1)} %first_b.1), channel_id=1, source_target_pairs={{4,8},{8,4},{5,9},{9,5},{6,10},{10,6},{7,11},{11,7},{20,24},{24,20... | collective-permute-start | bytes 1572872 | tf_op jit(solution)/shard_map/ppermute | solution.py:408
  6.7 3.7 %collective-permute-start.1 = (bf16[512,512]{1,0:T(8,128)(2,1)}, bf16[512,512]{1,0:T(8,128)(2,1)S(1)}, u32[]{:S(2)}, u32[]{:S(2)}) collective-permute-start(bf16[512,512]{1,0:T(8,128)(2,1)} %first_a.3), channel_id=1, source_target_pairs={{0,4},{4,0},{8,12},{12,8},{1,5},{5,1},{9,13},{13,9},{2,6},{6,2},{1... | collective-permute-start | bytes 1572872 | tf_op jit(solution)/shard_map/ppermute | solution.py:408
  11.1 5.7 %collective-permute-done.3 = bf16[512,512]{1,0:T(8,128)(2,1)S(1)} collective-permute-done((bf16[512,512]{1,0:T(8,128)(2,1)}, bf16[512,512]{1,0:T(8,128)(2,1)S(1)}, u32[]{:S(2)}, u32[]{:S(2)}) %collective-permute-start.3) | collective-permute-done | bytes 524320 | tf_op jit(solution)/shard_map/ppermute | solution.py:408
  18.0 1.5 %collective-permute-start.4 = (bf16[512,512]{1,0:T(8,128)(2,1)S(1)}, bf16[512,512]{1,0:T(8,128)(2,1)S(1)}, u32[]{:S(2)}, u32[]{:S(2)}) collective-permute-start(bf16[512,512]{1,0:T(8,128)(2,1)S(1)} %collective-permute-done.3), channel_id=1, source_target_pairs={{0,2},{2,0},{1,3},{3,1},{4,6},{6,4},{5,7},{7,5},{8,10},{10,8},{9,1... | collective-permute-start | bytes 1572872 | tf_op jit(solution)/shard_map/ppermute | solution.py:19
  19.5 1.3 collective-permute-start.9
  20.8 1.2 convert_reduce_fusion.1
  22.0 6.0 %collective-permute-done.1 = bf16[512,512]{1,0:T(8,128)(2,1)S(1)} collective-permute-done((bf16[512,512]{1,0:T(8,128)(2,1)}, bf16[512,512]{1,0:T(8,128)(2,1)S(1)}, u32[]{:S(2)}, u32[]{:S(2)}) %collective-permute-start.1) | collective-permute-done | bytes 524320 | tf_op jit(solution)/shard_map/ppermute | solution.py:408
  28.0 1.5 %collective-permute-start.2 = (bf16[512,512]{1,0:T(8,128)(2,1)S(1)}, bf16[512,512]{1,0:T(8,128)(2,1)}, u32[]{:S(2)}, u32[]{:S(2)}) collective-permute-start(bf16[512,512]{1,0:T(8,128)(2,1)S(1)} %collective-permute-done.1), channel_id=1, source_target_pairs={{4,8},{8,4},{5,9},{9,5},{6,10},{10,6},{7,11},{11,7},{20,24},{24,20... | collective-permute-start | bytes 1572872 | tf_op jit(solution)/shard_map/ppermute | solution.py:408
  29.6 1.3 collective-permute-start.15
  30.9 1.2 convert_reduce_fusion
  32.1 6.9 %collective-permute-done.9 = bf16[512,512]{1,0:T(8,128)(2,1)S(1)} collective-permute-done((bf16[512,512]{1,0:T(8,128)(2,1)}, bf16[512,512]{1,0:T(8,128)(2,1)S(1)}, u32[]{:S(2)}, u32[]{:S(2)}) %collective-permute-start.9) | collective-permute-done | bytes 524320 | tf_op jit(solution)/shard_map/ppermute | solution.py:408
  39.0 1.3 collective-permute-start.12
  40.4 1.7 %collective-permute-start.10 = (bf16[512,512]{1,0:T(8,128)(2,1)S(1)}, bf16[512,512]{1,0:T(8,128)(2,1)S(1)}, u32[]{:S(2)}, u32[]{:S(2)}) collective-permute-start(bf16[512,512]{1,0:T(8,128)(2,1)S(1)} %broadcast_select_fusion.2), channel_id=1, source_target_pairs={{0,2},{2,0},{1,3},{3,1},{4,6},{6,4},{5,7},{7,5},{8,10},{10,8},{9,1... | collective-permute-start | bytes 1572872 | tf_op jit(solution)/shard_map/ppermute | solution.py:19
  42.1 1.3 collective-permute-start.6
  43.4 16.4 %collective-permute-done.15 = bf16[512,512]{1,0:T(8,128)(2,1)S(1)} collective-permute-done((bf16[512,512]{1,0:T(8,128)(2,1)S(1)}, bf16[512,512]{1,0:T(8,128)(2,1)S(1)}, u32[]{:S(2)}, u32[]{:S(2)}) %collective-permute-start.15) | collective-permute-done | bytes 524320 | tf_op jit(solution)/shard_map/ppermute | solution.py:408
  60.5 10.6 %collective-permute-done.12 = bf16[512,512]{1,0:T(8,128)(2,1)S(1)} collective-permute-done((bf16[512,512]{1,0:T(8,128)(2,1)S(1)}, bf16[512,512]{1,0:T(8,128)(2,1)S(1)}, u32[]{:S(2)}, u32[]{:S(2)}) %collective-permute-start.12) | collective-permute-done | bytes 524320 | tf_op jit(solution)/shard_map/ppermute | solution.py:408
  71.3 1.3 fusion.21
  72.6 1.6 %convert_reduce_fusion.8 = (f32[1024]{0:T(1024)S(1)}, f32[1024]{0:T(1024)S(1)}, f32[1024]{0:T(1024)S(1)}, bf16[1024,512]{0,1:T(8,128)(2,1)S(1)}, f32[1024]{0:T(1...) fusion(f32[1024]{0:T(1024)S(1)} %broadcast_multiply_fusion.1, ...), kind=kLoop, calls=%fused_computation.24 | loop fusion | flops 23056384 | bytes 5296128 | tf_op jit(solution)/shard_map/reduce_sum | solution.py:466
  76.5 1.3 fusion.24
  78.1 3.3 %add_add_fusion = f32[1024,1024]{1,0:T(8,128)} fusion(f32[1024,1024]{1,0:T(8,128)S(1)} %fusion.24, f32[1024,1024]{1,0:T(8,128)S(1)} %fusion.21, f32[1024]{0:T(1024)S(1)} %broadcast_multiply_fusion.1, f32[1024]{0:T(1024)S(1)} %broadcast_multiply_fusion, bf16[512,512]{1,0:T(8,128)(2,1)S(1)} %collective-permute-done.first_other, ...), kind=kOutput, calls=%fused_computation | convolution fusion | flops 1082130432 | bytes 14688256 | tf_op jit(solution)/shard_map/dot_general | solution.py:470
  83.4 1.3 pad_maximum_fusion.norm_b
  84.7 4.8 %fusion.32 = (f32[512,1024]{1,0:T(8,128)}, f32[512,1024]{1,0:T(8,128)}) fusion(f32[1024,1024]{1,0:T(8,128)} %add_add_fusion), kind=kLoop, calls=%fused_computation.77 | loop fusion | bytes 8388608 | tf_op jit(solution)/shard_map/slice | solution.py:493
  91.2 2.0 %copy.17.late_b = bf16[512,512]{1,0:T(8,128)(2,1)} copy(bf16[512,512]{0,1:T(8,128)(2,1)} %get-tuple-element.40) | data formatting | bytes 1048576 | tf_op jit(solution)/shard_map/optimization_barrier | solution.py:489
  93.3 2.0 %copy.16.late_b = bf16[512,512]{1,0:T(8,128)(2,1)} copy(bf16[512,512]{0,1:T(8,128)(2,1)} %get-tuple-element.45) | data formatting | bytes 1048576 | tf_op jit(solution)/shard_map/optimization_barrier | solution.py:489
  95.3 1.6 %copy-done.2 = f32[512,1024]{1,0:T(8,128)S(1)} copy-done((f32[512,1024]{1,0:T(8,128)S(1)}, f32[512,1024]{1,0:T(8,128)}, u32[]{:S(2)}) %copy-start.2) | copy-done | bytes 2097176
  100.0 5.1 %shard_map.57 = (bf16[512,512]{1,0:T(8,128)(2,1)S(1)}, bf16[512,1024]{1,0:T(8,128)(2,1)S(1)}, f32[512,256]{1,0:T(8,128)S(1)}, f32[8,1024]{1,0:T(8,128)S(1)}) custom-call(s32[2]{0:T(128)S(1)} %pad_add_fusion.own_tile, bf16[512,512]{1,0:T(8,128)(2,1)S(1)} %broadcast_select_fusion.3.late_a, bf16[512,512]{1,0:T(8,128)(2,1)} %collective-permute-done.17.late_other, ...), custom_call_target="tpu_custom_call" | custom-call | flops 1073741824 | bytes 7409664 | tf_op jit(solution)/shard_map/pallas_call | solution.py:381
  105.1 7.2 %shard_map.58 = (f32[512,512]{1,0:T(8,128)S(1)}, f32[512,512]{1,0:T(8,128)S(1)}, bf16[512,512]{1,0:T(8,128)(2,1)S(1)}, f32[256,1024]{1,0:T(8,128)}, f32[8,128]{1,0:T(8,128)S(1)}) custom-call(s32[2]{0:T(128)S(1)} %pad_add_fusion.own_tile, bf16[512,512]{1,0:T(8,128)(2,1)S(1)} %broadcast_select_fusion.3.late_a, ...), custom_call_target="tpu_custom_call" | custom-call | flops 2147483648 | bytes 11673600 | tf_op jit(solution)/shard_map/pallas_call | solution.py:381
  113.1 1.1 collective-permute-done.18
  115.2 11.4 %collective-permute-done.20 = bf16[512,512]{1,0:T(8,128)(2,1)S(1)} collective-permute-done((bf16[512,512]{1,0:T(8,128)(2,1)S(1)}, bf16[512,512]{1,0:T(8,128)(2,1)S(1)}, u32[]{:S(2)}, u32[]{:S(2)}) %collective-permute-start.20) | collective-permute-done | bytes 524320 | tf_op jit(solution)/shard_map/ppermute | solution.py:19
  128.2 2.1 %collective-permute-done.21 = f32[8,128]{1,0:T(8,128)S(1)} collective-permute-done((f32[8,128]{1,0:T(8,128)S(1)}, f32[8,128]{1,0:T(8,128)S(1)}, u32[]{:S(2)}, u32[]{:S(2)}) %collective-permute-start.21) | collective-permute-done | bytes 4128 | tf_op jit(solution)/shard_map/ppermute | solution.py:19
  (74 shorter events, 16.4 us)
Async XLA Ops:
  0.6 6.1 %collective-permute-start = (bf16[512,512]{1,0:T(8,128)(2,1)}, bf16[512,512]{1,0:T(8,128)(2,1)S(1)}, u32[]{:S(2)}, u32[]{:S(2)}) collective-permute-start(bf16[512,512]{1,0:T(8,128)(2,1)} %first_a.3), channel_id=1, source_target_pairs={{0,1},{1,0},{2,3},{3,2},{4,5},{5,4},{6,7},{7,6},{8,9},{9,8},{10,11... | collective-permute-start | bytes 1572872 | tf_op jit(solution)/shard_map/ppermute | solution.py:19
  1.1 15.6 %collective-permute-start.3 = (bf16[512,512]{1,0:T(8,128)(2,1)}, bf16[512,512]{1,0:T(8,128)(2,1)S(1)}, u32[]{:S(2)}, u32[]{:S(2)}) collective-permute-start(bf16[512,512]{1,0:T(8,128)(2,1)} %first_b.1), channel_id=1, source_target_pairs={{0,4},{4,0},{8,12},{12,8},{1,5},{5,1},{9,13},{13,9},{2,6},{6,2},{1... | collective-permute-start | bytes 1572872 | tf_op jit(solution)/shard_map/ppermute | solution.py:408
  3.8 14.2 %collective-permute-start.7 = (bf16[512,512]{1,0:T(8,128)(2,1)}, bf16[512,512]{1,0:T(8,128)(2,1)S(1)}, u32[]{:S(2)}, u32[]{:S(2)}) collective-permute-start(bf16[512,512]{1,0:T(8,128)(2,1)} %first_b.1), channel_id=1, source_target_pairs={{0,2},{2,0},{1,3},{3,1},{4,6},{6,4},{5,7},{7,5},{8,10},{10,8},{9,1... | collective-permute-start | bytes 1572872 | tf_op jit(solution)/shard_map/ppermute | solution.py:19
  5.3 14.2 %collective-permute-start.8 = (bf16[512,512]{1,0:T(8,128)(2,1)}, bf16[512,512]{1,0:T(8,128)(2,1)}, u32[]{:S(2)}, u32[]{:S(2)}) collective-permute-start(bf16[512,512]{1,0:T(8,128)(2,1)} %first_b.1), channel_id=1, source_target_pairs={{4,8},{8,4},{5,9},{9,5},{6,10},{10,6},{7,11},{11,7},{20,24},{24,20... | collective-permute-start | bytes 1572872 | tf_op jit(solution)/shard_map/ppermute | solution.py:408
  6.7 21.3 %collective-permute-start.1 = (bf16[512,512]{1,0:T(8,128)(2,1)}, bf16[512,512]{1,0:T(8,128)(2,1)S(1)}, u32[]{:S(2)}, u32[]{:S(2)}) collective-permute-start(bf16[512,512]{1,0:T(8,128)(2,1)} %first_a.3), channel_id=1, source_target_pairs={{0,4},{4,0},{8,12},{12,8},{1,5},{5,1},{9,13},{13,9},{2,6},{6,2},{1... | collective-permute-start | bytes 1572872 | tf_op jit(solution)/shard_map/ppermute | solution.py:408
  10.4 19.1 %collective-permute-start.11 = (bf16[512,512]{1,0:T(8,128)(2,1)}, bf16[512,512]{1,0:T(8,128)(2,1)S(1)}, u32[]{:S(2)}, u32[]{:S(2)}) collective-permute-start(bf16[512,512]{1,0:T(8,128)(2,1)} %first_a.3), channel_id=1, source_target_pairs={{4,8},{8,4},{5,9},{9,5},{6,10},{10,6},{7,11},{11,7},{20,24},{24,20... | collective-permute-start | bytes 1572872 | tf_op jit(solution)/shard_map/ppermute | solution.py:408
  16.8 12.7 %collective-permute-start.14 = (bf16[512,512]{1,0:T(8,128)(2,1)S(1)}, bf16[512,512]{1,0:T(8,128)(2,1)S(1)}, u32[]{:S(2)}, u32[]{:S(2)}) collective-permute-start(bf16[512,512]{1,0:T(8,128)(2,1)S(1)} %collective-permute-done.3), channel_id=1, source_target_pairs={{4,8},{8,4},{5,9},{9,5},{6,10},{10,6},{7,11},{11,7},{20,24},{24,20... | collective-permute-start | bytes 1572872 | tf_op jit(solution)/shard_map/ppermute | solution.py:408
  18.0 22.4 %collective-permute-start.4 = (bf16[512,512]{1,0:T(8,128)(2,1)S(1)}, bf16[512,512]{1,0:T(8,128)(2,1)S(1)}, u32[]{:S(2)}, u32[]{:S(2)}) collective-permute-start(bf16[512,512]{1,0:T(8,128)(2,1)S(1)} %collective-permute-done.3), channel_id=1, source_target_pairs={{0,2},{2,0},{1,3},{3,1},{4,6},{6,4},{5,7},{7,5},{8,10},{10,8},{9,1... | collective-permute-start | bytes 1572872 | tf_op jit(solution)/shard_map/ppermute | solution.py:19
  19.5 19.5 %collective-permute-start.9 = (bf16[512,512]{1,0:T(8,128)(2,1)}, bf16[512,512]{1,0:T(8,128)(2,1)S(1)}, u32[]{:S(2)}, u32[]{:S(2)}) collective-permute-start(bf16[512,512]{1,0:T(8,128)(2,1)} %collective-permute-done.8), channel_id=1, source_target_pairs={{4,0},{8,12},{5,1},{9,13},{6,2},{10,14},{7,3},{11,15},{20,16},{24,... | collective-permute-start | bytes 1572872 | tf_op jit(solution)/shard_map/ppermute | solution.py:408
  28.0 14.1 %collective-permute-start.2 = (bf16[512,512]{1,0:T(8,128)(2,1)S(1)}, bf16[512,512]{1,0:T(8,128)(2,1)}, u32[]{:S(2)}, u32[]{:S(2)}) collective-permute-start(bf16[512,512]{1,0:T(8,128)(2,1)S(1)} %collective-permute-done.1), channel_id=1, source_target_pairs={{4,8},{8,4},{5,9},{9,5},{6,10},{10,6},{7,11},{11,7},{20,24},{24,20... | collective-permute-start | bytes 1572872 | tf_op jit(solution)/shard_map/ppermute | solution.py:408
  29.5 12.6 %collective-permute-start.5 = (bf16[512,512]{1,0:T(8,128)(2,1)S(1)}, bf16[512,512]{1,0:T(8,128)(2,1)S(1)}, u32[]{:S(2)}, u32[]{:S(2)}) collective-permute-start(bf16[512,512]{1,0:T(8,128)(2,1)S(1)} %collective-permute-done.1), channel_id=1, source_target_pairs={{0,1},{1,0},{2,3},{3,2},{4,5},{5,4},{6,7},{7,6},{8,9},{9,8},{10,11... | collective-permute-start | bytes 1572872 | tf_op jit(solution)/shard_map/ppermute | solution.py:19
  29.5 13.9 %copy-start.9 = (bf16[512,512]{1,0:T(8,128)(2,1)}, bf16[512,512]{1,0:T(8,128)(2,1)S(1)}, u32[]{:S(2)}) copy-start(bf16[512,512]{1,0:T(8,128)(2,1)S(1)} %collective-permute-done.14) | copy-start | bytes 1572868
  29.6 30.3 %collective-permute-start.15 = (bf16[512,512]{1,0:T(8,128)(2,1)S(1)}, bf16[512,512]{1,0:T(8,128)(2,1)S(1)}, u32[]{:S(2)}, u32[]{:S(2)}) collective-permute-start(bf16[512,512]{1,0:T(8,128)(2,1)S(1)} %collective-permute-done.14), channel_id=1, source_target_pairs={{4,0},{8,12},{5,1},{9,13},{6,2},{10,14},{7,3},{11,15},{20,16},{24,... | collective-permute-start | bytes 1572872 | tf_op jit(solution)/shard_map/ppermute | solution.py:408
  39.0 32.1 %collective-permute-start.12 = (bf16[512,512]{1,0:T(8,128)(2,1)S(1)}, bf16[512,512]{1,0:T(8,128)(2,1)S(1)}, u32[]{:S(2)}, u32[]{:S(2)}) collective-permute-start(bf16[512,512]{1,0:T(8,128)(2,1)S(1)} %collective-permute-done.11), channel_id=1, source_target_pairs={{4,0},{8,12},{5,1},{9,13},{6,2},{10,14},{7,3},{11,15},{20,16},{24,... | collective-permute-start | bytes 1572872 | tf_op jit(solution)/shard_map/ppermute | solution.py:408
  40.4 32.2 %collective-permute-start.10 = (bf16[512,512]{1,0:T(8,128)(2,1)S(1)}, bf16[512,512]{1,0:T(8,128)(2,1)S(1)}, u32[]{:S(2)}, u32[]{:S(2)}) collective-permute-start(bf16[512,512]{1,0:T(8,128)(2,1)S(1)} %broadcast_select_fusion.2), channel_id=1, source_target_pairs={{0,2},{2,0},{1,3},{3,1},{4,6},{6,4},{5,7},{7,5},{8,10},{10,8},{9,1... | collective-permute-start | bytes 1572872 | tf_op jit(solution)/shard_map/ppermute | solution.py:19
  42.1 47.4 %collective-permute-start.6 = (bf16[512,512]{1,0:T(8,128)(2,1)}, bf16[512,512]{1,0:T(8,128)(2,1)}, u32[]{:S(2)}, u32[]{:S(2)}) collective-permute-start(bf16[512,512]{1,0:T(8,128)(2,1)} %collective-permute-done.2), channel_id=1, source_target_pairs={{4,0},{8,12},{5,1},{9,13},{6,2},{10,14},{7,3},{11,15},{20,16},{24,... | collective-permute-start | bytes 1572872 | tf_op jit(solution)/shard_map/ppermute | solution.py:408
  59.9 12.6 %collective-permute-start.16 = (bf16[512,512]{1,0:T(8,128)(2,1)S(1)}, bf16[512,512]{1,0:T(8,128)(2,1)S(1)}, u32[]{:S(2)}, u32[]{:S(2)}) collective-permute-start(bf16[512,512]{1,0:T(8,128)(2,1)S(1)} %broadcast_select_fusion), channel_id=1, source_target_pairs={{0,2},{2,0},{1,3},{3,1},{4,6},{6,4},{5,7},{7,5},{8,10},{10,8},{9,1... | collective-permute-start | bytes 1572872 | tf_op jit(solution)/shard_map/ppermute | solution.py:19
  71.2 1.4 %copy-start.1 = (bf16[512,512]{1,0:T(8,128)(2,1)S(1)}, bf16[512,512]{1,0:T(8,128)(2,1)}, u32[]{:S(2)}) copy-start(bf16[512,512]{1,0:T(8,128)(2,1)} %first_b.1) | copy-start | bytes 1572868
  71.2 4.1 %collective-permute-start.13 = (bf16[512,512]{1,0:T(8,128)(2,1)S(1)}, bf16[512,512]{1,0:T(8,128)(2,1)S(1)}, u32[]{:S(2)}, u32[]{:S(2)}) collective-permute-start(bf16[512,512]{1,0:T(8,128)(2,1)S(1)} %broadcast_select_fusion.1), channel_id=1, source_target_pairs={{0,1},{1,0},{2,3},{3,2},{4,5},{5,4},{6,7},{7,6},{8,9},{9,8},{10,11... | collective-permute-start | bytes 1572872 | tf_op jit(solution)/shard_map/ppermute | solution.py:19
  74.2 1.1 copy-start
  78.1 4.3 %copy-start.8 = (bf16[512,1024]{1,0:T(8,128)(2,1)}, bf16[512,1024]{1,0:T(8,128)(2,1)S(1)}, u32[]{:S(2)}) copy-start(bf16[512,1024]{1,0:T(8,128)(2,1)S(1)} %fusion.9) | copy-start | bytes 3145732
  90.6 4.7 %collective-permute-start.17 = (bf16[512,512]{1,0:T(8,128)(2,1)S(1)}, bf16[512,512]{1,0:T(8,128)(2,1)}, u32[]{:S(2)}, u32[]{:S(2)}) collective-permute-start(bf16[512,512]{1,0:T(8,128)(2,1)S(1)} %broadcast_select_fusion.3.late_a), channel_id=1, source_target_pairs={{0,1},{1,0},{2,3},{3,2},{4,5},{5,4},{6,7},{7,6},{8,9},{9,8},{10,11... | collective-permute-start | bytes 1572872 | tf_op jit(solution)/shard_map/ppermute | solution.py:19
  95.3 1.6 %copy-start.2 = (f32[512,1024]{1,0:T(8,128)S(1)}, f32[512,1024]{1,0:T(8,128)}, u32[]{:S(2)}) copy-start(f32[512,1024]{1,0:T(8,128)} %get-tuple-element.44.prev) | copy-start | bytes 6291460
  96.9 1.0 copy-start.4
  98.0 1.0 copy-start.6
  99.0 0.9 copy-start.7
  100.0 5.1 %copy-start.3 = (f32[512,1024]{1,0:T(8,128)S(1)}, f32[512,1024]{1,0:T(8,128)}, u32[]{:S(2)}) copy-start(f32[512,1024]{1,0:T(8,128)} %get-tuple-element.39.prev) | copy-start | bytes 6291460
  100.0 5.1 %copy-start.5 = (bf16[512,512]{1,0:T(8,128)(2,1)S(1)}, bf16[512,512]{1,0:T(8,128)(2,1)}, u32[]{:S(2)}) copy-start(bf16[512,512]{1,0:T(8,128)(2,1)} %copy.17.late_b) | copy-start | bytes 1572868
  112.3 1.9 %collective-permute-start.19 = (bf16[512,512]{1,0:T(8,128)(2,1)S(1)}, bf16[512,512]{1,0:T(8,128)(2,1)S(1)}, u32[]{:S(2)}, u32[]{:S(2)}) collective-permute-start(bf16[512,512]{1,0:T(8,128)(2,1)S(1)} %get-tuple-element.53), channel_id=1, source_target_pairs={{0,1},{1,0},{2,3},{3,2},{4,5},{5,4},{6,7},{7,6},{8,9},{9,8},{10,11... | collective-permute-start | bytes 1572872 | tf_op jit(solution)/shard_map/ppermute | solution.py:19
  112.4 14.3 %collective-permute-start.20 = (bf16[512,512]{1,0:T(8,128)(2,1)S(1)}, bf16[512,512]{1,0:T(8,128)(2,1)S(1)}, u32[]{:S(2)}, u32[]{:S(2)}) collective-permute-start(bf16[512,512]{1,0:T(8,128)(2,1)S(1)} %get-tuple-element.54), channel_id=1, source_target_pairs={{0,2},{2,0},{1,3},{3,1},{4,6},{6,4},{5,7},{7,5},{8,10},{10,8},{9,1... | collective-permute-start | bytes 1572872 | tf_op jit(solution)/shard_map/ppermute | solution.py:19
  112.9 1.3 %collective-permute-start.18 = (f32[8,128]{1,0:T(8,128)S(1)}, f32[8,128]{1,0:T(8,128)S(1)}, u32[]{:S(2)}, u32[]{:S(2)}) collective-permute-start(f32[8,128]{1,0:T(8,128)S(1)} %get-tuple-element.51), channel_id=1, source_target_pairs={{0,1},{1,0},{2,3},{3,2},{4,5},{5,4},{6,7},{7,6},{8,9},{9,8},{10,11... | collective-permute-start | bytes 12296 | tf_op jit(solution)/shard_map/ppermute | solution.py:19
  126.7 3.6 %collective-permute-start.21 = (f32[8,128]{1,0:T(8,128)S(1)}, f32[8,128]{1,0:T(8,128)S(1)}, u32[]{:S(2)}, u32[]{:S(2)}) collective-permute-start(f32[8,128]{1,0:T(8,128)S(1)} %add.385), channel_id=1, source_target_pairs={{0,2},{2,0},{1,3},{3,1},{4,6},{6,4},{5,7},{7,5},{8,10},{10,8},{9,1... | collective-permute-start | bytes 12296 | tf_op jit(solution)/shard_map/ppermute | solution.py:19

commit v4 on v3

--- a/solution.py
+++ b/solution.py
@@ -176,104 +176,138 @@
     return row[:1, :]
 
 
+def three_parts(row):
+    high = row.astype(jnp.bfloat16)
+    rest = row - high.astype(jnp.float32)
+    middle = rest.astype(jnp.bfloat16)
+    low = (rest - middle.astype(jnp.float32)).astype(jnp.bfloat16)
+    return [high, middle, low]
+
+
+def joined_parts(ref, at):
+    parts = ref[at : at + 16, :].astype(jnp.float32)
+    return [parts[3 * i : 3 * i + 1] + parts[3 * i + 1 : 3 * i + 2] + parts[3 * i + 2 : 3 * i + 3] for i in range(4)]
+
+
+def moments(sums, images):
+    total, squares, rounded = sums
+    delta = total / images
+    rstd = lax.rsqrt(squares / images - delta * delta + 1e-05)
+    return delta, rstd, (rounded / images - delta) * rstd
+
+
 def fold_lanes(values):
     width = values.shape[1]
     return sum(values[:, at : at + 128] for at in range(0, width, 128))
 
 
-def partner_kernel(
-    images,
-    own_tile,
-    late_a,
-    late_other,
-    first_a,
-    first_other,
-    row_a,
-    prev,
-    late_b,
-    col_b,
-    norm_b,
-    partial_out,
-    dcorr_out,
-    mine_out,
-    vec_out,
-    centred,
-    norms,
-):
-    rows, quart = late_a.shape
-    half = 2 * quart
+def late_right_kernel(images, late, row, out, stats):
+    rows, quart = late.shape
+    shift = row[0:1, :]
+    zero = jnp.zeros((8, quart), jnp.float32)
+    sums = [zero, zero, zero]
+    fold = lambda v: jnp.sum(v.reshape(v.shape[0] // 8, 8, quart), axis=0)
+    for at in range(0, rows, 128):
+        centred = late[at : at + 128, :].astype(jnp.float32) - shift
+        low = centred.astype(jnp.bfloat16)
+        out[:quart, at : at + 128] = jnp.transpose(low)
+        sums = [
+            sums[0] + fold(centred),
+            sums[1] + fold(centred * centred),
+            sums[2] + fold(low.astype(jnp.float32)),
+        ]
+    sums = [row[i + 1 : i + 2, :] + jnp.sum(s, axis=0, keepdims=True) for i, s in enumerate(sums)]
+    delta, rstd, rest = moments(sums, images)
+    values = [shift + delta, rstd, rest, delta]
+    stats[...] = jnp.concatenate(values + [jnp.zeros((4, quart), jnp.float32)], axis=0)
+    parts = sum([three_parts(v) for v in values], [])
+    parts = [p.astype(jnp.float32) for p in parts] + [jnp.zeros((4, quart), jnp.float32)]
+    out[quart:, :] = jnp.concatenate(parts, axis=0).astype(jnp.bfloat16)
+
+
+def partner_kernel(images, part, own_tile, late, first, row, sums_all, late_b, first_b, *refs):
+    if part:
+        (terms_in, across_in, partial_out, dcorr_out, mine_out, vec_out, centred, norms) = refs
+    else:
+        (terms_out, across_out, dcorr_out, mine_out, vec_out, centred, norms) = refs
+    rows, quart = late.shape
     inverse = 1.0 / images
-    shift = row_a[0:1, :]
-    own = centre_rows(late_a, shift[:, :quart], centred, slice(0, quart), 64)
-    other = centre_rows(late_other, shift[:, quart:], centred, slice(quart, half), 64)
-    total, squares, rounded = [
-        row_a[i + 1 : i + 2, :] + jnp.concatenate([own[i], other[i]], axis=1) for i in range(3)
-    ]
-    delta = total * inverse
-    rstd = lax.rsqrt(squares * inverse - delta * delta + 1e-05)
-    rest = (rounded * inverse - delta) * rstd
-    offset = shift + delta
-    normalise_rows(first_a, offset[:, :quart], rstd[:, :quart], norms, slice(0, quart), 64)
-    normalise_rows(first_other, offset[:, quart:], rstd[:, quart:], norms, slice(quart, half), 64)
-    norms[rows : rows + 16, :] = jnp.broadcast_to(rest, (16, half)).astype(jnp.bfloat16)
-
-    delta_col = col_b[:, 0:1]
-    rstd_col = col_b[:, 1:2]
-    width = half // 4
-    across = jnp.zeros((quart, 128), jnp.float32)
-    down = []
-    for tile in range(4):
+    shift = row[0:1, :]
+    everything = slice(0, quart)
+    sums = centre_rows(late, shift, centred, everything, 64)
+    delta, rstd, rest = moments([row[i + 1 : i + 2, :] + sums[i] for i in range(3)], images)
+    normalise_rows(first, shift + delta, rstd, norms, everything, 64)
+    norms[rows : rows + 16, :] = jnp.broadcast_to(rest, (16, quart)).astype(jnp.bfloat16)
+
+    offset_b, rstd_b, _, delta_b = joined_parts(late_b, quart)
+    columns = jnp.transpose(
+        jnp.concatenate([delta_b, rstd_b, jnp.zeros((6, quart), jnp.float32)], axis=0)
+    )
+    delta_col = columns[:, 0:1]
+    rstd_col = columns[:, 1:2]
+    width = quart // 2
+    across = across_in[...] if part else jnp.zeros((quart, 128), jnp.float32)
+    for tile in range(2):
         at = slice(tile * width, (tile + 1) * width)
-        sums = prev[:, at] + jnp.dot(
-            late_b[...], centred[:, at], preferred_element_type=jnp.float32
+        wide = slice(part * quart + tile * width, part * quart + (tile + 1) * width)
+        sums = sums_all[quart:, wide] + jnp.dot(
+            late_b[:quart, :], centred[:, at], preferred_element_type=jnp.float32
         )
         corr = tile_scaled(sums, delta_col, rstd_col, delta[:, at], rstd[:, at], inverse)
         dcorr = off_weight * corr
         dcorr_out[:, at] = dcorr.astype(jnp.bfloat16)
         product = dcorr * corr
         across = across + fold_lanes(product)
-        down.append(jnp.sum(product, axis=0, keepdims=True))
-
-        @pl.when(own_tile[0] == tile)
+        vec_out[3:4, at] = jnp.sum(product, axis=0, keepdims=True)
+
+        @pl.when(own_tile[0] == 2 * part + tile)
         def _():
             mine_out[...] = corr
 
     vec_out[0:1, :] = delta
     vec_out[1:2, :] = rstd
     vec_out[2:3, :] = rest
-    vec_out[3:4, :] = jnp.concatenate(down, axis=1)
-    vec_out[4:8, :] = jnp.zeros((4, half), jnp.float32)
-    second = lanes_to_row(across)
+    vec_out[4:8, :] = jnp.zeros((4, quart), jnp.float32)
     contract = (((1,), (1,)), ((), ()))
+    if part:
+        second = lanes_to_row(across)
+    else:
+        across_out[...] = across
     for tile in range(2):
         at = slice(tile * width, (tile + 1) * width)
         terms = lax.dot_general(
             norms[...], dcorr_out[at, :], contract, preferred_element_type=jnp.float32
         )
-        partial_out[:, at] = (
-            terms[:rows]
-            - terms[rows : rows + 1]
-            - norm_b[:, at].astype(jnp.float32) * second[:, at]
-        ).astype(jnp.bfloat16)
+        if part:
+            terms = terms + terms_in[:, at]
+            xhat = (first_b[:, at].astype(jnp.float32) - offset_b[:, at]) * rstd_b[:, at]
+            partial_out[:, at] = (
+                terms[:rows] - terms[rows : rows + 1] - xhat * second[:, at]
+            ).astype(jnp.bfloat16)
+        else:
+            terms_out[:, at] = terms
 
 
 def own_kernel(
     images,
     own_tile,
-    late_a,
+    late_own,
     late_other,
-    first_a,
+    first_own,
     first_other,
-    row_a,
-    prev,
+    row_own,
+    row_other,
+    sums_all,
     late_b,
-    col_b,
-    norm_b,
+    late_b_other,
     first_b,
-    row_b,
-    partner_dcorr,
-    partner_mine,
-    vec_a,
+    first_b_other,
+    dcorr_left,
+    dcorr_right,
+    mine_left,
+    mine_right,
+    vec_own,
+    vec_other,
     right_out,
     left_out,
     left_partial_out,
@@ -281,33 +315,44 @@
     loss_out,
     centred,
     norms,
+    norm_b,
     dcorr_own,
     mine_own,
 ):
-    rows, quart = late_a.shape
+    rows, quart = late_own.shape
     half = 2 * quart
     inverse = 1.0 / images
-    shift = row_a[0:1, :]
-    delta = vec_a[0:1, :]
-    rstd = vec_a[1:2, :]
-    rest = vec_a[2:3, :]
+    both = lambda i: jnp.concatenate([vec_own[i : i + 1, :], vec_other[i : i + 1, :]], axis=1)
+    delta, rstd, rest, second_partner = [both(i) for i in range(4)]
+    shift = jnp.concatenate([row_own[0:1, :], row_other[0:1, :]], axis=1)
     offset = shift + delta
-    for source, lanes in ((late_a, slice(0, quart)), (late_other, slice(quart, half))):
+    left, right = slice(0, quart), slice(quart, half)
+    for source, lanes in ((late_own, left), (late_other, right)):
         normalise_rows(source, shift[:, lanes], 1.0, centred, lanes, 64)
-    for source, lanes in ((first_a, slice(0, quart)), (first_other, slice(quart, half))):
+    for source, lanes in ((first_own, left), (first_other, right)):
         normalise_rows(source, offset[:, lanes], rstd[:, lanes], norms, lanes, 64)
     norms[rows : rows + 16, :] = jnp.broadcast_to(rest, (16, half)).astype(jnp.bfloat16)
-
-    delta_col = col_b[:, 0:1]
-    rstd_col = col_b[:, 1:2]
-    width = half // 4
+    own_b = joined_parts(late_b, quart)
+    other_b = joined_parts(late_b_other, quart)
+    for source, stats, lanes in ((first_b, own_b, left), (first_b_other, other_b, right)):
+        normalise_rows(source, stats[0], stats[1], norm_b, lanes, 64)
+        norm_b[rows : rows + 16, lanes] = jnp.broadcast_to(stats[2], (16, quart)).astype(
+            jnp.bfloat16
+        )
+
+    columns = jnp.transpose(
+        jnp.concatenate([own_b[3], own_b[1], jnp.zeros((6, quart), jnp.float32)], axis=0)
+    )
+    delta_col = columns[:, 0:1]
+    rstd_col = columns[:, 1:2]
+    width = quart // 2
     across = jnp.zeros((quart, 128), jnp.float32)
     losses = jnp.zeros((8, 128), jnp.float32)
     down = []
     for tile in range(4):
         at = slice(tile * width, (tile + 1) * width)
-        sums = prev[:, at] + jnp.dot(
-            late_b[...], centred[:, at], preferred_element_type=jnp.float32
+        sums = sums_all[:quart, at] + jnp.dot(
+            late_b[:quart, :], centred[:, at], preferred_element_type=jnp.float32
         )
         corr = tile_scaled(sums, delta_col, rstd_col, delta[:, at], rstd[:, at], inverse)
         dcorr = off_weight * corr
@@ -330,18 +375,19 @@
         def _():
             mine_own[...] = corr
 
-    second_a = vec_a[3:4, :] + jnp.concatenate(down, axis=1)
+    second_a = second_partner + jnp.concatenate(down, axis=1)
     second_b = lanes_to_row(across)
-    total_loss = jnp.sum(losses, keepdims=True) + jnp.sum(vec_a[3:4, :], keepdims=True)
-    loss_out[...] = jnp.broadcast_to(total_loss, (8, 128))
+    loss_out[0, 0] = jnp.sum(losses) + jnp.sum(second_partner)
 
     for tile in (2, 3, 0, 1):
         at = slice(tile * width, (tile + 1) * width)
+        source, partner_dcorr = (
+            (first_own, dcorr_left) if tile < 2 else (first_other, dcorr_right)
+        )
+        inner = slice((tile % 2) * width, (tile % 2 + 1) * width)
         terms = jnp.dot(
-            norm_b[:, :quart], dcorr_own[:, at], preferred_element_type=jnp.float32
-        ) + jnp.dot(norm_b[:, quart:], partner_dcorr[:, at], preferred_element_type=jnp.float32)
-        source = first_a if tile < 2 else first_other
-        inner = slice((tile % 2) * width, (tile % 2 + 1) * width)
+            norm_b[:, left], dcorr_own[:, at], preferred_element_type=jnp.float32
+        ) + jnp.dot(norm_b[:, right], partner_dcorr[:, inner], preferred_element_type=jnp.float32)
         xhat = (source[:, inner].astype(jnp.float32) - offset[:, at]) * rstd[:, at]
         value = terms[:rows] - terms[rows : rows + 1] - xhat * second_a[:, at]
         if tile < 2:
@@ -355,38 +401,39 @@
         terms = lax.dot_general(
             norms[...], dcorr_own[at, :], contract, preferred_element_type=jnp.float32
         )
-        xhat = (first_b[:, at].astype(jnp.float32) - row_b[0:1, at]) * row_b[1:2, at]
+        xhat = (first_b[:, at].astype(jnp.float32) - own_b[0][:, at]) * own_b[1][:, at]
         right_out[:, at] = terms[:rows] - terms[rows : rows + 1] - xhat * second_b[:, at]
 
     own_columns = jnp.transpose(mine_own[...])
-    partner_columns = jnp.transpose(partner_mine[...])
+    in_left = own_tile[0] < 2
+    partner_columns = jnp.transpose(jnp.where(in_left, mine_left[...], mine_right[...]))
 
     @pl.when(own_tile[1] == 0)
     def _():
-        mine_out[:, :quart] = own_columns
-        mine_out[:, quart:] = partner_columns
+        mine_out[:, left] = own_columns
+        mine_out[:, right] = partner_columns
 
     @pl.when(own_tile[1] != 0)
     def _():
-        mine_out[:, :quart] = partner_columns
-        mine_out[:, quart:] = own_columns
+        mine_out[:, left] = partner_columns
+        mine_out[:, right] = own_columns
 
 
 vmem = pl.BlockSpec(memory_space=pltpu.VMEM)
 smem = pl.BlockSpec(memory_space=pltpu.SMEM)
 
 
-def local_call(kernel, scalars, operands, outs, scratch, flops):
+def local_call(kernel, operands, outs, scratch, flops, specs=None):
     moved = sum(x.size * x.dtype.itemsize for x in (*operands, *outs))
     return pl.pallas_call(
         kernel,
         out_shape=outs,
-        in_specs=[smem] + [vmem] * len(operands),
-        out_specs=[vmem] * len(outs),
+        in_specs=[smem if x.dtype == jnp.int32 else vmem for x in operands],
+        out_specs=[smem if x.shape == (1, 1) else vmem for x in outs],
         scratch_shapes=scratch,
-        compiler_params=pltpu.CompilerParams(vmem_limit_bytes=28 * 2**20),
+        compiler_params=pltpu.CompilerParams(vmem_limit_bytes=20 * 2**20),
         cost_estimate=pl.CostEstimate(flops=flops, bytes_accessed=moved, transcendentals=0),
-    )(scalars, *operands)
+    )(*operands)
 
 
 def gathered_device(left_outputs, right_outputs):
@@ -413,8 +460,11 @@
     def x_swap(block):
         return swapped(block, "tile", 1)
 
+    def after(value, *others):
+        return lax.optimization_barrier((value, *others))
+
     other_a0 = core_swap(left_outputs)
-    left_behind, other_a0 = lax.optimization_barrier((left_outputs, other_a0))
+    left_behind, other_a0 = after(left_outputs, other_a0)
 
     first_b = along(right_outputs, pairs)
     inner_b = along(right_outputs, middle)
@@ -431,156 +481,146 @@
 
     last_b = along(third_b, outward)
     second_b = jnp.where(at_end, outer_b, inner_b)
+    second_b, other_b1 = after(second_b, other_b1)
     other_b2 = x_swap(second_b)
-    third_a, other_b1, other_a1 = lax.optimization_barrier((third_a, other_b1, other_a1))
     last_a = along(third_a, outward)
     second_a = jnp.where(at_end, outer_a, inner_a)
+    second_a, other_a1 = after(second_a, other_a1)
     other_a2 = core_swap(second_a)
+
+    def centred(blocks, shift):
+        wide = [
+            jnp.concatenate([own, other], axis=1).astype(jnp.float32) - shift
+            for own, other in blocks
+        ]
+        return wide, [x.astype(jnp.bfloat16) for x in wide]
+
+    def three_sums(wide, low):
+        return (
+            sum(jnp.sum(x, axis=0) for x in wide),
+            sum(jnp.sum(x * x, axis=0) for x in wide),
+            sum(jnp.sum(x.astype(jnp.float32), axis=0) for x in low),
+        )
+
+    def column_mean(own, other):
+        return jnp.sum(jnp.concatenate([own, other], axis=1).astype(jnp.float32), axis=0) / rows
+
+    def products(lows_a, lows_b):
+        return sum(
+            lax.dot_general(y, x, (((0,), (0,)), ((), ())), preferred_element_type=jnp.float32)
+            for x, y in zip(lows_a, lows_b)
+        )
+
+    shift_a = column_mean(left_outputs, other_a0)
+    shift_b = column_mean(right_outputs, other_b0)
+    wide_a, low_a = centred(((left_outputs, other_a0), (first_a, other_a1)), shift_a)
+    wide_b, low_b = centred(((right_outputs, other_b0), (first_b, other_b1)), shift_b)
+    total = products(low_a, low_b)
+    sums_a = three_sums(wide_a, low_a)
+    sums_b = three_sums(wide_b, low_b)
+
     late_b = jnp.where(at_end, last_b, third_b)
-    other_b3 = x_swap(late_b)
-
-    def paired(own, other):
-        return jnp.concatenate([own, other], axis=1).astype(jnp.float32)
-
-    raw_a = [paired(*p) for p in ((left_outputs, other_a0), (first_a, other_a1), (second_a, other_a2))]
-    raw_b = [
-        paired(*p)
-        for p in (
-            (right_outputs, other_b0),
-            (first_b, other_b1),
-            (second_b, other_b2),
-            (late_b, other_b3),
-        )
-    ]
-    shift_a = jnp.sum(raw_a[0], axis=0) / rows
-    shift_b = jnp.sum(raw_b[0], axis=0) / rows
-    centred_a = [x - shift_a for x in raw_a]
-    centred_b = [x - shift_b for x in raw_b]
-    low_a = [x.astype(jnp.bfloat16) for x in centred_a]
-    low_b = [x.astype(jnp.bfloat16) for x in centred_b]
-
-    def three_sums(centred, low):
-        return (
-            sum(jnp.sum(x, axis=0) for x in centred),
-            sum(jnp.sum(x * x, axis=0) for x in centred),
-            sum(jnp.sum(x.astype(jnp.float32), axis=0) for x in low),
-        )
-
-    prev = sum(
-        lax.dot_general(y, x, (((0,), (0,)), ((), ())), preferred_element_type=jnp.float32)
-        for x, y in zip(low_a, low_b)
-    )
-    sums_a = three_sums(centred_a, low_a)
-    sums_b = three_sums(centred_b, low_b)
-    delta_b = sums_b[0] / batch_images
-    rstd_b = lax.rsqrt(sums_b[1] / batch_images - delta_b * delta_b + 1e-05)
-    rest_b = (sums_b[2] / batch_images - delta_b) * rstd_b
-    norm_b = ((centred_b[0] - delta_b) * rstd_b).astype(jnp.bfloat16)
-    norm_b = jnp.concatenate(
-        [norm_b, jnp.broadcast_to(rest_b.astype(jnp.bfloat16), (16, half))], axis=0
-    )
-    late_low_b = low_b[3].T
-    col_b = jnp.stack([delta_b, rstd_b], axis=1)
-    row_b = jnp.stack([shift_b + delta_b, rstd_b] + [rest_b] * 6)
+    late_b, total, sums_a, sums_b = after(late_b, total, sums_a, sums_b)
+    wide_b, low_b = centred(((second_b, other_b2),), shift_b)
+    sums_b = [x + y for x, y in zip(sums_b, three_sums(wide_b, low_b))]
+    row_b = jnp.stack([shift_b, *sums_b] + [shift_b] * 4)[:, :quart]
+    gemm = 2 * rows * quart * quart
+    extended = jax.ShapeDtypeStruct((quart + 16, rows), jnp.bfloat16)
+    row_out = jax.ShapeDtypeStruct((8, quart), jnp.float32)
+    late_low_b, stats_b = local_call(
+        functools.partial(late_right_kernel, batch_images),
+        (late_b, row_b),
+        (extended, row_out),
+        [],
+        gemm,
+    )
+    late_low_other = x_swap(late_low_b)
+
+    wide_a, low_a = centred(((second_a, other_a2),), shift_a)
+    total = total + products(low_a, low_b)
+    sums_a = [x + y for x, y in zip(sums_a, three_sums(wide_a, low_a))]
     row_a = jnp.stack([shift_a, *sums_a] + [shift_a] * 4)
-
+    row_own, row_other = row_a[:, :quart], row_a[:, quart:]
     late_a = jnp.where(at_end, last_a, third_a)
-    (late_a, prev_own, prev_other, late_low_own, late_low_other, col_own, col_other, norm_b, norm_b_other, row_a, row_b) = (
-        lax.optimization_barrier(
-            (
-                late_a,
-                prev[:quart],
-                prev[quart:],
-                late_low_b[:quart],
-                late_low_b[quart:],
-                col_b[:quart],
-                col_b[quart:],
-                norm_b,
-                norm_b[:rows, quart:],
-                row_a,
-                row_b,
-            )
-        )
-    )
-    other_a3 = core_swap(late_a)
+    late_a, total, row_own, row_other = after(late_a, total, row_own, row_other)
+    late_other = core_swap(late_a)
 
     owned_tile = jnp.where(dpos // 2 == column_halves, 0, 2) + dpos % 2
     scalars = jnp.stack([owned_tile, row_halves]).astype(jnp.int32)
     quarter_f32 = jax.ShapeDtypeStruct((rows, quart), jnp.float32)
     quarter_bf16 = jax.ShapeDtypeStruct((rows, quart), jnp.bfloat16)
-    width = half // 4
-    wide_low = pltpu.VMEM((rows, half), jnp.bfloat16)
-    wide_ext = pltpu.VMEM((rows + 16, half), jnp.bfloat16)
-    gemm = 2 * rows * half * quart
-    partial_right, dcorr_other, mine_other, vec_a = local_call(
-        functools.partial(partner_kernel, batch_images),
-        scalars,
+    width = quart // 2
+    mine_shape = jax.ShapeDtypeStruct((quart, width), jnp.float32)
+    across_shape = jax.ShapeDtypeStruct((quart, 128), jnp.float32)
+    low = lambda n, m: pltpu.VMEM((n, m), jnp.bfloat16)
+    half_scratch = [low(rows, quart), low(rows + 16, quart)]
+    terms, across, dcorr_left, mine_left, vec_own = local_call(
+        functools.partial(partner_kernel, batch_images, 0),
+        (scalars, late_a, left_outputs, row_own, total, late_low_other, other_b0),
         (
-            late_a,
-            other_a3,
-            left_outputs,
-            other_a0,
-            row_a,
-            prev_other,
-            late_low_other,
-            col_other,
-            norm_b_other,
+            jax.ShapeDtypeStruct((rows + 16, quart), jnp.float32),
+            across_shape,
+            quarter_bf16,
+            mine_shape,
+            row_out,
         ),
-        (
-            quarter_bf16,
-            jax.ShapeDtypeStruct((quart, half), jnp.bfloat16),
-            jax.ShapeDtypeStruct((quart, width), jnp.float32),
-            jax.ShapeDtypeStruct((8, half), jnp.float32),
-        ),
-        [wide_low, wide_ext],
+        half_scratch,
+        2 * gemm,
+    )
+    partial_right, dcorr_right, mine_right, vec_other = local_call(
+        functools.partial(partner_kernel, batch_images, 1),
+        (scalars, late_other, other_a0, row_other, total, late_low_other, other_b0, terms, across),
+        (quarter_bf16, quarter_bf16, mine_shape, row_out),
+        half_scratch,
         2 * gemm,
     )
     from_x = x_swap(partial_right)
     right_own, left_own, partial_left, mine, part_loss = local_call(
         functools.partial(own_kernel, batch_images),
-        scalars,
         (
+            scalars,
             late_a,
-            other_a3,
+            late_other,
             left_outputs,
             other_a0,
-            row_a,
-            prev_own,
-            late_low_own,
-            col_own,
-            norm_b,
+            row_own,
+            row_other,
+            total,
+            late_low_b,
+            late_low_other,
             right_outputs,
-            row_b,
-            dcorr_other,
-            mine_other,
-            vec_a,
+            other_b0,
+            dcorr_left,
+            dcorr_right,
+            mine_left,
+            mine_right,
+            vec_own,
+            vec_other,
         ),
         (
             quarter_f32,
             quarter_f32,
             quarter_bf16,
             jax.ShapeDtypeStruct((width, half), jnp.float32),
-            jax.ShapeDtypeStruct((8, 128), jnp.float32),
+            jax.ShapeDtypeStruct((1, 1), jnp.float32),
         ),
         [
-            wide_low,
-            wide_ext,
-            pltpu.VMEM((quart, half), jnp.bfloat16),
+            low(rows, half),
+            low(rows + 16, half),
+            low(rows + 16, half),
+            low(quart, half),
             pltpu.VMEM((quart, width), jnp.float32),
         ],
-        4 * gemm,
+        8 * gemm,
     )
     from_core = core_swap(partial_left)
-    loss = part_loss + core_swap(part_loss)
-    left_gradient = (vec_a[1, :quart] * (left_own + from_core.astype(jnp.float32))).astype(
-        jnp.bfloat16
-    )
-    loss, left_gradient, from_x = lax.optimization_barrier((loss, left_gradient, from_x))
+    loss = part_loss[0, 0]
+    loss = loss + core_swap(loss)
+    left_gradient = (vec_own[1] * (left_own + from_core.astype(jnp.float32))).astype(jnp.bfloat16)
+    loss, from_x = after(loss, from_x)
     loss = loss + x_swap(loss)
-    right_gradient = (row_b[1, :quart] * (right_own + from_x.astype(jnp.float32))).astype(
-        jnp.bfloat16
-    )
-    return (left_gradient, right_gradient, mine[None, :, :], loss[0, :1] / feats)
+    right_gradient = (stats_b[1] * (right_own + from_x.astype(jnp.float32))).astype(jnp.bfloat16)
+    return (left_gradient, right_gradient, mine[None, :, :], jnp.reshape(loss / feats, (1,)))
 
 
 def solution(mesh):

time: 133 us -> 117 us (0.88)
  waiting for transfers between devices: 60.8 us -> 35.2 us
  starting transfers between devices: 23.5 us -> 37.9 us
  local copies, waits for them, and re-layouts: 17.1 us -> 4.39 us
  Pallas kernels: 12.3 us -> 15.6 us
  other arithmetic: 10.2 us -> 12.3 us
  matrix products: 5.86 us -> 7.4 us
  between operations: 2.71 us -> 4.05 us
    ppermute x10, waiting for transfers between devices: 45.6 us -> 29.9 us  [along(): return lax.ppermute(block, 'dp', route)]
    ppermute x10, starting transfers between devices: 15.8 us -> 27.7 us  [along(): return lax.ppermute(block, 'dp', route)]
    ppermute x12, waiting for transfers between devices: 15.3 us -> 5.27 us  [swapped(): return lax.ppermute(block, axis, route)]
    slice x6 -> x4, local copies, waits for them, and re-layouts: 7.19 us -> 0.02 us  [the longest x1 0.01 us: gathered_device(): row_own, row_other = (row_a[:, :quart], row_a[:, quart:])]
    optimization_barrier x4 -> x0, local copies, waits for them, and re-layouts: 5.11 us -> none  [gathered_device(): lax.optimization_barrier((late_a, prev[:quart], prev[quart:], late_low_b[...]
    pallas_call x2 -> x4, Pallas kernels: 12.3 us -> 15.6 us  [local_call(): pl.pallas_call(kernel, out_shape=outs, in_specs=[smem if x.dtype == jnp.i...]
    add x4 -> x11, other arithmetic: 0.02 us -> 2.9 us  [the longest x1 2.86 us: gathered_device(): total = total + products(low_a, low_b)]
    ppermute x12, starting transfers between devices: 7.76 us -> 10.2 us  [swapped(): return lax.ppermute(block, axis, route)]
  transfers between devices with their start and end apart: 22 -> 22, of which waited for: 9 -> 7; matrix products, arithmetic and copies ran while one was open for 20% -> 17% of each run, Pallas kernels for 0% -> 10%
where the time goes in v4:
time: 117 us
  starting transfers between devices  37.9 us (32%)
  waiting for transfers between devices  35.2 us (30%)
  Pallas kernels  15.6 us (13%)
  other arithmetic  12.3 us (11%)
  matrix products  7.4 us (6%)
  local copies, waits for them, and re-layouts  4.39 us (4%)
  between operations  4.05 us (3%)
    ppermute x10, waiting for transfers between devices, along(): return lax.ppermute(block, 'dp', route)  29.9 us
    ppermute x10, starting transfers between devices, along(): return lax.ppermute(block, 'dp', route)  27.7 us
    pallas_call x4, Pallas kernels, local_call(): pl.pallas_call(kernel, out_shape=outs, in_specs=[smem if x.dtype == jnp.i...  15.6 us
    ppermute x12, starting transfers between devices, swapped(): return lax.ppermute(block, axis, route)  10.2 us
    dot_general x3, matrix products, products(): lax.dot_general(y, x, (((0,), (0,)), ((), ())), preferred_element_type=jn...  7.4 us
    ppermute x12, waiting for transfers between devices, swapped(): return lax.ppermute(block, axis, route)  5.27 us
    unnamed x24, local copies, waits for them, and re-layouts  4.25 us
    add x1, other arithmetic, gathered_device(): total = total + products(low_a, low_b)  2.86 us
  transfers between devices with their start and end apart: 22, of which 7 were waited for; matrix products, arithmetic and copies ran while one was open for 17% of the time, Pallas kernels for 10%

profile of v4, /device:TPU:0, one launch (start us, length us, event | category | flops | bytes accessed | tf_op | source)
XLA Modules:
  0.0 116.8 jit_solution(13079294743861534221)
XLA Ops:
  1.8 5.6 %collective-permute-start.4 = (bf16[512,512]{1,0:T(8,128)(2,1)}, bf16[512,512]{1,0:T(8,128)(2,1)S(1)}, u32[]{:S(2)}, u32[]{:S(2)}) collective-permute-start(bf16[512,512]{1,0:T(8,128)(2,1)} %first_b.1), channel_id=1, source_target_pairs={{0,4},{4,0},{8,12},{12,8},{1,5},{5,1},{9,13},{13,9},{2,6},{6,2},{1... | collective-permute-start | bytes 1572872 | tf_op jit(solution)/shard_map/ppermute | solution.py:455
  8.2 1.3 %collective-permute-start.9 = (bf16[512,512]{1,0:T(8,128)(2,1)S(1)}, bf16[512,512]{1,0:T(8,128)(2,1)}, u32[]{:S(2)}, u32[]{:S(2)}) collective-permute-start(bf16[512,512]{1,0:T(8,128)(2,1)S(1)} %collective-permute-done.8), channel_id=1, source_target_pairs={{4,0},{8,12},{5,1},{9,13},{6,2},{10,14},{7,3},{11,15},{20,16},{24,... | collective-permute-start | bytes 1572872 | tf_op jit(solution)/shard_map/ppermute | solution.py:455
  9.5 1.6 %collective-permute-start.7 = (bf16[512,512]{1,0:T(8,128)(2,1)}, bf16[512,512]{1,0:T(8,128)(2,1)S(1)}, u32[]{:S(2)}, u32[]{:S(2)}) collective-permute-start(bf16[512,512]{1,0:T(8,128)(2,1)} %first_b.1), channel_id=1, source_target_pairs={{0,2},{2,0},{1,3},{3,1},{4,6},{6,4},{5,7},{7,5},{8,10},{10,8},{9,1... | collective-permute-start | bytes 1572872 | tf_op jit(solution)/shard_map/ppermute | solution.py:19
  11.0 13.3 %collective-permute-start.1 = (bf16[512,512]{1,0:T(8,128)(2,1)}, bf16[512,512]{1,0:T(8,128)(2,1)S(1)}, u32[]{:S(2)}, u32[]{:S(2)}) collective-permute-start(bf16[512,512]{1,0:T(8,128)(2,1)} %first_own.1), channel_id=1, source_target_pairs={{0,4},{4,0},{8,12},{12,8},{1,5},{5,1},{9,13},{13,9},{2,6},{6,2},{1... | collective-permute-start | bytes 1572872 | tf_op jit(solution)/shard_map/ppermute | solution.py:455
  24.8 1.2 %convert_reduce_fusion = f32[1024]{0:T(1024)S(1)} fusion(bf16[512,512]{1,0:T(8,128)(2,1)S(1)} %collective-permute-done.first.first_other, bf16[512,512]{1,0:T(8,128)(2,1)} %first_own.1), kind=kLoop, calls=%fused_computation.1 | loop fusion | flops 2620416 | bytes 1052672 | tf_op jit(solution)/shard_map/reduce_sum | solution.py:506
  26.8 8.2 %collective-permute-done.9 = bf16[512,512]{1,0:T(8,128)(2,1)} collective-permute-done((bf16[512,512]{1,0:T(8,128)(2,1)S(1)}, bf16[512,512]{1,0:T(8,128)(2,1)}, u32[]{:S(2)}, u32[]{:S(2)}) %collective-permute-start.9) | collective-permute-done | bytes 524320 | tf_op jit(solution)/shard_map/ppermute | solution.py:455
  34.9 1.3 %collective-permute-start.12 = (bf16[512,512]{1,0:T(8,128)(2,1)S(1)}, bf16[512,512]{1,0:T(8,128)(2,1)S(1)}, u32[]{:S(2)}, u32[]{:S(2)}) collective-permute-start(bf16[512,512]{1,0:T(8,128)(2,1)S(1)} %collective-permute-done.11), channel_id=1, source_target_pairs={{4,0},{8,12},{5,1},{9,13},{6,2},{10,14},{7,3},{11,15},{20,16},{24,... | collective-permute-start | bytes 1572872 | tf_op jit(solution)/shard_map/ppermute | solution.py:455
  36.2 1.1 broadcast_select_fusion.1
  37.3 1.6 %collective-permute-start.14 = (bf16[512,512]{1,0:T(8,128)(2,1)S(1)}, bf16[512,512]{1,0:T(8,128)(2,1)S(1)}, u32[]{:S(2)}, u32[]{:S(2)}) collective-permute-start(bf16[512,512]{1,0:T(8,128)(2,1)S(1)} %broadcast_select_fusion.1), channel_id=1, source_target_pairs={{0,2},{2,0},{1,3},{3,1},{4,6},{6,4},{5,7},{7,5},{8,10},{10,8},{9,1... | collective-permute-start | bytes 1572872 | tf_op jit(solution)/shard_map/ppermute | solution.py:19
  38.9 7.2 %collective-permute-done.1 = bf16[512,512]{1,0:T(8,128)(2,1)S(1)} collective-permute-done((bf16[512,512]{1,0:T(8,128)(2,1)}, bf16[512,512]{1,0:T(8,128)(2,1)S(1)}, u32[]{:S(2)}, u32[]{:S(2)}) %collective-permute-start.1) | collective-permute-done | bytes 524320 | tf_op jit(solution)/shard_map/ppermute | solution.py:455
  46.3 1.5 %collective-permute-start.2 = (bf16[512,512]{1,0:T(8,128)(2,1)S(1)}, bf16[512,512]{1,0:T(8,128)(2,1)}, u32[]{:S(2)}, u32[]{:S(2)}) collective-permute-start(bf16[512,512]{1,0:T(8,128)(2,1)S(1)} %collective-permute-done.1), channel_id=1, source_target_pairs={{4,8},{8,4},{5,9},{9,5},{6,10},{10,6},{7,11},{11,7},{20,24},{24,20... | collective-permute-start | bytes 1572872 | tf_op jit(solution)/shard_map/ppermute | solution.py:455
  47.7 1.3 %collective-permute-start.6 = (bf16[512,512]{1,0:T(8,128)(2,1)S(1)}, bf16[512,512]{1,0:T(8,128)(2,1)S(1)}, u32[]{:S(2)}, u32[]{:S(2)}) collective-permute-start(bf16[512,512]{1,0:T(8,128)(2,1)S(1)} %collective-permute-done.5), channel_id=1, source_target_pairs={{4,0},{8,12},{5,1},{9,13},{6,2},{10,14},{7,3},{11,15},{20,16},{24,... | collective-permute-start | bytes 1572872 | tf_op jit(solution)/shard_map/ppermute | solution.py:455
  49.0 7.3 %collective-permute-done.12 = bf16[512,512]{1,0:T(8,128)(2,1)S(1)} collective-permute-done((bf16[512,512]{1,0:T(8,128)(2,1)S(1)}, bf16[512,512]{1,0:T(8,128)(2,1)S(1)}, u32[]{:S(2)}, u32[]{:S(2)}) %collective-permute-start.12) | collective-permute-done | bytes 524320 | tf_op jit(solution)/shard_map/ppermute | solution.py:455
  56.6 1.1 convert_reduce_fusion.2
  57.8 1.4 %collective-permute-start.3 = (bf16[512,512]{1,0:T(8,128)(2,1)}, bf16[512,512]{1,0:T(8,128)(2,1)}, u32[]{:S(2)}, u32[]{:S(2)}) collective-permute-start(bf16[512,512]{1,0:T(8,128)(2,1)} %collective-permute-done.2), channel_id=1, source_target_pairs={{4,0},{8,12},{5,1},{9,13},{6,2},{10,14},{7,3},{11,15},{20,16},{24,... | collective-permute-start | bytes 1572872 | tf_op jit(solution)/shard_map/ppermute | solution.py:455
  59.2 1.3 %fusion.16 = f32[1024,1024]{1,0:T(8,128)S(1)} fusion(f32[1024]{0:T(1024)S(1)} %broadcast_multiply_fusion.1, f32[1024]{0:T(1024)S(1)} %broadcast_multiply_fusion, bf16[512,512]{1,0:T(8,128)(2,1)S(1)} %collective-permute-done.13, bf16[512,512]{1,0:T(8,128)(2,1)S(1)} %collective-permute-done.1, bf16[512,512]{1,0:T(8,128)(2,1)S(1)} %collective-permute-done.10, ...), kind=kOutput, calls=%fused_computation.43 | convolution fusion | flops 1080033280 | bytes 6299648 | tf_op jit(solution)/shard_map/dot_general | solution.py:510
  60.5 6.2 %collective-permute-done.6 = bf16[512,512]{1,0:T(8,128)(2,1)S(1)} collective-permute-done((bf16[512,512]{1,0:T(8,128)(2,1)S(1)}, bf16[512,512]{1,0:T(8,128)(2,1)S(1)}, u32[]{:S(2)}, u32[]{:S(2)}) %collective-permute-start.6) | collective-permute-done | bytes 524320 | tf_op jit(solution)/shard_map/ppermute | solution.py:455
  66.9 3.3 %convolution_add_fusion = f32[1024,1024]{1,0:T(8,128)} fusion(f32[1024,1024]{1,0:T(8,128)S(1)} %fusion.16, f32[1024]{0:T(1024)S(1)} %broadcast_multiply_fusion.1, f32[1024]{0:T(1024)S(1)} %broadcast_multiply_fusion, bf16[512,512]{1,0:T(8,128)(2,1)S(1)} %collective-permute-done.first.first_other, bf16[512,512]{1,0:T(8,128)(2,1)S(1)} %copy-done.2, ...), kind=kOutput, calls=%fused_computation.10 | convolution fusion | flops 1081081856 | bytes 10493952 | tf_op jit(solution)/shard_map/dot_general | solution.py:510
  70.1 1.1 convert_reduce_fusion.3
  71.4 1.1 shard_map.57
  72.6 2.0 %collective-permute-start.16 = (bf16[528,512]{1,0:T(8,128)(2,1)}, bf16[528,512]{1,0:T(8,128)(2,1)S(1)}, u32[]{:S(2)}, u32[]{:S(2)}) collective-permute-start(bf16[528,512]{1,0:T(8,128)(2,1)} %get-tuple-element.57.late_b), channel_id=1, source_target_pairs={{0,2},{2,0},{1,3},{3,1},{4,6},{6,4},{5,7},{7,5},{8,10},{10,8},{9,1... | collective-permute-start | bytes 1622024 | tf_op jit(solution)/shard_map/ppermute | solution.py:19
  74.7 2.8 %fusion.19 = f32[1024,1024]{1,0:T(8,128)S(1)} fusion(f32[1024]{0:T(1024)S(1)} %broadcast_multiply_fusion.1, f32[1024]{0:T(1024)S(1)} %broadcast_multiply_fusion, bf16[512,512]{1,0:T(8,128)(2,1)} %copy-done.10, bf16[512,512]{1,0:T(8,128)(2,1)} %copy-done.8, bf16[512,512]{1,0:T(8,128)(2,1)} %copy-done.9, bf16[512,512]{1,0:T(8,128)(2,1)S(1)} %broadcast_select_fusion.1), kind=kOutput, calls=%fused_computation.44 | convolution fusion | flops 1080033280 | bytes 6299648 | tf_op jit(solution)/shard_map/dot_general | solution.py:510
  78.5 1.1 broadcast_select_fusion.3.late.late_own
  79.6 2.9 %add.76.sums_all = f32[1024,1024]{1,0:T(8,128)} add(f32[1024,1024]{1,0:T(8,128)S(1)} %copy-done.7, f32[1024,1024]{1,0:T(8,128)S(1)} %fusion.19) | non-fusion elementwise | flops 1048576 | bytes 12582912 | tf_op jit(solution)/shard_map/add | solution.py:540
  82.5 3.7 %collective-permute-done.16.late_b.late_b_other = bf16[528,512]{1,0:T(8,128)(2,1)S(1)} collective-permute-done((bf16[528,512]{1,0:T(8,128)(2,1)}, bf16[528,512]{1,0:T(8,128)(2,1)S(1)}, u32[]{:S(2)}, u32[]{:S(2)}) %collective-permute-start.16) | collective-permute-done | bytes 540704 | tf_op jit(solution)/shard_map/ppermute | solution.py:19
  86.2 2.2 %copy-done = f32[1024,1024]{1,0:T(8,128)S(1)} copy-done((f32[1024,1024]{1,0:T(8,128)S(1)}, f32[1024,1024]{1,0:T(8,128)}, u32[]{:S(2)}) %copy-start) | copy-done | bytes 4194328
  88.4 2.4 %shard_map.58 = (f32[528,512]{1,0:T(8,128)S(1)}, f32[512,128]{1,0:T(8,128)S(1)}, bf16[512,512]{1,0:T(8,128)(2,1)S(1)}, f32[512,256]{1,0:T(8,128)S(1)}, f32[8,512]{1,0:T(8,128)S(1)}) custom-call(s32[2]{0:T(128)S(1)} %pad_add_fusion.own_tile, bf16[512,512]{1,0:T(8,128)(2,1)S(1)} %broadcast_select_fusion.3.late.late_own, bf16[512,512]{1,0:T(8,128)(2,1)S(1)} %copy-done.2, ...), custom_call_target="tpu_custom_call" | custom-call | flops 536870912 | bytes 8732680 | tf_op jit(solution)/shard_map/pallas_call | solution.py:428
  90.8 4.2 %shard_map.59 = (bf16[512,512]{1,0:T(8,128)(2,1)}, bf16[512,512]{1,0:T(8,128)(2,1)S(1)}, f32[512,256]{1,0:T(8,128)S(1)}, f32[8,512]{1,0:T(8,128)S(1)}) custom-call(s32[2]{0:T(128)S(1)} %pad_add_fusion.own_tile, bf16[512,512]{1,0:T(8,128)(2,1)} %collective-permute-done.17.late.late_other, bf16[512,512]{1,0:T(8,128)(2,1)S(1)} %collective-permute-done.first.first_other, ...), custom_call_target="tpu_custom_call" | custom-call | flops 536870912 | bytes 9256968 | tf_op jit(solution)/shard_map/pallas_call | solution.py:428
  95.6 7.9 %shard_map.60 = (f32[512,512]{1,0:T(8,128)S(1)}, f32[512,512]{1,0:T(8,128)S(1)}, bf16[512,512]{1,0:T(8,128)(2,1)}, f32[256,1024]{1,0:T(8,128)}, f32[1,1]{1,0:T(1,128)}) custom-call(s32[2]{0:T(128)S(1)} %pad_add_fusion.own_tile, bf16[512,512]{1,0:T(8,128)(2,1)S(1)} %broadcast_select_fusion.3.late.late_own, ...), custom_call_target="tpu_custom_call" | custom-call | flops 2147483648 | bytes 14254092 | tf_op jit(solution)/shard_map/pallas_call | solution.py:428
  106.1 1.5 %collective-permute-done.19 = f32[]{:T(128)} collective-permute-done((f32[]{:T(128)}, f32[]{:T(128)}, u32[]{:S(2)}, u32[]{:S(2)}) %collective-permute-start.19) | collective-permute-done | bytes 36 | tf_op jit(solution)/shard_map/ppermute | solution.py:19
  109.0 2.8 %collective-permute-start.21 = (f32[]{:T(128)}, f32[]{:T(128)}, u32[]{:S(2)}, u32[]{:S(2)}) collective-permute-start(f32[]{:T(128)} %add.84), channel_id=1, source_target_pairs={{0,2},{2,0},{1,3},{3,1},{4,6},{6,4},{5,7},{7,5},{8,10},{10,8},{9,1... | collective-permute-start | bytes 20 | tf_op jit(solution)/shard_map/ppermute | solution.py:19
  111.8 2.3 %multiply_convert_fusion = bf16[512,512]{1,0:T(8,128)(2,1)} fusion(f32[512,512]{1,0:T(8,128)} %copy-done.6, bf16[512,512]{1,0:T(8,128)(2,1)} %collective-permute-done.20, f32[512]{0:T(512)S(1)} %bitcast.32), kind=kLoop, calls=%fused_computation.41 | loop fusion | flops 1048576 | bytes 2099200 | tf_op jit(solution)/shard_map/convert_element_type | solution.py:622
  (75 shorter events, 9.0 us)
Async XLA Ops:
  0.6 45.4 %copy-start.3 = (bf16[512,512]{1,0:T(8,128)(2,1)S(1)}, bf16[512,512]{1,0:T(8,128)(2,1)}, u32[]{:S(2)}) copy-start(bf16[512,512]{1,0:T(8,128)(2,1)} %first_b.1) | copy-start | bytes 1572868
  0.6 6.8 %collective-permute-start = (bf16[512,512]{1,0:T(8,128)(2,1)}, bf16[512,512]{1,0:T(8,128)(2,1)S(1)}, u32[]{:S(2)}, u32[]{:S(2)}) collective-permute-start(bf16[512,512]{1,0:T(8,128)(2,1)} %first_own.1), channel_id=1, source_target_pairs={{0,1},{1,0},{2,3},{3,2},{4,5},{5,4},{6,7},{7,6},{8,9},{9,8},{10,11... | collective-permute-start | bytes 1572872 | tf_op jit(solution)/shard_map/ppermute | solution.py:19
  1.2 7.0 %collective-permute-start.8 = (bf16[512,512]{1,0:T(8,128)(2,1)}, bf16[512,512]{1,0:T(8,128)(2,1)S(1)}, u32[]{:S(2)}, u32[]{:S(2)}) collective-permute-start(bf16[512,512]{1,0:T(8,128)(2,1)} %first_b.1), channel_id=1, source_target_pairs={{4,8},{8,4},{5,9},{9,5},{6,10},{10,6},{7,11},{11,7},{20,24},{24,20... | collective-permute-start | bytes 1572872 | tf_op jit(solution)/shard_map/ppermute | solution.py:455
  1.8 22.4 %collective-permute-start.4 = (bf16[512,512]{1,0:T(8,128)(2,1)}, bf16[512,512]{1,0:T(8,128)(2,1)S(1)}, u32[]{:S(2)}, u32[]{:S(2)}) collective-permute-start(bf16[512,512]{1,0:T(8,128)(2,1)} %first_b.1), channel_id=1, source_target_pairs={{0,4},{4,0},{8,12},{12,8},{1,5},{5,1},{9,13},{13,9},{2,6},{6,2},{1... | collective-permute-start | bytes 1572872 | tf_op jit(solution)/shard_map/ppermute | solution.py:455
  7.4 18.6 %collective-permute-start.11 = (bf16[512,512]{1,0:T(8,128)(2,1)}, bf16[512,512]{1,0:T(8,128)(2,1)S(1)}, u32[]{:S(2)}, u32[]{:S(2)}) collective-permute-start(bf16[512,512]{1,0:T(8,128)(2,1)} %first_own.1), channel_id=1, source_target_pairs={{4,8},{8,4},{5,9},{9,5},{6,10},{10,6},{7,11},{11,7},{20,24},{24,20... | collective-permute-start | bytes 1572872 | tf_op jit(solution)/shard_map/ppermute | solution.py:455
  8.1 26.8 %copy-start.11 = (bf16[512,512]{1,0:T(8,128)(2,1)}, bf16[512,512]{1,0:T(8,128)(2,1)S(1)}, u32[]{:S(2)}) copy-start(bf16[512,512]{1,0:T(8,128)(2,1)S(1)} %collective-permute-done.8) | copy-start | bytes 1572868
  8.2 26.8 %collective-permute-start.9 = (bf16[512,512]{1,0:T(8,128)(2,1)S(1)}, bf16[512,512]{1,0:T(8,128)(2,1)}, u32[]{:S(2)}, u32[]{:S(2)}) collective-permute-start(bf16[512,512]{1,0:T(8,128)(2,1)S(1)} %collective-permute-done.8), channel_id=1, source_target_pairs={{4,0},{8,12},{5,1},{9,13},{6,2},{10,14},{7,3},{11,15},{20,16},{24,... | collective-permute-start | bytes 1572872 | tf_op jit(solution)/shard_map/ppermute | solution.py:455
  9.5 36.6 %collective-permute-start.7 = (bf16[512,512]{1,0:T(8,128)(2,1)}, bf16[512,512]{1,0:T(8,128)(2,1)S(1)}, u32[]{:S(2)}, u32[]{:S(2)}) collective-permute-start(bf16[512,512]{1,0:T(8,128)(2,1)} %first_b.1), channel_id=1, source_target_pairs={{0,2},{2,0},{1,3},{3,1},{4,6},{6,4},{5,7},{7,5},{8,10},{10,8},{9,1... | collective-permute-start | bytes 1572872 | tf_op jit(solution)/shard_map/ppermute | solution.py:19
  11.0 35.1 %collective-permute-start.1 = (bf16[512,512]{1,0:T(8,128)(2,1)}, bf16[512,512]{1,0:T(8,128)(2,1)S(1)}, u32[]{:S(2)}, u32[]{:S(2)}) collective-permute-start(bf16[512,512]{1,0:T(8,128)(2,1)} %first_own.1), channel_id=1, source_target_pairs={{0,4},{4,0},{8,12},{12,8},{1,5},{5,1},{9,13},{13,9},{2,6},{6,2},{1... | collective-permute-start | bytes 1572872 | tf_op jit(solution)/shard_map/ppermute | solution.py:455
  24.3 13.0 %collective-permute-start.10 = (bf16[512,512]{1,0:T(8,128)(2,1)S(1)}, bf16[512,512]{1,0:T(8,128)(2,1)S(1)}, u32[]{:S(2)}, u32[]{:S(2)}) collective-permute-start(bf16[512,512]{1,0:T(8,128)(2,1)S(1)} %collective-permute-done.4), channel_id=1, source_target_pairs={{0,2},{2,0},{1,3},{3,1},{4,6},{6,4},{5,7},{7,5},{8,10},{10,8},{9,1... | collective-permute-start | bytes 1572872 | tf_op jit(solution)/shard_map/ppermute | solution.py:19
  26.1 21.7 %collective-permute-start.5 = (bf16[512,512]{1,0:T(8,128)(2,1)S(1)}, bf16[512,512]{1,0:T(8,128)(2,1)S(1)}, u32[]{:S(2)}, u32[]{:S(2)}) collective-permute-start(bf16[512,512]{1,0:T(8,128)(2,1)S(1)} %collective-permute-done.4), channel_id=1, source_target_pairs={{4,8},{8,4},{5,9},{9,5},{6,10},{10,6},{7,11},{11,7},{20,24},{24,20... | collective-permute-start | bytes 1572872 | tf_op jit(solution)/shard_map/ppermute | solution.py:455
  34.9 21.5 %collective-permute-start.12 = (bf16[512,512]{1,0:T(8,128)(2,1)S(1)}, bf16[512,512]{1,0:T(8,128)(2,1)S(1)}, u32[]{:S(2)}, u32[]{:S(2)}) collective-permute-start(bf16[512,512]{1,0:T(8,128)(2,1)S(1)} %collective-permute-done.11), channel_id=1, source_target_pairs={{4,0},{8,12},{5,1},{9,13},{6,2},{10,14},{7,3},{11,15},{20,16},{24,... | collective-permute-start | bytes 1572872 | tf_op jit(solution)/shard_map/ppermute | solution.py:455
  37.3 19.2 %collective-permute-start.14 = (bf16[512,512]{1,0:T(8,128)(2,1)S(1)}, bf16[512,512]{1,0:T(8,128)(2,1)S(1)}, u32[]{:S(2)}, u32[]{:S(2)}) collective-permute-start(bf16[512,512]{1,0:T(8,128)(2,1)S(1)} %broadcast_select_fusion.1), channel_id=1, source_target_pairs={{0,2},{2,0},{1,3},{3,1},{4,6},{6,4},{5,7},{7,5},{8,10},{10,8},{9,1... | collective-permute-start | bytes 1572872 | tf_op jit(solution)/shard_map/ppermute | solution.py:19
  46.1 10.4 %collective-permute-start.13 = (bf16[512,512]{1,0:T(8,128)(2,1)S(1)}, bf16[512,512]{1,0:T(8,128)(2,1)S(1)}, u32[]{:S(2)}, u32[]{:S(2)}) collective-permute-start(bf16[512,512]{1,0:T(8,128)(2,1)S(1)} %collective-permute-done.1), channel_id=1, source_target_pairs={{0,1},{1,0},{2,3},{3,2},{4,5},{5,4},{6,7},{7,6},{8,9},{9,8},{10,11... | collective-permute-start | bytes 1572872 | tf_op jit(solution)/shard_map/ppermute | solution.py:19
  46.3 11.5 %collective-permute-start.2 = (bf16[512,512]{1,0:T(8,128)(2,1)S(1)}, bf16[512,512]{1,0:T(8,128)(2,1)}, u32[]{:S(2)}, u32[]{:S(2)}) collective-permute-start(bf16[512,512]{1,0:T(8,128)(2,1)S(1)} %collective-permute-done.1), channel_id=1, source_target_pairs={{4,8},{8,4},{5,9},{9,5},{6,10},{10,6},{7,11},{11,7},{20,24},{24,20... | collective-permute-start | bytes 1572872 | tf_op jit(solution)/shard_map/ppermute | solution.py:455
  47.7 19.0 %collective-permute-start.6 = (bf16[512,512]{1,0:T(8,128)(2,1)S(1)}, bf16[512,512]{1,0:T(8,128)(2,1)S(1)}, u32[]{:S(2)}, u32[]{:S(2)}) collective-permute-start(bf16[512,512]{1,0:T(8,128)(2,1)S(1)} %collective-permute-done.5), channel_id=1, source_target_pairs={{4,0},{8,12},{5,1},{9,13},{6,2},{10,14},{7,3},{11,15},{20,16},{24,... | collective-permute-start | bytes 1572872 | tf_op jit(solution)/shard_map/ppermute | solution.py:455
  56.4 13.7 %copy-start.8 = (bf16[512,512]{1,0:T(8,128)(2,1)}, bf16[512,512]{1,0:T(8,128)(2,1)S(1)}, u32[]{:S(2)}) copy-start(bf16[512,512]{1,0:T(8,128)(2,1)S(1)} %broadcast_select_fusion) | copy-start | bytes 1572868
  56.5 13.7 %collective-permute-start.15 = (bf16[512,512]{1,0:T(8,128)(2,1)S(1)}, bf16[512,512]{1,0:T(8,128)(2,1)S(1)}, u32[]{:S(2)}, u32[]{:S(2)}) collective-permute-start(bf16[512,512]{1,0:T(8,128)(2,1)S(1)} %broadcast_select_fusion), channel_id=1, source_target_pairs={{0,1},{1,0},{2,3},{3,2},{4,5},{5,4},{6,7},{7,6},{8,9},{9,8},{10,11... | collective-permute-start | bytes 1572872 | tf_op jit(solution)/shard_map/ppermute | solution.py:19
  56.6 1.2 %copy-start.9 = (bf16[512,512]{1,0:T(8,128)(2,1)}, bf16[512,512]{1,0:T(8,128)(2,1)S(1)}, u32[]{:S(2)}) copy-start(bf16[512,512]{1,0:T(8,128)(2,1)S(1)} %collective-permute-done.14) | copy-start | bytes 1572868
  57.7 9.1 %copy-start.2 = (bf16[512,512]{1,0:T(8,128)(2,1)S(1)}, bf16[512,512]{1,0:T(8,128)(2,1)}, u32[]{:S(2)}) copy-start(bf16[512,512]{1,0:T(8,128)(2,1)} %first_own.1) | copy-start | bytes 1572868
  57.8 20.7 %collective-permute-start.3 = (bf16[512,512]{1,0:T(8,128)(2,1)}, bf16[512,512]{1,0:T(8,128)(2,1)}, u32[]{:S(2)}, u32[]{:S(2)}) collective-permute-start(bf16[512,512]{1,0:T(8,128)(2,1)} %collective-permute-done.2), channel_id=1, source_target_pairs={{4,0},{8,12},{5,1},{9,13},{6,2},{10,14},{7,3},{11,15},{20,16},{24,... | collective-permute-start | bytes 1572872 | tf_op jit(solution)/shard_map/ppermute | solution.py:455
  70.1 1.1 copy-start.10
  72.6 13.7 %collective-permute-start.16 = (bf16[528,512]{1,0:T(8,128)(2,1)}, bf16[528,512]{1,0:T(8,128)(2,1)S(1)}, u32[]{:S(2)}, u32[]{:S(2)}) collective-permute-start(bf16[528,512]{1,0:T(8,128)(2,1)} %get-tuple-element.57.late_b), channel_id=1, source_target_pairs={{0,2},{2,0},{1,3},{3,1},{4,6},{6,4},{5,7},{7,5},{8,10},{10,8},{9,1... | collective-permute-start | bytes 1622024 | tf_op jit(solution)/shard_map/ppermute | solution.py:19
  74.7 4.9 %copy-start.7 = (f32[1024,1024]{1,0:T(8,128)S(1)}, f32[1024,1024]{1,0:T(8,128)}, u32[]{:S(2)}) copy-start(f32[1024,1024]{1,0:T(8,128)} %convolution_add_fusion) | copy-start | bytes 12582916
  82.5 8.3 %collective-permute-start.17 = (bf16[512,512]{1,0:T(8,128)(2,1)S(1)}, bf16[512,512]{1,0:T(8,128)(2,1)}, u32[]{:S(2)}, u32[]{:S(2)}) collective-permute-start(bf16[512,512]{1,0:T(8,128)(2,1)S(1)} %broadcast_select_fusion.3.late.late_own), channel_id=1, source_target_pairs={{0,1},{1,0},{2,3},{3,2},{4,5},{5,4},{6,7},{7,6},{8,9},{9,8},{10,11... | collective-permute-start | bytes 1572872 | tf_op jit(solution)/shard_map/ppermute | solution.py:19
  86.2 2.2 %copy-start = (f32[1024,1024]{1,0:T(8,128)S(1)}, f32[1024,1024]{1,0:T(8,128)}, u32[]{:S(2)}) copy-start(f32[1024,1024]{1,0:T(8,128)} %add.76.sums_all) | copy-start | bytes 12582916
  88.4 2.4 %copy-start.1 = (f32[1024,1024]{1,0:T(8,128)S(1)}, f32[1024,1024]{1,0:T(8,128)}, u32[]{:S(2)}) copy-start(f32[1024,1024]{1,0:T(8,128)} %add.76.sums_all) | copy-start | bytes 12582916
  95.0 14.0 %collective-permute-start.20 = (bf16[512,512]{1,0:T(8,128)(2,1)}, bf16[512,512]{1,0:T(8,128)(2,1)}, u32[]{:S(2)}, u32[]{:S(2)}) collective-permute-start(bf16[512,512]{1,0:T(8,128)(2,1)} %get-tuple-element.72), channel_id=1, source_target_pairs={{0,2},{2,0},{1,3},{3,1},{4,6},{6,4},{5,7},{7,5},{8,10},{10,8},{9,1... | collective-permute-start | bytes 1572872 | tf_op jit(solution)/shard_map/ppermute | solution.py:19
  105.5 8.5 %copy-start.5 = (f32[512,512]{1,0:T(8,128)S(1)}, f32[512,512]{1,0:T(8,128)}, u32[]{:S(2)}) copy-start(f32[512,512]{1,0:T(8,128)} %copy-done.4) | copy-start | bytes 3145732
  105.5 8.5 %collective-permute-start.18 = (bf16[512,512]{1,0:T(8,128)(2,1)}, bf16[512,512]{1,0:T(8,128)(2,1)S(1)}, u32[]{:S(2)}, u32[]{:S(2)}) collective-permute-start(bf16[512,512]{1,0:T(8,128)(2,1)} %get-tuple-element.68), channel_id=1, source_target_pairs={{0,1},{1,0},{2,3},{3,2},{4,5},{5,4},{6,7},{7,6},{8,9},{9,8},{10,11... | collective-permute-start | bytes 1572872 | tf_op jit(solution)/shard_map/ppermute | solution.py:19
  105.6 2.1 %collective-permute-start.19 = (f32[]{:T(128)}, f32[]{:T(128)}, u32[]{:S(2)}, u32[]{:S(2)}) collective-permute-start(f32[]{:T(128)} %bitcast.12), channel_id=1, source_target_pairs={{0,1},{1,0},{2,3},{3,2},{4,5},{5,4},{6,7},{7,6},{8,9},{9,8},{10,11... | collective-permute-start | bytes 20 | tf_op jit(solution)/shard_map/ppermute | solution.py:19
  109.0 6.1 %collective-permute-start.21 = (f32[]{:T(128)}, f32[]{:T(128)}, u32[]{:S(2)}, u32[]{:S(2)}) collective-permute-start(f32[]{:T(128)} %add.84), channel_id=1, source_target_pairs={{0,2},{2,0},{1,3},{3,1},{4,6},{6,4},{5,7},{7,5},{8,10},{10,8},{9,1... | collective-permute-start | bytes 20 | tf_op jit(solution)/shard_map/ppermute | solution.py:19
  (2 other events, 2.0 us)

commit v5 on v4

--- a/solution.py
+++ b/solution.py
@@ -201,28 +201,91 @@
     return sum(values[:, at : at + 128] for at in range(0, width, 128))
 
 
-def late_right_kernel(images, late, row, out, stats):
+def column_mean(block):
+    rows, width = block.shape
+    folded = jnp.zeros((8, width), jnp.float32)
+    for at in range(0, rows, 64):
+        piece = block[at : at + 64, :].astype(jnp.float32)
+        folded = folded + jnp.sum(piece.reshape(8, 8, width), axis=0)
+    return jnp.sum(folded, axis=0, keepdims=True) / rows
+
+
+def add_sums(sums, centred, low):
+    fold = lambda v: jnp.sum(v.reshape(v.shape[0] // 8, 8, v.shape[1]), axis=0)
+    return [
+        sums[0] + fold(centred),
+        sums[1] + fold(centred * centred),
+        sums[2] + fold(low.astype(jnp.float32)),
+    ]
+
+
+def late_right_kernel(images, first, second, third, late, out, stats):
     rows, quart = late.shape
-    shift = row[0:1, :]
-    zero = jnp.zeros((8, quart), jnp.float32)
-    sums = [zero, zero, zero]
-    fold = lambda v: jnp.sum(v.reshape(v.shape[0] // 8, 8, quart), axis=0)
-    for at in range(0, rows, 128):
-        centred = late[at : at + 128, :].astype(jnp.float32) - shift
-        low = centred.astype(jnp.bfloat16)
-        out[:quart, at : at + 128] = jnp.transpose(low)
-        sums = [
-            sums[0] + fold(centred),
-            sums[1] + fold(centred * centred),
-            sums[2] + fold(low.astype(jnp.float32)),
-        ]
-    sums = [row[i + 1 : i + 2, :] + jnp.sum(s, axis=0, keepdims=True) for i, s in enumerate(sums)]
+    shift = column_mean(first)
+    sums = [jnp.zeros((8, quart), jnp.float32)] * 3
+    for block in (first, second, third, late):
+        for at in range(0, rows, 128):
+            centred = block[at : at + 128, :].astype(jnp.float32) - shift
+            low = centred.astype(jnp.bfloat16)
+            if block is late:
+                out[:quart, at : at + 128] = jnp.transpose(low)
+            sums = add_sums(sums, centred, low)
+    sums = [jnp.sum(s, axis=0, keepdims=True) for s in sums]
     delta, rstd, rest = moments(sums, images)
     values = [shift + delta, rstd, rest, delta]
     stats[...] = jnp.concatenate(values + [jnp.zeros((4, quart), jnp.float32)], axis=0)
     parts = sum([three_parts(v) for v in values], [])
     parts = [p.astype(jnp.float32) for p in parts] + [jnp.zeros((4, quart), jnp.float32)]
     out[quart:, :] = jnp.concatenate(parts, axis=0).astype(jnp.bfloat16)
+
+
+def products_kernel(*refs):
+    lefts, rights = refs[0:6], refs[6:12]
+    partner_own, partner_other, own_all, row_own, low_left, low_right = refs[12:]
+    rows, quart = lefts[0].shape
+    width = quart // 2
+    for half in range(2):
+        lanes = slice(half * quart, (half + 1) * quart)
+        shift = column_mean(lefts[half])
+        sums = [jnp.zeros((8, quart), jnp.float32)] * 3
+        for block in range(3):
+            source = lefts[2 * block + half]
+            for at in range(0, rows, 64):
+                centred = source[at : at + 64, :].astype(jnp.float32) - shift
+                low = centred.astype(jnp.bfloat16)
+                low_left[block * rows + at : block * rows + at + 64, lanes] = low
+                if half == 0:
+                    sums = add_sums(sums, centred, low)
+        if half == 0:
+            sums = [jnp.sum(s, axis=0, keepdims=True) for s in sums]
+            zeros = jnp.zeros((4, quart), jnp.float32)
+            row_own[...] = jnp.concatenate([shift, *sums, zeros], axis=0)
+    for half in range(2):
+        lanes = slice(half * quart, (half + 1) * quart)
+        shift = column_mean(rights[half])
+        for block in range(3):
+            source = rights[2 * block + half]
+            for at in range(0, rows, 128):
+                low = (source[at : at + 128, :].astype(jnp.float32) - shift).astype(jnp.bfloat16)
+                low_right[lanes, block * rows + at : block * rows + at + 128] = jnp.transpose(low)
+    for tile in range(4):
+        wide = slice(tile * width, (tile + 1) * width)
+        inner = slice((tile % 2) * width, (tile % 2 + 1) * width)
+        target = partner_own if tile < 2 else partner_other
+        target[:, inner] = jnp.dot(
+            low_right[quart:, :], low_left[:, wide], preferred_element_type=jnp.float32
+        )
+        own_all[:, wide] = jnp.dot(
+            low_right[:quart, :], low_left[:, wide], preferred_element_type=jnp.float32
+        )
+
+
+def final_kernel(own, other, stats, out):
+    rows = own.shape[0]
+    for at in range(0, rows, 64):
+        piece = slice(at, at + 64)
+        value = stats[1:2, :] * (own[piece, :] + other[piece, :].astype(jnp.float32))
+        out[piece, :] = value.astype(jnp.bfloat16)
 
 
 def partner_kernel(images, part, own_tile, late, first, row, sums_all, late_b, first_b, *refs):
@@ -249,8 +312,7 @@
     across = across_in[...] if part else jnp.zeros((quart, 128), jnp.float32)
     for tile in range(2):
         at = slice(tile * width, (tile + 1) * width)
-        wide = slice(part * quart + tile * width, part * quart + (tile + 1) * width)
-        sums = sums_all[quart:, wide] + jnp.dot(
+        sums = sums_all[:, at] + jnp.dot(
             late_b[:quart, :], centred[:, at], preferred_element_type=jnp.float32
         )
         corr = tile_scaled(sums, delta_col, rstd_col, delta[:, at], rstd[:, at], inverse)
@@ -351,7 +413,7 @@
     down = []
     for tile in range(4):
         at = slice(tile * width, (tile + 1) * width)
-        sums = sums_all[:quart, at] + jnp.dot(
+        sums = sums_all[:, at] + jnp.dot(
             late_b[:quart, :], centred[:, at], preferred_element_type=jnp.float32
         )
         corr = tile_scaled(sums, delta_col, rstd_col, delta[:, at], rstd[:, at], inverse)
@@ -431,7 +493,7 @@
         in_specs=[smem if x.dtype == jnp.int32 else vmem for x in operands],
         out_specs=[smem if x.shape == (1, 1) else vmem for x in outs],
         scratch_shapes=scratch,
-        compiler_params=pltpu.CompilerParams(vmem_limit_bytes=20 * 2**20),
+        compiler_params=pltpu.CompilerParams(vmem_limit_bytes=24 * 2**20),
         cost_estimate=pl.CostEstimate(flops=flops, bytes_accessed=moved, transcendentals=0),
     )(*operands)
 
@@ -463,18 +525,18 @@
     def after(value, *others):
         return lax.optimization_barrier((value, *others))
 
+    first_b = along(right_outputs, pairs)
+    inner_b = along(right_outputs, middle)
+    first_a = along(left_outputs, pairs)
+    other_b0 = x_swap(right_outputs)
     other_a0 = core_swap(left_outputs)
     left_behind, other_a0 = after(left_outputs, other_a0)
-
-    first_b = along(right_outputs, pairs)
-    inner_b = along(right_outputs, middle)
-    other_b0 = x_swap(right_outputs)
-    first_a = along(left_behind, pairs)
     inner_a = along(left_behind, middle)
 
     outer_b = along(inner_b, outward)
     third_b = along(first_b, middle)
-    other_b1 = x_swap(first_b)
+    ready_b, other_b0 = after(first_b, other_b0)
+    other_b1 = x_swap(ready_b)
     outer_a = along(inner_a, outward)
     third_a = along(first_a, middle)
     other_a1 = core_swap(first_a)
@@ -488,75 +550,48 @@
     second_a, other_a1 = after(second_a, other_a1)
     other_a2 = core_swap(second_a)
 
-    def centred(blocks, shift):
-        wide = [
-            jnp.concatenate([own, other], axis=1).astype(jnp.float32) - shift
-            for own, other in blocks
-        ]
-        return wide, [x.astype(jnp.bfloat16) for x in wide]
-
-    def three_sums(wide, low):
-        return (
-            sum(jnp.sum(x, axis=0) for x in wide),
-            sum(jnp.sum(x * x, axis=0) for x in wide),
-            sum(jnp.sum(x.astype(jnp.float32), axis=0) for x in low),
-        )
-
-    def column_mean(own, other):
-        return jnp.sum(jnp.concatenate([own, other], axis=1).astype(jnp.float32), axis=0) / rows
-
-    def products(lows_a, lows_b):
-        return sum(
-            lax.dot_general(y, x, (((0,), (0,)), ((), ())), preferred_element_type=jnp.float32)
-            for x, y in zip(lows_a, lows_b)
-        )
-
-    shift_a = column_mean(left_outputs, other_a0)
-    shift_b = column_mean(right_outputs, other_b0)
-    wide_a, low_a = centred(((left_outputs, other_a0), (first_a, other_a1)), shift_a)
-    wide_b, low_b = centred(((right_outputs, other_b0), (first_b, other_b1)), shift_b)
-    total = products(low_a, low_b)
-    sums_a = three_sums(wide_a, low_a)
-    sums_b = three_sums(wide_b, low_b)
-
-    late_b = jnp.where(at_end, last_b, third_b)
-    late_b, total, sums_a, sums_b = after(late_b, total, sums_a, sums_b)
-    wide_b, low_b = centred(((second_b, other_b2),), shift_b)
-    sums_b = [x + y for x, y in zip(sums_b, three_sums(wide_b, low_b))]
-    row_b = jnp.stack([shift_b, *sums_b] + [shift_b] * 4)[:, :quart]
     gemm = 2 * rows * quart * quart
+    quarter_f32 = jax.ShapeDtypeStruct((rows, quart), jnp.float32)
+    quarter_bf16 = jax.ShapeDtypeStruct((rows, quart), jnp.bfloat16)
     extended = jax.ShapeDtypeStruct((quart + 16, rows), jnp.bfloat16)
     row_out = jax.ShapeDtypeStruct((8, quart), jnp.float32)
+    low = lambda n, m: pltpu.VMEM((n, m), jnp.bfloat16)
+    late_b = jnp.where(at_end, last_b, third_b)
     late_low_b, stats_b = local_call(
         functools.partial(late_right_kernel, batch_images),
-        (late_b, row_b),
+        (right_outputs, first_b, second_b, late_b),
         (extended, row_out),
         [],
         gemm,
     )
     late_low_other = x_swap(late_low_b)
-
-    wide_a, low_a = centred(((second_a, other_a2),), shift_a)
-    total = total + products(low_a, low_b)
-    sums_a = [x + y for x, y in zip(sums_a, three_sums(wide_a, low_a))]
-    row_a = jnp.stack([shift_a, *sums_a] + [shift_a] * 4)
-    row_own, row_other = row_a[:, :quart], row_a[:, quart:]
+    partner_own, partner_other, own_all, row_own = local_call(
+        products_kernel,
+        (left_outputs, other_a0, first_a, other_a1, second_a, other_a2)
+        + (right_outputs, other_b0, first_b, other_b1, second_b, other_b2),
+        (
+            quarter_f32,
+            quarter_f32,
+            jax.ShapeDtypeStruct((quart, half), jnp.float32),
+            row_out,
+        ),
+        [low(3 * rows, half), low(half, 3 * rows)],
+        12 * gemm,
+    )
     late_a = jnp.where(at_end, last_a, third_a)
-    late_a, total, row_own, row_other = after(late_a, total, row_own, row_other)
+    row_other = core_swap(row_own)
+    late_a, row_other = after(late_a, row_other)
     late_other = core_swap(late_a)
 
     owned_tile = jnp.where(dpos // 2 == column_halves, 0, 2) + dpos % 2
     scalars = jnp.stack([owned_tile, row_halves]).astype(jnp.int32)
-    quarter_f32 = jax.ShapeDtypeStruct((rows, quart), jnp.float32)
-    quarter_bf16 = jax.ShapeDtypeStruct((rows, quart), jnp.bfloat16)
     width = quart // 2
     mine_shape = jax.ShapeDtypeStruct((quart, width), jnp.float32)
     across_shape = jax.ShapeDtypeStruct((quart, 128), jnp.float32)
-    low = lambda n, m: pltpu.VMEM((n, m), jnp.bfloat16)
     half_scratch = [low(rows, quart), low(rows + 16, quart)]
     terms, across, dcorr_left, mine_left, vec_own = local_call(
         functools.partial(partner_kernel, batch_images, 0),
-        (scalars, late_a, left_outputs, row_own, total, late_low_other, other_b0),
+        (scalars, late_a, left_outputs, row_own, partner_own, late_low_other, other_b0),
         (
             jax.ShapeDtypeStruct((rows + 16, quart), jnp.float32),
             across_shape,
@@ -569,7 +604,8 @@
     )
     partial_right, dcorr_right, mine_right, vec_other = local_call(
         functools.partial(partner_kernel, batch_images, 1),
-        (scalars, late_other, other_a0, row_other, total, late_low_other, other_b0, terms, across),
+        (scalars, late_other, other_a0, row_other, partner_other, late_low_other, other_b0)
+        + (terms, across),
         (quarter_bf16, quarter_bf16, mine_shape, row_out),
         half_scratch,
         2 * gemm,
@@ -585,7 +621,7 @@
             other_a0,
             row_own,
             row_other,
-            total,
+            own_all,
             late_low_b,
             late_low_other,
             right_outputs,
@@ -616,10 +652,14 @@
     from_core = core_swap(partial_left)
     loss = part_loss[0, 0]
     loss = loss + core_swap(loss)
-    left_gradient = (vec_own[1] * (left_own + from_core.astype(jnp.float32))).astype(jnp.bfloat16)
+    (left_gradient,) = local_call(
+        final_kernel, (left_own, from_core, vec_own), (quarter_bf16,), [], gemm // 16
+    )
     loss, from_x = after(loss, from_x)
     loss = loss + x_swap(loss)
-    right_gradient = (stats_b[1] * (right_own + from_x.astype(jnp.float32))).astype(jnp.bfloat16)
+    (right_gradient,) = local_call(
+        final_kernel, (right_own, from_x, stats_b), (quarter_bf16,), [], gemm // 16
+    )
     return (left_gradient, right_gradient, mine[None, :, :], jnp.reshape(loss / feats, (1,)))
 
 

time: 117 us -> 111 us (0.949)
  starting transfers between devices: 37.9 us -> 26.7 us
  other arithmetic: 12.3 us -> 2.4 us
  waiting for transfers between devices: 35.2 us -> 44.6 us
  Pallas kernels: 15.6 us -> 23.2 us
  matrix products: 7.4 us -> 0 us
  local copies, waits for them, and re-layouts: 4.39 us -> 9.51 us
    ppermute x10, starting transfers between devices: 27.7 us -> 16.1 us  [along(): return lax.ppermute(block, 'dp', route)]
    ppermute x10, waiting for transfers between devices: 29.9 us -> 40.2 us  [along(): return lax.ppermute(block, 'dp', route)]
    pallas_call x4 -> x7, Pallas kernels: 15.6 us -> 23.2 us  [local_call(): pl.pallas_call(kernel, out_shape=outs, in_specs=[smem if x.dtype == jnp.i...]
    dot_general x3 -> x0, matrix products: 7.4 us -> none  [products(): lax.dot_general(y, x, (((0,), (0,)), ((), ())), preferred_element_type=jn...]
    unnamed x24 -> x38, local copies, waits for them, and re-layouts: 4.25 us -> 9.51 us
    reduce_sum x4 -> x0, other arithmetic: 3.68 us -> none  [the longest x2 2.28 us: three_sums(): jnp.sum(x.astype(jnp.float32), axis=0)]
    convert_element_type x2 -> x0, other arithmetic: 3.28 us -> none  [the longest x1 2.32 us: gathered_device(): (stats_b[1] * (right_own + from_x.astype(jnp.float32))).astype(jnp.bfloat16)]
    add x13 -> x0, other arithmetic: 2.91 us -> none  [the longest x1 2.86 us: gathered_device(): total = total + products(low_a, low_b)]
  transfers between devices with their start and end apart: 22 -> 23, of which waited for: 7 -> 8; matrix products, arithmetic and copies ran while one was open for 17% -> 2% of each run, Pallas kernels for 10% -> 18%
where the time goes in v5:
time: 111 us; the launch traced here: 110 us
  waiting for transfers between devices  44.6 us (40%)
  starting transfers between devices  26.7 us (24%)
  Pallas kernels  23.2 us (21%)
  local copies, waits for them, and re-layouts  9.51 us (9%)
  between operations  3.96 us (4%)
  other arithmetic  2.4 us (2%)
    ppermute x10, waiting for transfers between devices, along(): return lax.ppermute(block, 'dp', route)  40.2 us
    pallas_call x7, Pallas kernels, local_call(): pl.pallas_call(kernel, out_shape=outs, in_specs=[smem if x.dtype == jnp.i...  23.2 us
    ppermute x10, starting transfers between devices, along(): return lax.ppermute(block, 'dp', route)  16.1 us
    ppermute x13, starting transfers between devices, swapped(): return lax.ppermute(block, axis, route)  10.6 us
    unnamed x38, local copies, waits for them, and re-layouts  9.51 us
    ppermute x13, waiting for transfers between devices, swapped(): return lax.ppermute(block, axis, route)  4.44 us
  transfers between devices with their start and end apart: 23, of which 8 were waited for; matrix products, arithmetic and copies ran while one was open for 2% of the time, Pallas kernels for 18%

profile of v5, /device:TPU:0, one launch (start us, length us, event | category | flops | bytes accessed | tf_op | source)
XLA Modules:
  0.0 110.4 jit_solution(11431740685756914872)
XLA Ops:
  1.8 5.5 %collective-permute-start.8 = (bf16[512,512]{1,0:T(8,128)(2,1)}, bf16[512,512]{1,0:T(8,128)(2,1)S(1)}, u32[]{:S(2)}, u32[]{:S(2)}) collective-permute-start(bf16[512,512]{1,0:T(8,128)(2,1)} %first_b.1), channel_id=1, source_target_pairs={{0,4},{4,0},{8,12},{12,8},{1,5},{5,1},{9,13},{13,9},{2,6},{6,2},{1... | collective-permute-start | bytes 1572872 | tf_op jit(solution)/shard_map/ppermute | solution.py:517
  7.3 1.5 %collective-permute-start.9 = (bf16[512,512]{1,0:T(8,128)(2,1)}, bf16[512,512]{1,0:T(8,128)(2,1)S(1)}, u32[]{:S(2)}, u32[]{:S(2)}) collective-permute-start(bf16[512,512]{1,0:T(8,128)(2,1)} %first_b.1), channel_id=1, source_target_pairs={{0,2},{2,0},{1,3},{3,1},{4,6},{6,4},{5,7},{7,5},{8,10},{10,8},{9,1... | collective-permute-start | bytes 1572872 | tf_op jit(solution)/shard_map/ppermute | solution.py:19
  8.8 1.5 %collective-permute-start.4 = (bf16[512,512]{1,0:T(8,128)(2,1)}, bf16[512,512]{1,0:T(8,128)(2,1)}, u32[]{:S(2)}, u32[]{:S(2)}) collective-permute-start(bf16[512,512]{1,0:T(8,128)(2,1)} %first_own.1), channel_id=1, source_target_pairs={{4,8},{8,4},{5,9},{9,5},{6,10},{10,6},{7,11},{11,7},{20,24},{24,20... | collective-permute-start | bytes 1572872 | tf_op jit(solution)/shard_map/ppermute | solution.py:517
  10.3 1.0 collective-permute-start
  11.3 1.3 %collective-permute-start.11 = (bf16[512,512]{1,0:T(8,128)(2,1)S(1)}, bf16[512,512]{1,0:T(8,128)(2,1)}, u32[]{:S(2)}, u32[]{:S(2)}) collective-permute-start(bf16[512,512]{1,0:T(8,128)(2,1)S(1)} %collective-permute-done.10), channel_id=1, source_target_pairs={{4,0},{8,12},{5,1},{9,13},{6,2},{10,14},{7,3},{11,15},{20,16},{24,... | collective-permute-start | bytes 1572872 | tf_op jit(solution)/shard_map/ppermute | solution.py:517
  12.6 7.6 %collective-permute-done.8.refs_8_.second = bf16[512,512]{1,0:T(8,128)(2,1)S(1)} collective-permute-done((bf16[512,512]{1,0:T(8,128)(2,1)}, bf16[512,512]{1,0:T(8,128)(2,1)S(1)}, u32[]{:S(2)}, u32[]{:S(2)}) %collective-permute-start.8) | collective-permute-done | bytes 524320 | tf_op jit(solution)/shard_map/ppermute | solution.py:517
  20.2 1.5 %collective-permute-start.16 = (bf16[512,512]{1,0:T(8,128)(2,1)S(1)}, bf16[512,512]{1,0:T(8,128)(2,1)}, u32[]{:S(2)}, u32[]{:S(2)}) collective-permute-start(bf16[512,512]{1,0:T(8,128)(2,1)S(1)} %collective-permute-done.8.refs_8_.second), channel_id=1, source_target_pairs={{4,8},{8,4},{5,9},{9,5},{6,10},{10,6},{7,11},{11,7},{20,24},{24,20... | collective-permute-start | bytes 1572872 | tf_op jit(solution)/shard_map/ppermute | solution.py:517
  21.7 1.5 %collective-permute-start.12 = (bf16[512,512]{1,0:T(8,128)(2,1)S(1)}, bf16[512,512]{1,0:T(8,128)(2,1)S(1)}, u32[]{:S(2)}, u32[]{:S(2)}) collective-permute-start(bf16[512,512]{1,0:T(8,128)(2,1)S(1)} %collective-permute-done.8.refs_8_.second), channel_id=1, source_target_pairs={{0,2},{2,0},{1,3},{3,1},{4,6},{6,4},{5,7},{7,5},{8,10},{10,8},{9,1... | collective-permute-start | bytes 1572872 | tf_op jit(solution)/shard_map/ppermute | solution.py:19
  23.2 1.3 %collective-permute-start.5 = (bf16[512,512]{1,0:T(8,128)(2,1)}, bf16[512,512]{1,0:T(8,128)(2,1)}, u32[]{:S(2)}, u32[]{:S(2)}) collective-permute-start(bf16[512,512]{1,0:T(8,128)(2,1)} %collective-permute-done.4), channel_id=1, source_target_pairs={{4,0},{8,12},{5,1},{9,13},{6,2},{10,14},{7,3},{11,15},{20,16},{24,... | collective-permute-start | bytes 1572872 | tf_op jit(solution)/shard_map/ppermute | solution.py:517
  24.5 6.9 %collective-permute-done.refs_2_ = bf16[512,512]{1,0:T(8,128)(2,1)S(1)} collective-permute-done((bf16[512,512]{1,0:T(8,128)(2,1)}, bf16[512,512]{1,0:T(8,128)(2,1)S(1)}, u32[]{:S(2)}, u32[]{:S(2)}) %collective-permute-start) | collective-permute-done | bytes 524320 | tf_op jit(solution)/shard_map/ppermute | solution.py:517
  31.4 11.3 %collective-permute-done.11 = bf16[512,512]{1,0:T(8,128)(2,1)} collective-permute-done((bf16[512,512]{1,0:T(8,128)(2,1)S(1)}, bf16[512,512]{1,0:T(8,128)(2,1)}, u32[]{:S(2)}, u32[]{:S(2)}) %collective-permute-start.11) | collective-permute-done | bytes 524320 | tf_op jit(solution)/shard_map/ppermute | solution.py:517
  43.5 1.3 %collective-permute-start.17 = (bf16[512,512]{1,0:T(8,128)(2,1)}, bf16[512,512]{1,0:T(8,128)(2,1)S(1)}, u32[]{:S(2)}, u32[]{:S(2)}) collective-permute-start(bf16[512,512]{1,0:T(8,128)(2,1)} %collective-permute-done.16), channel_id=1, source_target_pairs={{4,0},{8,12},{5,1},{9,13},{6,2},{10,14},{7,3},{11,15},{20,16},{24,... | collective-permute-start | bytes 1572872 | tf_op jit(solution)/shard_map/ppermute | solution.py:517
  44.8 1.1 %broadcast_select_fusion.1.refs_10_.third = bf16[512,512]{1,0:T(8,128)(2,1)S(1)} fusion(bf16[512,512]{1,0:T(8,128)(2,1)} %collective-permute-done.11, bf16[512,512]{1,0:T(8,128)(2,1)S(1)} %collective-permute-done.10, pred[]{:T(512)S(6)} %or.3), kind=kLoop, calls=%fused_computation.1 | loop fusion | flops 262144 | bytes 1572865 | tf_op jit(solution)/shard_map/jit(_where)/select_n | solution.py:545
  46.7 1.5 %collective-permute-start.13 = (bf16[512,512]{1,0:T(8,128)(2,1)S(1)}, bf16[512,512]{1,0:T(8,128)(2,1)S(1)}, u32[]{:S(2)}, u32[]{:S(2)}) collective-permute-start(bf16[512,512]{1,0:T(8,128)(2,1)S(1)} %broadcast_select_fusion.1.refs_10_.third), channel_id=1, source_target_pairs={{0,2},{2,0},{1,3},{3,1},{4,6},{6,4},{5,7},{7,5},{8,10},{10,8},{9,1... | collective-permute-start | bytes 1572872 | tf_op jit(solution)/shard_map/ppermute | solution.py:19
  48.2 5.8 %collective-permute-done.5 = bf16[512,512]{1,0:T(8,128)(2,1)} collective-permute-done((bf16[512,512]{1,0:T(8,128)(2,1)}, bf16[512,512]{1,0:T(8,128)(2,1)}, u32[]{:S(2)}, u32[]{:S(2)}) %collective-permute-start.5) | collective-permute-done | bytes 524320 | tf_op jit(solution)/shard_map/ppermute | solution.py:517
  54.0 1.1 broadcast_select_fusion.2.refs_4_
  55.2 1.4 %collective-permute-start.2 = (bf16[512,512]{1,0:T(8,128)(2,1)S(1)}, bf16[512,512]{1,0:T(8,128)(2,1)S(1)}, u32[]{:S(2)}, u32[]{:S(2)}) collective-permute-start(bf16[512,512]{1,0:T(8,128)(2,1)S(1)} %collective-permute-done.1), channel_id=1, source_target_pairs={{4,0},{8,12},{5,1},{9,13},{6,2},{10,14},{7,3},{11,15},{20,16},{24,... | collective-permute-start | bytes 1572872 | tf_op jit(solution)/shard_map/ppermute | solution.py:517
  56.7 8.5 %collective-permute-done.17 = bf16[512,512]{1,0:T(8,128)(2,1)S(1)} collective-permute-done((bf16[512,512]{1,0:T(8,128)(2,1)}, bf16[512,512]{1,0:T(8,128)(2,1)S(1)}, u32[]{:S(2)}, u32[]{:S(2)}) %collective-permute-start.17) | collective-permute-done | bytes 524320 | tf_op jit(solution)/shard_map/ppermute | solution.py:517
  65.2 2.2 %shard_map.58 = (bf16[528,512]{1,0:T(8,128)(2,1)}, f32[8,512]{1,0:T(8,128)S(1)}) custom-call(bf16[512,512]{1,0:T(8,128)(2,1)S(1)} %copy-done.1, bf16[512,512]{1,0:T(8,128)(2,1)S(1)} %collective-permute-done.8.refs_8_.second, bf16[512,512]{1,0:T(8,128)(2,1)S(1)} %broadcast_select_fusion.1.refs_10_.third, bf16[512,512]{1,0:T(8,128)(2,1)S(1)} %broadcast_select_fusion.late), custom_call_target="tpu_custom_call" | custom-call | flops 268435456 | bytes 2654208 | tf_op jit(solution)/shard_map/pallas_call | solution.py:490
  67.4 1.5 %collective-permute-start.18 = (bf16[528,512]{1,0:T(8,128)(2,1)}, bf16[528,512]{1,0:T(8,128)(2,1)S(1)}, u32[]{:S(2)}, u32[]{:S(2)}) collective-permute-start(bf16[528,512]{1,0:T(8,128)(2,1)} %get-tuple-element.48.late_b), channel_id=1, source_target_pairs={{0,2},{2,0},{1,3},{3,1},{4,6},{6,4},{5,7},{7,5},{8,10},{10,8},{9,1... | collective-permute-start | bytes 1622024 | tf_op jit(solution)/shard_map/ppermute | solution.py:19
  70.0 4.3 %shard_map.57 = (f32[512,512]{1,0:T(8,128)S(1)}, f32[512,512]{1,0:T(8,128)S(1)}, f32[512,1024]{1,0:T(8,128)S(1)}, f32[8,512]{1,0:T(8,128)S(1)}) custom-call(bf16[512,512]{1,0:T(8,128)(2,1)S(1)} %copy-done, bf16[512,512]{1,0:T(8,128)(2,1)S(1)} %collective-permute-done.3.refs_1_.first.first_other, bf16[512,512]{1,0:T(8,128)(2,1)S(1)} %copy-done.16, ...), custom_call_target="tpu_custom_call" | custom-call | flops 3221225472 | bytes 10502144 | tf_op jit(solution)/shard_map/pallas_call | solution.py:490
  74.3 1.3 %copy-done.3 = f32[512,1024]{1,0:T(8,128)} copy-done((f32[512,1024]{1,0:T(8,128)}, f32[512,1024]{1,0:T(8,128)S(1)}, u32[]{:S(2)}) %copy-start.3) | copy-done | bytes 2097176
  78.1 3.0 %collective-permute-done.18.late_b.late_b_other = bf16[528,512]{1,0:T(8,128)(2,1)S(1)} collective-permute-done((bf16[528,512]{1,0:T(8,128)(2,1)}, bf16[528,512]{1,0:T(8,128)(2,1)S(1)}, u32[]{:S(2)}, u32[]{:S(2)}) %collective-permute-start.18) | collective-permute-done | bytes 540704 | tf_op jit(solution)/shard_map/ppermute | solution.py:19
  81.1 1.2 %copy-done.8 = f32[512,512]{1,0:T(8,128)S(1)} copy-done((f32[512,512]{1,0:T(8,128)S(1)}, f32[512,512]{1,0:T(8,128)}, u32[]{:S(2)}) %copy-start.8) | copy-done | bytes 1048600
  82.3 2.4 %shard_map.59 = (f32[528,512]{1,0:T(8,128)S(1)}, f32[512,128]{1,0:T(8,128)S(1)}, bf16[512,512]{1,0:T(8,128)(2,1)S(1)}, f32[512,256]{1,0:T(8,128)S(1)}, f32[8,512]{1,0:T(8,128)S(1)}) custom-call(s32[2]{0:T(128)S(1)} %pad_add_fusion.own_tile, bf16[512,512]{1,0:T(8,128)(2,1)S(1)} %broadcast_select_fusion.3.late.late_own, bf16[512,512]{1,0:T(8,128)(2,1)S(1)} %copy-done, ...), custom_call_target="tpu_custom_call" | custom-call | flops 536870912 | bytes 5586952 | tf_op jit(solution)/shard_map/pallas_call | solution.py:490
  84.7 3.6 %shard_map.60 = (bf16[512,512]{1,0:T(8,128)(2,1)}, bf16[512,512]{1,0:T(8,128)(2,1)S(1)}, f32[512,256]{1,0:T(8,128)S(1)}, f32[8,512]{1,0:T(8,128)S(1)}) custom-call(s32[2]{0:T(128)S(1)} %pad_add_fusion.own_tile, bf16[512,512]{1,0:T(8,128)(2,1)S(1)} %collective-permute-done.15.late.late_other, ...), custom_call_target="tpu_custom_call" | custom-call | flops 536870912 | bytes 6111240 | tf_op jit(solution)/shard_map/pallas_call | solution.py:490
  88.4 1.5 %collective-permute-start.21 = (bf16[512,512]{1,0:T(8,128)(2,1)}, bf16[512,512]{1,0:T(8,128)(2,1)}, u32[]{:S(2)}, u32[]{:S(2)}) collective-permute-start(bf16[512,512]{1,0:T(8,128)(2,1)} %get-tuple-element.63), channel_id=1, source_target_pairs={{0,2},{2,0},{1,3},{3,1},{4,6},{6,4},{5,7},{7,5},{8,10},{10,8},{9,1... | collective-permute-start | bytes 1572872 | tf_op jit(solution)/shard_map/ppermute | solution.py:19
  89.9 7.8 %shard_map.61 = (f32[512,512]{1,0:T(8,128)S(1)}, f32[512,512]{1,0:T(8,128)S(1)}, bf16[512,512]{1,0:T(8,128)(2,1)}, f32[256,1024]{1,0:T(8,128)}, f32[1,1]{1,0:T(1,128)}) custom-call(s32[2]{0:T(128)S(1)} %pad_add_fusion.own_tile, bf16[512,512]{1,0:T(8,128)(2,1)S(1)} %broadcast_select_fusion.3.late.late_own, ...), custom_call_target="tpu_custom_call" | custom-call | flops 2147483648 | bytes 12156940 | tf_op jit(solution)/shard_map/pallas_call | solution.py:490
  100.2 1.2 %collective-permute-done.20 = f32[]{:T(128)} collective-permute-done((f32[]{:T(128)}, f32[]{:T(128)}, u32[]{:S(2)}, u32[]{:S(2)}) %collective-permute-start.20) | collective-permute-done | bytes 36 | tf_op jit(solution)/shard_map/ppermute | solution.py:19
  102.6 1.9 %collective-permute-start.22 = (f32[]{:T(128)}, f32[]{:T(128)}, u32[]{:S(2)}, u32[]{:S(2)}) collective-permute-start(f32[]{:T(128)} %add.21), channel_id=1, source_target_pairs={{0,2},{2,0},{1,3},{3,1},{4,6},{6,4},{5,7},{7,5},{8,10},{10,8},{9,1... | collective-permute-start | bytes 20 | tf_op jit(solution)/shard_map/ppermute | solution.py:19
  104.5 1.2 %copy-done.12 = f32[512,512]{1,0:T(8,128)S(1)} copy-done((f32[512,512]{1,0:T(8,128)S(1)}, f32[512,512]{1,0:T(8,128)}, u32[]{:S(2)}) %copy-start.12) | copy-done | bytes 1048600
  105.7 2.0 %shard_map.63 = bf16[512,512]{1,0:T(8,128)(2,1)} custom-call(f32[512,512]{1,0:T(8,128)S(1)} %copy-done.12, bf16[512,512]{1,0:T(8,128)(2,1)} %collective-permute-done.21.other, f32[8,512]{1,0:T(8,128)S(1)} %get-tuple-element.65.stats), custom_call_target="tpu_custom_call" | custom-call | flops 16777216 | bytes 2113536 | tf_op jit(solution)/shard_map/pallas_call | solution.py:490
  (64 shorter events, 9.7 us)
Async XLA Ops:
  0.6 8.2 %collective-permute-start.3 = (bf16[512,512]{1,0:T(8,128)(2,1)}, bf16[512,512]{1,0:T(8,128)(2,1)S(1)}, u32[]{:S(2)}, u32[]{:S(2)}) collective-permute-start(bf16[512,512]{1,0:T(8,128)(2,1)} %first_own.1), channel_id=1, source_target_pairs={{0,1},{1,0},{2,3},{3,2},{4,5},{5,4},{6,7},{7,6},{8,9},{9,8},{10,11... | collective-permute-start | bytes 1572872 | tf_op jit(solution)/shard_map/ppermute | solution.py:19
  1.1 10.1 %collective-permute-start.10 = (bf16[512,512]{1,0:T(8,128)(2,1)}, bf16[512,512]{1,0:T(8,128)(2,1)S(1)}, u32[]{:S(2)}, u32[]{:S(2)}) collective-permute-start(bf16[512,512]{1,0:T(8,128)(2,1)} %first_b.1), channel_id=1, source_target_pairs={{4,8},{8,4},{5,9},{9,5},{6,10},{10,6},{7,11},{11,7},{20,24},{24,20... | collective-permute-start | bytes 1572872 | tf_op jit(solution)/shard_map/ppermute | solution.py:517
  1.8 18.4 %collective-permute-start.8 = (bf16[512,512]{1,0:T(8,128)(2,1)}, bf16[512,512]{1,0:T(8,128)(2,1)S(1)}, u32[]{:S(2)}, u32[]{:S(2)}) collective-permute-start(bf16[512,512]{1,0:T(8,128)(2,1)} %first_b.1), channel_id=1, source_target_pairs={{0,4},{4,0},{8,12},{12,8},{1,5},{5,1},{9,13},{13,9},{2,6},{6,2},{1... | collective-permute-start | bytes 1572872 | tf_op jit(solution)/shard_map/ppermute | solution.py:517
  7.3 14.4 %collective-permute-start.9 = (bf16[512,512]{1,0:T(8,128)(2,1)}, bf16[512,512]{1,0:T(8,128)(2,1)S(1)}, u32[]{:S(2)}, u32[]{:S(2)}) collective-permute-start(bf16[512,512]{1,0:T(8,128)(2,1)} %first_b.1), channel_id=1, source_target_pairs={{0,2},{2,0},{1,3},{3,1},{4,6},{6,4},{5,7},{7,5},{8,10},{10,8},{9,1... | collective-permute-start | bytes 1572872 | tf_op jit(solution)/shard_map/ppermute | solution.py:19
  8.8 14.4 %collective-permute-start.4 = (bf16[512,512]{1,0:T(8,128)(2,1)}, bf16[512,512]{1,0:T(8,128)(2,1)}, u32[]{:S(2)}, u32[]{:S(2)}) collective-permute-start(bf16[512,512]{1,0:T(8,128)(2,1)} %first_own.1), channel_id=1, source_target_pairs={{4,8},{8,4},{5,9},{9,5},{6,10},{10,6},{7,11},{11,7},{20,24},{24,20... | collective-permute-start | bytes 1572872 | tf_op jit(solution)/shard_map/ppermute | solution.py:517
  10.3 21.2 %collective-permute-start = (bf16[512,512]{1,0:T(8,128)(2,1)}, bf16[512,512]{1,0:T(8,128)(2,1)S(1)}, u32[]{:S(2)}, u32[]{:S(2)}) collective-permute-start(bf16[512,512]{1,0:T(8,128)(2,1)} %first_own.1), channel_id=1, source_target_pairs={{0,4},{4,0},{8,12},{12,8},{1,5},{5,1},{9,13},{13,9},{2,6},{6,2},{1... | collective-permute-start | bytes 1572872 | tf_op jit(solution)/shard_map/ppermute | solution.py:517
  11.3 31.5 %collective-permute-start.11 = (bf16[512,512]{1,0:T(8,128)(2,1)S(1)}, bf16[512,512]{1,0:T(8,128)(2,1)}, u32[]{:S(2)}, u32[]{:S(2)}) collective-permute-start(bf16[512,512]{1,0:T(8,128)(2,1)S(1)} %collective-permute-done.10), channel_id=1, source_target_pairs={{4,0},{8,12},{5,1},{9,13},{6,2},{10,14},{7,3},{11,15},{20,16},{24,... | collective-permute-start | bytes 1572872 | tf_op jit(solution)/shard_map/ppermute | solution.py:517
  20.2 45.0 %copy-start.13 = (bf16[512,512]{1,0:T(8,128)(2,1)}, bf16[512,512]{1,0:T(8,128)(2,1)S(1)}, u32[]{:S(2)}) copy-start(bf16[512,512]{1,0:T(8,128)(2,1)S(1)} %collective-permute-done.8.refs_8_.second) | copy-start | bytes 1572868
  20.2 23.3 %collective-permute-start.16 = (bf16[512,512]{1,0:T(8,128)(2,1)S(1)}, bf16[512,512]{1,0:T(8,128)(2,1)}, u32[]{:S(2)}, u32[]{:S(2)}) collective-permute-start(bf16[512,512]{1,0:T(8,128)(2,1)S(1)} %collective-permute-done.8.refs_8_.second), channel_id=1, source_target_pairs={{4,8},{8,4},{5,9},{9,5},{6,10},{10,6},{7,11},{11,7},{20,24},{24,20... | collective-permute-start | bytes 1572872 | tf_op jit(solution)/shard_map/ppermute | solution.py:517
  21.7 24.2 %collective-permute-start.12 = (bf16[512,512]{1,0:T(8,128)(2,1)S(1)}, bf16[512,512]{1,0:T(8,128)(2,1)S(1)}, u32[]{:S(2)}, u32[]{:S(2)}) collective-permute-start(bf16[512,512]{1,0:T(8,128)(2,1)S(1)} %collective-permute-done.8.refs_8_.second), channel_id=1, source_target_pairs={{0,2},{2,0},{1,3},{3,1},{4,6},{6,4},{5,7},{7,5},{8,10},{10,8},{9,1... | collective-permute-start | bytes 1572872 | tf_op jit(solution)/shard_map/ppermute | solution.py:19
  23.2 30.8 %collective-permute-start.5 = (bf16[512,512]{1,0:T(8,128)(2,1)}, bf16[512,512]{1,0:T(8,128)(2,1)}, u32[]{:S(2)}, u32[]{:S(2)}) collective-permute-start(bf16[512,512]{1,0:T(8,128)(2,1)} %collective-permute-done.4), channel_id=1, source_target_pairs={{4,0},{8,12},{5,1},{9,13},{6,2},{10,14},{7,3},{11,15},{20,16},{24,... | collective-permute-start | bytes 1572872 | tf_op jit(solution)/shard_map/ppermute | solution.py:517
  24.5 40.7 %copy-start.1 = (bf16[512,512]{1,0:T(8,128)(2,1)S(1)}, bf16[512,512]{1,0:T(8,128)(2,1)}, u32[]{:S(2)}) copy-start(bf16[512,512]{1,0:T(8,128)(2,1)} %first_b.1) | copy-start | bytes 1572868
  31.4 25.2 %copy-start.15 = (bf16[512,512]{1,0:T(8,128)(2,1)}, bf16[512,512]{1,0:T(8,128)(2,1)S(1)}, u32[]{:S(2)}) copy-start(bf16[512,512]{1,0:T(8,128)(2,1)S(1)} %collective-permute-done.refs_2_) | copy-start | bytes 1572868
  31.4 23.7 %collective-permute-start.6 = (bf16[512,512]{1,0:T(8,128)(2,1)S(1)}, bf16[512,512]{1,0:T(8,128)(2,1)S(1)}, u32[]{:S(2)}, u32[]{:S(2)}) collective-permute-start(bf16[512,512]{1,0:T(8,128)(2,1)S(1)} %collective-permute-done.refs_2_), channel_id=1, source_target_pairs={{0,1},{1,0},{2,3},{3,2},{4,5},{5,4},{6,7},{7,6},{8,9},{9,8},{10,11... | collective-permute-start | bytes 1572872 | tf_op jit(solution)/shard_map/ppermute | solution.py:19
  42.8 12.5 %collective-permute-start.1 = (bf16[512,512]{1,0:T(8,128)(2,1)S(1)}, bf16[512,512]{1,0:T(8,128)(2,1)S(1)}, u32[]{:S(2)}, u32[]{:S(2)}) collective-permute-start(bf16[512,512]{1,0:T(8,128)(2,1)S(1)} %collective-permute-done.refs_2_), channel_id=1, source_target_pairs={{4,8},{8,4},{5,9},{9,5},{6,10},{10,6},{7,11},{11,7},{20,24},{24,20... | collective-permute-start | bytes 1572872 | tf_op jit(solution)/shard_map/ppermute | solution.py:517
  43.5 21.7 %collective-permute-start.17 = (bf16[512,512]{1,0:T(8,128)(2,1)}, bf16[512,512]{1,0:T(8,128)(2,1)S(1)}, u32[]{:S(2)}, u32[]{:S(2)}) collective-permute-start(bf16[512,512]{1,0:T(8,128)(2,1)} %collective-permute-done.16), channel_id=1, source_target_pairs={{4,0},{8,12},{5,1},{9,13},{6,2},{10,14},{7,3},{11,15},{20,16},{24,... | collective-permute-start | bytes 1572872 | tf_op jit(solution)/shard_map/ppermute | solution.py:517
  46.7 22.2 %collective-permute-start.13 = (bf16[512,512]{1,0:T(8,128)(2,1)S(1)}, bf16[512,512]{1,0:T(8,128)(2,1)S(1)}, u32[]{:S(2)}, u32[]{:S(2)}) collective-permute-start(bf16[512,512]{1,0:T(8,128)(2,1)S(1)} %broadcast_select_fusion.1.refs_10_.third), channel_id=1, source_target_pairs={{0,2},{2,0},{1,3},{3,1},{4,6},{6,4},{5,7},{7,5},{8,10},{10,8},{9,1... | collective-permute-start | bytes 1572872 | tf_op jit(solution)/shard_map/ppermute | solution.py:19
  55.1 13.8 %copy-start = (bf16[512,512]{1,0:T(8,128)(2,1)S(1)}, bf16[512,512]{1,0:T(8,128)(2,1)}, u32[]{:S(2)}) copy-start(bf16[512,512]{1,0:T(8,128)(2,1)} %first_own.1) | copy-start | bytes 1572868
  55.1 13.8 %copy-start.18 = (bf16[512,512]{1,0:T(8,128)(2,1)S(1)}, bf16[512,512]{1,0:T(8,128)(2,1)}, u32[]{:S(2)}) copy-start(bf16[512,512]{1,0:T(8,128)(2,1)} %copy-done.17) | copy-start | bytes 1572868
  55.2 13.8 %collective-permute-start.7 = (bf16[512,512]{1,0:T(8,128)(2,1)S(1)}, bf16[512,512]{1,0:T(8,128)(2,1)S(1)}, u32[]{:S(2)}, u32[]{:S(2)}) collective-permute-start(bf16[512,512]{1,0:T(8,128)(2,1)S(1)} %broadcast_select_fusion.2.refs_4_), channel_id=1, source_target_pairs={{0,1},{1,0},{2,3},{3,2},{4,5},{5,4},{6,7},{7,6},{8,9},{9,8},{10,11... | collective-permute-start | bytes 1572872 | tf_op jit(solution)/shard_map/ppermute | solution.py:19
  55.2 21.4 %collective-permute-start.2 = (bf16[512,512]{1,0:T(8,128)(2,1)S(1)}, bf16[512,512]{1,0:T(8,128)(2,1)S(1)}, u32[]{:S(2)}, u32[]{:S(2)}) collective-permute-start(bf16[512,512]{1,0:T(8,128)(2,1)S(1)} %collective-permute-done.1), channel_id=1, source_target_pairs={{4,0},{8,12},{5,1},{9,13},{6,2},{10,14},{7,3},{11,15},{20,16},{24,... | collective-permute-start | bytes 1572872 | tf_op jit(solution)/shard_map/ppermute | solution.py:517
  67.4 13.7 %collective-permute-start.18 = (bf16[528,512]{1,0:T(8,128)(2,1)}, bf16[528,512]{1,0:T(8,128)(2,1)S(1)}, u32[]{:S(2)}, u32[]{:S(2)}) collective-permute-start(bf16[528,512]{1,0:T(8,128)(2,1)} %get-tuple-element.48.late_b), channel_id=1, source_target_pairs={{0,2},{2,0},{1,3},{3,1},{4,6},{6,4},{5,7},{7,5},{8,10},{10,8},{9,1... | collective-permute-start | bytes 1622024 | tf_op jit(solution)/shard_map/ppermute | solution.py:19
  76.6 1.2 %collective-permute-start.14 = (f32[8,512]{1,0:T(8,128)S(1)}, f32[8,512]{1,0:T(8,128)S(1)}, u32[]{:S(2)}, u32[]{:S(2)}) collective-permute-start(f32[8,512]{1,0:T(8,128)S(1)} %get-tuple-element.44.row.row_own), channel_id=1, source_target_pairs={{0,1},{1,0},{2,3},{3,2},{4,5},{5,4},{6,7},{7,6},{8,9},{9,8},{10,11... | collective-permute-start | bytes 49160 | tf_op jit(solution)/shard_map/ppermute | solution.py:19
  77.8 6.9 %collective-permute-start.15 = (bf16[512,512]{1,0:T(8,128)(2,1)S(1)}, bf16[512,512]{1,0:T(8,128)(2,1)S(1)}, u32[]{:S(2)}, u32[]{:S(2)}) collective-permute-start(bf16[512,512]{1,0:T(8,128)(2,1)S(1)} %broadcast_select_fusion.3.late.late_own), channel_id=1, source_target_pairs={{0,1},{1,0},{2,3},{3,2},{4,5},{5,4},{6,7},{7,6},{8,9},{9,8},{10,11... | collective-permute-start | bytes 1572872 | tf_op jit(solution)/shard_map/ppermute | solution.py:19
  78.0 6.7 %copy-start.6 = (f32[512,512]{1,0:T(8,128)S(1)}, f32[512,512]{1,0:T(8,128)}, u32[]{:S(2)}) copy-start(f32[512,512]{1,0:T(8,128)} %copy-done.5) | copy-start | bytes 3145732
  84.7 5.2 %copy-start.2 = (bf16[512,512]{1,0:T(8,128)(2,1)S(1)}, bf16[512,512]{1,0:T(8,128)(2,1)}, u32[]{:S(2)}) copy-start(bf16[512,512]{1,0:T(8,128)(2,1)} %first_b.1) | copy-start | bytes 1572868
  84.7 5.2 %copy-start.4 = (f32[512,1024]{1,0:T(8,128)S(1)}, f32[512,1024]{1,0:T(8,128)}, u32[]{:S(2)}) copy-start(f32[512,1024]{1,0:T(8,128)} %copy-done.3) | copy-start | bytes 6291460
  88.4 14.2 %collective-permute-start.21 = (bf16[512,512]{1,0:T(8,128)(2,1)}, bf16[512,512]{1,0:T(8,128)(2,1)}, u32[]{:S(2)}, u32[]{:S(2)}) collective-permute-start(bf16[512,512]{1,0:T(8,128)(2,1)} %get-tuple-element.63), channel_id=1, source_target_pairs={{0,2},{2,0},{1,3},{3,1},{4,6},{6,4},{5,7},{7,5},{8,10},{10,8},{9,1... | collective-permute-start | bytes 1572872 | tf_op jit(solution)/shard_map/ppermute | solution.py:19
  99.7 8.0 %copy-start.10 = (f32[512,512]{1,0:T(8,128)S(1)}, f32[512,512]{1,0:T(8,128)}, u32[]{:S(2)}) copy-start(f32[512,512]{1,0:T(8,128)} %copy-done.9) | copy-start | bytes 3145732
  99.7 8.0 %collective-permute-start.19 = (bf16[512,512]{1,0:T(8,128)(2,1)}, bf16[512,512]{1,0:T(8,128)(2,1)S(1)}, u32[]{:S(2)}, u32[]{:S(2)}) collective-permute-start(bf16[512,512]{1,0:T(8,128)(2,1)} %get-tuple-element.60), channel_id=1, source_target_pairs={{0,1},{1,0},{2,3},{3,2},{4,5},{5,4},{6,7},{7,6},{8,9},{9,8},{10,11... | collective-permute-start | bytes 1572872 | tf_op jit(solution)/shard_map/ppermute | solution.py:19
  99.7 1.7 %collective-permute-start.20 = (f32[]{:T(128)}, f32[]{:T(128)}, u32[]{:S(2)}, u32[]{:S(2)}) collective-permute-start(f32[]{:T(128)} %bitcast.2), channel_id=1, source_target_pairs={{0,1},{1,0},{2,3},{3,2},{4,5},{5,4},{6,7},{7,6},{8,9},{9,8},{10,11... | collective-permute-start | bytes 20 | tf_op jit(solution)/shard_map/ppermute | solution.py:19
  102.6 6.0 %collective-permute-start.22 = (f32[]{:T(128)}, f32[]{:T(128)}, u32[]{:S(2)}, u32[]{:S(2)}) collective-permute-start(f32[]{:T(128)} %add.21), channel_id=1, source_target_pairs={{0,2},{2,0},{1,3},{3,1},{4,6},{6,4},{5,7},{7,5},{8,10},{10,8},{9,1... | collective-permute-start | bytes 20 | tf_op jit(solution)/shard_map/ppermute | solution.py:19
  (10 other events, 13.4 us)

commit v6 on v5

--- a/solution.py
+++ b/solution.py
@@ -221,9 +221,11 @@
 
 def late_right_kernel(images, first, second, third, late, out, stats):
     rows, quart = late.shape
+    first = first()
     shift = column_mean(first)
     sums = [jnp.zeros((8, quart), jnp.float32)] * 3
     for block in (first, second, third, late):
+        block = block() if callable(block) else block
         for at in range(0, rows, 128):
             centred = block[at : at + 128, :].astype(jnp.float32) - shift
             low = centred.astype(jnp.bfloat16)
@@ -242,14 +244,15 @@
 def products_kernel(*refs):
     lefts, rights = refs[0:6], refs[6:12]
     partner_own, partner_other, own_all, row_own, low_left, low_right = refs[12:]
-    rows, quart = lefts[0].shape
+    lefts, rights = [[x if callable(x) else (lambda x=x: x) for x in xs] for xs in (lefts, rights)]
+    rows, quart = lefts[0]().shape
     width = quart // 2
     for half in range(2):
         lanes = slice(half * quart, (half + 1) * quart)
-        shift = column_mean(lefts[half])
+        shift = column_mean(lefts[half]())
         sums = [jnp.zeros((8, quart), jnp.float32)] * 3
         for block in range(3):
-            source = lefts[2 * block + half]
+            source = lefts[2 * block + half]()
             for at in range(0, rows, 64):
                 centred = source[at : at + 64, :].astype(jnp.float32) - shift
                 low = centred.astype(jnp.bfloat16)
@@ -262,9 +265,9 @@
             row_own[...] = jnp.concatenate([shift, *sums, zeros], axis=0)
     for half in range(2):
         lanes = slice(half * quart, (half + 1) * quart)
-        shift = column_mean(rights[half])
+        shift = column_mean(rights[half]())
         for block in range(3):
-            source = rights[2 * block + half]
+            source = rights[2 * block + half]()
             for at in range(0, rows, 128):
                 low = (source[at : at + 128, :].astype(jnp.float32) - shift).astype(jnp.bfloat16)
                 low_right[lanes, block * rows + at : block * rows + at + 128] = jnp.transpose(low)
@@ -272,25 +275,32 @@
         wide = slice(tile * width, (tile + 1) * width)
         inner = slice((tile % 2) * width, (tile % 2 + 1) * width)
         target = partner_own if tile < 2 else partner_other
-        target[:, inner] = jnp.dot(
+        target.buffer[:, inner] = jnp.dot(
             low_right[quart:, :], low_left[:, wide], preferred_element_type=jnp.float32
         )
-        own_all[:, wide] = jnp.dot(
+        if tile % 2:
+            target.send()
+    for tile in range(4):
+        wide = slice(tile * width, (tile + 1) * width)
+        own_all.buffer[:, wide] = jnp.dot(
             low_right[:quart, :], low_left[:, wide], preferred_element_type=jnp.float32
         )
+    own_all.send()
 
 
 def final_kernel(own, other, stats, out):
-    rows = own.shape[0]
+    rows = other.shape[0]
+    own = own()
     for at in range(0, rows, 64):
         piece = slice(at, at + 64)
         value = stats[1:2, :] * (own[piece, :] + other[piece, :].astype(jnp.float32))
         out[piece, :] = value.astype(jnp.bfloat16)
 
 
-def partner_kernel(images, part, own_tile, late, first, row, sums_all, late_b, first_b, *refs):
+def partner_kernel(images, part, own_tile, late, first, row, sums_all, late_b, *refs):
     if part:
-        (terms_in, across_in, partial_out, dcorr_out, mine_out, vec_out, centred, norms) = refs
+        (first_b, terms_in, across_in, *refs) = refs
+        (partial_out, dcorr_out, mine_out, vec_out, centred, norms) = refs
     else:
         (terms_out, across_out, dcorr_out, mine_out, vec_out, centred, norms) = refs
     rows, quart = late.shape
@@ -299,9 +309,10 @@
     everything = slice(0, quart)
     sums = centre_rows(late, shift, centred, everything, 64)
     delta, rstd, rest = moments([row[i + 1 : i + 2, :] + sums[i] for i in range(3)], images)
-    normalise_rows(first, shift + delta, rstd, norms, everything, 64)
+    normalise_rows(first(), shift + delta, rstd, norms, everything, 64)
     norms[rows : rows + 16, :] = jnp.broadcast_to(rest, (16, quart)).astype(jnp.bfloat16)
 
+    sums_all = sums_all()
     offset_b, rstd_b, _, delta_b = joined_parts(late_b, quart)
     columns = jnp.transpose(
         jnp.concatenate([delta_b, rstd_b, jnp.zeros((6, quart), jnp.float32)], axis=0)
@@ -342,7 +353,7 @@
         )
         if part:
             terms = terms + terms_in[:, at]
-            xhat = (first_b[:, at].astype(jnp.float32) - offset_b[:, at]) * rstd_b[:, at]
+            xhat = (first_b()[:, at].astype(jnp.float32) - offset_b[:, at]) * rstd_b[:, at]
             partial_out[:, at] = (
                 terms[:rows] - terms[rows : rows + 1] - xhat * second[:, at]
             ).astype(jnp.bfloat16)
@@ -384,6 +395,9 @@
     rows, quart = late_own.shape
     half = 2 * quart
     inverse = 1.0 / images
+    first_own, first_other, late_b, first_b, first_b_other, sums_all = [
+        x() for x in (first_own, first_other, late_b, first_b, first_b_other, sums_all)
+    ]
     both = lambda i: jnp.concatenate([vec_own[i : i + 1, :], vec_other[i : i + 1, :]], axis=1)
     delta, rstd, rest, second_partner = [both(i) for i in range(4)]
     shift = jnp.concatenate([row_own[0:1, :], row_other[0:1, :]], axis=1)
@@ -453,7 +467,7 @@
         xhat = (source[:, inner].astype(jnp.float32) - offset[:, at]) * rstd[:, at]
         value = terms[:rows] - terms[rows : rows + 1] - xhat * second_a[:, at]
         if tile < 2:
-            left_out[:, inner] = value
+            left_out.buffer[:, inner] = value
         else:
             left_partial_out[:, inner] = value.astype(jnp.bfloat16)
 
@@ -464,7 +478,9 @@
             norms[...], dcorr_own[at, :], contract, preferred_element_type=jnp.float32
         )
         xhat = (first_b[:, at].astype(jnp.float32) - own_b[0][:, at]) * own_b[1][:, at]
-        right_out[:, at] = terms[:rows] - terms[rows : rows + 1] - xhat * second_b[:, at]
+        right_out.buffer[:, at] = terms[:rows] - terms[rows : rows + 1] - xhat * second_b[:, at]
+    left_out.send()
+    right_out.send()
 
     own_columns = jnp.transpose(mine_own[...])
     in_left = own_tile[0] < 2
@@ -485,17 +501,66 @@
 smem = pl.BlockSpec(memory_space=pltpu.SMEM)
 
 
-def local_call(kernel, operands, outs, scratch, flops, specs=None):
+class Result:
+    def __init__(self, buffer, copy):
+        self.buffer = buffer
+        self.send = copy.start
+        self.wait = copy.wait
+
+
+def local_call(kernel, operands, outs, scratch, flops, fetched=(), sent=()):
     moved = sum(x.size * x.dtype.itemsize for x in (*operands, *outs))
+    hbm = pl.BlockSpec(memory_space=pltpu.HBM)
+
+    def in_space(i, x):
+        return smem if x.dtype == jnp.int32 else hbm if i in fetched else vmem
+
+    def out_space(i, x):
+        return smem if x.shape == (1, 1) else hbm if i in sent else vmem
+
+    def body(*refs):
+        count, total = len(operands), len(operands) + len(outs)
+        ins, results = list(refs[:count]), list(refs[count:total])
+        staging, sems = refs[total + len(scratch) : -1], refs[-1]
+        for slot, i in enumerate(fetched):
+            copy = pltpu.make_async_copy(ins[i], staging[slot], sems.at[slot])
+            copy.start()
+
+            def arrived(waiting=[copy], buffer=staging[slot]):
+                if waiting:
+                    waiting.pop().wait()
+                return buffer
+
+            ins[i] = arrived
+        for slot, i in enumerate(sent, len(fetched)):
+            results[i] = Result(
+                staging[slot], pltpu.make_async_copy(staging[slot], results[i], sems.at[slot])
+            )
+        kernel(*ins, *results, *refs[total : total + len(scratch)])
+        for i in fetched:
+            ins[i]()
+        for i in sent:
+            results[i].wait()
+
+    buffers = [operands[i] for i in fetched] + [outs[i] for i in sent]
     return pl.pallas_call(
-        kernel,
-        out_shape=outs,
-        in_specs=[smem if x.dtype == jnp.int32 else vmem for x in operands],
-        out_specs=[smem if x.shape == (1, 1) else vmem for x in outs],
-        scratch_shapes=scratch,
-        compiler_params=pltpu.CompilerParams(vmem_limit_bytes=24 * 2**20),
+        body,
+        out_shape=[pltpu.HBM(x.shape, x.dtype) if i in sent else x for i, x in enumerate(outs)],
+        in_specs=[in_space(i, x) for i, x in enumerate(operands)],
+        out_specs=[out_space(i, x) for i, x in enumerate(outs)],
+        scratch_shapes=[
+            *scratch,
+            *(pltpu.VMEM(x.shape, x.dtype) for x in buffers),
+            pltpu.SemaphoreType.DMA((max(len(buffers), 1),)),
+        ],
+        compiler_params=pltpu.CompilerParams(vmem_limit_bytes=28 * 2**20),
         cost_estimate=pl.CostEstimate(flops=flops, bytes_accessed=moved, transcendentals=0),
-    )(*operands)
+    )(
+        *(
+            pltpu.with_memory_space_constraint(x, pltpu.HBM) if i in fetched else x
+            for i, x in enumerate(operands)
+        )
+    )
 
 
 def gathered_device(left_outputs, right_outputs):
@@ -530,7 +595,7 @@
     first_a = along(left_outputs, pairs)
     other_b0 = x_swap(right_outputs)
     other_a0 = core_swap(left_outputs)
-    left_behind, other_a0 = after(left_outputs, other_a0)
+    left_behind, first_a = after(left_outputs, first_a)
     inner_a = along(left_behind, middle)
 
     outer_b = along(inner_b, outward)
@@ -563,6 +628,7 @@
         (extended, row_out),
         [],
         gemm,
+        fetched=(0, 1, 2),
     )
     late_low_other = x_swap(late_low_b)
     partner_own, partner_other, own_all, row_own = local_call(
@@ -577,6 +643,8 @@
         ),
         [low(3 * rows, half), low(half, 3 * rows)],
         12 * gemm,
+        fetched=(0, 1, 2, 3, 6, 7, 8, 9, 10),
+        sent=(0, 1, 2),
     )
     late_a = jnp.where(at_end, last_a, third_a)
     row_other = core_swap(row_own)
@@ -591,7 +659,7 @@
     half_scratch = [low(rows, quart), low(rows + 16, quart)]
     terms, across, dcorr_left, mine_left, vec_own = local_call(
         functools.partial(partner_kernel, batch_images, 0),
-        (scalars, late_a, left_outputs, row_own, partner_own, late_low_other, other_b0),
+        (scalars, late_a, left_outputs, row_own, partner_own, late_low_other),
         (
             jax.ShapeDtypeStruct((rows + 16, quart), jnp.float32),
             across_shape,
@@ -601,6 +669,7 @@
         ),
         half_scratch,
         2 * gemm,
+        fetched=(2, 4),
     )
     partial_right, dcorr_right, mine_right, vec_other = local_call(
         functools.partial(partner_kernel, batch_images, 1),
@@ -609,6 +678,7 @@
         (quarter_bf16, quarter_bf16, mine_shape, row_out),
         half_scratch,
         2 * gemm,
+        fetched=(2, 4, 6),
     )
     from_x = x_swap(partial_right)
     right_own, left_own, partial_left, mine, part_loss = local_call(
@@ -648,17 +718,19 @@
             pltpu.VMEM((quart, width), jnp.float32),
         ],
         8 * gemm,
+        fetched=(3, 4, 8, 10, 11, 7),
+        sent=(0, 1),
     )
     from_core = core_swap(partial_left)
     loss = part_loss[0, 0]
     loss = loss + core_swap(loss)
     (left_gradient,) = local_call(
-        final_kernel, (left_own, from_core, vec_own), (quarter_bf16,), [], gemm // 16
+        final_kernel, (left_own, from_core, vec_own), (quarter_bf16,), [], gemm // 16, fetched=(0,)
     )
     loss, from_x = after(loss, from_x)
     loss = loss + x_swap(loss)
     (right_gradient,) = local_call(
-        final_kernel, (right_own, from_x, stats_b), (quarter_bf16,), [], gemm // 16
+        final_kernel, (right_own, from_x, stats_b), (quarter_bf16,), [], gemm // 16, fetched=(0,)
     )
     return (left_gradient, right_gradient, mine[None, :, :], jnp.reshape(loss / feats, (1,)))
 

time: 111 us -> 108 us (0.973)
  Pallas kernels: 23.2 us -> 32.9 us
  local copies, waits for them, and re-layouts: 9.51 us -> 0.79 us
  waiting for transfers between devices: 44.6 us -> 41.5 us
    pallas_call x7, Pallas kernels: 23.2 us -> 32.9 us  [local_call(): pl.pallas_call(body, out_shape=[pltpu.HBM(x.shape, x.dtype) if i in sent...]
    unnamed x38 -> x10, local copies, waits for them, and re-layouts: 9.51 us -> 0.79 us
    ppermute x10, waiting for transfers between devices: 40.2 us -> 38.4 us  [along(): return lax.ppermute(block, 'dp', route)]
    ppermute x13, waiting for transfers between devices: 4.44 us -> 3.08 us  [swapped(): return lax.ppermute(block, axis, route)]
    ppermute x13, starting transfers between devices: 10.6 us -> 11.9 us  [swapped(): return lax.ppermute(block, axis, route)]
  transfers between devices with their start and end apart: 23 -> 23, of which waited for: 8 -> 9; matrix products, arithmetic and copies ran while one was open for 2% -> 1% of each run, Pallas kernels for 18% -> 26%
where the time goes in v6:
time: 108 us
  waiting for transfers between devices  41.5 us (38%)
  Pallas kernels  32.9 us (30%)
  starting transfers between devices  27.3 us (25%)
  between operations  3.89 us (4%)
  other arithmetic  1.34 us (1%)
    ppermute x10, waiting for transfers between devices, along(): return lax.ppermute(block, 'dp', route)  38.4 us
    pallas_call x7, Pallas kernels, local_call(): pl.pallas_call(body, out_shape=[pltpu.HBM(x.shape, x.dtype) if i in sent...  32.9 us
    ppermute x10, starting transfers between devices, along(): return lax.ppermute(block, 'dp', route)  15.4 us
    ppermute x13, starting transfers between devices, swapped(): return lax.ppermute(block, axis, route)  11.9 us
    ppermute x13, waiting for transfers between devices, swapped(): return lax.ppermute(block, axis, route)  3.08 us
  transfers between devices with their start and end apart: 23, of which 9 were waited for; matrix products, arithmetic and copies ran while one was open for 1% of the time, Pallas kernels for 26%

profile of v6, /device:TPU:0, one launch (start us, length us, event | category | flops | bytes accessed | tf_op | source)
XLA Modules:
  0.0 107.8 jit_solution(2838206989658449613)
XLA Ops:
  0.6 3.1 %collective-permute-start = (bf16[512,512]{1,0:T(8,128)(2,1)}, bf16[512,512]{1,0:T(8,128)(2,1)}, u32[]{:S(2)}, u32[]{:S(2)}) collective-permute-start(bf16[512,512]{1,0:T(8,128)(2,1)} %refs_3_.1), channel_id=1, source_target_pairs={{0,4},{4,0},{8,12},{12,8},{1,5},{5,1},{9,13},{13,9},{2,6},{6,2},{1... | collective-permute-start | bytes 1572872 | tf_op jit(solution)/shard_map/ppermute | solution.py:582
  3.7 0.7 collective-permute-start.10
  4.4 4.4 %collective-permute-start.8 = (bf16[512,512]{1,0:T(8,128)(2,1)}, bf16[512,512]{1,0:T(8,128)(2,1)}, u32[]{:S(2)}, u32[]{:S(2)}) collective-permute-start(bf16[512,512]{1,0:T(8,128)(2,1)} %refs_10_.1), channel_id=1, source_target_pairs={{0,4},{4,0},{8,12},{12,8},{1,5},{5,1},{9,13},{13,9},{2,6},{6,2},{1... | collective-permute-start | bytes 1572872 | tf_op jit(solution)/shard_map/ppermute | solution.py:582
  8.8 1.5 %collective-permute-start.9 = (bf16[512,512]{1,0:T(8,128)(2,1)}, bf16[512,512]{1,0:T(8,128)(2,1)S(1)}, u32[]{:S(2)}, u32[]{:S(2)}) collective-permute-start(bf16[512,512]{1,0:T(8,128)(2,1)} %refs_10_.1), channel_id=1, source_target_pairs={{0,2},{2,0},{1,3},{3,1},{4,6},{6,4},{5,7},{7,5},{8,10},{10,8},{9,1... | collective-permute-start | bytes 1572872 | tf_op jit(solution)/shard_map/ppermute | solution.py:19
  10.3 6.5 %collective-permute-done.refs_2_ = bf16[512,512]{1,0:T(8,128)(2,1)} collective-permute-done((bf16[512,512]{1,0:T(8,128)(2,1)}, bf16[512,512]{1,0:T(8,128)(2,1)}, u32[]{:S(2)}, u32[]{:S(2)}) %collective-permute-start) | collective-permute-done | bytes 524320 | tf_op jit(solution)/shard_map/ppermute | solution.py:582
  16.8 0.7 collective-permute-start.4
  17.5 1.3 %collective-permute-start.11 = (bf16[512,512]{1,0:T(8,128)(2,1)S(1)}, bf16[512,512]{1,0:T(8,128)(2,1)S(1)}, u32[]{:S(2)}, u32[]{:S(2)}) collective-permute-start(bf16[512,512]{1,0:T(8,128)(2,1)S(1)} %collective-permute-done.10), channel_id=1, source_target_pairs={{4,0},{8,12},{5,1},{9,13},{6,2},{10,14},{7,3},{11,15},{20,16},{24,... | collective-permute-start | bytes 1572872 | tf_op jit(solution)/shard_map/ppermute | solution.py:582
  18.8 9.2 %collective-permute-done.8.refs_8_.refs_1_ = bf16[512,512]{1,0:T(8,128)(2,1)} collective-permute-done((bf16[512,512]{1,0:T(8,128)(2,1)}, bf16[512,512]{1,0:T(8,128)(2,1)}, u32[]{:S(2)}, u32[]{:S(2)}) %collective-permute-start.8) | collective-permute-done | bytes 524320 | tf_op jit(solution)/shard_map/ppermute | solution.py:582
  28.0 0.7 collective-permute-start.16
  28.7 2.0 %collective-permute-start.12 = (bf16[512,512]{1,0:T(8,128)(2,1)}, bf16[512,512]{1,0:T(8,128)(2,1)}, u32[]{:S(2)}, u32[]{:S(2)}) collective-permute-start(bf16[512,512]{1,0:T(8,128)(2,1)} %collective-permute-done.8.refs_8_.refs_1_), channel_id=1, source_target_pairs={{0,2},{2,0},{1,3},{3,1},{4,6},{6,4},{5,7},{7,5},{8,10},{10,8},{9,1... | collective-permute-start | bytes 1572872 | tf_op jit(solution)/shard_map/ppermute | solution.py:19
  30.8 1.3 %collective-permute-start.5 = (bf16[512,512]{1,0:T(8,128)(2,1)S(1)}, bf16[512,512]{1,0:T(8,128)(2,1)}, u32[]{:S(2)}, u32[]{:S(2)}) collective-permute-start(bf16[512,512]{1,0:T(8,128)(2,1)S(1)} %collective-permute-done.4), channel_id=1, source_target_pairs={{4,0},{8,12},{5,1},{9,13},{6,2},{10,14},{7,3},{11,15},{20,16},{24,... | collective-permute-start | bytes 1572872 | tf_op jit(solution)/shard_map/ppermute | solution.py:582
  32.2 7.0 %collective-permute-done.11 = bf16[512,512]{1,0:T(8,128)(2,1)S(1)} collective-permute-done((bf16[512,512]{1,0:T(8,128)(2,1)S(1)}, bf16[512,512]{1,0:T(8,128)(2,1)S(1)}, u32[]{:S(2)}, u32[]{:S(2)}) %collective-permute-start.11) | collective-permute-done | bytes 524320 | tf_op jit(solution)/shard_map/ppermute | solution.py:582
  39.2 0.7 collective-permute-start.1
  39.9 1.3 %collective-permute-start.17 = (bf16[512,512]{1,0:T(8,128)(2,1)S(1)}, bf16[512,512]{1,0:T(8,128)(2,1)S(1)}, u32[]{:S(2)}, u32[]{:S(2)}) collective-permute-start(bf16[512,512]{1,0:T(8,128)(2,1)S(1)} %collective-permute-done.16), channel_id=1, source_target_pairs={{4,0},{8,12},{5,1},{9,13},{6,2},{10,14},{7,3},{11,15},{20,16},{24,... | collective-permute-start | bytes 1572872 | tf_op jit(solution)/shard_map/ppermute | solution.py:582
  41.4 9.1 %collective-permute-done.5 = bf16[512,512]{1,0:T(8,128)(2,1)} collective-permute-done((bf16[512,512]{1,0:T(8,128)(2,1)S(1)}, bf16[512,512]{1,0:T(8,128)(2,1)}, u32[]{:S(2)}, u32[]{:S(2)}) %collective-permute-start.5) | collective-permute-done | bytes 524320 | tf_op jit(solution)/shard_map/ppermute | solution.py:582
  50.5 2.0 %collective-permute-start.13 = (bf16[512,512]{1,0:T(8,128)(2,1)S(1)}, bf16[512,512]{1,0:T(8,128)(2,1)S(1)}, u32[]{:S(2)}, u32[]{:S(2)}) collective-permute-start(bf16[512,512]{1,0:T(8,128)(2,1)S(1)} %broadcast_select_fusion.1.refs_10_.refs_2_), channel_id=1, source_target_pairs={{0,2},{2,0},{1,3},{3,1},{4,6},{6,4},{5,7},{7,5},{8,10},{10,8},{9,1... | collective-permute-start | bytes 1572872 | tf_op jit(solution)/shard_map/ppermute | solution.py:19
  52.5 1.1 %broadcast_select_fusion.2.refs_4_ = bf16[512,512]{1,0:T(8,128)(2,1)S(1)} fusion(bf16[512,512]{1,0:T(8,128)(2,1)} %collective-permute-done.5, bf16[512,512]{1,0:T(8,128)(2,1)S(1)} %collective-permute-done.4, pred[]{:T(512)S(6)} %or.3), kind=kLoop, calls=%fused_computation.2 | loop fusion | flops 262144 | bytes 1572865 | tf_op jit(solution)/shard_map/jit(_where)/select_n | solution.py:614
  53.7 1.3 %collective-permute-start.2 = (bf16[512,512]{1,0:T(8,128)(2,1)S(1)}, bf16[512,512]{1,0:T(8,128)(2,1)S(1)}, u32[]{:S(2)}, u32[]{:S(2)}) collective-permute-start(bf16[512,512]{1,0:T(8,128)(2,1)S(1)} %collective-permute-done.1), channel_id=1, source_target_pairs={{4,0},{8,12},{5,1},{9,13},{6,2},{10,14},{7,3},{11,15},{20,16},{24,... | collective-permute-start | bytes 1572872 | tf_op jit(solution)/shard_map/ppermute | solution.py:582
  55.0 6.6 %collective-permute-done.17 = bf16[512,512]{1,0:T(8,128)(2,1)S(1)} collective-permute-done((bf16[512,512]{1,0:T(8,128)(2,1)S(1)}, bf16[512,512]{1,0:T(8,128)(2,1)S(1)}, u32[]{:S(2)}, u32[]{:S(2)}) %collective-permute-start.17) | collective-permute-done | bytes 524320 | tf_op jit(solution)/shard_map/ppermute | solution.py:582
  61.7 2.4 %shard_map.58 = (bf16[528,512]{1,0:T(8,128)(2,1)S(1)}, f32[8,512]{1,0:T(8,128)S(1)}) custom-call(bf16[512,512]{1,0:T(8,128)(2,1)} %refs_10_.1, bf16[512,512]{1,0:T(8,128)(2,1)} %collective-permute-done.8.refs_8_.refs_1_, bf16[512,512]{1,0:T(8,128)(2,1)} %copy-done.3, bf16[512,512]{1,0:T(8,128)(2,1)S(1)} %broadcast_select_fusion.refs_3_), custom_call_target="tpu_custom_call" | custom-call | flops 268435456 | bytes 2654208 | tf_op jit(solution)/shard_map/pallas_call | solution.py:546
  64.1 2.0 %collective-permute-start.18 = (bf16[528,512]{1,0:T(8,128)(2,1)S(1)}, bf16[528,512]{1,0:T(8,128)(2,1)S(1)}, u32[]{:S(2)}, u32[]{:S(2)}) collective-permute-start(bf16[528,512]{1,0:T(8,128)(2,1)S(1)} %get-tuple-element.48.refs_8_), channel_id=1, source_target_pairs={{0,2},{2,0},{1,3},{3,1},{4,6},{6,4},{5,7},{7,5},{8,10},{10,8},{9,1... | collective-permute-start | bytes 1622024 | tf_op jit(solution)/shard_map/ppermute | solution.py:19
  66.2 0.8 copy-done.2
  67.0 8.2 %shard_map.57 = (f32[512,512]{1,0:T(8,128)}, f32[512,512]{1,0:T(8,128)}, f32[512,1024]{1,0:T(8,128)}, f32[8,512]{1,0:T(8,128)S(1)}) custom-call(bf16[512,512]{1,0:T(8,128)(2,1)} %refs_3_.1, bf16[512,512]{1,0:T(8,128)(2,1)} %copy-done.2, bf16[512,512]{1,0:T(8,128)(2,1)} %collective-permute-done.refs_2_, bf16[512,512]{1,0:T(8,128)(2,1)} %copy-done.4, ...), custom_call_target="tpu_custom_call" | custom-call | flops 3221225472 | bytes 10502144 | tf_op jit(solution)/shard_map/pallas_call | solution.py:546
  75.3 1.1 %collective-permute-done.14.refs_3_.refs_6_ = f32[8,512]{1,0:T(8,128)S(1)} collective-permute-done((f32[8,512]{1,0:T(8,128)S(1)}, f32[8,512]{1,0:T(8,128)S(1)}, u32[]{:S(2)}, u32[]{:S(2)}) %collective-permute-start.14) | collective-permute-done | bytes 16416 | tf_op jit(solution)/shard_map/ppermute | solution.py:19
  76.8 3.4 %shard_map.59 = (f32[528,512]{1,0:T(8,128)S(1)}, f32[512,128]{1,0:T(8,128)S(1)}, bf16[512,512]{1,0:T(8,128)(2,1)S(1)}, f32[512,256]{1,0:T(8,128)S(1)}, f32[8,512]{1,0:T(8,128)S(1)}) custom-call(s32[2]{0:T(128)S(1)} %pad_add_fusion.refs_0_, bf16[512,512]{1,0:T(8,128)(2,1)S(1)} %broadcast_select_fusion.3.refs_1_, bf16[512,512]{1,0:T(8,128)(2,1)} %refs_3_.1, ...), custom_call_target="tpu_custom_call" | custom-call | flops 536870912 | bytes 5062664 | tf_op jit(solution)/shard_map/pallas_call | solution.py:546
  80.3 4.3 %shard_map.60 = (bf16[512,512]{1,0:T(8,128)(2,1)S(1)}, bf16[512,512]{1,0:T(8,128)(2,1)S(1)}, f32[512,256]{1,0:T(8,128)S(1)}, f32[8,512]{1,0:T(8,128)S(1)}) custom-call(s32[2]{0:T(128)S(1)} %pad_add_fusion.refs_0_, bf16[512,512]{1,0:T(8,128)(2,1)S(1)} %collective-permute-done.15.refs_1_.refs_2_, bf16[512,512]{1,0:T(8,128)(2,1)} %copy-done.2, ...), custom_call_target="tpu_custom_call" | custom-call | flops 536870912 | bytes 6111240 | tf_op jit(solution)/shard_map/pallas_call | solution.py:546
  84.6 1.4 %collective-permute-start.21 = (bf16[512,512]{1,0:T(8,128)(2,1)S(1)}, bf16[512,512]{1,0:T(8,128)(2,1)S(1)}, u32[]{:S(2)}, u32[]{:S(2)}) collective-permute-start(bf16[512,512]{1,0:T(8,128)(2,1)S(1)} %get-tuple-element.63), channel_id=1, source_target_pairs={{0,2},{2,0},{1,3},{3,1},{4,6},{6,4},{5,7},{7,5},{8,10},{10,8},{9,1... | collective-permute-start | bytes 1572872 | tf_op jit(solution)/shard_map/ppermute | solution.py:19
  86.0 10.2 %shard_map.61 = (f32[512,512]{1,0:T(8,128)}, f32[512,512]{1,0:T(8,128)}, bf16[512,512]{1,0:T(8,128)(2,1)S(1)}, f32[256,1024]{1,0:T(8,128)}, f32[1,1]{1,0:T(1,128)}) custom-call(s32[2]{0:T(128)S(1)} %pad_add_fusion.refs_0_, bf16[512,512]{1,0:T(8,128)(2,1)S(1)} %broadcast_select_fusion.3.refs_1_, bf16[512,512]{1,0:T(8,128)(2,1)S(1)} %collective-permute-done.15.refs_1_.refs_2_, ...), custom_call_target="tpu_custom_call" | custom-call | flops 2147483648 | bytes 12156940 | tf_op jit(solution)/shard_map/pallas_call | solution.py:546
  96.8 1.6 %collective-permute-done.20 = f32[]{:T(128)} collective-permute-done((f32[]{:T(128)}, f32[]{:T(128)}, u32[]{:S(2)}, u32[]{:S(2)}) %collective-permute-start.20) | collective-permute-done | bytes 36 | tf_op jit(solution)/shard_map/ppermute | solution.py:19
  99.7 2.1 %collective-permute-start.22 = (f32[]{:T(128)}, f32[]{:T(128)}, u32[]{:S(2)}, u32[]{:S(2)}) collective-permute-start(f32[]{:T(128)} %add.21), channel_id=1, source_target_pairs={{0,2},{2,0},{1,3},{3,1},{4,6},{6,4},{5,7},{7,5},{8,10},{10,8},{9,1... | collective-permute-start | bytes 20 | tf_op jit(solution)/shard_map/ppermute | solution.py:19
  101.7 2.1 %shard_map.63 = bf16[512,512]{1,0:T(8,128)(2,1)} custom-call(f32[512,512]{1,0:T(8,128)} %get-tuple-element.61.refs_0_, bf16[512,512]{1,0:T(8,128)(2,1)S(1)} %collective-permute-done.21.refs_1_, f32[8,512]{1,0:T(8,128)S(1)} %get-tuple-element.65.refs_2_), custom_call_target="tpu_custom_call" | custom-call | flops 16777216 | bytes 2113536 | tf_op jit(solution)/shard_map/pallas_call | solution.py:546
  103.9 2.1 %shard_map.62 = bf16[512,512]{1,0:T(8,128)(2,1)} custom-call(f32[512,512]{1,0:T(8,128)} %get-tuple-element.59.refs_0_, bf16[512,512]{1,0:T(8,128)(2,1)S(1)} %collective-permute-done.19.refs_1_, f32[8,512]{1,0:T(8,128)S(1)} %get-tuple-element.57.refs_16_.refs_2_), custom_call_target="tpu_custom_call" | custom-call | flops 16777216 | bytes 2113536 | tf_op jit(solution)/shard_map/pallas_call | solution.py:546
  (36 shorter events, 1.6 us)
Async XLA Ops:
  0.6 16.2 %collective-permute-start = (bf16[512,512]{1,0:T(8,128)(2,1)}, bf16[512,512]{1,0:T(8,128)(2,1)}, u32[]{:S(2)}, u32[]{:S(2)}) collective-permute-start(bf16[512,512]{1,0:T(8,128)(2,1)} %refs_3_.1), channel_id=1, source_target_pairs={{0,4},{4,0},{8,12},{12,8},{1,5},{5,1},{9,13},{13,9},{2,6},{6,2},{1... | collective-permute-start | bytes 1572872 | tf_op jit(solution)/shard_map/ppermute | solution.py:582
  3.7 13.8 %collective-permute-start.10 = (bf16[512,512]{1,0:T(8,128)(2,1)}, bf16[512,512]{1,0:T(8,128)(2,1)S(1)}, u32[]{:S(2)}, u32[]{:S(2)}) collective-permute-start(bf16[512,512]{1,0:T(8,128)(2,1)} %refs_10_.1), channel_id=1, source_target_pairs={{4,8},{8,4},{5,9},{9,5},{6,10},{10,6},{7,11},{11,7},{20,24},{24,20... | collective-permute-start | bytes 1572872 | tf_op jit(solution)/shard_map/ppermute | solution.py:582
  4.4 23.6 %collective-permute-start.8 = (bf16[512,512]{1,0:T(8,128)(2,1)}, bf16[512,512]{1,0:T(8,128)(2,1)}, u32[]{:S(2)}, u32[]{:S(2)}) collective-permute-start(bf16[512,512]{1,0:T(8,128)(2,1)} %refs_10_.1), channel_id=1, source_target_pairs={{0,4},{4,0},{8,12},{12,8},{1,5},{5,1},{9,13},{13,9},{2,6},{6,2},{1... | collective-permute-start | bytes 1572872 | tf_op jit(solution)/shard_map/ppermute | solution.py:582
  8.8 19.9 %collective-permute-start.9 = (bf16[512,512]{1,0:T(8,128)(2,1)}, bf16[512,512]{1,0:T(8,128)(2,1)S(1)}, u32[]{:S(2)}, u32[]{:S(2)}) collective-permute-start(bf16[512,512]{1,0:T(8,128)(2,1)} %refs_10_.1), channel_id=1, source_target_pairs={{0,2},{2,0},{1,3},{3,1},{4,6},{6,4},{5,7},{7,5},{8,10},{10,8},{9,1... | collective-permute-start | bytes 1572872 | tf_op jit(solution)/shard_map/ppermute | solution.py:19
  16.8 14.0 %collective-permute-start.4 = (bf16[512,512]{1,0:T(8,128)(2,1)}, bf16[512,512]{1,0:T(8,128)(2,1)S(1)}, u32[]{:S(2)}, u32[]{:S(2)}) collective-permute-start(bf16[512,512]{1,0:T(8,128)(2,1)} %refs_3_.1), channel_id=1, source_target_pairs={{4,8},{8,4},{5,9},{9,5},{6,10},{10,6},{7,11},{11,7},{20,24},{24,20... | collective-permute-start | bytes 1572872 | tf_op jit(solution)/shard_map/ppermute | solution.py:582
  17.5 21.7 %collective-permute-start.11 = (bf16[512,512]{1,0:T(8,128)(2,1)S(1)}, bf16[512,512]{1,0:T(8,128)(2,1)S(1)}, u32[]{:S(2)}, u32[]{:S(2)}) collective-permute-start(bf16[512,512]{1,0:T(8,128)(2,1)S(1)} %collective-permute-done.10), channel_id=1, source_target_pairs={{4,0},{8,12},{5,1},{9,13},{6,2},{10,14},{7,3},{11,15},{20,16},{24,... | collective-permute-start | bytes 1572872 | tf_op jit(solution)/shard_map/ppermute | solution.py:582
  28.0 11.8 %collective-permute-start.16 = (bf16[512,512]{1,0:T(8,128)(2,1)}, bf16[512,512]{1,0:T(8,128)(2,1)S(1)}, u32[]{:S(2)}, u32[]{:S(2)}) collective-permute-start(bf16[512,512]{1,0:T(8,128)(2,1)} %collective-permute-done.8.refs_8_.refs_1_), channel_id=1, source_target_pairs={{4,8},{8,4},{5,9},{9,5},{6,10},{10,6},{7,11},{11,7},{20,24},{24,20... | collective-permute-start | bytes 1572872 | tf_op jit(solution)/shard_map/ppermute | solution.py:582
  28.7 33.0 %copy-start.1 = (bf16[512,512]{1,0:T(8,128)(2,1)}, bf16[512,512]{1,0:T(8,128)(2,1)S(1)}, u32[]{:S(2)}) copy-start(bf16[512,512]{1,0:T(8,128)(2,1)S(1)} %collective-permute-done.9.refs_7_.refs_6_.refs_11_) | copy-start | bytes 1572868
  28.7 12.7 %collective-permute-start.12 = (bf16[512,512]{1,0:T(8,128)(2,1)}, bf16[512,512]{1,0:T(8,128)(2,1)}, u32[]{:S(2)}, u32[]{:S(2)}) collective-permute-start(bf16[512,512]{1,0:T(8,128)(2,1)} %collective-permute-done.8.refs_8_.refs_1_), channel_id=1, source_target_pairs={{0,2},{2,0},{1,3},{3,1},{4,6},{6,4},{5,7},{7,5},{8,10},{10,8},{9,1... | collective-permute-start | bytes 1572872 | tf_op jit(solution)/shard_map/ppermute | solution.py:19
  30.8 19.7 %collective-permute-start.5 = (bf16[512,512]{1,0:T(8,128)(2,1)S(1)}, bf16[512,512]{1,0:T(8,128)(2,1)}, u32[]{:S(2)}, u32[]{:S(2)}) collective-permute-start(bf16[512,512]{1,0:T(8,128)(2,1)S(1)} %collective-permute-done.4), channel_id=1, source_target_pairs={{4,0},{8,12},{5,1},{9,13},{6,2},{10,14},{7,3},{11,15},{20,16},{24,... | collective-permute-start | bytes 1572872 | tf_op jit(solution)/shard_map/ppermute | solution.py:582
  32.1 21.5 %collective-permute-start.6 = (bf16[512,512]{1,0:T(8,128)(2,1)}, bf16[512,512]{1,0:T(8,128)(2,1)S(1)}, u32[]{:S(2)}, u32[]{:S(2)}) collective-permute-start(bf16[512,512]{1,0:T(8,128)(2,1)} %collective-permute-done.refs_2_), channel_id=1, source_target_pairs={{0,1},{1,0},{2,3},{3,2},{4,5},{5,4},{6,7},{7,6},{8,9},{9,8},{10,11... | collective-permute-start | bytes 1572872 | tf_op jit(solution)/shard_map/ppermute | solution.py:19
  39.2 14.5 %collective-permute-start.1 = (bf16[512,512]{1,0:T(8,128)(2,1)}, bf16[512,512]{1,0:T(8,128)(2,1)S(1)}, u32[]{:S(2)}, u32[]{:S(2)}) collective-permute-start(bf16[512,512]{1,0:T(8,128)(2,1)} %collective-permute-done.refs_2_), channel_id=1, source_target_pairs={{4,8},{8,4},{5,9},{9,5},{6,10},{10,6},{7,11},{11,7},{20,24},{24,20... | collective-permute-start | bytes 1572872 | tf_op jit(solution)/shard_map/ppermute | solution.py:582
  39.9 21.8 %collective-permute-start.17 = (bf16[512,512]{1,0:T(8,128)(2,1)S(1)}, bf16[512,512]{1,0:T(8,128)(2,1)S(1)}, u32[]{:S(2)}, u32[]{:S(2)}) collective-permute-start(bf16[512,512]{1,0:T(8,128)(2,1)S(1)} %collective-permute-done.16), channel_id=1, source_target_pairs={{4,0},{8,12},{5,1},{9,13},{6,2},{10,14},{7,3},{11,15},{20,16},{24,... | collective-permute-start | bytes 1572872 | tf_op jit(solution)/shard_map/ppermute | solution.py:582
  41.2 20.5 %copy-start.3 = (bf16[512,512]{1,0:T(8,128)(2,1)}, bf16[512,512]{1,0:T(8,128)(2,1)S(1)}, u32[]{:S(2)}) copy-start(bf16[512,512]{1,0:T(8,128)(2,1)S(1)} %broadcast_select_fusion.1.refs_10_.refs_2_) | copy-start | bytes 1572868
  41.4 24.8 %collective-permute-start.3 = (bf16[512,512]{1,0:T(8,128)(2,1)}, bf16[512,512]{1,0:T(8,128)(2,1)S(1)}, u32[]{:S(2)}, u32[]{:S(2)}) collective-permute-start(bf16[512,512]{1,0:T(8,128)(2,1)} %refs_3_.1), channel_id=1, source_target_pairs={{0,1},{1,0},{2,3},{3,2},{4,5},{5,4},{6,7},{7,6},{8,9},{9,8},{10,11... | collective-permute-start | bytes 1572872 | tf_op jit(solution)/shard_map/ppermute | solution.py:19
  50.5 15.7 %collective-permute-start.13 = (bf16[512,512]{1,0:T(8,128)(2,1)S(1)}, bf16[512,512]{1,0:T(8,128)(2,1)S(1)}, u32[]{:S(2)}, u32[]{:S(2)}) collective-permute-start(bf16[512,512]{1,0:T(8,128)(2,1)S(1)} %broadcast_select_fusion.1.refs_10_.refs_2_), channel_id=1, source_target_pairs={{0,2},{2,0},{1,3},{3,1},{4,6},{6,4},{5,7},{7,5},{8,10},{10,8},{9,1... | collective-permute-start | bytes 1572872 | tf_op jit(solution)/shard_map/ppermute | solution.py:19
  53.6 12.6 %copy-start.4 = (bf16[512,512]{1,0:T(8,128)(2,1)}, bf16[512,512]{1,0:T(8,128)(2,1)S(1)}, u32[]{:S(2)}) copy-start(bf16[512,512]{1,0:T(8,128)(2,1)S(1)} %collective-permute-done.6.refs_3_) | copy-start | bytes 1572868
  53.6 12.6 %collective-permute-start.7 = (bf16[512,512]{1,0:T(8,128)(2,1)S(1)}, bf16[512,512]{1,0:T(8,128)(2,1)S(1)}, u32[]{:S(2)}, u32[]{:S(2)}) collective-permute-start(bf16[512,512]{1,0:T(8,128)(2,1)S(1)} %broadcast_select_fusion.2.refs_4_), channel_id=1, source_target_pairs={{0,1},{1,0},{2,3},{3,2},{4,5},{5,4},{6,7},{7,6},{8,9},{9,8},{10,11... | collective-permute-start | bytes 1572872 | tf_op jit(solution)/shard_map/ppermute | solution.py:19
  53.7 21.6 %collective-permute-start.2 = (bf16[512,512]{1,0:T(8,128)(2,1)S(1)}, bf16[512,512]{1,0:T(8,128)(2,1)S(1)}, u32[]{:S(2)}, u32[]{:S(2)}) collective-permute-start(bf16[512,512]{1,0:T(8,128)(2,1)S(1)} %collective-permute-done.1), channel_id=1, source_target_pairs={{4,0},{8,12},{5,1},{9,13},{6,2},{10,14},{7,3},{11,15},{20,16},{24,... | collective-permute-start | bytes 1572872 | tf_op jit(solution)/shard_map/ppermute | solution.py:582
  64.1 11.0 %copy-start = (bf16[528,512]{1,0:T(8,128)(2,1)}, bf16[528,512]{1,0:T(8,128)(2,1)S(1)}, u32[]{:S(2)}) copy-start(bf16[528,512]{1,0:T(8,128)(2,1)S(1)} %get-tuple-element.48.refs_8_) | copy-start | bytes 1622020
  64.1 12.7 %collective-permute-start.18 = (bf16[528,512]{1,0:T(8,128)(2,1)S(1)}, bf16[528,512]{1,0:T(8,128)(2,1)S(1)}, u32[]{:S(2)}, u32[]{:S(2)}) collective-permute-start(bf16[528,512]{1,0:T(8,128)(2,1)S(1)} %get-tuple-element.48.refs_8_), channel_id=1, source_target_pairs={{0,2},{2,0},{1,3},{3,1},{4,6},{6,4},{5,7},{7,5},{8,10},{10,8},{9,1... | collective-permute-start | bytes 1622024 | tf_op jit(solution)/shard_map/ppermute | solution.py:19
  66.2 0.8 copy-start.2
  75.2 1.2 %collective-permute-start.14 = (f32[8,512]{1,0:T(8,128)S(1)}, f32[8,512]{1,0:T(8,128)S(1)}, u32[]{:S(2)}, u32[]{:S(2)}) collective-permute-start(f32[8,512]{1,0:T(8,128)S(1)} %get-tuple-element.44.refs_3_.refs_5_), channel_id=1, source_target_pairs={{0,1},{1,0},{2,3},{3,2},{4,5},{5,4},{6,7},{7,6},{8,9},{9,8},{10,11... | collective-permute-start | bytes 49160 | tf_op jit(solution)/shard_map/ppermute | solution.py:19
  76.4 3.9 %collective-permute-start.15 = (bf16[512,512]{1,0:T(8,128)(2,1)S(1)}, bf16[512,512]{1,0:T(8,128)(2,1)S(1)}, u32[]{:S(2)}, u32[]{:S(2)}) collective-permute-start(bf16[512,512]{1,0:T(8,128)(2,1)S(1)} %broadcast_select_fusion.3.refs_1_), channel_id=1, source_target_pairs={{0,1},{1,0},{2,3},{3,2},{4,5},{5,4},{6,7},{7,6},{8,9},{9,8},{10,11... | collective-permute-start | bytes 1572872 | tf_op jit(solution)/shard_map/ppermute | solution.py:19
  84.6 15.0 %collective-permute-start.21 = (bf16[512,512]{1,0:T(8,128)(2,1)S(1)}, bf16[512,512]{1,0:T(8,128)(2,1)S(1)}, u32[]{:S(2)}, u32[]{:S(2)}) collective-permute-start(bf16[512,512]{1,0:T(8,128)(2,1)S(1)} %get-tuple-element.63), channel_id=1, source_target_pairs={{0,2},{2,0},{1,3},{3,1},{4,6},{6,4},{5,7},{7,5},{8,10},{10,8},{9,1... | collective-permute-start | bytes 1572872 | tf_op jit(solution)/shard_map/ppermute | solution.py:19
  96.2 7.6 %collective-permute-start.19 = (bf16[512,512]{1,0:T(8,128)(2,1)S(1)}, bf16[512,512]{1,0:T(8,128)(2,1)S(1)}, u32[]{:S(2)}, u32[]{:S(2)}) collective-permute-start(bf16[512,512]{1,0:T(8,128)(2,1)S(1)} %get-tuple-element.60), channel_id=1, source_target_pairs={{0,1},{1,0},{2,3},{3,2},{4,5},{5,4},{6,7},{7,6},{8,9},{9,8},{10,11... | collective-permute-start | bytes 1572872 | tf_op jit(solution)/shard_map/ppermute | solution.py:19
  96.3 2.1 %collective-permute-start.20 = (f32[]{:T(128)}, f32[]{:T(128)}, u32[]{:S(2)}, u32[]{:S(2)}) collective-permute-start(f32[]{:T(128)} %bitcast.2), channel_id=1, source_target_pairs={{0,1},{1,0},{2,3},{3,2},{4,5},{5,4},{6,7},{7,6},{8,9},{9,8},{10,11... | collective-permute-start | bytes 20 | tf_op jit(solution)/shard_map/ppermute | solution.py:19
  99.7 6.4 %collective-permute-start.22 = (f32[]{:T(128)}, f32[]{:T(128)}, u32[]{:S(2)}, u32[]{:S(2)}) collective-permute-start(f32[]{:T(128)} %add.21), channel_id=1, source_target_pairs={{0,2},{2,0},{1,3},{3,1},{4,6},{6,4},{5,7},{7,5},{8,10},{10,8},{9,1... | collective-permute-start | bytes 20 | tf_op jit(solution)/shard_map/ppermute | solution.py:19

commit v7 on v0

--- a/solution.py
+++ b/solution.py
@@ -1,6 +1,9 @@
+import functools
 import jax
 import jax.numpy as jnp
 from jax import lax
+from jax.experimental import pallas as pl
+from jax.experimental.pallas import tpu as pltpu
 from jax.sharding import PartitionSpec as P
 
 off_weight = 0.0051
@@ -43,7 +46,7 @@
     return (jnp.sum(as_float, axis=0), jnp.sum(as_float * as_float, axis=0))
 
 
-def per_device(left_outputs, right_outputs):
+def reduced_device(left_outputs, right_outputs):
     rows, quart = left_outputs.shape
     half = 2 * quart
     feats = 4 * quart
@@ -125,7 +128,523 @@
     return (left_gradient, right_gradient, corr_rows[None, :, :], jnp.reshape(loss, (1,)))
 
 
+def fold_rows(values):
+    rows, width = values.shape
+    return jnp.sum(values.reshape(rows // 8, 8, width), axis=0)
+
+
+def fold_lanes(values):
+    return sum(values[:, at : at + 128] for at in range(0, values.shape[1], 128))
+
+
+def column_mean(block):
+    rows, width = block.shape
+    folded = jnp.zeros((8, width), jnp.float32)
+    for at in range(0, rows, 64):
+        folded = folded + fold_rows(block[at : at + 64, :].astype(jnp.float32))
+    return jnp.sum(folded, axis=0, keepdims=True) / rows
+
+
+def add_sums(sums, centred, low):
+    return [
+        sums[0] + fold_rows(centred),
+        sums[1] + fold_rows(centred * centred),
+        sums[2] + fold_rows(low.astype(jnp.float32)),
+    ]
+
+
+def rows_of(values):
+    pad = jnp.zeros((8 - len(values), values[0].shape[1]), jnp.float32)
+    return jnp.concatenate([*values, pad], axis=0)
+
+
+def joined_sums(row, sums):
+    return [row[i + 1 : i + 2, :] + jnp.sum(s, axis=0, keepdims=True) for i, s in enumerate(sums)]
+
+
+def moments(sums, images):
+    total, squares, rounded = sums
+    delta = total / images
+    return delta, lax.rsqrt(squares / images - delta * delta + 1e-05), rounded / images - delta
+
+
+def three_parts(row):
+    high = row.astype(jnp.bfloat16)
+    rest = row - high.astype(jnp.float32)
+    middle = rest.astype(jnp.bfloat16)
+    low = (rest - middle.astype(jnp.float32)).astype(jnp.bfloat16)
+    return [high, middle, low]
+
+
+def split_rows(values):
+    parts = sum([three_parts(v) for v in values], [])
+    pad = jnp.zeros((4, values[0].shape[1]), jnp.float32)
+    return jnp.concatenate([*(p.astype(jnp.float32) for p in parts), pad], axis=0).astype(
+        jnp.bfloat16
+    )
+
+
+def joined_rows(ref, at):
+    parts = ref[at : at + 16, :].astype(jnp.float32)
+    part = lambda i: parts[i : i + 1]
+    return [part(3 * i) + part(3 * i + 1) + part(3 * i + 2) for i in range(4)]
+
+
+def lanes_to_row(partial):
+    ones = jnp.ones((16, partial.shape[1]), jnp.bfloat16)
+    high = partial.astype(jnp.bfloat16)
+    low = (partial - high.astype(jnp.float32)).astype(jnp.bfloat16)
+    row = dot_rows(ones, high) + dot_rows(ones, low)
+    return row[:1, :]
+
+
+def dot_rows(left, right):
+    return lax.dot_general(
+        left, right, (((1,), (1,)), ((), ())), preferred_element_type=jnp.float32
+    )
+
+
+def dot(left, right):
+    return jnp.dot(left, right, preferred_element_type=jnp.float32)
+
+
+def pick_kernel(flags, outer, inner, out):
+    @pl.when(flags[2] != 0)
+    def _():
+        out[...] = outer[...]
+
+    @pl.when(flags[2] == 0)
+    def _():
+        out[...] = inner[...]
+
+
+def right_sums_kernel(first, second, third, row):
+    rows, quart = first.shape
+    shift = column_mean(first)
+    sums = [jnp.zeros((8, quart), jnp.float32)] * 3
+    for block in (first, second, third):
+        for at in range(0, rows, 64):
+            centred = block[at : at + 64, :].astype(jnp.float32) - shift
+            sums = add_sums(sums, centred, centred.astype(jnp.bfloat16))
+    row[...] = rows_of([shift] + [jnp.sum(s, axis=0, keepdims=True) for s in sums])
+
+
+def late_kernel(images, turned, flags, outer, inner, row, out, stats):
+    rows, quart = outer.shape
+    shift = row[0:1, :]
+    sums = [jnp.zeros((8, quart), jnp.float32)] * 3
+    from_outer = flags[2] != 0
+    for at in range(0, rows, 128):
+        piece = slice(at, at + 128)
+        value = jnp.where(
+            from_outer, outer[piece, :].astype(jnp.float32), inner[piece, :].astype(jnp.float32)
+        )
+        centred = value - shift
+        low = centred.astype(jnp.bfloat16)
+        if turned:
+            out[:quart, piece] = jnp.transpose(low)
+        else:
+            out[piece, :] = low
+        sums = add_sums(sums, centred, low)
+    delta, rstd, gap = moments(joined_sums(row, sums), images)
+    values = [shift + delta, rstd, gap, delta]
+    stats[...] = rows_of(values)
+    out[rows:, :] = split_rows(values)
+
+
+def products_kernel(*refs):
+    lefts, rights = refs[0:6], refs[6:12]
+    partner_own, partner_other, own_all, row_other, zero_own, zero_other = refs[12:18]
+    low_left, low_right = refs[18:]
+    rows, quart = lefts[0].shape
+    width = quart // 2
+    for half in range(2):
+        lanes = slice(half * quart, (half + 1) * quart)
+        shift = column_mean(lefts[half])
+        sums = [jnp.zeros((8, quart), jnp.float32)] * 3
+        for block in range(3):
+            source = lefts[2 * block + half]
+            for at in range(0, rows, 64):
+                centred = source[at : at + 64, :].astype(jnp.float32) - shift
+                low = centred.astype(jnp.bfloat16)
+                low_left[block * rows + at : block * rows + at + 64, lanes] = low
+                if block == 0:
+                    (zero_own, zero_other)[half][at : at + 64, :] = low
+                if half:
+                    sums = add_sums(sums, centred, low)
+        if half:
+            row_other[...] = rows_of([shift] + [jnp.sum(s, axis=0, keepdims=True) for s in sums])
+    for half in range(2):
+        lanes = slice(half * quart, (half + 1) * quart)
+        shift = column_mean(rights[half])
+        for block in range(3):
+            source = rights[2 * block + half]
+            for at in range(0, rows, 128):
+                low = (source[at : at + 128, :].astype(jnp.float32) - shift).astype(jnp.bfloat16)
+                low_right[lanes, block * rows + at : block * rows + at + 128] = jnp.transpose(low)
+    for tile in range(4):
+        wide = slice(tile * width, (tile + 1) * width)
+        inner = slice((tile % 2) * width, (tile % 2 + 1) * width)
+        target = partner_own if tile < 2 else partner_other
+        target[:, inner] = dot(low_right[quart:, :], low_left[:, wide])
+        own_all[:, wide] = dot(low_right[:quart, :], low_left[:, wide])
+
+
+def left_operand(zero, late, target, lanes):
+    rows, quart = zero.shape
+    _, _, gap, delta = joined_rows(late, rows)
+    high, middle, _ = three_parts(delta)
+    target[:rows, lanes] = zero[...]
+    extra = [high.astype(jnp.float32), middle.astype(jnp.float32), gap]
+    pad = jnp.zeros((13, quart), jnp.float32)
+    target[rows:, lanes] = jnp.concatenate([*extra, pad], axis=0).astype(jnp.bfloat16)
+
+
+def without_extra(terms, rows):
+    return terms[:rows] - (terms[rows : rows + 1] + terms[rows + 1 : rows + 2] + terms[rows + 2 : rows + 3])
+
+
+def scale_columns(late_b, images):
+    quart = late_b.shape[1]
+    _, rstd, _, delta = joined_rows(late_b, quart)
+    columns = jnp.transpose(rows_of([rstd / images, delta * rstd]))
+    return columns[:, 0:1], columns[:, 1:2]
+
+
+def partner_kernel(images, part, flags, late, zero, sums, late_b, *refs):
+    if part:
+        (first_b, terms_in, across_in, vec_in, partial_out, e_out, mine_out, vec_out, left) = refs
+    else:
+        (terms_out, across_out, e_out, mine_out, vec_out, left) = refs
+    rows, quart = zero.shape
+    width = quart // 2
+    _, rstd, _, delta = joined_rows(late, rows)
+    left_operand(zero, late, left, slice(0, quart))
+    scale_col, delta_col = scale_columns(late_b, images)
+    across = across_in[...] if part else jnp.zeros((quart, 128), jnp.float32)
+    down = []
+    for tile in range(2):
+        at = slice(tile * width, (tile + 1) * width)
+        total = sums[:, at] + dot(late_b[:quart, :], late[:rows, at])
+        corr = (total * scale_col - delta_col * delta[:, at]) * rstd[:, at]
+        e_out[:, at] = (corr * (off_weight * rstd[:, at])).astype(jnp.bfloat16)
+        square = corr * corr
+        across = across + fold_lanes(square)
+        down.append(jnp.sum(square, axis=0, keepdims=True))
+
+        @pl.when(flags[0] == 2 * part + tile)
+        def _():
+            mine_out[...] = corr
+
+    second_a = off_weight * jnp.concatenate(down, axis=1)
+    if part:
+        vec_out[...] = rows_of([second_a, second_a + vec_in[0:1, :]])
+        second = off_weight * lanes_to_row(across)
+        offset_b, rstd_b, _, _ = joined_rows(late_b, quart)
+    else:
+        vec_out[...] = rows_of([second_a])
+        across_out[...] = across
+    for tile in range(2):
+        at = slice(tile * width, (tile + 1) * width)
+        terms = dot_rows(left[...], e_out[at, :])
+        if part:
+            xhat = (first_b[:, at].astype(jnp.float32) - offset_b[:, at]) * rstd_b[:, at]
+            partial_out[:, at] = (
+                without_extra(terms + terms_in[:, at], rows) - xhat * second[:, at]
+            ).astype(jnp.bfloat16)
+        else:
+            terms_out[:, at] = terms
+
+
+def own_kernel(images, flags, *refs):
+    (late_own, late_other, first_own, first_other, zero_own, zero_other, sums, late_b) = refs[:8]
+    (late_b_other, first_b, first_b_other, e_left, e_right, mine_left, mine_right) = refs[8:15]
+    (vec_own, vec_other, vec_core, right_out, left_out, left_partial_out, mine_out) = refs[15:22]
+    (own_loss_out, loss_out, left, norm_b, e_own, mine_own) = refs[22:]
+    rows, quart = zero_own.shape
+    width = quart // 2
+    lower, upper = slice(0, quart), slice(quart, 2 * quart)
+    stats_own, stats_other = joined_rows(late_own, rows), joined_rows(late_other, rows)
+    both = lambda i: jnp.concatenate([stats_own[i], stats_other[i]], axis=1)
+    offset, rstd, _, delta = [both(i) for i in range(4)]
+    left_operand(zero_own, late_own, left, lower)
+    left_operand(zero_other, late_other, left, upper)
+    own_b = joined_rows(late_b, quart)
+    other_b = joined_rows(late_b_other, quart)
+    for source, stats, lanes in ((first_b, own_b, lower), (first_b_other, other_b, upper)):
+        for at in range(0, rows, 64):
+            piece = slice(at, at + 64)
+            norm_b[piece, lanes] = (
+                (source[piece, :].astype(jnp.float32) - stats[0]) * stats[1]
+            ).astype(jnp.bfloat16)
+        rest = jnp.broadcast_to(stats[2] * stats[1], (16, quart))
+        norm_b[rows:, lanes] = rest.astype(jnp.bfloat16)
+
+    scale_col, delta_col = scale_columns(late_b, images)
+    across = jnp.zeros((quart, 128), jnp.float32)
+    losses = jnp.zeros((8, 128), jnp.float32)
+    down = []
+    for tile in range(4):
+        at = slice(tile * width, (tile + 1) * width)
+        inner = slice((tile % 2) * width, (tile % 2 + 1) * width)
+        late = late_own if tile < 2 else late_other
+        total = sums[:, at] + dot(late_b[:quart, :], late[:rows, inner])
+        corr = (total * scale_col - delta_col * delta[:, at]) * rstd[:, at]
+        dcorr = off_weight * corr
+        product = dcorr * corr
+        loss = product
+        if tile < 2:
+            feature = lax.broadcasted_iota(jnp.int32, (quart, width), 0)
+            lane = lax.broadcasted_iota(jnp.int32, (quart, width), 1) + tile * width
+            diagonal = feature == lane
+            dcorr = jnp.where(diagonal, corr - 1.0, dcorr)
+            product = dcorr * corr
+            loss = jnp.where(diagonal, dcorr * dcorr, product)
+        e_own[:, at] = (dcorr * rstd[:, at]).astype(jnp.bfloat16)
+        across = across + fold_lanes(product)
+        losses = losses + fold_rows(fold_lanes(loss))
+        down.append(jnp.sum(product, axis=0, keepdims=True))
+
+        @pl.when(flags[0] == tile)
+        def _():
+            mine_own[...] = corr
+
+    partner_second = jnp.concatenate([vec_own[0:1, :], vec_other[0:1, :]], axis=1)
+    second_a = rstd * (partner_second + jnp.concatenate(down, axis=1))
+    second_b = lanes_to_row(across)
+    own_loss = jnp.sum(losses)
+    own_loss_out[0, 0] = own_loss
+    loss_out[0, 0] = own_loss + jnp.sum(vec_other[1:2, :] + vec_core[1:2, :])
+
+    for tile in (2, 3, 0, 1):
+        at = slice(tile * width, (tile + 1) * width)
+        inner = slice((tile % 2) * width, (tile % 2 + 1) * width)
+        source, e_partner = (first_own, e_left) if tile < 2 else (first_other, e_right)
+        terms = dot(norm_b[:, lower], e_own[:, at]) + dot(norm_b[:, upper], e_partner[:, inner])
+        xhat = (source[:, inner].astype(jnp.float32) - offset[:, at]) * rstd[:, at]
+        value = terms[:rows] - terms[rows : rows + 1] - xhat * second_a[:, at]
+        if tile < 2:
+            left_out[:, inner] = value
+        else:
+            left_partial_out[:, inner] = value.astype(jnp.bfloat16)
+
+    for tile in range(2):
+        at = slice(tile * width, (tile + 1) * width)
+        terms = dot_rows(left[...], e_own[at, :])
+        xhat = (first_b[:, at].astype(jnp.float32) - own_b[0][:, at]) * own_b[1][:, at]
+        right_out[:, at] = without_extra(terms, rows) - xhat * second_b[:, at]
+
+    own_columns = jnp.transpose(mine_own[...])
+    partner_columns = jnp.transpose(jnp.where(flags[0] < 2, mine_left[...], mine_right[...]))
+
+    @pl.when(flags[1] == 0)
+    def _():
+        mine_out[:, lower] = own_columns
+        mine_out[:, upper] = partner_columns
+
+    @pl.when(flags[1] != 0)
+    def _():
+        mine_out[:, lower] = partner_columns
+        mine_out[:, upper] = own_columns
+
+
+def left_final_kernel(own, other, loss, core_loss, out, loss_out):
+    for at in range(0, own.shape[0], 64):
+        piece = slice(at, at + 64)
+        out[piece, :] = (own[piece, :] + other[piece, :].astype(jnp.float32)).astype(jnp.bfloat16)
+    loss_out[0, 0] = loss[0, 0] + core_loss[0, 0]
+
+
+def right_final_kernel(own, other, stats, out):
+    for at in range(0, own.shape[0], 64):
+        piece = slice(at, at + 64)
+        value = stats[1:2, :] * (own[piece, :] + other[piece, :].astype(jnp.float32))
+        out[piece, :] = value.astype(jnp.bfloat16)
+
+
+vmem = pl.BlockSpec(memory_space=pltpu.VMEM)
+smem = pl.BlockSpec(memory_space=pltpu.SMEM)
+
+
+def local_call(kernel, operands, outs, scratch=(), flops=2**20, room=8):
+    moved = sum(x.size * x.dtype.itemsize for x in (*operands, *outs))
+
+    def space(x):
+        return smem if x.dtype == jnp.int32 or x.shape == (1, 1) else vmem
+
+    return pl.pallas_call(
+        kernel,
+        out_shape=list(outs),
+        in_specs=[space(x) for x in operands],
+        out_specs=[space(x) for x in outs],
+        scratch_shapes=list(scratch),
+        compiler_params=pltpu.CompilerParams(vmem_limit_bytes=room * 2**20),
+        cost_estimate=pl.CostEstimate(flops=flops, bytes_accessed=moved, transcendentals=0),
+    )(*operands)
+
+
+def gathered_device(left_outputs, right_outputs):
+    rows, quart = left_outputs.shape
+    half = 2 * quart
+    feats = 4 * quart
+    batch_images = rows * 4
+    tpos = lax.axis_index("tile")
+    dpos = lax.axis_index("dp")
+    row_halves = tpos // 2
+    column_halves = tpos % 2
+    at_end = (dpos == 0) | (dpos == 3)
+    owned_tile = jnp.where(dpos // 2 == column_halves, 0, 2) + dpos % 2
+    flags = jnp.stack([owned_tile, row_halves, at_end, dpos]).astype(jnp.int32)
+
+    pairs = [(0, 1), (1, 0), (2, 3), (3, 2)]
+    middle = [(1, 2), (2, 1)]
+    outward = [(1, 0), (2, 3)]
+
+    def along(block, route):
+        return lax.ppermute(block, "dp", route)
+
+    def core_swap(block):
+        return swapped(block, "tile", 0)
+
+    def x_swap(block):
+        return swapped(block, "tile", 1)
+
+    def after(value, *others):
+        return lax.optimization_barrier((value, *others))
+
+    gemm = 2 * rows * quart * quart
+    width = quart // 2
+    quarter_f32 = jax.ShapeDtypeStruct((rows, quart), jnp.float32)
+    quarter_bf16 = jax.ShapeDtypeStruct((rows, quart), jnp.bfloat16)
+    extended = jax.ShapeDtypeStruct((rows + 16, quart), jnp.bfloat16)
+    row_out = jax.ShapeDtypeStruct((8, quart), jnp.float32)
+    one_out = jax.ShapeDtypeStruct((1, 1), jnp.float32)
+    mine_shape = jax.ShapeDtypeStruct((quart, width), jnp.float32)
+    across_shape = jax.ShapeDtypeStruct((quart, 128), jnp.float32)
+    low = lambda n, m: pltpu.VMEM((n, m), jnp.bfloat16)
+
+    def picked(outer, inner):
+        return local_call(pick_kernel, (flags, outer, inner), (quarter_bf16,))[0]
+
+    first_b = along(right_outputs, pairs)
+    inner_b = along(right_outputs, middle)
+    first_a = along(left_outputs, pairs)
+    other_b0 = x_swap(right_outputs)
+    other_a0 = core_swap(left_outputs)
+    left_behind, first_a = after(left_outputs, first_a)
+    inner_a = along(left_behind, middle)
+
+    outer_b = along(inner_b, outward)
+    third_b = along(first_b, middle)
+    ready_b, other_b0 = after(first_b, other_b0)
+    other_b1 = x_swap(ready_b)
+    outer_a = along(inner_a, outward)
+    third_a = along(first_a, middle)
+    other_a1 = core_swap(first_a)
+
+    last_b = along(third_b, outward)
+    second_b = picked(outer_b, inner_b)
+    row_b = local_call(right_sums_kernel, (right_outputs, first_b, second_b), (row_out,))[0]
+    second_b, other_b1 = after(second_b, other_b1)
+    other_b2 = x_swap(second_b)
+    last_a = along(third_a, outward)
+    second_a = picked(outer_a, inner_a)
+    second_a, other_a1, row_b = after(second_a, other_a1, row_b)
+    other_a2 = core_swap(second_a)
+
+    late_b, stats_b = local_call(
+        functools.partial(late_kernel, batch_images, True),
+        (flags, last_b, third_b, row_b),
+        (extended, row_out),
+    )
+    late_b_other = x_swap(late_b)
+    partner_own, partner_other, own_all, row_other, zero_own, zero_other = local_call(
+        products_kernel,
+        (left_outputs, other_a0, first_a, other_a1, second_a, other_a2)
+        + (right_outputs, other_b0, first_b, other_b1, second_b, other_b2),
+        (
+            quarter_f32,
+            quarter_f32,
+            jax.ShapeDtypeStruct((quart, half), jnp.float32),
+            row_out,
+            quarter_bf16,
+            quarter_bf16,
+        ),
+        [low(3 * rows, half), low(half, 3 * rows)],
+        12 * gemm,
+        room=20,
+    )
+    row_a = core_swap(row_other)
+    late_a, stats_a = local_call(
+        functools.partial(late_kernel, batch_images, False),
+        (flags, last_a, third_a, row_a),
+        (extended, row_out),
+    )
+    late_a_other = core_swap(late_a)
+
+    terms, across, e_left, mine_left, vec_own = local_call(
+        functools.partial(partner_kernel, batch_images, 0),
+        (flags, late_a, zero_own, partner_own, late_b_other),
+        (
+            jax.ShapeDtypeStruct((rows + 16, quart), jnp.float32),
+            across_shape,
+            quarter_bf16,
+            mine_shape,
+            row_out,
+        ),
+        [low(rows + 16, quart)],
+        2 * gemm,
+        room=12,
+    )
+    partial_right, e_right, mine_right, vec_other = local_call(
+        functools.partial(partner_kernel, batch_images, 1),
+        (flags, late_a_other, zero_other, partner_other, late_b_other, other_b0)
+        + (terms, across, vec_own),
+        (quarter_bf16, quarter_bf16, mine_shape, row_out),
+        [low(rows + 16, quart)],
+        2 * gemm,
+        room=12,
+    )
+    from_x = x_swap(partial_right)
+    vec_core = core_swap(vec_other)
+    right_own, left_own, partial_left, mine, own_loss, loss = local_call(
+        functools.partial(own_kernel, batch_images),
+        (flags, late_a, late_a_other, left_outputs, other_a0, zero_own, zero_other, own_all)
+        + (late_b, late_b_other, right_outputs, other_b0, e_left, e_right, mine_left, mine_right)
+        + (vec_own, vec_other, vec_core),
+        (
+            quarter_f32,
+            quarter_f32,
+            quarter_bf16,
+            jax.ShapeDtypeStruct((width, half), jnp.float32),
+            one_out,
+            one_out,
+        ),
+        [
+            low(rows + 16, half),
+            low(rows + 16, half),
+            low(quart, half),
+            pltpu.VMEM((quart, width), jnp.float32),
+        ],
+        8 * gemm,
+        room=20,
+    )
+    from_core = core_swap(partial_left)
+    core_loss = jnp.reshape(core_swap(jnp.reshape(own_loss, ())), (1, 1))
+    left_gradient, loss = local_call(
+        left_final_kernel, (left_own, from_core, loss, core_loss), (quarter_bf16, one_out)
+    )
+    loss = jnp.reshape(loss, ())
+    right_own, loss = after(right_own, loss)
+    loss = loss + x_swap(loss)
+    (right_gradient,) = local_call(
+        right_final_kernel, (right_own, from_x, stats_b), (quarter_bf16,)
+    )
+    return (left_gradient, right_gradient, mine[None, :, :], jnp.reshape(loss / feats, (1,)))
+
+
 def solution(mesh):
+    per_device = gathered_device if mesh.shape["dp"] == 4 else reduced_device
     return jax.shard_map(
         per_device,
         mesh=mesh,

time: 244 us -> 107 us (0.44)
  waiting for transfers between devices: 135 us -> 48.9 us
  blocking collectives: 65.4 us -> 0 us
  Pallas kernels: 0 us -> 25.8 us
  starting transfers between devices: 3.18 us -> 27.2 us
  other arithmetic: 14 us -> 0.08 us
  between operations: 16 us -> 3.29 us
  matrix products: 10.5 us -> 0 us
    reduce_scatter x1 -> x0, waiting for transfers between devices: 75 us -> none  [per_device(): lax.psum_scatter(lax.dot_general(picked, cols_b, (((0,), (0,)), ((), ()))...]
    psum x3 -> x0, blocking collectives: 65.4 us -> none  [the longest x1 43.2 us: per_device(): loss = lax.psum(part_loss, ('dp', 'tile')) / feats]
    all_gather x1 -> x0, waiting for transfers between devices: 46.6 us -> none  [per_device(): piece = lax.all_gather(dcorr_part, 'dp', axis=0, tiled=True)]
    ppermute x0 -> x10, waiting for transfers between devices: none -> 36.3 us  [along(): return lax.ppermute(block, 'dp', route)]
    pallas_call x0 -> x11, Pallas kernels: none -> 25.8 us  [local_call(): pl.pallas_call(kernel, out_shape=list(outs), in_specs=[space(x) for x in...]
    ppermute x0 -> x10, starting transfers between devices: none -> 16.9 us  [along(): return lax.ppermute(block, 'dp', route)]
    dot_general x3 -> x0, matrix products: 10.5 us -> none  [the longest x1 4.29 us: per_device(): into_b = jnp.dot(picked, piece, preferred_element_type=jnp.float32)]
    reduce_sum x4 -> x0, other arithmetic: 7.99 us -> none  [the longest x1 3.42 us: per_device(): jnp.sum(jnp.where(diagonal, (1.0 - corr_rows) ** 2, off_weight * corr_row...]
  transfers between devices with their start and end apart: 6 -> 24, of which waited for: 4 -> 10; matrix products, arithmetic and copies ran while one was open for 2% -> 0% of each run, Pallas kernels for 0% -> 15%
where the time goes in v7:
time: 107 us; the launch traced here: 106 us
  waiting for transfers between devices  48.9 us (46%)
  starting transfers between devices  27.2 us (25%)
  Pallas kernels  25.8 us (24%)
  between operations  3.29 us (3%)
    ppermute x10, waiting for transfers between devices, along(): return lax.ppermute(block, 'dp', route)  36.3 us
    pallas_call x11, Pallas kernels, local_call(): pl.pallas_call(kernel, out_shape=list(outs), in_specs=[space(x) for x in...  25.8 us
    ppermute x10, starting transfers between devices, along(): return lax.ppermute(block, 'dp', route)  16.9 us
    ppermute x14, waiting for transfers between devices, swapped(): return lax.ppermute(block, axis, route)  12.7 us
    ppermute x14, starting transfers between devices, swapped(): return lax.ppermute(block, axis, route)  10.3 us
  transfers between devices with their start and end apart: 24, of which 10 were waited for; matrix products, arithmetic and copies ran while one was open for 0% of the time, Pallas kernels for 15%

profile of v7, /device:TPU:0, one launch (start us, length us, event | category | flops | bytes accessed | tf_op | source)
XLA Modules:
  0.0 106.3 jit_solution(8110032852741297000)
XLA Ops:
  0.6 3.1 %collective-permute-start = (bf16[512,512]{1,0:T(8,128)(2,1)}, bf16[512,512]{1,0:T(8,128)(2,1)}, u32[]{:S(2)}, u32[]{:S(2)}) collective-permute-start(bf16[512,512]{1,0:T(8,128)(2,1)} %refs_2_.1), channel_id=1, source_target_pairs={{0,4},{4,0},{8,12},{12,8},{1,5},{5,1},{9,13},{13,9},{2,6},{6,2},{1... | collective-permute-start | bytes 1572872 | tf_op jit(solution)/shard_map/ppermute | solution.py:504
  4.4 1.6 %collective-permute-start.11 = (bf16[512,512]{1,0:T(8,128)(2,1)}, bf16[512,512]{1,0:T(8,128)(2,1)S(1)}, u32[]{:S(2)}, u32[]{:S(2)}) collective-permute-start(bf16[512,512]{1,0:T(8,128)(2,1)} %refs_9_.1), channel_id=1, source_target_pairs={{0,2},{2,0},{1,3},{3,1},{4,6},{6,4},{5,7},{7,5},{8,10},{10,8},{9,1... | collective-permute-start | bytes 1572872 | tf_op jit(solution)/shard_map/ppermute | solution.py:19
  6.0 4.4 %collective-permute-start.7 = (bf16[512,512]{1,0:T(8,128)(2,1)}, bf16[512,512]{1,0:T(8,128)(2,1)S(1)}, u32[]{:S(2)}, u32[]{:S(2)}) collective-permute-start(bf16[512,512]{1,0:T(8,128)(2,1)} %refs_9_.1), channel_id=1, source_target_pairs={{0,4},{4,0},{8,12},{12,8},{1,5},{5,1},{9,13},{13,9},{2,6},{6,2},{1... | collective-permute-start | bytes 1572872 | tf_op jit(solution)/shard_map/ppermute | solution.py:504
  10.3 6.5 %collective-permute-done.refs_2_ = bf16[512,512]{1,0:T(8,128)(2,1)} collective-permute-done((bf16[512,512]{1,0:T(8,128)(2,1)}, bf16[512,512]{1,0:T(8,128)(2,1)}, u32[]{:S(2)}, u32[]{:S(2)}) %collective-permute-start) | collective-permute-done | bytes 524320 | tf_op jit(solution)/shard_map/ppermute | solution.py:504
  17.5 1.3 %collective-permute-start.9 = (bf16[512,512]{1,0:T(8,128)(2,1)S(1)}, bf16[512,512]{1,0:T(8,128)(2,1)S(1)}, u32[]{:S(2)}, u32[]{:S(2)}) collective-permute-start(bf16[512,512]{1,0:T(8,128)(2,1)S(1)} %collective-permute-done.8.inner), channel_id=1, source_target_pairs={{4,0},{8,12},{5,1},{9,13},{6,2},{10,14},{7,3},{11,15},{20,16},{24,... | collective-permute-start | bytes 1572872 | tf_op jit(solution)/shard_map/ppermute | solution.py:504
  18.8 9.1 %collective-permute-done.7.second.refs_8_ = bf16[512,512]{1,0:T(8,128)(2,1)S(1)} collective-permute-done((bf16[512,512]{1,0:T(8,128)(2,1)}, bf16[512,512]{1,0:T(8,128)(2,1)S(1)}, u32[]{:S(2)}, u32[]{:S(2)}) %collective-permute-start.7) | collective-permute-done | bytes 524320 | tf_op jit(solution)/shard_map/ppermute | solution.py:504
  27.9 2.0 %collective-permute-start.12 = (bf16[512,512]{1,0:T(8,128)(2,1)S(1)}, bf16[512,512]{1,0:T(8,128)(2,1)}, u32[]{:S(2)}, u32[]{:S(2)}) collective-permute-start(bf16[512,512]{1,0:T(8,128)(2,1)S(1)} %collective-permute-done.7.second.refs_8_), channel_id=1, source_target_pairs={{0,2},{2,0},{1,3},{3,1},{4,6},{6,4},{5,7},{7,5},{8,10},{10,8},{9,1... | collective-permute-start | bytes 1572872 | tf_op jit(solution)/shard_map/ppermute | solution.py:19
  29.9 1.5 %collective-permute-start.16 = (bf16[512,512]{1,0:T(8,128)(2,1)S(1)}, bf16[512,512]{1,0:T(8,128)(2,1)}, u32[]{:S(2)}, u32[]{:S(2)}) collective-permute-start(bf16[512,512]{1,0:T(8,128)(2,1)S(1)} %collective-permute-done.7.second.refs_8_), channel_id=1, source_target_pairs={{4,8},{8,4},{5,9},{9,5},{6,10},{10,6},{7,11},{11,7},{20,24},{24,20... | collective-permute-start | bytes 1572872 | tf_op jit(solution)/shard_map/ppermute | solution.py:504
  31.4 1.3 %collective-permute-start.5 = (bf16[512,512]{1,0:T(8,128)(2,1)S(1)}, bf16[512,512]{1,0:T(8,128)(2,1)S(1)}, u32[]{:S(2)}, u32[]{:S(2)}) collective-permute-start(bf16[512,512]{1,0:T(8,128)(2,1)S(1)} %collective-permute-done.4.inner), channel_id=1, source_target_pairs={{4,0},{8,12},{5,1},{9,13},{6,2},{10,14},{7,3},{11,15},{20,16},{24,... | collective-permute-start | bytes 1572872 | tf_op jit(solution)/shard_map/ppermute | solution.py:504
  32.7 6.4 %collective-permute-done.9.outer = bf16[512,512]{1,0:T(8,128)(2,1)S(1)} collective-permute-done((bf16[512,512]{1,0:T(8,128)(2,1)S(1)}, bf16[512,512]{1,0:T(8,128)(2,1)S(1)}, u32[]{:S(2)}, u32[]{:S(2)}) %collective-permute-start.9) | collective-permute-done | bytes 524320 | tf_op jit(solution)/shard_map/ppermute | solution.py:504
  39.2 1.5 %collective-permute-start.1 = (bf16[512,512]{1,0:T(8,128)(2,1)}, bf16[512,512]{1,0:T(8,128)(2,1)}, u32[]{:S(2)}, u32[]{:S(2)}) collective-permute-start(bf16[512,512]{1,0:T(8,128)(2,1)} %collective-permute-done.refs_2_), channel_id=1, source_target_pairs={{4,8},{8,4},{5,9},{9,5},{6,10},{10,6},{7,11},{11,7},{20,24},{24,20... | collective-permute-start | bytes 1572872 | tf_op jit(solution)/shard_map/ppermute | solution.py:504
  41.4 1.3 %collective-permute-start.17 = (bf16[512,512]{1,0:T(8,128)(2,1)}, bf16[512,512]{1,0:T(8,128)(2,1)S(1)}, u32[]{:S(2)}, u32[]{:S(2)}) collective-permute-start(bf16[512,512]{1,0:T(8,128)(2,1)} %collective-permute-done.16.inner), channel_id=1, source_target_pairs={{4,0},{8,12},{5,1},{9,13},{6,2},{10,14},{7,3},{11,15},{20,16},{24,... | collective-permute-start | bytes 1572872 | tf_op jit(solution)/shard_map/ppermute | solution.py:504
  42.7 1.0 copy-done
  43.7 1.0 shard_map.59.row
  44.7 5.7 %collective-permute-done.5.outer = bf16[512,512]{1,0:T(8,128)(2,1)S(1)} collective-permute-done((bf16[512,512]{1,0:T(8,128)(2,1)S(1)}, bf16[512,512]{1,0:T(8,128)(2,1)S(1)}, u32[]{:S(2)}, u32[]{:S(2)}) %collective-permute-start.5) | collective-permute-done | bytes 524320 | tf_op jit(solution)/shard_map/ppermute | solution.py:504
  50.4 2.0 %collective-permute-start.13 = (bf16[512,512]{1,0:T(8,128)(2,1)S(1)}, bf16[512,512]{1,0:T(8,128)(2,1)S(1)}, u32[]{:S(2)}, u32[]{:S(2)}) collective-permute-start(bf16[512,512]{1,0:T(8,128)(2,1)S(1)} %shard_map.58.third.refs_10_), channel_id=1, source_target_pairs={{0,2},{2,0},{1,3},{3,1},{4,6},{6,4},{5,7},{7,5},{8,10},{10,8},{9,1... | collective-permute-start | bytes 1572872 | tf_op jit(solution)/shard_map/ppermute | solution.py:19
  53.1 1.3 %collective-permute-start.2 = (bf16[512,512]{1,0:T(8,128)(2,1)}, bf16[512,512]{1,0:T(8,128)(2,1)S(1)}, u32[]{:S(2)}, u32[]{:S(2)}) collective-permute-start(bf16[512,512]{1,0:T(8,128)(2,1)} %collective-permute-done.1.inner), channel_id=1, source_target_pairs={{4,0},{8,12},{5,1},{9,13},{6,2},{10,14},{7,3},{11,15},{20,16},{24,... | collective-permute-start | bytes 1572872 | tf_op jit(solution)/shard_map/ppermute | solution.py:504
  54.4 7.3 %collective-permute-done.17.outer = bf16[512,512]{1,0:T(8,128)(2,1)S(1)} collective-permute-done((bf16[512,512]{1,0:T(8,128)(2,1)}, bf16[512,512]{1,0:T(8,128)(2,1)S(1)}, u32[]{:S(2)}, u32[]{:S(2)}) %collective-permute-start.17) | collective-permute-done | bytes 524320 | tf_op jit(solution)/shard_map/ppermute | solution.py:504
  61.6 1.5 %shard_map.62 = (bf16[528,512]{1,0:T(8,128)(2,1)S(1)}, f32[8,512]{1,0:T(8,128)S(1)}) custom-call(s32[4]{0:T(128)S(1)} %pad_add_fusion.flags, bf16[512,512]{1,0:T(8,128)(2,1)S(1)} %collective-permute-done.17.outer, bf16[512,512]{1,0:T(8,128)(2,1)} %collective-permute-done.16.inner, f32[8,512]{1,0:T(8,128)S(1)} %shard_map.59.row), custom_call_target="tpu_custom_call" | custom-call | flops 1048576 | bytes 1622032 | tf_op jit(solution)/shard_map/pallas_call | solution.py:475
  63.1 2.0 %collective-permute-start.18 = (bf16[528,512]{1,0:T(8,128)(2,1)S(1)}, bf16[528,512]{1,0:T(8,128)(2,1)S(1)}, u32[]{:S(2)}, u32[]{:S(2)}) collective-permute-start(bf16[528,512]{1,0:T(8,128)(2,1)S(1)} %get-tuple-element.55.refs_7_), channel_id=1, source_target_pairs={{0,2},{2,0},{1,3},{3,1},{4,6},{6,4},{5,7},{7,5},{8,10},{10,8},{9,1... | collective-permute-start | bytes 1622024 | tf_op jit(solution)/shard_map/ppermute | solution.py:19
  65.2 5.5 %shard_map.60 = (f32[512,512]{1,0:T(8,128)S(1)}, f32[512,512]{1,0:T(8,128)S(1)}, f32[512,1024]{1,0:T(8,128)S(1)}, f32[8,512]{1,0:T(8,128)S(1)}, bf16[512,512]{1,...) custom-call(bf16[512,512]{1,0:T(8,128)(2,1)S(1)} %copy-done.2, bf16[512,512]{1,0:T(8,128)(2,1)S(1)} %collective-permute-done.3.refs_1_.refs_3_, ...), custom_call_target="tpu_custom_call" | custom-call | flops 3221225472 | bytes 11550720 | tf_op jit(solution)/shard_map/pallas_call | solution.py:475
  70.7 1.3 %collective-permute-done.2.outer = bf16[512,512]{1,0:T(8,128)(2,1)S(1)} collective-permute-done((bf16[512,512]{1,0:T(8,128)(2,1)}, bf16[512,512]{1,0:T(8,128)(2,1)S(1)}, u32[]{:S(2)}, u32[]{:S(2)}) %collective-permute-start.2) | collective-permute-done | bytes 524320 | tf_op jit(solution)/shard_map/ppermute | solution.py:504
  72.0 2.1 %shard_map.61 = (bf16[528,512]{1,0:T(8,128)(2,1)S(1)}, f32[8,512]{1,0:T(8,128)}) custom-call(s32[4]{0:T(128)S(1)} %pad_add_fusion.flags, bf16[512,512]{1,0:T(8,128)(2,1)S(1)} %collective-permute-done.2.outer, bf16[512,512]{1,0:T(8,128)(2,1)} %collective-permute-done.1.inner, f32[8,512]{1,0:T(8,128)S(1)} %collective-permute-done.14.row), custom_call_target="tpu_custom_call" | custom-call | flops 1048576 | bytes 1622032 | tf_op jit(solution)/shard_map/pallas_call | solution.py:475
  74.2 1.6 %collective-permute-done.18.late_b.refs_8_ = bf16[528,512]{1,0:T(8,128)(2,1)S(1)} collective-permute-done((bf16[528,512]{1,0:T(8,128)(2,1)S(1)}, bf16[528,512]{1,0:T(8,128)(2,1)S(1)}, u32[]{:S(2)}, u32[]{:S(2)}) %collective-permute-start.18) | collective-permute-done | bytes 540704 | tf_op jit(solution)/shard_map/ppermute | solution.py:19
  75.8 2.0 %shard_map.63 = (f32[528,512]{1,0:T(8,128)S(1)}, f32[512,128]{1,0:T(8,128)S(1)}, bf16[512,512]{1,0:T(8,128)(2,1)S(1)}, f32[512,256]{1,0:T(8,128)S(1)}, f32[8,512]{1,0:T(8,128)S(1)}) custom-call(s32[4]{0:T(128)S(1)} %pad_add_fusion.flags, bf16[528,512]{1,0:T(8,128)(2,1)S(1)} %get-tuple-element.50.late.refs_0_, ...), custom_call_target="tpu_custom_call" | custom-call | flops 536870912 | bytes 5062672 | tf_op jit(solution)/shard_map/pallas_call | solution.py:475
  77.9 2.4 %shard_map.64 = (bf16[512,512]{1,0:T(8,128)(2,1)S(1)}, bf16[512,512]{1,0:T(8,128)(2,1)S(1)}, f32[512,256]{1,0:T(8,128)S(1)}, f32[8,512]{1,0:T(8,128)S(1)}) custom-call(s32[4]{0:T(128)S(1)} %pad_add_fusion.flags, bf16[528,512]{1,0:T(8,128)(2,1)S(1)} %collective-permute-done.15.late.refs_1_, bf16[512,512]{1,0:T(8,128)(2,1)S(1)} %get-tuple-element.52.zero.refs_5_, ...), custom_call_target="tpu_custom_call" | custom-call | flops 536870912 | bytes 6127632 | tf_op jit(solution)/shard_map/pallas_call | solution.py:475
  80.3 1.2 %collective-permute-done.19.refs_17_ = f32[8,512]{1,0:T(8,128)S(1)} collective-permute-done((f32[8,512]{1,0:T(8,128)S(1)}, f32[8,512]{1,0:T(8,128)S(1)}, u32[]{:S(2)}, u32[]{:S(2)}) %collective-permute-start.19) | collective-permute-done | bytes 16416 | tf_op jit(solution)/shard_map/ppermute | solution.py:19
  81.5 7.0 %shard_map.65 = (f32[512,512]{1,0:T(8,128)S(1)}, f32[512,512]{1,0:T(8,128)S(1)}, bf16[512,512]{1,0:T(8,128)(2,1)S(1)}, f32[256,1024]{1,0:T(8,128)}, f32[1,1]{1,0:T(1,128)}, /*index=5*/f32[1,1]{1,0:T(1,128)}) custom-call(s32[4]{0:T(128)S(1)} %pad_add_fusion.flags, bf16[528,512]{1,0:T(8,128)(2,1)S(1)} %get-tuple-element.50.late.refs_0_, ...), custom_call_target="tpu_custom_call" | custom-call | flops 2147483648 | bytes 13221912 | tf_op jit(solution)/shard_map/pallas_call | solution.py:475
  88.8 1.3 %collective-permute-start.22 = (bf16[512,512]{1,0:T(8,128)(2,1)S(1)}, bf16[512,512]{1,0:T(8,128)(2,1)S(1)}, u32[]{:S(2)}, u32[]{:S(2)}) collective-permute-start(bf16[512,512]{1,0:T(8,128)(2,1)S(1)} %get-tuple-element.74), channel_id=1, source_target_pairs={{0,2},{2,0},{1,3},{3,1},{4,6},{6,4},{5,7},{7,5},{8,10},{10,8},{9,1... | collective-permute-start | bytes 1572872 | tf_op jit(solution)/shard_map/ppermute | solution.py:19
  90.2 1.2 %collective-permute-done.21 = f32[]{:T(128)} collective-permute-done((f32[]{:T(128)}, f32[]{:T(128)}, u32[]{:S(2)}, u32[]{:S(2)}) %collective-permute-start.21) | collective-permute-done | bytes 36 | tf_op jit(solution)/shard_map/ppermute | solution.py:19
  91.3 2.2 %shard_map.66 = (bf16[512,512]{1,0:T(8,128)(2,1)}, f32[1,1]{1,0:T(1,128)}) custom-call(f32[512,512]{1,0:T(8,128)S(1)} %get-tuple-element.66.own, bf16[512,512]{1,0:T(8,128)(2,1)S(1)} %collective-permute-done.20.other, f32[1,1]{1,0:T(1,128)} %get-tuple-element.68.loss, f32[1,1]{1,0:T(1,128)} %bitcast.5.core_loss), custom_call_target="tpu_custom_call" | custom-call | flops 1048576 | bytes 2097164 | tf_op jit(solution)/shard_map/pallas_call | solution.py:475
  94.3 8.7 %collective-permute-done.22.other = bf16[512,512]{1,0:T(8,128)(2,1)S(1)} collective-permute-done((bf16[512,512]{1,0:T(8,128)(2,1)S(1)}, bf16[512,512]{1,0:T(8,128)(2,1)S(1)}, u32[]{:S(2)}, u32[]{:S(2)}) %collective-permute-start.22) | collective-permute-done | bytes 524320 | tf_op jit(solution)/shard_map/ppermute | solution.py:19
  (34 shorter events, 5.0 us)
Async XLA Ops:
  0.6 16.2 %collective-permute-start = (bf16[512,512]{1,0:T(8,128)(2,1)}, bf16[512,512]{1,0:T(8,128)(2,1)}, u32[]{:S(2)}, u32[]{:S(2)}) collective-permute-start(bf16[512,512]{1,0:T(8,128)(2,1)} %refs_2_.1), channel_id=1, source_target_pairs={{0,4},{4,0},{8,12},{12,8},{1,5},{5,1},{9,13},{13,9},{2,6},{6,2},{1... | collective-permute-start | bytes 1572872 | tf_op jit(solution)/shard_map/ppermute | solution.py:504
  3.7 13.8 %collective-permute-start.8 = (bf16[512,512]{1,0:T(8,128)(2,1)}, bf16[512,512]{1,0:T(8,128)(2,1)S(1)}, u32[]{:S(2)}, u32[]{:S(2)}) collective-permute-start(bf16[512,512]{1,0:T(8,128)(2,1)} %refs_9_.1), channel_id=1, source_target_pairs={{4,8},{8,4},{5,9},{9,5},{6,10},{10,6},{7,11},{11,7},{20,24},{24,20... | collective-permute-start | bytes 1572872 | tf_op jit(solution)/shard_map/ppermute | solution.py:504
  4.4 14.4 %collective-permute-start.11 = (bf16[512,512]{1,0:T(8,128)(2,1)}, bf16[512,512]{1,0:T(8,128)(2,1)S(1)}, u32[]{:S(2)}, u32[]{:S(2)}) collective-permute-start(bf16[512,512]{1,0:T(8,128)(2,1)} %refs_9_.1), channel_id=1, source_target_pairs={{0,2},{2,0},{1,3},{3,1},{4,6},{6,4},{5,7},{7,5},{8,10},{10,8},{9,1... | collective-permute-start | bytes 1572872 | tf_op jit(solution)/shard_map/ppermute | solution.py:19
  6.0 22.0 %collective-permute-start.7 = (bf16[512,512]{1,0:T(8,128)(2,1)}, bf16[512,512]{1,0:T(8,128)(2,1)S(1)}, u32[]{:S(2)}, u32[]{:S(2)}) collective-permute-start(bf16[512,512]{1,0:T(8,128)(2,1)} %refs_9_.1), channel_id=1, source_target_pairs={{0,4},{4,0},{8,12},{12,8},{1,5},{5,1},{9,13},{13,9},{2,6},{6,2},{1... | collective-permute-start | bytes 1572872 | tf_op jit(solution)/shard_map/ppermute | solution.py:504
  16.8 14.6 %collective-permute-start.4 = (bf16[512,512]{1,0:T(8,128)(2,1)}, bf16[512,512]{1,0:T(8,128)(2,1)S(1)}, u32[]{:S(2)}, u32[]{:S(2)}) collective-permute-start(bf16[512,512]{1,0:T(8,128)(2,1)} %refs_2_.1), channel_id=1, source_target_pairs={{4,8},{8,4},{5,9},{9,5},{6,10},{10,6},{7,11},{11,7},{20,24},{24,20... | collective-permute-start | bytes 1572872 | tf_op jit(solution)/shard_map/ppermute | solution.py:504
  17.5 21.7 %collective-permute-start.9 = (bf16[512,512]{1,0:T(8,128)(2,1)S(1)}, bf16[512,512]{1,0:T(8,128)(2,1)S(1)}, u32[]{:S(2)}, u32[]{:S(2)}) collective-permute-start(bf16[512,512]{1,0:T(8,128)(2,1)S(1)} %collective-permute-done.8.inner), channel_id=1, source_target_pairs={{4,0},{8,12},{5,1},{9,13},{6,2},{10,14},{7,3},{11,15},{20,16},{24,... | collective-permute-start | bytes 1572872 | tf_op jit(solution)/shard_map/ppermute | solution.py:504
  27.9 13.4 %collective-permute-start.12 = (bf16[512,512]{1,0:T(8,128)(2,1)S(1)}, bf16[512,512]{1,0:T(8,128)(2,1)}, u32[]{:S(2)}, u32[]{:S(2)}) collective-permute-start(bf16[512,512]{1,0:T(8,128)(2,1)S(1)} %collective-permute-done.7.second.refs_8_), channel_id=1, source_target_pairs={{0,2},{2,0},{1,3},{3,1},{4,6},{6,4},{5,7},{7,5},{8,10},{10,8},{9,1... | collective-permute-start | bytes 1572872 | tf_op jit(solution)/shard_map/ppermute | solution.py:19
  29.9 11.5 %collective-permute-start.16 = (bf16[512,512]{1,0:T(8,128)(2,1)S(1)}, bf16[512,512]{1,0:T(8,128)(2,1)}, u32[]{:S(2)}, u32[]{:S(2)}) collective-permute-start(bf16[512,512]{1,0:T(8,128)(2,1)S(1)} %collective-permute-done.7.second.refs_8_), channel_id=1, source_target_pairs={{4,8},{8,4},{5,9},{9,5},{6,10},{10,6},{7,11},{11,7},{20,24},{24,20... | collective-permute-start | bytes 1572872 | tf_op jit(solution)/shard_map/ppermute | solution.py:504
  31.4 19.0 %collective-permute-start.5 = (bf16[512,512]{1,0:T(8,128)(2,1)S(1)}, bf16[512,512]{1,0:T(8,128)(2,1)S(1)}, u32[]{:S(2)}, u32[]{:S(2)}) collective-permute-start(bf16[512,512]{1,0:T(8,128)(2,1)S(1)} %collective-permute-done.4.inner), channel_id=1, source_target_pairs={{4,0},{8,12},{5,1},{9,13},{6,2},{10,14},{7,3},{11,15},{20,16},{24,... | collective-permute-start | bytes 1572872 | tf_op jit(solution)/shard_map/ppermute | solution.py:504
  32.6 20.3 %collective-permute-start.6 = (bf16[512,512]{1,0:T(8,128)(2,1)}, bf16[512,512]{1,0:T(8,128)(2,1)}, u32[]{:S(2)}, u32[]{:S(2)}) collective-permute-start(bf16[512,512]{1,0:T(8,128)(2,1)} %collective-permute-done.refs_2_), channel_id=1, source_target_pairs={{0,1},{1,0},{2,3},{3,2},{4,5},{5,4},{6,7},{7,6},{8,9},{9,8},{10,11... | collective-permute-start | bytes 1572872 | tf_op jit(solution)/shard_map/ppermute | solution.py:19
  39.2 13.9 %collective-permute-start.1 = (bf16[512,512]{1,0:T(8,128)(2,1)}, bf16[512,512]{1,0:T(8,128)(2,1)}, u32[]{:S(2)}, u32[]{:S(2)}) collective-permute-start(bf16[512,512]{1,0:T(8,128)(2,1)} %collective-permute-done.refs_2_), channel_id=1, source_target_pairs={{4,8},{8,4},{5,9},{9,5},{6,10},{10,6},{7,11},{11,7},{20,24},{24,20... | collective-permute-start | bytes 1572872 | tf_op jit(solution)/shard_map/ppermute | solution.py:504
  40.7 24.5 %copy-start.1 = (bf16[512,512]{1,0:T(8,128)(2,1)S(1)}, bf16[512,512]{1,0:T(8,128)(2,1)}, u32[]{:S(2)}) copy-start(bf16[512,512]{1,0:T(8,128)(2,1)} %refs_9_.1) | copy-start | bytes 1572868
  40.7 24.5 %copy-start.2 = (bf16[512,512]{1,0:T(8,128)(2,1)S(1)}, bf16[512,512]{1,0:T(8,128)(2,1)}, u32[]{:S(2)}) copy-start(bf16[512,512]{1,0:T(8,128)(2,1)} %refs_2_.1) | copy-start | bytes 1572868
  41.3 23.8 %collective-permute-start.3 = (bf16[512,512]{1,0:T(8,128)(2,1)}, bf16[512,512]{1,0:T(8,128)(2,1)S(1)}, u32[]{:S(2)}, u32[]{:S(2)}) collective-permute-start(bf16[512,512]{1,0:T(8,128)(2,1)} %refs_2_.1), channel_id=1, source_target_pairs={{0,1},{1,0},{2,3},{3,2},{4,5},{5,4},{6,7},{7,6},{8,9},{9,8},{10,11... | collective-permute-start | bytes 1572872 | tf_op jit(solution)/shard_map/ppermute | solution.py:19
  41.4 20.2 %collective-permute-start.17 = (bf16[512,512]{1,0:T(8,128)(2,1)}, bf16[512,512]{1,0:T(8,128)(2,1)S(1)}, u32[]{:S(2)}, u32[]{:S(2)}) collective-permute-start(bf16[512,512]{1,0:T(8,128)(2,1)} %collective-permute-done.16.inner), channel_id=1, source_target_pairs={{4,0},{8,12},{5,1},{9,13},{6,2},{10,14},{7,3},{11,15},{20,16},{24,... | collective-permute-start | bytes 1572872 | tf_op jit(solution)/shard_map/ppermute | solution.py:504
  42.7 1.0 copy-start
  50.4 14.7 %collective-permute-start.13 = (bf16[512,512]{1,0:T(8,128)(2,1)S(1)}, bf16[512,512]{1,0:T(8,128)(2,1)S(1)}, u32[]{:S(2)}, u32[]{:S(2)}) collective-permute-start(bf16[512,512]{1,0:T(8,128)(2,1)S(1)} %shard_map.58.third.refs_10_), channel_id=1, source_target_pairs={{0,2},{2,0},{1,3},{3,1},{4,6},{6,4},{5,7},{7,5},{8,10},{10,8},{9,1... | collective-permute-start | bytes 1572872 | tf_op jit(solution)/shard_map/ppermute | solution.py:19
  53.0 12.2 %collective-permute-start.10 = (bf16[512,512]{1,0:T(8,128)(2,1)S(1)}, bf16[512,512]{1,0:T(8,128)(2,1)S(1)}, u32[]{:S(2)}, u32[]{:S(2)}) collective-permute-start(bf16[512,512]{1,0:T(8,128)(2,1)S(1)} %shard_map.57.refs_4_), channel_id=1, source_target_pairs={{0,1},{1,0},{2,3},{3,2},{4,5},{5,4},{6,7},{7,6},{8,9},{9,8},{10,11... | collective-permute-start | bytes 1572872 | tf_op jit(solution)/shard_map/ppermute | solution.py:19
  53.1 19.0 %collective-permute-start.2 = (bf16[512,512]{1,0:T(8,128)(2,1)}, bf16[512,512]{1,0:T(8,128)(2,1)S(1)}, u32[]{:S(2)}, u32[]{:S(2)}) collective-permute-start(bf16[512,512]{1,0:T(8,128)(2,1)} %collective-permute-done.1.inner), channel_id=1, source_target_pairs={{4,0},{8,12},{5,1},{9,13},{6,2},{10,14},{7,3},{11,15},{20,16},{24,... | collective-permute-start | bytes 1572872 | tf_op jit(solution)/shard_map/ppermute | solution.py:504
  63.1 12.7 %collective-permute-start.18 = (bf16[528,512]{1,0:T(8,128)(2,1)S(1)}, bf16[528,512]{1,0:T(8,128)(2,1)S(1)}, u32[]{:S(2)}, u32[]{:S(2)}) collective-permute-start(bf16[528,512]{1,0:T(8,128)(2,1)S(1)} %get-tuple-element.55.refs_7_), channel_id=1, source_target_pairs={{0,2},{2,0},{1,3},{3,1},{4,6},{6,4},{5,7},{7,5},{8,10},{10,8},{9,1... | collective-permute-start | bytes 1622024 | tf_op jit(solution)/shard_map/ppermute | solution.py:19
  70.6 1.4 %collective-permute-start.14 = (f32[8,512]{1,0:T(8,128)S(1)}, f32[8,512]{1,0:T(8,128)S(1)}, u32[]{:S(2)}, u32[]{:S(2)}) collective-permute-start(f32[8,512]{1,0:T(8,128)S(1)} %get-tuple-element.49), channel_id=1, source_target_pairs={{0,1},{1,0},{2,3},{3,2},{4,5},{5,4},{6,7},{7,6},{8,9},{9,8},{10,11... | collective-permute-start | bytes 49160 | tf_op jit(solution)/shard_map/ppermute | solution.py:19
  74.1 3.7 %collective-permute-start.15 = (bf16[528,512]{1,0:T(8,128)(2,1)S(1)}, bf16[528,512]{1,0:T(8,128)(2,1)S(1)}, u32[]{:S(2)}, u32[]{:S(2)}) collective-permute-start(bf16[528,512]{1,0:T(8,128)(2,1)S(1)} %get-tuple-element.50.late.refs_0_), channel_id=1, source_target_pairs={{0,1},{1,0},{2,3},{3,2},{4,5},{5,4},{6,7},{7,6},{8,9},{9,8},{10,11... | collective-permute-start | bytes 1622024 | tf_op jit(solution)/shard_map/ppermute | solution.py:19
  80.3 1.2 %collective-permute-start.19 = (f32[8,512]{1,0:T(8,128)S(1)}, f32[8,512]{1,0:T(8,128)S(1)}, u32[]{:S(2)}, u32[]{:S(2)}) collective-permute-start(f32[8,512]{1,0:T(8,128)S(1)} %get-tuple-element.65.refs_16_), channel_id=1, source_target_pairs={{0,1},{1,0},{2,3},{3,2},{4,5},{5,4},{6,7},{7,6},{8,9},{9,8},{10,11... | collective-permute-start | bytes 49160 | tf_op jit(solution)/shard_map/ppermute | solution.py:19
  88.6 2.8 %collective-permute-start.20 = (bf16[512,512]{1,0:T(8,128)(2,1)S(1)}, bf16[512,512]{1,0:T(8,128)(2,1)S(1)}, u32[]{:S(2)}, u32[]{:S(2)}) collective-permute-start(bf16[512,512]{1,0:T(8,128)(2,1)S(1)} %get-tuple-element.67), channel_id=1, source_target_pairs={{0,1},{1,0},{2,3},{3,2},{4,5},{5,4},{6,7},{7,6},{8,9},{9,8},{10,11... | collective-permute-start | bytes 1572872 | tf_op jit(solution)/shard_map/ppermute | solution.py:19
  88.8 14.2 %collective-permute-start.22 = (bf16[512,512]{1,0:T(8,128)(2,1)S(1)}, bf16[512,512]{1,0:T(8,128)(2,1)S(1)}, u32[]{:S(2)}, u32[]{:S(2)}) collective-permute-start(bf16[512,512]{1,0:T(8,128)(2,1)S(1)} %get-tuple-element.74), channel_id=1, source_target_pairs={{0,2},{2,0},{1,3},{3,1},{4,6},{6,4},{5,7},{7,5},{8,10},{10,8},{9,1... | collective-permute-start | bytes 1572872 | tf_op jit(solution)/shard_map/ppermute | solution.py:19
  90.1 1.2 %collective-permute-start.21 = (f32[]{:T(128)}, f32[]{:T(128)}, u32[]{:S(2)}, u32[]{:S(2)}) collective-permute-start(f32[]{:T(128)} %bitcast.4), channel_id=1, source_target_pairs={{0,1},{1,0},{2,3},{3,2},{4,5},{5,4},{6,7},{7,6},{8,9},{9,8},{10,11... | collective-permute-start | bytes 20 | tf_op jit(solution)/shard_map/ppermute | solution.py:19
  93.5 10.4 %collective-permute-start.23 = (f32[]{:T(128)}, f32[]{:T(128)}, u32[]{:S(2)}, u32[]{:S(2)}) collective-permute-start(f32[]{:T(128)} %bitcast.6), channel_id=1, source_target_pairs={{0,2},{2,0},{1,3},{3,1},{4,6},{6,4},{5,7},{7,5},{8,10},{10,8},{9,1... | collective-permute-start | bytes 20 | tf_op jit(solution)/shard_map/ppermute | solution.py:19

commit v8 on v7

--- a/solution.py
+++ b/solution.py
@@ -208,14 +208,16 @@
     return jnp.dot(left, right, preferred_element_type=jnp.float32)
 
 
-def pick_kernel(flags, outer, inner, out):
-    @pl.when(flags[2] != 0)
-    def _():
-        out[...] = outer[...]
-
-    @pl.when(flags[2] == 0)
-    def _():
-        out[...] = inner[...]
+def pick(mask, outer, inner, piece):
+    return jnp.where(
+        mask[0:1, :] != 0.0, outer[piece, :].astype(jnp.float32), inner[piece, :].astype(jnp.float32)
+    )
+
+
+def pick_kernel(mask, outer, inner, out):
+    for at in range(0, outer.shape[0], 64):
+        piece = slice(at, at + 64)
+        out[piece, :] = pick(mask, outer, inner, piece).astype(out.dtype)
 
 
 def right_sums_kernel(first, second, third, row):
@@ -229,17 +231,13 @@
     row[...] = rows_of([shift] + [jnp.sum(s, axis=0, keepdims=True) for s in sums])
 
 
-def late_kernel(images, turned, flags, outer, inner, row, out, stats):
+def late_kernel(images, turned, mask, outer, inner, row, out):
     rows, quart = outer.shape
     shift = row[0:1, :]
     sums = [jnp.zeros((8, quart), jnp.float32)] * 3
-    from_outer = flags[2] != 0
     for at in range(0, rows, 128):
         piece = slice(at, at + 128)
-        value = jnp.where(
-            from_outer, outer[piece, :].astype(jnp.float32), inner[piece, :].astype(jnp.float32)
-        )
-        centred = value - shift
+        centred = pick(mask, outer, inner, piece) - shift
         low = centred.astype(jnp.bfloat16)
         if turned:
             out[:quart, piece] = jnp.transpose(low)
@@ -247,9 +245,7 @@
             out[piece, :] = low
         sums = add_sums(sums, centred, low)
     delta, rstd, gap = moments(joined_sums(row, sums), images)
-    values = [shift + delta, rstd, gap, delta]
-    stats[...] = rows_of(values)
-    out[rows:, :] = split_rows(values)
+    out[rows:, :] = split_rows([shift + delta, rstd, gap, delta])
 
 
 def products_kernel(*refs):
@@ -311,11 +307,11 @@
     return columns[:, 0:1], columns[:, 1:2]
 
 
-def partner_kernel(images, part, flags, late, zero, sums, late_b, *refs):
+def partner_kernel(images, part, late, zero, sums, late_b, *refs):
     if part:
-        (first_b, terms_in, across_in, vec_in, partial_out, e_out, mine_out, vec_out, left) = refs
+        (terms_in, across_in, vec_in, partial_out, e_out, vec_out, left) = refs
     else:
-        (terms_out, across_out, e_out, mine_out, vec_out, left) = refs
+        (terms_out, across_out, e_out, vec_out, left) = refs
     rows, quart = zero.shape
     width = quart // 2
     _, rstd, _, delta = joined_rows(late, rows)
@@ -331,16 +327,12 @@
         square = corr * corr
         across = across + fold_lanes(square)
         down.append(jnp.sum(square, axis=0, keepdims=True))
-
-        @pl.when(flags[0] == 2 * part + tile)
-        def _():
-            mine_out[...] = corr
-
     second_a = off_weight * jnp.concatenate(down, axis=1)
     if part:
         vec_out[...] = rows_of([second_a, second_a + vec_in[0:1, :]])
+        nothing = jnp.zeros((1, quart), jnp.float32)
         second = off_weight * lanes_to_row(across)
-        offset_b, rstd_b, _, _ = joined_rows(late_b, quart)
+        partial_out[rows:, :] = split_rows([second, nothing, nothing, nothing])
     else:
         vec_out[...] = rows_of([second_a])
         across_out[...] = across
@@ -348,19 +340,18 @@
         at = slice(tile * width, (tile + 1) * width)
         terms = dot_rows(left[...], e_out[at, :])
         if part:
-            xhat = (first_b[:, at].astype(jnp.float32) - offset_b[:, at]) * rstd_b[:, at]
-            partial_out[:, at] = (
-                without_extra(terms + terms_in[:, at], rows) - xhat * second[:, at]
-            ).astype(jnp.bfloat16)
+            partial_out[:rows, at] = without_extra(terms + terms_in[:, at], rows).astype(
+                jnp.bfloat16
+            )
         else:
             terms_out[:, at] = terms
 
 
 def own_kernel(images, flags, *refs):
     (late_own, late_other, first_own, first_other, zero_own, zero_other, sums, late_b) = refs[:8]
-    (late_b_other, first_b, first_b_other, e_left, e_right, mine_left, mine_right) = refs[8:15]
+    (late_b_other, first_b, first_b_other, e_left, e_right, partner_own, partner_other) = refs[8:15]
     (vec_own, vec_other, vec_core, right_out, left_out, left_partial_out, mine_out) = refs[15:22]
-    (own_loss_out, loss_out, left, norm_b, e_own, mine_own) = refs[22:]
+    (own_loss_out, loss_out, left, norm_b, e_own, mine_own, mine_partner) = refs[22:]
     rows, quart = zero_own.shape
     width = quart // 2
     lower, upper = slice(0, quart), slice(quart, 2 * quart)
@@ -380,16 +371,22 @@
         rest = jnp.broadcast_to(stats[2] * stats[1], (16, quart))
         norm_b[rows:, lanes] = rest.astype(jnp.bfloat16)
 
-    scale_col, delta_col = scale_columns(late_b, images)
+    def tile_corr(late, inner, total, columns, block):
+        scale_col, delta_col = columns
+        total = total + dot(block[:quart, :], late[:rows, inner])
+        row = joined_rows(late, rows)
+        return (total * scale_col - delta_col * row[3][:, inner]) * row[1][:, inner]
+
+    columns = scale_columns(late_b, images)
+    columns_partner = scale_columns(late_b_other, images)
     across = jnp.zeros((quart, 128), jnp.float32)
     losses = jnp.zeros((8, 128), jnp.float32)
-    down = []
+    down, diagonals = [], []
     for tile in range(4):
         at = slice(tile * width, (tile + 1) * width)
         inner = slice((tile % 2) * width, (tile % 2 + 1) * width)
         late = late_own if tile < 2 else late_other
-        total = sums[:, at] + dot(late_b[:quart, :], late[:rows, inner])
-        corr = (total * scale_col - delta_col * delta[:, at]) * rstd[:, at]
+        corr = tile_corr(late, inner, sums[:, at], columns, late_b)
         dcorr = off_weight * corr
         product = dcorr * corr
         loss = product
@@ -397,9 +394,11 @@
             feature = lax.broadcasted_iota(jnp.int32, (quart, width), 0)
             lane = lax.broadcasted_iota(jnp.int32, (quart, width), 1) + tile * width
             diagonal = feature == lane
-            dcorr = jnp.where(diagonal, corr - 1.0, dcorr)
-            product = dcorr * corr
-            loss = jnp.where(diagonal, dcorr * dcorr, product)
+            slope = jnp.where(diagonal, (corr - 1.0).astype(jnp.bfloat16).astype(jnp.float32), 0.0)
+            diagonals.append(jnp.sum(slope, axis=0, keepdims=True))
+            dcorr = jnp.where(diagonal, 0.0, dcorr)
+            product = jnp.where(diagonal, slope * corr, product)
+            loss = jnp.where(diagonal, (1.0 - corr) * (1.0 - corr), loss)
         e_own[:, at] = (dcorr * rstd[:, at]).astype(jnp.bfloat16)
         across = across + fold_lanes(product)
         losses = losses + fold_rows(fold_lanes(loss))
@@ -408,7 +407,12 @@
         @pl.when(flags[0] == tile)
         def _():
             mine_own[...] = corr
-
+            partner = partner_own if tile < 2 else partner_other
+            mine_partner[...] = tile_corr(
+                late, inner, partner[:, inner], columns_partner, late_b_other
+            )
+
+    diagonal_row = jnp.concatenate(diagonals, axis=1)
     partner_second = jnp.concatenate([vec_own[0:1, :], vec_other[0:1, :]], axis=1)
     second_a = rstd * (partner_second + jnp.concatenate(down, axis=1))
     second_b = lanes_to_row(across)
@@ -424,7 +428,8 @@
         xhat = (source[:, inner].astype(jnp.float32) - offset[:, at]) * rstd[:, at]
         value = terms[:rows] - terms[rows : rows + 1] - xhat * second_a[:, at]
         if tile < 2:
-            left_out[:, inner] = value
+            slope = rstd[:, at] * diagonal_row[:, inner]
+            left_out[:, inner] = value + norm_b[:rows, inner].astype(jnp.float32) * slope
         else:
             left_partial_out[:, inner] = value.astype(jnp.bfloat16)
 
@@ -432,10 +437,14 @@
         at = slice(tile * width, (tile + 1) * width)
         terms = dot_rows(left[...], e_own[at, :])
         xhat = (first_b[:, at].astype(jnp.float32) - own_b[0][:, at]) * own_b[1][:, at]
-        right_out[:, at] = without_extra(terms, rows) - xhat * second_b[:, at]
+        norm_a = (first_own[:, at].astype(jnp.float32) - offset[:, at]) * rstd[:, at]
+        norm_a = norm_a.astype(jnp.bfloat16).astype(jnp.float32)
+        right_out[:, at] = (
+            without_extra(terms, rows) - xhat * second_b[:, at] + norm_a * diagonal_row[:, at]
+        )
 
     own_columns = jnp.transpose(mine_own[...])
-    partner_columns = jnp.transpose(jnp.where(flags[0] < 2, mine_left[...], mine_right[...]))
+    partner_columns = jnp.transpose(mine_partner[...])
 
     @pl.when(flags[1] == 0)
     def _():
@@ -448,25 +457,28 @@
         mine_out[:, upper] = own_columns
 
 
-def left_final_kernel(own, other, loss, core_loss, out, loss_out):
-    for at in range(0, own.shape[0], 64):
+def add_kernel(one, other, out):
+    out[0, 0] = one[0, 0] + other[0, 0]
+
+
+def final_kernel(right, from_x, late_b, first_b, left, from_core, right_out, left_out):
+    rows, quart = left.shape
+    offset, rstd, _, _ = joined_rows(late_b, quart)
+    second = joined_rows(from_x, rows)[0]
+    for at in range(0, rows, 64):
         piece = slice(at, at + 64)
-        out[piece, :] = (own[piece, :] + other[piece, :].astype(jnp.float32)).astype(jnp.bfloat16)
-    loss_out[0, 0] = loss[0, 0] + core_loss[0, 0]
-
-
-def right_final_kernel(own, other, stats, out):
-    for at in range(0, own.shape[0], 64):
-        piece = slice(at, at + 64)
-        value = stats[1:2, :] * (own[piece, :] + other[piece, :].astype(jnp.float32))
-        out[piece, :] = value.astype(jnp.bfloat16)
+        xhat = (first_b[piece, :].astype(jnp.float32) - offset) * rstd
+        value = right[piece, :] + from_x[piece, :].astype(jnp.float32) - xhat * second
+        right_out[piece, :] = (rstd * value).astype(jnp.bfloat16)
+        value = left[piece, :] + from_core[piece, :].astype(jnp.float32)
+        left_out[piece, :] = value.astype(jnp.bfloat16)
 
 
 vmem = pl.BlockSpec(memory_space=pltpu.VMEM)
 smem = pl.BlockSpec(memory_space=pltpu.SMEM)
 
 
-def local_call(kernel, operands, outs, scratch=(), flops=2**20, room=8):
+def local_call(kernel, operands, outs, scratch=(), flops=2**20, room=8, held=()):
     moved = sum(x.size * x.dtype.itemsize for x in (*operands, *outs))
 
     def space(x):
@@ -480,7 +492,7 @@
         scratch_shapes=list(scratch),
         compiler_params=pltpu.CompilerParams(vmem_limit_bytes=room * 2**20),
         cost_estimate=pl.CostEstimate(flops=flops, bytes_accessed=moved, transcendentals=0),
-    )(*operands)
+    )(*(pltpu.with_memory_space_constraint(x, pltpu.VMEM) if i in held else x for i, x in enumerate(operands)))
 
 
 def gathered_device(left_outputs, right_outputs):
@@ -494,7 +506,9 @@
     column_halves = tpos % 2
     at_end = (dpos == 0) | (dpos == 3)
     owned_tile = jnp.where(dpos // 2 == column_halves, 0, 2) + dpos % 2
-    flags = jnp.stack([owned_tile, row_halves, at_end, dpos]).astype(jnp.int32)
+    flags = jnp.stack([owned_tile, row_halves]).astype(jnp.int32)
+    mask = jnp.broadcast_to(at_end.astype(jnp.float32), (8, quart))
+    mask, flags = lax.optimization_barrier((mask, flags))
 
     pairs = [(0, 1), (1, 0), (2, 3), (3, 2)]
     middle = [(1, 2), (2, 1)]
@@ -519,12 +533,11 @@
     extended = jax.ShapeDtypeStruct((rows + 16, quart), jnp.bfloat16)
     row_out = jax.ShapeDtypeStruct((8, quart), jnp.float32)
     one_out = jax.ShapeDtypeStruct((1, 1), jnp.float32)
-    mine_shape = jax.ShapeDtypeStruct((quart, width), jnp.float32)
     across_shape = jax.ShapeDtypeStruct((quart, 128), jnp.float32)
     low = lambda n, m: pltpu.VMEM((n, m), jnp.bfloat16)
 
     def picked(outer, inner):
-        return local_call(pick_kernel, (flags, outer, inner), (quarter_bf16,))[0]
+        return local_call(pick_kernel, (mask, outer, inner), (quarter_bf16,))[0]
 
     first_b = along(right_outputs, pairs)
     inner_b = along(right_outputs, middle)
@@ -552,10 +565,11 @@
     second_a, other_a1, row_b = after(second_a, other_a1, row_b)
     other_a2 = core_swap(second_a)
 
-    late_b, stats_b = local_call(
+    (late_b,) = local_call(
         functools.partial(late_kernel, batch_images, True),
-        (flags, last_b, third_b, row_b),
-        (extended, row_out),
+        (mask, last_b, third_b, row_b),
+        (extended,),
+        held=(0, 1, 2, 3),
     )
     late_b_other = x_swap(late_b)
     partner_own, partner_other, own_all, row_other, zero_own, zero_other = local_call(
@@ -575,32 +589,31 @@
         room=20,
     )
     row_a = core_swap(row_other)
-    late_a, stats_a = local_call(
+    (late_a,) = local_call(
         functools.partial(late_kernel, batch_images, False),
-        (flags, last_a, third_a, row_a),
-        (extended, row_out),
+        (mask, last_a, third_a, row_a),
+        (extended,),
+        held=(0, 1, 2, 3),
     )
     late_a_other = core_swap(late_a)
 
-    terms, across, e_left, mine_left, vec_own = local_call(
+    terms, across, e_left, vec_own = local_call(
         functools.partial(partner_kernel, batch_images, 0),
-        (flags, late_a, zero_own, partner_own, late_b_other),
+        (late_a, zero_own, partner_own, late_b_other),
         (
             jax.ShapeDtypeStruct((rows + 16, quart), jnp.float32),
             across_shape,
             quarter_bf16,
-            mine_shape,
             row_out,
         ),
         [low(rows + 16, quart)],
         2 * gemm,
         room=12,
     )
-    partial_right, e_right, mine_right, vec_other = local_call(
+    partial_right, e_right, vec_other = local_call(
         functools.partial(partner_kernel, batch_images, 1),
-        (flags, late_a_other, zero_other, partner_other, late_b_other, other_b0)
-        + (terms, across, vec_own),
-        (quarter_bf16, quarter_bf16, mine_shape, row_out),
+        (late_a_other, zero_other, partner_other, late_b_other, terms, across, vec_own),
+        (extended, quarter_bf16, row_out),
         [low(rows + 16, quart)],
         2 * gemm,
         room=12,
@@ -610,7 +623,8 @@
     right_own, left_own, partial_left, mine, own_loss, loss = local_call(
         functools.partial(own_kernel, batch_images),
         (flags, late_a, late_a_other, left_outputs, other_a0, zero_own, zero_other, own_all)
-        + (late_b, late_b_other, right_outputs, other_b0, e_left, e_right, mine_left, mine_right)
+        + (late_b, late_b_other, right_outputs, other_b0, e_left, e_right)
+        + (partner_own, partner_other)
         + (vec_own, vec_other, vec_core),
         (
             quarter_f32,
@@ -625,22 +639,24 @@
             low(rows + 16, half),
             low(quart, half),
             pltpu.VMEM((quart, width), jnp.float32),
+            pltpu.VMEM((quart, width), jnp.float32),
         ],
         8 * gemm,
         room=20,
     )
     from_core = core_swap(partial_left)
     core_loss = jnp.reshape(core_swap(jnp.reshape(own_loss, ())), (1, 1))
-    left_gradient, loss = local_call(
-        left_final_kernel, (left_own, from_core, loss, core_loss), (quarter_bf16, one_out)
-    )
+    (loss,) = local_call(add_kernel, (loss, core_loss), (one_out,))
     loss = jnp.reshape(loss, ())
-    right_own, loss = after(right_own, loss)
-    loss = loss + x_swap(loss)
-    (right_gradient,) = local_call(
-        right_final_kernel, (right_own, from_x, stats_b), (quarter_bf16,)
-    )
-    return (left_gradient, right_gradient, mine[None, :, :], jnp.reshape(loss / feats, (1,)))
+    x_loss = x_swap(loss)
+    right_gradient, left_gradient = local_call(
+        final_kernel,
+        (right_own, from_x, late_b, right_outputs, left_own, from_core),
+        (quarter_bf16, quarter_bf16),
+    )
+    right_gradient, x_loss = after(right_gradient, x_loss)
+    loss = jnp.reshape((loss + x_loss) / feats, (1,))
+    return (left_gradient, right_gradient, mine[None, :, :], loss)
 
 
 def solution(mesh):

time: 107 us -> 99.4 us (0.929)
  Pallas kernels: 25.8 us -> 20.5 us
  waiting for transfers between devices: 48.9 us -> 45.4 us
  local copies, waits for them, and re-layouts: 1.04 us -> 3.78 us
  starting transfers between devices: 27.2 us -> 25.8 us
    ppermute x14, waiting for transfers between devices: 12.7 us -> 4.46 us  [swapped(): return lax.ppermute(block, axis, route)]
    pallas_call x11, Pallas kernels: 25.8 us -> 20.5 us  [local_call(): pl.pallas_call(kernel, out_shape=list(outs), in_specs=[space(x) for x in...]
    ppermute x10, waiting for transfers between devices: 36.3 us -> 41 us  [along(): return lax.ppermute(block, 'dp', route)]
    unnamed x6 -> x14, local copies, waits for them, and re-layouts: 1.04 us -> 3.78 us
    ppermute x10, starting transfers between devices: 16.9 us -> 15.3 us  [along(): return lax.ppermute(block, 'dp', route)]
  transfers between devices with their start and end apart: 24 -> 24, of which waited for: 10 -> 11; matrix products, arithmetic and copies ran while one was open for 0% -> 0% of each run, Pallas kernels for 15% -> 19%
where the time goes in v8:
time: 99.4 us; the launch traced here: 98.9 us
  waiting for transfers between devices  45.4 us (46%)
  starting transfers between devices  25.8 us (26%)
  Pallas kernels  20.5 us (21%)
  local copies, waits for them, and re-layouts  3.78 us (4%)
  between operations  3.29 us (3%)
    ppermute x10, waiting for transfers between devices, along(): return lax.ppermute(block, 'dp', route)  41 us
    pallas_call x11, Pallas kernels, local_call(): pl.pallas_call(kernel, out_shape=list(outs), in_specs=[space(x) for x in...  20.5 us
    ppermute x10, starting transfers between devices, along(): return lax.ppermute(block, 'dp', route)  15.3 us
    ppermute x14, starting transfers between devices, swapped(): return lax.ppermute(block, axis, route)  10.5 us
    ppermute x14, waiting for transfers between devices, swapped(): return lax.ppermute(block, axis, route)  4.46 us
    unnamed x14, local copies, waits for them, and re-layouts  3.78 us
  transfers between devices with their start and end apart: 24, of which 11 were waited for; matrix products, arithmetic and copies ran while one was open for 0% of the time, Pallas kernels for 19%

profile of v8, /device:TPU:0, one launch (start us, length us, event | category | flops | bytes accessed | tf_op | source)
XLA Modules:
  0.0 98.9 jit_solution(9022200641562893428)
XLA Ops:
  0.6 3.1 %collective-permute-start = (bf16[512,512]{1,0:T(8,128)(2,1)}, bf16[512,512]{1,0:T(8,128)(2,1)}, u32[]{:S(2)}, u32[]{:S(2)}) collective-permute-start(bf16[512,512]{1,0:T(8,128)(2,1)} %refs_2_.1), channel_id=1, source_target_pairs={{0,4},{4,0},{8,12},{12,8},{1,5},{5,1},{9,13},{13,9},{2,6},{6,2},{1... | collective-permute-start | bytes 1572872 | tf_op jit(solution)/shard_map/ppermute | solution.py:518
  4.4 1.6 %collective-permute-start.11 = (bf16[512,512]{1,0:T(8,128)(2,1)}, bf16[512,512]{1,0:T(8,128)(2,1)S(1)}, u32[]{:S(2)}, u32[]{:S(2)}) collective-permute-start(bf16[512,512]{1,0:T(8,128)(2,1)} %first_b.1), channel_id=1, source_target_pairs={{0,2},{2,0},{1,3},{3,1},{4,6},{6,4},{5,7},{7,5},{8,10},{10,8},{9,1... | collective-permute-start | bytes 1572872 | tf_op jit(solution)/shard_map/ppermute | solution.py:19
  6.0 4.4 %collective-permute-start.7 = (bf16[512,512]{1,0:T(8,128)(2,1)}, bf16[512,512]{1,0:T(8,128)(2,1)S(1)}, u32[]{:S(2)}, u32[]{:S(2)}) collective-permute-start(bf16[512,512]{1,0:T(8,128)(2,1)} %first_b.1), channel_id=1, source_target_pairs={{0,4},{4,0},{8,12},{12,8},{1,5},{5,1},{9,13},{13,9},{2,6},{6,2},{1... | collective-permute-start | bytes 1572872 | tf_op jit(solution)/shard_map/ppermute | solution.py:518
  10.3 6.5 %collective-permute-done.refs_2_ = bf16[512,512]{1,0:T(8,128)(2,1)} collective-permute-done((bf16[512,512]{1,0:T(8,128)(2,1)}, bf16[512,512]{1,0:T(8,128)(2,1)}, u32[]{:S(2)}, u32[]{:S(2)}) %collective-permute-start) | collective-permute-done | bytes 524320 | tf_op jit(solution)/shard_map/ppermute | solution.py:518
  17.5 1.3 %collective-permute-start.9 = (bf16[512,512]{1,0:T(8,128)(2,1)S(1)}, bf16[512,512]{1,0:T(8,128)(2,1)S(1)}, u32[]{:S(2)}, u32[]{:S(2)}) collective-permute-start(bf16[512,512]{1,0:T(8,128)(2,1)S(1)} %collective-permute-done.8.inner), channel_id=1, source_target_pairs={{4,0},{8,12},{5,1},{9,13},{6,2},{10,14},{7,3},{11,15},{20,16},{24,... | collective-permute-start | bytes 1572872 | tf_op jit(solution)/shard_map/ppermute | solution.py:518
  18.8 0.8 copy-done.5
  19.6 8.3 %collective-permute-done.7.second.refs_8_ = bf16[512,512]{1,0:T(8,128)(2,1)S(1)} collective-permute-done((bf16[512,512]{1,0:T(8,128)(2,1)}, bf16[512,512]{1,0:T(8,128)(2,1)S(1)}, u32[]{:S(2)}, u32[]{:S(2)}) %collective-permute-start.7) | collective-permute-done | bytes 524320 | tf_op jit(solution)/shard_map/ppermute | solution.py:518
  27.9 2.0 %collective-permute-start.12 = (bf16[512,512]{1,0:T(8,128)(2,1)S(1)}, bf16[512,512]{1,0:T(8,128)(2,1)}, u32[]{:S(2)}, u32[]{:S(2)}) collective-permute-start(bf16[512,512]{1,0:T(8,128)(2,1)S(1)} %collective-permute-done.7.second.refs_8_), channel_id=1, source_target_pairs={{0,2},{2,0},{1,3},{3,1},{4,6},{6,4},{5,7},{7,5},{8,10},{10,8},{9,1... | collective-permute-start | bytes 1572872 | tf_op jit(solution)/shard_map/ppermute | solution.py:19
  30.6 1.3 %collective-permute-start.5 = (bf16[512,512]{1,0:T(8,128)(2,1)S(1)}, bf16[512,512]{1,0:T(8,128)(2,1)S(1)}, u32[]{:S(2)}, u32[]{:S(2)}) collective-permute-start(bf16[512,512]{1,0:T(8,128)(2,1)S(1)} %collective-permute-done.4.inner), channel_id=1, source_target_pairs={{4,0},{8,12},{5,1},{9,13},{6,2},{10,14},{7,3},{11,15},{20,16},{24,... | collective-permute-start | bytes 1572872 | tf_op jit(solution)/shard_map/ppermute | solution.py:518
  32.0 7.2 %collective-permute-done.9.outer = bf16[512,512]{1,0:T(8,128)(2,1)S(1)} collective-permute-done((bf16[512,512]{1,0:T(8,128)(2,1)S(1)}, bf16[512,512]{1,0:T(8,128)(2,1)S(1)}, u32[]{:S(2)}, u32[]{:S(2)}) %collective-permute-start.9) | collective-permute-done | bytes 524320 | tf_op jit(solution)/shard_map/ppermute | solution.py:518
  39.2 0.8 copy-done.2
  40.8 1.0 %copy-done.3 = bf16[512,512]{1,0:T(8,128)(2,1)S(1)} copy-done((bf16[512,512]{1,0:T(8,128)(2,1)S(1)}, bf16[512,512]{1,0:T(8,128)(2,1)}, u32[]{:S(2)}) %copy-start.3) | copy-done | bytes 524312
  42.0 1.1 %copy-done = bf16[512,512]{1,0:T(8,128)(2,1)S(1)} copy-done((bf16[512,512]{1,0:T(8,128)(2,1)S(1)}, bf16[512,512]{1,0:T(8,128)(2,1)}, u32[]{:S(2)}) %copy-start) | copy-done | bytes 524312
  43.2 1.0 %shard_map.59.row = f32[8,512]{1,0:T(8,128)S(1)} custom-call(bf16[512,512]{1,0:T(8,128)(2,1)S(1)} %copy-done, bf16[512,512]{1,0:T(8,128)(2,1)S(1)} %collective-permute-done.7.second.refs_8_, bf16[512,512]{1,0:T(8,128)(2,1)S(1)} %shard_map.58.third.refs_10_), custom_call_target="tpu_custom_call" | custom-call | flops 1048576 | bytes 1589248 | tf_op jit(solution)/shard_map/pallas_call | solution.py:487
  44.2 2.1 %collective-permute-start.13 = (bf16[512,512]{1,0:T(8,128)(2,1)S(1)}, bf16[512,512]{1,0:T(8,128)(2,1)S(1)}, u32[]{:S(2)}, u32[]{:S(2)}) collective-permute-start(bf16[512,512]{1,0:T(8,128)(2,1)S(1)} %shard_map.58.third.refs_10_), channel_id=1, source_target_pairs={{0,2},{2,0},{1,3},{3,1},{4,6},{6,4},{5,7},{7,5},{8,10},{10,8},{9,1... | collective-permute-start | bytes 1572872 | tf_op jit(solution)/shard_map/ppermute | solution.py:19
  46.3 3.3 %collective-permute-done.5.outer = bf16[512,512]{1,0:T(8,128)(2,1)S(1)} collective-permute-done((bf16[512,512]{1,0:T(8,128)(2,1)S(1)}, bf16[512,512]{1,0:T(8,128)(2,1)S(1)}, u32[]{:S(2)}, u32[]{:S(2)}) %collective-permute-start.5) | collective-permute-done | bytes 524320 | tf_op jit(solution)/shard_map/ppermute | solution.py:518
  49.6 1.3 %collective-permute-start.17 = (bf16[512,512]{1,0:T(8,128)(2,1)S(1)}, bf16[512,512]{1,0:T(8,128)(2,1)S(1)}, u32[]{:S(2)}, u32[]{:S(2)}) collective-permute-start(bf16[512,512]{1,0:T(8,128)(2,1)S(1)} %collective-permute-done.16.inner), channel_id=1, source_target_pairs={{4,0},{8,12},{5,1},{9,13},{6,2},{10,14},{7,3},{11,15},{20,16},{24,... | collective-permute-start | bytes 1572872 | tf_op jit(solution)/shard_map/ppermute | solution.py:518
  51.1 1.3 %collective-permute-start.2 = (bf16[512,512]{1,0:T(8,128)(2,1)S(1)}, bf16[512,512]{1,0:T(8,128)(2,1)S(1)}, u32[]{:S(2)}, u32[]{:S(2)}) collective-permute-start(bf16[512,512]{1,0:T(8,128)(2,1)S(1)} %collective-permute-done.1.inner), channel_id=1, source_target_pairs={{4,0},{8,12},{5,1},{9,13},{6,2},{10,14},{7,3},{11,15},{20,16},{24,... | collective-permute-start | bytes 1572872 | tf_op jit(solution)/shard_map/ppermute | solution.py:518
  52.4 13.9 %collective-permute-done.17.outer = bf16[512,512]{1,0:T(8,128)(2,1)S(1)} collective-permute-done((bf16[512,512]{1,0:T(8,128)(2,1)S(1)}, bf16[512,512]{1,0:T(8,128)(2,1)S(1)}, u32[]{:S(2)}, u32[]{:S(2)}) %collective-permute-start.17) | collective-permute-done | bytes 524320 | tf_op jit(solution)/shard_map/ppermute | solution.py:518
  66.7 1.7 %collective-permute-start.18 = (bf16[528,512]{1,0:T(8,128)(2,1)S(1)}, bf16[528,512]{1,0:T(8,128)(2,1)S(1)}, u32[]{:S(2)}, u32[]{:S(2)}) collective-permute-start(bf16[528,512]{1,0:T(8,128)(2,1)S(1)} %shard_map.62.refs_7_.late_b), channel_id=1, source_target_pairs={{0,2},{2,0},{1,3},{3,1},{4,6},{6,4},{5,7},{7,5},{8,10},{10,8},{9,1... | collective-permute-start | bytes 1622024 | tf_op jit(solution)/shard_map/ppermute | solution.py:19
  68.5 5.4 %shard_map.60 = (f32[512,512]{1,0:T(8,128)S(1)}, f32[512,512]{1,0:T(8,128)S(1)}, f32[512,1024]{1,0:T(8,128)S(1)}, f32[8,512]{1,0:T(8,128)S(1)}, bf16[512,512]{1,...) custom-call(bf16[512,512]{1,0:T(8,128)(2,1)S(1)} %copy-done.4, bf16[512,512]{1,0:T(8,128)(2,1)S(1)} %collective-permute-done.3.refs_1_.refs_3_, ...), custom_call_target="tpu_custom_call" | custom-call | flops 3221225472 | bytes 11550720 | tf_op jit(solution)/shard_map/pallas_call | solution.py:487
  74.0 1.8 %collective-permute-done.2.outer = bf16[512,512]{1,0:T(8,128)(2,1)S(1)} collective-permute-done((bf16[512,512]{1,0:T(8,128)(2,1)S(1)}, bf16[512,512]{1,0:T(8,128)(2,1)S(1)}, u32[]{:S(2)}, u32[]{:S(2)}) %collective-permute-start.2) | collective-permute-done | bytes 524320 | tf_op jit(solution)/shard_map/ppermute | solution.py:518
  76.3 1.3 %collective-permute-done.18.late_b.refs_8_ = bf16[528,512]{1,0:T(8,128)(2,1)S(1)} collective-permute-done((bf16[528,512]{1,0:T(8,128)(2,1)S(1)}, bf16[528,512]{1,0:T(8,128)(2,1)S(1)}, u32[]{:S(2)}, u32[]{:S(2)}) %collective-permute-start.18) | collective-permute-done | bytes 540704 | tf_op jit(solution)/shard_map/ppermute | solution.py:19
  77.6 1.1 %shard_map.63 = (f32[528,512]{1,0:T(8,128)S(1)}, f32[512,128]{1,0:T(8,128)S(1)}, bf16[512,512]{1,0:T(8,128)(2,1)S(1)}, f32[8,512]{1,0:T(8,128)S(1)}) custom-call(bf16[528,512]{1,0:T(8,128)(2,1)S(1)} %shard_map.61.late.refs_0_, bf16[512,512]{1,0:T(8,128)(2,1)S(1)} %get-tuple-element.49.zero.refs_4_, f32[512,512]{1,0:T(8,128)S(1)} %get-tuple-element.53.sums.refs_13_, ...), custom_call_target="tpu_custom_call" | custom-call | flops 536870912 | bytes 4538368 | tf_op jit(solution)/shard_map/pallas_call | solution.py:487
  78.7 1.3 %shard_map.64 = (bf16[528,512]{1,0:T(8,128)(2,1)S(1)}, bf16[512,512]{1,0:T(8,128)(2,1)S(1)}, f32[8,512]{1,0:T(8,128)S(1)}) custom-call(bf16[528,512]{1,0:T(8,128)(2,1)S(1)} %collective-permute-done.15.late.refs_1_, bf16[512,512]{1,0:T(8,128)(2,1)S(1)} %get-tuple-element.50.zero.refs_5_, f32[512,512]{1,0:T(8,128)S(1)} %get-tuple-element.55.sums.refs_14_, ...), custom_call_target="tpu_custom_call" | custom-call | flops 536870912 | bytes 5095424 | tf_op jit(solution)/shard_map/pallas_call | solution.py:487
  80.0 1.1 %collective-permute-start.20 = (bf16[528,512]{1,0:T(8,128)(2,1)S(1)}, bf16[528,512]{1,0:T(8,128)(2,1)S(1)}, u32[]{:S(2)}, u32[]{:S(2)}) collective-permute-start(bf16[528,512]{1,0:T(8,128)(2,1)S(1)} %get-tuple-element.62), channel_id=1, source_target_pairs={{0,2},{2,0},{1,3},{3,1},{4,6},{6,4},{5,7},{7,5},{8,10},{10,8},{9,1... | collective-permute-start | bytes 1622024 | tf_op jit(solution)/shard_map/ppermute | solution.py:19
  81.2 7.6 %shard_map.65 = (f32[512,512]{1,0:T(8,128)S(1)}, f32[512,512]{1,0:T(8,128)S(1)}, bf16[512,512]{1,0:T(8,128)(2,1)S(1)}, f32[256,1024]{1,0:T(8,128)}, f32[1,1]{1,0:T(1,128)}, /*index=5*/f32[1,1]{1,0:T(1,128)}) custom-call(s32[2]{0:T(128)S(1)} %pad_add_fusion.flags, bf16[528,512]{1,0:T(8,128)(2,1)S(1)} %shard_map.61.late.refs_0_, ...), custom_call_target="tpu_custom_call" | custom-call | flops 2147483648 | bytes 14270480 | tf_op jit(solution)/shard_map/pallas_call | solution.py:487
  89.4 1.6 %collective-permute-done.22 = f32[]{:T(128)} collective-permute-done((f32[]{:T(128)}, f32[]{:T(128)}, u32[]{:S(2)}, u32[]{:S(2)}) %collective-permute-start.22) | collective-permute-done | bytes 36 | tf_op jit(solution)/shard_map/ppermute | solution.py:19
  91.0 1.7 %shard_map.67 = f32[1,1]{1,0:T(1,128)} custom-call(f32[1,1]{1,0:T(1,128)} %get-tuple-element.67.one, f32[1,1]{1,0:T(1,128)} %bitcast.3.other), custom_call_target="tpu_custom_call" | custom-call | flops 1048576 | bytes 12 | tf_op jit(solution)/shard_map/pallas_call | solution.py:487
  92.8 1.1 %collective-permute-start.23 = (f32[]{:T(128)}, f32[]{:T(128)}, u32[]{:S(2)}, u32[]{:S(2)}) collective-permute-start(f32[]{:T(128)} %bitcast.4), channel_id=1, source_target_pairs={{0,2},{2,0},{1,3},{3,1},{4,6},{6,4},{5,7},{7,5},{8,10},{10,8},{9,1... | collective-permute-start | bytes 20 | tf_op jit(solution)/shard_map/ppermute | solution.py:19
  93.8 0.9 collective-permute-done.20.from_x
  94.7 1.3 %shard_map.66 = (bf16[512,512]{1,0:T(8,128)(2,1)}, bf16[512,512]{1,0:T(8,128)(2,1)}) custom-call(f32[512,512]{1,0:T(8,128)S(1)} %get-tuple-element.61.right, bf16[528,512]{1,0:T(8,128)(2,1)S(1)} %collective-permute-done.20.from_x, bf16[528,512]{1,0:T(8,128)(2,1)S(1)} %shard_map.62.refs_7_.late_b, bf16[512,512]{1,0:T(8,128)(2,1)S(1)} %copy-done.1, ...), custom_call_target="tpu_custom_call" | custom-call | flops 1048576 | bytes 5275648 | tf_op jit(solution)/shard_map/pallas_call | solution.py:487
  (43 shorter events, 5.6 us)
Async XLA Ops:
  0.6 16.2 %collective-permute-start = (bf16[512,512]{1,0:T(8,128)(2,1)}, bf16[512,512]{1,0:T(8,128)(2,1)}, u32[]{:S(2)}, u32[]{:S(2)}) collective-permute-start(bf16[512,512]{1,0:T(8,128)(2,1)} %refs_2_.1), channel_id=1, source_target_pairs={{0,4},{4,0},{8,12},{12,8},{1,5},{5,1},{9,13},{13,9},{2,6},{6,2},{1... | collective-permute-start | bytes 1572872 | tf_op jit(solution)/shard_map/ppermute | solution.py:518
  3.7 13.8 %collective-permute-start.8 = (bf16[512,512]{1,0:T(8,128)(2,1)}, bf16[512,512]{1,0:T(8,128)(2,1)S(1)}, u32[]{:S(2)}, u32[]{:S(2)}) collective-permute-start(bf16[512,512]{1,0:T(8,128)(2,1)} %first_b.1), channel_id=1, source_target_pairs={{4,8},{8,4},{5,9},{9,5},{6,10},{10,6},{7,11},{11,7},{20,24},{24,20... | collective-permute-start | bytes 1572872 | tf_op jit(solution)/shard_map/ppermute | solution.py:518
  4.4 14.4 %collective-permute-start.11 = (bf16[512,512]{1,0:T(8,128)(2,1)}, bf16[512,512]{1,0:T(8,128)(2,1)S(1)}, u32[]{:S(2)}, u32[]{:S(2)}) collective-permute-start(bf16[512,512]{1,0:T(8,128)(2,1)} %first_b.1), channel_id=1, source_target_pairs={{0,2},{2,0},{1,3},{3,1},{4,6},{6,4},{5,7},{7,5},{8,10},{10,8},{9,1... | collective-permute-start | bytes 1572872 | tf_op jit(solution)/shard_map/ppermute | solution.py:19
  6.0 22.0 %collective-permute-start.7 = (bf16[512,512]{1,0:T(8,128)(2,1)}, bf16[512,512]{1,0:T(8,128)(2,1)S(1)}, u32[]{:S(2)}, u32[]{:S(2)}) collective-permute-start(bf16[512,512]{1,0:T(8,128)(2,1)} %first_b.1), channel_id=1, source_target_pairs={{0,4},{4,0},{8,12},{12,8},{1,5},{5,1},{9,13},{13,9},{2,6},{6,2},{1... | collective-permute-start | bytes 1572872 | tf_op jit(solution)/shard_map/ppermute | solution.py:518
  16.8 13.8 %collective-permute-start.4 = (bf16[512,512]{1,0:T(8,128)(2,1)}, bf16[512,512]{1,0:T(8,128)(2,1)S(1)}, u32[]{:S(2)}, u32[]{:S(2)}) collective-permute-start(bf16[512,512]{1,0:T(8,128)(2,1)} %refs_2_.1), channel_id=1, source_target_pairs={{4,8},{8,4},{5,9},{9,5},{6,10},{10,6},{7,11},{11,7},{20,24},{24,20... | collective-permute-start | bytes 1572872 | tf_op jit(solution)/shard_map/ppermute | solution.py:518
  17.5 21.7 %collective-permute-start.9 = (bf16[512,512]{1,0:T(8,128)(2,1)S(1)}, bf16[512,512]{1,0:T(8,128)(2,1)S(1)}, u32[]{:S(2)}, u32[]{:S(2)}) collective-permute-start(bf16[512,512]{1,0:T(8,128)(2,1)S(1)} %collective-permute-done.8.inner), channel_id=1, source_target_pairs={{4,0},{8,12},{5,1},{9,13},{6,2},{10,14},{7,3},{11,15},{20,16},{24,... | collective-permute-start | bytes 1572872 | tf_op jit(solution)/shard_map/ppermute | solution.py:518
  18.8 0.8 copy-start.5
  27.9 14.0 %collective-permute-start.12 = (bf16[512,512]{1,0:T(8,128)(2,1)S(1)}, bf16[512,512]{1,0:T(8,128)(2,1)}, u32[]{:S(2)}, u32[]{:S(2)}) collective-permute-start(bf16[512,512]{1,0:T(8,128)(2,1)S(1)} %collective-permute-done.7.second.refs_8_), channel_id=1, source_target_pairs={{0,2},{2,0},{1,3},{3,1},{4,6},{6,4},{5,7},{7,5},{8,10},{10,8},{9,1... | collective-permute-start | bytes 1572872 | tf_op jit(solution)/shard_map/ppermute | solution.py:19
  29.9 14.3 %collective-permute-start.16 = (bf16[512,512]{1,0:T(8,128)(2,1)S(1)}, bf16[512,512]{1,0:T(8,128)(2,1)S(1)}, u32[]{:S(2)}, u32[]{:S(2)}) collective-permute-start(bf16[512,512]{1,0:T(8,128)(2,1)S(1)} %collective-permute-done.7.second.refs_8_), channel_id=1, source_target_pairs={{4,8},{8,4},{5,9},{9,5},{6,10},{10,6},{7,11},{11,7},{20,24},{24,20... | collective-permute-start | bytes 1572872 | tf_op jit(solution)/shard_map/ppermute | solution.py:518
  30.6 19.0 %collective-permute-start.5 = (bf16[512,512]{1,0:T(8,128)(2,1)S(1)}, bf16[512,512]{1,0:T(8,128)(2,1)S(1)}, u32[]{:S(2)}, u32[]{:S(2)}) collective-permute-start(bf16[512,512]{1,0:T(8,128)(2,1)S(1)} %collective-permute-done.4.inner), channel_id=1, source_target_pairs={{4,0},{8,12},{5,1},{9,13},{6,2},{10,14},{7,3},{11,15},{20,16},{24,... | collective-permute-start | bytes 1572872 | tf_op jit(solution)/shard_map/ppermute | solution.py:518
  31.9 19.1 %collective-permute-start.6 = (bf16[512,512]{1,0:T(8,128)(2,1)}, bf16[512,512]{1,0:T(8,128)(2,1)}, u32[]{:S(2)}, u32[]{:S(2)}) collective-permute-start(bf16[512,512]{1,0:T(8,128)(2,1)} %collective-permute-done.refs_2_), channel_id=1, source_target_pairs={{0,1},{1,0},{2,3},{3,2},{4,5},{5,4},{6,7},{7,6},{8,9},{9,8},{10,11... | collective-permute-start | bytes 1572872 | tf_op jit(solution)/shard_map/ppermute | solution.py:19
  39.2 0.8 copy-start.2
  39.9 11.1 %collective-permute-start.1 = (bf16[512,512]{1,0:T(8,128)(2,1)}, bf16[512,512]{1,0:T(8,128)(2,1)S(1)}, u32[]{:S(2)}, u32[]{:S(2)}) collective-permute-start(bf16[512,512]{1,0:T(8,128)(2,1)} %collective-permute-done.refs_2_), channel_id=1, source_target_pairs={{4,8},{8,4},{5,9},{9,5},{6,10},{10,6},{7,11},{11,7},{20,24},{24,20... | collective-permute-start | bytes 1572872 | tf_op jit(solution)/shard_map/ppermute | solution.py:518
  40.8 1.0 %copy-start.3 = (bf16[512,512]{1,0:T(8,128)(2,1)S(1)}, bf16[512,512]{1,0:T(8,128)(2,1)}, u32[]{:S(2)}) copy-start(bf16[512,512]{1,0:T(8,128)(2,1)} %copy-done.2) | copy-start | bytes 1572868
  41.8 26.7 %copy-start.1 = (bf16[512,512]{1,0:T(8,128)(2,1)S(1)}, bf16[512,512]{1,0:T(8,128)(2,1)}, u32[]{:S(2)}) copy-start(bf16[512,512]{1,0:T(8,128)(2,1)} %first_b.1) | copy-start | bytes 1572868
  41.8 26.7 %copy-start.4 = (bf16[512,512]{1,0:T(8,128)(2,1)S(1)}, bf16[512,512]{1,0:T(8,128)(2,1)}, u32[]{:S(2)}) copy-start(bf16[512,512]{1,0:T(8,128)(2,1)} %refs_2_.1) | copy-start | bytes 1572868
  41.8 26.7 %copy-start.6 = (bf16[512,512]{1,0:T(8,128)(2,1)S(1)}, bf16[512,512]{1,0:T(8,128)(2,1)}, u32[]{:S(2)}) copy-start(bf16[512,512]{1,0:T(8,128)(2,1)} %copy-done.5) | copy-start | bytes 1572868
  42.0 26.5 %collective-permute-start.3 = (bf16[512,512]{1,0:T(8,128)(2,1)}, bf16[512,512]{1,0:T(8,128)(2,1)S(1)}, u32[]{:S(2)}, u32[]{:S(2)}) collective-permute-start(bf16[512,512]{1,0:T(8,128)(2,1)} %refs_2_.1), channel_id=1, source_target_pairs={{0,1},{1,0},{2,3},{3,2},{4,5},{5,4},{6,7},{7,6},{8,9},{9,8},{10,11... | collective-permute-start | bytes 1572872 | tf_op jit(solution)/shard_map/ppermute | solution.py:19
  42.0 1.2 %copy-start = (bf16[512,512]{1,0:T(8,128)(2,1)S(1)}, bf16[512,512]{1,0:T(8,128)(2,1)}, u32[]{:S(2)}) copy-start(bf16[512,512]{1,0:T(8,128)(2,1)} %first_b.1) | copy-start | bytes 1572868
  44.2 24.3 %collective-permute-start.13 = (bf16[512,512]{1,0:T(8,128)(2,1)S(1)}, bf16[512,512]{1,0:T(8,128)(2,1)S(1)}, u32[]{:S(2)}, u32[]{:S(2)}) collective-permute-start(bf16[512,512]{1,0:T(8,128)(2,1)S(1)} %shard_map.58.third.refs_10_), channel_id=1, source_target_pairs={{0,2},{2,0},{1,3},{3,1},{4,6},{6,4},{5,7},{7,5},{8,10},{10,8},{9,1... | collective-permute-start | bytes 1572872 | tf_op jit(solution)/shard_map/ppermute | solution.py:19
  49.6 16.7 %collective-permute-start.17 = (bf16[512,512]{1,0:T(8,128)(2,1)S(1)}, bf16[512,512]{1,0:T(8,128)(2,1)S(1)}, u32[]{:S(2)}, u32[]{:S(2)}) collective-permute-start(bf16[512,512]{1,0:T(8,128)(2,1)S(1)} %collective-permute-done.16.inner), channel_id=1, source_target_pairs={{4,0},{8,12},{5,1},{9,13},{6,2},{10,14},{7,3},{11,15},{20,16},{24,... | collective-permute-start | bytes 1572872 | tf_op jit(solution)/shard_map/ppermute | solution.py:518
  51.0 17.5 %collective-permute-start.10 = (bf16[512,512]{1,0:T(8,128)(2,1)S(1)}, bf16[512,512]{1,0:T(8,128)(2,1)S(1)}, u32[]{:S(2)}, u32[]{:S(2)}) collective-permute-start(bf16[512,512]{1,0:T(8,128)(2,1)S(1)} %shard_map.57.refs_4_), channel_id=1, source_target_pairs={{0,1},{1,0},{2,3},{3,2},{4,5},{5,4},{6,7},{7,6},{8,9},{9,8},{10,11... | collective-permute-start | bytes 1572872 | tf_op jit(solution)/shard_map/ppermute | solution.py:19
  51.1 24.7 %collective-permute-start.2 = (bf16[512,512]{1,0:T(8,128)(2,1)S(1)}, bf16[512,512]{1,0:T(8,128)(2,1)S(1)}, u32[]{:S(2)}, u32[]{:S(2)}) collective-permute-start(bf16[512,512]{1,0:T(8,128)(2,1)S(1)} %collective-permute-done.1.inner), channel_id=1, source_target_pairs={{4,0},{8,12},{5,1},{9,13},{6,2},{10,14},{7,3},{11,15},{20,16},{24,... | collective-permute-start | bytes 1572872 | tf_op jit(solution)/shard_map/ppermute | solution.py:518
  66.7 10.9 %collective-permute-start.18 = (bf16[528,512]{1,0:T(8,128)(2,1)S(1)}, bf16[528,512]{1,0:T(8,128)(2,1)S(1)}, u32[]{:S(2)}, u32[]{:S(2)}) collective-permute-start(bf16[528,512]{1,0:T(8,128)(2,1)S(1)} %shard_map.62.refs_7_.late_b), channel_id=1, source_target_pairs={{0,2},{2,0},{1,3},{3,1},{4,6},{6,4},{5,7},{7,5},{8,10},{10,8},{9,1... | collective-permute-start | bytes 1622024 | tf_op jit(solution)/shard_map/ppermute | solution.py:19
  73.9 1.9 %collective-permute-start.14 = (f32[8,512]{1,0:T(8,128)S(1)}, f32[8,512]{1,0:T(8,128)S(1)}, u32[]{:S(2)}, u32[]{:S(2)}) collective-permute-start(f32[8,512]{1,0:T(8,128)S(1)} %get-tuple-element.48), channel_id=1, source_target_pairs={{0,1},{1,0},{2,3},{3,2},{4,5},{5,4},{6,7},{7,6},{8,9},{9,8},{10,11... | collective-permute-start | bytes 49160 | tf_op jit(solution)/shard_map/ppermute | solution.py:19
  76.2 2.5 %collective-permute-start.15 = (bf16[528,512]{1,0:T(8,128)(2,1)S(1)}, bf16[528,512]{1,0:T(8,128)(2,1)S(1)}, u32[]{:S(2)}, u32[]{:S(2)}) collective-permute-start(bf16[528,512]{1,0:T(8,128)(2,1)S(1)} %shard_map.61.late.refs_0_), channel_id=1, source_target_pairs={{0,1},{1,0},{2,3},{3,2},{4,5},{5,4},{6,7},{7,6},{8,9},{9,8},{10,11... | collective-permute-start | bytes 1622024 | tf_op jit(solution)/shard_map/ppermute | solution.py:19
  80.0 1.2 %collective-permute-start.19 = (f32[8,512]{1,0:T(8,128)S(1)}, f32[8,512]{1,0:T(8,128)S(1)}, u32[]{:S(2)}, u32[]{:S(2)}) collective-permute-start(f32[8,512]{1,0:T(8,128)S(1)} %get-tuple-element.60.refs_16_), channel_id=1, source_target_pairs={{0,1},{1,0},{2,3},{3,2},{4,5},{5,4},{6,7},{7,6},{8,9},{9,8},{10,11... | collective-permute-start | bytes 49160 | tf_op jit(solution)/shard_map/ppermute | solution.py:19
  80.0 14.7 %collective-permute-start.20 = (bf16[528,512]{1,0:T(8,128)(2,1)S(1)}, bf16[528,512]{1,0:T(8,128)(2,1)S(1)}, u32[]{:S(2)}, u32[]{:S(2)}) collective-permute-start(bf16[528,512]{1,0:T(8,128)(2,1)S(1)} %get-tuple-element.62), channel_id=1, source_target_pairs={{0,2},{2,0},{1,3},{3,1},{4,6},{6,4},{5,7},{7,5},{8,10},{10,8},{9,1... | collective-permute-start | bytes 1622024 | tf_op jit(solution)/shard_map/ppermute | solution.py:19
  88.8 5.0 %collective-permute-start.21 = (bf16[512,512]{1,0:T(8,128)(2,1)S(1)}, bf16[512,512]{1,0:T(8,128)(2,1)S(1)}, u32[]{:S(2)}, u32[]{:S(2)}) collective-permute-start(bf16[512,512]{1,0:T(8,128)(2,1)S(1)} %get-tuple-element.64), channel_id=1, source_target_pairs={{0,1},{1,0},{2,3},{3,2},{4,5},{5,4},{6,7},{7,6},{8,9},{9,8},{10,11... | collective-permute-start | bytes 1572872 | tf_op jit(solution)/shard_map/ppermute | solution.py:19
  89.0 2.0 %collective-permute-start.22 = (f32[]{:T(128)}, f32[]{:T(128)}, u32[]{:S(2)}, u32[]{:S(2)}) collective-permute-start(f32[]{:T(128)} %bitcast.2), channel_id=1, source_target_pairs={{0,1},{1,0},{2,3},{3,2},{4,5},{5,4},{6,7},{7,6},{8,9},{9,8},{10,11... | collective-permute-start | bytes 20 | tf_op jit(solution)/shard_map/ppermute | solution.py:19
  92.8 3.8 %collective-permute-start.23 = (f32[]{:T(128)}, f32[]{:T(128)}, u32[]{:S(2)}, u32[]{:S(2)}) collective-permute-start(f32[]{:T(128)} %bitcast.4), channel_id=1, source_target_pairs={{0,2},{2,0},{1,3},{3,1},{4,6},{6,4},{5,7},{7,5},{8,10},{10,8},{9,1... | collective-permute-start | bytes 20 | tf_op jit(solution)/shard_map/ppermute | solution.py:19

commit v9 on v8

--- a/solution.py
+++ b/solution.py
@@ -417,8 +417,9 @@
     second_a = rstd * (partner_second + jnp.concatenate(down, axis=1))
     second_b = lanes_to_row(across)
     own_loss = jnp.sum(losses)
-    own_loss_out[0, 0] = own_loss
-    loss_out[0, 0] = own_loss + jnp.sum(vec_other[1:2, :] + vec_core[1:2, :])
+    own_loss_out[...] = jnp.broadcast_to(own_loss, (8, 128))
+    loss = own_loss + jnp.sum(vec_other[1:2, :] + vec_core[1:2, :])
+    loss_out[...] = jnp.broadcast_to(loss, (8, 128))
 
     for tile in (2, 3, 0, 1):
         at = slice(tile * width, (tile + 1) * width)
@@ -458,7 +459,11 @@
 
 
 def add_kernel(one, other, out):
-    out[0, 0] = one[0, 0] + other[0, 0]
+    out[...] = one[...] + other[...]
+
+
+def loss_kernel(feats, one, other, out):
+    out[0] = (one[0, 0] + other[0, 0]) / feats
 
 
 def final_kernel(right, from_x, late_b, first_b, left, from_core, right_out, left_out):
@@ -482,7 +487,7 @@
     moved = sum(x.size * x.dtype.itemsize for x in (*operands, *outs))
 
     def space(x):
-        return smem if x.dtype == jnp.int32 or x.shape == (1, 1) else vmem
+        return smem if x.ndim == 1 else vmem
 
     return pl.pallas_call(
         kernel,
@@ -508,7 +513,6 @@
     owned_tile = jnp.where(dpos // 2 == column_halves, 0, 2) + dpos % 2
     flags = jnp.stack([owned_tile, row_halves]).astype(jnp.int32)
     mask = jnp.broadcast_to(at_end.astype(jnp.float32), (8, quart))
-    mask, flags = lax.optimization_barrier((mask, flags))
 
     pairs = [(0, 1), (1, 0), (2, 3), (3, 2)]
     middle = [(1, 2), (2, 1)]
@@ -532,7 +536,7 @@
     quarter_bf16 = jax.ShapeDtypeStruct((rows, quart), jnp.bfloat16)
     extended = jax.ShapeDtypeStruct((rows + 16, quart), jnp.bfloat16)
     row_out = jax.ShapeDtypeStruct((8, quart), jnp.float32)
-    one_out = jax.ShapeDtypeStruct((1, 1), jnp.float32)
+    one_out = jax.ShapeDtypeStruct((8, 128), jnp.float32)
     across_shape = jax.ShapeDtypeStruct((quart, 128), jnp.float32)
     low = lambda n, m: pltpu.VMEM((n, m), jnp.bfloat16)
 
@@ -543,8 +547,8 @@
     inner_b = along(right_outputs, middle)
     first_a = along(left_outputs, pairs)
     other_b0 = x_swap(right_outputs)
-    other_a0 = core_swap(left_outputs)
-    left_behind, first_a = after(left_outputs, first_a)
+    other_a0, mask, flags = after(core_swap(left_outputs), mask, flags)
+    left_behind, first_a, other_a0 = after(left_outputs, first_a, other_a0)
     inner_a = along(left_behind, middle)
 
     outer_b = along(inner_b, outward)
@@ -558,11 +562,11 @@
     last_b = along(third_b, outward)
     second_b = picked(outer_b, inner_b)
     row_b = local_call(right_sums_kernel, (right_outputs, first_b, second_b), (row_out,))[0]
-    second_b, other_b1 = after(second_b, other_b1)
+    second_b, other_b1, other_a1 = after(second_b, other_b1, other_a1)
     other_b2 = x_swap(second_b)
     last_a = along(third_a, outward)
     second_a = picked(outer_a, inner_a)
-    second_a, other_a1, row_b = after(second_a, other_a1, row_b)
+    second_a, row_b = after(second_a, row_b)
     other_a2 = core_swap(second_a)
 
     (late_b,) = local_call(
@@ -645,9 +649,8 @@
         room=20,
     )
     from_core = core_swap(partial_left)
-    core_loss = jnp.reshape(core_swap(jnp.reshape(own_loss, ())), (1, 1))
+    core_loss = core_swap(own_loss)
     (loss,) = local_call(add_kernel, (loss, core_loss), (one_out,))
-    loss = jnp.reshape(loss, ())
     x_loss = x_swap(loss)
     right_gradient, left_gradient = local_call(
         final_kernel,
@@ -655,7 +658,11 @@
         (quarter_bf16, quarter_bf16),
     )
     right_gradient, x_loss = after(right_gradient, x_loss)
-    loss = jnp.reshape((loss + x_loss) / feats, (1,))
+    (loss,) = local_call(
+        functools.partial(loss_kernel, feats),
+        (loss, x_loss),
+        (jax.ShapeDtypeStruct((1,), jnp.float32),),
+    )
     return (left_gradient, right_gradient, mine[None, :, :], loss)
 
 

time: 99.4 us -> 95.5 us (0.961)
  waiting for transfers between devices: 45.4 us -> 49.1 us
  local copies, waits for them, and re-layouts: 3.78 us -> 1.05 us
  Pallas kernels: 20.5 us -> 18.2 us
  between operations: 3.29 us -> 1.03 us
    ppermute x14, waiting for transfers between devices: 4.46 us -> 7.81 us  [swapped(): return lax.ppermute(block, axis, route)]
    unnamed x14 -> x6, local copies, waits for them, and re-layouts: 3.78 us -> 1.05 us
    pallas_call x11 -> x12, Pallas kernels: 20.5 us -> 18.2 us  [local_call(): pl.pallas_call(kernel, out_shape=list(outs), in_specs=[space(x) for x in...]
  transfers between devices with their start and end apart: 24 -> 24, of which waited for: 11 -> 10; matrix products, arithmetic and copies ran while one was open for 0% -> 0% of each run, Pallas kernels for 19% -> 17%
where the time goes in v9:
time: 95.5 us; the launch traced here: 95.2 us
  waiting for transfers between devices  49.1 us (51%)
  starting transfers between devices  25.8 us (27%)
  Pallas kernels  18.2 us (19%)
  local copies, waits for them, and re-layouts  1.05 us (1%)
  between operations  1.03 us (1%)
    ppermute x10, waiting for transfers between devices, along(): return lax.ppermute(block, 'dp', route)  41.3 us
    pallas_call x12, Pallas kernels, local_call(): pl.pallas_call(kernel, out_shape=list(outs), in_specs=[space(x) for x in...  18.2 us
    ppermute x10, starting transfers between devices, along(): return lax.ppermute(block, 'dp', route)  14.9 us
    ppermute x14, starting transfers between devices, swapped(): return lax.ppermute(block, axis, route)  10.8 us
    ppermute x14, waiting for transfers between devices, swapped(): return lax.ppermute(block, axis, route)  7.81 us
  transfers between devices with their start and end apart: 24, of which 10 were waited for; matrix products, arithmetic and copies ran while one was open for 0% of the time, Pallas kernels for 17%

profile of v9, /device:TPU:0, one launch (start us, length us, event | category | flops | bytes accessed | tf_op | source)
XLA Modules:
  0.0 95.2 jit_solution(17831923182635209599)
XLA Ops:
  1.1 2.7 %collective-permute-start.1 = (bf16[512,512]{1,0:T(8,128)(2,1)}, bf16[512,512]{1,0:T(8,128)(2,1)S(1)}, u32[]{:S(2)}, u32[]{:S(2)}) collective-permute-start(bf16[512,512]{1,0:T(8,128)(2,1)} %refs_2_.1), channel_id=1, source_target_pairs={{0,4},{4,0},{8,12},{12,8},{1,5},{5,1},{9,13},{13,9},{2,6},{6,2},{1... | collective-permute-start | bytes 1572872 | tf_op jit(solution)/shard_map/ppermute | solution.py:522
  4.5 1.6 %collective-permute-start.7 = (bf16[512,512]{1,0:T(8,128)(2,1)}, bf16[512,512]{1,0:T(8,128)(2,1)S(1)}, u32[]{:S(2)}, u32[]{:S(2)}) collective-permute-start(bf16[512,512]{1,0:T(8,128)(2,1)} %first_b.1), channel_id=1, source_target_pairs={{0,2},{2,0},{1,3},{3,1},{4,6},{6,4},{5,7},{7,5},{8,10},{10,8},{9,1... | collective-permute-start | bytes 1572872 | tf_op jit(solution)/shard_map/ppermute | solution.py:19
  6.0 4.4 %collective-permute-start.6 = (bf16[512,512]{1,0:T(8,128)(2,1)}, bf16[512,512]{1,0:T(8,128)(2,1)S(1)}, u32[]{:S(2)}, u32[]{:S(2)}) collective-permute-start(bf16[512,512]{1,0:T(8,128)(2,1)} %first_b.1), channel_id=1, source_target_pairs={{0,4},{4,0},{8,12},{12,8},{1,5},{5,1},{9,13},{13,9},{2,6},{6,2},{1... | collective-permute-start | bytes 1572872 | tf_op jit(solution)/shard_map/ppermute | solution.py:522
  10.5 6.3 %collective-permute-done.1.refs_2_ = bf16[512,512]{1,0:T(8,128)(2,1)S(1)} collective-permute-done((bf16[512,512]{1,0:T(8,128)(2,1)}, bf16[512,512]{1,0:T(8,128)(2,1)S(1)}, u32[]{:S(2)}, u32[]{:S(2)}) %collective-permute-start.1) | collective-permute-done | bytes 524320 | tf_op jit(solution)/shard_map/ppermute | solution.py:522
  16.8 0.7 collective-permute-start.10
  17.5 1.3 %collective-permute-start.5 = (bf16[512,512]{1,0:T(8,128)(2,1)S(1)}, bf16[512,512]{1,0:T(8,128)(2,1)S(1)}, u32[]{:S(2)}, u32[]{:S(2)}) collective-permute-start(bf16[512,512]{1,0:T(8,128)(2,1)S(1)} %collective-permute-done.4.inner), channel_id=1, source_target_pairs={{4,0},{8,12},{5,1},{9,13},{6,2},{10,14},{7,3},{11,15},{20,16},{24,... | collective-permute-start | bytes 1572872 | tf_op jit(solution)/shard_map/ppermute | solution.py:522
  18.9 9.1 %collective-permute-done.6.second.refs_8_ = bf16[512,512]{1,0:T(8,128)(2,1)S(1)} collective-permute-done((bf16[512,512]{1,0:T(8,128)(2,1)}, bf16[512,512]{1,0:T(8,128)(2,1)S(1)}, u32[]{:S(2)}, u32[]{:S(2)}) %collective-permute-start.6) | collective-permute-done | bytes 524320 | tf_op jit(solution)/shard_map/ppermute | solution.py:522
  28.0 1.9 %collective-permute-start.8 = (bf16[512,512]{1,0:T(8,128)(2,1)S(1)}, bf16[512,512]{1,0:T(8,128)(2,1)S(1)}, u32[]{:S(2)}, u32[]{:S(2)}) collective-permute-start(bf16[512,512]{1,0:T(8,128)(2,1)S(1)} %collective-permute-done.6.second.refs_8_), channel_id=1, source_target_pairs={{0,2},{2,0},{1,3},{3,1},{4,6},{6,4},{5,7},{7,5},{8,10},{10,8},{9,1... | collective-permute-start | bytes 1572872 | tf_op jit(solution)/shard_map/ppermute | solution.py:19
  29.9 0.7 collective-permute-start.16
  30.6 1.3 %collective-permute-start.11 = (bf16[512,512]{1,0:T(8,128)(2,1)S(1)}, bf16[512,512]{1,0:T(8,128)(2,1)S(1)}, u32[]{:S(2)}, u32[]{:S(2)}) collective-permute-start(bf16[512,512]{1,0:T(8,128)(2,1)S(1)} %collective-permute-done.10.inner), channel_id=1, source_target_pairs={{4,0},{8,12},{5,1},{9,13},{6,2},{10,14},{7,3},{11,15},{20,16},{24,... | collective-permute-start | bytes 1572872 | tf_op jit(solution)/shard_map/ppermute | solution.py:522
  31.9 7.4 %collective-permute-done.5.outer = bf16[512,512]{1,0:T(8,128)(2,1)S(1)} collective-permute-done((bf16[512,512]{1,0:T(8,128)(2,1)S(1)}, bf16[512,512]{1,0:T(8,128)(2,1)S(1)}, u32[]{:S(2)}, u32[]{:S(2)}) %collective-permute-start.5) | collective-permute-done | bytes 524320 | tf_op jit(solution)/shard_map/ppermute | solution.py:522
  39.3 0.7 collective-permute-start.2
  40.1 1.3 %collective-permute-done.8.refs_9_ = bf16[512,512]{1,0:T(8,128)(2,1)S(1)} collective-permute-done((bf16[512,512]{1,0:T(8,128)(2,1)S(1)}, bf16[512,512]{1,0:T(8,128)(2,1)S(1)}, u32[]{:S(2)}, u32[]{:S(2)}) %collective-permute-start.8) | collective-permute-done | bytes 524320 | tf_op jit(solution)/shard_map/ppermute | solution.py:19
  41.4 1.5 %collective-permute-start.13 = (bf16[512,512]{1,0:T(8,128)(2,1)S(1)}, bf16[512,512]{1,0:T(8,128)(2,1)S(1)}, u32[]{:S(2)}, u32[]{:S(2)}) collective-permute-start(bf16[512,512]{1,0:T(8,128)(2,1)S(1)} %shard_map.57.third.refs_10_), channel_id=1, source_target_pairs={{0,2},{2,0},{1,3},{3,1},{4,6},{6,4},{5,7},{7,5},{8,10},{10,8},{9,1... | collective-permute-start | bytes 1572872 | tf_op jit(solution)/shard_map/ppermute | solution.py:19
  42.9 1.3 %collective-permute-start.17 = (bf16[512,512]{1,0:T(8,128)(2,1)S(1)}, bf16[512,512]{1,0:T(8,128)(2,1)S(1)}, u32[]{:S(2)}, u32[]{:S(2)}) collective-permute-start(bf16[512,512]{1,0:T(8,128)(2,1)S(1)} %collective-permute-done.16.inner), channel_id=1, source_target_pairs={{4,0},{8,12},{5,1},{9,13},{6,2},{10,14},{7,3},{11,15},{20,16},{24,... | collective-permute-start | bytes 1572872 | tf_op jit(solution)/shard_map/ppermute | solution.py:522
  44.2 1.0 %copy-done = bf16[512,512]{1,0:T(8,128)(2,1)S(1)} copy-done((bf16[512,512]{1,0:T(8,128)(2,1)S(1)}, bf16[512,512]{1,0:T(8,128)(2,1)}, u32[]{:S(2)}) %copy-start) | copy-done | bytes 524312
  45.3 1.0 %shard_map.59.row = f32[8,512]{1,0:T(8,128)S(1)} custom-call(bf16[512,512]{1,0:T(8,128)(2,1)S(1)} %copy-done, bf16[512,512]{1,0:T(8,128)(2,1)S(1)} %collective-permute-done.6.second.refs_8_, bf16[512,512]{1,0:T(8,128)(2,1)S(1)} %shard_map.57.third.refs_10_), custom_call_target="tpu_custom_call" | custom-call | flops 1048576 | bytes 1589248 | tf_op jit(solution)/shard_map/pallas_call | solution.py:492
  46.3 4.2 %collective-permute-done.11.outer = bf16[512,512]{1,0:T(8,128)(2,1)S(1)} collective-permute-done((bf16[512,512]{1,0:T(8,128)(2,1)S(1)}, bf16[512,512]{1,0:T(8,128)(2,1)S(1)}, u32[]{:S(2)}, u32[]{:S(2)}) %collective-permute-start.11) | collective-permute-done | bytes 524320 | tf_op jit(solution)/shard_map/ppermute | solution.py:522
  50.7 1.3 %collective-permute-start.3 = (bf16[512,512]{1,0:T(8,128)(2,1)S(1)}, bf16[512,512]{1,0:T(8,128)(2,1)S(1)}, u32[]{:S(2)}, u32[]{:S(2)}) collective-permute-start(bf16[512,512]{1,0:T(8,128)(2,1)S(1)} %collective-permute-done.2.inner), channel_id=1, source_target_pairs={{4,0},{8,12},{5,1},{9,13},{6,2},{10,14},{7,3},{11,15},{20,16},{24,... | collective-permute-start | bytes 1572872 | tf_op jit(solution)/shard_map/ppermute | solution.py:522
  52.0 9.8 %collective-permute-done.17.outer = bf16[512,512]{1,0:T(8,128)(2,1)S(1)} collective-permute-done((bf16[512,512]{1,0:T(8,128)(2,1)S(1)}, bf16[512,512]{1,0:T(8,128)(2,1)S(1)}, u32[]{:S(2)}, u32[]{:S(2)}) %collective-permute-start.17) | collective-permute-done | bytes 524320 | tf_op jit(solution)/shard_map/ppermute | solution.py:522
  62.3 1.8 %collective-permute-start.18 = (bf16[528,512]{1,0:T(8,128)(2,1)S(1)}, bf16[528,512]{1,0:T(8,128)(2,1)S(1)}, u32[]{:S(2)}, u32[]{:S(2)}) collective-permute-start(bf16[528,512]{1,0:T(8,128)(2,1)S(1)} %shard_map.62.refs_7_.late_b), channel_id=1, source_target_pairs={{0,2},{2,0},{1,3},{3,1},{4,6},{6,4},{5,7},{7,5},{8,10},{10,8},{9,1... | collective-permute-start | bytes 1622024 | tf_op jit(solution)/shard_map/ppermute | solution.py:19
  64.1 4.1 %shard_map.60 = (f32[512,512]{1,0:T(8,128)S(1)}, f32[512,512]{1,0:T(8,128)S(1)}, f32[512,1024]{1,0:T(8,128)S(1)}, f32[8,512]{1,0:T(8,128)S(1)}, bf16[512,512]{1,...) custom-call(bf16[512,512]{1,0:T(8,128)(2,1)S(1)} %copy-done.2, bf16[512,512]{1,0:T(8,128)(2,1)S(1)} %collective-permute-done.refs_1_.refs_3_, ...), custom_call_target="tpu_custom_call" | custom-call | flops 3221225472 | bytes 11550720 | tf_op jit(solution)/shard_map/pallas_call | solution.py:492
  68.3 4.4 %collective-permute-done.3.outer = bf16[512,512]{1,0:T(8,128)(2,1)S(1)} collective-permute-done((bf16[512,512]{1,0:T(8,128)(2,1)S(1)}, bf16[512,512]{1,0:T(8,128)(2,1)S(1)}, u32[]{:S(2)}, u32[]{:S(2)}) %collective-permute-start.3) | collective-permute-done | bytes 524320 | tf_op jit(solution)/shard_map/ppermute | solution.py:522
  73.2 2.7 %collective-permute-done.18.late_b.refs_8_ = bf16[528,512]{1,0:T(8,128)(2,1)S(1)} collective-permute-done((bf16[528,512]{1,0:T(8,128)(2,1)S(1)}, bf16[528,512]{1,0:T(8,128)(2,1)S(1)}, u32[]{:S(2)}, u32[]{:S(2)}) %collective-permute-start.18) | collective-permute-done | bytes 540704 | tf_op jit(solution)/shard_map/ppermute | solution.py:19
  75.9 1.1 %shard_map.63 = (f32[528,512]{1,0:T(8,128)S(1)}, f32[512,128]{1,0:T(8,128)S(1)}, bf16[512,512]{1,0:T(8,128)(2,1)S(1)}, f32[8,512]{1,0:T(8,128)S(1)}) custom-call(bf16[528,512]{1,0:T(8,128)(2,1)S(1)} %shard_map.61.late.refs_0_, bf16[512,512]{1,0:T(8,128)(2,1)S(1)} %get-tuple-element.53.zero.refs_4_, f32[512,512]{1,0:T(8,128)S(1)} %get-tuple-element.57.sums.refs_13_, ...), custom_call_target="tpu_custom_call" | custom-call | flops 536870912 | bytes 4538368 | tf_op jit(solution)/shard_map/pallas_call | solution.py:492
  77.0 1.3 %shard_map.64 = (bf16[528,512]{1,0:T(8,128)(2,1)S(1)}, bf16[512,512]{1,0:T(8,128)(2,1)S(1)}, f32[8,512]{1,0:T(8,128)S(1)}) custom-call(bf16[528,512]{1,0:T(8,128)(2,1)S(1)} %collective-permute-done.15.late.refs_1_, bf16[512,512]{1,0:T(8,128)(2,1)S(1)} %get-tuple-element.54.zero.refs_5_, f32[512,512]{1,0:T(8,128)S(1)} %get-tuple-element.59.sums.refs_14_, ...), custom_call_target="tpu_custom_call" | custom-call | flops 536870912 | bytes 5095424 | tf_op jit(solution)/shard_map/pallas_call | solution.py:492
  78.4 1.7 %collective-permute-start.20 = (bf16[528,512]{1,0:T(8,128)(2,1)S(1)}, bf16[528,512]{1,0:T(8,128)(2,1)S(1)}, u32[]{:S(2)}, u32[]{:S(2)}) collective-permute-start(bf16[528,512]{1,0:T(8,128)(2,1)S(1)} %get-tuple-element.66), channel_id=1, source_target_pairs={{0,2},{2,0},{1,3},{3,1},{4,6},{6,4},{5,7},{7,5},{8,10},{10,8},{9,1... | collective-permute-start | bytes 1622024 | tf_op jit(solution)/shard_map/ppermute | solution.py:19
  80.0 7.7 %shard_map.65 = (f32[512,512]{1,0:T(8,128)S(1)}, f32[512,512]{1,0:T(8,128)S(1)}, bf16[512,512]{1,0:T(8,128)(2,1)S(1)}, f32[256,1024]{1,0:T(8,128)}, f32[8,128]{1,0:T(8,128)S(1)}, /*index=5*/f32[8,128]{1,0:T(8,128)S(1)}) custom-call(s32[2]{0:T(128)S(1)} %pad_add_fusion.flags, bf16[528,512]{1,0:T(8,128)(2,1)S(1)} %shard_map.61.late.refs_0_, ...), custom_call_target="tpu_custom_call" | custom-call | flops 2147483648 | bytes 14278664 | tf_op jit(solution)/shard_map/pallas_call | solution.py:492
  88.2 1.4 %collective-permute-done.22.other = f32[8,128]{1,0:T(8,128)S(1)} collective-permute-done((f32[8,128]{1,0:T(8,128)S(1)}, f32[8,128]{1,0:T(8,128)S(1)}, u32[]{:S(2)}, u32[]{:S(2)}) %collective-permute-start.22) | collective-permute-done | bytes 4128 | tf_op jit(solution)/shard_map/ppermute | solution.py:19
  89.6 1.1 %collective-permute-start.23 = (f32[8,128]{1,0:T(8,128)S(1)}, f32[8,128]{1,0:T(8,128)S(1)}, u32[]{:S(2)}, u32[]{:S(2)}) collective-permute-start(f32[8,128]{1,0:T(8,128)S(1)} %shard_map.67.one), channel_id=1, source_target_pairs={{0,2},{2,0},{1,3},{3,1},{4,6},{6,4},{5,7},{7,5},{8,10},{10,8},{9,1... | collective-permute-start | bytes 12296 | tf_op jit(solution)/shard_map/ppermute | solution.py:19
  90.7 2.4 %collective-permute-done.20.from_x = bf16[528,512]{1,0:T(8,128)(2,1)S(1)} collective-permute-done((bf16[528,512]{1,0:T(8,128)(2,1)S(1)}, bf16[528,512]{1,0:T(8,128)(2,1)S(1)}, u32[]{:S(2)}, u32[]{:S(2)}) %collective-permute-start.20) | collective-permute-done | bytes 540704 | tf_op jit(solution)/shard_map/ppermute | solution.py:19
  93.1 1.4 %shard_map.66 = (bf16[512,512]{1,0:T(8,128)(2,1)}, bf16[512,512]{1,0:T(8,128)(2,1)}) custom-call(f32[512,512]{1,0:T(8,128)S(1)} %get-tuple-element.65.right, bf16[528,512]{1,0:T(8,128)(2,1)S(1)} %collective-permute-done.20.from_x, bf16[528,512]{1,0:T(8,128)(2,1)S(1)} %shard_map.62.refs_7_.late_b, bf16[512,512]{1,0:T(8,128)(2,1)S(1)} %copy-done.1, ...), custom_call_target="tpu_custom_call" | custom-call | flops 1048576 | bytes 5275648 | tf_op jit(solution)/shard_map/pallas_call | solution.py:492
  (36 shorter events, 3.8 us)
Async XLA Ops:
  0.6 9.9 %collective-permute-start = (bf16[512,512]{1,0:T(8,128)(2,1)}, bf16[512,512]{1,0:T(8,128)(2,1)S(1)}, u32[]{:S(2)}, u32[]{:S(2)}) collective-permute-start(bf16[512,512]{1,0:T(8,128)(2,1)} %refs_2_.1), channel_id=1, source_target_pairs={{0,1},{1,0},{2,3},{3,2},{4,5},{5,4},{6,7},{7,6},{8,9},{9,8},{10,11... | collective-permute-start | bytes 1572872 | tf_op jit(solution)/shard_map/ppermute | solution.py:19
  1.1 15.6 %collective-permute-start.1 = (bf16[512,512]{1,0:T(8,128)(2,1)}, bf16[512,512]{1,0:T(8,128)(2,1)S(1)}, u32[]{:S(2)}, u32[]{:S(2)}) collective-permute-start(bf16[512,512]{1,0:T(8,128)(2,1)} %refs_2_.1), channel_id=1, source_target_pairs={{0,4},{4,0},{8,12},{12,8},{1,5},{5,1},{9,13},{13,9},{2,6},{6,2},{1... | collective-permute-start | bytes 1572872 | tf_op jit(solution)/shard_map/ppermute | solution.py:522
  3.8 13.7 %collective-permute-start.4 = (bf16[512,512]{1,0:T(8,128)(2,1)}, bf16[512,512]{1,0:T(8,128)(2,1)S(1)}, u32[]{:S(2)}, u32[]{:S(2)}) collective-permute-start(bf16[512,512]{1,0:T(8,128)(2,1)} %first_b.1), channel_id=1, source_target_pairs={{4,8},{8,4},{5,9},{9,5},{6,10},{10,6},{7,11},{11,7},{20,24},{24,20... | collective-permute-start | bytes 1572872 | tf_op jit(solution)/shard_map/ppermute | solution.py:522
  4.5 14.4 %collective-permute-start.7 = (bf16[512,512]{1,0:T(8,128)(2,1)}, bf16[512,512]{1,0:T(8,128)(2,1)S(1)}, u32[]{:S(2)}, u32[]{:S(2)}) collective-permute-start(bf16[512,512]{1,0:T(8,128)(2,1)} %first_b.1), channel_id=1, source_target_pairs={{0,2},{2,0},{1,3},{3,1},{4,6},{6,4},{5,7},{7,5},{8,10},{10,8},{9,1... | collective-permute-start | bytes 1572872 | tf_op jit(solution)/shard_map/ppermute | solution.py:19
  6.0 22.0 %collective-permute-start.6 = (bf16[512,512]{1,0:T(8,128)(2,1)}, bf16[512,512]{1,0:T(8,128)(2,1)S(1)}, u32[]{:S(2)}, u32[]{:S(2)}) collective-permute-start(bf16[512,512]{1,0:T(8,128)(2,1)} %first_b.1), channel_id=1, source_target_pairs={{0,4},{4,0},{8,12},{12,8},{1,5},{5,1},{9,13},{13,9},{2,6},{6,2},{1... | collective-permute-start | bytes 1572872 | tf_op jit(solution)/shard_map/ppermute | solution.py:522
  16.8 13.8 %collective-permute-start.10 = (bf16[512,512]{1,0:T(8,128)(2,1)}, bf16[512,512]{1,0:T(8,128)(2,1)S(1)}, u32[]{:S(2)}, u32[]{:S(2)}) collective-permute-start(bf16[512,512]{1,0:T(8,128)(2,1)} %refs_2_.1), channel_id=1, source_target_pairs={{4,8},{8,4},{5,9},{9,5},{6,10},{10,6},{7,11},{11,7},{20,24},{24,20... | collective-permute-start | bytes 1572872 | tf_op jit(solution)/shard_map/ppermute | solution.py:522
  17.5 21.8 %collective-permute-start.5 = (bf16[512,512]{1,0:T(8,128)(2,1)S(1)}, bf16[512,512]{1,0:T(8,128)(2,1)S(1)}, u32[]{:S(2)}, u32[]{:S(2)}) collective-permute-start(bf16[512,512]{1,0:T(8,128)(2,1)S(1)} %collective-permute-done.4.inner), channel_id=1, source_target_pairs={{4,0},{8,12},{5,1},{9,13},{6,2},{10,14},{7,3},{11,15},{20,16},{24,... | collective-permute-start | bytes 1572872 | tf_op jit(solution)/shard_map/ppermute | solution.py:522
  18.8 21.3 %collective-permute-start.9 = (bf16[512,512]{1,0:T(8,128)(2,1)S(1)}, bf16[512,512]{1,0:T(8,128)(2,1)S(1)}, u32[]{:S(2)}, u32[]{:S(2)}) collective-permute-start(bf16[512,512]{1,0:T(8,128)(2,1)S(1)} %collective-permute-done.1.refs_2_), channel_id=1, source_target_pairs={{0,1},{1,0},{2,3},{3,2},{4,5},{5,4},{6,7},{7,6},{8,9},{9,8},{10,11... | collective-permute-start | bytes 1572872 | tf_op jit(solution)/shard_map/ppermute | solution.py:19
  28.0 13.4 %collective-permute-start.8 = (bf16[512,512]{1,0:T(8,128)(2,1)S(1)}, bf16[512,512]{1,0:T(8,128)(2,1)S(1)}, u32[]{:S(2)}, u32[]{:S(2)}) collective-permute-start(bf16[512,512]{1,0:T(8,128)(2,1)S(1)} %collective-permute-done.6.second.refs_8_), channel_id=1, source_target_pairs={{0,2},{2,0},{1,3},{3,1},{4,6},{6,4},{5,7},{7,5},{8,10},{10,8},{9,1... | collective-permute-start | bytes 1572872 | tf_op jit(solution)/shard_map/ppermute | solution.py:19
  29.9 13.0 %collective-permute-start.16 = (bf16[512,512]{1,0:T(8,128)(2,1)S(1)}, bf16[512,512]{1,0:T(8,128)(2,1)S(1)}, u32[]{:S(2)}, u32[]{:S(2)}) collective-permute-start(bf16[512,512]{1,0:T(8,128)(2,1)S(1)} %collective-permute-done.6.second.refs_8_), channel_id=1, source_target_pairs={{4,8},{8,4},{5,9},{9,5},{6,10},{10,6},{7,11},{11,7},{20,24},{24,20... | collective-permute-start | bytes 1572872 | tf_op jit(solution)/shard_map/ppermute | solution.py:522
  30.6 19.9 %collective-permute-start.11 = (bf16[512,512]{1,0:T(8,128)(2,1)S(1)}, bf16[512,512]{1,0:T(8,128)(2,1)S(1)}, u32[]{:S(2)}, u32[]{:S(2)}) collective-permute-start(bf16[512,512]{1,0:T(8,128)(2,1)S(1)} %collective-permute-done.10.inner), channel_id=1, source_target_pairs={{4,0},{8,12},{5,1},{9,13},{6,2},{10,14},{7,3},{11,15},{20,16},{24,... | collective-permute-start | bytes 1572872 | tf_op jit(solution)/shard_map/ppermute | solution.py:522
  39.3 11.4 %collective-permute-start.2 = (bf16[512,512]{1,0:T(8,128)(2,1)S(1)}, bf16[512,512]{1,0:T(8,128)(2,1)S(1)}, u32[]{:S(2)}, u32[]{:S(2)}) collective-permute-start(bf16[512,512]{1,0:T(8,128)(2,1)S(1)} %collective-permute-done.1.refs_2_), channel_id=1, source_target_pairs={{4,8},{8,4},{5,9},{9,5},{6,10},{10,6},{7,11},{11,7},{20,24},{24,20... | collective-permute-start | bytes 1572872 | tf_op jit(solution)/shard_map/ppermute | solution.py:522
  39.9 24.1 %copy-start.1 = (bf16[512,512]{1,0:T(8,128)(2,1)S(1)}, bf16[512,512]{1,0:T(8,128)(2,1)}, u32[]{:S(2)}) copy-start(bf16[512,512]{1,0:T(8,128)(2,1)} %first_b.1) | copy-start | bytes 1572868
  40.0 24.1 %copy-start.2 = (bf16[512,512]{1,0:T(8,128)(2,1)S(1)}, bf16[512,512]{1,0:T(8,128)(2,1)}, u32[]{:S(2)}) copy-start(bf16[512,512]{1,0:T(8,128)(2,1)} %refs_2_.1) | copy-start | bytes 1572868
  41.4 22.6 %collective-permute-start.13 = (bf16[512,512]{1,0:T(8,128)(2,1)S(1)}, bf16[512,512]{1,0:T(8,128)(2,1)S(1)}, u32[]{:S(2)}, u32[]{:S(2)}) collective-permute-start(bf16[512,512]{1,0:T(8,128)(2,1)S(1)} %shard_map.57.third.refs_10_), channel_id=1, source_target_pairs={{0,2},{2,0},{1,3},{3,1},{4,6},{6,4},{5,7},{7,5},{8,10},{10,8},{9,1... | collective-permute-start | bytes 1572872 | tf_op jit(solution)/shard_map/ppermute | solution.py:19
  42.9 18.9 %collective-permute-start.17 = (bf16[512,512]{1,0:T(8,128)(2,1)S(1)}, bf16[512,512]{1,0:T(8,128)(2,1)S(1)}, u32[]{:S(2)}, u32[]{:S(2)}) collective-permute-start(bf16[512,512]{1,0:T(8,128)(2,1)S(1)} %collective-permute-done.16.inner), channel_id=1, source_target_pairs={{4,0},{8,12},{5,1},{9,13},{6,2},{10,14},{7,3},{11,15},{20,16},{24,... | collective-permute-start | bytes 1572872 | tf_op jit(solution)/shard_map/ppermute | solution.py:522
  44.2 1.0 %copy-start = (bf16[512,512]{1,0:T(8,128)(2,1)S(1)}, bf16[512,512]{1,0:T(8,128)(2,1)}, u32[]{:S(2)}) copy-start(bf16[512,512]{1,0:T(8,128)(2,1)} %first_b.1) | copy-start | bytes 1572868
  50.6 13.5 %collective-permute-start.12 = (bf16[512,512]{1,0:T(8,128)(2,1)S(1)}, bf16[512,512]{1,0:T(8,128)(2,1)S(1)}, u32[]{:S(2)}, u32[]{:S(2)}) collective-permute-start(bf16[512,512]{1,0:T(8,128)(2,1)S(1)} %shard_map.58.refs_4_), channel_id=1, source_target_pairs={{0,1},{1,0},{2,3},{3,2},{4,5},{5,4},{6,7},{7,6},{8,9},{9,8},{10,11... | collective-permute-start | bytes 1572872 | tf_op jit(solution)/shard_map/ppermute | solution.py:19
  50.7 22.0 %collective-permute-start.3 = (bf16[512,512]{1,0:T(8,128)(2,1)S(1)}, bf16[512,512]{1,0:T(8,128)(2,1)S(1)}, u32[]{:S(2)}, u32[]{:S(2)}) collective-permute-start(bf16[512,512]{1,0:T(8,128)(2,1)S(1)} %collective-permute-done.2.inner), channel_id=1, source_target_pairs={{4,0},{8,12},{5,1},{9,13},{6,2},{10,14},{7,3},{11,15},{20,16},{24,... | collective-permute-start | bytes 1572872 | tf_op jit(solution)/shard_map/ppermute | solution.py:522
  62.3 13.6 %collective-permute-start.18 = (bf16[528,512]{1,0:T(8,128)(2,1)S(1)}, bf16[528,512]{1,0:T(8,128)(2,1)S(1)}, u32[]{:S(2)}, u32[]{:S(2)}) collective-permute-start(bf16[528,512]{1,0:T(8,128)(2,1)S(1)} %shard_map.62.refs_7_.late_b), channel_id=1, source_target_pairs={{0,2},{2,0},{1,3},{3,1},{4,6},{6,4},{5,7},{7,5},{8,10},{10,8},{9,1... | collective-permute-start | bytes 1622024 | tf_op jit(solution)/shard_map/ppermute | solution.py:19
  68.2 4.5 %collective-permute-start.14 = (f32[8,512]{1,0:T(8,128)S(1)}, f32[8,512]{1,0:T(8,128)S(1)}, u32[]{:S(2)}, u32[]{:S(2)}) collective-permute-start(f32[8,512]{1,0:T(8,128)S(1)} %get-tuple-element.52), channel_id=1, source_target_pairs={{0,1},{1,0},{2,3},{3,2},{4,5},{5,4},{6,7},{7,6},{8,9},{9,8},{10,11... | collective-permute-start | bytes 49160 | tf_op jit(solution)/shard_map/ppermute | solution.py:19
  73.1 3.9 %collective-permute-start.15 = (bf16[528,512]{1,0:T(8,128)(2,1)S(1)}, bf16[528,512]{1,0:T(8,128)(2,1)S(1)}, u32[]{:S(2)}, u32[]{:S(2)}) collective-permute-start(bf16[528,512]{1,0:T(8,128)(2,1)S(1)} %shard_map.61.late.refs_0_), channel_id=1, source_target_pairs={{0,1},{1,0},{2,3},{3,2},{4,5},{5,4},{6,7},{7,6},{8,9},{9,8},{10,11... | collective-permute-start | bytes 1622024 | tf_op jit(solution)/shard_map/ppermute | solution.py:19
  78.3 1.8 %collective-permute-start.19 = (f32[8,512]{1,0:T(8,128)S(1)}, f32[8,512]{1,0:T(8,128)S(1)}, u32[]{:S(2)}, u32[]{:S(2)}) collective-permute-start(f32[8,512]{1,0:T(8,128)S(1)} %get-tuple-element.64.refs_16_), channel_id=1, source_target_pairs={{0,1},{1,0},{2,3},{3,2},{4,5},{5,4},{6,7},{7,6},{8,9},{9,8},{10,11... | collective-permute-start | bytes 49160 | tf_op jit(solution)/shard_map/ppermute | solution.py:19
  78.4 14.7 %collective-permute-start.20 = (bf16[528,512]{1,0:T(8,128)(2,1)S(1)}, bf16[528,512]{1,0:T(8,128)(2,1)S(1)}, u32[]{:S(2)}, u32[]{:S(2)}) collective-permute-start(bf16[528,512]{1,0:T(8,128)(2,1)S(1)} %get-tuple-element.66), channel_id=1, source_target_pairs={{0,2},{2,0},{1,3},{3,1},{4,6},{6,4},{5,7},{7,5},{8,10},{10,8},{9,1... | collective-permute-start | bytes 1622024 | tf_op jit(solution)/shard_map/ppermute | solution.py:19
  87.7 3.0 %collective-permute-start.21 = (bf16[512,512]{1,0:T(8,128)(2,1)S(1)}, bf16[512,512]{1,0:T(8,128)(2,1)S(1)}, u32[]{:S(2)}, u32[]{:S(2)}) collective-permute-start(bf16[512,512]{1,0:T(8,128)(2,1)S(1)} %get-tuple-element.68), channel_id=1, source_target_pairs={{0,1},{1,0},{2,3},{3,2},{4,5},{5,4},{6,7},{7,6},{8,9},{9,8},{10,11... | collective-permute-start | bytes 1572872 | tf_op jit(solution)/shard_map/ppermute | solution.py:19
  87.8 1.8 %collective-permute-start.22 = (f32[8,128]{1,0:T(8,128)S(1)}, f32[8,128]{1,0:T(8,128)S(1)}, u32[]{:S(2)}, u32[]{:S(2)}) collective-permute-start(f32[8,128]{1,0:T(8,128)S(1)} %get-tuple-element.72), channel_id=1, source_target_pairs={{0,1},{1,0},{2,3},{3,2},{4,5},{5,4},{6,7},{7,6},{8,9},{9,8},{10,11... | collective-permute-start | bytes 12296 | tf_op jit(solution)/shard_map/ppermute | solution.py:19
  89.6 4.9 %collective-permute-start.23 = (f32[8,128]{1,0:T(8,128)S(1)}, f32[8,128]{1,0:T(8,128)S(1)}, u32[]{:S(2)}, u32[]{:S(2)}) collective-permute-start(f32[8,128]{1,0:T(8,128)S(1)} %shard_map.67.one), channel_id=1, source_target_pairs={{0,2},{2,0},{1,3},{3,1},{4,6},{6,4},{5,7},{7,5},{8,10},{10,8},{9,1... | collective-permute-start | bytes 12296 | tf_op jit(solution)/shard_map/ppermute | solution.py:19

commit v10 on v9

--- a/solution.py
+++ b/solution.py
@@ -250,8 +250,7 @@
 
 def products_kernel(*refs):
     lefts, rights = refs[0:6], refs[6:12]
-    partner_own, partner_other, own_all, row_other, zero_own, zero_other = refs[12:18]
-    low_left, low_right = refs[18:]
+    partner_all, own_all, row_other, zero_own, zero_other, low_left, low_right = refs[12:]
     rows, quart = lefts[0].shape
     width = quart // 2
     for half in range(2):
@@ -280,9 +279,7 @@
                 low_right[lanes, block * rows + at : block * rows + at + 128] = jnp.transpose(low)
     for tile in range(4):
         wide = slice(tile * width, (tile + 1) * width)
-        inner = slice((tile % 2) * width, (tile % 2 + 1) * width)
-        target = partner_own if tile < 2 else partner_other
-        target[:, inner] = dot(low_right[quart:, :], low_left[:, wide])
+        partner_all[:, wide] = dot(low_right[quart:, :], low_left[:, wide])
         own_all[:, wide] = dot(low_right[:quart, :], low_left[:, wide])
 
 
@@ -307,51 +304,39 @@
     return columns[:, 0:1], columns[:, 1:2]
 
 
-def partner_kernel(images, part, late, zero, sums, late_b, *refs):
-    if part:
-        (terms_in, across_in, vec_in, partial_out, e_out, vec_out, left) = refs
-    else:
-        (terms_out, across_out, e_out, vec_out, left) = refs
-    rows, quart = zero.shape
+def partner_kernel(images, late_own, late_other, zero_own, zero_other, sums, late_b, *refs):
+    partial_out, e_out, vec_out, left = refs
+    rows, quart = zero_own.shape
     width = quart // 2
-    _, rstd, _, delta = joined_rows(late, rows)
-    left_operand(zero, late, left, slice(0, quart))
     scale_col, delta_col = scale_columns(late_b, images)
-    across = across_in[...] if part else jnp.zeros((quart, 128), jnp.float32)
-    down = []
-    for tile in range(2):
-        at = slice(tile * width, (tile + 1) * width)
-        total = sums[:, at] + dot(late_b[:quart, :], late[:rows, at])
-        corr = (total * scale_col - delta_col * delta[:, at]) * rstd[:, at]
-        e_out[:, at] = (corr * (off_weight * rstd[:, at])).astype(jnp.bfloat16)
-        square = corr * corr
-        across = across + fold_lanes(square)
-        down.append(jnp.sum(square, axis=0, keepdims=True))
-    second_a = off_weight * jnp.concatenate(down, axis=1)
-    if part:
-        vec_out[...] = rows_of([second_a, second_a + vec_in[0:1, :]])
-        nothing = jnp.zeros((1, quart), jnp.float32)
-        second = off_weight * lanes_to_row(across)
-        partial_out[rows:, :] = split_rows([second, nothing, nothing, nothing])
-    else:
-        vec_out[...] = rows_of([second_a])
-        across_out[...] = across
+    across = jnp.zeros((quart, 128), jnp.float32)
+    for part, late in enumerate((late_own, late_other)):
+        zero = (zero_own, zero_other)[part]
+        left_operand(zero, late, left, slice(part * quart, (part + 1) * quart))
+        _, rstd, _, delta = joined_rows(late, rows)
+        for tile in range(2):
+            at = slice(tile * width, (tile + 1) * width)
+            wide = slice(part * quart + tile * width, part * quart + (tile + 1) * width)
+            total = sums[:, wide] + dot(late_b[:quart, :], late[:rows, at])
+            corr = (total * scale_col - delta_col * delta[:, at]) * rstd[:, at]
+            e_out[:, wide] = (corr * (off_weight * rstd[:, at])).astype(jnp.bfloat16)
+            square = corr * corr
+            across = across + fold_lanes(square)
+            vec_out[:, wide] = rows_of([off_weight * jnp.sum(square, axis=0, keepdims=True)])
+    nothing = jnp.zeros((1, quart), jnp.float32)
+    second = off_weight * lanes_to_row(across)
+    partial_out[rows:, :] = split_rows([second, nothing, nothing, nothing])
     for tile in range(2):
         at = slice(tile * width, (tile + 1) * width)
         terms = dot_rows(left[...], e_out[at, :])
-        if part:
-            partial_out[:rows, at] = without_extra(terms + terms_in[:, at], rows).astype(
-                jnp.bfloat16
-            )
-        else:
-            terms_out[:, at] = terms
+        partial_out[:rows, at] = without_extra(terms, rows).astype(jnp.bfloat16)
 
 
 def own_kernel(images, flags, *refs):
     (late_own, late_other, first_own, first_other, zero_own, zero_other, sums, late_b) = refs[:8]
-    (late_b_other, first_b, first_b_other, e_left, e_right, partner_own, partner_other) = refs[8:15]
-    (vec_own, vec_other, vec_core, right_out, left_out, left_partial_out, mine_out) = refs[15:22]
-    (own_loss_out, loss_out, left, norm_b, e_own, mine_own, mine_partner) = refs[22:]
+    (late_b_other, first_b, first_b_other, e_partner, partner_sums) = refs[8:13]
+    (vec_partner, vec_core, right_out, left_out, left_partial_out, mine_out) = refs[13:19]
+    (own_loss_out, loss_out, left, norm_b, e_own, mine_own, mine_partner) = refs[19:]
     rows, quart = zero_own.shape
     width = quart // 2
     lower, upper = slice(0, quart), slice(quart, 2 * quart)
@@ -407,25 +392,23 @@
         @pl.when(flags[0] == tile)
         def _():
             mine_own[...] = corr
-            partner = partner_own if tile < 2 else partner_other
             mine_partner[...] = tile_corr(
-                late, inner, partner[:, inner], columns_partner, late_b_other
+                late, inner, partner_sums[:, at], columns_partner, late_b_other
             )
 
     diagonal_row = jnp.concatenate(diagonals, axis=1)
-    partner_second = jnp.concatenate([vec_own[0:1, :], vec_other[0:1, :]], axis=1)
-    second_a = rstd * (partner_second + jnp.concatenate(down, axis=1))
+    second_a = rstd * (vec_partner[0:1, :] + jnp.concatenate(down, axis=1))
     second_b = lanes_to_row(across)
     own_loss = jnp.sum(losses)
     own_loss_out[...] = jnp.broadcast_to(own_loss, (8, 128))
-    loss = own_loss + jnp.sum(vec_other[1:2, :] + vec_core[1:2, :])
+    loss = own_loss + jnp.sum(vec_partner[0:1, :] + vec_core[0:1, :])
     loss_out[...] = jnp.broadcast_to(loss, (8, 128))
 
     for tile in (2, 3, 0, 1):
         at = slice(tile * width, (tile + 1) * width)
         inner = slice((tile % 2) * width, (tile % 2 + 1) * width)
-        source, e_partner = (first_own, e_left) if tile < 2 else (first_other, e_right)
-        terms = dot(norm_b[:, lower], e_own[:, at]) + dot(norm_b[:, upper], e_partner[:, inner])
+        source = first_own if tile < 2 else first_other
+        terms = dot(norm_b[:, lower], e_own[:, at]) + dot(norm_b[:, upper], e_partner[:, at])
         xhat = (source[:, inner].astype(jnp.float32) - offset[:, at]) * rstd[:, at]
         value = terms[:rows] - terms[rows : rows + 1] - xhat * second_a[:, at]
         if tile < 2:
@@ -466,8 +449,15 @@
     out[0] = (one[0, 0] + other[0, 0]) / feats
 
 
-def final_kernel(right, from_x, late_b, first_b, left, from_core, right_out, left_out):
-    rows, quart = left.shape
+def left_final_kernel(left, from_core, left_out):
+    for at in range(0, left.shape[0], 64):
+        piece = slice(at, at + 64)
+        value = left[piece, :] + from_core[piece, :].astype(jnp.float32)
+        left_out[piece, :] = value.astype(jnp.bfloat16)
+
+
+def right_final_kernel(right, from_x, late_b, first_b, right_out):
+    rows, quart = right.shape
     offset, rstd, _, _ = joined_rows(late_b, quart)
     second = joined_rows(from_x, rows)[0]
     for at in range(0, rows, 64):
@@ -475,8 +465,6 @@
         xhat = (first_b[piece, :].astype(jnp.float32) - offset) * rstd
         value = right[piece, :] + from_x[piece, :].astype(jnp.float32) - xhat * second
         right_out[piece, :] = (rstd * value).astype(jnp.bfloat16)
-        value = left[piece, :] + from_core[piece, :].astype(jnp.float32)
-        left_out[piece, :] = value.astype(jnp.bfloat16)
 
 
 vmem = pl.BlockSpec(memory_space=pltpu.VMEM)
@@ -537,7 +525,6 @@
     extended = jax.ShapeDtypeStruct((rows + 16, quart), jnp.bfloat16)
     row_out = jax.ShapeDtypeStruct((8, quart), jnp.float32)
     one_out = jax.ShapeDtypeStruct((8, 128), jnp.float32)
-    across_shape = jax.ShapeDtypeStruct((quart, 128), jnp.float32)
     low = lambda n, m: pltpu.VMEM((n, m), jnp.bfloat16)
 
     def picked(outer, inner):
@@ -576,13 +563,12 @@
         held=(0, 1, 2, 3),
     )
     late_b_other = x_swap(late_b)
-    partner_own, partner_other, own_all, row_other, zero_own, zero_other = local_call(
+    partner_all, own_all, row_other, zero_own, zero_other = local_call(
         products_kernel,
         (left_outputs, other_a0, first_a, other_a1, second_a, other_a2)
         + (right_outputs, other_b0, first_b, other_b1, second_b, other_b2),
         (
-            quarter_f32,
-            quarter_f32,
+            jax.ShapeDtypeStruct((quart, half), jnp.float32),
             jax.ShapeDtypeStruct((quart, half), jnp.float32),
             row_out,
             quarter_bf16,
@@ -601,35 +587,25 @@
     )
     late_a_other = core_swap(late_a)
 
-    terms, across, e_left, vec_own = local_call(
-        functools.partial(partner_kernel, batch_images, 0),
-        (late_a, zero_own, partner_own, late_b_other),
+    partial_right, e_partner, vec_partner = local_call(
+        functools.partial(partner_kernel, batch_images),
+        (late_a, late_a_other, zero_own, zero_other, partner_all, late_b_other),
         (
-            jax.ShapeDtypeStruct((rows + 16, quart), jnp.float32),
-            across_shape,
-            quarter_bf16,
-            row_out,
+            extended,
+            jax.ShapeDtypeStruct((quart, half), jnp.bfloat16),
+            jax.ShapeDtypeStruct((8, half), jnp.float32),
         ),
-        [low(rows + 16, quart)],
-        2 * gemm,
-        room=12,
-    )
-    partial_right, e_right, vec_other = local_call(
-        functools.partial(partner_kernel, batch_images, 1),
-        (late_a_other, zero_other, partner_other, late_b_other, terms, across, vec_own),
-        (extended, quarter_bf16, row_out),
-        [low(rows + 16, quart)],
-        2 * gemm,
-        room=12,
+        [low(rows + 16, half)],
+        4 * gemm,
+        room=16,
     )
     from_x = x_swap(partial_right)
-    vec_core = core_swap(vec_other)
+    vec_core = core_swap(vec_partner)
     right_own, left_own, partial_left, mine, own_loss, loss = local_call(
         functools.partial(own_kernel, batch_images),
         (flags, late_a, late_a_other, left_outputs, other_a0, zero_own, zero_other, own_all)
-        + (late_b, late_b_other, right_outputs, other_b0, e_left, e_right)
-        + (partner_own, partner_other)
-        + (vec_own, vec_other, vec_core),
+        + (late_b, late_b_other, right_outputs, other_b0, e_partner)
+        + (partner_all, vec_partner, vec_core),
         (
             quarter_f32,
             quarter_f32,
@@ -652,10 +628,10 @@
     core_loss = core_swap(own_loss)
     (loss,) = local_call(add_kernel, (loss, core_loss), (one_out,))
     x_loss = x_swap(loss)
-    right_gradient, left_gradient = local_call(
-        final_kernel,
-        (right_own, from_x, late_b, right_outputs, left_own, from_core),
-        (quarter_bf16, quarter_bf16),
+    (left_gradient,) = local_call(left_final_kernel, (left_own, from_core), (quarter_bf16,))
+    right_own, left_gradient = after(right_own, left_gradient)
+    (right_gradient,) = local_call(
+        right_final_kernel, (right_own, from_x, late_b, right_outputs), (quarter_bf16,)
     )
     right_gradient, x_loss = after(right_gradient, x_loss)
     (loss,) = local_call(

time: 95.5 us -> 99.9 us (1.046)
  waiting for transfers between devices: 49.1 us -> 53.4 us
    ppermute x10, waiting for transfers between devices: 41.3 us -> 45.7 us  [along(): return lax.ppermute(block, 'dp', route)]
  transfers between devices with their start and end apart: 24 -> 24, of which waited for: 10 -> 11; matrix products, arithmetic and copies ran while one was open for 0% -> 0% of each run, Pallas kernels for 17% -> 16%
where the time goes in v10:
time: 99.9 us; the launch traced here: 99.6 us
  waiting for transfers between devices  53.4 us (53%)
  starting transfers between devices  25.8 us (26%)
  Pallas kernels  18.3 us (18%)
  local copies, waits for them, and re-layouts  1.05 us (1%)
    ppermute x10, waiting for transfers between devices, along(): return lax.ppermute(block, 'dp', route)  45.7 us
    pallas_call x12, Pallas kernels, local_call(): pl.pallas_call(kernel, out_shape=list(outs), in_specs=[space(x) for x in...  18.3 us
    ppermute x10, starting transfers between devices, along(): return lax.ppermute(block, 'dp', route)  14.9 us
    ppermute x14, starting transfers between devices, swapped(): return lax.ppermute(block, axis, route)  10.9 us
    ppermute x14, waiting for transfers between devices, swapped(): return lax.ppermute(block, axis, route)  7.73 us
  transfers between devices with their start and end apart: 24, of which 11 were waited for; matrix products, arithmetic and copies ran while one was open for 0% of the time, Pallas kernels for 16%

profile of v10, /device:TPU:0, one launch (start us, length us, event | category | flops | bytes accessed | tf_op | source)
XLA Modules:
  0.0 99.6 jit_solution(14712866220195105109)
XLA Ops:
  1.1 2.7 %collective-permute-start.1 = (bf16[512,512]{1,0:T(8,128)(2,1)}, bf16[512,512]{1,0:T(8,128)(2,1)S(1)}, u32[]{:S(2)}, u32[]{:S(2)}) collective-permute-start(bf16[512,512]{1,0:T(8,128)(2,1)} %refs_2_.1), channel_id=1, source_target_pairs={{0,4},{4,0},{8,12},{12,8},{1,5},{5,1},{9,13},{13,9},{2,6},{6,2},{1... | collective-permute-start | bytes 1572872 | tf_op jit(solution)/shard_map/ppermute | solution.py:510
  4.5 1.6 %collective-permute-start.7 = (bf16[512,512]{1,0:T(8,128)(2,1)}, bf16[512,512]{1,0:T(8,128)(2,1)S(1)}, u32[]{:S(2)}, u32[]{:S(2)}) collective-permute-start(bf16[512,512]{1,0:T(8,128)(2,1)} %first_b.1), channel_id=1, source_target_pairs={{0,2},{2,0},{1,3},{3,1},{4,6},{6,4},{5,7},{7,5},{8,10},{10,8},{9,1... | collective-permute-start | bytes 1572872 | tf_op jit(solution)/shard_map/ppermute | solution.py:19
  6.0 4.4 %collective-permute-start.6 = (bf16[512,512]{1,0:T(8,128)(2,1)}, bf16[512,512]{1,0:T(8,128)(2,1)S(1)}, u32[]{:S(2)}, u32[]{:S(2)}) collective-permute-start(bf16[512,512]{1,0:T(8,128)(2,1)} %first_b.1), channel_id=1, source_target_pairs={{0,4},{4,0},{8,12},{12,8},{1,5},{5,1},{9,13},{13,9},{2,6},{6,2},{1... | collective-permute-start | bytes 1572872 | tf_op jit(solution)/shard_map/ppermute | solution.py:510
  10.5 6.3 %collective-permute-done.1.refs_2_ = bf16[512,512]{1,0:T(8,128)(2,1)S(1)} collective-permute-done((bf16[512,512]{1,0:T(8,128)(2,1)}, bf16[512,512]{1,0:T(8,128)(2,1)S(1)}, u32[]{:S(2)}, u32[]{:S(2)}) %collective-permute-start.1) | collective-permute-done | bytes 524320 | tf_op jit(solution)/shard_map/ppermute | solution.py:510
  16.8 0.7 collective-permute-start.10
  17.5 1.3 %collective-permute-start.5 = (bf16[512,512]{1,0:T(8,128)(2,1)S(1)}, bf16[512,512]{1,0:T(8,128)(2,1)S(1)}, u32[]{:S(2)}, u32[]{:S(2)}) collective-permute-start(bf16[512,512]{1,0:T(8,128)(2,1)S(1)} %collective-permute-done.4.inner), channel_id=1, source_target_pairs={{4,0},{8,12},{5,1},{9,13},{6,2},{10,14},{7,3},{11,15},{20,16},{24,... | collective-permute-start | bytes 1572872 | tf_op jit(solution)/shard_map/ppermute | solution.py:510
  18.9 9.1 %collective-permute-done.6.second.refs_8_ = bf16[512,512]{1,0:T(8,128)(2,1)S(1)} collective-permute-done((bf16[512,512]{1,0:T(8,128)(2,1)}, bf16[512,512]{1,0:T(8,128)(2,1)S(1)}, u32[]{:S(2)}, u32[]{:S(2)}) %collective-permute-start.6) | collective-permute-done | bytes 524320 | tf_op jit(solution)/shard_map/ppermute | solution.py:510
  28.0 1.9 %collective-permute-start.8 = (bf16[512,512]{1,0:T(8,128)(2,1)S(1)}, bf16[512,512]{1,0:T(8,128)(2,1)S(1)}, u32[]{:S(2)}, u32[]{:S(2)}) collective-permute-start(bf16[512,512]{1,0:T(8,128)(2,1)S(1)} %collective-permute-done.6.second.refs_8_), channel_id=1, source_target_pairs={{0,2},{2,0},{1,3},{3,1},{4,6},{6,4},{5,7},{7,5},{8,10},{10,8},{9,1... | collective-permute-start | bytes 1572872 | tf_op jit(solution)/shard_map/ppermute | solution.py:19
  29.9 1.3 %collective-permute-start.11 = (bf16[512,512]{1,0:T(8,128)(2,1)S(1)}, bf16[512,512]{1,0:T(8,128)(2,1)S(1)}, u32[]{:S(2)}, u32[]{:S(2)}) collective-permute-start(bf16[512,512]{1,0:T(8,128)(2,1)S(1)} %collective-permute-done.10.inner), channel_id=1, source_target_pairs={{4,0},{8,12},{5,1},{9,13},{6,2},{10,14},{7,3},{11,15},{20,16},{24,... | collective-permute-start | bytes 1572872 | tf_op jit(solution)/shard_map/ppermute | solution.py:510
  31.2 0.7 collective-permute-start.16
  31.9 7.4 %collective-permute-done.5.outer = bf16[512,512]{1,0:T(8,128)(2,1)S(1)} collective-permute-done((bf16[512,512]{1,0:T(8,128)(2,1)S(1)}, bf16[512,512]{1,0:T(8,128)(2,1)S(1)}, u32[]{:S(2)}, u32[]{:S(2)}) %collective-permute-start.5) | collective-permute-done | bytes 524320 | tf_op jit(solution)/shard_map/ppermute | solution.py:510
  40.1 1.4 %collective-permute-done.8.refs_9_ = bf16[512,512]{1,0:T(8,128)(2,1)S(1)} collective-permute-done((bf16[512,512]{1,0:T(8,128)(2,1)S(1)}, bf16[512,512]{1,0:T(8,128)(2,1)S(1)}, u32[]{:S(2)}, u32[]{:S(2)}) %collective-permute-start.8) | collective-permute-done | bytes 524320 | tf_op jit(solution)/shard_map/ppermute | solution.py:19
  41.4 1.5 %collective-permute-start.13 = (bf16[512,512]{1,0:T(8,128)(2,1)S(1)}, bf16[512,512]{1,0:T(8,128)(2,1)S(1)}, u32[]{:S(2)}, u32[]{:S(2)}) collective-permute-start(bf16[512,512]{1,0:T(8,128)(2,1)S(1)} %shard_map.57.third.refs_10_), channel_id=1, source_target_pairs={{0,2},{2,0},{1,3},{3,1},{4,6},{6,4},{5,7},{7,5},{8,10},{10,8},{9,1... | collective-permute-start | bytes 1572872 | tf_op jit(solution)/shard_map/ppermute | solution.py:19
  42.9 1.0 %copy-done = bf16[512,512]{1,0:T(8,128)(2,1)S(1)} copy-done((bf16[512,512]{1,0:T(8,128)(2,1)S(1)}, bf16[512,512]{1,0:T(8,128)(2,1)}, u32[]{:S(2)}) %copy-start) | copy-done | bytes 524312
  44.0 1.0 shard_map.59.row
  45.0 5.3 %collective-permute-done.11.outer = bf16[512,512]{1,0:T(8,128)(2,1)S(1)} collective-permute-done((bf16[512,512]{1,0:T(8,128)(2,1)S(1)}, bf16[512,512]{1,0:T(8,128)(2,1)S(1)}, u32[]{:S(2)}, u32[]{:S(2)}) %collective-permute-start.11) | collective-permute-done | bytes 524320 | tf_op jit(solution)/shard_map/ppermute | solution.py:510
  50.5 1.3 %collective-permute-start.17 = (bf16[512,512]{1,0:T(8,128)(2,1)S(1)}, bf16[512,512]{1,0:T(8,128)(2,1)S(1)}, u32[]{:S(2)}, u32[]{:S(2)}) collective-permute-start(bf16[512,512]{1,0:T(8,128)(2,1)S(1)} %collective-permute-done.16.inner), channel_id=1, source_target_pairs={{4,0},{8,12},{5,1},{9,13},{6,2},{10,14},{7,3},{11,15},{20,16},{24,... | collective-permute-start | bytes 1572872 | tf_op jit(solution)/shard_map/ppermute | solution.py:510
  51.8 1.3 %collective-permute-start.3 = (bf16[512,512]{1,0:T(8,128)(2,1)S(1)}, bf16[512,512]{1,0:T(8,128)(2,1)S(1)}, u32[]{:S(2)}, u32[]{:S(2)}) collective-permute-start(bf16[512,512]{1,0:T(8,128)(2,1)S(1)} %collective-permute-done.2.inner), channel_id=1, source_target_pairs={{4,0},{8,12},{5,1},{9,13},{6,2},{10,14},{7,3},{11,15},{20,16},{24,... | collective-permute-start | bytes 1572872 | tf_op jit(solution)/shard_map/ppermute | solution.py:510
  53.1 0.9 collective-permute-done.13.refs_11_
  54.0 4.1 %shard_map.60 = (f32[512,1024]{1,0:T(8,128)S(1)}, f32[512,1024]{1,0:T(8,128)S(1)}, f32[8,512]{1,0:T(8,128)S(1)}, bf16[512,512]{1,0:T(8,128)(2,1)S(1)}, bf16[512,512]{1,0:T(8,128)(2,1)S(1)}) custom-call(bf16[512,512]{1,0:T(8,128)(2,1)S(1)} %copy-done.2, bf16[512,512]{1,0:T(8,128)(2,1)S(1)} %collective-permute-done.refs_1_.refs_3_, ...), custom_call_target="tpu_custom_call" | custom-call | flops 3221225472 | bytes 11550720 | tf_op jit(solution)/shard_map/pallas_call | solution.py:480
  58.1 8.9 %collective-permute-done.17.outer = bf16[512,512]{1,0:T(8,128)(2,1)S(1)} collective-permute-done((bf16[512,512]{1,0:T(8,128)(2,1)S(1)}, bf16[512,512]{1,0:T(8,128)(2,1)S(1)}, u32[]{:S(2)}, u32[]{:S(2)}) %collective-permute-start.17) | collective-permute-done | bytes 524320 | tf_op jit(solution)/shard_map/ppermute | solution.py:510
  67.5 1.7 %collective-permute-start.18 = (bf16[528,512]{1,0:T(8,128)(2,1)S(1)}, bf16[528,512]{1,0:T(8,128)(2,1)S(1)}, u32[]{:S(2)}, u32[]{:S(2)}) collective-permute-start(bf16[528,512]{1,0:T(8,128)(2,1)S(1)} %shard_map.62.refs_7_.late_b), channel_id=1, source_target_pairs={{0,2},{2,0},{1,3},{3,1},{4,6},{6,4},{5,7},{7,5},{8,10},{10,8},{9,1... | collective-permute-start | bytes 1622024 | tf_op jit(solution)/shard_map/ppermute | solution.py:19
  69.2 8.7 %collective-permute-done.3.outer = bf16[512,512]{1,0:T(8,128)(2,1)S(1)} collective-permute-done((bf16[512,512]{1,0:T(8,128)(2,1)S(1)}, bf16[512,512]{1,0:T(8,128)(2,1)S(1)}, u32[]{:S(2)}, u32[]{:S(2)}) %collective-permute-start.3) | collective-permute-done | bytes 524320 | tf_op jit(solution)/shard_map/ppermute | solution.py:510
  78.4 2.6 %collective-permute-done.18.late_b.refs_8_ = bf16[528,512]{1,0:T(8,128)(2,1)S(1)} collective-permute-done((bf16[528,512]{1,0:T(8,128)(2,1)S(1)}, bf16[528,512]{1,0:T(8,128)(2,1)S(1)}, u32[]{:S(2)}, u32[]{:S(2)}) %collective-permute-start.18) | collective-permute-done | bytes 540704 | tf_op jit(solution)/shard_map/ppermute | solution.py:19
  81.0 2.0 %shard_map.63 = (bf16[528,512]{1,0:T(8,128)(2,1)S(1)}, bf16[512,1024]{1,0:T(8,128)(2,1)S(1)}, f32[8,1024]{1,0:T(8,128)S(1)}) custom-call(bf16[528,512]{1,0:T(8,128)(2,1)S(1)} %shard_map.61.late_own.refs_0_, bf16[528,512]{1,0:T(8,128)(2,1)S(1)} %collective-permute-done.15.late_other.refs_1_, bf16[512,512]{1,0:T(8,128)(2,1)S(1)} %get-tuple-element.48.zero_own.refs_4_, ...), custom_call_target="tpu_custom_call" | custom-call | flops 1073741824 | bytes 6389760 | tf_op jit(solution)/shard_map/pallas_call | solution.py:480
  83.1 1.7 %collective-permute-start.21 = (bf16[528,512]{1,0:T(8,128)(2,1)S(1)}, bf16[528,512]{1,0:T(8,128)(2,1)S(1)}, u32[]{:S(2)}, u32[]{:S(2)}) collective-permute-start(bf16[528,512]{1,0:T(8,128)(2,1)S(1)} %get-tuple-element.60), channel_id=1, source_target_pairs={{0,2},{2,0},{1,3},{3,1},{4,6},{6,4},{5,7},{7,5},{8,10},{10,8},{9,1... | collective-permute-start | bytes 1622024 | tf_op jit(solution)/shard_map/ppermute | solution.py:19
  84.8 7.6 %shard_map.64 = (f32[512,512]{1,0:T(8,128)S(1)}, f32[512,512]{1,0:T(8,128)S(1)}, bf16[512,512]{1,0:T(8,128)(2,1)S(1)}, f32[256,1024]{1,0:T(8,128)}, f32[8,128]{1,0:T(8,128)S(1)}, /*index=5*/f32[8,128]{1,0:T(8,128)S(1)}) custom-call(s32[2]{0:T(128)S(1)} %pad_add_fusion.flags, bf16[528,512]{1,0:T(8,128)(2,1)S(1)} %shard_map.61.late_own.refs_0_, ...), custom_call_target="tpu_custom_call" | custom-call | flops 2147483648 | bytes 14295048 | tf_op jit(solution)/shard_map/pallas_call | solution.py:480
  92.9 1.4 %collective-permute-done.22.other = f32[8,128]{1,0:T(8,128)S(1)} collective-permute-done((f32[8,128]{1,0:T(8,128)S(1)}, f32[8,128]{1,0:T(8,128)S(1)}, u32[]{:S(2)}, u32[]{:S(2)}) %collective-permute-start.22) | collective-permute-done | bytes 4128 | tf_op jit(solution)/shard_map/ppermute | solution.py:19
  94.3 1.1 %collective-permute-start.23 = (f32[8,128]{1,0:T(8,128)S(1)}, f32[8,128]{1,0:T(8,128)S(1)}, u32[]{:S(2)}, u32[]{:S(2)}) collective-permute-start(f32[8,128]{1,0:T(8,128)S(1)} %shard_map.67.one), channel_id=1, source_target_pairs={{0,2},{2,0},{1,3},{3,1},{4,6},{6,4},{5,7},{7,5},{8,10},{10,8},{9,1... | collective-permute-start | bytes 12296 | tf_op jit(solution)/shard_map/ppermute | solution.py:19
  95.5 0.9 shard_map.65
  96.4 1.4 %collective-permute-done.21.from_x = bf16[528,512]{1,0:T(8,128)(2,1)S(1)} collective-permute-done((bf16[528,512]{1,0:T(8,128)(2,1)S(1)}, bf16[528,512]{1,0:T(8,128)(2,1)S(1)}, u32[]{:S(2)}, u32[]{:S(2)}) %collective-permute-start.21) | collective-permute-done | bytes 540704 | tf_op jit(solution)/shard_map/ppermute | solution.py:19
  97.8 1.1 %shard_map.66 = bf16[512,512]{1,0:T(8,128)(2,1)} custom-call(f32[512,512]{1,0:T(8,128)S(1)} %get-tuple-element.59.right, bf16[528,512]{1,0:T(8,128)(2,1)S(1)} %collective-permute-done.21.from_x, bf16[528,512]{1,0:T(8,128)(2,1)S(1)} %shard_map.62.refs_7_.late_b, bf16[512,512]{1,0:T(8,128)(2,1)S(1)} %copy-done.1), custom_call_target="tpu_custom_call" | custom-call | flops 1048576 | bytes 3178496 | tf_op jit(solution)/shard_map/pallas_call | solution.py:480
  (36 shorter events, 4.5 us)
Async XLA Ops:
  0.6 9.9 %collective-permute-start = (bf16[512,512]{1,0:T(8,128)(2,1)}, bf16[512,512]{1,0:T(8,128)(2,1)S(1)}, u32[]{:S(2)}, u32[]{:S(2)}) collective-permute-start(bf16[512,512]{1,0:T(8,128)(2,1)} %refs_2_.1), channel_id=1, source_target_pairs={{0,1},{1,0},{2,3},{3,2},{4,5},{5,4},{6,7},{7,6},{8,9},{9,8},{10,11... | collective-permute-start | bytes 1572872 | tf_op jit(solution)/shard_map/ppermute | solution.py:19
  1.1 15.6 %collective-permute-start.1 = (bf16[512,512]{1,0:T(8,128)(2,1)}, bf16[512,512]{1,0:T(8,128)(2,1)S(1)}, u32[]{:S(2)}, u32[]{:S(2)}) collective-permute-start(bf16[512,512]{1,0:T(8,128)(2,1)} %refs_2_.1), channel_id=1, source_target_pairs={{0,4},{4,0},{8,12},{12,8},{1,5},{5,1},{9,13},{13,9},{2,6},{6,2},{1... | collective-permute-start | bytes 1572872 | tf_op jit(solution)/shard_map/ppermute | solution.py:510
  3.8 13.7 %collective-permute-start.4 = (bf16[512,512]{1,0:T(8,128)(2,1)}, bf16[512,512]{1,0:T(8,128)(2,1)S(1)}, u32[]{:S(2)}, u32[]{:S(2)}) collective-permute-start(bf16[512,512]{1,0:T(8,128)(2,1)} %first_b.1), channel_id=1, source_target_pairs={{4,8},{8,4},{5,9},{9,5},{6,10},{10,6},{7,11},{11,7},{20,24},{24,20... | collective-permute-start | bytes 1572872 | tf_op jit(solution)/shard_map/ppermute | solution.py:510
  4.5 14.4 %collective-permute-start.7 = (bf16[512,512]{1,0:T(8,128)(2,1)}, bf16[512,512]{1,0:T(8,128)(2,1)S(1)}, u32[]{:S(2)}, u32[]{:S(2)}) collective-permute-start(bf16[512,512]{1,0:T(8,128)(2,1)} %first_b.1), channel_id=1, source_target_pairs={{0,2},{2,0},{1,3},{3,1},{4,6},{6,4},{5,7},{7,5},{8,10},{10,8},{9,1... | collective-permute-start | bytes 1572872 | tf_op jit(solution)/shard_map/ppermute | solution.py:19
  6.0 22.0 %collective-permute-start.6 = (bf16[512,512]{1,0:T(8,128)(2,1)}, bf16[512,512]{1,0:T(8,128)(2,1)S(1)}, u32[]{:S(2)}, u32[]{:S(2)}) collective-permute-start(bf16[512,512]{1,0:T(8,128)(2,1)} %first_b.1), channel_id=1, source_target_pairs={{0,4},{4,0},{8,12},{12,8},{1,5},{5,1},{9,13},{13,9},{2,6},{6,2},{1... | collective-permute-start | bytes 1572872 | tf_op jit(solution)/shard_map/ppermute | solution.py:510
  10.5 43.5 %copy-start.1 = (bf16[512,512]{1,0:T(8,128)(2,1)S(1)}, bf16[512,512]{1,0:T(8,128)(2,1)}, u32[]{:S(2)}) copy-start(bf16[512,512]{1,0:T(8,128)(2,1)} %first_b.1) | copy-start | bytes 1572868
  10.5 43.5 %copy-start.2 = (bf16[512,512]{1,0:T(8,128)(2,1)S(1)}, bf16[512,512]{1,0:T(8,128)(2,1)}, u32[]{:S(2)}) copy-start(bf16[512,512]{1,0:T(8,128)(2,1)} %refs_2_.1) | copy-start | bytes 1572868
  16.8 13.1 %collective-permute-start.10 = (bf16[512,512]{1,0:T(8,128)(2,1)}, bf16[512,512]{1,0:T(8,128)(2,1)S(1)}, u32[]{:S(2)}, u32[]{:S(2)}) collective-permute-start(bf16[512,512]{1,0:T(8,128)(2,1)} %refs_2_.1), channel_id=1, source_target_pairs={{4,8},{8,4},{5,9},{9,5},{6,10},{10,6},{7,11},{11,7},{20,24},{24,20... | collective-permute-start | bytes 1572872 | tf_op jit(solution)/shard_map/ppermute | solution.py:510
  17.5 21.8 %collective-permute-start.5 = (bf16[512,512]{1,0:T(8,128)(2,1)S(1)}, bf16[512,512]{1,0:T(8,128)(2,1)S(1)}, u32[]{:S(2)}, u32[]{:S(2)}) collective-permute-start(bf16[512,512]{1,0:T(8,128)(2,1)S(1)} %collective-permute-done.4.inner), channel_id=1, source_target_pairs={{4,0},{8,12},{5,1},{9,13},{6,2},{10,14},{7,3},{11,15},{20,16},{24,... | collective-permute-start | bytes 1572872 | tf_op jit(solution)/shard_map/ppermute | solution.py:510
  18.8 21.3 %collective-permute-start.9 = (bf16[512,512]{1,0:T(8,128)(2,1)S(1)}, bf16[512,512]{1,0:T(8,128)(2,1)S(1)}, u32[]{:S(2)}, u32[]{:S(2)}) collective-permute-start(bf16[512,512]{1,0:T(8,128)(2,1)S(1)} %collective-permute-done.1.refs_2_), channel_id=1, source_target_pairs={{0,1},{1,0},{2,3},{3,2},{4,5},{5,4},{6,7},{7,6},{8,9},{9,8},{10,11... | collective-permute-start | bytes 1572872 | tf_op jit(solution)/shard_map/ppermute | solution.py:19
  28.0 13.4 %collective-permute-start.8 = (bf16[512,512]{1,0:T(8,128)(2,1)S(1)}, bf16[512,512]{1,0:T(8,128)(2,1)S(1)}, u32[]{:S(2)}, u32[]{:S(2)}) collective-permute-start(bf16[512,512]{1,0:T(8,128)(2,1)S(1)} %collective-permute-done.6.second.refs_8_), channel_id=1, source_target_pairs={{0,2},{2,0},{1,3},{3,1},{4,6},{6,4},{5,7},{7,5},{8,10},{10,8},{9,1... | collective-permute-start | bytes 1572872 | tf_op jit(solution)/shard_map/ppermute | solution.py:19
  29.9 20.3 %collective-permute-start.11 = (bf16[512,512]{1,0:T(8,128)(2,1)S(1)}, bf16[512,512]{1,0:T(8,128)(2,1)S(1)}, u32[]{:S(2)}, u32[]{:S(2)}) collective-permute-start(bf16[512,512]{1,0:T(8,128)(2,1)S(1)} %collective-permute-done.10.inner), channel_id=1, source_target_pairs={{4,0},{8,12},{5,1},{9,13},{6,2},{10,14},{7,3},{11,15},{20,16},{24,... | collective-permute-start | bytes 1572872 | tf_op jit(solution)/shard_map/ppermute | solution.py:510
  31.2 19.3 %collective-permute-start.16 = (bf16[512,512]{1,0:T(8,128)(2,1)S(1)}, bf16[512,512]{1,0:T(8,128)(2,1)S(1)}, u32[]{:S(2)}, u32[]{:S(2)}) collective-permute-start(bf16[512,512]{1,0:T(8,128)(2,1)S(1)} %collective-permute-done.6.second.refs_8_), channel_id=1, source_target_pairs={{4,8},{8,4},{5,9},{9,5},{6,10},{10,6},{7,11},{11,7},{20,24},{24,20... | collective-permute-start | bytes 1572872 | tf_op jit(solution)/shard_map/ppermute | solution.py:510
  39.3 12.5 %collective-permute-start.2 = (bf16[512,512]{1,0:T(8,128)(2,1)S(1)}, bf16[512,512]{1,0:T(8,128)(2,1)S(1)}, u32[]{:S(2)}, u32[]{:S(2)}) collective-permute-start(bf16[512,512]{1,0:T(8,128)(2,1)S(1)} %collective-permute-done.1.refs_2_), channel_id=1, source_target_pairs={{4,8},{8,4},{5,9},{9,5},{6,10},{10,6},{7,11},{11,7},{20,24},{24,20... | collective-permute-start | bytes 1572872 | tf_op jit(solution)/shard_map/ppermute | solution.py:510
  41.4 12.5 %collective-permute-start.13 = (bf16[512,512]{1,0:T(8,128)(2,1)S(1)}, bf16[512,512]{1,0:T(8,128)(2,1)S(1)}, u32[]{:S(2)}, u32[]{:S(2)}) collective-permute-start(bf16[512,512]{1,0:T(8,128)(2,1)S(1)} %shard_map.57.third.refs_10_), channel_id=1, source_target_pairs={{0,2},{2,0},{1,3},{3,1},{4,6},{6,4},{5,7},{7,5},{8,10},{10,8},{9,1... | collective-permute-start | bytes 1572872 | tf_op jit(solution)/shard_map/ppermute | solution.py:19
  42.9 1.0 %copy-start = (bf16[512,512]{1,0:T(8,128)(2,1)S(1)}, bf16[512,512]{1,0:T(8,128)(2,1)}, u32[]{:S(2)}) copy-start(bf16[512,512]{1,0:T(8,128)(2,1)} %first_b.1) | copy-start | bytes 1572868
  50.4 3.6 %collective-permute-start.12 = (bf16[512,512]{1,0:T(8,128)(2,1)S(1)}, bf16[512,512]{1,0:T(8,128)(2,1)S(1)}, u32[]{:S(2)}, u32[]{:S(2)}) collective-permute-start(bf16[512,512]{1,0:T(8,128)(2,1)S(1)} %shard_map.58.refs_4_), channel_id=1, source_target_pairs={{0,1},{1,0},{2,3},{3,2},{4,5},{5,4},{6,7},{7,6},{8,9},{9,8},{10,11... | collective-permute-start | bytes 1572872 | tf_op jit(solution)/shard_map/ppermute | solution.py:19
  50.5 16.6 %collective-permute-start.17 = (bf16[512,512]{1,0:T(8,128)(2,1)S(1)}, bf16[512,512]{1,0:T(8,128)(2,1)S(1)}, u32[]{:S(2)}, u32[]{:S(2)}) collective-permute-start(bf16[512,512]{1,0:T(8,128)(2,1)S(1)} %collective-permute-done.16.inner), channel_id=1, source_target_pairs={{4,0},{8,12},{5,1},{9,13},{6,2},{10,14},{7,3},{11,15},{20,16},{24,... | collective-permute-start | bytes 1572872 | tf_op jit(solution)/shard_map/ppermute | solution.py:510
  51.8 26.1 %collective-permute-start.3 = (bf16[512,512]{1,0:T(8,128)(2,1)S(1)}, bf16[512,512]{1,0:T(8,128)(2,1)S(1)}, u32[]{:S(2)}, u32[]{:S(2)}) collective-permute-start(bf16[512,512]{1,0:T(8,128)(2,1)S(1)} %collective-permute-done.2.inner), channel_id=1, source_target_pairs={{4,0},{8,12},{5,1},{9,13},{6,2},{10,14},{7,3},{11,15},{20,16},{24,... | collective-permute-start | bytes 1572872 | tf_op jit(solution)/shard_map/ppermute | solution.py:510
  58.1 19.8 %collective-permute-start.14 = (f32[8,512]{1,0:T(8,128)S(1)}, f32[8,512]{1,0:T(8,128)S(1)}, u32[]{:S(2)}, u32[]{:S(2)}) collective-permute-start(f32[8,512]{1,0:T(8,128)S(1)} %get-tuple-element.47), channel_id=1, source_target_pairs={{0,1},{1,0},{2,3},{3,2},{4,5},{5,4},{6,7},{7,6},{8,9},{9,8},{10,11... | collective-permute-start | bytes 49160 | tf_op jit(solution)/shard_map/ppermute | solution.py:19
  67.5 13.5 %collective-permute-start.18 = (bf16[528,512]{1,0:T(8,128)(2,1)S(1)}, bf16[528,512]{1,0:T(8,128)(2,1)S(1)}, u32[]{:S(2)}, u32[]{:S(2)}) collective-permute-start(bf16[528,512]{1,0:T(8,128)(2,1)S(1)} %shard_map.62.refs_7_.late_b), channel_id=1, source_target_pairs={{0,2},{2,0},{1,3},{3,1},{4,6},{6,4},{5,7},{7,5},{8,10},{10,8},{9,1... | collective-permute-start | bytes 1622024 | tf_op jit(solution)/shard_map/ppermute | solution.py:19
  78.3 2.7 %collective-permute-start.15 = (bf16[528,512]{1,0:T(8,128)(2,1)S(1)}, bf16[528,512]{1,0:T(8,128)(2,1)S(1)}, u32[]{:S(2)}, u32[]{:S(2)}) collective-permute-start(bf16[528,512]{1,0:T(8,128)(2,1)S(1)} %shard_map.61.late_own.refs_0_), channel_id=1, source_target_pairs={{0,1},{1,0},{2,3},{3,2},{4,5},{5,4},{6,7},{7,6},{8,9},{9,8},{10,11... | collective-permute-start | bytes 1622024 | tf_op jit(solution)/shard_map/ppermute | solution.py:19
  83.0 1.8 %collective-permute-start.19 = (f32[8,1024]{1,0:T(8,128)S(1)}, f32[8,1024]{1,0:T(8,128)S(1)}, u32[]{:S(2)}, u32[]{:S(2)}) collective-permute-start(f32[8,1024]{1,0:T(8,128)S(1)} %get-tuple-element.54.refs_13_), channel_id=1, source_target_pairs={{0,1},{1,0},{2,3},{3,2},{4,5},{5,4},{6,7},{7,6},{8,9},{9,8},{10,11... | collective-permute-start | bytes 98312 | tf_op jit(solution)/shard_map/ppermute | solution.py:19
  83.1 14.7 %collective-permute-start.21 = (bf16[528,512]{1,0:T(8,128)(2,1)S(1)}, bf16[528,512]{1,0:T(8,128)(2,1)S(1)}, u32[]{:S(2)}, u32[]{:S(2)}) collective-permute-start(bf16[528,512]{1,0:T(8,128)(2,1)S(1)} %get-tuple-element.60), channel_id=1, source_target_pairs={{0,2},{2,0},{1,3},{3,1},{4,6},{6,4},{5,7},{7,5},{8,10},{10,8},{9,1... | collective-permute-start | bytes 1622024 | tf_op jit(solution)/shard_map/ppermute | solution.py:19
  92.4 3.0 %collective-permute-start.20 = (bf16[512,512]{1,0:T(8,128)(2,1)S(1)}, bf16[512,512]{1,0:T(8,128)(2,1)S(1)}, u32[]{:S(2)}, u32[]{:S(2)}) collective-permute-start(bf16[512,512]{1,0:T(8,128)(2,1)S(1)} %get-tuple-element.57), channel_id=1, source_target_pairs={{0,1},{1,0},{2,3},{3,2},{4,5},{5,4},{6,7},{7,6},{8,9},{9,8},{10,11... | collective-permute-start | bytes 1572872 | tf_op jit(solution)/shard_map/ppermute | solution.py:19
  92.6 1.8 %collective-permute-start.22 = (f32[8,128]{1,0:T(8,128)S(1)}, f32[8,128]{1,0:T(8,128)S(1)}, u32[]{:S(2)}, u32[]{:S(2)}) collective-permute-start(f32[8,128]{1,0:T(8,128)S(1)} %get-tuple-element.62), channel_id=1, source_target_pairs={{0,1},{1,0},{2,3},{3,2},{4,5},{5,4},{6,7},{7,6},{8,9},{9,8},{10,11... | collective-permute-start | bytes 12296 | tf_op jit(solution)/shard_map/ppermute | solution.py:19
  94.3 4.6 %collective-permute-start.23 = (f32[8,128]{1,0:T(8,128)S(1)}, f32[8,128]{1,0:T(8,128)S(1)}, u32[]{:S(2)}, u32[]{:S(2)}) collective-permute-start(f32[8,128]{1,0:T(8,128)S(1)} %shard_map.67.one), channel_id=1, source_target_pairs={{0,2},{2,0},{1,3},{3,1},{4,6},{6,4},{5,7},{7,5},{8,10},{10,8},{9,1... | collective-permute-start | bytes 12296 | tf_op jit(solution)/shard_map/ppermute | solution.py:19

commit v11 on v10

--- a/solution.py
+++ b/solution.py
@@ -304,15 +304,21 @@
     return columns[:, 0:1], columns[:, 1:2]
 
 
-def partner_kernel(images, late_own, late_other, zero_own, zero_other, sums, late_b, *refs):
-    partial_out, e_out, vec_out, left = refs
-    rows, quart = zero_own.shape
+def columns_kernel(images, late_b, late, zero, columns_out, left_out):
+    rows, quart = zero.shape
+    _, rstd, _, delta = joined_rows(late_b, quart)
+    columns_out[...] = jnp.transpose(rows_of([rstd / images, delta * rstd]))
+    left_operand(zero, late, left_out, slice(0, quart))
+
+
+def partner_kernel(columns, left_own, late_own, late_other, zero_other, sums, late_b, *refs):
+    partial_out, e_out, vec_out, left_other = refs
+    rows, quart = zero_other.shape
     width = quart // 2
-    scale_col, delta_col = scale_columns(late_b, images)
+    scale_col, delta_col = columns[:, 0:1], columns[:, 1:2]
+    left_operand(zero_other, late_other, left_other, slice(0, quart))
     across = jnp.zeros((quart, 128), jnp.float32)
     for part, late in enumerate((late_own, late_other)):
-        zero = (zero_own, zero_other)[part]
-        left_operand(zero, late, left, slice(part * quart, (part + 1) * quart))
         _, rstd, _, delta = joined_rows(late, rows)
         for tile in range(2):
             at = slice(tile * width, (tile + 1) * width)
@@ -328,7 +334,8 @@
     partial_out[rows:, :] = split_rows([second, nothing, nothing, nothing])
     for tile in range(2):
         at = slice(tile * width, (tile + 1) * width)
-        terms = dot_rows(left[...], e_out[at, :])
+        terms = dot_rows(left_own[...], e_out[at, :quart])
+        terms = terms + dot_rows(left_other[...], e_out[at, quart:])
         partial_out[:rows, at] = without_extra(terms, rows).astype(jnp.bfloat16)
 
 
@@ -563,6 +570,7 @@
         held=(0, 1, 2, 3),
     )
     late_b_other = x_swap(late_b)
+    other_b2, late_b = after(other_b2, late_b)
     partner_all, own_all, row_other, zero_own, zero_other = local_call(
         products_kernel,
         (left_outputs, other_a0, first_a, other_a1, second_a, other_a2)
@@ -587,15 +595,21 @@
     )
     late_a_other = core_swap(late_a)
 
+    columns, left_own_operand = local_call(
+        functools.partial(columns_kernel, batch_images),
+        (late_b_other, late_a, zero_own),
+        (jax.ShapeDtypeStruct((quart, 8), jnp.float32), extended),
+        flops=4 * gemm,
+    )
     partial_right, e_partner, vec_partner = local_call(
-        functools.partial(partner_kernel, batch_images),
-        (late_a, late_a_other, zero_own, zero_other, partner_all, late_b_other),
+        partner_kernel,
+        (columns, left_own_operand, late_a, late_a_other, zero_other, partner_all, late_b_other),
         (
             extended,
             jax.ShapeDtypeStruct((quart, half), jnp.bfloat16),
             jax.ShapeDtypeStruct((8, half), jnp.float32),
         ),
-        [low(rows + 16, half)],
+        [low(rows + 16, quart)],
         4 * gemm,
         room=16,
     )

time: 99.9 us -> 94.9 us (0.950)
  waiting for transfers between devices: 53.4 us -> 48.2 us
    ppermute x10, waiting for transfers between devices: 45.7 us -> 41.3 us  [along(): return lax.ppermute(block, 'dp', route)]
    pallas_call x12 -> x13, Pallas kernels: 18.3 us -> 18.5 us  [local_call(): pl.pallas_call(kernel, out_shape=list(outs), in_specs=[space(x) for x in...]
  transfers between devices with their start and end apart: 24 -> 24, of which waited for: 11 -> 10; matrix products, arithmetic and copies ran while one was open for 0% -> 0% of each run, Pallas kernels for 16% -> 17%
where the time goes in v11:
time: 94.9 us; the launch traced here: 94.6 us
  waiting for transfers between devices  48.2 us (51%)
  starting transfers between devices  25.8 us (27%)
  Pallas kernels  18.5 us (19%)
  local copies, waits for them, and re-layouts  1.05 us (1%)
  between operations  1.03 us (1%)
    ppermute x10, waiting for transfers between devices, along(): return lax.ppermute(block, 'dp', route)  41.3 us
    pallas_call x13, Pallas kernels, local_call(): pl.pallas_call(kernel, out_shape=list(outs), in_specs=[space(x) for x in...  18.5 us
    ppermute x10, starting transfers between devices, along(): return lax.ppermute(block, 'dp', route)  14.9 us
    ppermute x14, starting transfers between devices, swapped(): return lax.ppermute(block, axis, route)  10.9 us
    ppermute x14, waiting for transfers between devices, swapped(): return lax.ppermute(block, axis, route)  6.9 us
  transfers between devices with their start and end apart: 24, of which 10 were waited for; matrix products, arithmetic and copies ran while one was open for 0% of the time, Pallas kernels for 17%

profile of v11, /device:TPU:0, one launch (start us, length us, event | category | flops | bytes accessed | tf_op | source)
XLA Modules:
  0.0 94.6 jit_solution(939193482074568555)
XLA Ops:
  1.1 2.7 %collective-permute-start.1 = (bf16[512,512]{1,0:T(8,128)(2,1)}, bf16[512,512]{1,0:T(8,128)(2,1)S(1)}, u32[]{:S(2)}, u32[]{:S(2)}) collective-permute-start(bf16[512,512]{1,0:T(8,128)(2,1)} %refs_2_.1), channel_id=1, source_target_pairs={{0,4},{4,0},{8,12},{12,8},{1,5},{5,1},{9,13},{13,9},{2,6},{6,2},{1... | collective-permute-start | bytes 1572872 | tf_op jit(solution)/shard_map/ppermute | solution.py:517
  3.8 0.7 collective-permute-start.4
  4.5 1.6 %collective-permute-start.7 = (bf16[512,512]{1,0:T(8,128)(2,1)}, bf16[512,512]{1,0:T(8,128)(2,1)S(1)}, u32[]{:S(2)}, u32[]{:S(2)}) collective-permute-start(bf16[512,512]{1,0:T(8,128)(2,1)} %first_b.1), channel_id=1, source_target_pairs={{0,2},{2,0},{1,3},{3,1},{4,6},{6,4},{5,7},{7,5},{8,10},{10,8},{9,1... | collective-permute-start | bytes 1572872 | tf_op jit(solution)/shard_map/ppermute | solution.py:19
  6.0 4.4 %collective-permute-start.6 = (bf16[512,512]{1,0:T(8,128)(2,1)}, bf16[512,512]{1,0:T(8,128)(2,1)S(1)}, u32[]{:S(2)}, u32[]{:S(2)}) collective-permute-start(bf16[512,512]{1,0:T(8,128)(2,1)} %first_b.1), channel_id=1, source_target_pairs={{0,4},{4,0},{8,12},{12,8},{1,5},{5,1},{9,13},{13,9},{2,6},{6,2},{1... | collective-permute-start | bytes 1572872 | tf_op jit(solution)/shard_map/ppermute | solution.py:517
  10.5 6.3 %collective-permute-done.1.refs_2_ = bf16[512,512]{1,0:T(8,128)(2,1)S(1)} collective-permute-done((bf16[512,512]{1,0:T(8,128)(2,1)}, bf16[512,512]{1,0:T(8,128)(2,1)S(1)}, u32[]{:S(2)}, u32[]{:S(2)}) %collective-permute-start.1) | collective-permute-done | bytes 524320 | tf_op jit(solution)/shard_map/ppermute | solution.py:517
  16.8 0.7 collective-permute-start.10
  17.5 1.3 %collective-permute-start.5 = (bf16[512,512]{1,0:T(8,128)(2,1)S(1)}, bf16[512,512]{1,0:T(8,128)(2,1)S(1)}, u32[]{:S(2)}, u32[]{:S(2)}) collective-permute-start(bf16[512,512]{1,0:T(8,128)(2,1)S(1)} %collective-permute-done.4.inner), channel_id=1, source_target_pairs={{4,0},{8,12},{5,1},{9,13},{6,2},{10,14},{7,3},{11,15},{20,16},{24,... | collective-permute-start | bytes 1572872 | tf_op jit(solution)/shard_map/ppermute | solution.py:517
  18.9 9.1 %collective-permute-done.6.second.refs_8_ = bf16[512,512]{1,0:T(8,128)(2,1)S(1)} collective-permute-done((bf16[512,512]{1,0:T(8,128)(2,1)}, bf16[512,512]{1,0:T(8,128)(2,1)S(1)}, u32[]{:S(2)}, u32[]{:S(2)}) %collective-permute-start.6) | collective-permute-done | bytes 524320 | tf_op jit(solution)/shard_map/ppermute | solution.py:517
  28.0 1.9 %collective-permute-start.8 = (bf16[512,512]{1,0:T(8,128)(2,1)S(1)}, bf16[512,512]{1,0:T(8,128)(2,1)S(1)}, u32[]{:S(2)}, u32[]{:S(2)}) collective-permute-start(bf16[512,512]{1,0:T(8,128)(2,1)S(1)} %collective-permute-done.6.second.refs_8_), channel_id=1, source_target_pairs={{0,2},{2,0},{1,3},{3,1},{4,6},{6,4},{5,7},{7,5},{8,10},{10,8},{9,1... | collective-permute-start | bytes 1572872 | tf_op jit(solution)/shard_map/ppermute | solution.py:19
  30.6 1.3 %collective-permute-start.11 = (bf16[512,512]{1,0:T(8,128)(2,1)S(1)}, bf16[512,512]{1,0:T(8,128)(2,1)S(1)}, u32[]{:S(2)}, u32[]{:S(2)}) collective-permute-start(bf16[512,512]{1,0:T(8,128)(2,1)S(1)} %collective-permute-done.10.inner), channel_id=1, source_target_pairs={{4,0},{8,12},{5,1},{9,13},{6,2},{10,14},{7,3},{11,15},{20,16},{24,... | collective-permute-start | bytes 1572872 | tf_op jit(solution)/shard_map/ppermute | solution.py:517
  31.9 7.4 %collective-permute-done.5.outer = bf16[512,512]{1,0:T(8,128)(2,1)S(1)} collective-permute-done((bf16[512,512]{1,0:T(8,128)(2,1)S(1)}, bf16[512,512]{1,0:T(8,128)(2,1)S(1)}, u32[]{:S(2)}, u32[]{:S(2)}) %collective-permute-start.5) | collective-permute-done | bytes 524320 | tf_op jit(solution)/shard_map/ppermute | solution.py:517
  39.3 0.7 collective-permute-start.2
  40.1 1.3 %collective-permute-done.8.refs_9_ = bf16[512,512]{1,0:T(8,128)(2,1)S(1)} collective-permute-done((bf16[512,512]{1,0:T(8,128)(2,1)S(1)}, bf16[512,512]{1,0:T(8,128)(2,1)S(1)}, u32[]{:S(2)}, u32[]{:S(2)}) %collective-permute-start.8) | collective-permute-done | bytes 524320 | tf_op jit(solution)/shard_map/ppermute | solution.py:19
  41.4 1.5 %collective-permute-start.13 = (bf16[512,512]{1,0:T(8,128)(2,1)S(1)}, bf16[512,512]{1,0:T(8,128)(2,1)S(1)}, u32[]{:S(2)}, u32[]{:S(2)}) collective-permute-start(bf16[512,512]{1,0:T(8,128)(2,1)S(1)} %shard_map.57.third.refs_10_), channel_id=1, source_target_pairs={{0,2},{2,0},{1,3},{3,1},{4,6},{6,4},{5,7},{7,5},{8,10},{10,8},{9,1... | collective-permute-start | bytes 1572872 | tf_op jit(solution)/shard_map/ppermute | solution.py:19
  42.9 1.3 %collective-permute-start.15 = (bf16[512,512]{1,0:T(8,128)(2,1)S(1)}, bf16[512,512]{1,0:T(8,128)(2,1)S(1)}, u32[]{:S(2)}, u32[]{:S(2)}) collective-permute-start(bf16[512,512]{1,0:T(8,128)(2,1)S(1)} %collective-permute-done.14.inner), channel_id=1, source_target_pairs={{4,0},{8,12},{5,1},{9,13},{6,2},{10,14},{7,3},{11,15},{20,16},{24,... | collective-permute-start | bytes 1572872 | tf_op jit(solution)/shard_map/ppermute | solution.py:517
  44.2 1.0 %copy-done = bf16[512,512]{1,0:T(8,128)(2,1)S(1)} copy-done((bf16[512,512]{1,0:T(8,128)(2,1)S(1)}, bf16[512,512]{1,0:T(8,128)(2,1)}, u32[]{:S(2)}) %copy-start) | copy-done | bytes 524312
  45.3 1.0 %shard_map.59.row = f32[8,512]{1,0:T(8,128)S(1)} custom-call(bf16[512,512]{1,0:T(8,128)(2,1)S(1)} %copy-done, bf16[512,512]{1,0:T(8,128)(2,1)S(1)} %collective-permute-done.6.second.refs_8_, bf16[512,512]{1,0:T(8,128)(2,1)S(1)} %shard_map.57.third.refs_10_), custom_call_target="tpu_custom_call" | custom-call | flops 1048576 | bytes 1589248 | tf_op jit(solution)/shard_map/pallas_call | solution.py:487
  46.3 4.2 %collective-permute-done.11.outer = bf16[512,512]{1,0:T(8,128)(2,1)S(1)} collective-permute-done((bf16[512,512]{1,0:T(8,128)(2,1)S(1)}, bf16[512,512]{1,0:T(8,128)(2,1)S(1)}, u32[]{:S(2)}, u32[]{:S(2)}) %collective-permute-start.11) | collective-permute-done | bytes 524320 | tf_op jit(solution)/shard_map/ppermute | solution.py:517
  50.7 1.3 %collective-permute-start.3 = (bf16[512,512]{1,0:T(8,128)(2,1)S(1)}, bf16[512,512]{1,0:T(8,128)(2,1)S(1)}, u32[]{:S(2)}, u32[]{:S(2)}) collective-permute-start(bf16[512,512]{1,0:T(8,128)(2,1)S(1)} %collective-permute-done.2.inner), channel_id=1, source_target_pairs={{4,0},{8,12},{5,1},{9,13},{6,2},{10,14},{7,3},{11,15},{20,16},{24,... | collective-permute-start | bytes 1572872 | tf_op jit(solution)/shard_map/ppermute | solution.py:517
  52.0 9.8 %collective-permute-done.15.outer = bf16[512,512]{1,0:T(8,128)(2,1)S(1)} collective-permute-done((bf16[512,512]{1,0:T(8,128)(2,1)S(1)}, bf16[512,512]{1,0:T(8,128)(2,1)S(1)}, u32[]{:S(2)}, u32[]{:S(2)}) %collective-permute-start.15) | collective-permute-done | bytes 524320 | tf_op jit(solution)/shard_map/ppermute | solution.py:517
  62.3 1.8 %collective-permute-start.18 = (bf16[528,512]{1,0:T(8,128)(2,1)S(1)}, bf16[528,512]{1,0:T(8,128)(2,1)S(1)}, u32[]{:S(2)}, u32[]{:S(2)}) collective-permute-start(bf16[528,512]{1,0:T(8,128)(2,1)S(1)} %shard_map.60.refs_7_.late_b), channel_id=1, source_target_pairs={{0,2},{2,0},{1,3},{3,1},{4,6},{6,4},{5,7},{7,5},{8,10},{10,8},{9,1... | collective-permute-start | bytes 1622024 | tf_op jit(solution)/shard_map/ppermute | solution.py:19
  64.1 4.1 %shard_map.61 = (f32[512,1024]{1,0:T(8,128)S(1)}, f32[512,1024]{1,0:T(8,128)S(1)}, f32[8,512]{1,0:T(8,128)S(1)}, bf16[512,512]{1,0:T(8,128)(2,1)S(1)}, bf16[512,512]{1,0:T(8,128)(2,1)S(1)}) custom-call(bf16[512,512]{1,0:T(8,128)(2,1)S(1)} %copy-done.2, bf16[512,512]{1,0:T(8,128)(2,1)S(1)} %collective-permute-done.refs_1_.refs_3_, ...), custom_call_target="tpu_custom_call" | custom-call | flops 3221225472 | bytes 11550720 | tf_op jit(solution)/shard_map/pallas_call | solution.py:487
  68.3 4.4 %collective-permute-done.3.outer = bf16[512,512]{1,0:T(8,128)(2,1)S(1)} collective-permute-done((bf16[512,512]{1,0:T(8,128)(2,1)S(1)}, bf16[512,512]{1,0:T(8,128)(2,1)S(1)}, u32[]{:S(2)}, u32[]{:S(2)}) %collective-permute-start.3) | collective-permute-done | bytes 524320 | tf_op jit(solution)/shard_map/ppermute | solution.py:517
  73.2 2.7 %collective-permute-done.18.late_b.refs_8_ = bf16[528,512]{1,0:T(8,128)(2,1)S(1)} collective-permute-done((bf16[528,512]{1,0:T(8,128)(2,1)S(1)}, bf16[528,512]{1,0:T(8,128)(2,1)S(1)}, u32[]{:S(2)}, u32[]{:S(2)}) %collective-permute-start.18) | collective-permute-done | bytes 540704 | tf_op jit(solution)/shard_map/ppermute | solution.py:19
  76.0 1.9 %shard_map.64 = (bf16[528,512]{1,0:T(8,128)(2,1)S(1)}, bf16[512,1024]{1,0:T(8,128)(2,1)S(1)}, f32[8,1024]{1,0:T(8,128)S(1)}) custom-call(f32[512,8]{1,0:T(8,128)S(1)} %get-tuple-element.58.columns, bf16[528,512]{1,0:T(8,128)(2,1)S(1)} %get-tuple-element.59.left_own, bf16[528,512]{1,0:T(8,128)(2,1)S(1)} %shard_map.62.late.late_own.refs_0_, ...), custom_call_target="tpu_custom_call" | custom-call | flops 1073741824 | bytes 6422528 | tf_op jit(solution)/shard_map/pallas_call | solution.py:487
  78.1 1.7 %collective-permute-start.21 = (bf16[528,512]{1,0:T(8,128)(2,1)S(1)}, bf16[528,512]{1,0:T(8,128)(2,1)S(1)}, u32[]{:S(2)}, u32[]{:S(2)}) collective-permute-start(bf16[528,512]{1,0:T(8,128)(2,1)S(1)} %get-tuple-element.68), channel_id=1, source_target_pairs={{0,2},{2,0},{1,3},{3,1},{4,6},{6,4},{5,7},{7,5},{8,10},{10,8},{9,1... | collective-permute-start | bytes 1622024 | tf_op jit(solution)/shard_map/ppermute | solution.py:19
  79.7 7.6 %shard_map.65 = (f32[512,512]{1,0:T(8,128)S(1)}, f32[512,512]{1,0:T(8,128)S(1)}, bf16[512,512]{1,0:T(8,128)(2,1)S(1)}, f32[256,1024]{1,0:T(8,128)}, f32[8,128]{1,0:T(8,128)S(1)}, /*index=5*/f32[8,128]{1,0:T(8,128)S(1)}) custom-call(s32[2]{0:T(128)S(1)} %pad_add_fusion.flags, bf16[528,512]{1,0:T(8,128)(2,1)S(1)} %shard_map.62.late.late_own.refs_0_, ...), custom_call_target="tpu_custom_call" | custom-call | flops 2147483648 | bytes 14295048 | tf_op jit(solution)/shard_map/pallas_call | solution.py:487
  87.9 1.4 %collective-permute-done.22.other = f32[8,128]{1,0:T(8,128)S(1)} collective-permute-done((f32[8,128]{1,0:T(8,128)S(1)}, f32[8,128]{1,0:T(8,128)S(1)}, u32[]{:S(2)}, u32[]{:S(2)}) %collective-permute-start.22) | collective-permute-done | bytes 4128 | tf_op jit(solution)/shard_map/ppermute | solution.py:19
  89.3 1.1 %collective-permute-start.23 = (f32[8,128]{1,0:T(8,128)S(1)}, f32[8,128]{1,0:T(8,128)S(1)}, u32[]{:S(2)}, u32[]{:S(2)}) collective-permute-start(f32[8,128]{1,0:T(8,128)S(1)} %shard_map.68.one), channel_id=1, source_target_pairs={{0,2},{2,0},{1,3},{3,1},{4,6},{6,4},{5,7},{7,5},{8,10},{10,8},{9,1... | collective-permute-start | bytes 12296 | tf_op jit(solution)/shard_map/ppermute | solution.py:19
  90.4 0.9 shard_map.66
  91.3 1.5 %collective-permute-done.21.from_x = bf16[528,512]{1,0:T(8,128)(2,1)S(1)} collective-permute-done((bf16[528,512]{1,0:T(8,128)(2,1)S(1)}, bf16[528,512]{1,0:T(8,128)(2,1)S(1)}, u32[]{:S(2)}, u32[]{:S(2)}) %collective-permute-start.21) | collective-permute-done | bytes 540704 | tf_op jit(solution)/shard_map/ppermute | solution.py:19
  92.8 1.1 %shard_map.67 = bf16[512,512]{1,0:T(8,128)(2,1)} custom-call(f32[512,512]{1,0:T(8,128)S(1)} %get-tuple-element.67.right, bf16[528,512]{1,0:T(8,128)(2,1)S(1)} %collective-permute-done.21.from_x, bf16[528,512]{1,0:T(8,128)(2,1)S(1)} %shard_map.60.refs_7_.late_b, bf16[512,512]{1,0:T(8,128)(2,1)S(1)} %copy-done.1), custom_call_target="tpu_custom_call" | custom-call | flops 1048576 | bytes 3178496 | tf_op jit(solution)/shard_map/pallas_call | solution.py:487
  (37 shorter events, 4.0 us)
Async XLA Ops:
  0.6 9.9 %collective-permute-start = (bf16[512,512]{1,0:T(8,128)(2,1)}, bf16[512,512]{1,0:T(8,128)(2,1)S(1)}, u32[]{:S(2)}, u32[]{:S(2)}) collective-permute-start(bf16[512,512]{1,0:T(8,128)(2,1)} %refs_2_.1), channel_id=1, source_target_pairs={{0,1},{1,0},{2,3},{3,2},{4,5},{5,4},{6,7},{7,6},{8,9},{9,8},{10,11... | collective-permute-start | bytes 1572872 | tf_op jit(solution)/shard_map/ppermute | solution.py:19
  1.1 15.6 %collective-permute-start.1 = (bf16[512,512]{1,0:T(8,128)(2,1)}, bf16[512,512]{1,0:T(8,128)(2,1)S(1)}, u32[]{:S(2)}, u32[]{:S(2)}) collective-permute-start(bf16[512,512]{1,0:T(8,128)(2,1)} %refs_2_.1), channel_id=1, source_target_pairs={{0,4},{4,0},{8,12},{12,8},{1,5},{5,1},{9,13},{13,9},{2,6},{6,2},{1... | collective-permute-start | bytes 1572872 | tf_op jit(solution)/shard_map/ppermute | solution.py:517
  3.8 13.7 %collective-permute-start.4 = (bf16[512,512]{1,0:T(8,128)(2,1)}, bf16[512,512]{1,0:T(8,128)(2,1)S(1)}, u32[]{:S(2)}, u32[]{:S(2)}) collective-permute-start(bf16[512,512]{1,0:T(8,128)(2,1)} %first_b.1), channel_id=1, source_target_pairs={{4,8},{8,4},{5,9},{9,5},{6,10},{10,6},{7,11},{11,7},{20,24},{24,20... | collective-permute-start | bytes 1572872 | tf_op jit(solution)/shard_map/ppermute | solution.py:517
  4.5 14.4 %collective-permute-start.7 = (bf16[512,512]{1,0:T(8,128)(2,1)}, bf16[512,512]{1,0:T(8,128)(2,1)S(1)}, u32[]{:S(2)}, u32[]{:S(2)}) collective-permute-start(bf16[512,512]{1,0:T(8,128)(2,1)} %first_b.1), channel_id=1, source_target_pairs={{0,2},{2,0},{1,3},{3,1},{4,6},{6,4},{5,7},{7,5},{8,10},{10,8},{9,1... | collective-permute-start | bytes 1572872 | tf_op jit(solution)/shard_map/ppermute | solution.py:19
  6.0 22.0 %collective-permute-start.6 = (bf16[512,512]{1,0:T(8,128)(2,1)}, bf16[512,512]{1,0:T(8,128)(2,1)S(1)}, u32[]{:S(2)}, u32[]{:S(2)}) collective-permute-start(bf16[512,512]{1,0:T(8,128)(2,1)} %first_b.1), channel_id=1, source_target_pairs={{0,4},{4,0},{8,12},{12,8},{1,5},{5,1},{9,13},{13,9},{2,6},{6,2},{1... | collective-permute-start | bytes 1572872 | tf_op jit(solution)/shard_map/ppermute | solution.py:517
  16.8 13.8 %collective-permute-start.10 = (bf16[512,512]{1,0:T(8,128)(2,1)}, bf16[512,512]{1,0:T(8,128)(2,1)S(1)}, u32[]{:S(2)}, u32[]{:S(2)}) collective-permute-start(bf16[512,512]{1,0:T(8,128)(2,1)} %refs_2_.1), channel_id=1, source_target_pairs={{4,8},{8,4},{5,9},{9,5},{6,10},{10,6},{7,11},{11,7},{20,24},{24,20... | collective-permute-start | bytes 1572872 | tf_op jit(solution)/shard_map/ppermute | solution.py:517
  17.5 21.8 %collective-permute-start.5 = (bf16[512,512]{1,0:T(8,128)(2,1)S(1)}, bf16[512,512]{1,0:T(8,128)(2,1)S(1)}, u32[]{:S(2)}, u32[]{:S(2)}) collective-permute-start(bf16[512,512]{1,0:T(8,128)(2,1)S(1)} %collective-permute-done.4.inner), channel_id=1, source_target_pairs={{4,0},{8,12},{5,1},{9,13},{6,2},{10,14},{7,3},{11,15},{20,16},{24,... | collective-permute-start | bytes 1572872 | tf_op jit(solution)/shard_map/ppermute | solution.py:517
  18.8 21.3 %collective-permute-start.9 = (bf16[512,512]{1,0:T(8,128)(2,1)S(1)}, bf16[512,512]{1,0:T(8,128)(2,1)S(1)}, u32[]{:S(2)}, u32[]{:S(2)}) collective-permute-start(bf16[512,512]{1,0:T(8,128)(2,1)S(1)} %collective-permute-done.1.refs_2_), channel_id=1, source_target_pairs={{0,1},{1,0},{2,3},{3,2},{4,5},{5,4},{6,7},{7,6},{8,9},{9,8},{10,11... | collective-permute-start | bytes 1572872 | tf_op jit(solution)/shard_map/ppermute | solution.py:19
  28.0 13.4 %collective-permute-start.8 = (bf16[512,512]{1,0:T(8,128)(2,1)S(1)}, bf16[512,512]{1,0:T(8,128)(2,1)S(1)}, u32[]{:S(2)}, u32[]{:S(2)}) collective-permute-start(bf16[512,512]{1,0:T(8,128)(2,1)S(1)} %collective-permute-done.6.second.refs_8_), channel_id=1, source_target_pairs={{0,2},{2,0},{1,3},{3,1},{4,6},{6,4},{5,7},{7,5},{8,10},{10,8},{9,1... | collective-permute-start | bytes 1572872 | tf_op jit(solution)/shard_map/ppermute | solution.py:19
  29.9 13.0 %collective-permute-start.14 = (bf16[512,512]{1,0:T(8,128)(2,1)S(1)}, bf16[512,512]{1,0:T(8,128)(2,1)S(1)}, u32[]{:S(2)}, u32[]{:S(2)}) collective-permute-start(bf16[512,512]{1,0:T(8,128)(2,1)S(1)} %collective-permute-done.6.second.refs_8_), channel_id=1, source_target_pairs={{4,8},{8,4},{5,9},{9,5},{6,10},{10,6},{7,11},{11,7},{20,24},{24,20... | collective-permute-start | bytes 1572872 | tf_op jit(solution)/shard_map/ppermute | solution.py:517
  30.6 19.9 %collective-permute-start.11 = (bf16[512,512]{1,0:T(8,128)(2,1)S(1)}, bf16[512,512]{1,0:T(8,128)(2,1)S(1)}, u32[]{:S(2)}, u32[]{:S(2)}) collective-permute-start(bf16[512,512]{1,0:T(8,128)(2,1)S(1)} %collective-permute-done.10.inner), channel_id=1, source_target_pairs={{4,0},{8,12},{5,1},{9,13},{6,2},{10,14},{7,3},{11,15},{20,16},{24,... | collective-permute-start | bytes 1572872 | tf_op jit(solution)/shard_map/ppermute | solution.py:517
  39.3 11.4 %collective-permute-start.2 = (bf16[512,512]{1,0:T(8,128)(2,1)S(1)}, bf16[512,512]{1,0:T(8,128)(2,1)S(1)}, u32[]{:S(2)}, u32[]{:S(2)}) collective-permute-start(bf16[512,512]{1,0:T(8,128)(2,1)S(1)} %collective-permute-done.1.refs_2_), channel_id=1, source_target_pairs={{4,8},{8,4},{5,9},{9,5},{6,10},{10,6},{7,11},{11,7},{20,24},{24,20... | collective-permute-start | bytes 1572872 | tf_op jit(solution)/shard_map/ppermute | solution.py:517
  39.9 24.1 %copy-start.1 = (bf16[512,512]{1,0:T(8,128)(2,1)S(1)}, bf16[512,512]{1,0:T(8,128)(2,1)}, u32[]{:S(2)}) copy-start(bf16[512,512]{1,0:T(8,128)(2,1)} %first_b.1) | copy-start | bytes 1572868
  40.0 24.1 %copy-start.2 = (bf16[512,512]{1,0:T(8,128)(2,1)S(1)}, bf16[512,512]{1,0:T(8,128)(2,1)}, u32[]{:S(2)}) copy-start(bf16[512,512]{1,0:T(8,128)(2,1)} %refs_2_.1) | copy-start | bytes 1572868
  41.4 22.6 %collective-permute-start.13 = (bf16[512,512]{1,0:T(8,128)(2,1)S(1)}, bf16[512,512]{1,0:T(8,128)(2,1)S(1)}, u32[]{:S(2)}, u32[]{:S(2)}) collective-permute-start(bf16[512,512]{1,0:T(8,128)(2,1)S(1)} %shard_map.57.third.refs_10_), channel_id=1, source_target_pairs={{0,2},{2,0},{1,3},{3,1},{4,6},{6,4},{5,7},{7,5},{8,10},{10,8},{9,1... | collective-permute-start | bytes 1572872 | tf_op jit(solution)/shard_map/ppermute | solution.py:19
  42.9 18.9 %collective-permute-start.15 = (bf16[512,512]{1,0:T(8,128)(2,1)S(1)}, bf16[512,512]{1,0:T(8,128)(2,1)S(1)}, u32[]{:S(2)}, u32[]{:S(2)}) collective-permute-start(bf16[512,512]{1,0:T(8,128)(2,1)S(1)} %collective-permute-done.14.inner), channel_id=1, source_target_pairs={{4,0},{8,12},{5,1},{9,13},{6,2},{10,14},{7,3},{11,15},{20,16},{24,... | collective-permute-start | bytes 1572872 | tf_op jit(solution)/shard_map/ppermute | solution.py:517
  44.2 1.0 %copy-start = (bf16[512,512]{1,0:T(8,128)(2,1)S(1)}, bf16[512,512]{1,0:T(8,128)(2,1)}, u32[]{:S(2)}) copy-start(bf16[512,512]{1,0:T(8,128)(2,1)} %first_b.1) | copy-start | bytes 1572868
  50.6 13.5 %collective-permute-start.12 = (bf16[512,512]{1,0:T(8,128)(2,1)S(1)}, bf16[512,512]{1,0:T(8,128)(2,1)S(1)}, u32[]{:S(2)}, u32[]{:S(2)}) collective-permute-start(bf16[512,512]{1,0:T(8,128)(2,1)S(1)} %shard_map.58.refs_4_), channel_id=1, source_target_pairs={{0,1},{1,0},{2,3},{3,2},{4,5},{5,4},{6,7},{7,6},{8,9},{9,8},{10,11... | collective-permute-start | bytes 1572872 | tf_op jit(solution)/shard_map/ppermute | solution.py:19
  50.7 22.0 %collective-permute-start.3 = (bf16[512,512]{1,0:T(8,128)(2,1)S(1)}, bf16[512,512]{1,0:T(8,128)(2,1)S(1)}, u32[]{:S(2)}, u32[]{:S(2)}) collective-permute-start(bf16[512,512]{1,0:T(8,128)(2,1)S(1)} %collective-permute-done.2.inner), channel_id=1, source_target_pairs={{4,0},{8,12},{5,1},{9,13},{6,2},{10,14},{7,3},{11,15},{20,16},{24,... | collective-permute-start | bytes 1572872 | tf_op jit(solution)/shard_map/ppermute | solution.py:517
  62.3 13.6 %collective-permute-start.18 = (bf16[528,512]{1,0:T(8,128)(2,1)S(1)}, bf16[528,512]{1,0:T(8,128)(2,1)S(1)}, u32[]{:S(2)}, u32[]{:S(2)}) collective-permute-start(bf16[528,512]{1,0:T(8,128)(2,1)S(1)} %shard_map.60.refs_7_.late_b), channel_id=1, source_target_pairs={{0,2},{2,0},{1,3},{3,1},{4,6},{6,4},{5,7},{7,5},{8,10},{10,8},{9,1... | collective-permute-start | bytes 1622024 | tf_op jit(solution)/shard_map/ppermute | solution.py:19
  68.2 4.5 %collective-permute-start.16 = (f32[8,512]{1,0:T(8,128)S(1)}, f32[8,512]{1,0:T(8,128)S(1)}, u32[]{:S(2)}, u32[]{:S(2)}) collective-permute-start(f32[8,512]{1,0:T(8,128)S(1)} %get-tuple-element.53), channel_id=1, source_target_pairs={{0,1},{1,0},{2,3},{3,2},{4,5},{5,4},{6,7},{7,6},{8,9},{9,8},{10,11... | collective-permute-start | bytes 49160 | tf_op jit(solution)/shard_map/ppermute | solution.py:19
  73.1 2.9 %collective-permute-start.17 = (bf16[528,512]{1,0:T(8,128)(2,1)S(1)}, bf16[528,512]{1,0:T(8,128)(2,1)S(1)}, u32[]{:S(2)}, u32[]{:S(2)}) collective-permute-start(bf16[528,512]{1,0:T(8,128)(2,1)S(1)} %shard_map.62.late.late_own.refs_0_), channel_id=1, source_target_pairs={{0,1},{1,0},{2,3},{3,2},{4,5},{5,4},{6,7},{7,6},{8,9},{9,8},{10,11... | collective-permute-start | bytes 1622024 | tf_op jit(solution)/shard_map/ppermute | solution.py:19
  78.0 1.8 %collective-permute-start.19 = (f32[8,1024]{1,0:T(8,128)S(1)}, f32[8,1024]{1,0:T(8,128)S(1)}, u32[]{:S(2)}, u32[]{:S(2)}) collective-permute-start(f32[8,1024]{1,0:T(8,128)S(1)} %get-tuple-element.62.refs_13_), channel_id=1, source_target_pairs={{0,1},{1,0},{2,3},{3,2},{4,5},{5,4},{6,7},{7,6},{8,9},{9,8},{10,11... | collective-permute-start | bytes 98312 | tf_op jit(solution)/shard_map/ppermute | solution.py:19
  78.1 14.7 %collective-permute-start.21 = (bf16[528,512]{1,0:T(8,128)(2,1)S(1)}, bf16[528,512]{1,0:T(8,128)(2,1)S(1)}, u32[]{:S(2)}, u32[]{:S(2)}) collective-permute-start(bf16[528,512]{1,0:T(8,128)(2,1)S(1)} %get-tuple-element.68), channel_id=1, source_target_pairs={{0,2},{2,0},{1,3},{3,1},{4,6},{6,4},{5,7},{7,5},{8,10},{10,8},{9,1... | collective-permute-start | bytes 1622024 | tf_op jit(solution)/shard_map/ppermute | solution.py:19
  87.4 3.0 %collective-permute-start.20 = (bf16[512,512]{1,0:T(8,128)(2,1)S(1)}, bf16[512,512]{1,0:T(8,128)(2,1)S(1)}, u32[]{:S(2)}, u32[]{:S(2)}) collective-permute-start(bf16[512,512]{1,0:T(8,128)(2,1)S(1)} %get-tuple-element.65), channel_id=1, source_target_pairs={{0,1},{1,0},{2,3},{3,2},{4,5},{5,4},{6,7},{7,6},{8,9},{9,8},{10,11... | collective-permute-start | bytes 1572872 | tf_op jit(solution)/shard_map/ppermute | solution.py:19
  87.5 1.8 %collective-permute-start.22 = (f32[8,128]{1,0:T(8,128)S(1)}, f32[8,128]{1,0:T(8,128)S(1)}, u32[]{:S(2)}, u32[]{:S(2)}) collective-permute-start(f32[8,128]{1,0:T(8,128)S(1)} %get-tuple-element.70), channel_id=1, source_target_pairs={{0,1},{1,0},{2,3},{3,2},{4,5},{5,4},{6,7},{7,6},{8,9},{9,8},{10,11... | collective-permute-start | bytes 12296 | tf_op jit(solution)/shard_map/ppermute | solution.py:19
  89.3 4.6 %collective-permute-start.23 = (f32[8,128]{1,0:T(8,128)S(1)}, f32[8,128]{1,0:T(8,128)S(1)}, u32[]{:S(2)}, u32[]{:S(2)}) collective-permute-start(f32[8,128]{1,0:T(8,128)S(1)} %shard_map.68.one), channel_id=1, source_target_pairs={{0,2},{2,0},{1,3},{3,1},{4,6},{6,4},{5,7},{7,5},{8,10},{10,8},{9,1... | collective-permute-start | bytes 12296 | tf_op jit(solution)/shard_map/ppermute | solution.py:19

commit v12 on v11

--- a/solution.py
+++ b/solution.py
@@ -312,7 +312,7 @@
 
 
 def partner_kernel(columns, left_own, late_own, late_other, zero_other, sums, late_b, *refs):
-    partial_out, e_out, vec_out, left_other = refs
+    partial_out, e_out, vec_out, left_other, terms_own = refs
     rows, quart = zero_other.shape
     width = quart // 2
     scale_col, delta_col = columns[:, 0:1], columns[:, 1:2]
@@ -329,13 +329,16 @@
             square = corr * corr
             across = across + fold_lanes(square)
             vec_out[:, wide] = rows_of([off_weight * jnp.sum(square, axis=0, keepdims=True)])
+        if part == 0:
+            for tile in range(2):
+                at = slice(tile * width, (tile + 1) * width)
+                terms_own[:, at] = dot_rows(left_own[...], e_out[at, :quart])
     nothing = jnp.zeros((1, quart), jnp.float32)
     second = off_weight * lanes_to_row(across)
     partial_out[rows:, :] = split_rows([second, nothing, nothing, nothing])
     for tile in range(2):
         at = slice(tile * width, (tile + 1) * width)
-        terms = dot_rows(left_own[...], e_out[at, :quart])
-        terms = terms + dot_rows(left_other[...], e_out[at, quart:])
+        terms = terms_own[:, at] + dot_rows(left_other[...], e_out[at, quart:])
         partial_out[:rows, at] = without_extra(terms, rows).astype(jnp.bfloat16)
 
 
@@ -452,10 +455,6 @@
     out[...] = one[...] + other[...]
 
 
-def loss_kernel(feats, one, other, out):
-    out[0] = (one[0, 0] + other[0, 0]) / feats
-
-
 def left_final_kernel(left, from_core, left_out):
     for at in range(0, left.shape[0], 64):
         piece = slice(at, at + 64)
@@ -463,22 +462,34 @@
         left_out[piece, :] = value.astype(jnp.bfloat16)
 
 
-def right_final_kernel(right, from_x, late_b, first_b, right_out):
+def right_final_kernel(feats, right, from_x, late_b, first_b, loss, x_loss, right_out, loss_out, made, sems):
     rows, quart = right.shape
     offset, rstd, _, _ = joined_rows(late_b, quart)
     second = joined_rows(from_x, rows)[0]
-    for at in range(0, rows, 64):
-        piece = slice(at, at + 64)
-        xhat = (first_b[piece, :].astype(jnp.float32) - offset) * rstd
-        value = right[piece, :] + from_x[piece, :].astype(jnp.float32) - xhat * second
-        right_out[piece, :] = (rstd * value).astype(jnp.bfloat16)
+    step = rows // 4
+    sent = []
+    for part in range(4):
+        for at in range(part * step, (part + 1) * step, 64):
+            piece = slice(at, at + 64)
+            xhat = (first_b[piece, :].astype(jnp.float32) - offset) * rstd
+            value = right[piece, :] + from_x[piece, :].astype(jnp.float32) - xhat * second
+            made[piece, :] = (rstd * value).astype(jnp.bfloat16)
+        piece = pl.ds(part * step, step)
+        sent.append(
+            pltpu.make_async_copy(made.at[piece, :], right_out.at[piece, :], sems.at[part])
+        )
+        sent[-1].start()
+    loss_out[0] = (loss[0, 0] + x_loss[0, 0]) / feats
+    for copy in sent:
+        copy.wait()
 
 
 vmem = pl.BlockSpec(memory_space=pltpu.VMEM)
 smem = pl.BlockSpec(memory_space=pltpu.SMEM)
-
-
-def local_call(kernel, operands, outs, scratch=(), flops=2**20, room=8, held=()):
+hbm = pl.BlockSpec(memory_space=pltpu.HBM)
+
+
+def local_call(kernel, operands, outs, scratch=(), flops=2**20, room=8, held=(), sent=()):
     moved = sum(x.size * x.dtype.itemsize for x in (*operands, *outs))
 
     def space(x):
@@ -486,9 +497,9 @@
 
     return pl.pallas_call(
         kernel,
-        out_shape=list(outs),
+        out_shape=[pltpu.HBM(x.shape, x.dtype) if i in sent else x for i, x in enumerate(outs)],
         in_specs=[space(x) for x in operands],
-        out_specs=[space(x) for x in outs],
+        out_specs=[hbm if i in sent else space(x) for i, x in enumerate(outs)],
         scratch_shapes=list(scratch),
         compiler_params=pltpu.CompilerParams(vmem_limit_bytes=room * 2**20),
         cost_estimate=pl.CostEstimate(flops=flops, bytes_accessed=moved, transcendentals=0),
@@ -609,7 +620,7 @@
             jax.ShapeDtypeStruct((quart, half), jnp.bfloat16),
             jax.ShapeDtypeStruct((8, half), jnp.float32),
         ),
-        [low(rows + 16, quart)],
+        [low(rows + 16, quart), pltpu.VMEM((rows + 16, quart), jnp.float32)],
         4 * gemm,
         room=16,
     )
@@ -644,14 +655,12 @@
     x_loss = x_swap(loss)
     (left_gradient,) = local_call(left_final_kernel, (left_own, from_core), (quarter_bf16,))
     right_own, left_gradient = after(right_own, left_gradient)
-    (right_gradient,) = local_call(
-        right_final_kernel, (right_own, from_x, late_b, right_outputs), (quarter_bf16,)
-    )
-    right_gradient, x_loss = after(right_gradient, x_loss)
-    (loss,) = local_call(
-        functools.partial(loss_kernel, feats),
-        (loss, x_loss),
-        (jax.ShapeDtypeStruct((1,), jnp.float32),),
+    right_gradient, loss = local_call(
+        functools.partial(right_final_kernel, feats),
+        (right_own, from_x, late_b, right_outputs, loss, x_loss),
+        (quarter_bf16, jax.ShapeDtypeStruct((1,), jnp.float32)),
+        [low(rows, quart), pltpu.SemaphoreType.DMA((4,))],
+        sent=(0,),
     )
     return (left_gradient, right_gradient, mine[None, :, :], loss)
 

time: 94.9 us -> 95 us (level)
    pallas_call x13 -> x12, Pallas kernels: 18.5 us -> 18.4 us  [local_call(): pl.pallas_call(kernel, out_shape=[pltpu.HBM(x.shape, x.dtype) if i in sen...]
  transfers between devices with their start and end apart: 24 -> 24, of which waited for: 10 -> 10; matrix products, arithmetic and copies ran while one was open for 0% -> 0% of each run, Pallas kernels for 17% -> 16%
where the time goes in v12:
time: 95 us; the launch traced here: 94.7 us
  waiting for transfers between devices  48.3 us (51%)
  starting transfers between devices  25.8 us (27%)
  Pallas kernels  18.4 us (19%)
  local copies, waits for them, and re-layouts  1.05 us (1%)
  between operations  1.03 us (1%)
    ppermute x10, waiting for transfers between devices, along(): return lax.ppermute(block, 'dp', route)  41.3 us
    pallas_call x12, Pallas kernels, local_call(): pl.pallas_call(kernel, out_shape=[pltpu.HBM(x.shape, x.dtype) if i in sen...  18.4 us
    ppermute x10, starting transfers between devices, along(): return lax.ppermute(block, 'dp', route)  14.9 us
    ppermute x14, starting transfers between devices, swapped(): return lax.ppermute(block, axis, route)  10.9 us
    ppermute x14, waiting for transfers between devices, swapped(): return lax.ppermute(block, axis, route)  6.99 us
  transfers between devices with their start and end apart: 24, of which 10 were waited for; matrix products, arithmetic and copies ran while one was open for 0% of the time, Pallas kernels for 16%

profile of v12, /device:TPU:0, one launch (start us, length us, event | category | flops | bytes accessed | tf_op | source)
XLA Modules:
  0.0 94.7 jit_solution(12593315210279347014)
XLA Ops:
  1.1 2.7 %collective-permute-start.1 = (bf16[512,512]{1,0:T(8,128)(2,1)}, bf16[512,512]{1,0:T(8,128)(2,1)S(1)}, u32[]{:S(2)}, u32[]{:S(2)}) collective-permute-start(bf16[512,512]{1,0:T(8,128)(2,1)} %refs_2_.1), channel_id=1, source_target_pairs={{0,4},{4,0},{8,12},{12,8},{1,5},{5,1},{9,13},{13,9},{2,6},{6,2},{1... | collective-permute-start | bytes 1572872 | tf_op jit(solution)/shard_map/ppermute | solution.py:528
  3.8 0.7 collective-permute-start.4
  4.5 1.6 %collective-permute-start.7 = (bf16[512,512]{1,0:T(8,128)(2,1)}, bf16[512,512]{1,0:T(8,128)(2,1)S(1)}, u32[]{:S(2)}, u32[]{:S(2)}) collective-permute-start(bf16[512,512]{1,0:T(8,128)(2,1)} %first_b.1), channel_id=1, source_target_pairs={{0,2},{2,0},{1,3},{3,1},{4,6},{6,4},{5,7},{7,5},{8,10},{10,8},{9,1... | collective-permute-start | bytes 1572872 | tf_op jit(solution)/shard_map/ppermute | solution.py:19
  6.0 4.4 %collective-permute-start.6 = (bf16[512,512]{1,0:T(8,128)(2,1)}, bf16[512,512]{1,0:T(8,128)(2,1)S(1)}, u32[]{:S(2)}, u32[]{:S(2)}) collective-permute-start(bf16[512,512]{1,0:T(8,128)(2,1)} %first_b.1), channel_id=1, source_target_pairs={{0,4},{4,0},{8,12},{12,8},{1,5},{5,1},{9,13},{13,9},{2,6},{6,2},{1... | collective-permute-start | bytes 1572872 | tf_op jit(solution)/shard_map/ppermute | solution.py:528
  10.5 6.3 %collective-permute-done.1.refs_2_ = bf16[512,512]{1,0:T(8,128)(2,1)S(1)} collective-permute-done((bf16[512,512]{1,0:T(8,128)(2,1)}, bf16[512,512]{1,0:T(8,128)(2,1)S(1)}, u32[]{:S(2)}, u32[]{:S(2)}) %collective-permute-start.1) | collective-permute-done | bytes 524320 | tf_op jit(solution)/shard_map/ppermute | solution.py:528
  16.8 0.7 collective-permute-start.10
  17.5 1.3 %collective-permute-start.5 = (bf16[512,512]{1,0:T(8,128)(2,1)S(1)}, bf16[512,512]{1,0:T(8,128)(2,1)S(1)}, u32[]{:S(2)}, u32[]{:S(2)}) collective-permute-start(bf16[512,512]{1,0:T(8,128)(2,1)S(1)} %collective-permute-done.4.inner), channel_id=1, source_target_pairs={{4,0},{8,12},{5,1},{9,13},{6,2},{10,14},{7,3},{11,15},{20,16},{24,... | collective-permute-start | bytes 1572872 | tf_op jit(solution)/shard_map/ppermute | solution.py:528
  18.9 9.1 %collective-permute-done.6.second.refs_8_ = bf16[512,512]{1,0:T(8,128)(2,1)S(1)} collective-permute-done((bf16[512,512]{1,0:T(8,128)(2,1)}, bf16[512,512]{1,0:T(8,128)(2,1)S(1)}, u32[]{:S(2)}, u32[]{:S(2)}) %collective-permute-start.6) | collective-permute-done | bytes 524320 | tf_op jit(solution)/shard_map/ppermute | solution.py:528
  28.0 1.9 %collective-permute-start.8 = (bf16[512,512]{1,0:T(8,128)(2,1)S(1)}, bf16[512,512]{1,0:T(8,128)(2,1)S(1)}, u32[]{:S(2)}, u32[]{:S(2)}) collective-permute-start(bf16[512,512]{1,0:T(8,128)(2,1)S(1)} %collective-permute-done.6.second.refs_8_), channel_id=1, source_target_pairs={{0,2},{2,0},{1,3},{3,1},{4,6},{6,4},{5,7},{7,5},{8,10},{10,8},{9,1... | collective-permute-start | bytes 1572872 | tf_op jit(solution)/shard_map/ppermute | solution.py:19
  30.6 1.3 %collective-permute-start.11 = (bf16[512,512]{1,0:T(8,128)(2,1)S(1)}, bf16[512,512]{1,0:T(8,128)(2,1)S(1)}, u32[]{:S(2)}, u32[]{:S(2)}) collective-permute-start(bf16[512,512]{1,0:T(8,128)(2,1)S(1)} %collective-permute-done.10.inner), channel_id=1, source_target_pairs={{4,0},{8,12},{5,1},{9,13},{6,2},{10,14},{7,3},{11,15},{20,16},{24,... | collective-permute-start | bytes 1572872 | tf_op jit(solution)/shard_map/ppermute | solution.py:528
  31.9 7.4 %collective-permute-done.5.outer = bf16[512,512]{1,0:T(8,128)(2,1)S(1)} collective-permute-done((bf16[512,512]{1,0:T(8,128)(2,1)S(1)}, bf16[512,512]{1,0:T(8,128)(2,1)S(1)}, u32[]{:S(2)}, u32[]{:S(2)}) %collective-permute-start.5) | collective-permute-done | bytes 524320 | tf_op jit(solution)/shard_map/ppermute | solution.py:528
  39.3 0.7 collective-permute-start.2
  40.1 1.3 %collective-permute-done.8.refs_9_ = bf16[512,512]{1,0:T(8,128)(2,1)S(1)} collective-permute-done((bf16[512,512]{1,0:T(8,128)(2,1)S(1)}, bf16[512,512]{1,0:T(8,128)(2,1)S(1)}, u32[]{:S(2)}, u32[]{:S(2)}) %collective-permute-start.8) | collective-permute-done | bytes 524320 | tf_op jit(solution)/shard_map/ppermute | solution.py:19
  41.4 1.5 %collective-permute-start.13 = (bf16[512,512]{1,0:T(8,128)(2,1)S(1)}, bf16[512,512]{1,0:T(8,128)(2,1)S(1)}, u32[]{:S(2)}, u32[]{:S(2)}) collective-permute-start(bf16[512,512]{1,0:T(8,128)(2,1)S(1)} %shard_map.57.third.refs_10_), channel_id=1, source_target_pairs={{0,2},{2,0},{1,3},{3,1},{4,6},{6,4},{5,7},{7,5},{8,10},{10,8},{9,1... | collective-permute-start | bytes 1572872 | tf_op jit(solution)/shard_map/ppermute | solution.py:19
  42.9 1.3 %collective-permute-start.15 = (bf16[512,512]{1,0:T(8,128)(2,1)S(1)}, bf16[512,512]{1,0:T(8,128)(2,1)S(1)}, u32[]{:S(2)}, u32[]{:S(2)}) collective-permute-start(bf16[512,512]{1,0:T(8,128)(2,1)S(1)} %collective-permute-done.14.inner), channel_id=1, source_target_pairs={{4,0},{8,12},{5,1},{9,13},{6,2},{10,14},{7,3},{11,15},{20,16},{24,... | collective-permute-start | bytes 1572872 | tf_op jit(solution)/shard_map/ppermute | solution.py:528
  44.2 1.0 %copy-done = bf16[512,512]{1,0:T(8,128)(2,1)S(1)} copy-done((bf16[512,512]{1,0:T(8,128)(2,1)S(1)}, bf16[512,512]{1,0:T(8,128)(2,1)}, u32[]{:S(2)}) %copy-start) | copy-done | bytes 524312
  45.3 1.0 %shard_map.59.row = f32[8,512]{1,0:T(8,128)S(1)} custom-call(bf16[512,512]{1,0:T(8,128)(2,1)S(1)} %copy-done, bf16[512,512]{1,0:T(8,128)(2,1)S(1)} %collective-permute-done.6.second.refs_8_, bf16[512,512]{1,0:T(8,128)(2,1)S(1)} %shard_map.57.third.refs_10_), custom_call_target="tpu_custom_call" | custom-call | flops 1048576 | bytes 1589248 | tf_op jit(solution)/shard_map/pallas_call | solution.py:498
  46.3 4.2 %collective-permute-done.11.outer = bf16[512,512]{1,0:T(8,128)(2,1)S(1)} collective-permute-done((bf16[512,512]{1,0:T(8,128)(2,1)S(1)}, bf16[512,512]{1,0:T(8,128)(2,1)S(1)}, u32[]{:S(2)}, u32[]{:S(2)}) %collective-permute-start.11) | collective-permute-done | bytes 524320 | tf_op jit(solution)/shard_map/ppermute | solution.py:528
  50.7 1.3 %collective-permute-start.3 = (bf16[512,512]{1,0:T(8,128)(2,1)S(1)}, bf16[512,512]{1,0:T(8,128)(2,1)S(1)}, u32[]{:S(2)}, u32[]{:S(2)}) collective-permute-start(bf16[512,512]{1,0:T(8,128)(2,1)S(1)} %collective-permute-done.2.inner), channel_id=1, source_target_pairs={{4,0},{8,12},{5,1},{9,13},{6,2},{10,14},{7,3},{11,15},{20,16},{24,... | collective-permute-start | bytes 1572872 | tf_op jit(solution)/shard_map/ppermute | solution.py:528
  52.0 9.8 %collective-permute-done.15.outer = bf16[512,512]{1,0:T(8,128)(2,1)S(1)} collective-permute-done((bf16[512,512]{1,0:T(8,128)(2,1)S(1)}, bf16[512,512]{1,0:T(8,128)(2,1)S(1)}, u32[]{:S(2)}, u32[]{:S(2)}) %collective-permute-start.15) | collective-permute-done | bytes 524320 | tf_op jit(solution)/shard_map/ppermute | solution.py:528
  62.3 1.8 %collective-permute-start.18 = (bf16[528,512]{1,0:T(8,128)(2,1)S(1)}, bf16[528,512]{1,0:T(8,128)(2,1)S(1)}, u32[]{:S(2)}, u32[]{:S(2)}) collective-permute-start(bf16[528,512]{1,0:T(8,128)(2,1)S(1)} %shard_map.60.refs_7_.late_b), channel_id=1, source_target_pairs={{0,2},{2,0},{1,3},{3,1},{4,6},{6,4},{5,7},{7,5},{8,10},{10,8},{9,1... | collective-permute-start | bytes 1622024 | tf_op jit(solution)/shard_map/ppermute | solution.py:19
  64.1 4.1 %shard_map.61 = (f32[512,1024]{1,0:T(8,128)S(1)}, f32[512,1024]{1,0:T(8,128)S(1)}, f32[8,512]{1,0:T(8,128)S(1)}, bf16[512,512]{1,0:T(8,128)(2,1)S(1)}, bf16[512,512]{1,0:T(8,128)(2,1)S(1)}) custom-call(bf16[512,512]{1,0:T(8,128)(2,1)S(1)} %copy-done.2, bf16[512,512]{1,0:T(8,128)(2,1)S(1)} %collective-permute-done.refs_1_.refs_3_, ...), custom_call_target="tpu_custom_call" | custom-call | flops 3221225472 | bytes 11550720 | tf_op jit(solution)/shard_map/pallas_call | solution.py:498
  68.3 4.4 %collective-permute-done.3.outer = bf16[512,512]{1,0:T(8,128)(2,1)S(1)} collective-permute-done((bf16[512,512]{1,0:T(8,128)(2,1)S(1)}, bf16[512,512]{1,0:T(8,128)(2,1)S(1)}, u32[]{:S(2)}, u32[]{:S(2)}) %collective-permute-start.3) | collective-permute-done | bytes 524320 | tf_op jit(solution)/shard_map/ppermute | solution.py:528
  73.2 2.7 %collective-permute-done.18.late_b.refs_8_ = bf16[528,512]{1,0:T(8,128)(2,1)S(1)} collective-permute-done((bf16[528,512]{1,0:T(8,128)(2,1)S(1)}, bf16[528,512]{1,0:T(8,128)(2,1)S(1)}, u32[]{:S(2)}, u32[]{:S(2)}) %collective-permute-start.18) | collective-permute-done | bytes 540704 | tf_op jit(solution)/shard_map/ppermute | solution.py:19
  76.0 2.0 %shard_map.64 = (bf16[528,512]{1,0:T(8,128)(2,1)S(1)}, bf16[512,1024]{1,0:T(8,128)(2,1)S(1)}, f32[8,1024]{1,0:T(8,128)S(1)}) custom-call(f32[512,8]{1,0:T(8,128)S(1)} %get-tuple-element.58.columns, bf16[528,512]{1,0:T(8,128)(2,1)S(1)} %get-tuple-element.59.left_own, bf16[528,512]{1,0:T(8,128)(2,1)S(1)} %shard_map.62.late.late_own.refs_0_, ...), custom_call_target="tpu_custom_call" | custom-call | flops 1073741824 | bytes 6422528 | tf_op jit(solution)/shard_map/pallas_call | solution.py:498
  78.1 1.7 %collective-permute-start.21 = (bf16[528,512]{1,0:T(8,128)(2,1)S(1)}, bf16[528,512]{1,0:T(8,128)(2,1)S(1)}, u32[]{:S(2)}, u32[]{:S(2)}) collective-permute-start(bf16[528,512]{1,0:T(8,128)(2,1)S(1)} %get-tuple-element.68), channel_id=1, source_target_pairs={{0,2},{2,0},{1,3},{3,1},{4,6},{6,4},{5,7},{7,5},{8,10},{10,8},{9,1... | collective-permute-start | bytes 1622024 | tf_op jit(solution)/shard_map/ppermute | solution.py:19
  79.8 7.6 %shard_map.65 = (f32[512,512]{1,0:T(8,128)S(1)}, f32[512,512]{1,0:T(8,128)S(1)}, bf16[512,512]{1,0:T(8,128)(2,1)S(1)}, f32[256,1024]{1,0:T(8,128)}, f32[8,128]{1,0:T(8,128)S(1)}, /*index=5*/f32[8,128]{1,0:T(8,128)S(1)}) custom-call(s32[2]{0:T(128)S(1)} %pad_add_fusion.flags, bf16[528,512]{1,0:T(8,128)(2,1)S(1)} %shard_map.62.late.late_own.refs_0_, ...), custom_call_target="tpu_custom_call" | custom-call | flops 2147483648 | bytes 14295048 | tf_op jit(solution)/shard_map/pallas_call | solution.py:498
  87.9 1.4 %collective-permute-done.22.other = f32[8,128]{1,0:T(8,128)S(1)} collective-permute-done((f32[8,128]{1,0:T(8,128)S(1)}, f32[8,128]{1,0:T(8,128)S(1)}, u32[]{:S(2)}, u32[]{:S(2)}) %collective-permute-start.22) | collective-permute-done | bytes 4128 | tf_op jit(solution)/shard_map/ppermute | solution.py:19
  89.3 1.1 %collective-permute-start.23 = (f32[8,128]{1,0:T(8,128)S(1)}, f32[8,128]{1,0:T(8,128)S(1)}, u32[]{:S(2)}, u32[]{:S(2)}) collective-permute-start(f32[8,128]{1,0:T(8,128)S(1)} %shard_map.67.loss), channel_id=1, source_target_pairs={{0,2},{2,0},{1,3},{3,1},{4,6},{6,4},{5,7},{7,5},{8,10},{10,8},{9,1... | collective-permute-start | bytes 12296 | tf_op jit(solution)/shard_map/ppermute | solution.py:19
  90.5 0.9 shard_map.66
  91.4 1.6 %collective-permute-done.23.x_loss = f32[8,128]{1,0:T(8,128)S(1)} collective-permute-done((f32[8,128]{1,0:T(8,128)S(1)}, f32[8,128]{1,0:T(8,128)S(1)}, u32[]{:S(2)}, u32[]{:S(2)}) %collective-permute-start.23) | collective-permute-done | bytes 4128 | tf_op jit(solution)/shard_map/ppermute | solution.py:19
  93.0 1.5 %shard_map.68 = (bf16[512,512]{1,0:T(8,128)(2,1)}, f32[1]{0:T(128)}) custom-call(f32[512,512]{1,0:T(8,128)S(1)} %get-tuple-element.67.right, bf16[528,512]{1,0:T(8,128)(2,1)S(1)} %collective-permute-done.21.from_x, bf16[528,512]{1,0:T(8,128)(2,1)S(1)} %shard_map.60.refs_7_.late_b, bf16[512,512]{1,0:T(8,128)(2,1)S(1)} %copy-done.1, ...), custom_call_target="tpu_custom_call" | custom-call | flops 1048576 | bytes 3186692 | tf_op jit(solution)/shard_map/pallas_call | solution.py:498
  (36 shorter events, 3.4 us)
Async XLA Ops:
  0.6 9.9 %collective-permute-start = (bf16[512,512]{1,0:T(8,128)(2,1)}, bf16[512,512]{1,0:T(8,128)(2,1)S(1)}, u32[]{:S(2)}, u32[]{:S(2)}) collective-permute-start(bf16[512,512]{1,0:T(8,128)(2,1)} %refs_2_.1), channel_id=1, source_target_pairs={{0,1},{1,0},{2,3},{3,2},{4,5},{5,4},{6,7},{7,6},{8,9},{9,8},{10,11... | collective-permute-start | bytes 1572872 | tf_op jit(solution)/shard_map/ppermute | solution.py:19
  1.1 15.6 %collective-permute-start.1 = (bf16[512,512]{1,0:T(8,128)(2,1)}, bf16[512,512]{1,0:T(8,128)(2,1)S(1)}, u32[]{:S(2)}, u32[]{:S(2)}) collective-permute-start(bf16[512,512]{1,0:T(8,128)(2,1)} %refs_2_.1), channel_id=1, source_target_pairs={{0,4},{4,0},{8,12},{12,8},{1,5},{5,1},{9,13},{13,9},{2,6},{6,2},{1... | collective-permute-start | bytes 1572872 | tf_op jit(solution)/shard_map/ppermute | solution.py:528
  3.8 13.7 %collective-permute-start.4 = (bf16[512,512]{1,0:T(8,128)(2,1)}, bf16[512,512]{1,0:T(8,128)(2,1)S(1)}, u32[]{:S(2)}, u32[]{:S(2)}) collective-permute-start(bf16[512,512]{1,0:T(8,128)(2,1)} %first_b.1), channel_id=1, source_target_pairs={{4,8},{8,4},{5,9},{9,5},{6,10},{10,6},{7,11},{11,7},{20,24},{24,20... | collective-permute-start | bytes 1572872 | tf_op jit(solution)/shard_map/ppermute | solution.py:528
  4.5 14.4 %collective-permute-start.7 = (bf16[512,512]{1,0:T(8,128)(2,1)}, bf16[512,512]{1,0:T(8,128)(2,1)S(1)}, u32[]{:S(2)}, u32[]{:S(2)}) collective-permute-start(bf16[512,512]{1,0:T(8,128)(2,1)} %first_b.1), channel_id=1, source_target_pairs={{0,2},{2,0},{1,3},{3,1},{4,6},{6,4},{5,7},{7,5},{8,10},{10,8},{9,1... | collective-permute-start | bytes 1572872 | tf_op jit(solution)/shard_map/ppermute | solution.py:19
  6.0 22.0 %collective-permute-start.6 = (bf16[512,512]{1,0:T(8,128)(2,1)}, bf16[512,512]{1,0:T(8,128)(2,1)S(1)}, u32[]{:S(2)}, u32[]{:S(2)}) collective-permute-start(bf16[512,512]{1,0:T(8,128)(2,1)} %first_b.1), channel_id=1, source_target_pairs={{0,4},{4,0},{8,12},{12,8},{1,5},{5,1},{9,13},{13,9},{2,6},{6,2},{1... | collective-permute-start | bytes 1572872 | tf_op jit(solution)/shard_map/ppermute | solution.py:528
  16.8 13.8 %collective-permute-start.10 = (bf16[512,512]{1,0:T(8,128)(2,1)}, bf16[512,512]{1,0:T(8,128)(2,1)S(1)}, u32[]{:S(2)}, u32[]{:S(2)}) collective-permute-start(bf16[512,512]{1,0:T(8,128)(2,1)} %refs_2_.1), channel_id=1, source_target_pairs={{4,8},{8,4},{5,9},{9,5},{6,10},{10,6},{7,11},{11,7},{20,24},{24,20... | collective-permute-start | bytes 1572872 | tf_op jit(solution)/shard_map/ppermute | solution.py:528
  17.5 21.8 %collective-permute-start.5 = (bf16[512,512]{1,0:T(8,128)(2,1)S(1)}, bf16[512,512]{1,0:T(8,128)(2,1)S(1)}, u32[]{:S(2)}, u32[]{:S(2)}) collective-permute-start(bf16[512,512]{1,0:T(8,128)(2,1)S(1)} %collective-permute-done.4.inner), channel_id=1, source_target_pairs={{4,0},{8,12},{5,1},{9,13},{6,2},{10,14},{7,3},{11,15},{20,16},{24,... | collective-permute-start | bytes 1572872 | tf_op jit(solution)/shard_map/ppermute | solution.py:528
  18.8 21.3 %collective-permute-start.9 = (bf16[512,512]{1,0:T(8,128)(2,1)S(1)}, bf16[512,512]{1,0:T(8,128)(2,1)S(1)}, u32[]{:S(2)}, u32[]{:S(2)}) collective-permute-start(bf16[512,512]{1,0:T(8,128)(2,1)S(1)} %collective-permute-done.1.refs_2_), channel_id=1, source_target_pairs={{0,1},{1,0},{2,3},{3,2},{4,5},{5,4},{6,7},{7,6},{8,9},{9,8},{10,11... | collective-permute-start | bytes 1572872 | tf_op jit(solution)/shard_map/ppermute | solution.py:19
  28.0 13.4 %collective-permute-start.8 = (bf16[512,512]{1,0:T(8,128)(2,1)S(1)}, bf16[512,512]{1,0:T(8,128)(2,1)S(1)}, u32[]{:S(2)}, u32[]{:S(2)}) collective-permute-start(bf16[512,512]{1,0:T(8,128)(2,1)S(1)} %collective-permute-done.6.second.refs_8_), channel_id=1, source_target_pairs={{0,2},{2,0},{1,3},{3,1},{4,6},{6,4},{5,7},{7,5},{8,10},{10,8},{9,1... | collective-permute-start | bytes 1572872 | tf_op jit(solution)/shard_map/ppermute | solution.py:19
  29.9 13.0 %collective-permute-start.14 = (bf16[512,512]{1,0:T(8,128)(2,1)S(1)}, bf16[512,512]{1,0:T(8,128)(2,1)S(1)}, u32[]{:S(2)}, u32[]{:S(2)}) collective-permute-start(bf16[512,512]{1,0:T(8,128)(2,1)S(1)} %collective-permute-done.6.second.refs_8_), channel_id=1, source_target_pairs={{4,8},{8,4},{5,9},{9,5},{6,10},{10,6},{7,11},{11,7},{20,24},{24,20... | collective-permute-start | bytes 1572872 | tf_op jit(solution)/shard_map/ppermute | solution.py:528
  30.6 19.9 %collective-permute-start.11 = (bf16[512,512]{1,0:T(8,128)(2,1)S(1)}, bf16[512,512]{1,0:T(8,128)(2,1)S(1)}, u32[]{:S(2)}, u32[]{:S(2)}) collective-permute-start(bf16[512,512]{1,0:T(8,128)(2,1)S(1)} %collective-permute-done.10.inner), channel_id=1, source_target_pairs={{4,0},{8,12},{5,1},{9,13},{6,2},{10,14},{7,3},{11,15},{20,16},{24,... | collective-permute-start | bytes 1572872 | tf_op jit(solution)/shard_map/ppermute | solution.py:528
  39.3 11.4 %collective-permute-start.2 = (bf16[512,512]{1,0:T(8,128)(2,1)S(1)}, bf16[512,512]{1,0:T(8,128)(2,1)S(1)}, u32[]{:S(2)}, u32[]{:S(2)}) collective-permute-start(bf16[512,512]{1,0:T(8,128)(2,1)S(1)} %collective-permute-done.1.refs_2_), channel_id=1, source_target_pairs={{4,8},{8,4},{5,9},{9,5},{6,10},{10,6},{7,11},{11,7},{20,24},{24,20... | collective-permute-start | bytes 1572872 | tf_op jit(solution)/shard_map/ppermute | solution.py:528
  39.9 24.1 %copy-start.1 = (bf16[512,512]{1,0:T(8,128)(2,1)S(1)}, bf16[512,512]{1,0:T(8,128)(2,1)}, u32[]{:S(2)}) copy-start(bf16[512,512]{1,0:T(8,128)(2,1)} %first_b.1) | copy-start | bytes 1572868
  40.0 24.1 %copy-start.2 = (bf16[512,512]{1,0:T(8,128)(2,1)S(1)}, bf16[512,512]{1,0:T(8,128)(2,1)}, u32[]{:S(2)}) copy-start(bf16[512,512]{1,0:T(8,128)(2,1)} %refs_2_.1) | copy-start | bytes 1572868
  41.4 22.6 %collective-permute-start.13 = (bf16[512,512]{1,0:T(8,128)(2,1)S(1)}, bf16[512,512]{1,0:T(8,128)(2,1)S(1)}, u32[]{:S(2)}, u32[]{:S(2)}) collective-permute-start(bf16[512,512]{1,0:T(8,128)(2,1)S(1)} %shard_map.57.third.refs_10_), channel_id=1, source_target_pairs={{0,2},{2,0},{1,3},{3,1},{4,6},{6,4},{5,7},{7,5},{8,10},{10,8},{9,1... | collective-permute-start | bytes 1572872 | tf_op jit(solution)/shard_map/ppermute | solution.py:19
  42.9 18.9 %collective-permute-start.15 = (bf16[512,512]{1,0:T(8,128)(2,1)S(1)}, bf16[512,512]{1,0:T(8,128)(2,1)S(1)}, u32[]{:S(2)}, u32[]{:S(2)}) collective-permute-start(bf16[512,512]{1,0:T(8,128)(2,1)S(1)} %collective-permute-done.14.inner), channel_id=1, source_target_pairs={{4,0},{8,12},{5,1},{9,13},{6,2},{10,14},{7,3},{11,15},{20,16},{24,... | collective-permute-start | bytes 1572872 | tf_op jit(solution)/shard_map/ppermute | solution.py:528
  44.2 1.0 %copy-start = (bf16[512,512]{1,0:T(8,128)(2,1)S(1)}, bf16[512,512]{1,0:T(8,128)(2,1)}, u32[]{:S(2)}) copy-start(bf16[512,512]{1,0:T(8,128)(2,1)} %first_b.1) | copy-start | bytes 1572868
  50.6 13.5 %collective-permute-start.12 = (bf16[512,512]{1,0:T(8,128)(2,1)S(1)}, bf16[512,512]{1,0:T(8,128)(2,1)S(1)}, u32[]{:S(2)}, u32[]{:S(2)}) collective-permute-start(bf16[512,512]{1,0:T(8,128)(2,1)S(1)} %shard_map.58.refs_4_), channel_id=1, source_target_pairs={{0,1},{1,0},{2,3},{3,2},{4,5},{5,4},{6,7},{7,6},{8,9},{9,8},{10,11... | collective-permute-start | bytes 1572872 | tf_op jit(solution)/shard_map/ppermute | solution.py:19
  50.7 22.0 %collective-permute-start.3 = (bf16[512,512]{1,0:T(8,128)(2,1)S(1)}, bf16[512,512]{1,0:T(8,128)(2,1)S(1)}, u32[]{:S(2)}, u32[]{:S(2)}) collective-permute-start(bf16[512,512]{1,0:T(8,128)(2,1)S(1)} %collective-permute-done.2.inner), channel_id=1, source_target_pairs={{4,0},{8,12},{5,1},{9,13},{6,2},{10,14},{7,3},{11,15},{20,16},{24,... | collective-permute-start | bytes 1572872 | tf_op jit(solution)/shard_map/ppermute | solution.py:528
  62.3 13.6 %collective-permute-start.18 = (bf16[528,512]{1,0:T(8,128)(2,1)S(1)}, bf16[528,512]{1,0:T(8,128)(2,1)S(1)}, u32[]{:S(2)}, u32[]{:S(2)}) collective-permute-start(bf16[528,512]{1,0:T(8,128)(2,1)S(1)} %shard_map.60.refs_7_.late_b), channel_id=1, source_target_pairs={{0,2},{2,0},{1,3},{3,1},{4,6},{6,4},{5,7},{7,5},{8,10},{10,8},{9,1... | collective-permute-start | bytes 1622024 | tf_op jit(solution)/shard_map/ppermute | solution.py:19
  68.2 4.5 %collective-permute-start.16 = (f32[8,512]{1,0:T(8,128)S(1)}, f32[8,512]{1,0:T(8,128)S(1)}, u32[]{:S(2)}, u32[]{:S(2)}) collective-permute-start(f32[8,512]{1,0:T(8,128)S(1)} %get-tuple-element.53), channel_id=1, source_target_pairs={{0,1},{1,0},{2,3},{3,2},{4,5},{5,4},{6,7},{7,6},{8,9},{9,8},{10,11... | collective-permute-start | bytes 49160 | tf_op jit(solution)/shard_map/ppermute | solution.py:19
  73.1 2.9 %collective-permute-start.17 = (bf16[528,512]{1,0:T(8,128)(2,1)S(1)}, bf16[528,512]{1,0:T(8,128)(2,1)S(1)}, u32[]{:S(2)}, u32[]{:S(2)}) collective-permute-start(bf16[528,512]{1,0:T(8,128)(2,1)S(1)} %shard_map.62.late.late_own.refs_0_), channel_id=1, source_target_pairs={{0,1},{1,0},{2,3},{3,2},{4,5},{5,4},{6,7},{7,6},{8,9},{9,8},{10,11... | collective-permute-start | bytes 1622024 | tf_op jit(solution)/shard_map/ppermute | solution.py:19
  78.0 1.8 %collective-permute-start.19 = (f32[8,1024]{1,0:T(8,128)S(1)}, f32[8,1024]{1,0:T(8,128)S(1)}, u32[]{:S(2)}, u32[]{:S(2)}) collective-permute-start(f32[8,1024]{1,0:T(8,128)S(1)} %get-tuple-element.62.refs_13_), channel_id=1, source_target_pairs={{0,1},{1,0},{2,3},{3,2},{4,5},{5,4},{6,7},{7,6},{8,9},{9,8},{10,11... | collective-permute-start | bytes 98312 | tf_op jit(solution)/shard_map/ppermute | solution.py:19
  78.1 14.8 %collective-permute-start.21 = (bf16[528,512]{1,0:T(8,128)(2,1)S(1)}, bf16[528,512]{1,0:T(8,128)(2,1)S(1)}, u32[]{:S(2)}, u32[]{:S(2)}) collective-permute-start(bf16[528,512]{1,0:T(8,128)(2,1)S(1)} %get-tuple-element.68), channel_id=1, source_target_pairs={{0,2},{2,0},{1,3},{3,1},{4,6},{6,4},{5,7},{7,5},{8,10},{10,8},{9,1... | collective-permute-start | bytes 1622024 | tf_op jit(solution)/shard_map/ppermute | solution.py:19
  87.4 3.1 %collective-permute-start.20 = (bf16[512,512]{1,0:T(8,128)(2,1)S(1)}, bf16[512,512]{1,0:T(8,128)(2,1)S(1)}, u32[]{:S(2)}, u32[]{:S(2)}) collective-permute-start(bf16[512,512]{1,0:T(8,128)(2,1)S(1)} %get-tuple-element.65), channel_id=1, source_target_pairs={{0,1},{1,0},{2,3},{3,2},{4,5},{5,4},{6,7},{7,6},{8,9},{9,8},{10,11... | collective-permute-start | bytes 1572872 | tf_op jit(solution)/shard_map/ppermute | solution.py:19
  87.6 1.7 %collective-permute-start.22 = (f32[8,128]{1,0:T(8,128)S(1)}, f32[8,128]{1,0:T(8,128)S(1)}, u32[]{:S(2)}, u32[]{:S(2)}) collective-permute-start(f32[8,128]{1,0:T(8,128)S(1)} %get-tuple-element.70), channel_id=1, source_target_pairs={{0,1},{1,0},{2,3},{3,2},{4,5},{5,4},{6,7},{7,6},{8,9},{9,8},{10,11... | collective-permute-start | bytes 12296 | tf_op jit(solution)/shard_map/ppermute | solution.py:19
  89.3 3.6 %collective-permute-start.23 = (f32[8,128]{1,0:T(8,128)S(1)}, f32[8,128]{1,0:T(8,128)S(1)}, u32[]{:S(2)}, u32[]{:S(2)}) collective-permute-start(f32[8,128]{1,0:T(8,128)S(1)} %shard_map.67.loss), channel_id=1, source_target_pairs={{0,2},{2,0},{1,3},{3,1},{4,6},{6,4},{5,7},{7,5},{8,10},{10,8},{9,1... | collective-permute-start | bytes 12296 | tf_op jit(solution)/shard_map/ppermute | solution.py:19

commit v13 on v9

--- a/solution.py
+++ b/solution.py
@@ -231,7 +231,13 @@
     row[...] = rows_of([shift] + [jnp.sum(s, axis=0, keepdims=True) for s in sums])
 
 
-def late_kernel(images, turned, mask, outer, inner, row, out):
+def halves_kernel(block, first, second):
+    half = first.shape[0]
+    first[...] = block[:half, :]
+    second[...] = block[half:, :]
+
+
+def late_left_kernel(images, mask, outer, inner, row, out):
     rows, quart = outer.shape
     shift = row[0:1, :]
     sums = [jnp.zeros((8, quart), jnp.float32)] * 3
@@ -239,13 +245,44 @@
         piece = slice(at, at + 128)
         centred = pick(mask, outer, inner, piece) - shift
         low = centred.astype(jnp.bfloat16)
-        if turned:
-            out[:quart, piece] = jnp.transpose(low)
-        else:
-            out[piece, :] = low
+        out[piece, :] = low
         sums = add_sums(sums, centred, low)
     delta, rstd, gap = moments(joined_sums(row, sums), images)
     out[rows:, :] = split_rows([shift + delta, rstd, gap, delta])
+
+
+def late_right_kernel(images, last, mask, outer, inner, row, out, *rest):
+    some, quart = outer.shape
+    shift = row[0:1, :]
+    sums = [jnp.zeros((8, quart), jnp.float32)] * 3
+    for at in range(0, some, 128):
+        piece = slice(at, at + 128)
+        centred = pick(mask, outer, inner, piece) - shift
+        low = centred.astype(jnp.bfloat16)
+        out[:quart, piece] = jnp.transpose(low)
+        sums = add_sums(sums, centred, low)
+    sums = joined_sums(row, sums)
+    if not last:
+        (row_out,) = rest
+        row_out[...] = rows_of([shift, *sums])
+        return
+    delta, rstd, gap = moments(sums, images)
+    parts = split_rows([shift + delta, rstd, gap, delta])
+    for i in range(quart // some):
+        below = quart + 16 * i
+        out[below : below + 16, :] = parts[:, i * some : (i + 1) * some]
+
+
+def right_stats(late):
+    quart, some = late[0].shape
+    found = [joined_rows(late[1], quart + 16 * i) for i in range(quart // some)]
+    return [jnp.concatenate(values, axis=1) for values in zip(*found)]
+
+
+def late_products(right, left, lanes):
+    quart, some = right[0].shape
+    first = dot(right[0][...], left[:some, lanes])
+    return first + dot(right[1][:quart, :], left[some : 2 * some, lanes])
 
 
 def products_kernel(*refs):
@@ -301,17 +338,17 @@
 
 
 def scale_columns(late_b, images):
-    quart = late_b.shape[1]
-    _, rstd, _, delta = joined_rows(late_b, quart)
+    _, rstd, _, delta = right_stats(late_b)
     columns = jnp.transpose(rows_of([rstd / images, delta * rstd]))
     return columns[:, 0:1], columns[:, 1:2]
 
 
-def partner_kernel(images, part, late, zero, sums, late_b, *refs):
+def partner_kernel(images, part, late, zero, sums, late_b_0, late_b_1, *refs):
     if part:
         (terms_in, across_in, vec_in, partial_out, e_out, vec_out, left) = refs
     else:
         (terms_out, across_out, e_out, vec_out, left) = refs
+    late_b = (late_b_0, late_b_1)
     rows, quart = zero.shape
     width = quart // 2
     _, rstd, _, delta = joined_rows(late, rows)
@@ -321,7 +358,7 @@
     down = []
     for tile in range(2):
         at = slice(tile * width, (tile + 1) * width)
-        total = sums[:, at] + dot(late_b[:quart, :], late[:rows, at])
+        total = sums[:, at] + late_products(late_b, late, at)
         corr = (total * scale_col - delta_col * delta[:, at]) * rstd[:, at]
         e_out[:, at] = (corr * (off_weight * rstd[:, at])).astype(jnp.bfloat16)
         square = corr * corr
@@ -348,10 +385,11 @@
 
 
 def own_kernel(images, flags, *refs):
-    (late_own, late_other, first_own, first_other, zero_own, zero_other, sums, late_b) = refs[:8]
-    (late_b_other, first_b, first_b_other, e_left, e_right, partner_own, partner_other) = refs[8:15]
-    (vec_own, vec_other, vec_core, right_out, left_out, left_partial_out, mine_out) = refs[15:22]
-    (own_loss_out, loss_out, left, norm_b, e_own, mine_own, mine_partner) = refs[22:]
+    late_b, late_b_other, refs = refs[:2], refs[2:4], refs[4:]
+    (late_own, late_other, first_own, first_other, zero_own, zero_other, sums) = refs[:7]
+    (first_b, first_b_other, e_left, e_right, partner_own, partner_other) = refs[7:13]
+    (vec_own, vec_other, vec_core, right_out, left_out, left_partial_out, mine_out) = refs[13:20]
+    (own_loss_out, loss_out, left, norm_b, e_own, mine_own, mine_partner) = refs[20:]
     rows, quart = zero_own.shape
     width = quart // 2
     lower, upper = slice(0, quart), slice(quart, 2 * quart)
@@ -360,8 +398,8 @@
     offset, rstd, _, delta = [both(i) for i in range(4)]
     left_operand(zero_own, late_own, left, lower)
     left_operand(zero_other, late_other, left, upper)
-    own_b = joined_rows(late_b, quart)
-    other_b = joined_rows(late_b_other, quart)
+    own_b = right_stats(late_b)
+    other_b = right_stats(late_b_other)
     for source, stats, lanes in ((first_b, own_b, lower), (first_b_other, other_b, upper)):
         for at in range(0, rows, 64):
             piece = slice(at, at + 64)
@@ -373,7 +411,7 @@
 
     def tile_corr(late, inner, total, columns, block):
         scale_col, delta_col = columns
-        total = total + dot(block[:quart, :], late[:rows, inner])
+        total = total + late_products(block, late, inner)
         row = joined_rows(late, rows)
         return (total * scale_col - delta_col * row[3][:, inner]) * row[1][:, inner]
 
@@ -466,25 +504,31 @@
     out[0] = (one[0, 0] + other[0, 0]) / feats
 
 
-def final_kernel(right, from_x, late_b, first_b, left, from_core, right_out, left_out):
-    rows, quart = left.shape
-    offset, rstd, _, _ = joined_rows(late_b, quart)
+def left_final_kernel(left, from_core, left_out):
+    for at in range(0, left.shape[0], 64):
+        piece = slice(at, at + 64)
+        value = left[piece, :] + from_core[piece, :].astype(jnp.float32)
+        left_out[piece, :] = value.astype(jnp.bfloat16)
+
+
+def right_final_kernel(right, from_x, late_b_0, late_b_1, first_b, right_out):
+    rows = right.shape[0]
+    offset, rstd, _, _ = right_stats((late_b_0, late_b_1))
     second = joined_rows(from_x, rows)[0]
     for at in range(0, rows, 64):
         piece = slice(at, at + 64)
         xhat = (first_b[piece, :].astype(jnp.float32) - offset) * rstd
         value = right[piece, :] + from_x[piece, :].astype(jnp.float32) - xhat * second
         right_out[piece, :] = (rstd * value).astype(jnp.bfloat16)
-        value = left[piece, :] + from_core[piece, :].astype(jnp.float32)
-        left_out[piece, :] = value.astype(jnp.bfloat16)
 
 
 vmem = pl.BlockSpec(memory_space=pltpu.VMEM)
 smem = pl.BlockSpec(memory_space=pltpu.SMEM)
 
 
-def local_call(kernel, operands, outs, scratch=(), flops=2**20, room=8, held=()):
-    moved = sum(x.size * x.dtype.itemsize for x in (*operands, *outs))
+def local_call(kernel, operands, outs, scratch=(), flops=2**20, room=8, held=(), moved=None):
+    if moved is None:
+        moved = sum(x.size * x.dtype.itemsize for x in (*operands, *outs))
 
     def space(x):
         return smem if x.ndim == 1 else vmem
@@ -543,6 +587,8 @@
     def picked(outer, inner):
         return local_call(pick_kernel, (mask, outer, inner), (quarter_bf16,))[0]
 
+    some = rows // 2
+    half_block = jax.ShapeDtypeStruct((some, quart), jnp.bfloat16)
     first_b = along(right_outputs, pairs)
     inner_b = along(right_outputs, middle)
     first_a = along(left_outputs, pairs)
@@ -559,7 +605,8 @@
     third_a = along(first_a, middle)
     other_a1 = core_swap(first_a)
 
-    last_b = along(third_b, outward)
+    third_b = local_call(halves_kernel, (third_b,), (half_block, half_block))
+    last_b = [along(x, outward) for x in third_b]
     second_b = picked(outer_b, inner_b)
     row_b = local_call(right_sums_kernel, (right_outputs, first_b, second_b), (row_out,))[0]
     second_b, other_b1, other_a1 = after(second_b, other_b1, other_a1)
@@ -569,13 +616,22 @@
     second_a, row_b = after(second_a, row_b)
     other_a2 = core_swap(second_a)
 
-    (late_b,) = local_call(
-        functools.partial(late_kernel, batch_images, True),
-        (mask, last_b, third_b, row_b),
-        (extended,),
+    late_b_0, row_b = local_call(
+        functools.partial(late_right_kernel, batch_images, False),
+        (mask, last_b[0], third_b[0], row_b),
+        (jax.ShapeDtypeStruct((quart, some), jnp.bfloat16), row_out),
         held=(0, 1, 2, 3),
     )
-    late_b_other = x_swap(late_b)
+    late_b_other_0 = x_swap(late_b_0)
+    (late_b_1,) = local_call(
+        functools.partial(late_right_kernel, batch_images, True),
+        (mask, last_b[1], third_b[1], row_b),
+        (jax.ShapeDtypeStruct((quart + 16 * (quart // some), some), jnp.bfloat16),),
+        held=(0, 1, 2, 3),
+    )
+    late_b_other_1 = x_swap(late_b_1)
+    late_b = (late_b_0, late_b_1)
+    other_b2, late_b_1, late_b_other_0 = after(other_b2, late_b_1, late_b_other_0)
     partner_own, partner_other, own_all, row_other, zero_own, zero_other = local_call(
         products_kernel,
         (left_outputs, other_a0, first_a, other_a1, second_a, other_a2)
@@ -589,12 +645,13 @@
             quarter_bf16,
         ),
         [low(3 * rows, half), low(half, 3 * rows)],
-        12 * gemm,
         room=20,
-    )
-    row_a = core_swap(row_other)
+        moved=2**16,
+    )
+    row_a, late_b_other_1 = after(core_swap(row_other), late_b_other_1)
+    late_b_other = (late_b_other_0, late_b_other_1)
     (late_a,) = local_call(
-        functools.partial(late_kernel, batch_images, False),
+        functools.partial(late_left_kernel, batch_images),
         (mask, last_a, third_a, row_a),
         (extended,),
         held=(0, 1, 2, 3),
@@ -603,7 +660,7 @@
 
     terms, across, e_left, vec_own = local_call(
         functools.partial(partner_kernel, batch_images, 0),
-        (late_a, zero_own, partner_own, late_b_other),
+        (late_a, zero_own, partner_own, *late_b_other),
         (
             jax.ShapeDtypeStruct((rows + 16, quart), jnp.float32),
             across_shape,
@@ -616,7 +673,7 @@
     )
     partial_right, e_right, vec_other = local_call(
         functools.partial(partner_kernel, batch_images, 1),
-        (late_a_other, zero_other, partner_other, late_b_other, terms, across, vec_own),
+        (late_a_other, zero_other, partner_other, *late_b_other, terms, across, vec_own),
         (extended, quarter_bf16, row_out),
         [low(rows + 16, quart)],
         2 * gemm,
@@ -626,8 +683,9 @@
     vec_core = core_swap(vec_other)
     right_own, left_own, partial_left, mine, own_loss, loss = local_call(
         functools.partial(own_kernel, batch_images),
-        (flags, late_a, late_a_other, left_outputs, other_a0, zero_own, zero_other, own_all)
-        + (late_b, late_b_other, right_outputs, other_b0, e_left, e_right)
+        (flags, *late_b, *late_b_other)
+        + (late_a, late_a_other, left_outputs, other_a0, zero_own, zero_other, own_all)
+        + (right_outputs, other_b0, e_left, e_right)
         + (partner_own, partner_other)
         + (vec_own, vec_other, vec_core),
         (
@@ -652,10 +710,10 @@
     core_loss = core_swap(own_loss)
     (loss,) = local_call(add_kernel, (loss, core_loss), (one_out,))
     x_loss = x_swap(loss)
-    right_gradient, left_gradient = local_call(
-        final_kernel,
-        (right_own, from_x, late_b, right_outputs, left_own, from_core),
-        (quarter_bf16, quarter_bf16),
+    (left_gradient,) = local_call(left_final_kernel, (left_own, from_core), (quarter_bf16,))
+    right_own, left_gradient = after(right_own, left_gradient)
+    (right_gradient,) = local_call(
+        right_final_kernel, (right_own, from_x, *late_b, right_outputs), (quarter_bf16,)
     )
     right_gradient, x_loss = after(right_gradient, x_loss)
     (loss,) = local_call(

time: 95.5 us -> 93.3 us (0.977)
  waiting for transfers between devices: 49.1 us -> 44.1 us
  starting transfers between devices: 25.8 us -> 29 us
  local copies, waits for them, and re-layouts: 1.05 us -> 0.01 us
    ppermute x10 -> x11, waiting for transfers between devices: 41.3 us -> 37 us  [along(): return lax.ppermute(block, 'dp', route)]
    ppermute x14 -> x15, starting transfers between devices: 10.8 us -> 12.6 us  [swapped(): return lax.ppermute(block, axis, route)]
    ppermute x10 -> x11, starting transfers between devices: 14.9 us -> 16.3 us  [along(): return lax.ppermute(block, 'dp', route)]
    unnamed x6 -> x4, local copies, waits for them, and re-layouts: 1.05 us -> 0.01 us
    ppermute x14 -> x15, waiting for transfers between devices: 7.81 us -> 7.1 us  [swapped(): return lax.ppermute(block, axis, route)]
    pallas_call x12 -> x15, Pallas kernels: 18.2 us -> 18.8 us  [local_call(): pl.pallas_call(kernel, out_shape=list(outs), in_specs=[space(x) for x in...]
  transfers between devices with their start and end apart: 24 -> 26, of which waited for: 10 -> 13; matrix products, arithmetic and copies ran while one was open for 0% -> 0% of each run, Pallas kernels for 17% -> 18%
where the time goes in v13:
time: 93.3 us; the launch traced here: 93 us
  waiting for transfers between devices  44.1 us (47%)
  starting transfers between devices  29 us (31%)
  Pallas kernels  18.8 us (20%)
  between operations  1.02 us (1%)
    ppermute x11, waiting for transfers between devices, along(): return lax.ppermute(block, 'dp', route)  37 us
    pallas_call x15, Pallas kernels, local_call(): pl.pallas_call(kernel, out_shape=list(outs), in_specs=[space(x) for x in...  18.8 us
    ppermute x11, starting transfers between devices, along(): return lax.ppermute(block, 'dp', route)  16.3 us
    ppermute x15, starting transfers between devices, swapped(): return lax.ppermute(block, axis, route)  12.6 us
    ppermute x15, waiting for transfers between devices, swapped(): return lax.ppermute(block, axis, route)  7.1 us
  transfers between devices with their start and end apart: 26, of which 13 were waited for; matrix products, arithmetic and copies ran while one was open for 0% of the time, Pallas kernels for 18%

profile of v13, /device:TPU:0, one launch (start us, length us, event | category | flops | bytes accessed | tf_op | source)
XLA Modules:
  0.0 93.0 jit_solution(10702095165620113008)
XLA Ops:
  1.2 2.7 %collective-permute-start.4 = (bf16[512,512]{1,0:T(8,128)(2,1)}, bf16[512,512]{1,0:T(8,128)(2,1)S(1)}, u32[]{:S(2)}, u32[]{:S(2)}) collective-permute-start(bf16[512,512]{1,0:T(8,128)(2,1)} %refs_6_.3), channel_id=1, source_target_pairs={{0,4},{4,0},{8,12},{12,8},{1,5},{5,1},{9,13},{13,9},{2,6},{6,2},{1... | collective-permute-start | bytes 1572872 | tf_op jit(solution)/shard_map/ppermute | solution.py:566
  4.5 1.6 %collective-permute-start.10 = (bf16[512,512]{1,0:T(8,128)(2,1)}, bf16[512,512]{1,0:T(8,128)(2,1)S(1)}, u32[]{:S(2)}, u32[]{:S(2)}) collective-permute-start(bf16[512,512]{1,0:T(8,128)(2,1)} %first_b.1), channel_id=1, source_target_pairs={{0,2},{2,0},{1,3},{3,1},{4,6},{6,4},{5,7},{7,5},{8,10},{10,8},{9,1... | collective-permute-start | bytes 1572872 | tf_op jit(solution)/shard_map/ppermute | solution.py:19
  6.1 4.4 %collective-permute-start.1 = (bf16[512,512]{1,0:T(8,128)(2,1)}, bf16[512,512]{1,0:T(8,128)(2,1)S(1)}, u32[]{:S(2)}, u32[]{:S(2)}) collective-permute-start(bf16[512,512]{1,0:T(8,128)(2,1)} %first_b.1), channel_id=1, source_target_pairs={{0,4},{4,0},{8,12},{12,8},{1,5},{5,1},{9,13},{13,9},{2,6},{6,2},{1... | collective-permute-start | bytes 1572872 | tf_op jit(solution)/shard_map/ppermute | solution.py:566
  10.5 6.3 %collective-permute-done.4.refs_2_ = bf16[512,512]{1,0:T(8,128)(2,1)S(1)} collective-permute-done((bf16[512,512]{1,0:T(8,128)(2,1)}, bf16[512,512]{1,0:T(8,128)(2,1)S(1)}, u32[]{:S(2)}, u32[]{:S(2)}) %collective-permute-start.4) | collective-permute-done | bytes 524320 | tf_op jit(solution)/shard_map/ppermute | solution.py:566
  17.5 1.3 %collective-permute-start.8 = (bf16[512,512]{1,0:T(8,128)(2,1)S(1)}, bf16[512,512]{1,0:T(8,128)(2,1)S(1)}, u32[]{:S(2)}, u32[]{:S(2)}) collective-permute-start(bf16[512,512]{1,0:T(8,128)(2,1)S(1)} %collective-permute-done.7.inner), channel_id=1, source_target_pairs={{4,0},{8,12},{5,1},{9,13},{6,2},{10,14},{7,3},{11,15},{20,16},{24,... | collective-permute-start | bytes 1572872 | tf_op jit(solution)/shard_map/ppermute | solution.py:566
  18.9 9.1 %collective-permute-done.1.second.refs_8_ = bf16[512,512]{1,0:T(8,128)(2,1)S(1)} collective-permute-done((bf16[512,512]{1,0:T(8,128)(2,1)}, bf16[512,512]{1,0:T(8,128)(2,1)S(1)}, u32[]{:S(2)}, u32[]{:S(2)}) %collective-permute-start.1) | collective-permute-done | bytes 524320 | tf_op jit(solution)/shard_map/ppermute | solution.py:566
  28.0 1.9 %collective-permute-start.11 = (bf16[512,512]{1,0:T(8,128)(2,1)S(1)}, bf16[512,512]{1,0:T(8,128)(2,1)S(1)}, u32[]{:S(2)}, u32[]{:S(2)}) collective-permute-start(bf16[512,512]{1,0:T(8,128)(2,1)S(1)} %collective-permute-done.1.second.refs_8_), channel_id=1, source_target_pairs={{0,2},{2,0},{1,3},{3,1},{4,6},{6,4},{5,7},{7,5},{8,10},{10,8},{9,1... | collective-permute-start | bytes 1572872 | tf_op jit(solution)/shard_map/ppermute | solution.py:19
  30.6 1.3 %collective-permute-start.6 = (bf16[512,512]{1,0:T(8,128)(2,1)S(1)}, bf16[512,512]{1,0:T(8,128)(2,1)S(1)}, u32[]{:S(2)}, u32[]{:S(2)}) collective-permute-start(bf16[512,512]{1,0:T(8,128)(2,1)S(1)} %collective-permute-done.5.inner), channel_id=1, source_target_pairs={{4,0},{8,12},{5,1},{9,13},{6,2},{10,14},{7,3},{11,15},{20,16},{24,... | collective-permute-start | bytes 1572872 | tf_op jit(solution)/shard_map/ppermute | solution.py:566
  31.9 7.4 %collective-permute-done.8.outer = bf16[512,512]{1,0:T(8,128)(2,1)S(1)} collective-permute-done((bf16[512,512]{1,0:T(8,128)(2,1)S(1)}, bf16[512,512]{1,0:T(8,128)(2,1)S(1)}, u32[]{:S(2)}, u32[]{:S(2)}) %collective-permute-start.8) | collective-permute-done | bytes 524320 | tf_op jit(solution)/shard_map/ppermute | solution.py:566
  40.1 1.4 %collective-permute-done.11.refs_9_ = bf16[512,512]{1,0:T(8,128)(2,1)S(1)} collective-permute-done((bf16[512,512]{1,0:T(8,128)(2,1)S(1)}, bf16[512,512]{1,0:T(8,128)(2,1)S(1)}, u32[]{:S(2)}, u32[]{:S(2)}) %collective-permute-start.11) | collective-permute-done | bytes 524320 | tf_op jit(solution)/shard_map/ppermute | solution.py:19
  41.5 1.5 %collective-permute-start.13 = (bf16[512,512]{1,0:T(8,128)(2,1)S(1)}, bf16[512,512]{1,0:T(8,128)(2,1)S(1)}, u32[]{:S(2)}, u32[]{:S(2)}) collective-permute-start(bf16[512,512]{1,0:T(8,128)(2,1)S(1)} %shard_map.59.third.refs_10_), channel_id=1, source_target_pairs={{0,2},{2,0},{1,3},{3,1},{4,6},{6,4},{5,7},{7,5},{8,10},{10,8},{9,1... | collective-permute-start | bytes 1572872 | tf_op jit(solution)/shard_map/ppermute | solution.py:19
  43.0 1.4 %collective-permute-start.3 = (bf16[256,512]{1,0:T(8,128)(2,1)S(1)}, bf16[256,512]{1,0:T(8,128)(2,1)S(1)}, u32[]{:S(2)}, u32[]{:S(2)}) collective-permute-start(bf16[256,512]{1,0:T(8,128)(2,1)S(1)} %get-tuple-element.50.inner), channel_id=1, source_target_pairs={{4,0},{8,12},{5,1},{9,13},{6,2},{10,14},{7,3},{11,15},{20,16},{24,... | collective-permute-start | bytes 786440 | tf_op jit(solution)/shard_map/ppermute | solution.py:566
  44.4 1.0 %shard_map.60.row = f32[8,512]{1,0:T(8,128)S(1)} custom-call(bf16[512,512]{1,0:T(8,128)(2,1)S(1)} %copy-done, bf16[512,512]{1,0:T(8,128)(2,1)S(1)} %collective-permute-done.1.second.refs_8_, bf16[512,512]{1,0:T(8,128)(2,1)S(1)} %shard_map.59.third.refs_10_), custom_call_target="tpu_custom_call" | custom-call | flops 1048576 | bytes 1589248 | tf_op jit(solution)/shard_map/pallas_call | solution.py:536
  45.4 5.1 %collective-permute-done.6.outer = bf16[512,512]{1,0:T(8,128)(2,1)S(1)} collective-permute-done((bf16[512,512]{1,0:T(8,128)(2,1)S(1)}, bf16[512,512]{1,0:T(8,128)(2,1)S(1)}, u32[]{:S(2)}, u32[]{:S(2)}) %collective-permute-start.6) | collective-permute-done | bytes 524320 | tf_op jit(solution)/shard_map/ppermute | solution.py:566
  50.7 1.3 %collective-permute-start.9 = (bf16[256,512]{1,0:T(8,128)(2,1)S(1)}, bf16[256,512]{1,0:T(8,128)(2,1)S(1)}, u32[]{:S(2)}, u32[]{:S(2)}) collective-permute-start(bf16[256,512]{1,0:T(8,128)(2,1)S(1)} %get-tuple-element.55.inner), channel_id=1, source_target_pairs={{4,0},{8,12},{5,1},{9,13},{6,2},{10,14},{7,3},{11,15},{20,16},{24,... | collective-permute-start | bytes 786440 | tf_op jit(solution)/shard_map/ppermute | solution.py:566
  52.0 1.3 %collective-permute-start.19 = (bf16[512,512]{1,0:T(8,128)(2,1)S(1)}, bf16[512,512]{1,0:T(8,128)(2,1)S(1)}, u32[]{:S(2)}, u32[]{:S(2)}) collective-permute-start(bf16[512,512]{1,0:T(8,128)(2,1)S(1)} %collective-permute-done.18.inner), channel_id=1, source_target_pairs={{4,0},{8,12},{5,1},{9,13},{6,2},{10,14},{7,3},{11,15},{20,16},{24,... | collective-permute-start | bytes 1572872 | tf_op jit(solution)/shard_map/ppermute | solution.py:566
  53.3 2.7 %collective-permute-done.3.outer = bf16[256,512]{1,0:T(8,128)(2,1)S(1)} collective-permute-done((bf16[256,512]{1,0:T(8,128)(2,1)S(1)}, bf16[256,512]{1,0:T(8,128)(2,1)S(1)}, u32[]{:S(2)}, u32[]{:S(2)}) %collective-permute-start.3) | collective-permute-done | bytes 262176 | tf_op jit(solution)/shard_map/ppermute | solution.py:566
  56.2 1.6 %collective-permute-start.14 = (bf16[512,256]{1,0:T(8,128)(2,1)S(1)}, bf16[512,256]{1,0:T(8,128)(2,1)S(1)}, u32[]{:S(2)}, u32[]{:S(2)}) collective-permute-start(bf16[512,256]{1,0:T(8,128)(2,1)S(1)} %get-tuple-element.54.refs_0_.late_b_0), channel_id=1, source_target_pairs={{0,2},{2,0},{1,3},{3,1},{4,6},{6,4},{5,7},{7,5},{8,10},{10,8},{9,1... | collective-permute-start | bytes 786440 | tf_op jit(solution)/shard_map/ppermute | solution.py:19
  57.8 4.0 %collective-permute-done.9.outer = bf16[256,512]{1,0:T(8,128)(2,1)S(1)} collective-permute-done((bf16[256,512]{1,0:T(8,128)(2,1)S(1)}, bf16[256,512]{1,0:T(8,128)(2,1)S(1)}, u32[]{:S(2)}, u32[]{:S(2)}) %collective-permute-start.9) | collective-permute-done | bytes 262176 | tf_op jit(solution)/shard_map/ppermute | solution.py:566
  62.0 1.9 %collective-permute-start.17 = (bf16[544,256]{1,0:T(8,128)(2,1)S(1)}, bf16[544,256]{1,0:T(8,128)(2,1)S(1)}, u32[]{:S(2)}, u32[]{:S(2)}) collective-permute-start(bf16[544,256]{1,0:T(8,128)(2,1)S(1)} %shard_map.62.refs_1_.late_b_1), channel_id=1, source_target_pairs={{0,2},{2,0},{1,3},{3,1},{4,6},{6,4},{5,7},{7,5},{8,10},{10,8},{9,1... | collective-permute-start | bytes 835592 | tf_op jit(solution)/shard_map/ppermute | solution.py:19
  64.0 4.1 %shard_map.63 = (f32[512,512]{1,0:T(8,128)S(1)}, f32[512,512]{1,0:T(8,128)S(1)}, f32[512,1024]{1,0:T(8,128)S(1)}, f32[8,512]{1,0:T(8,128)S(1)}, bf16[512,512]{1,...) custom-call(bf16[512,512]{1,0:T(8,128)(2,1)S(1)} %copy-done.1, bf16[512,512]{1,0:T(8,128)(2,1)S(1)} %collective-permute-done.refs_1_.refs_7_, ...), custom_call_target="tpu_custom_call" | custom-call | flops 1048576 | bytes 65536 | tf_op jit(solution)/shard_map/pallas_call | solution.py:536
  68.1 2.0 %collective-permute-done.17.late_b_1.refs_3_ = bf16[544,256]{1,0:T(8,128)(2,1)S(1)} collective-permute-done((bf16[544,256]{1,0:T(8,128)(2,1)S(1)}, bf16[544,256]{1,0:T(8,128)(2,1)S(1)}, u32[]{:S(2)}, u32[]{:S(2)}) %collective-permute-start.17) | collective-permute-done | bytes 278560 | tf_op jit(solution)/shard_map/ppermute | solution.py:19
  70.2 2.6 %collective-permute-done.19.outer = bf16[512,512]{1,0:T(8,128)(2,1)S(1)} collective-permute-done((bf16[512,512]{1,0:T(8,128)(2,1)S(1)}, bf16[512,512]{1,0:T(8,128)(2,1)S(1)}, u32[]{:S(2)}, u32[]{:S(2)}) %collective-permute-start.19) | collective-permute-done | bytes 524320 | tf_op jit(solution)/shard_map/ppermute | solution.py:566
  73.2 1.1 %shard_map.65 = (f32[528,512]{1,0:T(8,128)S(1)}, f32[512,128]{1,0:T(8,128)S(1)}, bf16[512,512]{1,0:T(8,128)(2,1)S(1)}, f32[8,512]{1,0:T(8,128)S(1)}) custom-call(bf16[528,512]{1,0:T(8,128)(2,1)S(1)} %shard_map.64.late.refs_4_, bf16[512,512]{1,0:T(8,128)(2,1)S(1)} %get-tuple-element.70.zero.refs_8_, f32[512,512]{1,0:T(8,128)S(1)} %get-tuple-element.73.sums.refs_15_, ...), custom_call_target="tpu_custom_call" | custom-call | flops 536870912 | bytes 4538368 | tf_op jit(solution)/shard_map/pallas_call | solution.py:536
  75.1 1.3 %shard_map.66 = (bf16[528,512]{1,0:T(8,128)(2,1)S(1)}, bf16[512,512]{1,0:T(8,128)(2,1)S(1)}, f32[8,512]{1,0:T(8,128)S(1)}) custom-call(bf16[528,512]{1,0:T(8,128)(2,1)S(1)} %collective-permute-done.20.late.refs_5_, bf16[512,512]{1,0:T(8,128)(2,1)S(1)} %get-tuple-element.71.zero.refs_9_, f32[512,512]{1,0:T(8,128)S(1)} %get-tuple-element.75.sums.refs_16_, ...), custom_call_target="tpu_custom_call" | custom-call | flops 536870912 | bytes 5095424 | tf_op jit(solution)/shard_map/pallas_call | solution.py:536
  76.6 1.7 %collective-permute-start.23 = (bf16[528,512]{1,0:T(8,128)(2,1)S(1)}, bf16[528,512]{1,0:T(8,128)(2,1)S(1)}, u32[]{:S(2)}, u32[]{:S(2)}) collective-permute-start(bf16[528,512]{1,0:T(8,128)(2,1)S(1)} %get-tuple-element.86), channel_id=1, source_target_pairs={{0,2},{2,0},{1,3},{3,1},{4,6},{6,4},{5,7},{7,5},{8,10},{10,8},{9,1... | collective-permute-start | bytes 1622024 | tf_op jit(solution)/shard_map/ppermute | solution.py:19
  78.3 7.6 %shard_map.67 = (f32[512,512]{1,0:T(8,128)S(1)}, f32[512,512]{1,0:T(8,128)S(1)}, bf16[512,512]{1,0:T(8,128)(2,1)S(1)}, f32[256,1024]{1,0:T(8,128)}, f32[8,128]{1,0:T(8,128)S(1)}, /*index=5*/f32[8,128]{1,0:T(8,128)S(1)}) custom-call(s32[2]{0:T(128)S(1)} %pad_add_fusion.flags, bf16[512,256]{1,0:T(8,128)(2,1)S(1)} %get-tuple-element.54.refs_0_.late_b_0, ...), custom_call_target="tpu_custom_call" | custom-call | flops 2147483648 | bytes 14278664 | tf_op jit(solution)/shard_map/pallas_call | solution.py:536
  86.5 1.4 %collective-permute-done.24.other = f32[8,128]{1,0:T(8,128)S(1)} collective-permute-done((f32[8,128]{1,0:T(8,128)S(1)}, f32[8,128]{1,0:T(8,128)S(1)}, u32[]{:S(2)}, u32[]{:S(2)}) %collective-permute-start.24) | collective-permute-done | bytes 4128 | tf_op jit(solution)/shard_map/ppermute | solution.py:19
  87.9 1.0 %collective-permute-start.25 = (f32[8,128]{1,0:T(8,128)S(1)}, f32[8,128]{1,0:T(8,128)S(1)}, u32[]{:S(2)}, u32[]{:S(2)}) collective-permute-start(f32[8,128]{1,0:T(8,128)S(1)} %shard_map.70.one), channel_id=1, source_target_pairs={{0,2},{2,0},{1,3},{3,1},{4,6},{6,4},{5,7},{7,5},{8,10},{10,8},{9,1... | collective-permute-start | bytes 12296 | tf_op jit(solution)/shard_map/ppermute | solution.py:19
  88.9 0.9 shard_map.68
  89.8 1.4 %collective-permute-done.23.from_x = bf16[528,512]{1,0:T(8,128)(2,1)S(1)} collective-permute-done((bf16[528,512]{1,0:T(8,128)(2,1)S(1)}, bf16[528,512]{1,0:T(8,128)(2,1)S(1)}, u32[]{:S(2)}, u32[]{:S(2)}) %collective-permute-start.23) | collective-permute-done | bytes 540704 | tf_op jit(solution)/shard_map/ppermute | solution.py:19
  91.2 1.1 %shard_map.69 = bf16[512,512]{1,0:T(8,128)(2,1)} custom-call(f32[512,512]{1,0:T(8,128)S(1)} %get-tuple-element.85.right, bf16[528,512]{1,0:T(8,128)(2,1)S(1)} %collective-permute-done.23.from_x, bf16[512,256]{1,0:T(8,128)(2,1)S(1)} %get-tuple-element.54.refs_0_.late_b_0, bf16[544,256]{1,0:T(8,128)(2,1)S(1)} %shard_map.62.refs_1_.late_b_1, ...), custom_call_target="tpu_custom_call" | custom-call | flops 1048576 | bytes 3178496 | tf_op jit(solution)/shard_map/pallas_call | solution.py:536
  (41 shorter events, 7.0 us)
Async XLA Ops:
  0.6 43.8 %copy-start = (bf16[512,512]{1,0:T(8,128)(2,1)S(1)}, bf16[512,512]{1,0:T(8,128)(2,1)}, u32[]{:S(2)}) copy-start(bf16[512,512]{1,0:T(8,128)(2,1)} %first_b.1) | copy-start | bytes 1572868
  0.6 9.9 %collective-permute-start = (bf16[512,512]{1,0:T(8,128)(2,1)}, bf16[512,512]{1,0:T(8,128)(2,1)S(1)}, u32[]{:S(2)}, u32[]{:S(2)}) collective-permute-start(bf16[512,512]{1,0:T(8,128)(2,1)} %refs_6_.3), channel_id=1, source_target_pairs={{0,1},{1,0},{2,3},{3,2},{4,5},{5,4},{6,7},{7,6},{8,9},{9,8},{10,11... | collective-permute-start | bytes 1572872 | tf_op jit(solution)/shard_map/ppermute | solution.py:19
  1.2 15.6 %collective-permute-start.4 = (bf16[512,512]{1,0:T(8,128)(2,1)}, bf16[512,512]{1,0:T(8,128)(2,1)S(1)}, u32[]{:S(2)}, u32[]{:S(2)}) collective-permute-start(bf16[512,512]{1,0:T(8,128)(2,1)} %refs_6_.3), channel_id=1, source_target_pairs={{0,4},{4,0},{8,12},{12,8},{1,5},{5,1},{9,13},{13,9},{2,6},{6,2},{1... | collective-permute-start | bytes 1572872 | tf_op jit(solution)/shard_map/ppermute | solution.py:566
  3.8 13.7 %collective-permute-start.7 = (bf16[512,512]{1,0:T(8,128)(2,1)}, bf16[512,512]{1,0:T(8,128)(2,1)S(1)}, u32[]{:S(2)}, u32[]{:S(2)}) collective-permute-start(bf16[512,512]{1,0:T(8,128)(2,1)} %first_b.1), channel_id=1, source_target_pairs={{4,8},{8,4},{5,9},{9,5},{6,10},{10,6},{7,11},{11,7},{20,24},{24,20... | collective-permute-start | bytes 1572872 | tf_op jit(solution)/shard_map/ppermute | solution.py:566
  4.5 14.4 %collective-permute-start.10 = (bf16[512,512]{1,0:T(8,128)(2,1)}, bf16[512,512]{1,0:T(8,128)(2,1)S(1)}, u32[]{:S(2)}, u32[]{:S(2)}) collective-permute-start(bf16[512,512]{1,0:T(8,128)(2,1)} %first_b.1), channel_id=1, source_target_pairs={{0,2},{2,0},{1,3},{3,1},{4,6},{6,4},{5,7},{7,5},{8,10},{10,8},{9,1... | collective-permute-start | bytes 1572872 | tf_op jit(solution)/shard_map/ppermute | solution.py:19
  6.1 22.0 %collective-permute-start.1 = (bf16[512,512]{1,0:T(8,128)(2,1)}, bf16[512,512]{1,0:T(8,128)(2,1)S(1)}, u32[]{:S(2)}, u32[]{:S(2)}) collective-permute-start(bf16[512,512]{1,0:T(8,128)(2,1)} %first_b.1), channel_id=1, source_target_pairs={{0,4},{4,0},{8,12},{12,8},{1,5},{5,1},{9,13},{13,9},{2,6},{6,2},{1... | collective-permute-start | bytes 1572872 | tf_op jit(solution)/shard_map/ppermute | solution.py:566
  16.8 13.8 %collective-permute-start.5 = (bf16[512,512]{1,0:T(8,128)(2,1)}, bf16[512,512]{1,0:T(8,128)(2,1)S(1)}, u32[]{:S(2)}, u32[]{:S(2)}) collective-permute-start(bf16[512,512]{1,0:T(8,128)(2,1)} %refs_6_.3), channel_id=1, source_target_pairs={{4,8},{8,4},{5,9},{9,5},{6,10},{10,6},{7,11},{11,7},{20,24},{24,20... | collective-permute-start | bytes 1572872 | tf_op jit(solution)/shard_map/ppermute | solution.py:566
  17.5 21.8 %collective-permute-start.8 = (bf16[512,512]{1,0:T(8,128)(2,1)S(1)}, bf16[512,512]{1,0:T(8,128)(2,1)S(1)}, u32[]{:S(2)}, u32[]{:S(2)}) collective-permute-start(bf16[512,512]{1,0:T(8,128)(2,1)S(1)} %collective-permute-done.7.inner), channel_id=1, source_target_pairs={{4,0},{8,12},{5,1},{9,13},{6,2},{10,14},{7,3},{11,15},{20,16},{24,... | collective-permute-start | bytes 1572872 | tf_op jit(solution)/shard_map/ppermute | solution.py:566
  18.8 21.3 %collective-permute-start.12 = (bf16[512,512]{1,0:T(8,128)(2,1)S(1)}, bf16[512,512]{1,0:T(8,128)(2,1)S(1)}, u32[]{:S(2)}, u32[]{:S(2)}) collective-permute-start(bf16[512,512]{1,0:T(8,128)(2,1)S(1)} %collective-permute-done.4.refs_2_), channel_id=1, source_target_pairs={{0,1},{1,0},{2,3},{3,2},{4,5},{5,4},{6,7},{7,6},{8,9},{9,8},{10,11... | collective-permute-start | bytes 1572872 | tf_op jit(solution)/shard_map/ppermute | solution.py:19
  28.0 13.4 %collective-permute-start.11 = (bf16[512,512]{1,0:T(8,128)(2,1)S(1)}, bf16[512,512]{1,0:T(8,128)(2,1)S(1)}, u32[]{:S(2)}, u32[]{:S(2)}) collective-permute-start(bf16[512,512]{1,0:T(8,128)(2,1)S(1)} %collective-permute-done.1.second.refs_8_), channel_id=1, source_target_pairs={{0,2},{2,0},{1,3},{3,1},{4,6},{6,4},{5,7},{7,5},{8,10},{10,8},{9,1... | collective-permute-start | bytes 1572872 | tf_op jit(solution)/shard_map/ppermute | solution.py:19
  29.9 13.0 %collective-permute-start.2 = (bf16[512,512]{1,0:T(8,128)(2,1)S(1)}, bf16[512,512]{1,0:T(8,128)(2,1)S(1)}, u32[]{:S(2)}, u32[]{:S(2)}) collective-permute-start(bf16[512,512]{1,0:T(8,128)(2,1)S(1)} %collective-permute-done.1.second.refs_8_), channel_id=1, source_target_pairs={{4,8},{8,4},{5,9},{9,5},{6,10},{10,6},{7,11},{11,7},{20,24},{24,20... | collective-permute-start | bytes 1572872 | tf_op jit(solution)/shard_map/ppermute | solution.py:566
  30.6 19.9 %collective-permute-start.6 = (bf16[512,512]{1,0:T(8,128)(2,1)S(1)}, bf16[512,512]{1,0:T(8,128)(2,1)S(1)}, u32[]{:S(2)}, u32[]{:S(2)}) collective-permute-start(bf16[512,512]{1,0:T(8,128)(2,1)S(1)} %collective-permute-done.5.inner), channel_id=1, source_target_pairs={{4,0},{8,12},{5,1},{9,13},{6,2},{10,14},{7,3},{11,15},{20,16},{24,... | collective-permute-start | bytes 1572872 | tf_op jit(solution)/shard_map/ppermute | solution.py:566
  39.3 12.7 %collective-permute-start.18 = (bf16[512,512]{1,0:T(8,128)(2,1)S(1)}, bf16[512,512]{1,0:T(8,128)(2,1)S(1)}, u32[]{:S(2)}, u32[]{:S(2)}) collective-permute-start(bf16[512,512]{1,0:T(8,128)(2,1)S(1)} %collective-permute-done.4.refs_2_), channel_id=1, source_target_pairs={{4,8},{8,4},{5,9},{9,5},{6,10},{10,6},{7,11},{11,7},{20,24},{24,20... | collective-permute-start | bytes 1572872 | tf_op jit(solution)/shard_map/ppermute | solution.py:566
  41.5 22.4 %collective-permute-start.13 = (bf16[512,512]{1,0:T(8,128)(2,1)S(1)}, bf16[512,512]{1,0:T(8,128)(2,1)S(1)}, u32[]{:S(2)}, u32[]{:S(2)}) collective-permute-start(bf16[512,512]{1,0:T(8,128)(2,1)S(1)} %shard_map.59.third.refs_10_), channel_id=1, source_target_pairs={{0,2},{2,0},{1,3},{3,1},{4,6},{6,4},{5,7},{7,5},{8,10},{10,8},{9,1... | collective-permute-start | bytes 1572872 | tf_op jit(solution)/shard_map/ppermute | solution.py:19
  43.0 21.0 %copy-start.1 = (bf16[512,512]{1,0:T(8,128)(2,1)S(1)}, bf16[512,512]{1,0:T(8,128)(2,1)}, u32[]{:S(2)}) copy-start(bf16[512,512]{1,0:T(8,128)(2,1)} %refs_6_.3) | copy-start | bytes 1572868
  43.0 13.0 %collective-permute-start.3 = (bf16[256,512]{1,0:T(8,128)(2,1)S(1)}, bf16[256,512]{1,0:T(8,128)(2,1)S(1)}, u32[]{:S(2)}, u32[]{:S(2)}) collective-permute-start(bf16[256,512]{1,0:T(8,128)(2,1)S(1)} %get-tuple-element.50.inner), channel_id=1, source_target_pairs={{4,0},{8,12},{5,1},{9,13},{6,2},{10,14},{7,3},{11,15},{20,16},{24,... | collective-permute-start | bytes 786440 | tf_op jit(solution)/shard_map/ppermute | solution.py:566
  50.6 13.3 %collective-permute-start.15 = (bf16[512,512]{1,0:T(8,128)(2,1)S(1)}, bf16[512,512]{1,0:T(8,128)(2,1)S(1)}, u32[]{:S(2)}, u32[]{:S(2)}) collective-permute-start(bf16[512,512]{1,0:T(8,128)(2,1)S(1)} %shard_map.58.refs_4_), channel_id=1, source_target_pairs={{0,1},{1,0},{2,3},{3,2},{4,5},{5,4},{6,7},{7,6},{8,9},{9,8},{10,11... | collective-permute-start | bytes 1572872 | tf_op jit(solution)/shard_map/ppermute | solution.py:19
  50.7 11.1 %collective-permute-start.9 = (bf16[256,512]{1,0:T(8,128)(2,1)S(1)}, bf16[256,512]{1,0:T(8,128)(2,1)S(1)}, u32[]{:S(2)}, u32[]{:S(2)}) collective-permute-start(bf16[256,512]{1,0:T(8,128)(2,1)S(1)} %get-tuple-element.55.inner), channel_id=1, source_target_pairs={{4,0},{8,12},{5,1},{9,13},{6,2},{10,14},{7,3},{11,15},{20,16},{24,... | collective-permute-start | bytes 786440 | tf_op jit(solution)/shard_map/ppermute | solution.py:566
  52.0 20.7 %collective-permute-start.19 = (bf16[512,512]{1,0:T(8,128)(2,1)S(1)}, bf16[512,512]{1,0:T(8,128)(2,1)S(1)}, u32[]{:S(2)}, u32[]{:S(2)}) collective-permute-start(bf16[512,512]{1,0:T(8,128)(2,1)S(1)} %collective-permute-done.18.inner), channel_id=1, source_target_pairs={{4,0},{8,12},{5,1},{9,13},{6,2},{10,14},{7,3},{11,15},{20,16},{24,... | collective-permute-start | bytes 1572872 | tf_op jit(solution)/shard_map/ppermute | solution.py:566
  56.2 7.8 %collective-permute-start.14 = (bf16[512,256]{1,0:T(8,128)(2,1)S(1)}, bf16[512,256]{1,0:T(8,128)(2,1)S(1)}, u32[]{:S(2)}, u32[]{:S(2)}) collective-permute-start(bf16[512,256]{1,0:T(8,128)(2,1)S(1)} %get-tuple-element.54.refs_0_.late_b_0), channel_id=1, source_target_pairs={{0,2},{2,0},{1,3},{3,1},{4,6},{6,4},{5,7},{7,5},{8,10},{10,8},{9,1... | collective-permute-start | bytes 786440 | tf_op jit(solution)/shard_map/ppermute | solution.py:19
  62.0 8.1 %collective-permute-start.17 = (bf16[544,256]{1,0:T(8,128)(2,1)S(1)}, bf16[544,256]{1,0:T(8,128)(2,1)S(1)}, u32[]{:S(2)}, u32[]{:S(2)}) collective-permute-start(bf16[544,256]{1,0:T(8,128)(2,1)S(1)} %shard_map.62.refs_1_.late_b_1), channel_id=1, source_target_pairs={{0,2},{2,0},{1,3},{3,1},{4,6},{6,4},{5,7},{7,5},{8,10},{10,8},{9,1... | collective-permute-start | bytes 835592 | tf_op jit(solution)/shard_map/ppermute | solution.py:19
  68.0 2.1 %collective-permute-start.16 = (f32[8,512]{1,0:T(8,128)S(1)}, f32[8,512]{1,0:T(8,128)S(1)}, u32[]{:S(2)}, u32[]{:S(2)}) collective-permute-start(f32[8,512]{1,0:T(8,128)S(1)} %get-tuple-element.67), channel_id=1, source_target_pairs={{0,1},{1,0},{2,3},{3,2},{4,5},{5,4},{6,7},{7,6},{8,9},{9,8},{10,11... | collective-permute-start | bytes 49160 | tf_op jit(solution)/shard_map/ppermute | solution.py:19
  73.1 2.0 %collective-permute-start.20 = (bf16[528,512]{1,0:T(8,128)(2,1)S(1)}, bf16[528,512]{1,0:T(8,128)(2,1)S(1)}, u32[]{:S(2)}, u32[]{:S(2)}) collective-permute-start(bf16[528,512]{1,0:T(8,128)(2,1)S(1)} %shard_map.64.late.refs_4_), channel_id=1, source_target_pairs={{0,1},{1,0},{2,3},{3,2},{4,5},{5,4},{6,7},{7,6},{8,9},{9,8},{10,11... | collective-permute-start | bytes 1622024 | tf_op jit(solution)/shard_map/ppermute | solution.py:19
  76.4 1.9 %collective-permute-start.21 = (f32[8,512]{1,0:T(8,128)S(1)}, f32[8,512]{1,0:T(8,128)S(1)}, u32[]{:S(2)}, u32[]{:S(2)}) collective-permute-start(f32[8,512]{1,0:T(8,128)S(1)} %get-tuple-element.80.refs_18_), channel_id=1, source_target_pairs={{0,1},{1,0},{2,3},{3,2},{4,5},{5,4},{6,7},{7,6},{8,9},{9,8},{10,11... | collective-permute-start | bytes 49160 | tf_op jit(solution)/shard_map/ppermute | solution.py:19
  76.6 14.6 %collective-permute-start.23 = (bf16[528,512]{1,0:T(8,128)(2,1)S(1)}, bf16[528,512]{1,0:T(8,128)(2,1)S(1)}, u32[]{:S(2)}, u32[]{:S(2)}) collective-permute-start(bf16[528,512]{1,0:T(8,128)(2,1)S(1)} %get-tuple-element.86), channel_id=1, source_target_pairs={{0,2},{2,0},{1,3},{3,1},{4,6},{6,4},{5,7},{7,5},{8,10},{10,8},{9,1... | collective-permute-start | bytes 1622024 | tf_op jit(solution)/shard_map/ppermute | solution.py:19
  86.0 3.0 %collective-permute-start.22 = (bf16[512,512]{1,0:T(8,128)(2,1)S(1)}, bf16[512,512]{1,0:T(8,128)(2,1)S(1)}, u32[]{:S(2)}, u32[]{:S(2)}) collective-permute-start(bf16[512,512]{1,0:T(8,128)(2,1)S(1)} %get-tuple-element.83), channel_id=1, source_target_pairs={{0,1},{1,0},{2,3},{3,2},{4,5},{5,4},{6,7},{7,6},{8,9},{9,8},{10,11... | collective-permute-start | bytes 1572872 | tf_op jit(solution)/shard_map/ppermute | solution.py:19
  86.0 1.9 %collective-permute-start.24 = (f32[8,128]{1,0:T(8,128)S(1)}, f32[8,128]{1,0:T(8,128)S(1)}, u32[]{:S(2)}, u32[]{:S(2)}) collective-permute-start(f32[8,128]{1,0:T(8,128)S(1)} %get-tuple-element.88), channel_id=1, source_target_pairs={{0,1},{1,0},{2,3},{3,2},{4,5},{5,4},{6,7},{7,6},{8,9},{9,8},{10,11... | collective-permute-start | bytes 12296 | tf_op jit(solution)/shard_map/ppermute | solution.py:19
  87.9 4.4 %collective-permute-start.25 = (f32[8,128]{1,0:T(8,128)S(1)}, f32[8,128]{1,0:T(8,128)S(1)}, u32[]{:S(2)}, u32[]{:S(2)}) collective-permute-start(f32[8,128]{1,0:T(8,128)S(1)} %shard_map.70.one), channel_id=1, source_target_pairs={{0,2},{2,0},{1,3},{3,1},{4,6},{6,4},{5,7},{7,5},{8,10},{10,8},{9,1... | collective-permute-start | bytes 12296 | tf_op jit(solution)/shard_map/ppermute | solution.py:19

commit v14 on v13

--- a/solution.py
+++ b/solution.py
@@ -345,15 +345,17 @@
 
 def partner_kernel(images, part, late, zero, sums, late_b_0, late_b_1, *refs):
     if part:
-        (terms_in, across_in, vec_in, partial_out, e_out, vec_out, left) = refs
+        (terms_in, across_in, vec_in, columns, partial_out, e_out, vec_out, left) = refs
     else:
-        (terms_out, across_out, e_out, vec_out, left) = refs
+        (terms_out, across_out, e_out, vec_out, columns, left) = refs
+        _, rstd_b, _, delta_b = right_stats((late_b_0, late_b_1))
+        columns[...] = jnp.transpose(rows_of([rstd_b / images, delta_b * rstd_b]))
     late_b = (late_b_0, late_b_1)
     rows, quart = zero.shape
     width = quart // 2
     _, rstd, _, delta = joined_rows(late, rows)
     left_operand(zero, late, left, slice(0, quart))
-    scale_col, delta_col = scale_columns(late_b, images)
+    scale_col, delta_col = columns[:, 0:1], columns[:, 1:2]
     across = across_in[...] if part else jnp.zeros((quart, 128), jnp.float32)
     down = []
     for tile in range(2):
@@ -500,10 +502,6 @@
     out[...] = one[...] + other[...]
 
 
-def loss_kernel(feats, one, other, out):
-    out[0] = (one[0, 0] + other[0, 0]) / feats
-
-
 def left_final_kernel(left, from_core, left_out):
     for at in range(0, left.shape[0], 64):
         piece = slice(at, at + 64)
@@ -511,10 +509,11 @@
         left_out[piece, :] = value.astype(jnp.bfloat16)
 
 
-def right_final_kernel(right, from_x, late_b_0, late_b_1, first_b, right_out):
+def right_final_kernel(feats, right, from_x, late_b_0, late_b_1, first_b, loss, x_loss, right_out, loss_out):
     rows = right.shape[0]
     offset, rstd, _, _ = right_stats((late_b_0, late_b_1))
     second = joined_rows(from_x, rows)[0]
+    loss_out[0] = (loss[0, 0] + x_loss[0, 0]) / feats
     for at in range(0, rows, 64):
         piece = slice(at, at + 64)
         xhat = (first_b[piece, :].astype(jnp.float32) - offset) * rstd
@@ -658,7 +657,7 @@
     )
     late_a_other = core_swap(late_a)
 
-    terms, across, e_left, vec_own = local_call(
+    terms, across, e_left, vec_own, columns = local_call(
         functools.partial(partner_kernel, batch_images, 0),
         (late_a, zero_own, partner_own, *late_b_other),
         (
@@ -666,6 +665,7 @@
             across_shape,
             quarter_bf16,
             row_out,
+            jax.ShapeDtypeStruct((quart, 8), jnp.float32),
         ),
         [low(rows + 16, quart)],
         2 * gemm,
@@ -673,7 +673,7 @@
     )
     partial_right, e_right, vec_other = local_call(
         functools.partial(partner_kernel, batch_images, 1),
-        (late_a_other, zero_other, partner_other, *late_b_other, terms, across, vec_own),
+        (late_a_other, zero_other, partner_other, *late_b_other, terms, across, vec_own, columns),
         (extended, quarter_bf16, row_out),
         [low(rows + 16, quart)],
         2 * gemm,
@@ -712,14 +712,10 @@
     x_loss = x_swap(loss)
     (left_gradient,) = local_call(left_final_kernel, (left_own, from_core), (quarter_bf16,))
     right_own, left_gradient = after(right_own, left_gradient)
-    (right_gradient,) = local_call(
-        right_final_kernel, (right_own, from_x, *late_b, right_outputs), (quarter_bf16,)
-    )
-    right_gradient, x_loss = after(right_gradient, x_loss)
-    (loss,) = local_call(
-        functools.partial(loss_kernel, feats),
-        (loss, x_loss),
-        (jax.ShapeDtypeStruct((1,), jnp.float32),),
+    right_gradient, loss = local_call(
+        functools.partial(right_final_kernel, feats),
+        (right_own, from_x, *late_b, right_outputs, loss, x_loss),
+        (quarter_bf16, jax.ShapeDtypeStruct((1,), jnp.float32)),
     )
     return (left_gradient, right_gradient, mine[None, :, :], loss)
 

time: 93.3 us -> 93 us (level)
    pallas_call x15 -> x14, Pallas kernels: 18.8 us -> 18.3 us  [local_call(): pl.pallas_call(kernel, out_shape=list(outs), in_specs=[space(x) for x in...]
  transfers between devices with their start and end apart: 26 -> 26, of which waited for: 13 -> 13; matrix products, arithmetic and copies ran while one was open for 0% -> 0% of each run, Pallas kernels for 18% -> 17%
where the time goes in v14:
time: 93 us; the launch traced here: 92.8 us
  waiting for transfers between devices  44.4 us (48%)
  starting transfers between devices  29 us (31%)
  Pallas kernels  18.3 us (20%)
  between operations  1.02 us (1%)
    ppermute x11, waiting for transfers between devices, along(): return lax.ppermute(block, 'dp', route)  37 us
    pallas_call x14, Pallas kernels, local_call(): pl.pallas_call(kernel, out_shape=list(outs), in_specs=[space(x) for x in...  18.3 us
    ppermute x11, starting transfers between devices, along(): return lax.ppermute(block, 'dp', route)  16.3 us
    ppermute x15, starting transfers between devices, swapped(): return lax.ppermute(block, axis, route)  12.6 us
    ppermute x15, waiting for transfers between devices, swapped(): return lax.ppermute(block, axis, route)  7.39 us
  transfers between devices with their start and end apart: 26, of which 13 were waited for; matrix products, arithmetic and copies ran while one was open for 0% of the time, Pallas kernels for 17%

profile of v14, /device:TPU:0, one launch (start us, length us, event | category | flops | bytes accessed | tf_op | source)
XLA Modules:
  0.0 92.8 jit_solution(6309570534622179873)
XLA Ops:
  1.2 2.7 %collective-permute-start.4 = (bf16[512,512]{1,0:T(8,128)(2,1)}, bf16[512,512]{1,0:T(8,128)(2,1)S(1)}, u32[]{:S(2)}, u32[]{:S(2)}) collective-permute-start(bf16[512,512]{1,0:T(8,128)(2,1)} %refs_6_.3), channel_id=1, source_target_pairs={{0,4},{4,0},{8,12},{12,8},{1,5},{5,1},{9,13},{13,9},{2,6},{6,2},{1... | collective-permute-start | bytes 1572872 | tf_op jit(solution)/shard_map/ppermute | solution.py:565
  4.5 1.6 %collective-permute-start.10 = (bf16[512,512]{1,0:T(8,128)(2,1)}, bf16[512,512]{1,0:T(8,128)(2,1)S(1)}, u32[]{:S(2)}, u32[]{:S(2)}) collective-permute-start(bf16[512,512]{1,0:T(8,128)(2,1)} %first_b.1), channel_id=1, source_target_pairs={{0,2},{2,0},{1,3},{3,1},{4,6},{6,4},{5,7},{7,5},{8,10},{10,8},{9,1... | collective-permute-start | bytes 1572872 | tf_op jit(solution)/shard_map/ppermute | solution.py:19
  6.1 4.4 %collective-permute-start.1 = (bf16[512,512]{1,0:T(8,128)(2,1)}, bf16[512,512]{1,0:T(8,128)(2,1)S(1)}, u32[]{:S(2)}, u32[]{:S(2)}) collective-permute-start(bf16[512,512]{1,0:T(8,128)(2,1)} %first_b.1), channel_id=1, source_target_pairs={{0,4},{4,0},{8,12},{12,8},{1,5},{5,1},{9,13},{13,9},{2,6},{6,2},{1... | collective-permute-start | bytes 1572872 | tf_op jit(solution)/shard_map/ppermute | solution.py:565
  10.5 6.3 %collective-permute-done.4.refs_2_ = bf16[512,512]{1,0:T(8,128)(2,1)S(1)} collective-permute-done((bf16[512,512]{1,0:T(8,128)(2,1)}, bf16[512,512]{1,0:T(8,128)(2,1)S(1)}, u32[]{:S(2)}, u32[]{:S(2)}) %collective-permute-start.4) | collective-permute-done | bytes 524320 | tf_op jit(solution)/shard_map/ppermute | solution.py:565
  17.5 1.3 %collective-permute-start.8 = (bf16[512,512]{1,0:T(8,128)(2,1)S(1)}, bf16[512,512]{1,0:T(8,128)(2,1)S(1)}, u32[]{:S(2)}, u32[]{:S(2)}) collective-permute-start(bf16[512,512]{1,0:T(8,128)(2,1)S(1)} %collective-permute-done.7.inner), channel_id=1, source_target_pairs={{4,0},{8,12},{5,1},{9,13},{6,2},{10,14},{7,3},{11,15},{20,16},{24,... | collective-permute-start | bytes 1572872 | tf_op jit(solution)/shard_map/ppermute | solution.py:565
  18.9 9.1 %collective-permute-done.1.second.refs_8_ = bf16[512,512]{1,0:T(8,128)(2,1)S(1)} collective-permute-done((bf16[512,512]{1,0:T(8,128)(2,1)}, bf16[512,512]{1,0:T(8,128)(2,1)S(1)}, u32[]{:S(2)}, u32[]{:S(2)}) %collective-permute-start.1) | collective-permute-done | bytes 524320 | tf_op jit(solution)/shard_map/ppermute | solution.py:565
  28.0 1.9 %collective-permute-start.11 = (bf16[512,512]{1,0:T(8,128)(2,1)S(1)}, bf16[512,512]{1,0:T(8,128)(2,1)S(1)}, u32[]{:S(2)}, u32[]{:S(2)}) collective-permute-start(bf16[512,512]{1,0:T(8,128)(2,1)S(1)} %collective-permute-done.1.second.refs_8_), channel_id=1, source_target_pairs={{0,2},{2,0},{1,3},{3,1},{4,6},{6,4},{5,7},{7,5},{8,10},{10,8},{9,1... | collective-permute-start | bytes 1572872 | tf_op jit(solution)/shard_map/ppermute | solution.py:19
  30.6 1.3 %collective-permute-start.6 = (bf16[512,512]{1,0:T(8,128)(2,1)S(1)}, bf16[512,512]{1,0:T(8,128)(2,1)S(1)}, u32[]{:S(2)}, u32[]{:S(2)}) collective-permute-start(bf16[512,512]{1,0:T(8,128)(2,1)S(1)} %collective-permute-done.5.inner), channel_id=1, source_target_pairs={{4,0},{8,12},{5,1},{9,13},{6,2},{10,14},{7,3},{11,15},{20,16},{24,... | collective-permute-start | bytes 1572872 | tf_op jit(solution)/shard_map/ppermute | solution.py:565
  31.9 7.4 %collective-permute-done.8.outer = bf16[512,512]{1,0:T(8,128)(2,1)S(1)} collective-permute-done((bf16[512,512]{1,0:T(8,128)(2,1)S(1)}, bf16[512,512]{1,0:T(8,128)(2,1)S(1)}, u32[]{:S(2)}, u32[]{:S(2)}) %collective-permute-start.8) | collective-permute-done | bytes 524320 | tf_op jit(solution)/shard_map/ppermute | solution.py:565
  40.1 1.4 %collective-permute-done.11.refs_9_ = bf16[512,512]{1,0:T(8,128)(2,1)S(1)} collective-permute-done((bf16[512,512]{1,0:T(8,128)(2,1)S(1)}, bf16[512,512]{1,0:T(8,128)(2,1)S(1)}, u32[]{:S(2)}, u32[]{:S(2)}) %collective-permute-start.11) | collective-permute-done | bytes 524320 | tf_op jit(solution)/shard_map/ppermute | solution.py:19
  41.5 1.5 %collective-permute-start.13 = (bf16[512,512]{1,0:T(8,128)(2,1)S(1)}, bf16[512,512]{1,0:T(8,128)(2,1)S(1)}, u32[]{:S(2)}, u32[]{:S(2)}) collective-permute-start(bf16[512,512]{1,0:T(8,128)(2,1)S(1)} %shard_map.59.third.refs_10_), channel_id=1, source_target_pairs={{0,2},{2,0},{1,3},{3,1},{4,6},{6,4},{5,7},{7,5},{8,10},{10,8},{9,1... | collective-permute-start | bytes 1572872 | tf_op jit(solution)/shard_map/ppermute | solution.py:19
  43.0 1.4 %collective-permute-start.3 = (bf16[256,512]{1,0:T(8,128)(2,1)S(1)}, bf16[256,512]{1,0:T(8,128)(2,1)S(1)}, u32[]{:S(2)}, u32[]{:S(2)}) collective-permute-start(bf16[256,512]{1,0:T(8,128)(2,1)S(1)} %get-tuple-element.51.inner), channel_id=1, source_target_pairs={{4,0},{8,12},{5,1},{9,13},{6,2},{10,14},{7,3},{11,15},{20,16},{24,... | collective-permute-start | bytes 786440 | tf_op jit(solution)/shard_map/ppermute | solution.py:565
  44.4 1.0 %shard_map.60.row = f32[8,512]{1,0:T(8,128)S(1)} custom-call(bf16[512,512]{1,0:T(8,128)(2,1)S(1)} %copy-done, bf16[512,512]{1,0:T(8,128)(2,1)S(1)} %collective-permute-done.1.second.refs_8_, bf16[512,512]{1,0:T(8,128)(2,1)S(1)} %shard_map.59.third.refs_10_), custom_call_target="tpu_custom_call" | custom-call | flops 1048576 | bytes 1589248 | tf_op jit(solution)/shard_map/pallas_call | solution.py:535
  45.4 5.1 %collective-permute-done.6.outer = bf16[512,512]{1,0:T(8,128)(2,1)S(1)} collective-permute-done((bf16[512,512]{1,0:T(8,128)(2,1)S(1)}, bf16[512,512]{1,0:T(8,128)(2,1)S(1)}, u32[]{:S(2)}, u32[]{:S(2)}) %collective-permute-start.6) | collective-permute-done | bytes 524320 | tf_op jit(solution)/shard_map/ppermute | solution.py:565
  50.7 1.3 %collective-permute-start.9 = (bf16[256,512]{1,0:T(8,128)(2,1)S(1)}, bf16[256,512]{1,0:T(8,128)(2,1)S(1)}, u32[]{:S(2)}, u32[]{:S(2)}) collective-permute-start(bf16[256,512]{1,0:T(8,128)(2,1)S(1)} %get-tuple-element.56.inner), channel_id=1, source_target_pairs={{4,0},{8,12},{5,1},{9,13},{6,2},{10,14},{7,3},{11,15},{20,16},{24,... | collective-permute-start | bytes 786440 | tf_op jit(solution)/shard_map/ppermute | solution.py:565
  52.0 1.3 %collective-permute-start.19 = (bf16[512,512]{1,0:T(8,128)(2,1)S(1)}, bf16[512,512]{1,0:T(8,128)(2,1)S(1)}, u32[]{:S(2)}, u32[]{:S(2)}) collective-permute-start(bf16[512,512]{1,0:T(8,128)(2,1)S(1)} %collective-permute-done.18.inner), channel_id=1, source_target_pairs={{4,0},{8,12},{5,1},{9,13},{6,2},{10,14},{7,3},{11,15},{20,16},{24,... | collective-permute-start | bytes 1572872 | tf_op jit(solution)/shard_map/ppermute | solution.py:565
  53.3 2.7 %collective-permute-done.3.outer = bf16[256,512]{1,0:T(8,128)(2,1)S(1)} collective-permute-done((bf16[256,512]{1,0:T(8,128)(2,1)S(1)}, bf16[256,512]{1,0:T(8,128)(2,1)S(1)}, u32[]{:S(2)}, u32[]{:S(2)}) %collective-permute-start.3) | collective-permute-done | bytes 262176 | tf_op jit(solution)/shard_map/ppermute | solution.py:565
  56.2 1.6 %collective-permute-start.14 = (bf16[512,256]{1,0:T(8,128)(2,1)S(1)}, bf16[512,256]{1,0:T(8,128)(2,1)S(1)}, u32[]{:S(2)}, u32[]{:S(2)}) collective-permute-start(bf16[512,256]{1,0:T(8,128)(2,1)S(1)} %get-tuple-element.55.refs_0_.late_b_0), channel_id=1, source_target_pairs={{0,2},{2,0},{1,3},{3,1},{4,6},{6,4},{5,7},{7,5},{8,10},{10,8},{9,1... | collective-permute-start | bytes 786440 | tf_op jit(solution)/shard_map/ppermute | solution.py:19
  57.8 4.0 %collective-permute-done.9.outer = bf16[256,512]{1,0:T(8,128)(2,1)S(1)} collective-permute-done((bf16[256,512]{1,0:T(8,128)(2,1)S(1)}, bf16[256,512]{1,0:T(8,128)(2,1)S(1)}, u32[]{:S(2)}, u32[]{:S(2)}) %collective-permute-start.9) | collective-permute-done | bytes 262176 | tf_op jit(solution)/shard_map/ppermute | solution.py:565
  62.0 1.9 %collective-permute-start.17 = (bf16[544,256]{1,0:T(8,128)(2,1)S(1)}, bf16[544,256]{1,0:T(8,128)(2,1)S(1)}, u32[]{:S(2)}, u32[]{:S(2)}) collective-permute-start(bf16[544,256]{1,0:T(8,128)(2,1)S(1)} %shard_map.62.refs_1_.late_b_1), channel_id=1, source_target_pairs={{0,2},{2,0},{1,3},{3,1},{4,6},{6,4},{5,7},{7,5},{8,10},{10,8},{9,1... | collective-permute-start | bytes 835592 | tf_op jit(solution)/shard_map/ppermute | solution.py:19
  64.0 4.1 %shard_map.63 = (f32[512,512]{1,0:T(8,128)S(1)}, f32[512,512]{1,0:T(8,128)S(1)}, f32[512,1024]{1,0:T(8,128)S(1)}, f32[8,512]{1,0:T(8,128)S(1)}, bf16[512,512]{1,...) custom-call(bf16[512,512]{1,0:T(8,128)(2,1)S(1)} %copy-done.1, bf16[512,512]{1,0:T(8,128)(2,1)S(1)} %collective-permute-done.refs_1_.refs_7_, ...), custom_call_target="tpu_custom_call" | custom-call | flops 1048576 | bytes 65536 | tf_op jit(solution)/shard_map/pallas_call | solution.py:535
  68.1 2.0 %collective-permute-done.17.late_b_1.refs_3_ = bf16[544,256]{1,0:T(8,128)(2,1)S(1)} collective-permute-done((bf16[544,256]{1,0:T(8,128)(2,1)S(1)}, bf16[544,256]{1,0:T(8,128)(2,1)S(1)}, u32[]{:S(2)}, u32[]{:S(2)}) %collective-permute-start.17) | collective-permute-done | bytes 278560 | tf_op jit(solution)/shard_map/ppermute | solution.py:19
  70.2 2.6 %collective-permute-done.19.outer = bf16[512,512]{1,0:T(8,128)(2,1)S(1)} collective-permute-done((bf16[512,512]{1,0:T(8,128)(2,1)S(1)}, bf16[512,512]{1,0:T(8,128)(2,1)S(1)}, u32[]{:S(2)}, u32[]{:S(2)}) %collective-permute-start.19) | collective-permute-done | bytes 524320 | tf_op jit(solution)/shard_map/ppermute | solution.py:565
  73.2 1.1 %shard_map.65 = (f32[528,512]{1,0:T(8,128)S(1)}, f32[512,128]{1,0:T(8,128)S(1)}, bf16[512,512]{1,0:T(8,128)(2,1)S(1)}, f32[8,512]{1,0:T(8,128)S(1)}, f32[512,8]{1,0:T(8,128)S(1)}) custom-call(bf16[528,512]{1,0:T(8,128)(2,1)S(1)} %shard_map.64.late.refs_4_, bf16[512,512]{1,0:T(8,128)(2,1)S(1)} %get-tuple-element.71.zero.refs_8_, ...), custom_call_target="tpu_custom_call" | custom-call | flops 536870912 | bytes 4554752 | tf_op jit(solution)/shard_map/pallas_call | solution.py:535
  75.1 1.3 %shard_map.66 = (bf16[528,512]{1,0:T(8,128)(2,1)S(1)}, bf16[512,512]{1,0:T(8,128)(2,1)S(1)}, f32[8,512]{1,0:T(8,128)S(1)}) custom-call(bf16[528,512]{1,0:T(8,128)(2,1)S(1)} %collective-permute-done.20.late.refs_5_, bf16[512,512]{1,0:T(8,128)(2,1)S(1)} %get-tuple-element.72.zero.refs_9_, f32[512,512]{1,0:T(8,128)S(1)} %get-tuple-element.76.sums.refs_16_, ...), custom_call_target="tpu_custom_call" | custom-call | flops 536870912 | bytes 5111808 | tf_op jit(solution)/shard_map/pallas_call | solution.py:535
  76.6 1.7 %collective-permute-start.23 = (bf16[528,512]{1,0:T(8,128)(2,1)S(1)}, bf16[528,512]{1,0:T(8,128)(2,1)S(1)}, u32[]{:S(2)}, u32[]{:S(2)}) collective-permute-start(bf16[528,512]{1,0:T(8,128)(2,1)S(1)} %get-tuple-element.88), channel_id=1, source_target_pairs={{0,2},{2,0},{1,3},{3,1},{4,6},{6,4},{5,7},{7,5},{8,10},{10,8},{9,1... | collective-permute-start | bytes 1622024 | tf_op jit(solution)/shard_map/ppermute | solution.py:19
  78.3 7.6 %shard_map.67 = (f32[512,512]{1,0:T(8,128)S(1)}, f32[512,512]{1,0:T(8,128)S(1)}, bf16[512,512]{1,0:T(8,128)(2,1)S(1)}, f32[256,1024]{1,0:T(8,128)}, f32[8,128]{1,0:T(8,128)S(1)}, /*index=5*/f32[8,128]{1,0:T(8,128)S(1)}) custom-call(s32[2]{0:T(128)S(1)} %pad_add_fusion.flags, bf16[512,256]{1,0:T(8,128)(2,1)S(1)} %get-tuple-element.55.refs_0_.late_b_0, ...), custom_call_target="tpu_custom_call" | custom-call | flops 2147483648 | bytes 14278664 | tf_op jit(solution)/shard_map/pallas_call | solution.py:535
  86.4 1.4 %collective-permute-done.24.other = f32[8,128]{1,0:T(8,128)S(1)} collective-permute-done((f32[8,128]{1,0:T(8,128)S(1)}, f32[8,128]{1,0:T(8,128)S(1)}, u32[]{:S(2)}, u32[]{:S(2)}) %collective-permute-start.24) | collective-permute-done | bytes 4128 | tf_op jit(solution)/shard_map/ppermute | solution.py:19
  87.9 1.0 %collective-permute-start.25 = (f32[8,128]{1,0:T(8,128)S(1)}, f32[8,128]{1,0:T(8,128)S(1)}, u32[]{:S(2)}, u32[]{:S(2)}) collective-permute-start(f32[8,128]{1,0:T(8,128)S(1)} %shard_map.69.loss), channel_id=1, source_target_pairs={{0,2},{2,0},{1,3},{3,1},{4,6},{6,4},{5,7},{7,5},{8,10},{10,8},{9,1... | collective-permute-start | bytes 12296 | tf_op jit(solution)/shard_map/ppermute | solution.py:19
  88.9 0.9 shard_map.68
  89.8 1.7 %collective-permute-done.25.x_loss = f32[8,128]{1,0:T(8,128)S(1)} collective-permute-done((f32[8,128]{1,0:T(8,128)S(1)}, f32[8,128]{1,0:T(8,128)S(1)}, u32[]{:S(2)}, u32[]{:S(2)}) %collective-permute-start.25) | collective-permute-done | bytes 4128 | tf_op jit(solution)/shard_map/ppermute | solution.py:19
  91.5 1.1 %shard_map.70 = (bf16[512,512]{1,0:T(8,128)(2,1)}, f32[1]{0:T(128)}) custom-call(f32[512,512]{1,0:T(8,128)S(1)} %get-tuple-element.87.right, bf16[528,512]{1,0:T(8,128)(2,1)S(1)} %collective-permute-done.23.from_x, bf16[512,256]{1,0:T(8,128)(2,1)S(1)} %get-tuple-element.55.refs_0_.late_b_0, bf16[544,256]{1,0:T(8,128)(2,1)S(1)} %shard_map.62.refs_1_.late_b_1, ...), custom_call_target="tpu_custom_call" | custom-call | flops 1048576 | bytes 3186692 | tf_op jit(solution)/shard_map/pallas_call | solution.py:535
  (40 shorter events, 6.4 us)
Async XLA Ops:
  0.6 43.8 %copy-start = (bf16[512,512]{1,0:T(8,128)(2,1)S(1)}, bf16[512,512]{1,0:T(8,128)(2,1)}, u32[]{:S(2)}) copy-start(bf16[512,512]{1,0:T(8,128)(2,1)} %first_b.1) | copy-start | bytes 1572868
  0.6 9.9 %collective-permute-start = (bf16[512,512]{1,0:T(8,128)(2,1)}, bf16[512,512]{1,0:T(8,128)(2,1)S(1)}, u32[]{:S(2)}, u32[]{:S(2)}) collective-permute-start(bf16[512,512]{1,0:T(8,128)(2,1)} %refs_6_.3), channel_id=1, source_target_pairs={{0,1},{1,0},{2,3},{3,2},{4,5},{5,4},{6,7},{7,6},{8,9},{9,8},{10,11... | collective-permute-start | bytes 1572872 | tf_op jit(solution)/shard_map/ppermute | solution.py:19
  1.2 15.6 %collective-permute-start.4 = (bf16[512,512]{1,0:T(8,128)(2,1)}, bf16[512,512]{1,0:T(8,128)(2,1)S(1)}, u32[]{:S(2)}, u32[]{:S(2)}) collective-permute-start(bf16[512,512]{1,0:T(8,128)(2,1)} %refs_6_.3), channel_id=1, source_target_pairs={{0,4},{4,0},{8,12},{12,8},{1,5},{5,1},{9,13},{13,9},{2,6},{6,2},{1... | collective-permute-start | bytes 1572872 | tf_op jit(solution)/shard_map/ppermute | solution.py:565
  3.8 13.7 %collective-permute-start.7 = (bf16[512,512]{1,0:T(8,128)(2,1)}, bf16[512,512]{1,0:T(8,128)(2,1)S(1)}, u32[]{:S(2)}, u32[]{:S(2)}) collective-permute-start(bf16[512,512]{1,0:T(8,128)(2,1)} %first_b.1), channel_id=1, source_target_pairs={{4,8},{8,4},{5,9},{9,5},{6,10},{10,6},{7,11},{11,7},{20,24},{24,20... | collective-permute-start | bytes 1572872 | tf_op jit(solution)/shard_map/ppermute | solution.py:565
  4.5 14.4 %collective-permute-start.10 = (bf16[512,512]{1,0:T(8,128)(2,1)}, bf16[512,512]{1,0:T(8,128)(2,1)S(1)}, u32[]{:S(2)}, u32[]{:S(2)}) collective-permute-start(bf16[512,512]{1,0:T(8,128)(2,1)} %first_b.1), channel_id=1, source_target_pairs={{0,2},{2,0},{1,3},{3,1},{4,6},{6,4},{5,7},{7,5},{8,10},{10,8},{9,1... | collective-permute-start | bytes 1572872 | tf_op jit(solution)/shard_map/ppermute | solution.py:19
  6.1 22.0 %collective-permute-start.1 = (bf16[512,512]{1,0:T(8,128)(2,1)}, bf16[512,512]{1,0:T(8,128)(2,1)S(1)}, u32[]{:S(2)}, u32[]{:S(2)}) collective-permute-start(bf16[512,512]{1,0:T(8,128)(2,1)} %first_b.1), channel_id=1, source_target_pairs={{0,4},{4,0},{8,12},{12,8},{1,5},{5,1},{9,13},{13,9},{2,6},{6,2},{1... | collective-permute-start | bytes 1572872 | tf_op jit(solution)/shard_map/ppermute | solution.py:565
  16.8 13.8 %collective-permute-start.5 = (bf16[512,512]{1,0:T(8,128)(2,1)}, bf16[512,512]{1,0:T(8,128)(2,1)S(1)}, u32[]{:S(2)}, u32[]{:S(2)}) collective-permute-start(bf16[512,512]{1,0:T(8,128)(2,1)} %refs_6_.3), channel_id=1, source_target_pairs={{4,8},{8,4},{5,9},{9,5},{6,10},{10,6},{7,11},{11,7},{20,24},{24,20... | collective-permute-start | bytes 1572872 | tf_op jit(solution)/shard_map/ppermute | solution.py:565
  17.5 21.8 %collective-permute-start.8 = (bf16[512,512]{1,0:T(8,128)(2,1)S(1)}, bf16[512,512]{1,0:T(8,128)(2,1)S(1)}, u32[]{:S(2)}, u32[]{:S(2)}) collective-permute-start(bf16[512,512]{1,0:T(8,128)(2,1)S(1)} %collective-permute-done.7.inner), channel_id=1, source_target_pairs={{4,0},{8,12},{5,1},{9,13},{6,2},{10,14},{7,3},{11,15},{20,16},{24,... | collective-permute-start | bytes 1572872 | tf_op jit(solution)/shard_map/ppermute | solution.py:565
  18.8 21.3 %collective-permute-start.12 = (bf16[512,512]{1,0:T(8,128)(2,1)S(1)}, bf16[512,512]{1,0:T(8,128)(2,1)S(1)}, u32[]{:S(2)}, u32[]{:S(2)}) collective-permute-start(bf16[512,512]{1,0:T(8,128)(2,1)S(1)} %collective-permute-done.4.refs_2_), channel_id=1, source_target_pairs={{0,1},{1,0},{2,3},{3,2},{4,5},{5,4},{6,7},{7,6},{8,9},{9,8},{10,11... | collective-permute-start | bytes 1572872 | tf_op jit(solution)/shard_map/ppermute | solution.py:19
  28.0 13.4 %collective-permute-start.11 = (bf16[512,512]{1,0:T(8,128)(2,1)S(1)}, bf16[512,512]{1,0:T(8,128)(2,1)S(1)}, u32[]{:S(2)}, u32[]{:S(2)}) collective-permute-start(bf16[512,512]{1,0:T(8,128)(2,1)S(1)} %collective-permute-done.1.second.refs_8_), channel_id=1, source_target_pairs={{0,2},{2,0},{1,3},{3,1},{4,6},{6,4},{5,7},{7,5},{8,10},{10,8},{9,1... | collective-permute-start | bytes 1572872 | tf_op jit(solution)/shard_map/ppermute | solution.py:19
  29.9 13.0 %collective-permute-start.2 = (bf16[512,512]{1,0:T(8,128)(2,1)S(1)}, bf16[512,512]{1,0:T(8,128)(2,1)S(1)}, u32[]{:S(2)}, u32[]{:S(2)}) collective-permute-start(bf16[512,512]{1,0:T(8,128)(2,1)S(1)} %collective-permute-done.1.second.refs_8_), channel_id=1, source_target_pairs={{4,8},{8,4},{5,9},{9,5},{6,10},{10,6},{7,11},{11,7},{20,24},{24,20... | collective-permute-start | bytes 1572872 | tf_op jit(solution)/shard_map/ppermute | solution.py:565
  30.6 19.9 %collective-permute-start.6 = (bf16[512,512]{1,0:T(8,128)(2,1)S(1)}, bf16[512,512]{1,0:T(8,128)(2,1)S(1)}, u32[]{:S(2)}, u32[]{:S(2)}) collective-permute-start(bf16[512,512]{1,0:T(8,128)(2,1)S(1)} %collective-permute-done.5.inner), channel_id=1, source_target_pairs={{4,0},{8,12},{5,1},{9,13},{6,2},{10,14},{7,3},{11,15},{20,16},{24,... | collective-permute-start | bytes 1572872 | tf_op jit(solution)/shard_map/ppermute | solution.py:565
  39.3 12.7 %collective-permute-start.18 = (bf16[512,512]{1,0:T(8,128)(2,1)S(1)}, bf16[512,512]{1,0:T(8,128)(2,1)S(1)}, u32[]{:S(2)}, u32[]{:S(2)}) collective-permute-start(bf16[512,512]{1,0:T(8,128)(2,1)S(1)} %collective-permute-done.4.refs_2_), channel_id=1, source_target_pairs={{4,8},{8,4},{5,9},{9,5},{6,10},{10,6},{7,11},{11,7},{20,24},{24,20... | collective-permute-start | bytes 1572872 | tf_op jit(solution)/shard_map/ppermute | solution.py:565
  41.5 22.4 %collective-permute-start.13 = (bf16[512,512]{1,0:T(8,128)(2,1)S(1)}, bf16[512,512]{1,0:T(8,128)(2,1)S(1)}, u32[]{:S(2)}, u32[]{:S(2)}) collective-permute-start(bf16[512,512]{1,0:T(8,128)(2,1)S(1)} %shard_map.59.third.refs_10_), channel_id=1, source_target_pairs={{0,2},{2,0},{1,3},{3,1},{4,6},{6,4},{5,7},{7,5},{8,10},{10,8},{9,1... | collective-permute-start | bytes 1572872 | tf_op jit(solution)/shard_map/ppermute | solution.py:19
  43.0 21.0 %copy-start.1 = (bf16[512,512]{1,0:T(8,128)(2,1)S(1)}, bf16[512,512]{1,0:T(8,128)(2,1)}, u32[]{:S(2)}) copy-start(bf16[512,512]{1,0:T(8,128)(2,1)} %refs_6_.3) | copy-start | bytes 1572868
  43.0 13.0 %collective-permute-start.3 = (bf16[256,512]{1,0:T(8,128)(2,1)S(1)}, bf16[256,512]{1,0:T(8,128)(2,1)S(1)}, u32[]{:S(2)}, u32[]{:S(2)}) collective-permute-start(bf16[256,512]{1,0:T(8,128)(2,1)S(1)} %get-tuple-element.51.inner), channel_id=1, source_target_pairs={{4,0},{8,12},{5,1},{9,13},{6,2},{10,14},{7,3},{11,15},{20,16},{24,... | collective-permute-start | bytes 786440 | tf_op jit(solution)/shard_map/ppermute | solution.py:565
  50.6 13.3 %collective-permute-start.15 = (bf16[512,512]{1,0:T(8,128)(2,1)S(1)}, bf16[512,512]{1,0:T(8,128)(2,1)S(1)}, u32[]{:S(2)}, u32[]{:S(2)}) collective-permute-start(bf16[512,512]{1,0:T(8,128)(2,1)S(1)} %shard_map.58.refs_4_), channel_id=1, source_target_pairs={{0,1},{1,0},{2,3},{3,2},{4,5},{5,4},{6,7},{7,6},{8,9},{9,8},{10,11... | collective-permute-start | bytes 1572872 | tf_op jit(solution)/shard_map/ppermute | solution.py:19
  50.7 11.1 %collective-permute-start.9 = (bf16[256,512]{1,0:T(8,128)(2,1)S(1)}, bf16[256,512]{1,0:T(8,128)(2,1)S(1)}, u32[]{:S(2)}, u32[]{:S(2)}) collective-permute-start(bf16[256,512]{1,0:T(8,128)(2,1)S(1)} %get-tuple-element.56.inner), channel_id=1, source_target_pairs={{4,0},{8,12},{5,1},{9,13},{6,2},{10,14},{7,3},{11,15},{20,16},{24,... | collective-permute-start | bytes 786440 | tf_op jit(solution)/shard_map/ppermute | solution.py:565
  52.0 20.7 %collective-permute-start.19 = (bf16[512,512]{1,0:T(8,128)(2,1)S(1)}, bf16[512,512]{1,0:T(8,128)(2,1)S(1)}, u32[]{:S(2)}, u32[]{:S(2)}) collective-permute-start(bf16[512,512]{1,0:T(8,128)(2,1)S(1)} %collective-permute-done.18.inner), channel_id=1, source_target_pairs={{4,0},{8,12},{5,1},{9,13},{6,2},{10,14},{7,3},{11,15},{20,16},{24,... | collective-permute-start | bytes 1572872 | tf_op jit(solution)/shard_map/ppermute | solution.py:565
  56.2 7.8 %collective-permute-start.14 = (bf16[512,256]{1,0:T(8,128)(2,1)S(1)}, bf16[512,256]{1,0:T(8,128)(2,1)S(1)}, u32[]{:S(2)}, u32[]{:S(2)}) collective-permute-start(bf16[512,256]{1,0:T(8,128)(2,1)S(1)} %get-tuple-element.55.refs_0_.late_b_0), channel_id=1, source_target_pairs={{0,2},{2,0},{1,3},{3,1},{4,6},{6,4},{5,7},{7,5},{8,10},{10,8},{9,1... | collective-permute-start | bytes 786440 | tf_op jit(solution)/shard_map/ppermute | solution.py:19
  62.0 8.1 %collective-permute-start.17 = (bf16[544,256]{1,0:T(8,128)(2,1)S(1)}, bf16[544,256]{1,0:T(8,128)(2,1)S(1)}, u32[]{:S(2)}, u32[]{:S(2)}) collective-permute-start(bf16[544,256]{1,0:T(8,128)(2,1)S(1)} %shard_map.62.refs_1_.late_b_1), channel_id=1, source_target_pairs={{0,2},{2,0},{1,3},{3,1},{4,6},{6,4},{5,7},{7,5},{8,10},{10,8},{9,1... | collective-permute-start | bytes 835592 | tf_op jit(solution)/shard_map/ppermute | solution.py:19
  68.0 2.1 %collective-permute-start.16 = (f32[8,512]{1,0:T(8,128)S(1)}, f32[8,512]{1,0:T(8,128)S(1)}, u32[]{:S(2)}, u32[]{:S(2)}) collective-permute-start(f32[8,512]{1,0:T(8,128)S(1)} %get-tuple-element.68), channel_id=1, source_target_pairs={{0,1},{1,0},{2,3},{3,2},{4,5},{5,4},{6,7},{7,6},{8,9},{9,8},{10,11... | collective-permute-start | bytes 49160 | tf_op jit(solution)/shard_map/ppermute | solution.py:19
  73.1 2.0 %collective-permute-start.20 = (bf16[528,512]{1,0:T(8,128)(2,1)S(1)}, bf16[528,512]{1,0:T(8,128)(2,1)S(1)}, u32[]{:S(2)}, u32[]{:S(2)}) collective-permute-start(bf16[528,512]{1,0:T(8,128)(2,1)S(1)} %shard_map.64.late.refs_4_), channel_id=1, source_target_pairs={{0,1},{1,0},{2,3},{3,2},{4,5},{5,4},{6,7},{7,6},{8,9},{9,8},{10,11... | collective-permute-start | bytes 1622024 | tf_op jit(solution)/shard_map/ppermute | solution.py:19
  76.4 1.9 %collective-permute-start.21 = (f32[8,512]{1,0:T(8,128)S(1)}, f32[8,512]{1,0:T(8,128)S(1)}, u32[]{:S(2)}, u32[]{:S(2)}) collective-permute-start(f32[8,512]{1,0:T(8,128)S(1)} %get-tuple-element.82.refs_18_), channel_id=1, source_target_pairs={{0,1},{1,0},{2,3},{3,2},{4,5},{5,4},{6,7},{7,6},{8,9},{9,8},{10,11... | collective-permute-start | bytes 49160 | tf_op jit(solution)/shard_map/ppermute | solution.py:19
  76.6 14.9 %collective-permute-start.23 = (bf16[528,512]{1,0:T(8,128)(2,1)S(1)}, bf16[528,512]{1,0:T(8,128)(2,1)S(1)}, u32[]{:S(2)}, u32[]{:S(2)}) collective-permute-start(bf16[528,512]{1,0:T(8,128)(2,1)S(1)} %get-tuple-element.88), channel_id=1, source_target_pairs={{0,2},{2,0},{1,3},{3,1},{4,6},{6,4},{5,7},{7,5},{8,10},{10,8},{9,1... | collective-permute-start | bytes 1622024 | tf_op jit(solution)/shard_map/ppermute | solution.py:19
  85.9 2.9 %collective-permute-start.22 = (bf16[512,512]{1,0:T(8,128)(2,1)S(1)}, bf16[512,512]{1,0:T(8,128)(2,1)S(1)}, u32[]{:S(2)}, u32[]{:S(2)}) collective-permute-start(bf16[512,512]{1,0:T(8,128)(2,1)S(1)} %get-tuple-element.85), channel_id=1, source_target_pairs={{0,1},{1,0},{2,3},{3,2},{4,5},{5,4},{6,7},{7,6},{8,9},{9,8},{10,11... | collective-permute-start | bytes 1572872 | tf_op jit(solution)/shard_map/ppermute | solution.py:19
  86.0 1.9 %collective-permute-start.24 = (f32[8,128]{1,0:T(8,128)S(1)}, f32[8,128]{1,0:T(8,128)S(1)}, u32[]{:S(2)}, u32[]{:S(2)}) collective-permute-start(f32[8,128]{1,0:T(8,128)S(1)} %get-tuple-element.90), channel_id=1, source_target_pairs={{0,1},{1,0},{2,3},{3,2},{4,5},{5,4},{6,7},{7,6},{8,9},{9,8},{10,11... | collective-permute-start | bytes 12296 | tf_op jit(solution)/shard_map/ppermute | solution.py:19
  87.9 3.6 %collective-permute-start.25 = (f32[8,128]{1,0:T(8,128)S(1)}, f32[8,128]{1,0:T(8,128)S(1)}, u32[]{:S(2)}, u32[]{:S(2)}) collective-permute-start(f32[8,128]{1,0:T(8,128)S(1)} %shard_map.69.loss), channel_id=1, source_target_pairs={{0,2},{2,0},{1,3},{3,1},{4,6},{6,4},{5,7},{7,5},{8,10},{10,8},{9,1... | collective-permute-start | bytes 12296 | tf_op jit(solution)/shard_map/ppermute | solution.py:19

commit v15 on v14

--- a/solution.py
+++ b/solution.py
@@ -345,7 +345,8 @@
 
 def partner_kernel(images, part, late, zero, sums, late_b_0, late_b_1, *refs):
     if part:
-        (terms_in, across_in, vec_in, columns, partial_out, e_out, vec_out, left) = refs
+        (terms_in, across_in, vec_in, columns) = refs[:4]
+        (partial_out, second_out, e_out, vec_out, left) = refs[4:]
     else:
         (terms_out, across_out, e_out, vec_out, columns, left) = refs
         _, rstd_b, _, delta_b = right_stats((late_b_0, late_b_1))
@@ -369,9 +370,7 @@
     second_a = off_weight * jnp.concatenate(down, axis=1)
     if part:
         vec_out[...] = rows_of([second_a, second_a + vec_in[0:1, :]])
-        nothing = jnp.zeros((1, quart), jnp.float32)
-        second = off_weight * lanes_to_row(across)
-        partial_out[rows:, :] = split_rows([second, nothing, nothing, nothing])
+        second_out[...] = rows_of([off_weight * lanes_to_row(across)])
     else:
         vec_out[...] = rows_of([second_a])
         across_out[...] = across
@@ -379,7 +378,7 @@
         at = slice(tile * width, (tile + 1) * width)
         terms = dot_rows(left[...], e_out[at, :])
         if part:
-            partial_out[:rows, at] = without_extra(terms + terms_in[:, at], rows).astype(
+            partial_out[:, at] = without_extra(terms + terms_in[:, at], rows).astype(
                 jnp.bfloat16
             )
         else:
@@ -390,8 +389,8 @@
     late_b, late_b_other, refs = refs[:2], refs[2:4], refs[4:]
     (late_own, late_other, first_own, first_other, zero_own, zero_other, sums) = refs[:7]
     (first_b, first_b_other, e_left, e_right, partner_own, partner_other) = refs[7:13]
-    (vec_own, vec_other, vec_core, right_out, left_out, left_partial_out, mine_out) = refs[13:20]
-    (own_loss_out, loss_out, left, norm_b, e_own, mine_own, mine_partner) = refs[20:]
+    (vec_own, vec_other, vec_core, right_out, left_out, *left_partials_out, mine_out) = refs[13:21]
+    (own_loss_out, loss_out, left, norm_b, e_own, mine_own, mine_partner) = refs[21:]
     rows, quart = zero_own.shape
     width = quart // 2
     lower, upper = slice(0, quart), slice(quart, 2 * quart)
@@ -472,7 +471,9 @@
             slope = rstd[:, at] * diagonal_row[:, inner]
             left_out[:, inner] = value + norm_b[:rows, inner].astype(jnp.float32) * slope
         else:
-            left_partial_out[:, inner] = value.astype(jnp.bfloat16)
+            for half, out in enumerate(left_partials_out):
+                some = out.shape[0]
+                out[:, inner] = value[half * some : (half + 1) * some].astype(jnp.bfloat16)
 
     for tile in range(2):
         at = slice(tile * width, (tile + 1) * width)
@@ -498,22 +499,25 @@
         mine_out[:, upper] = own_columns
 
 
-def add_kernel(one, other, out):
-    out[...] = one[...] + other[...]
-
-
-def left_final_kernel(left, from_core, left_out):
-    for at in range(0, left.shape[0], 64):
-        piece = slice(at, at + 64)
-        value = left[piece, :] + from_core[piece, :].astype(jnp.float32)
-        left_out[piece, :] = value.astype(jnp.bfloat16)
-
-
-def right_final_kernel(feats, right, from_x, late_b_0, late_b_1, first_b, loss, x_loss, right_out, loss_out):
+def for_partner_kernel(loss, core_loss, second, out):
+    total = loss[0:1, 0:1] + core_loss[0:1, 0:1]
+    out[...] = rows_of([jnp.broadcast_to(total, (1, out.shape[1])), second[0:1, :]])
+
+
+def left_final_kernel(left, from_core_0, from_core_1, left_out):
+    some = from_core_0.shape[0]
+    for half, from_core in enumerate((from_core_0, from_core_1)):
+        for at in range(0, some, 64):
+            piece = slice(half * some + at, half * some + at + 64)
+            value = left[piece, :] + from_core[at : at + 64, :].astype(jnp.float32)
+            left_out[piece, :] = value.astype(jnp.bfloat16)
+
+
+def right_final_kernel(feats, right, from_x, late_b_0, late_b_1, first_b, sent, got, right_out, loss_out):
     rows = right.shape[0]
     offset, rstd, _, _ = right_stats((late_b_0, late_b_1))
-    second = joined_rows(from_x, rows)[0]
-    loss_out[0] = (loss[0, 0] + x_loss[0, 0]) / feats
+    second = got[1:2, :]
+    loss_out[0] = (sent[0, 0] + got[0, 0]) / feats
     for at in range(0, rows, 64):
         piece = slice(at, at + 64)
         xhat = (first_b[piece, :].astype(jnp.float32) - offset) * rstd
@@ -671,17 +675,17 @@
         2 * gemm,
         room=12,
     )
-    partial_right, e_right, vec_other = local_call(
+    partial_right, second, e_right, vec_other = local_call(
         functools.partial(partner_kernel, batch_images, 1),
         (late_a_other, zero_other, partner_other, *late_b_other, terms, across, vec_own, columns),
-        (extended, quarter_bf16, row_out),
+        (quarter_bf16, row_out, quarter_bf16, row_out),
         [low(rows + 16, quart)],
         2 * gemm,
         room=12,
     )
     from_x = x_swap(partial_right)
     vec_core = core_swap(vec_other)
-    right_own, left_own, partial_left, mine, own_loss, loss = local_call(
+    right_own, left_own, *partials_left, mine, own_loss, loss = local_call(
         functools.partial(own_kernel, batch_images),
         (flags, *late_b, *late_b_other)
         + (late_a, late_a_other, left_outputs, other_a0, zero_own, zero_other, own_all)
@@ -691,7 +695,8 @@
         (
             quarter_f32,
             quarter_f32,
-            quarter_bf16,
+            half_block,
+            half_block,
             jax.ShapeDtypeStruct((width, half), jnp.float32),
             one_out,
             one_out,
@@ -706,15 +711,15 @@
         8 * gemm,
         room=20,
     )
-    from_core = core_swap(partial_left)
+    from_core = [core_swap(x) for x in partials_left]
     core_loss = core_swap(own_loss)
-    (loss,) = local_call(add_kernel, (loss, core_loss), (one_out,))
-    x_loss = x_swap(loss)
-    (left_gradient,) = local_call(left_final_kernel, (left_own, from_core), (quarter_bf16,))
+    (for_partner,) = local_call(for_partner_kernel, (loss, core_loss, second), (row_out,))
+    from_partner = x_swap(for_partner)
+    (left_gradient,) = local_call(left_final_kernel, (left_own, *from_core), (quarter_bf16,))
     right_own, left_gradient = after(right_own, left_gradient)
     right_gradient, loss = local_call(
         functools.partial(right_final_kernel, feats),
-        (right_own, from_x, *late_b, right_outputs, loss, x_loss),
+        (right_own, from_x, *late_b, right_outputs, for_partner, from_partner),
         (quarter_bf16, jax.ShapeDtypeStruct((1,), jnp.float32)),
     )
     return (left_gradient, right_gradient, mine[None, :, :], loss)

time: 93 us -> 94.3 us (1.014)
  waiting for transfers between devices: 44.4 us -> 46.3 us
    ppermute x15 -> x16, waiting for transfers between devices: 7.39 us -> 9.23 us  [swapped(): return lax.ppermute(block, axis, route)]
    ppermute x15 -> x16, starting transfers between devices: 12.6 us -> 11.9 us  [swapped(): return lax.ppermute(block, axis, route)]
  transfers between devices with their start and end apart: 26 -> 27, of which waited for: 13 -> 14; matrix products, arithmetic and copies ran while one was open for 0% -> 0% of each run, Pallas kernels for 17% -> 17%
where the time goes in v15:
time: 94.3 us; the launch traced here: 94 us
  waiting for transfers between devices  46.3 us (49%)
  starting transfers between devices  28.3 us (30%)
  Pallas kernels  18.4 us (20%)
  between operations  1.02 us (1%)
    ppermute x11, waiting for transfers between devices, along(): return lax.ppermute(block, 'dp', route)  37 us
    pallas_call x14, Pallas kernels, local_call(): pl.pallas_call(kernel, out_shape=list(outs), in_specs=[space(x) for x in...  18.4 us
    ppermute x11, starting transfers between devices, along(): return lax.ppermute(block, 'dp', route)  16.3 us
    ppermute x16, starting transfers between devices, swapped(): return lax.ppermute(block, axis, route)  11.9 us
    ppermute x16, waiting for transfers between devices, swapped(): return lax.ppermute(block, axis, route)  9.23 us
  transfers between devices with their start and end apart: 27, of which 14 were waited for; matrix products, arithmetic and copies ran while one was open for 0% of the time, Pallas kernels for 17%

profile of v15, /device:TPU:0, one launch (start us, length us, event | category | flops | bytes accessed | tf_op | source)
XLA Modules:
  0.0 94.0 jit_solution(8632074542364079151)
XLA Ops:
  1.2 2.7 %collective-permute-start.4 = (bf16[512,512]{1,0:T(8,128)(2,1)}, bf16[512,512]{1,0:T(8,128)(2,1)S(1)}, u32[]{:S(2)}, u32[]{:S(2)}) collective-permute-start(bf16[512,512]{1,0:T(8,128)(2,1)} %refs_6_.3), channel_id=1, source_target_pairs={{0,4},{4,0},{8,12},{12,8},{1,5},{5,1},{9,13},{13,9},{2,6},{6,2},{1... | collective-permute-start | bytes 1572872 | tf_op jit(solution)/shard_map/ppermute | solution.py:569
  4.5 1.6 %collective-permute-start.10 = (bf16[512,512]{1,0:T(8,128)(2,1)}, bf16[512,512]{1,0:T(8,128)(2,1)S(1)}, u32[]{:S(2)}, u32[]{:S(2)}) collective-permute-start(bf16[512,512]{1,0:T(8,128)(2,1)} %first_b.1), channel_id=1, source_target_pairs={{0,2},{2,0},{1,3},{3,1},{4,6},{6,4},{5,7},{7,5},{8,10},{10,8},{9,1... | collective-permute-start | bytes 1572872 | tf_op jit(solution)/shard_map/ppermute | solution.py:19
  6.1 4.4 %collective-permute-start.1 = (bf16[512,512]{1,0:T(8,128)(2,1)}, bf16[512,512]{1,0:T(8,128)(2,1)S(1)}, u32[]{:S(2)}, u32[]{:S(2)}) collective-permute-start(bf16[512,512]{1,0:T(8,128)(2,1)} %first_b.1), channel_id=1, source_target_pairs={{0,4},{4,0},{8,12},{12,8},{1,5},{5,1},{9,13},{13,9},{2,6},{6,2},{1... | collective-permute-start | bytes 1572872 | tf_op jit(solution)/shard_map/ppermute | solution.py:569
  10.5 6.3 %collective-permute-done.4.refs_2_ = bf16[512,512]{1,0:T(8,128)(2,1)S(1)} collective-permute-done((bf16[512,512]{1,0:T(8,128)(2,1)}, bf16[512,512]{1,0:T(8,128)(2,1)S(1)}, u32[]{:S(2)}, u32[]{:S(2)}) %collective-permute-start.4) | collective-permute-done | bytes 524320 | tf_op jit(solution)/shard_map/ppermute | solution.py:569
  17.5 1.3 %collective-permute-start.8 = (bf16[512,512]{1,0:T(8,128)(2,1)S(1)}, bf16[512,512]{1,0:T(8,128)(2,1)S(1)}, u32[]{:S(2)}, u32[]{:S(2)}) collective-permute-start(bf16[512,512]{1,0:T(8,128)(2,1)S(1)} %collective-permute-done.7.inner), channel_id=1, source_target_pairs={{4,0},{8,12},{5,1},{9,13},{6,2},{10,14},{7,3},{11,15},{20,16},{24,... | collective-permute-start | bytes 1572872 | tf_op jit(solution)/shard_map/ppermute | solution.py:569
  18.9 9.1 %collective-permute-done.1.second.refs_8_ = bf16[512,512]{1,0:T(8,128)(2,1)S(1)} collective-permute-done((bf16[512,512]{1,0:T(8,128)(2,1)}, bf16[512,512]{1,0:T(8,128)(2,1)S(1)}, u32[]{:S(2)}, u32[]{:S(2)}) %collective-permute-start.1) | collective-permute-done | bytes 524320 | tf_op jit(solution)/shard_map/ppermute | solution.py:569
  28.0 1.9 %collective-permute-start.11 = (bf16[512,512]{1,0:T(8,128)(2,1)S(1)}, bf16[512,512]{1,0:T(8,128)(2,1)S(1)}, u32[]{:S(2)}, u32[]{:S(2)}) collective-permute-start(bf16[512,512]{1,0:T(8,128)(2,1)S(1)} %collective-permute-done.1.second.refs_8_), channel_id=1, source_target_pairs={{0,2},{2,0},{1,3},{3,1},{4,6},{6,4},{5,7},{7,5},{8,10},{10,8},{9,1... | collective-permute-start | bytes 1572872 | tf_op jit(solution)/shard_map/ppermute | solution.py:19
  30.6 1.3 %collective-permute-start.6 = (bf16[512,512]{1,0:T(8,128)(2,1)S(1)}, bf16[512,512]{1,0:T(8,128)(2,1)S(1)}, u32[]{:S(2)}, u32[]{:S(2)}) collective-permute-start(bf16[512,512]{1,0:T(8,128)(2,1)S(1)} %collective-permute-done.5.inner), channel_id=1, source_target_pairs={{4,0},{8,12},{5,1},{9,13},{6,2},{10,14},{7,3},{11,15},{20,16},{24,... | collective-permute-start | bytes 1572872 | tf_op jit(solution)/shard_map/ppermute | solution.py:569
  31.9 7.4 %collective-permute-done.8.outer = bf16[512,512]{1,0:T(8,128)(2,1)S(1)} collective-permute-done((bf16[512,512]{1,0:T(8,128)(2,1)S(1)}, bf16[512,512]{1,0:T(8,128)(2,1)S(1)}, u32[]{:S(2)}, u32[]{:S(2)}) %collective-permute-start.8) | collective-permute-done | bytes 524320 | tf_op jit(solution)/shard_map/ppermute | solution.py:569
  40.1 1.4 %collective-permute-done.11.refs_9_ = bf16[512,512]{1,0:T(8,128)(2,1)S(1)} collective-permute-done((bf16[512,512]{1,0:T(8,128)(2,1)S(1)}, bf16[512,512]{1,0:T(8,128)(2,1)S(1)}, u32[]{:S(2)}, u32[]{:S(2)}) %collective-permute-start.11) | collective-permute-done | bytes 524320 | tf_op jit(solution)/shard_map/ppermute | solution.py:19
  41.5 1.5 %collective-permute-start.13 = (bf16[512,512]{1,0:T(8,128)(2,1)S(1)}, bf16[512,512]{1,0:T(8,128)(2,1)S(1)}, u32[]{:S(2)}, u32[]{:S(2)}) collective-permute-start(bf16[512,512]{1,0:T(8,128)(2,1)S(1)} %shard_map.59.third.refs_10_), channel_id=1, source_target_pairs={{0,2},{2,0},{1,3},{3,1},{4,6},{6,4},{5,7},{7,5},{8,10},{10,8},{9,1... | collective-permute-start | bytes 1572872 | tf_op jit(solution)/shard_map/ppermute | solution.py:19
  43.0 1.4 %collective-permute-start.3 = (bf16[256,512]{1,0:T(8,128)(2,1)S(1)}, bf16[256,512]{1,0:T(8,128)(2,1)S(1)}, u32[]{:S(2)}, u32[]{:S(2)}) collective-permute-start(bf16[256,512]{1,0:T(8,128)(2,1)S(1)} %get-tuple-element.53.inner), channel_id=1, source_target_pairs={{4,0},{8,12},{5,1},{9,13},{6,2},{10,14},{7,3},{11,15},{20,16},{24,... | collective-permute-start | bytes 786440 | tf_op jit(solution)/shard_map/ppermute | solution.py:569
  44.4 1.0 %shard_map.60.row = f32[8,512]{1,0:T(8,128)S(1)} custom-call(bf16[512,512]{1,0:T(8,128)(2,1)S(1)} %copy-done, bf16[512,512]{1,0:T(8,128)(2,1)S(1)} %collective-permute-done.1.second.refs_8_, bf16[512,512]{1,0:T(8,128)(2,1)S(1)} %shard_map.59.third.refs_10_), custom_call_target="tpu_custom_call" | custom-call | flops 1048576 | bytes 1589248 | tf_op jit(solution)/shard_map/pallas_call | solution.py:539
  45.4 5.1 %collective-permute-done.6.outer = bf16[512,512]{1,0:T(8,128)(2,1)S(1)} collective-permute-done((bf16[512,512]{1,0:T(8,128)(2,1)S(1)}, bf16[512,512]{1,0:T(8,128)(2,1)S(1)}, u32[]{:S(2)}, u32[]{:S(2)}) %collective-permute-start.6) | collective-permute-done | bytes 524320 | tf_op jit(solution)/shard_map/ppermute | solution.py:569
  50.7 1.3 %collective-permute-start.9 = (bf16[256,512]{1,0:T(8,128)(2,1)S(1)}, bf16[256,512]{1,0:T(8,128)(2,1)S(1)}, u32[]{:S(2)}, u32[]{:S(2)}) collective-permute-start(bf16[256,512]{1,0:T(8,128)(2,1)S(1)} %get-tuple-element.58.inner), channel_id=1, source_target_pairs={{4,0},{8,12},{5,1},{9,13},{6,2},{10,14},{7,3},{11,15},{20,16},{24,... | collective-permute-start | bytes 786440 | tf_op jit(solution)/shard_map/ppermute | solution.py:569
  52.0 1.3 %collective-permute-start.19 = (bf16[512,512]{1,0:T(8,128)(2,1)S(1)}, bf16[512,512]{1,0:T(8,128)(2,1)S(1)}, u32[]{:S(2)}, u32[]{:S(2)}) collective-permute-start(bf16[512,512]{1,0:T(8,128)(2,1)S(1)} %collective-permute-done.18.inner), channel_id=1, source_target_pairs={{4,0},{8,12},{5,1},{9,13},{6,2},{10,14},{7,3},{11,15},{20,16},{24,... | collective-permute-start | bytes 1572872 | tf_op jit(solution)/shard_map/ppermute | solution.py:569
  53.3 2.7 %collective-permute-done.3.outer = bf16[256,512]{1,0:T(8,128)(2,1)S(1)} collective-permute-done((bf16[256,512]{1,0:T(8,128)(2,1)S(1)}, bf16[256,512]{1,0:T(8,128)(2,1)S(1)}, u32[]{:S(2)}, u32[]{:S(2)}) %collective-permute-start.3) | collective-permute-done | bytes 262176 | tf_op jit(solution)/shard_map/ppermute | solution.py:569
  56.2 1.6 %collective-permute-start.14 = (bf16[512,256]{1,0:T(8,128)(2,1)S(1)}, bf16[512,256]{1,0:T(8,128)(2,1)S(1)}, u32[]{:S(2)}, u32[]{:S(2)}) collective-permute-start(bf16[512,256]{1,0:T(8,128)(2,1)S(1)} %get-tuple-element.57.refs_0_.late_b_0), channel_id=1, source_target_pairs={{0,2},{2,0},{1,3},{3,1},{4,6},{6,4},{5,7},{7,5},{8,10},{10,8},{9,1... | collective-permute-start | bytes 786440 | tf_op jit(solution)/shard_map/ppermute | solution.py:19
  57.8 4.0 %collective-permute-done.9.outer = bf16[256,512]{1,0:T(8,128)(2,1)S(1)} collective-permute-done((bf16[256,512]{1,0:T(8,128)(2,1)S(1)}, bf16[256,512]{1,0:T(8,128)(2,1)S(1)}, u32[]{:S(2)}, u32[]{:S(2)}) %collective-permute-start.9) | collective-permute-done | bytes 262176 | tf_op jit(solution)/shard_map/ppermute | solution.py:569
  62.0 1.9 %collective-permute-start.17 = (bf16[544,256]{1,0:T(8,128)(2,1)S(1)}, bf16[544,256]{1,0:T(8,128)(2,1)S(1)}, u32[]{:S(2)}, u32[]{:S(2)}) collective-permute-start(bf16[544,256]{1,0:T(8,128)(2,1)S(1)} %shard_map.62.refs_1_.late_b_1), channel_id=1, source_target_pairs={{0,2},{2,0},{1,3},{3,1},{4,6},{6,4},{5,7},{7,5},{8,10},{10,8},{9,1... | collective-permute-start | bytes 835592 | tf_op jit(solution)/shard_map/ppermute | solution.py:19
  64.0 4.1 %shard_map.63 = (f32[512,512]{1,0:T(8,128)S(1)}, f32[512,512]{1,0:T(8,128)S(1)}, f32[512,1024]{1,0:T(8,128)S(1)}, f32[8,512]{1,0:T(8,128)S(1)}, bf16[512,512]{1,...) custom-call(bf16[512,512]{1,0:T(8,128)(2,1)S(1)} %copy-done.1, bf16[512,512]{1,0:T(8,128)(2,1)S(1)} %collective-permute-done.refs_1_.refs_7_, ...), custom_call_target="tpu_custom_call" | custom-call | flops 1048576 | bytes 65536 | tf_op jit(solution)/shard_map/pallas_call | solution.py:539
  68.1 2.0 %collective-permute-done.17.late_b_1.refs_3_ = bf16[544,256]{1,0:T(8,128)(2,1)S(1)} collective-permute-done((bf16[544,256]{1,0:T(8,128)(2,1)S(1)}, bf16[544,256]{1,0:T(8,128)(2,1)S(1)}, u32[]{:S(2)}, u32[]{:S(2)}) %collective-permute-start.17) | collective-permute-done | bytes 278560 | tf_op jit(solution)/shard_map/ppermute | solution.py:19
  70.2 2.6 %collective-permute-done.19.outer = bf16[512,512]{1,0:T(8,128)(2,1)S(1)} collective-permute-done((bf16[512,512]{1,0:T(8,128)(2,1)S(1)}, bf16[512,512]{1,0:T(8,128)(2,1)S(1)}, u32[]{:S(2)}, u32[]{:S(2)}) %collective-permute-start.19) | collective-permute-done | bytes 524320 | tf_op jit(solution)/shard_map/ppermute | solution.py:569
  73.2 1.1 %shard_map.65 = (f32[528,512]{1,0:T(8,128)S(1)}, f32[512,128]{1,0:T(8,128)S(1)}, bf16[512,512]{1,0:T(8,128)(2,1)S(1)}, f32[8,512]{1,0:T(8,128)S(1)}, f32[512,8]{1,0:T(8,128)S(1)}) custom-call(bf16[528,512]{1,0:T(8,128)(2,1)S(1)} %shard_map.64.late.refs_4_, bf16[512,512]{1,0:T(8,128)(2,1)S(1)} %get-tuple-element.73.zero.refs_8_, ...), custom_call_target="tpu_custom_call" | custom-call | flops 536870912 | bytes 4554752 | tf_op jit(solution)/shard_map/pallas_call | solution.py:539
  75.1 1.3 %shard_map.66 = (bf16[512,512]{1,0:T(8,128)(2,1)S(1)}, f32[8,512]{1,0:T(8,128)S(1)}, bf16[512,512]{1,0:T(8,128)(2,1)S(1)}, f32[8,512]{1,0:T(8,128)S(1)}) custom-call(bf16[528,512]{1,0:T(8,128)(2,1)S(1)} %collective-permute-done.20.late.refs_5_, bf16[512,512]{1,0:T(8,128)(2,1)S(1)} %get-tuple-element.74.zero.refs_9_, ...), custom_call_target="tpu_custom_call" | custom-call | flops 536870912 | bytes 5111808 | tf_op jit(solution)/shard_map/pallas_call | solution.py:539
  76.4 1.8 %collective-permute-start.24 = (bf16[512,512]{1,0:T(8,128)(2,1)S(1)}, bf16[512,512]{1,0:T(8,128)(2,1)S(1)}, u32[]{:S(2)}, u32[]{:S(2)}) collective-permute-start(bf16[512,512]{1,0:T(8,128)(2,1)S(1)} %get-tuple-element.91), channel_id=1, source_target_pairs={{0,2},{2,0},{1,3},{3,1},{4,6},{6,4},{5,7},{7,5},{8,10},{10,8},{9,1... | collective-permute-start | bytes 1572872 | tf_op jit(solution)/shard_map/ppermute | solution.py:19
  78.2 1.2 %collective-permute-done.21.refs_19_ = f32[8,512]{1,0:T(8,128)S(1)} collective-permute-done((f32[8,512]{1,0:T(8,128)S(1)}, f32[8,512]{1,0:T(8,128)S(1)}, u32[]{:S(2)}, u32[]{:S(2)}) %collective-permute-start.21) | collective-permute-done | bytes 16416 | tf_op jit(solution)/shard_map/ppermute | solution.py:19
  79.3 7.6 %shard_map.67 = (f32[512,512]{1,0:T(8,128)S(1)}, f32[512,512]{1,0:T(8,128)S(1)}, bf16[256,512]{1,0:T(8,128)(2,1)S(1)}, bf16[256,512]{1,0:T(8,128)(2,1)S(1)}, f32...) custom-call(s32[2]{0:T(128)S(1)} %pad_add_fusion.flags, ...), custom_call_target="tpu_custom_call" | custom-call | flops 2147483648 | bytes 14278664 | tf_op jit(solution)/shard_map/pallas_call | solution.py:539
  87.6 1.3 %collective-permute-done.25.core_loss = f32[8,128]{1,0:T(8,128)S(1)} collective-permute-done((f32[8,128]{1,0:T(8,128)S(1)}, f32[8,128]{1,0:T(8,128)S(1)}, u32[]{:S(2)}, u32[]{:S(2)}) %collective-permute-start.25) | collective-permute-done | bytes 4128 | tf_op jit(solution)/shard_map/ppermute | solution.py:19
  89.3 0.9 shard_map.68
  90.2 2.5 %collective-permute-done.26.got = f32[8,512]{1,0:T(8,128)S(1)} collective-permute-done((f32[8,512]{1,0:T(8,128)S(1)}, f32[8,512]{1,0:T(8,128)S(1)}, u32[]{:S(2)}, u32[]{:S(2)}) %collective-permute-start.26) | collective-permute-done | bytes 16416 | tf_op jit(solution)/shard_map/ppermute | solution.py:19
  92.7 1.1 %shard_map.70 = (bf16[512,512]{1,0:T(8,128)(2,1)}, f32[1]{0:T(128)}) custom-call(f32[512,512]{1,0:T(8,128)S(1)} %get-tuple-element.90.right, bf16[512,512]{1,0:T(8,128)(2,1)S(1)} %collective-permute-done.24.from_x, bf16[512,256]{1,0:T(8,128)(2,1)S(1)} %get-tuple-element.57.refs_0_.late_b_0, bf16[544,256]{1,0:T(8,128)(2,1)S(1)} %shard_map.62.refs_1_.late_b_1, ...), custom_call_target="tpu_custom_call" | custom-call | flops 1048576 | bytes 3194884 | tf_op jit(solution)/shard_map/pallas_call | solution.py:539
  (42 shorter events, 6.7 us)
Async XLA Ops:
  0.6 43.8 %copy-start = (bf16[512,512]{1,0:T(8,128)(2,1)S(1)}, bf16[512,512]{1,0:T(8,128)(2,1)}, u32[]{:S(2)}) copy-start(bf16[512,512]{1,0:T(8,128)(2,1)} %first_b.1) | copy-start | bytes 1572868
  0.6 9.9 %collective-permute-start = (bf16[512,512]{1,0:T(8,128)(2,1)}, bf16[512,512]{1,0:T(8,128)(2,1)S(1)}, u32[]{:S(2)}, u32[]{:S(2)}) collective-permute-start(bf16[512,512]{1,0:T(8,128)(2,1)} %refs_6_.3), channel_id=1, source_target_pairs={{0,1},{1,0},{2,3},{3,2},{4,5},{5,4},{6,7},{7,6},{8,9},{9,8},{10,11... | collective-permute-start | bytes 1572872 | tf_op jit(solution)/shard_map/ppermute | solution.py:19
  1.2 15.6 %collective-permute-start.4 = (bf16[512,512]{1,0:T(8,128)(2,1)}, bf16[512,512]{1,0:T(8,128)(2,1)S(1)}, u32[]{:S(2)}, u32[]{:S(2)}) collective-permute-start(bf16[512,512]{1,0:T(8,128)(2,1)} %refs_6_.3), channel_id=1, source_target_pairs={{0,4},{4,0},{8,12},{12,8},{1,5},{5,1},{9,13},{13,9},{2,6},{6,2},{1... | collective-permute-start | bytes 1572872 | tf_op jit(solution)/shard_map/ppermute | solution.py:569
  3.8 13.7 %collective-permute-start.7 = (bf16[512,512]{1,0:T(8,128)(2,1)}, bf16[512,512]{1,0:T(8,128)(2,1)S(1)}, u32[]{:S(2)}, u32[]{:S(2)}) collective-permute-start(bf16[512,512]{1,0:T(8,128)(2,1)} %first_b.1), channel_id=1, source_target_pairs={{4,8},{8,4},{5,9},{9,5},{6,10},{10,6},{7,11},{11,7},{20,24},{24,20... | collective-permute-start | bytes 1572872 | tf_op jit(solution)/shard_map/ppermute | solution.py:569
  4.5 14.4 %collective-permute-start.10 = (bf16[512,512]{1,0:T(8,128)(2,1)}, bf16[512,512]{1,0:T(8,128)(2,1)S(1)}, u32[]{:S(2)}, u32[]{:S(2)}) collective-permute-start(bf16[512,512]{1,0:T(8,128)(2,1)} %first_b.1), channel_id=1, source_target_pairs={{0,2},{2,0},{1,3},{3,1},{4,6},{6,4},{5,7},{7,5},{8,10},{10,8},{9,1... | collective-permute-start | bytes 1572872 | tf_op jit(solution)/shard_map/ppermute | solution.py:19
  6.1 22.0 %collective-permute-start.1 = (bf16[512,512]{1,0:T(8,128)(2,1)}, bf16[512,512]{1,0:T(8,128)(2,1)S(1)}, u32[]{:S(2)}, u32[]{:S(2)}) collective-permute-start(bf16[512,512]{1,0:T(8,128)(2,1)} %first_b.1), channel_id=1, source_target_pairs={{0,4},{4,0},{8,12},{12,8},{1,5},{5,1},{9,13},{13,9},{2,6},{6,2},{1... | collective-permute-start | bytes 1572872 | tf_op jit(solution)/shard_map/ppermute | solution.py:569
  16.8 13.8 %collective-permute-start.5 = (bf16[512,512]{1,0:T(8,128)(2,1)}, bf16[512,512]{1,0:T(8,128)(2,1)S(1)}, u32[]{:S(2)}, u32[]{:S(2)}) collective-permute-start(bf16[512,512]{1,0:T(8,128)(2,1)} %refs_6_.3), channel_id=1, source_target_pairs={{4,8},{8,4},{5,9},{9,5},{6,10},{10,6},{7,11},{11,7},{20,24},{24,20... | collective-permute-start | bytes 1572872 | tf_op jit(solution)/shard_map/ppermute | solution.py:569
  17.5 21.8 %collective-permute-start.8 = (bf16[512,512]{1,0:T(8,128)(2,1)S(1)}, bf16[512,512]{1,0:T(8,128)(2,1)S(1)}, u32[]{:S(2)}, u32[]{:S(2)}) collective-permute-start(bf16[512,512]{1,0:T(8,128)(2,1)S(1)} %collective-permute-done.7.inner), channel_id=1, source_target_pairs={{4,0},{8,12},{5,1},{9,13},{6,2},{10,14},{7,3},{11,15},{20,16},{24,... | collective-permute-start | bytes 1572872 | tf_op jit(solution)/shard_map/ppermute | solution.py:569
  18.8 21.3 %collective-permute-start.12 = (bf16[512,512]{1,0:T(8,128)(2,1)S(1)}, bf16[512,512]{1,0:T(8,128)(2,1)S(1)}, u32[]{:S(2)}, u32[]{:S(2)}) collective-permute-start(bf16[512,512]{1,0:T(8,128)(2,1)S(1)} %collective-permute-done.4.refs_2_), channel_id=1, source_target_pairs={{0,1},{1,0},{2,3},{3,2},{4,5},{5,4},{6,7},{7,6},{8,9},{9,8},{10,11... | collective-permute-start | bytes 1572872 | tf_op jit(solution)/shard_map/ppermute | solution.py:19
  28.0 13.4 %collective-permute-start.11 = (bf16[512,512]{1,0:T(8,128)(2,1)S(1)}, bf16[512,512]{1,0:T(8,128)(2,1)S(1)}, u32[]{:S(2)}, u32[]{:S(2)}) collective-permute-start(bf16[512,512]{1,0:T(8,128)(2,1)S(1)} %collective-permute-done.1.second.refs_8_), channel_id=1, source_target_pairs={{0,2},{2,0},{1,3},{3,1},{4,6},{6,4},{5,7},{7,5},{8,10},{10,8},{9,1... | collective-permute-start | bytes 1572872 | tf_op jit(solution)/shard_map/ppermute | solution.py:19
  29.9 13.0 %collective-permute-start.2 = (bf16[512,512]{1,0:T(8,128)(2,1)S(1)}, bf16[512,512]{1,0:T(8,128)(2,1)S(1)}, u32[]{:S(2)}, u32[]{:S(2)}) collective-permute-start(bf16[512,512]{1,0:T(8,128)(2,1)S(1)} %collective-permute-done.1.second.refs_8_), channel_id=1, source_target_pairs={{4,8},{8,4},{5,9},{9,5},{6,10},{10,6},{7,11},{11,7},{20,24},{24,20... | collective-permute-start | bytes 1572872 | tf_op jit(solution)/shard_map/ppermute | solution.py:569
  30.6 19.9 %collective-permute-start.6 = (bf16[512,512]{1,0:T(8,128)(2,1)S(1)}, bf16[512,512]{1,0:T(8,128)(2,1)S(1)}, u32[]{:S(2)}, u32[]{:S(2)}) collective-permute-start(bf16[512,512]{1,0:T(8,128)(2,1)S(1)} %collective-permute-done.5.inner), channel_id=1, source_target_pairs={{4,0},{8,12},{5,1},{9,13},{6,2},{10,14},{7,3},{11,15},{20,16},{24,... | collective-permute-start | bytes 1572872 | tf_op jit(solution)/shard_map/ppermute | solution.py:569
  39.3 12.7 %collective-permute-start.18 = (bf16[512,512]{1,0:T(8,128)(2,1)S(1)}, bf16[512,512]{1,0:T(8,128)(2,1)S(1)}, u32[]{:S(2)}, u32[]{:S(2)}) collective-permute-start(bf16[512,512]{1,0:T(8,128)(2,1)S(1)} %collective-permute-done.4.refs_2_), channel_id=1, source_target_pairs={{4,8},{8,4},{5,9},{9,5},{6,10},{10,6},{7,11},{11,7},{20,24},{24,20... | collective-permute-start | bytes 1572872 | tf_op jit(solution)/shard_map/ppermute | solution.py:569
  41.5 22.4 %collective-permute-start.13 = (bf16[512,512]{1,0:T(8,128)(2,1)S(1)}, bf16[512,512]{1,0:T(8,128)(2,1)S(1)}, u32[]{:S(2)}, u32[]{:S(2)}) collective-permute-start(bf16[512,512]{1,0:T(8,128)(2,1)S(1)} %shard_map.59.third.refs_10_), channel_id=1, source_target_pairs={{0,2},{2,0},{1,3},{3,1},{4,6},{6,4},{5,7},{7,5},{8,10},{10,8},{9,1... | collective-permute-start | bytes 1572872 | tf_op jit(solution)/shard_map/ppermute | solution.py:19
  43.0 21.0 %copy-start.1 = (bf16[512,512]{1,0:T(8,128)(2,1)S(1)}, bf16[512,512]{1,0:T(8,128)(2,1)}, u32[]{:S(2)}) copy-start(bf16[512,512]{1,0:T(8,128)(2,1)} %refs_6_.3) | copy-start | bytes 1572868
  43.0 13.0 %collective-permute-start.3 = (bf16[256,512]{1,0:T(8,128)(2,1)S(1)}, bf16[256,512]{1,0:T(8,128)(2,1)S(1)}, u32[]{:S(2)}, u32[]{:S(2)}) collective-permute-start(bf16[256,512]{1,0:T(8,128)(2,1)S(1)} %get-tuple-element.53.inner), channel_id=1, source_target_pairs={{4,0},{8,12},{5,1},{9,13},{6,2},{10,14},{7,3},{11,15},{20,16},{24,... | collective-permute-start | bytes 786440 | tf_op jit(solution)/shard_map/ppermute | solution.py:569
  50.6 13.3 %collective-permute-start.15 = (bf16[512,512]{1,0:T(8,128)(2,1)S(1)}, bf16[512,512]{1,0:T(8,128)(2,1)S(1)}, u32[]{:S(2)}, u32[]{:S(2)}) collective-permute-start(bf16[512,512]{1,0:T(8,128)(2,1)S(1)} %shard_map.58.refs_4_), channel_id=1, source_target_pairs={{0,1},{1,0},{2,3},{3,2},{4,5},{5,4},{6,7},{7,6},{8,9},{9,8},{10,11... | collective-permute-start | bytes 1572872 | tf_op jit(solution)/shard_map/ppermute | solution.py:19
  50.7 11.1 %collective-permute-start.9 = (bf16[256,512]{1,0:T(8,128)(2,1)S(1)}, bf16[256,512]{1,0:T(8,128)(2,1)S(1)}, u32[]{:S(2)}, u32[]{:S(2)}) collective-permute-start(bf16[256,512]{1,0:T(8,128)(2,1)S(1)} %get-tuple-element.58.inner), channel_id=1, source_target_pairs={{4,0},{8,12},{5,1},{9,13},{6,2},{10,14},{7,3},{11,15},{20,16},{24,... | collective-permute-start | bytes 786440 | tf_op jit(solution)/shard_map/ppermute | solution.py:569
  52.0 20.7 %collective-permute-start.19 = (bf16[512,512]{1,0:T(8,128)(2,1)S(1)}, bf16[512,512]{1,0:T(8,128)(2,1)S(1)}, u32[]{:S(2)}, u32[]{:S(2)}) collective-permute-start(bf16[512,512]{1,0:T(8,128)(2,1)S(1)} %collective-permute-done.18.inner), channel_id=1, source_target_pairs={{4,0},{8,12},{5,1},{9,13},{6,2},{10,14},{7,3},{11,15},{20,16},{24,... | collective-permute-start | bytes 1572872 | tf_op jit(solution)/shard_map/ppermute | solution.py:569
  56.2 7.8 %collective-permute-start.14 = (bf16[512,256]{1,0:T(8,128)(2,1)S(1)}, bf16[512,256]{1,0:T(8,128)(2,1)S(1)}, u32[]{:S(2)}, u32[]{:S(2)}) collective-permute-start(bf16[512,256]{1,0:T(8,128)(2,1)S(1)} %get-tuple-element.57.refs_0_.late_b_0), channel_id=1, source_target_pairs={{0,2},{2,0},{1,3},{3,1},{4,6},{6,4},{5,7},{7,5},{8,10},{10,8},{9,1... | collective-permute-start | bytes 786440 | tf_op jit(solution)/shard_map/ppermute | solution.py:19
  62.0 8.1 %collective-permute-start.17 = (bf16[544,256]{1,0:T(8,128)(2,1)S(1)}, bf16[544,256]{1,0:T(8,128)(2,1)S(1)}, u32[]{:S(2)}, u32[]{:S(2)}) collective-permute-start(bf16[544,256]{1,0:T(8,128)(2,1)S(1)} %shard_map.62.refs_1_.late_b_1), channel_id=1, source_target_pairs={{0,2},{2,0},{1,3},{3,1},{4,6},{6,4},{5,7},{7,5},{8,10},{10,8},{9,1... | collective-permute-start | bytes 835592 | tf_op jit(solution)/shard_map/ppermute | solution.py:19
  68.0 2.1 %collective-permute-start.16 = (f32[8,512]{1,0:T(8,128)S(1)}, f32[8,512]{1,0:T(8,128)S(1)}, u32[]{:S(2)}, u32[]{:S(2)}) collective-permute-start(f32[8,512]{1,0:T(8,128)S(1)} %get-tuple-element.70), channel_id=1, source_target_pairs={{0,1},{1,0},{2,3},{3,2},{4,5},{5,4},{6,7},{7,6},{8,9},{9,8},{10,11... | collective-permute-start | bytes 49160 | tf_op jit(solution)/shard_map/ppermute | solution.py:19
  73.1 2.0 %collective-permute-start.20 = (bf16[528,512]{1,0:T(8,128)(2,1)S(1)}, bf16[528,512]{1,0:T(8,128)(2,1)S(1)}, u32[]{:S(2)}, u32[]{:S(2)}) collective-permute-start(bf16[528,512]{1,0:T(8,128)(2,1)S(1)} %shard_map.64.late.refs_4_), channel_id=1, source_target_pairs={{0,1},{1,0},{2,3},{3,2},{4,5},{5,4},{6,7},{7,6},{8,9},{9,8},{10,11... | collective-permute-start | bytes 1622024 | tf_op jit(solution)/shard_map/ppermute | solution.py:19
  76.4 16.3 %collective-permute-start.24 = (bf16[512,512]{1,0:T(8,128)(2,1)S(1)}, bf16[512,512]{1,0:T(8,128)(2,1)S(1)}, u32[]{:S(2)}, u32[]{:S(2)}) collective-permute-start(bf16[512,512]{1,0:T(8,128)(2,1)S(1)} %get-tuple-element.91), channel_id=1, source_target_pairs={{0,2},{2,0},{1,3},{3,1},{4,6},{6,4},{5,7},{7,5},{8,10},{10,8},{9,1... | collective-permute-start | bytes 1572872 | tf_op jit(solution)/shard_map/ppermute | solution.py:19
  78.2 1.2 %collective-permute-start.21 = (f32[8,512]{1,0:T(8,128)S(1)}, f32[8,512]{1,0:T(8,128)S(1)}, u32[]{:S(2)}, u32[]{:S(2)}) collective-permute-start(f32[8,512]{1,0:T(8,128)S(1)} %get-tuple-element.84.refs_18_), channel_id=1, source_target_pairs={{0,1},{1,0},{2,3},{3,2},{4,5},{5,4},{6,7},{7,6},{8,9},{9,8},{10,11... | collective-permute-start | bytes 49160 | tf_op jit(solution)/shard_map/ppermute | solution.py:19
  87.0 2.3 %collective-permute-start.22 = (bf16[256,512]{1,0:T(8,128)(2,1)S(1)}, bf16[256,512]{1,0:T(8,128)(2,1)S(1)}, u32[]{:S(2)}, u32[]{:S(2)}) collective-permute-start(bf16[256,512]{1,0:T(8,128)(2,1)S(1)} %get-tuple-element.87), channel_id=1, source_target_pairs={{0,1},{1,0},{2,3},{3,2},{4,5},{5,4},{6,7},{7,6},{8,9},{9,8},{10,11... | collective-permute-start | bytes 786440 | tf_op jit(solution)/shard_map/ppermute | solution.py:19
  87.1 2.2 %collective-permute-start.23 = (bf16[256,512]{1,0:T(8,128)(2,1)S(1)}, bf16[256,512]{1,0:T(8,128)(2,1)S(1)}, u32[]{:S(2)}, u32[]{:S(2)}) collective-permute-start(bf16[256,512]{1,0:T(8,128)(2,1)S(1)} %get-tuple-element.88), channel_id=1, source_target_pairs={{0,1},{1,0},{2,3},{3,2},{4,5},{5,4},{6,7},{7,6},{8,9},{9,8},{10,11... | collective-permute-start | bytes 786440 | tf_op jit(solution)/shard_map/ppermute | solution.py:19
  87.5 1.4 %collective-permute-start.25 = (f32[8,128]{1,0:T(8,128)S(1)}, f32[8,128]{1,0:T(8,128)S(1)}, u32[]{:S(2)}, u32[]{:S(2)}) collective-permute-start(f32[8,128]{1,0:T(8,128)S(1)} %get-tuple-element.93), channel_id=1, source_target_pairs={{0,1},{1,0},{2,3},{3,2},{4,5},{5,4},{6,7},{7,6},{8,9},{9,8},{10,11... | collective-permute-start | bytes 12296 | tf_op jit(solution)/shard_map/ppermute | solution.py:19
  89.0 3.7 %collective-permute-start.26 = (f32[8,512]{1,0:T(8,128)S(1)}, f32[8,512]{1,0:T(8,128)S(1)}, u32[]{:S(2)}, u32[]{:S(2)}) collective-permute-start(f32[8,512]{1,0:T(8,128)S(1)} %shard_map.69.sent), channel_id=1, source_target_pairs={{0,2},{2,0},{1,3},{3,1},{4,6},{6,4},{5,7},{7,5},{8,10},{10,8},{9,1... | collective-permute-start | bytes 49160 | tf_op jit(solution)/shard_map/ppermute | solution.py:19

commit v16 on v15

--- a/solution.py
+++ b/solution.py
@@ -389,8 +389,8 @@
     late_b, late_b_other, refs = refs[:2], refs[2:4], refs[4:]
     (late_own, late_other, first_own, first_other, zero_own, zero_other, sums) = refs[:7]
     (first_b, first_b_other, e_left, e_right, partner_own, partner_other) = refs[7:13]
-    (vec_own, vec_other, vec_core, right_out, left_out, *left_partials_out, mine_out) = refs[13:21]
-    (own_loss_out, loss_out, left, norm_b, e_own, mine_own, mine_partner) = refs[21:]
+    (vec_own, vec_other, right_out, left_out, *left_partials_out, mine_out) = refs[13:20]
+    (loss_out, left, norm_b, e_own, mine_own, mine_partner) = refs[20:]
     rows, quart = zero_own.shape
     width = quart // 2
     lower, upper = slice(0, quart), slice(quart, 2 * quart)
@@ -455,9 +455,7 @@
     partner_second = jnp.concatenate([vec_own[0:1, :], vec_other[0:1, :]], axis=1)
     second_a = rstd * (partner_second + jnp.concatenate(down, axis=1))
     second_b = lanes_to_row(across)
-    own_loss = jnp.sum(losses)
-    own_loss_out[...] = jnp.broadcast_to(own_loss, (8, 128))
-    loss = own_loss + jnp.sum(vec_other[1:2, :] + vec_core[1:2, :])
+    loss = jnp.sum(losses) + jnp.sum(vec_other[1:2, :])
     loss_out[...] = jnp.broadcast_to(loss, (8, 128))
 
     for tile in (2, 3, 0, 1):
@@ -684,21 +682,19 @@
         room=12,
     )
     from_x = x_swap(partial_right)
-    vec_core = core_swap(vec_other)
-    right_own, left_own, *partials_left, mine, own_loss, loss = local_call(
+    right_own, left_own, *partials_left, mine, loss = local_call(
         functools.partial(own_kernel, batch_images),
         (flags, *late_b, *late_b_other)
         + (late_a, late_a_other, left_outputs, other_a0, zero_own, zero_other, own_all)
         + (right_outputs, other_b0, e_left, e_right)
         + (partner_own, partner_other)
-        + (vec_own, vec_other, vec_core),
+        + (vec_own, vec_other),
         (
             quarter_f32,
             quarter_f32,
             half_block,
             half_block,
             jax.ShapeDtypeStruct((width, half), jnp.float32),
-            one_out,
             one_out,
         ),
         [
@@ -712,7 +708,7 @@
         room=20,
     )
     from_core = [core_swap(x) for x in partials_left]
-    core_loss = core_swap(own_loss)
+    core_loss = core_swap(loss)
     (for_partner,) = local_call(for_partner_kernel, (loss, core_loss, second), (row_out,))
     from_partner = x_swap(for_partner)
     (left_gradient,) = local_call(left_final_kernel, (left_own, *from_core), (quarter_bf16,))

time: 94.3 us -> 93.1 us (0.987)
  waiting for transfers between devices: 46.3 us -> 45.2 us
    ppermute x16 -> x15, waiting for transfers between devices: 9.23 us -> 8.19 us  [swapped(): return lax.ppermute(block, axis, route)]
    ppermute x16 -> x15, starting transfers between devices: 11.9 us -> 11.8 us  [swapped(): return lax.ppermute(block, axis, route)]
  transfers between devices with their start and end apart: 27 -> 26, of which waited for: 14 -> 13; matrix products, arithmetic and copies ran while one was open for 0% -> 0% of each run, Pallas kernels for 17% -> 17%
where the time goes in v16:
time: 93.1 us; the launch traced here: 92.8 us
  waiting for transfers between devices  45.2 us (49%)
  starting transfers between devices  28.1 us (30%)
  Pallas kernels  18.3 us (20%)
  between operations  1.02 us (1%)
    ppermute x11, waiting for transfers between devices, along(): return lax.ppermute(block, 'dp', route)  37 us
    pallas_call x14, Pallas kernels, local_call(): pl.pallas_call(kernel, out_shape=list(outs), in_specs=[space(x) for x in...  18.3 us
    ppermute x11, starting transfers between devices, along(): return lax.ppermute(block, 'dp', route)  16.3 us
    ppermute x15, starting transfers between devices, swapped(): return lax.ppermute(block, axis, route)  11.8 us
    ppermute x15, waiting for transfers between devices, swapped(): return lax.ppermute(block, axis, route)  8.19 us
  transfers between devices with their start and end apart: 26, of which 13 were waited for; matrix products, arithmetic and copies ran while one was open for 0% of the time, Pallas kernels for 17%

profile of v16, /device:TPU:0, one launch (start us, length us, event | category | flops | bytes accessed | tf_op | source)
XLA Modules:
  0.0 92.8 jit_solution(961124559329211836)
XLA Ops:
  1.2 2.7 %collective-permute-start.4 = (bf16[512,512]{1,0:T(8,128)(2,1)}, bf16[512,512]{1,0:T(8,128)(2,1)S(1)}, u32[]{:S(2)}, u32[]{:S(2)}) collective-permute-start(bf16[512,512]{1,0:T(8,128)(2,1)} %refs_6_.3), channel_id=1, source_target_pairs={{0,4},{4,0},{8,12},{12,8},{1,5},{5,1},{9,13},{13,9},{2,6},{6,2},{1... | collective-permute-start | bytes 1572872 | tf_op jit(solution)/shard_map/ppermute | solution.py:567
  4.5 1.6 %collective-permute-start.10 = (bf16[512,512]{1,0:T(8,128)(2,1)}, bf16[512,512]{1,0:T(8,128)(2,1)S(1)}, u32[]{:S(2)}, u32[]{:S(2)}) collective-permute-start(bf16[512,512]{1,0:T(8,128)(2,1)} %first_b.1), channel_id=1, source_target_pairs={{0,2},{2,0},{1,3},{3,1},{4,6},{6,4},{5,7},{7,5},{8,10},{10,8},{9,1... | collective-permute-start | bytes 1572872 | tf_op jit(solution)/shard_map/ppermute | solution.py:19
  6.1 4.4 %collective-permute-start.1 = (bf16[512,512]{1,0:T(8,128)(2,1)}, bf16[512,512]{1,0:T(8,128)(2,1)S(1)}, u32[]{:S(2)}, u32[]{:S(2)}) collective-permute-start(bf16[512,512]{1,0:T(8,128)(2,1)} %first_b.1), channel_id=1, source_target_pairs={{0,4},{4,0},{8,12},{12,8},{1,5},{5,1},{9,13},{13,9},{2,6},{6,2},{1... | collective-permute-start | bytes 1572872 | tf_op jit(solution)/shard_map/ppermute | solution.py:567
  10.5 6.3 %collective-permute-done.4.refs_2_ = bf16[512,512]{1,0:T(8,128)(2,1)S(1)} collective-permute-done((bf16[512,512]{1,0:T(8,128)(2,1)}, bf16[512,512]{1,0:T(8,128)(2,1)S(1)}, u32[]{:S(2)}, u32[]{:S(2)}) %collective-permute-start.4) | collective-permute-done | bytes 524320 | tf_op jit(solution)/shard_map/ppermute | solution.py:567
  17.5 1.3 %collective-permute-start.8 = (bf16[512,512]{1,0:T(8,128)(2,1)S(1)}, bf16[512,512]{1,0:T(8,128)(2,1)S(1)}, u32[]{:S(2)}, u32[]{:S(2)}) collective-permute-start(bf16[512,512]{1,0:T(8,128)(2,1)S(1)} %collective-permute-done.7.inner), channel_id=1, source_target_pairs={{4,0},{8,12},{5,1},{9,13},{6,2},{10,14},{7,3},{11,15},{20,16},{24,... | collective-permute-start | bytes 1572872 | tf_op jit(solution)/shard_map/ppermute | solution.py:567
  18.9 9.1 %collective-permute-done.1.second.refs_8_ = bf16[512,512]{1,0:T(8,128)(2,1)S(1)} collective-permute-done((bf16[512,512]{1,0:T(8,128)(2,1)}, bf16[512,512]{1,0:T(8,128)(2,1)S(1)}, u32[]{:S(2)}, u32[]{:S(2)}) %collective-permute-start.1) | collective-permute-done | bytes 524320 | tf_op jit(solution)/shard_map/ppermute | solution.py:567
  28.0 1.9 %collective-permute-start.11 = (bf16[512,512]{1,0:T(8,128)(2,1)S(1)}, bf16[512,512]{1,0:T(8,128)(2,1)S(1)}, u32[]{:S(2)}, u32[]{:S(2)}) collective-permute-start(bf16[512,512]{1,0:T(8,128)(2,1)S(1)} %collective-permute-done.1.second.refs_8_), channel_id=1, source_target_pairs={{0,2},{2,0},{1,3},{3,1},{4,6},{6,4},{5,7},{7,5},{8,10},{10,8},{9,1... | collective-permute-start | bytes 1572872 | tf_op jit(solution)/shard_map/ppermute | solution.py:19
  30.6 1.3 %collective-permute-start.6 = (bf16[512,512]{1,0:T(8,128)(2,1)S(1)}, bf16[512,512]{1,0:T(8,128)(2,1)S(1)}, u32[]{:S(2)}, u32[]{:S(2)}) collective-permute-start(bf16[512,512]{1,0:T(8,128)(2,1)S(1)} %collective-permute-done.5.inner), channel_id=1, source_target_pairs={{4,0},{8,12},{5,1},{9,13},{6,2},{10,14},{7,3},{11,15},{20,16},{24,... | collective-permute-start | bytes 1572872 | tf_op jit(solution)/shard_map/ppermute | solution.py:567
  31.9 7.4 %collective-permute-done.8.outer = bf16[512,512]{1,0:T(8,128)(2,1)S(1)} collective-permute-done((bf16[512,512]{1,0:T(8,128)(2,1)S(1)}, bf16[512,512]{1,0:T(8,128)(2,1)S(1)}, u32[]{:S(2)}, u32[]{:S(2)}) %collective-permute-start.8) | collective-permute-done | bytes 524320 | tf_op jit(solution)/shard_map/ppermute | solution.py:567
  40.1 1.4 %collective-permute-done.11.refs_9_ = bf16[512,512]{1,0:T(8,128)(2,1)S(1)} collective-permute-done((bf16[512,512]{1,0:T(8,128)(2,1)S(1)}, bf16[512,512]{1,0:T(8,128)(2,1)S(1)}, u32[]{:S(2)}, u32[]{:S(2)}) %collective-permute-start.11) | collective-permute-done | bytes 524320 | tf_op jit(solution)/shard_map/ppermute | solution.py:19
  41.5 1.5 %collective-permute-start.13 = (bf16[512,512]{1,0:T(8,128)(2,1)S(1)}, bf16[512,512]{1,0:T(8,128)(2,1)S(1)}, u32[]{:S(2)}, u32[]{:S(2)}) collective-permute-start(bf16[512,512]{1,0:T(8,128)(2,1)S(1)} %shard_map.59.third.refs_10_), channel_id=1, source_target_pairs={{0,2},{2,0},{1,3},{3,1},{4,6},{6,4},{5,7},{7,5},{8,10},{10,8},{9,1... | collective-permute-start | bytes 1572872 | tf_op jit(solution)/shard_map/ppermute | solution.py:19
  43.0 1.4 %collective-permute-start.3 = (bf16[256,512]{1,0:T(8,128)(2,1)S(1)}, bf16[256,512]{1,0:T(8,128)(2,1)S(1)}, u32[]{:S(2)}, u32[]{:S(2)}) collective-permute-start(bf16[256,512]{1,0:T(8,128)(2,1)S(1)} %get-tuple-element.52.inner), channel_id=1, source_target_pairs={{4,0},{8,12},{5,1},{9,13},{6,2},{10,14},{7,3},{11,15},{20,16},{24,... | collective-permute-start | bytes 786440 | tf_op jit(solution)/shard_map/ppermute | solution.py:567
  44.4 1.0 %shard_map.60.row = f32[8,512]{1,0:T(8,128)S(1)} custom-call(bf16[512,512]{1,0:T(8,128)(2,1)S(1)} %copy-done, bf16[512,512]{1,0:T(8,128)(2,1)S(1)} %collective-permute-done.1.second.refs_8_, bf16[512,512]{1,0:T(8,128)(2,1)S(1)} %shard_map.59.third.refs_10_), custom_call_target="tpu_custom_call" | custom-call | flops 1048576 | bytes 1589248 | tf_op jit(solution)/shard_map/pallas_call | solution.py:537
  45.4 5.1 %collective-permute-done.6.outer = bf16[512,512]{1,0:T(8,128)(2,1)S(1)} collective-permute-done((bf16[512,512]{1,0:T(8,128)(2,1)S(1)}, bf16[512,512]{1,0:T(8,128)(2,1)S(1)}, u32[]{:S(2)}, u32[]{:S(2)}) %collective-permute-start.6) | collective-permute-done | bytes 524320 | tf_op jit(solution)/shard_map/ppermute | solution.py:567
  50.7 1.3 %collective-permute-start.9 = (bf16[256,512]{1,0:T(8,128)(2,1)S(1)}, bf16[256,512]{1,0:T(8,128)(2,1)S(1)}, u32[]{:S(2)}, u32[]{:S(2)}) collective-permute-start(bf16[256,512]{1,0:T(8,128)(2,1)S(1)} %get-tuple-element.57.inner), channel_id=1, source_target_pairs={{4,0},{8,12},{5,1},{9,13},{6,2},{10,14},{7,3},{11,15},{20,16},{24,... | collective-permute-start | bytes 786440 | tf_op jit(solution)/shard_map/ppermute | solution.py:567
  52.0 1.3 %collective-permute-start.19 = (bf16[512,512]{1,0:T(8,128)(2,1)S(1)}, bf16[512,512]{1,0:T(8,128)(2,1)S(1)}, u32[]{:S(2)}, u32[]{:S(2)}) collective-permute-start(bf16[512,512]{1,0:T(8,128)(2,1)S(1)} %collective-permute-done.18.inner), channel_id=1, source_target_pairs={{4,0},{8,12},{5,1},{9,13},{6,2},{10,14},{7,3},{11,15},{20,16},{24,... | collective-permute-start | bytes 1572872 | tf_op jit(solution)/shard_map/ppermute | solution.py:567
  53.3 2.7 %collective-permute-done.3.outer = bf16[256,512]{1,0:T(8,128)(2,1)S(1)} collective-permute-done((bf16[256,512]{1,0:T(8,128)(2,1)S(1)}, bf16[256,512]{1,0:T(8,128)(2,1)S(1)}, u32[]{:S(2)}, u32[]{:S(2)}) %collective-permute-start.3) | collective-permute-done | bytes 262176 | tf_op jit(solution)/shard_map/ppermute | solution.py:567
  56.2 1.6 %collective-permute-start.14 = (bf16[512,256]{1,0:T(8,128)(2,1)S(1)}, bf16[512,256]{1,0:T(8,128)(2,1)S(1)}, u32[]{:S(2)}, u32[]{:S(2)}) collective-permute-start(bf16[512,256]{1,0:T(8,128)(2,1)S(1)} %get-tuple-element.56.refs_0_.late_b_0), channel_id=1, source_target_pairs={{0,2},{2,0},{1,3},{3,1},{4,6},{6,4},{5,7},{7,5},{8,10},{10,8},{9,1... | collective-permute-start | bytes 786440 | tf_op jit(solution)/shard_map/ppermute | solution.py:19
  57.8 4.0 %collective-permute-done.9.outer = bf16[256,512]{1,0:T(8,128)(2,1)S(1)} collective-permute-done((bf16[256,512]{1,0:T(8,128)(2,1)S(1)}, bf16[256,512]{1,0:T(8,128)(2,1)S(1)}, u32[]{:S(2)}, u32[]{:S(2)}) %collective-permute-start.9) | collective-permute-done | bytes 262176 | tf_op jit(solution)/shard_map/ppermute | solution.py:567
  62.0 1.9 %collective-permute-start.17 = (bf16[544,256]{1,0:T(8,128)(2,1)S(1)}, bf16[544,256]{1,0:T(8,128)(2,1)S(1)}, u32[]{:S(2)}, u32[]{:S(2)}) collective-permute-start(bf16[544,256]{1,0:T(8,128)(2,1)S(1)} %shard_map.62.refs_1_.late_b_1), channel_id=1, source_target_pairs={{0,2},{2,0},{1,3},{3,1},{4,6},{6,4},{5,7},{7,5},{8,10},{10,8},{9,1... | collective-permute-start | bytes 835592 | tf_op jit(solution)/shard_map/ppermute | solution.py:19
  64.0 4.1 %shard_map.63 = (f32[512,512]{1,0:T(8,128)S(1)}, f32[512,512]{1,0:T(8,128)S(1)}, f32[512,1024]{1,0:T(8,128)S(1)}, f32[8,512]{1,0:T(8,128)S(1)}, bf16[512,512]{1,...) custom-call(bf16[512,512]{1,0:T(8,128)(2,1)S(1)} %copy-done.1, bf16[512,512]{1,0:T(8,128)(2,1)S(1)} %collective-permute-done.refs_1_.refs_7_, ...), custom_call_target="tpu_custom_call" | custom-call | flops 1048576 | bytes 65536 | tf_op jit(solution)/shard_map/pallas_call | solution.py:537
  68.1 2.0 %collective-permute-done.17.late_b_1.refs_3_ = bf16[544,256]{1,0:T(8,128)(2,1)S(1)} collective-permute-done((bf16[544,256]{1,0:T(8,128)(2,1)S(1)}, bf16[544,256]{1,0:T(8,128)(2,1)S(1)}, u32[]{:S(2)}, u32[]{:S(2)}) %collective-permute-start.17) | collective-permute-done | bytes 278560 | tf_op jit(solution)/shard_map/ppermute | solution.py:19
  70.2 2.6 %collective-permute-done.19.outer = bf16[512,512]{1,0:T(8,128)(2,1)S(1)} collective-permute-done((bf16[512,512]{1,0:T(8,128)(2,1)S(1)}, bf16[512,512]{1,0:T(8,128)(2,1)S(1)}, u32[]{:S(2)}, u32[]{:S(2)}) %collective-permute-start.19) | collective-permute-done | bytes 524320 | tf_op jit(solution)/shard_map/ppermute | solution.py:567
  73.2 1.1 %shard_map.65 = (f32[528,512]{1,0:T(8,128)S(1)}, f32[512,128]{1,0:T(8,128)S(1)}, bf16[512,512]{1,0:T(8,128)(2,1)S(1)}, f32[8,512]{1,0:T(8,128)S(1)}, f32[512,8]{1,0:T(8,128)S(1)}) custom-call(bf16[528,512]{1,0:T(8,128)(2,1)S(1)} %shard_map.64.late.refs_4_, bf16[512,512]{1,0:T(8,128)(2,1)S(1)} %get-tuple-element.72.zero.refs_8_, ...), custom_call_target="tpu_custom_call" | custom-call | flops 536870912 | bytes 4554752 | tf_op jit(solution)/shard_map/pallas_call | solution.py:537
  74.3 0.8 collective-permute-done.20.late.refs_5_
  75.1 1.3 %shard_map.66 = (bf16[512,512]{1,0:T(8,128)(2,1)S(1)}, f32[8,512]{1,0:T(8,128)S(1)}, bf16[512,512]{1,0:T(8,128)(2,1)S(1)}, f32[8,512]{1,0:T(8,128)S(1)}) custom-call(bf16[528,512]{1,0:T(8,128)(2,1)S(1)} %collective-permute-done.20.late.refs_5_, bf16[512,512]{1,0:T(8,128)(2,1)S(1)} %get-tuple-element.73.zero.refs_9_, ...), custom_call_target="tpu_custom_call" | custom-call | flops 536870912 | bytes 5111808 | tf_op jit(solution)/shard_map/pallas_call | solution.py:537
  76.4 1.8 %collective-permute-start.23 = (bf16[512,512]{1,0:T(8,128)(2,1)S(1)}, bf16[512,512]{1,0:T(8,128)(2,1)S(1)}, u32[]{:S(2)}, u32[]{:S(2)}) collective-permute-start(bf16[512,512]{1,0:T(8,128)(2,1)S(1)} %get-tuple-element.90), channel_id=1, source_target_pairs={{0,2},{2,0},{1,3},{3,1},{4,6},{6,4},{5,7},{7,5},{8,10},{10,8},{9,1... | collective-permute-start | bytes 1572872 | tf_op jit(solution)/shard_map/ppermute | solution.py:19
  78.1 7.6 %shard_map.67 = (f32[512,512]{1,0:T(8,128)S(1)}, f32[512,512]{1,0:T(8,128)S(1)}, bf16[256,512]{1,0:T(8,128)(2,1)S(1)}, bf16[256,512]{1,0:T(8,128)(2,1)S(1)}, f32[256,1024]{1,0:T(8,128)}, /*index=5*/f32[8,128]{1,0:T(8,128)S(1)}) custom-call(s32[2]{0:T(128)S(1)} %pad_add_fusion.flags, bf16[512,256]{1,0:T(8,128)(2,1)S(1)} %get-tuple-element.56.refs_0_.late_b_0, ...), custom_call_target="tpu_custom_call" | custom-call | flops 2147483648 | bytes 14258184 | tf_op jit(solution)/shard_map/pallas_call | solution.py:537
  86.3 1.4 %collective-permute-done.24.core_loss = f32[8,128]{1,0:T(8,128)S(1)} collective-permute-done((f32[8,128]{1,0:T(8,128)S(1)}, f32[8,128]{1,0:T(8,128)S(1)}, u32[]{:S(2)}, u32[]{:S(2)}) %collective-permute-start.24) | collective-permute-done | bytes 4128 | tf_op jit(solution)/shard_map/ppermute | solution.py:19
  88.1 0.9 shard_map.68
  89.0 2.5 %collective-permute-done.25.got = f32[8,512]{1,0:T(8,128)S(1)} collective-permute-done((f32[8,512]{1,0:T(8,128)S(1)}, f32[8,512]{1,0:T(8,128)S(1)}, u32[]{:S(2)}, u32[]{:S(2)}) %collective-permute-start.25) | collective-permute-done | bytes 16416 | tf_op jit(solution)/shard_map/ppermute | solution.py:19
  91.5 1.1 %shard_map.70 = (bf16[512,512]{1,0:T(8,128)(2,1)}, f32[1]{0:T(128)}) custom-call(f32[512,512]{1,0:T(8,128)S(1)} %get-tuple-element.89.right, bf16[512,512]{1,0:T(8,128)(2,1)S(1)} %collective-permute-done.23.from_x, bf16[512,256]{1,0:T(8,128)(2,1)S(1)} %get-tuple-element.56.refs_0_.late_b_0, bf16[544,256]{1,0:T(8,128)(2,1)S(1)} %shard_map.62.refs_1_.late_b_1, ...), custom_call_target="tpu_custom_call" | custom-call | flops 1048576 | bytes 3194884 | tf_op jit(solution)/shard_map/pallas_call | solution.py:537
  (40 shorter events, 5.8 us)
Async XLA Ops:
  0.6 43.8 %copy-start = (bf16[512,512]{1,0:T(8,128)(2,1)S(1)}, bf16[512,512]{1,0:T(8,128)(2,1)}, u32[]{:S(2)}) copy-start(bf16[512,512]{1,0:T(8,128)(2,1)} %first_b.1) | copy-start | bytes 1572868
  0.6 9.9 %collective-permute-start = (bf16[512,512]{1,0:T(8,128)(2,1)}, bf16[512,512]{1,0:T(8,128)(2,1)S(1)}, u32[]{:S(2)}, u32[]{:S(2)}) collective-permute-start(bf16[512,512]{1,0:T(8,128)(2,1)} %refs_6_.3), channel_id=1, source_target_pairs={{0,1},{1,0},{2,3},{3,2},{4,5},{5,4},{6,7},{7,6},{8,9},{9,8},{10,11... | collective-permute-start | bytes 1572872 | tf_op jit(solution)/shard_map/ppermute | solution.py:19
  1.2 15.6 %collective-permute-start.4 = (bf16[512,512]{1,0:T(8,128)(2,1)}, bf16[512,512]{1,0:T(8,128)(2,1)S(1)}, u32[]{:S(2)}, u32[]{:S(2)}) collective-permute-start(bf16[512,512]{1,0:T(8,128)(2,1)} %refs_6_.3), channel_id=1, source_target_pairs={{0,4},{4,0},{8,12},{12,8},{1,5},{5,1},{9,13},{13,9},{2,6},{6,2},{1... | collective-permute-start | bytes 1572872 | tf_op jit(solution)/shard_map/ppermute | solution.py:567
  3.8 13.7 %collective-permute-start.7 = (bf16[512,512]{1,0:T(8,128)(2,1)}, bf16[512,512]{1,0:T(8,128)(2,1)S(1)}, u32[]{:S(2)}, u32[]{:S(2)}) collective-permute-start(bf16[512,512]{1,0:T(8,128)(2,1)} %first_b.1), channel_id=1, source_target_pairs={{4,8},{8,4},{5,9},{9,5},{6,10},{10,6},{7,11},{11,7},{20,24},{24,20... | collective-permute-start | bytes 1572872 | tf_op jit(solution)/shard_map/ppermute | solution.py:567
  4.5 14.4 %collective-permute-start.10 = (bf16[512,512]{1,0:T(8,128)(2,1)}, bf16[512,512]{1,0:T(8,128)(2,1)S(1)}, u32[]{:S(2)}, u32[]{:S(2)}) collective-permute-start(bf16[512,512]{1,0:T(8,128)(2,1)} %first_b.1), channel_id=1, source_target_pairs={{0,2},{2,0},{1,3},{3,1},{4,6},{6,4},{5,7},{7,5},{8,10},{10,8},{9,1... | collective-permute-start | bytes 1572872 | tf_op jit(solution)/shard_map/ppermute | solution.py:19
  6.1 22.0 %collective-permute-start.1 = (bf16[512,512]{1,0:T(8,128)(2,1)}, bf16[512,512]{1,0:T(8,128)(2,1)S(1)}, u32[]{:S(2)}, u32[]{:S(2)}) collective-permute-start(bf16[512,512]{1,0:T(8,128)(2,1)} %first_b.1), channel_id=1, source_target_pairs={{0,4},{4,0},{8,12},{12,8},{1,5},{5,1},{9,13},{13,9},{2,6},{6,2},{1... | collective-permute-start | bytes 1572872 | tf_op jit(solution)/shard_map/ppermute | solution.py:567
  16.8 13.8 %collective-permute-start.5 = (bf16[512,512]{1,0:T(8,128)(2,1)}, bf16[512,512]{1,0:T(8,128)(2,1)S(1)}, u32[]{:S(2)}, u32[]{:S(2)}) collective-permute-start(bf16[512,512]{1,0:T(8,128)(2,1)} %refs_6_.3), channel_id=1, source_target_pairs={{4,8},{8,4},{5,9},{9,5},{6,10},{10,6},{7,11},{11,7},{20,24},{24,20... | collective-permute-start | bytes 1572872 | tf_op jit(solution)/shard_map/ppermute | solution.py:567
  17.5 21.8 %collective-permute-start.8 = (bf16[512,512]{1,0:T(8,128)(2,1)S(1)}, bf16[512,512]{1,0:T(8,128)(2,1)S(1)}, u32[]{:S(2)}, u32[]{:S(2)}) collective-permute-start(bf16[512,512]{1,0:T(8,128)(2,1)S(1)} %collective-permute-done.7.inner), channel_id=1, source_target_pairs={{4,0},{8,12},{5,1},{9,13},{6,2},{10,14},{7,3},{11,15},{20,16},{24,... | collective-permute-start | bytes 1572872 | tf_op jit(solution)/shard_map/ppermute | solution.py:567
  18.8 21.3 %collective-permute-start.12 = (bf16[512,512]{1,0:T(8,128)(2,1)S(1)}, bf16[512,512]{1,0:T(8,128)(2,1)S(1)}, u32[]{:S(2)}, u32[]{:S(2)}) collective-permute-start(bf16[512,512]{1,0:T(8,128)(2,1)S(1)} %collective-permute-done.4.refs_2_), channel_id=1, source_target_pairs={{0,1},{1,0},{2,3},{3,2},{4,5},{5,4},{6,7},{7,6},{8,9},{9,8},{10,11... | collective-permute-start | bytes 1572872 | tf_op jit(solution)/shard_map/ppermute | solution.py:19
  28.0 13.4 %collective-permute-start.11 = (bf16[512,512]{1,0:T(8,128)(2,1)S(1)}, bf16[512,512]{1,0:T(8,128)(2,1)S(1)}, u32[]{:S(2)}, u32[]{:S(2)}) collective-permute-start(bf16[512,512]{1,0:T(8,128)(2,1)S(1)} %collective-permute-done.1.second.refs_8_), channel_id=1, source_target_pairs={{0,2},{2,0},{1,3},{3,1},{4,6},{6,4},{5,7},{7,5},{8,10},{10,8},{9,1... | collective-permute-start | bytes 1572872 | tf_op jit(solution)/shard_map/ppermute | solution.py:19
  29.9 13.0 %collective-permute-start.2 = (bf16[512,512]{1,0:T(8,128)(2,1)S(1)}, bf16[512,512]{1,0:T(8,128)(2,1)S(1)}, u32[]{:S(2)}, u32[]{:S(2)}) collective-permute-start(bf16[512,512]{1,0:T(8,128)(2,1)S(1)} %collective-permute-done.1.second.refs_8_), channel_id=1, source_target_pairs={{4,8},{8,4},{5,9},{9,5},{6,10},{10,6},{7,11},{11,7},{20,24},{24,20... | collective-permute-start | bytes 1572872 | tf_op jit(solution)/shard_map/ppermute | solution.py:567
  30.6 19.9 %collective-permute-start.6 = (bf16[512,512]{1,0:T(8,128)(2,1)S(1)}, bf16[512,512]{1,0:T(8,128)(2,1)S(1)}, u32[]{:S(2)}, u32[]{:S(2)}) collective-permute-start(bf16[512,512]{1,0:T(8,128)(2,1)S(1)} %collective-permute-done.5.inner), channel_id=1, source_target_pairs={{4,0},{8,12},{5,1},{9,13},{6,2},{10,14},{7,3},{11,15},{20,16},{24,... | collective-permute-start | bytes 1572872 | tf_op jit(solution)/shard_map/ppermute | solution.py:567
  39.3 12.7 %collective-permute-start.18 = (bf16[512,512]{1,0:T(8,128)(2,1)S(1)}, bf16[512,512]{1,0:T(8,128)(2,1)S(1)}, u32[]{:S(2)}, u32[]{:S(2)}) collective-permute-start(bf16[512,512]{1,0:T(8,128)(2,1)S(1)} %collective-permute-done.4.refs_2_), channel_id=1, source_target_pairs={{4,8},{8,4},{5,9},{9,5},{6,10},{10,6},{7,11},{11,7},{20,24},{24,20... | collective-permute-start | bytes 1572872 | tf_op jit(solution)/shard_map/ppermute | solution.py:567
  41.5 22.4 %collective-permute-start.13 = (bf16[512,512]{1,0:T(8,128)(2,1)S(1)}, bf16[512,512]{1,0:T(8,128)(2,1)S(1)}, u32[]{:S(2)}, u32[]{:S(2)}) collective-permute-start(bf16[512,512]{1,0:T(8,128)(2,1)S(1)} %shard_map.59.third.refs_10_), channel_id=1, source_target_pairs={{0,2},{2,0},{1,3},{3,1},{4,6},{6,4},{5,7},{7,5},{8,10},{10,8},{9,1... | collective-permute-start | bytes 1572872 | tf_op jit(solution)/shard_map/ppermute | solution.py:19
  43.0 21.0 %copy-start.1 = (bf16[512,512]{1,0:T(8,128)(2,1)S(1)}, bf16[512,512]{1,0:T(8,128)(2,1)}, u32[]{:S(2)}) copy-start(bf16[512,512]{1,0:T(8,128)(2,1)} %refs_6_.3) | copy-start | bytes 1572868
  43.0 13.0 %collective-permute-start.3 = (bf16[256,512]{1,0:T(8,128)(2,1)S(1)}, bf16[256,512]{1,0:T(8,128)(2,1)S(1)}, u32[]{:S(2)}, u32[]{:S(2)}) collective-permute-start(bf16[256,512]{1,0:T(8,128)(2,1)S(1)} %get-tuple-element.52.inner), channel_id=1, source_target_pairs={{4,0},{8,12},{5,1},{9,13},{6,2},{10,14},{7,3},{11,15},{20,16},{24,... | collective-permute-start | bytes 786440 | tf_op jit(solution)/shard_map/ppermute | solution.py:567
  50.6 13.3 %collective-permute-start.15 = (bf16[512,512]{1,0:T(8,128)(2,1)S(1)}, bf16[512,512]{1,0:T(8,128)(2,1)S(1)}, u32[]{:S(2)}, u32[]{:S(2)}) collective-permute-start(bf16[512,512]{1,0:T(8,128)(2,1)S(1)} %shard_map.58.refs_4_), channel_id=1, source_target_pairs={{0,1},{1,0},{2,3},{3,2},{4,5},{5,4},{6,7},{7,6},{8,9},{9,8},{10,11... | collective-permute-start | bytes 1572872 | tf_op jit(solution)/shard_map/ppermute | solution.py:19
  50.7 11.1 %collective-permute-start.9 = (bf16[256,512]{1,0:T(8,128)(2,1)S(1)}, bf16[256,512]{1,0:T(8,128)(2,1)S(1)}, u32[]{:S(2)}, u32[]{:S(2)}) collective-permute-start(bf16[256,512]{1,0:T(8,128)(2,1)S(1)} %get-tuple-element.57.inner), channel_id=1, source_target_pairs={{4,0},{8,12},{5,1},{9,13},{6,2},{10,14},{7,3},{11,15},{20,16},{24,... | collective-permute-start | bytes 786440 | tf_op jit(solution)/shard_map/ppermute | solution.py:567
  52.0 20.7 %collective-permute-start.19 = (bf16[512,512]{1,0:T(8,128)(2,1)S(1)}, bf16[512,512]{1,0:T(8,128)(2,1)S(1)}, u32[]{:S(2)}, u32[]{:S(2)}) collective-permute-start(bf16[512,512]{1,0:T(8,128)(2,1)S(1)} %collective-permute-done.18.inner), channel_id=1, source_target_pairs={{4,0},{8,12},{5,1},{9,13},{6,2},{10,14},{7,3},{11,15},{20,16},{24,... | collective-permute-start | bytes 1572872 | tf_op jit(solution)/shard_map/ppermute | solution.py:567
  56.2 7.8 %collective-permute-start.14 = (bf16[512,256]{1,0:T(8,128)(2,1)S(1)}, bf16[512,256]{1,0:T(8,128)(2,1)S(1)}, u32[]{:S(2)}, u32[]{:S(2)}) collective-permute-start(bf16[512,256]{1,0:T(8,128)(2,1)S(1)} %get-tuple-element.56.refs_0_.late_b_0), channel_id=1, source_target_pairs={{0,2},{2,0},{1,3},{3,1},{4,6},{6,4},{5,7},{7,5},{8,10},{10,8},{9,1... | collective-permute-start | bytes 786440 | tf_op jit(solution)/shard_map/ppermute | solution.py:19
  62.0 8.1 %collective-permute-start.17 = (bf16[544,256]{1,0:T(8,128)(2,1)S(1)}, bf16[544,256]{1,0:T(8,128)(2,1)S(1)}, u32[]{:S(2)}, u32[]{:S(2)}) collective-permute-start(bf16[544,256]{1,0:T(8,128)(2,1)S(1)} %shard_map.62.refs_1_.late_b_1), channel_id=1, source_target_pairs={{0,2},{2,0},{1,3},{3,1},{4,6},{6,4},{5,7},{7,5},{8,10},{10,8},{9,1... | collective-permute-start | bytes 835592 | tf_op jit(solution)/shard_map/ppermute | solution.py:19
  68.0 2.1 %collective-permute-start.16 = (f32[8,512]{1,0:T(8,128)S(1)}, f32[8,512]{1,0:T(8,128)S(1)}, u32[]{:S(2)}, u32[]{:S(2)}) collective-permute-start(f32[8,512]{1,0:T(8,128)S(1)} %get-tuple-element.69), channel_id=1, source_target_pairs={{0,1},{1,0},{2,3},{3,2},{4,5},{5,4},{6,7},{7,6},{8,9},{9,8},{10,11... | collective-permute-start | bytes 49160 | tf_op jit(solution)/shard_map/ppermute | solution.py:19
  73.1 2.0 %collective-permute-start.20 = (bf16[528,512]{1,0:T(8,128)(2,1)S(1)}, bf16[528,512]{1,0:T(8,128)(2,1)S(1)}, u32[]{:S(2)}, u32[]{:S(2)}) collective-permute-start(bf16[528,512]{1,0:T(8,128)(2,1)S(1)} %shard_map.64.late.refs_4_), channel_id=1, source_target_pairs={{0,1},{1,0},{2,3},{3,2},{4,5},{5,4},{6,7},{7,6},{8,9},{9,8},{10,11... | collective-permute-start | bytes 1622024 | tf_op jit(solution)/shard_map/ppermute | solution.py:19
  76.4 15.1 %collective-permute-start.23 = (bf16[512,512]{1,0:T(8,128)(2,1)S(1)}, bf16[512,512]{1,0:T(8,128)(2,1)S(1)}, u32[]{:S(2)}, u32[]{:S(2)}) collective-permute-start(bf16[512,512]{1,0:T(8,128)(2,1)S(1)} %get-tuple-element.90), channel_id=1, source_target_pairs={{0,2},{2,0},{1,3},{3,1},{4,6},{6,4},{5,7},{7,5},{8,10},{10,8},{9,1... | collective-permute-start | bytes 1572872 | tf_op jit(solution)/shard_map/ppermute | solution.py:19
  85.8 2.3 %collective-permute-start.21 = (bf16[256,512]{1,0:T(8,128)(2,1)S(1)}, bf16[256,512]{1,0:T(8,128)(2,1)S(1)}, u32[]{:S(2)}, u32[]{:S(2)}) collective-permute-start(bf16[256,512]{1,0:T(8,128)(2,1)S(1)} %get-tuple-element.86), channel_id=1, source_target_pairs={{0,1},{1,0},{2,3},{3,2},{4,5},{5,4},{6,7},{7,6},{8,9},{9,8},{10,11... | collective-permute-start | bytes 786440 | tf_op jit(solution)/shard_map/ppermute | solution.py:19
  85.8 2.3 %collective-permute-start.22 = (bf16[256,512]{1,0:T(8,128)(2,1)S(1)}, bf16[256,512]{1,0:T(8,128)(2,1)S(1)}, u32[]{:S(2)}, u32[]{:S(2)}) collective-permute-start(bf16[256,512]{1,0:T(8,128)(2,1)S(1)} %get-tuple-element.87), channel_id=1, source_target_pairs={{0,1},{1,0},{2,3},{3,2},{4,5},{5,4},{6,7},{7,6},{8,9},{9,8},{10,11... | collective-permute-start | bytes 786440 | tf_op jit(solution)/shard_map/ppermute | solution.py:19
  86.3 1.4 %collective-permute-start.24 = (f32[8,128]{1,0:T(8,128)S(1)}, f32[8,128]{1,0:T(8,128)S(1)}, u32[]{:S(2)}, u32[]{:S(2)}) collective-permute-start(f32[8,128]{1,0:T(8,128)S(1)} %get-tuple-element.91.loss), channel_id=1, source_target_pairs={{0,1},{1,0},{2,3},{3,2},{4,5},{5,4},{6,7},{7,6},{8,9},{9,8},{10,11... | collective-permute-start | bytes 12296 | tf_op jit(solution)/shard_map/ppermute | solution.py:19
  87.8 3.7 %collective-permute-start.25 = (f32[8,512]{1,0:T(8,128)S(1)}, f32[8,512]{1,0:T(8,128)S(1)}, u32[]{:S(2)}, u32[]{:S(2)}) collective-permute-start(f32[8,512]{1,0:T(8,128)S(1)} %shard_map.69.sent), channel_id=1, source_target_pairs={{0,2},{2,0},{1,3},{3,1},{4,6},{6,4},{5,7},{7,5},{8,10},{10,8},{9,1... | collective-permute-start | bytes 49160 | tf_op jit(solution)/shard_map/ppermute | solution.py:19

commit v17 on v16

--- a/solution.py
+++ b/solution.py
@@ -345,8 +345,8 @@
 
 def partner_kernel(images, part, late, zero, sums, late_b_0, late_b_1, *refs):
     if part:
-        (terms_in, across_in, vec_in, columns) = refs[:4]
-        (partial_out, second_out, e_out, vec_out, left) = refs[4:]
+        (terms_in, across_in, vec_in, columns, first_b) = refs[:5]
+        (partial_out, e_out, vec_out, left) = refs[5:]
     else:
         (terms_out, across_out, e_out, vec_out, columns, left) = refs
         _, rstd_b, _, delta_b = right_stats((late_b_0, late_b_1))
@@ -370,7 +370,8 @@
     second_a = off_weight * jnp.concatenate(down, axis=1)
     if part:
         vec_out[...] = rows_of([second_a, second_a + vec_in[0:1, :]])
-        second_out[...] = rows_of([off_weight * lanes_to_row(across)])
+        second = off_weight * lanes_to_row(across)
+        offset_b, rstd_b, _, _ = right_stats(late_b)
     else:
         vec_out[...] = rows_of([second_a])
         across_out[...] = across
@@ -378,9 +379,10 @@
         at = slice(tile * width, (tile + 1) * width)
         terms = dot_rows(left[...], e_out[at, :])
         if part:
-            partial_out[:, at] = without_extra(terms + terms_in[:, at], rows).astype(
-                jnp.bfloat16
-            )
+            xhat = (first_b[:, at].astype(jnp.float32) - offset_b[:, at]) * rstd_b[:, at]
+            partial_out[:, at] = (
+                without_extra(terms + terms_in[:, at], rows) - xhat * second[:, at]
+            ).astype(jnp.bfloat16)
         else:
             terms_out[:, at] = terms
 
@@ -497,9 +499,12 @@
         mine_out[:, upper] = own_columns
 
 
-def for_partner_kernel(loss, core_loss, second, out):
-    total = loss[0:1, 0:1] + core_loss[0:1, 0:1]
-    out[...] = rows_of([jnp.broadcast_to(total, (1, out.shape[1])), second[0:1, :]])
+def add_kernel(one, other, out):
+    out[...] = one[...] + other[...]
+
+
+def loss_kernel(feats, one, other, out):
+    out[0] = (one[0, 0] + other[0, 0]) / feats
 
 
 def left_final_kernel(left, from_core_0, from_core_1, left_out):
@@ -511,16 +516,12 @@
             left_out[piece, :] = value.astype(jnp.bfloat16)
 
 
-def right_final_kernel(feats, right, from_x, late_b_0, late_b_1, first_b, sent, got, right_out, loss_out):
-    rows = right.shape[0]
-    offset, rstd, _, _ = right_stats((late_b_0, late_b_1))
-    second = got[1:2, :]
-    loss_out[0] = (sent[0, 0] + got[0, 0]) / feats
-    for at in range(0, rows, 64):
+def right_final_kernel(right, from_x, late_b_0, late_b_1, right_out):
+    rstd = right_stats((late_b_0, late_b_1))[1]
+    for at in range(0, right.shape[0], 64):
         piece = slice(at, at + 64)
-        xhat = (first_b[piece, :].astype(jnp.float32) - offset) * rstd
-        value = right[piece, :] + from_x[piece, :].astype(jnp.float32) - xhat * second
-        right_out[piece, :] = (rstd * value).astype(jnp.bfloat16)
+        value = rstd * (right[piece, :] + from_x[piece, :].astype(jnp.float32))
+        right_out[piece, :] = value.astype(jnp.bfloat16)
 
 
 vmem = pl.BlockSpec(memory_space=pltpu.VMEM)
@@ -673,10 +674,11 @@
         2 * gemm,
         room=12,
     )
-    partial_right, second, e_right, vec_other = local_call(
+    partial_right, e_right, vec_other = local_call(
         functools.partial(partner_kernel, batch_images, 1),
-        (late_a_other, zero_other, partner_other, *late_b_other, terms, across, vec_own, columns),
-        (quarter_bf16, row_out, quarter_bf16, row_out),
+        (late_a_other, zero_other, partner_other, *late_b_other)
+        + (terms, across, vec_own, columns, other_b0),
+        (quarter_bf16, quarter_bf16, row_out),
         [low(rows + 16, quart)],
         2 * gemm,
         room=12,
@@ -709,14 +711,16 @@
     )
     from_core = [core_swap(x) for x in partials_left]
     core_loss = core_swap(loss)
-    (for_partner,) = local_call(for_partner_kernel, (loss, core_loss, second), (row_out,))
-    from_partner = x_swap(for_partner)
+    (loss,) = local_call(add_kernel, (loss, core_loss), (one_out,))
+    x_loss = x_swap(loss)
     (left_gradient,) = local_call(left_final_kernel, (left_own, *from_core), (quarter_bf16,))
     right_own, left_gradient = after(right_own, left_gradient)
-    right_gradient, loss = local_call(
-        functools.partial(right_final_kernel, feats),
-        (right_own, from_x, *late_b, right_outputs, for_partner, from_partner),
-        (quarter_bf16, jax.ShapeDtypeStruct((1,), jnp.float32)),
+    (right_gradient,) = local_call(right_final_kernel, (right_own, from_x, *late_b), (quarter_bf16,))
+    right_gradient, x_loss = after(right_gradient, x_loss)
+    (loss,) = local_call(
+        functools.partial(loss_kernel, feats),
+        (loss, x_loss),
+        (jax.ShapeDtypeStruct((1,), jnp.float32),),
     )
     return (left_gradient, right_gradient, mine[None, :, :], loss)
 

time: 93.1 us -> 92.5 us (level)
  waiting for transfers between devices: 45.2 us -> 44.2 us
    ppermute x15, waiting for transfers between devices: 8.19 us -> 7.18 us  [swapped(): return lax.ppermute(block, axis, route)]
    pallas_call x14 -> x15, Pallas kernels: 18.3 us -> 18.8 us  [local_call(): pl.pallas_call(kernel, out_shape=list(outs), in_specs=[space(x) for x in...]
  transfers between devices with their start and end apart: 26 -> 26, of which waited for: 13 -> 13; matrix products, arithmetic and copies ran while one was open for 0% -> 0% of each run, Pallas kernels for 17% -> 18%
where the time goes in v17:
time: 92.5 us; the launch traced here: 92.2 us
  waiting for transfers between devices  44.2 us (48%)
  starting transfers between devices  28.1 us (30%)
  Pallas kernels  18.8 us (20%)
  between operations  1.02 us (1%)
    ppermute x11, waiting for transfers between devices, along(): return lax.ppermute(block, 'dp', route)  37 us
    pallas_call x15, Pallas kernels, local_call(): pl.pallas_call(kernel, out_shape=list(outs), in_specs=[space(x) for x in...  18.8 us
    ppermute x11, starting transfers between devices, along(): return lax.ppermute(block, 'dp', route)  16.3 us
    ppermute x15, starting transfers between devices, swapped(): return lax.ppermute(block, axis, route)  11.8 us
    ppermute x15, waiting for transfers between devices, swapped(): return lax.ppermute(block, axis, route)  7.18 us
  transfers between devices with their start and end apart: 26, of which 13 were waited for; matrix products, arithmetic and copies ran while one was open for 0% of the time, Pallas kernels for 18%

profile of v17, /device:TPU:0, one launch (start us, length us, event | category | flops | bytes accessed | tf_op | source)
XLA Modules:
  0.0 92.2 jit_solution(11989556995585754320)
XLA Ops:
  1.2 2.7 %collective-permute-start.4 = (bf16[512,512]{1,0:T(8,128)(2,1)}, bf16[512,512]{1,0:T(8,128)(2,1)S(1)}, u32[]{:S(2)}, u32[]{:S(2)}) collective-permute-start(bf16[512,512]{1,0:T(8,128)(2,1)} %refs_6_.3), channel_id=1, source_target_pairs={{0,4},{4,0},{8,12},{12,8},{1,5},{5,1},{9,13},{13,9},{2,6},{6,2},{1... | collective-permute-start | bytes 1572872 | tf_op jit(solution)/shard_map/ppermute | solution.py:568
  4.5 1.6 %collective-permute-start.10 = (bf16[512,512]{1,0:T(8,128)(2,1)}, bf16[512,512]{1,0:T(8,128)(2,1)S(1)}, u32[]{:S(2)}, u32[]{:S(2)}) collective-permute-start(bf16[512,512]{1,0:T(8,128)(2,1)} %refs_11_.1), channel_id=1, source_target_pairs={{0,2},{2,0},{1,3},{3,1},{4,6},{6,4},{5,7},{7,5},{8,10},{10,8},{9,1... | collective-permute-start | bytes 1572872 | tf_op jit(solution)/shard_map/ppermute | solution.py:19
  6.1 4.4 %collective-permute-start.1 = (bf16[512,512]{1,0:T(8,128)(2,1)}, bf16[512,512]{1,0:T(8,128)(2,1)S(1)}, u32[]{:S(2)}, u32[]{:S(2)}) collective-permute-start(bf16[512,512]{1,0:T(8,128)(2,1)} %refs_11_.1), channel_id=1, source_target_pairs={{0,4},{4,0},{8,12},{12,8},{1,5},{5,1},{9,13},{13,9},{2,6},{6,2},{1... | collective-permute-start | bytes 1572872 | tf_op jit(solution)/shard_map/ppermute | solution.py:568
  10.5 6.3 %collective-permute-done.4.refs_2_ = bf16[512,512]{1,0:T(8,128)(2,1)S(1)} collective-permute-done((bf16[512,512]{1,0:T(8,128)(2,1)}, bf16[512,512]{1,0:T(8,128)(2,1)S(1)}, u32[]{:S(2)}, u32[]{:S(2)}) %collective-permute-start.4) | collective-permute-done | bytes 524320 | tf_op jit(solution)/shard_map/ppermute | solution.py:568
  17.5 1.3 %collective-permute-start.8 = (bf16[512,512]{1,0:T(8,128)(2,1)S(1)}, bf16[512,512]{1,0:T(8,128)(2,1)S(1)}, u32[]{:S(2)}, u32[]{:S(2)}) collective-permute-start(bf16[512,512]{1,0:T(8,128)(2,1)S(1)} %collective-permute-done.7.inner), channel_id=1, source_target_pairs={{4,0},{8,12},{5,1},{9,13},{6,2},{10,14},{7,3},{11,15},{20,16},{24,... | collective-permute-start | bytes 1572872 | tf_op jit(solution)/shard_map/ppermute | solution.py:568
  18.9 9.1 %collective-permute-done.1.second.refs_8_ = bf16[512,512]{1,0:T(8,128)(2,1)S(1)} collective-permute-done((bf16[512,512]{1,0:T(8,128)(2,1)}, bf16[512,512]{1,0:T(8,128)(2,1)S(1)}, u32[]{:S(2)}, u32[]{:S(2)}) %collective-permute-start.1) | collective-permute-done | bytes 524320 | tf_op jit(solution)/shard_map/ppermute | solution.py:568
  28.0 1.9 %collective-permute-start.11 = (bf16[512,512]{1,0:T(8,128)(2,1)S(1)}, bf16[512,512]{1,0:T(8,128)(2,1)S(1)}, u32[]{:S(2)}, u32[]{:S(2)}) collective-permute-start(bf16[512,512]{1,0:T(8,128)(2,1)S(1)} %collective-permute-done.1.second.refs_8_), channel_id=1, source_target_pairs={{0,2},{2,0},{1,3},{3,1},{4,6},{6,4},{5,7},{7,5},{8,10},{10,8},{9,1... | collective-permute-start | bytes 1572872 | tf_op jit(solution)/shard_map/ppermute | solution.py:19
  30.6 1.3 %collective-permute-start.6 = (bf16[512,512]{1,0:T(8,128)(2,1)S(1)}, bf16[512,512]{1,0:T(8,128)(2,1)S(1)}, u32[]{:S(2)}, u32[]{:S(2)}) collective-permute-start(bf16[512,512]{1,0:T(8,128)(2,1)S(1)} %collective-permute-done.5.inner), channel_id=1, source_target_pairs={{4,0},{8,12},{5,1},{9,13},{6,2},{10,14},{7,3},{11,15},{20,16},{24,... | collective-permute-start | bytes 1572872 | tf_op jit(solution)/shard_map/ppermute | solution.py:568
  31.9 7.4 %collective-permute-done.8.outer = bf16[512,512]{1,0:T(8,128)(2,1)S(1)} collective-permute-done((bf16[512,512]{1,0:T(8,128)(2,1)S(1)}, bf16[512,512]{1,0:T(8,128)(2,1)S(1)}, u32[]{:S(2)}, u32[]{:S(2)}) %collective-permute-start.8) | collective-permute-done | bytes 524320 | tf_op jit(solution)/shard_map/ppermute | solution.py:568
  40.1 1.4 %collective-permute-done.11.refs_9_ = bf16[512,512]{1,0:T(8,128)(2,1)S(1)} collective-permute-done((bf16[512,512]{1,0:T(8,128)(2,1)S(1)}, bf16[512,512]{1,0:T(8,128)(2,1)S(1)}, u32[]{:S(2)}, u32[]{:S(2)}) %collective-permute-start.11) | collective-permute-done | bytes 524320 | tf_op jit(solution)/shard_map/ppermute | solution.py:19
  41.5 1.5 %collective-permute-start.13 = (bf16[512,512]{1,0:T(8,128)(2,1)S(1)}, bf16[512,512]{1,0:T(8,128)(2,1)S(1)}, u32[]{:S(2)}, u32[]{:S(2)}) collective-permute-start(bf16[512,512]{1,0:T(8,128)(2,1)S(1)} %shard_map.59.third.refs_10_), channel_id=1, source_target_pairs={{0,2},{2,0},{1,3},{3,1},{4,6},{6,4},{5,7},{7,5},{8,10},{10,8},{9,1... | collective-permute-start | bytes 1572872 | tf_op jit(solution)/shard_map/ppermute | solution.py:19
  43.0 1.4 %collective-permute-start.3 = (bf16[256,512]{1,0:T(8,128)(2,1)S(1)}, bf16[256,512]{1,0:T(8,128)(2,1)S(1)}, u32[]{:S(2)}, u32[]{:S(2)}) collective-permute-start(bf16[256,512]{1,0:T(8,128)(2,1)S(1)} %get-tuple-element.51.inner), channel_id=1, source_target_pairs={{4,0},{8,12},{5,1},{9,13},{6,2},{10,14},{7,3},{11,15},{20,16},{24,... | collective-permute-start | bytes 786440 | tf_op jit(solution)/shard_map/ppermute | solution.py:568
  44.4 1.0 %shard_map.60.row = f32[8,512]{1,0:T(8,128)S(1)} custom-call(bf16[512,512]{1,0:T(8,128)(2,1)S(1)} %copy-done, bf16[512,512]{1,0:T(8,128)(2,1)S(1)} %collective-permute-done.1.second.refs_8_, bf16[512,512]{1,0:T(8,128)(2,1)S(1)} %shard_map.59.third.refs_10_), custom_call_target="tpu_custom_call" | custom-call | flops 1048576 | bytes 1589248 | tf_op jit(solution)/shard_map/pallas_call | solution.py:538
  45.4 5.1 %collective-permute-done.6.outer = bf16[512,512]{1,0:T(8,128)(2,1)S(1)} collective-permute-done((bf16[512,512]{1,0:T(8,128)(2,1)S(1)}, bf16[512,512]{1,0:T(8,128)(2,1)S(1)}, u32[]{:S(2)}, u32[]{:S(2)}) %collective-permute-start.6) | collective-permute-done | bytes 524320 | tf_op jit(solution)/shard_map/ppermute | solution.py:568
  50.7 1.3 %collective-permute-start.9 = (bf16[256,512]{1,0:T(8,128)(2,1)S(1)}, bf16[256,512]{1,0:T(8,128)(2,1)S(1)}, u32[]{:S(2)}, u32[]{:S(2)}) collective-permute-start(bf16[256,512]{1,0:T(8,128)(2,1)S(1)} %get-tuple-element.56.inner), channel_id=1, source_target_pairs={{4,0},{8,12},{5,1},{9,13},{6,2},{10,14},{7,3},{11,15},{20,16},{24,... | collective-permute-start | bytes 786440 | tf_op jit(solution)/shard_map/ppermute | solution.py:568
  52.0 1.3 %collective-permute-start.19 = (bf16[512,512]{1,0:T(8,128)(2,1)S(1)}, bf16[512,512]{1,0:T(8,128)(2,1)S(1)}, u32[]{:S(2)}, u32[]{:S(2)}) collective-permute-start(bf16[512,512]{1,0:T(8,128)(2,1)S(1)} %collective-permute-done.18.inner), channel_id=1, source_target_pairs={{4,0},{8,12},{5,1},{9,13},{6,2},{10,14},{7,3},{11,15},{20,16},{24,... | collective-permute-start | bytes 1572872 | tf_op jit(solution)/shard_map/ppermute | solution.py:568
  53.3 2.7 %collective-permute-done.3.outer = bf16[256,512]{1,0:T(8,128)(2,1)S(1)} collective-permute-done((bf16[256,512]{1,0:T(8,128)(2,1)S(1)}, bf16[256,512]{1,0:T(8,128)(2,1)S(1)}, u32[]{:S(2)}, u32[]{:S(2)}) %collective-permute-start.3) | collective-permute-done | bytes 262176 | tf_op jit(solution)/shard_map/ppermute | solution.py:568
  56.2 1.6 %collective-permute-start.14 = (bf16[512,256]{1,0:T(8,128)(2,1)S(1)}, bf16[512,256]{1,0:T(8,128)(2,1)S(1)}, u32[]{:S(2)}, u32[]{:S(2)}) collective-permute-start(bf16[512,256]{1,0:T(8,128)(2,1)S(1)} %get-tuple-element.55.refs_0_.late_b_0), channel_id=1, source_target_pairs={{0,2},{2,0},{1,3},{3,1},{4,6},{6,4},{5,7},{7,5},{8,10},{10,8},{9,1... | collective-permute-start | bytes 786440 | tf_op jit(solution)/shard_map/ppermute | solution.py:19
  57.8 4.0 %collective-permute-done.9.outer = bf16[256,512]{1,0:T(8,128)(2,1)S(1)} collective-permute-done((bf16[256,512]{1,0:T(8,128)(2,1)S(1)}, bf16[256,512]{1,0:T(8,128)(2,1)S(1)}, u32[]{:S(2)}, u32[]{:S(2)}) %collective-permute-start.9) | collective-permute-done | bytes 262176 | tf_op jit(solution)/shard_map/ppermute | solution.py:568
  62.0 1.9 %collective-permute-start.17 = (bf16[544,256]{1,0:T(8,128)(2,1)S(1)}, bf16[544,256]{1,0:T(8,128)(2,1)S(1)}, u32[]{:S(2)}, u32[]{:S(2)}) collective-permute-start(bf16[544,256]{1,0:T(8,128)(2,1)S(1)} %shard_map.62.refs_1_.late_b_1), channel_id=1, source_target_pairs={{0,2},{2,0},{1,3},{3,1},{4,6},{6,4},{5,7},{7,5},{8,10},{10,8},{9,1... | collective-permute-start | bytes 835592 | tf_op jit(solution)/shard_map/ppermute | solution.py:19
  64.0 4.1 %shard_map.63 = (f32[512,512]{1,0:T(8,128)S(1)}, f32[512,512]{1,0:T(8,128)S(1)}, f32[512,1024]{1,0:T(8,128)S(1)}, f32[8,512]{1,0:T(8,128)S(1)}, bf16[512,512]{1,...) custom-call(bf16[512,512]{1,0:T(8,128)(2,1)S(1)} %copy-done.1, bf16[512,512]{1,0:T(8,128)(2,1)S(1)} %collective-permute-done.refs_1_.refs_7_, ...), custom_call_target="tpu_custom_call" | custom-call | flops 1048576 | bytes 65536 | tf_op jit(solution)/shard_map/pallas_call | solution.py:538
  68.1 2.0 %collective-permute-done.17.late_b_1.refs_3_ = bf16[544,256]{1,0:T(8,128)(2,1)S(1)} collective-permute-done((bf16[544,256]{1,0:T(8,128)(2,1)S(1)}, bf16[544,256]{1,0:T(8,128)(2,1)S(1)}, u32[]{:S(2)}, u32[]{:S(2)}) %collective-permute-start.17) | collective-permute-done | bytes 278560 | tf_op jit(solution)/shard_map/ppermute | solution.py:19
  70.2 2.6 %collective-permute-done.19.outer = bf16[512,512]{1,0:T(8,128)(2,1)S(1)} collective-permute-done((bf16[512,512]{1,0:T(8,128)(2,1)S(1)}, bf16[512,512]{1,0:T(8,128)(2,1)S(1)}, u32[]{:S(2)}, u32[]{:S(2)}) %collective-permute-start.19) | collective-permute-done | bytes 524320 | tf_op jit(solution)/shard_map/ppermute | solution.py:568
  73.2 1.1 %shard_map.65 = (f32[528,512]{1,0:T(8,128)S(1)}, f32[512,128]{1,0:T(8,128)S(1)}, bf16[512,512]{1,0:T(8,128)(2,1)S(1)}, f32[8,512]{1,0:T(8,128)S(1)}, f32[512,8]{1,0:T(8,128)S(1)}) custom-call(bf16[528,512]{1,0:T(8,128)(2,1)S(1)} %shard_map.64.late.refs_4_, bf16[512,512]{1,0:T(8,128)(2,1)S(1)} %get-tuple-element.71.zero.refs_8_, ...), custom_call_target="tpu_custom_call" | custom-call | flops 536870912 | bytes 4554752 | tf_op jit(solution)/shard_map/pallas_call | solution.py:538
  74.3 0.8 collective-permute-done.20.late.refs_5_
  75.1 1.4 %shard_map.66 = (bf16[512,512]{1,0:T(8,128)(2,1)S(1)}, bf16[512,512]{1,0:T(8,128)(2,1)S(1)}, f32[8,512]{1,0:T(8,128)S(1)}) custom-call(bf16[528,512]{1,0:T(8,128)(2,1)S(1)} %collective-permute-done.20.late.refs_5_, bf16[512,512]{1,0:T(8,128)(2,1)S(1)} %get-tuple-element.72.zero.refs_9_, f32[512,512]{1,0:T(8,128)S(1)} %get-tuple-element.76.sums.refs_16_, ...), custom_call_target="tpu_custom_call" | custom-call | flops 536870912 | bytes 5619712 | tf_op jit(solution)/shard_map/pallas_call | solution.py:538
  76.5 1.8 %collective-permute-start.23 = (bf16[512,512]{1,0:T(8,128)(2,1)S(1)}, bf16[512,512]{1,0:T(8,128)(2,1)S(1)}, u32[]{:S(2)}, u32[]{:S(2)}) collective-permute-start(bf16[512,512]{1,0:T(8,128)(2,1)S(1)} %get-tuple-element.89), channel_id=1, source_target_pairs={{0,2},{2,0},{1,3},{3,1},{4,6},{6,4},{5,7},{7,5},{8,10},{10,8},{9,1... | collective-permute-start | bytes 1572872 | tf_op jit(solution)/shard_map/ppermute | solution.py:19
  78.3 7.6 %shard_map.67 = (f32[512,512]{1,0:T(8,128)S(1)}, f32[512,512]{1,0:T(8,128)S(1)}, bf16[256,512]{1,0:T(8,128)(2,1)S(1)}, bf16[256,512]{1,0:T(8,128)(2,1)S(1)}, f32[256,1024]{1,0:T(8,128)}, /*index=5*/f32[8,128]{1,0:T(8,128)S(1)}) custom-call(s32[2]{0:T(128)S(1)} %pad_add_fusion.flags, bf16[512,256]{1,0:T(8,128)(2,1)S(1)} %get-tuple-element.55.refs_0_.late_b_0, ...), custom_call_target="tpu_custom_call" | custom-call | flops 2147483648 | bytes 14258184 | tf_op jit(solution)/shard_map/pallas_call | solution.py:538
  86.4 1.4 %collective-permute-done.24.other = f32[8,128]{1,0:T(8,128)S(1)} collective-permute-done((f32[8,128]{1,0:T(8,128)S(1)}, f32[8,128]{1,0:T(8,128)S(1)}, u32[]{:S(2)}, u32[]{:S(2)}) %collective-permute-start.24) | collective-permute-done | bytes 4128 | tf_op jit(solution)/shard_map/ppermute | solution.py:19
  88.2 0.9 shard_map.68
  89.1 1.5 %collective-permute-done.23.from_x = bf16[512,512]{1,0:T(8,128)(2,1)S(1)} collective-permute-done((bf16[512,512]{1,0:T(8,128)(2,1)S(1)}, bf16[512,512]{1,0:T(8,128)(2,1)S(1)}, u32[]{:S(2)}, u32[]{:S(2)}) %collective-permute-start.23) | collective-permute-done | bytes 524320 | tf_op jit(solution)/shard_map/ppermute | solution.py:19
  90.6 0.9 shard_map.69
  (41 shorter events, 6.3 us)
Async XLA Ops:
  0.6 43.8 %copy-start = (bf16[512,512]{1,0:T(8,128)(2,1)S(1)}, bf16[512,512]{1,0:T(8,128)(2,1)}, u32[]{:S(2)}) copy-start(bf16[512,512]{1,0:T(8,128)(2,1)} %refs_11_.1) | copy-start | bytes 1572868
  0.6 9.9 %collective-permute-start = (bf16[512,512]{1,0:T(8,128)(2,1)}, bf16[512,512]{1,0:T(8,128)(2,1)S(1)}, u32[]{:S(2)}, u32[]{:S(2)}) collective-permute-start(bf16[512,512]{1,0:T(8,128)(2,1)} %refs_6_.3), channel_id=1, source_target_pairs={{0,1},{1,0},{2,3},{3,2},{4,5},{5,4},{6,7},{7,6},{8,9},{9,8},{10,11... | collective-permute-start | bytes 1572872 | tf_op jit(solution)/shard_map/ppermute | solution.py:19
  1.2 15.6 %collective-permute-start.4 = (bf16[512,512]{1,0:T(8,128)(2,1)}, bf16[512,512]{1,0:T(8,128)(2,1)S(1)}, u32[]{:S(2)}, u32[]{:S(2)}) collective-permute-start(bf16[512,512]{1,0:T(8,128)(2,1)} %refs_6_.3), channel_id=1, source_target_pairs={{0,4},{4,0},{8,12},{12,8},{1,5},{5,1},{9,13},{13,9},{2,6},{6,2},{1... | collective-permute-start | bytes 1572872 | tf_op jit(solution)/shard_map/ppermute | solution.py:568
  3.8 13.7 %collective-permute-start.7 = (bf16[512,512]{1,0:T(8,128)(2,1)}, bf16[512,512]{1,0:T(8,128)(2,1)S(1)}, u32[]{:S(2)}, u32[]{:S(2)}) collective-permute-start(bf16[512,512]{1,0:T(8,128)(2,1)} %refs_11_.1), channel_id=1, source_target_pairs={{4,8},{8,4},{5,9},{9,5},{6,10},{10,6},{7,11},{11,7},{20,24},{24,20... | collective-permute-start | bytes 1572872 | tf_op jit(solution)/shard_map/ppermute | solution.py:568
  4.5 14.4 %collective-permute-start.10 = (bf16[512,512]{1,0:T(8,128)(2,1)}, bf16[512,512]{1,0:T(8,128)(2,1)S(1)}, u32[]{:S(2)}, u32[]{:S(2)}) collective-permute-start(bf16[512,512]{1,0:T(8,128)(2,1)} %refs_11_.1), channel_id=1, source_target_pairs={{0,2},{2,0},{1,3},{3,1},{4,6},{6,4},{5,7},{7,5},{8,10},{10,8},{9,1... | collective-permute-start | bytes 1572872 | tf_op jit(solution)/shard_map/ppermute | solution.py:19
  6.1 22.0 %collective-permute-start.1 = (bf16[512,512]{1,0:T(8,128)(2,1)}, bf16[512,512]{1,0:T(8,128)(2,1)S(1)}, u32[]{:S(2)}, u32[]{:S(2)}) collective-permute-start(bf16[512,512]{1,0:T(8,128)(2,1)} %refs_11_.1), channel_id=1, source_target_pairs={{0,4},{4,0},{8,12},{12,8},{1,5},{5,1},{9,13},{13,9},{2,6},{6,2},{1... | collective-permute-start | bytes 1572872 | tf_op jit(solution)/shard_map/ppermute | solution.py:568
  16.8 13.8 %collective-permute-start.5 = (bf16[512,512]{1,0:T(8,128)(2,1)}, bf16[512,512]{1,0:T(8,128)(2,1)S(1)}, u32[]{:S(2)}, u32[]{:S(2)}) collective-permute-start(bf16[512,512]{1,0:T(8,128)(2,1)} %refs_6_.3), channel_id=1, source_target_pairs={{4,8},{8,4},{5,9},{9,5},{6,10},{10,6},{7,11},{11,7},{20,24},{24,20... | collective-permute-start | bytes 1572872 | tf_op jit(solution)/shard_map/ppermute | solution.py:568
  17.5 21.8 %collective-permute-start.8 = (bf16[512,512]{1,0:T(8,128)(2,1)S(1)}, bf16[512,512]{1,0:T(8,128)(2,1)S(1)}, u32[]{:S(2)}, u32[]{:S(2)}) collective-permute-start(bf16[512,512]{1,0:T(8,128)(2,1)S(1)} %collective-permute-done.7.inner), channel_id=1, source_target_pairs={{4,0},{8,12},{5,1},{9,13},{6,2},{10,14},{7,3},{11,15},{20,16},{24,... | collective-permute-start | bytes 1572872 | tf_op jit(solution)/shard_map/ppermute | solution.py:568
  18.8 21.3 %collective-permute-start.12 = (bf16[512,512]{1,0:T(8,128)(2,1)S(1)}, bf16[512,512]{1,0:T(8,128)(2,1)S(1)}, u32[]{:S(2)}, u32[]{:S(2)}) collective-permute-start(bf16[512,512]{1,0:T(8,128)(2,1)S(1)} %collective-permute-done.4.refs_2_), channel_id=1, source_target_pairs={{0,1},{1,0},{2,3},{3,2},{4,5},{5,4},{6,7},{7,6},{8,9},{9,8},{10,11... | collective-permute-start | bytes 1572872 | tf_op jit(solution)/shard_map/ppermute | solution.py:19
  28.0 13.4 %collective-permute-start.11 = (bf16[512,512]{1,0:T(8,128)(2,1)S(1)}, bf16[512,512]{1,0:T(8,128)(2,1)S(1)}, u32[]{:S(2)}, u32[]{:S(2)}) collective-permute-start(bf16[512,512]{1,0:T(8,128)(2,1)S(1)} %collective-permute-done.1.second.refs_8_), channel_id=1, source_target_pairs={{0,2},{2,0},{1,3},{3,1},{4,6},{6,4},{5,7},{7,5},{8,10},{10,8},{9,1... | collective-permute-start | bytes 1572872 | tf_op jit(solution)/shard_map/ppermute | solution.py:19
  29.9 13.0 %collective-permute-start.2 = (bf16[512,512]{1,0:T(8,128)(2,1)S(1)}, bf16[512,512]{1,0:T(8,128)(2,1)S(1)}, u32[]{:S(2)}, u32[]{:S(2)}) collective-permute-start(bf16[512,512]{1,0:T(8,128)(2,1)S(1)} %collective-permute-done.1.second.refs_8_), channel_id=1, source_target_pairs={{4,8},{8,4},{5,9},{9,5},{6,10},{10,6},{7,11},{11,7},{20,24},{24,20... | collective-permute-start | bytes 1572872 | tf_op jit(solution)/shard_map/ppermute | solution.py:568
  30.6 19.9 %collective-permute-start.6 = (bf16[512,512]{1,0:T(8,128)(2,1)S(1)}, bf16[512,512]{1,0:T(8,128)(2,1)S(1)}, u32[]{:S(2)}, u32[]{:S(2)}) collective-permute-start(bf16[512,512]{1,0:T(8,128)(2,1)S(1)} %collective-permute-done.5.inner), channel_id=1, source_target_pairs={{4,0},{8,12},{5,1},{9,13},{6,2},{10,14},{7,3},{11,15},{20,16},{24,... | collective-permute-start | bytes 1572872 | tf_op jit(solution)/shard_map/ppermute | solution.py:568
  39.3 12.7 %collective-permute-start.18 = (bf16[512,512]{1,0:T(8,128)(2,1)S(1)}, bf16[512,512]{1,0:T(8,128)(2,1)S(1)}, u32[]{:S(2)}, u32[]{:S(2)}) collective-permute-start(bf16[512,512]{1,0:T(8,128)(2,1)S(1)} %collective-permute-done.4.refs_2_), channel_id=1, source_target_pairs={{4,8},{8,4},{5,9},{9,5},{6,10},{10,6},{7,11},{11,7},{20,24},{24,20... | collective-permute-start | bytes 1572872 | tf_op jit(solution)/shard_map/ppermute | solution.py:568
  41.5 22.4 %collective-permute-start.13 = (bf16[512,512]{1,0:T(8,128)(2,1)S(1)}, bf16[512,512]{1,0:T(8,128)(2,1)S(1)}, u32[]{:S(2)}, u32[]{:S(2)}) collective-permute-start(bf16[512,512]{1,0:T(8,128)(2,1)S(1)} %shard_map.59.third.refs_10_), channel_id=1, source_target_pairs={{0,2},{2,0},{1,3},{3,1},{4,6},{6,4},{5,7},{7,5},{8,10},{10,8},{9,1... | collective-permute-start | bytes 1572872 | tf_op jit(solution)/shard_map/ppermute | solution.py:19
  43.0 21.0 %copy-start.1 = (bf16[512,512]{1,0:T(8,128)(2,1)S(1)}, bf16[512,512]{1,0:T(8,128)(2,1)}, u32[]{:S(2)}) copy-start(bf16[512,512]{1,0:T(8,128)(2,1)} %refs_6_.3) | copy-start | bytes 1572868
  43.0 13.0 %collective-permute-start.3 = (bf16[256,512]{1,0:T(8,128)(2,1)S(1)}, bf16[256,512]{1,0:T(8,128)(2,1)S(1)}, u32[]{:S(2)}, u32[]{:S(2)}) collective-permute-start(bf16[256,512]{1,0:T(8,128)(2,1)S(1)} %get-tuple-element.51.inner), channel_id=1, source_target_pairs={{4,0},{8,12},{5,1},{9,13},{6,2},{10,14},{7,3},{11,15},{20,16},{24,... | collective-permute-start | bytes 786440 | tf_op jit(solution)/shard_map/ppermute | solution.py:568
  50.6 13.3 %collective-permute-start.15 = (bf16[512,512]{1,0:T(8,128)(2,1)S(1)}, bf16[512,512]{1,0:T(8,128)(2,1)S(1)}, u32[]{:S(2)}, u32[]{:S(2)}) collective-permute-start(bf16[512,512]{1,0:T(8,128)(2,1)S(1)} %shard_map.58.refs_4_), channel_id=1, source_target_pairs={{0,1},{1,0},{2,3},{3,2},{4,5},{5,4},{6,7},{7,6},{8,9},{9,8},{10,11... | collective-permute-start | bytes 1572872 | tf_op jit(solution)/shard_map/ppermute | solution.py:19
  50.7 11.1 %collective-permute-start.9 = (bf16[256,512]{1,0:T(8,128)(2,1)S(1)}, bf16[256,512]{1,0:T(8,128)(2,1)S(1)}, u32[]{:S(2)}, u32[]{:S(2)}) collective-permute-start(bf16[256,512]{1,0:T(8,128)(2,1)S(1)} %get-tuple-element.56.inner), channel_id=1, source_target_pairs={{4,0},{8,12},{5,1},{9,13},{6,2},{10,14},{7,3},{11,15},{20,16},{24,... | collective-permute-start | bytes 786440 | tf_op jit(solution)/shard_map/ppermute | solution.py:568
  52.0 20.7 %collective-permute-start.19 = (bf16[512,512]{1,0:T(8,128)(2,1)S(1)}, bf16[512,512]{1,0:T(8,128)(2,1)S(1)}, u32[]{:S(2)}, u32[]{:S(2)}) collective-permute-start(bf16[512,512]{1,0:T(8,128)(2,1)S(1)} %collective-permute-done.18.inner), channel_id=1, source_target_pairs={{4,0},{8,12},{5,1},{9,13},{6,2},{10,14},{7,3},{11,15},{20,16},{24,... | collective-permute-start | bytes 1572872 | tf_op jit(solution)/shard_map/ppermute | solution.py:568
  56.2 7.8 %collective-permute-start.14 = (bf16[512,256]{1,0:T(8,128)(2,1)S(1)}, bf16[512,256]{1,0:T(8,128)(2,1)S(1)}, u32[]{:S(2)}, u32[]{:S(2)}) collective-permute-start(bf16[512,256]{1,0:T(8,128)(2,1)S(1)} %get-tuple-element.55.refs_0_.late_b_0), channel_id=1, source_target_pairs={{0,2},{2,0},{1,3},{3,1},{4,6},{6,4},{5,7},{7,5},{8,10},{10,8},{9,1... | collective-permute-start | bytes 786440 | tf_op jit(solution)/shard_map/ppermute | solution.py:19
  62.0 8.1 %collective-permute-start.17 = (bf16[544,256]{1,0:T(8,128)(2,1)S(1)}, bf16[544,256]{1,0:T(8,128)(2,1)S(1)}, u32[]{:S(2)}, u32[]{:S(2)}) collective-permute-start(bf16[544,256]{1,0:T(8,128)(2,1)S(1)} %shard_map.62.refs_1_.late_b_1), channel_id=1, source_target_pairs={{0,2},{2,0},{1,3},{3,1},{4,6},{6,4},{5,7},{7,5},{8,10},{10,8},{9,1... | collective-permute-start | bytes 835592 | tf_op jit(solution)/shard_map/ppermute | solution.py:19
  68.0 2.1 %collective-permute-start.16 = (f32[8,512]{1,0:T(8,128)S(1)}, f32[8,512]{1,0:T(8,128)S(1)}, u32[]{:S(2)}, u32[]{:S(2)}) collective-permute-start(f32[8,512]{1,0:T(8,128)S(1)} %get-tuple-element.68), channel_id=1, source_target_pairs={{0,1},{1,0},{2,3},{3,2},{4,5},{5,4},{6,7},{7,6},{8,9},{9,8},{10,11... | collective-permute-start | bytes 49160 | tf_op jit(solution)/shard_map/ppermute | solution.py:19
  73.1 2.0 %collective-permute-start.20 = (bf16[528,512]{1,0:T(8,128)(2,1)S(1)}, bf16[528,512]{1,0:T(8,128)(2,1)S(1)}, u32[]{:S(2)}, u32[]{:S(2)}) collective-permute-start(bf16[528,512]{1,0:T(8,128)(2,1)S(1)} %shard_map.64.late.refs_4_), channel_id=1, source_target_pairs={{0,1},{1,0},{2,3},{3,2},{4,5},{5,4},{6,7},{7,6},{8,9},{9,8},{10,11... | collective-permute-start | bytes 1622024 | tf_op jit(solution)/shard_map/ppermute | solution.py:19
  76.5 14.0 %collective-permute-start.23 = (bf16[512,512]{1,0:T(8,128)(2,1)S(1)}, bf16[512,512]{1,0:T(8,128)(2,1)S(1)}, u32[]{:S(2)}, u32[]{:S(2)}) collective-permute-start(bf16[512,512]{1,0:T(8,128)(2,1)S(1)} %get-tuple-element.89), channel_id=1, source_target_pairs={{0,2},{2,0},{1,3},{3,1},{4,6},{6,4},{5,7},{7,5},{8,10},{10,8},{9,1... | collective-permute-start | bytes 1572872 | tf_op jit(solution)/shard_map/ppermute | solution.py:19
  85.9 2.3 %collective-permute-start.21 = (bf16[256,512]{1,0:T(8,128)(2,1)S(1)}, bf16[256,512]{1,0:T(8,128)(2,1)S(1)}, u32[]{:S(2)}, u32[]{:S(2)}) collective-permute-start(bf16[256,512]{1,0:T(8,128)(2,1)S(1)} %get-tuple-element.85), channel_id=1, source_target_pairs={{0,1},{1,0},{2,3},{3,2},{4,5},{5,4},{6,7},{7,6},{8,9},{9,8},{10,11... | collective-permute-start | bytes 786440 | tf_op jit(solution)/shard_map/ppermute | solution.py:19
  85.9 2.3 %collective-permute-start.22 = (bf16[256,512]{1,0:T(8,128)(2,1)S(1)}, bf16[256,512]{1,0:T(8,128)(2,1)S(1)}, u32[]{:S(2)}, u32[]{:S(2)}) collective-permute-start(bf16[256,512]{1,0:T(8,128)(2,1)S(1)} %get-tuple-element.86), channel_id=1, source_target_pairs={{0,1},{1,0},{2,3},{3,2},{4,5},{5,4},{6,7},{7,6},{8,9},{9,8},{10,11... | collective-permute-start | bytes 786440 | tf_op jit(solution)/shard_map/ppermute | solution.py:19
  86.4 1.4 %collective-permute-start.24 = (f32[8,128]{1,0:T(8,128)S(1)}, f32[8,128]{1,0:T(8,128)S(1)}, u32[]{:S(2)}, u32[]{:S(2)}) collective-permute-start(f32[8,128]{1,0:T(8,128)S(1)} %get-tuple-element.90.one), channel_id=1, source_target_pairs={{0,1},{1,0},{2,3},{3,2},{4,5},{5,4},{6,7},{7,6},{8,9},{9,8},{10,11... | collective-permute-start | bytes 12296 | tf_op jit(solution)/shard_map/ppermute | solution.py:19
  87.8 3.7 %collective-permute-start.25 = (f32[8,128]{1,0:T(8,128)S(1)}, f32[8,128]{1,0:T(8,128)S(1)}, u32[]{:S(2)}, u32[]{:S(2)}) collective-permute-start(f32[8,128]{1,0:T(8,128)S(1)} %shard_map.70.one), channel_id=1, source_target_pairs={{0,2},{2,0},{1,3},{3,1},{4,6},{6,4},{5,7},{7,5},{8,10},{10,8},{9,1... | collective-permute-start | bytes 12296 | tf_op jit(solution)/shard_map/ppermute | solution.py:19

commit v18 on v17

--- a/solution.py
+++ b/solution.py
@@ -237,18 +237,25 @@
     second[...] = block[half:, :]
 
 
-def late_left_kernel(images, mask, outer, inner, row, out):
+def late_left_kernel(mask, outer, inner, row, out):
+    for at in range(0, out.shape[0], 64):
+        piece = slice(at, at + 64)
+        out[piece, :] = (pick(mask, outer, inner, piece) - row[0:1, :]).astype(out.dtype)
+
+
+def left_stats_kernel(images, mask, outer, inner, row, stats):
     rows, quart = outer.shape
     shift = row[0:1, :]
     sums = [jnp.zeros((8, quart), jnp.float32)] * 3
-    for at in range(0, rows, 128):
-        piece = slice(at, at + 128)
-        centred = pick(mask, outer, inner, piece) - shift
-        low = centred.astype(jnp.bfloat16)
-        out[piece, :] = low
-        sums = add_sums(sums, centred, low)
+    for at in range(0, rows, 64):
+        centred = pick(mask, outer, inner, slice(at, at + 64)) - shift
+        sums = add_sums(sums, centred, centred.astype(jnp.bfloat16))
     delta, rstd, gap = moments(joined_sums(row, sums), images)
-    out[rows:, :] = split_rows([shift + delta, rstd, gap, delta])
+    stats[...] = rows_of([shift + delta, rstd, gap, delta])
+
+
+def stats_rows(stats):
+    return [stats[i : i + 1, :] for i in range(4)]
 
 
 def late_right_kernel(images, last, mask, outer, inner, row, out, *rest):
@@ -323,9 +330,9 @@
         own_all[:, wide] = dot(low_right[:quart, :], low_left[:, wide])
 
 
-def left_operand(zero, late, target, lanes):
+def left_operand(zero, stats, target, lanes):
     rows, quart = zero.shape
-    _, _, gap, delta = joined_rows(late, rows)
+    _, _, gap, delta = stats_rows(stats)
     high, middle, _ = three_parts(delta)
     target[:rows, lanes] = zero[...]
     extra = [high.astype(jnp.float32), middle.astype(jnp.float32), gap]
@@ -343,7 +350,7 @@
     return columns[:, 0:1], columns[:, 1:2]
 
 
-def partner_kernel(images, part, late, zero, sums, late_b_0, late_b_1, *refs):
+def partner_kernel(images, part, late, stats, zero, sums, late_b_0, late_b_1, *refs):
     if part:
         (terms_in, across_in, vec_in, columns, first_b) = refs[:5]
         (partial_out, e_out, vec_out, left) = refs[5:]
@@ -354,8 +361,8 @@
     late_b = (late_b_0, late_b_1)
     rows, quart = zero.shape
     width = quart // 2
-    _, rstd, _, delta = joined_rows(late, rows)
-    left_operand(zero, late, left, slice(0, quart))
+    _, rstd, _, delta = stats_rows(stats)
+    left_operand(zero, stats, left, slice(0, quart))
     scale_col, delta_col = columns[:, 0:1], columns[:, 1:2]
     across = across_in[...] if part else jnp.zeros((quart, 128), jnp.float32)
     down = []
@@ -388,7 +395,8 @@
 
 
 def own_kernel(images, flags, *refs):
-    late_b, late_b_other, refs = refs[:2], refs[2:4], refs[4:]
+    late_b, late_b_other = refs[:2], refs[2:4]
+    (left_own, left_other), refs = refs[4:6], refs[6:]
     (late_own, late_other, first_own, first_other, zero_own, zero_other, sums) = refs[:7]
     (first_b, first_b_other, e_left, e_right, partner_own, partner_other) = refs[7:13]
     (vec_own, vec_other, right_out, left_out, *left_partials_out, mine_out) = refs[13:20]
@@ -396,11 +404,11 @@
     rows, quart = zero_own.shape
     width = quart // 2
     lower, upper = slice(0, quart), slice(quart, 2 * quart)
-    stats_own, stats_other = joined_rows(late_own, rows), joined_rows(late_other, rows)
+    stats_own, stats_other = stats_rows(left_own), stats_rows(left_other)
     both = lambda i: jnp.concatenate([stats_own[i], stats_other[i]], axis=1)
     offset, rstd, _, delta = [both(i) for i in range(4)]
-    left_operand(zero_own, late_own, left, lower)
-    left_operand(zero_other, late_other, left, upper)
+    left_operand(zero_own, left_own, left, lower)
+    left_operand(zero_other, left_other, left, upper)
     own_b = right_stats(late_b)
     other_b = right_stats(late_b_other)
     for source, stats, lanes in ((first_b, own_b, lower), (first_b_other, other_b, upper)):
@@ -415,7 +423,7 @@
     def tile_corr(late, inner, total, columns, block):
         scale_col, delta_col = columns
         total = total + late_products(block, late, inner)
-        row = joined_rows(late, rows)
+        row = stats_own if late is late_own else stats_other
         return (total * scale_col - delta_col * row[3][:, inner]) * row[1][:, inner]
 
     columns = scale_columns(late_b, images)
@@ -652,17 +660,17 @@
     )
     row_a, late_b_other_1 = after(core_swap(row_other), late_b_other_1)
     late_b_other = (late_b_other_0, late_b_other_1)
-    (late_a,) = local_call(
-        functools.partial(late_left_kernel, batch_images),
-        (mask, last_a, third_a, row_a),
-        (extended,),
-        held=(0, 1, 2, 3),
-    )
+    operands = (mask, last_a, third_a, row_a)
+    (late_a,) = local_call(late_left_kernel, operands, (quarter_bf16,), held=(0, 1, 2, 3))
     late_a_other = core_swap(late_a)
+    (stats_a,) = local_call(
+        functools.partial(left_stats_kernel, batch_images), operands, (row_out,), held=(0, 1, 2, 3)
+    )
+    stats_a_other = core_swap(stats_a)
 
     terms, across, e_left, vec_own, columns = local_call(
         functools.partial(partner_kernel, batch_images, 0),
-        (late_a, zero_own, partner_own, *late_b_other),
+        (late_a, stats_a, zero_own, partner_own, *late_b_other),
         (
             jax.ShapeDtypeStruct((rows + 16, quart), jnp.float32),
             across_shape,
@@ -676,7 +684,7 @@
     )
     partial_right, e_right, vec_other = local_call(
         functools.partial(partner_kernel, batch_images, 1),
-        (late_a_other, zero_other, partner_other, *late_b_other)
+        (late_a_other, stats_a_other, zero_other, partner_other, *late_b_other)
         + (terms, across, vec_own, columns, other_b0),
         (quarter_bf16, quarter_bf16, row_out),
         [low(rows + 16, quart)],
@@ -686,7 +694,7 @@
     from_x = x_swap(partial_right)
     right_own, left_own, *partials_left, mine, loss = local_call(
         functools.partial(own_kernel, batch_images),
-        (flags, *late_b, *late_b_other)
+        (flags, *late_b, *late_b_other, stats_a, stats_a_other)
         + (late_a, late_a_other, left_outputs, other_a0, zero_own, zero_other, own_all)
         + (right_outputs, other_b0, e_left, e_right)
         + (partner_own, partner_other)

time: 92.5 us -> 92.4 us (level)
    ppermute x15 -> x16, waiting for transfers between devices: 7.18 us -> 6.31 us  [swapped(): return lax.ppermute(block, axis, route)]
    ppermute x15 -> x16, starting transfers between devices: 11.8 us -> 12.3 us  [swapped(): return lax.ppermute(block, axis, route)]
    pallas_call x15 -> x16, Pallas kernels: 18.8 us -> 18.9 us  [local_call(): pl.pallas_call(kernel, out_shape=list(outs), in_specs=[space(x) for x in...]
  transfers between devices with their start and end apart: 26 -> 27, of which waited for: 13 -> 12; matrix products, arithmetic and copies ran while one was open for 0% -> 0% of each run, Pallas kernels for 18% -> 18%
where the time goes in v18:
time: 92.4 us; the launch traced here: 92.1 us
  waiting for transfers between devices  43.3 us (47%)
  starting transfers between devices  28.7 us (31%)
  Pallas kernels  18.9 us (20%)
  between operations  1.04 us (1%)
    ppermute x11, waiting for transfers between devices, along(): return lax.ppermute(block, 'dp', route)  37 us
    pallas_call x16, Pallas kernels, local_call(): pl.pallas_call(kernel, out_shape=list(outs), in_specs=[space(x) for x in...  18.9 us
    ppermute x11, starting transfers between devices, along(): return lax.ppermute(block, 'dp', route)  16.3 us
    ppermute x16, starting transfers between devices, swapped(): return lax.ppermute(block, axis, route)  12.3 us
    ppermute x16, waiting for transfers between devices, swapped(): return lax.ppermute(block, axis, route)  6.31 us
  transfers between devices with their start and end apart: 27, of which 12 were waited for; matrix products, arithmetic and copies ran while one was open for 0% of the time, Pallas kernels for 18%

profile of v18, /device:TPU:0, one launch (start us, length us, event | category | flops | bytes accessed | tf_op | source)
XLA Modules:
  0.0 92.1 jit_solution(1022065915739852040)
XLA Ops:
  1.2 2.7 %collective-permute-start.4 = (bf16[512,512]{1,0:T(8,128)(2,1)}, bf16[512,512]{1,0:T(8,128)(2,1)S(1)}, u32[]{:S(2)}, u32[]{:S(2)}) collective-permute-start(bf16[512,512]{1,0:T(8,128)(2,1)} %refs_8_.1), channel_id=1, source_target_pairs={{0,4},{4,0},{8,12},{12,8},{1,5},{5,1},{9,13},{13,9},{2,6},{6,2},{1... | collective-permute-start | bytes 1572872 | tf_op jit(solution)/shard_map/ppermute | solution.py:576
  4.5 1.6 %collective-permute-start.10 = (bf16[512,512]{1,0:T(8,128)(2,1)}, bf16[512,512]{1,0:T(8,128)(2,1)S(1)}, u32[]{:S(2)}, u32[]{:S(2)}) collective-permute-start(bf16[512,512]{1,0:T(8,128)(2,1)} %refs_13_.1), channel_id=1, source_target_pairs={{0,2},{2,0},{1,3},{3,1},{4,6},{6,4},{5,7},{7,5},{8,10},{10,8},{9,1... | collective-permute-start | bytes 1572872 | tf_op jit(solution)/shard_map/ppermute | solution.py:19
  6.1 4.4 %collective-permute-start.1 = (bf16[512,512]{1,0:T(8,128)(2,1)}, bf16[512,512]{1,0:T(8,128)(2,1)S(1)}, u32[]{:S(2)}, u32[]{:S(2)}) collective-permute-start(bf16[512,512]{1,0:T(8,128)(2,1)} %refs_13_.1), channel_id=1, source_target_pairs={{0,4},{4,0},{8,12},{12,8},{1,5},{5,1},{9,13},{13,9},{2,6},{6,2},{1... | collective-permute-start | bytes 1572872 | tf_op jit(solution)/shard_map/ppermute | solution.py:576
  10.5 6.3 %collective-permute-done.4.refs_2_ = bf16[512,512]{1,0:T(8,128)(2,1)S(1)} collective-permute-done((bf16[512,512]{1,0:T(8,128)(2,1)}, bf16[512,512]{1,0:T(8,128)(2,1)S(1)}, u32[]{:S(2)}, u32[]{:S(2)}) %collective-permute-start.4) | collective-permute-done | bytes 524320 | tf_op jit(solution)/shard_map/ppermute | solution.py:576
  16.8 0.7 collective-permute-start.5
  17.5 1.3 %collective-permute-start.8 = (bf16[512,512]{1,0:T(8,128)(2,1)S(1)}, bf16[512,512]{1,0:T(8,128)(2,1)S(1)}, u32[]{:S(2)}, u32[]{:S(2)}) collective-permute-start(bf16[512,512]{1,0:T(8,128)(2,1)S(1)} %collective-permute-done.7.inner), channel_id=1, source_target_pairs={{4,0},{8,12},{5,1},{9,13},{6,2},{10,14},{7,3},{11,15},{20,16},{24,... | collective-permute-start | bytes 1572872 | tf_op jit(solution)/shard_map/ppermute | solution.py:576
  18.9 9.1 %collective-permute-done.1.second.refs_8_ = bf16[512,512]{1,0:T(8,128)(2,1)S(1)} collective-permute-done((bf16[512,512]{1,0:T(8,128)(2,1)}, bf16[512,512]{1,0:T(8,128)(2,1)S(1)}, u32[]{:S(2)}, u32[]{:S(2)}) %collective-permute-start.1) | collective-permute-done | bytes 524320 | tf_op jit(solution)/shard_map/ppermute | solution.py:576
  28.0 1.9 %collective-permute-start.11 = (bf16[512,512]{1,0:T(8,128)(2,1)S(1)}, bf16[512,512]{1,0:T(8,128)(2,1)S(1)}, u32[]{:S(2)}, u32[]{:S(2)}) collective-permute-start(bf16[512,512]{1,0:T(8,128)(2,1)S(1)} %collective-permute-done.1.second.refs_8_), channel_id=1, source_target_pairs={{0,2},{2,0},{1,3},{3,1},{4,6},{6,4},{5,7},{7,5},{8,10},{10,8},{9,1... | collective-permute-start | bytes 1572872 | tf_op jit(solution)/shard_map/ppermute | solution.py:19
  30.6 1.3 %collective-permute-start.6 = (bf16[512,512]{1,0:T(8,128)(2,1)S(1)}, bf16[512,512]{1,0:T(8,128)(2,1)S(1)}, u32[]{:S(2)}, u32[]{:S(2)}) collective-permute-start(bf16[512,512]{1,0:T(8,128)(2,1)S(1)} %collective-permute-done.5.inner), channel_id=1, source_target_pairs={{4,0},{8,12},{5,1},{9,13},{6,2},{10,14},{7,3},{11,15},{20,16},{24,... | collective-permute-start | bytes 1572872 | tf_op jit(solution)/shard_map/ppermute | solution.py:576
  31.9 7.4 %collective-permute-done.8.outer = bf16[512,512]{1,0:T(8,128)(2,1)S(1)} collective-permute-done((bf16[512,512]{1,0:T(8,128)(2,1)S(1)}, bf16[512,512]{1,0:T(8,128)(2,1)S(1)}, u32[]{:S(2)}, u32[]{:S(2)}) %collective-permute-start.8) | collective-permute-done | bytes 524320 | tf_op jit(solution)/shard_map/ppermute | solution.py:576
  40.1 1.4 %collective-permute-done.11.refs_9_ = bf16[512,512]{1,0:T(8,128)(2,1)S(1)} collective-permute-done((bf16[512,512]{1,0:T(8,128)(2,1)S(1)}, bf16[512,512]{1,0:T(8,128)(2,1)S(1)}, u32[]{:S(2)}, u32[]{:S(2)}) %collective-permute-start.11) | collective-permute-done | bytes 524320 | tf_op jit(solution)/shard_map/ppermute | solution.py:19
  41.5 1.5 %collective-permute-start.13 = (bf16[512,512]{1,0:T(8,128)(2,1)S(1)}, bf16[512,512]{1,0:T(8,128)(2,1)S(1)}, u32[]{:S(2)}, u32[]{:S(2)}) collective-permute-start(bf16[512,512]{1,0:T(8,128)(2,1)S(1)} %shard_map.59.third.refs_10_), channel_id=1, source_target_pairs={{0,2},{2,0},{1,3},{3,1},{4,6},{6,4},{5,7},{7,5},{8,10},{10,8},{9,1... | collective-permute-start | bytes 1572872 | tf_op jit(solution)/shard_map/ppermute | solution.py:19
  43.0 1.4 %collective-permute-start.3 = (bf16[256,512]{1,0:T(8,128)(2,1)S(1)}, bf16[256,512]{1,0:T(8,128)(2,1)S(1)}, u32[]{:S(2)}, u32[]{:S(2)}) collective-permute-start(bf16[256,512]{1,0:T(8,128)(2,1)S(1)} %get-tuple-element.51.inner), channel_id=1, source_target_pairs={{4,0},{8,12},{5,1},{9,13},{6,2},{10,14},{7,3},{11,15},{20,16},{24,... | collective-permute-start | bytes 786440 | tf_op jit(solution)/shard_map/ppermute | solution.py:576
  44.4 1.0 %shard_map.60.row = f32[8,512]{1,0:T(8,128)S(1)} custom-call(bf16[512,512]{1,0:T(8,128)(2,1)S(1)} %copy-done, bf16[512,512]{1,0:T(8,128)(2,1)S(1)} %collective-permute-done.1.second.refs_8_, bf16[512,512]{1,0:T(8,128)(2,1)S(1)} %shard_map.59.third.refs_10_), custom_call_target="tpu_custom_call" | custom-call | flops 1048576 | bytes 1589248 | tf_op jit(solution)/shard_map/pallas_call | solution.py:546
  45.4 5.1 %collective-permute-done.6.outer = bf16[512,512]{1,0:T(8,128)(2,1)S(1)} collective-permute-done((bf16[512,512]{1,0:T(8,128)(2,1)S(1)}, bf16[512,512]{1,0:T(8,128)(2,1)S(1)}, u32[]{:S(2)}, u32[]{:S(2)}) %collective-permute-start.6) | collective-permute-done | bytes 524320 | tf_op jit(solution)/shard_map/ppermute | solution.py:576
  50.7 1.3 %collective-permute-start.9 = (bf16[256,512]{1,0:T(8,128)(2,1)S(1)}, bf16[256,512]{1,0:T(8,128)(2,1)S(1)}, u32[]{:S(2)}, u32[]{:S(2)}) collective-permute-start(bf16[256,512]{1,0:T(8,128)(2,1)S(1)} %get-tuple-element.56.inner), channel_id=1, source_target_pairs={{4,0},{8,12},{5,1},{9,13},{6,2},{10,14},{7,3},{11,15},{20,16},{24,... | collective-permute-start | bytes 786440 | tf_op jit(solution)/shard_map/ppermute | solution.py:576
  52.0 1.3 %collective-permute-start.19 = (bf16[512,512]{1,0:T(8,128)(2,1)S(1)}, bf16[512,512]{1,0:T(8,128)(2,1)S(1)}, u32[]{:S(2)}, u32[]{:S(2)}) collective-permute-start(bf16[512,512]{1,0:T(8,128)(2,1)S(1)} %collective-permute-done.18.inner), channel_id=1, source_target_pairs={{4,0},{8,12},{5,1},{9,13},{6,2},{10,14},{7,3},{11,15},{20,16},{24,... | collective-permute-start | bytes 1572872 | tf_op jit(solution)/shard_map/ppermute | solution.py:576
  53.3 2.7 %collective-permute-done.3.outer = bf16[256,512]{1,0:T(8,128)(2,1)S(1)} collective-permute-done((bf16[256,512]{1,0:T(8,128)(2,1)S(1)}, bf16[256,512]{1,0:T(8,128)(2,1)S(1)}, u32[]{:S(2)}, u32[]{:S(2)}) %collective-permute-start.3) | collective-permute-done | bytes 262176 | tf_op jit(solution)/shard_map/ppermute | solution.py:576
  56.2 1.6 %collective-permute-start.14 = (bf16[512,256]{1,0:T(8,128)(2,1)S(1)}, bf16[512,256]{1,0:T(8,128)(2,1)S(1)}, u32[]{:S(2)}, u32[]{:S(2)}) collective-permute-start(bf16[512,256]{1,0:T(8,128)(2,1)S(1)} %get-tuple-element.55.refs_0_.late_b_0), channel_id=1, source_target_pairs={{0,2},{2,0},{1,3},{3,1},{4,6},{6,4},{5,7},{7,5},{8,10},{10,8},{9,1... | collective-permute-start | bytes 786440 | tf_op jit(solution)/shard_map/ppermute | solution.py:19
  57.8 4.0 %collective-permute-done.9.outer = bf16[256,512]{1,0:T(8,128)(2,1)S(1)} collective-permute-done((bf16[256,512]{1,0:T(8,128)(2,1)S(1)}, bf16[256,512]{1,0:T(8,128)(2,1)S(1)}, u32[]{:S(2)}, u32[]{:S(2)}) %collective-permute-start.9) | collective-permute-done | bytes 262176 | tf_op jit(solution)/shard_map/ppermute | solution.py:576
  62.0 1.9 %collective-permute-start.17 = (bf16[544,256]{1,0:T(8,128)(2,1)S(1)}, bf16[544,256]{1,0:T(8,128)(2,1)S(1)}, u32[]{:S(2)}, u32[]{:S(2)}) collective-permute-start(bf16[544,256]{1,0:T(8,128)(2,1)S(1)} %shard_map.62.refs_1_.late_b_1), channel_id=1, source_target_pairs={{0,2},{2,0},{1,3},{3,1},{4,6},{6,4},{5,7},{7,5},{8,10},{10,8},{9,1... | collective-permute-start | bytes 835592 | tf_op jit(solution)/shard_map/ppermute | solution.py:19
  64.0 4.1 %shard_map.63 = (f32[512,512]{1,0:T(8,128)S(1)}, f32[512,512]{1,0:T(8,128)S(1)}, f32[512,1024]{1,0:T(8,128)S(1)}, f32[8,512]{1,0:T(8,128)S(1)}, bf16[512,512]{1,...) custom-call(bf16[512,512]{1,0:T(8,128)(2,1)S(1)} %copy-done.1, bf16[512,512]{1,0:T(8,128)(2,1)S(1)} %collective-permute-done.refs_1_.refs_9_, ...), custom_call_target="tpu_custom_call" | custom-call | flops 1048576 | bytes 65536 | tf_op jit(solution)/shard_map/pallas_call | solution.py:546
  68.1 2.0 %collective-permute-done.17.late_b_1.refs_3_ = bf16[544,256]{1,0:T(8,128)(2,1)S(1)} collective-permute-done((bf16[544,256]{1,0:T(8,128)(2,1)S(1)}, bf16[544,256]{1,0:T(8,128)(2,1)S(1)}, u32[]{:S(2)}, u32[]{:S(2)}) %collective-permute-start.17) | collective-permute-done | bytes 278560 | tf_op jit(solution)/shard_map/ppermute | solution.py:19
  70.2 2.6 %collective-permute-done.19.outer = bf16[512,512]{1,0:T(8,128)(2,1)S(1)} collective-permute-done((bf16[512,512]{1,0:T(8,128)(2,1)S(1)}, bf16[512,512]{1,0:T(8,128)(2,1)S(1)}, u32[]{:S(2)}, u32[]{:S(2)}) %collective-permute-start.19) | collective-permute-done | bytes 524320 | tf_op jit(solution)/shard_map/ppermute | solution.py:576
  73.9 1.1 %shard_map.66 = (f32[528,512]{1,0:T(8,128)S(1)}, f32[512,128]{1,0:T(8,128)S(1)}, bf16[512,512]{1,0:T(8,128)(2,1)S(1)}, f32[8,512]{1,0:T(8,128)S(1)}, f32[512,8]{1,0:T(8,128)S(1)}) custom-call(bf16[512,512]{1,0:T(8,128)(2,1)S(1)} %shard_map.65.late.refs_6_, f32[8,512]{1,0:T(8,128)S(1)} %shard_map.64.stats.refs_4_, ...), custom_call_target="tpu_custom_call" | custom-call | flops 536870912 | bytes 4554752 | tf_op jit(solution)/shard_map/pallas_call | solution.py:546
  75.0 1.4 %shard_map.67 = (bf16[512,512]{1,0:T(8,128)(2,1)S(1)}, bf16[512,512]{1,0:T(8,128)(2,1)S(1)}, f32[8,512]{1,0:T(8,128)S(1)}) custom-call(bf16[512,512]{1,0:T(8,128)(2,1)S(1)} %collective-permute-done.21.late.refs_7_, f32[8,512]{1,0:T(8,128)S(1)} %collective-permute-done.20.stats.refs_5_, bf16[512,512]{1,0:T(8,128)(2,1)S(1)} %get-tuple-element.72.zero.refs_11_, ...), custom_call_target="tpu_custom_call" | custom-call | flops 536870912 | bytes 5619712 | tf_op jit(solution)/shard_map/pallas_call | solution.py:546
  76.5 1.7 %collective-permute-start.24 = (bf16[512,512]{1,0:T(8,128)(2,1)S(1)}, bf16[512,512]{1,0:T(8,128)(2,1)S(1)}, u32[]{:S(2)}, u32[]{:S(2)}) collective-permute-start(bf16[512,512]{1,0:T(8,128)(2,1)S(1)} %get-tuple-element.89), channel_id=1, source_target_pairs={{0,2},{2,0},{1,3},{3,1},{4,6},{6,4},{5,7},{7,5},{8,10},{10,8},{9,1... | collective-permute-start | bytes 1572872 | tf_op jit(solution)/shard_map/ppermute | solution.py:19
  78.2 7.6 %shard_map.68 = (f32[512,512]{1,0:T(8,128)S(1)}, f32[512,512]{1,0:T(8,128)S(1)}, bf16[256,512]{1,0:T(8,128)(2,1)S(1)}, bf16[256,512]{1,0:T(8,128)(2,1)S(1)}, f32[256,1024]{1,0:T(8,128)}, /*index=5*/f32[8,128]{1,0:T(8,128)S(1)}) custom-call(s32[2]{0:T(128)S(1)} %pad_add_fusion.flags, bf16[512,256]{1,0:T(8,128)(2,1)S(1)} %get-tuple-element.55.refs_0_.late_b_0, ...), custom_call_target="tpu_custom_call" | custom-call | flops 2147483648 | bytes 14258184 | tf_op jit(solution)/shard_map/pallas_call | solution.py:546
  86.3 1.4 %collective-permute-done.25.other = f32[8,128]{1,0:T(8,128)S(1)} collective-permute-done((f32[8,128]{1,0:T(8,128)S(1)}, f32[8,128]{1,0:T(8,128)S(1)}, u32[]{:S(2)}, u32[]{:S(2)}) %collective-permute-start.25) | collective-permute-done | bytes 4128 | tf_op jit(solution)/shard_map/ppermute | solution.py:19
  88.1 0.9 shard_map.69
  89.0 1.4 %collective-permute-done.24.from_x = bf16[512,512]{1,0:T(8,128)(2,1)S(1)} collective-permute-done((bf16[512,512]{1,0:T(8,128)(2,1)S(1)}, bf16[512,512]{1,0:T(8,128)(2,1)S(1)}, u32[]{:S(2)}, u32[]{:S(2)}) %collective-permute-start.24) | collective-permute-done | bytes 524320 | tf_op jit(solution)/shard_map/ppermute | solution.py:19
  90.4 0.9 %shard_map.70 = bf16[512,512]{1,0:T(8,128)(2,1)} custom-call(f32[512,512]{1,0:T(8,128)S(1)} %get-tuple-element.88.right, bf16[512,512]{1,0:T(8,128)(2,1)S(1)} %collective-permute-done.24.from_x, bf16[512,256]{1,0:T(8,128)(2,1)S(1)} %get-tuple-element.55.refs_0_.late_b_0, bf16[544,256]{1,0:T(8,128)(2,1)S(1)} %shard_map.62.refs_1_.late_b_1), custom_call_target="tpu_custom_call" | custom-call | flops 1048576 | bytes 2637824 | tf_op jit(solution)/shard_map/pallas_call | solution.py:546
  (44 shorter events, 6.3 us)
Async XLA Ops:
  0.6 43.8 %copy-start = (bf16[512,512]{1,0:T(8,128)(2,1)S(1)}, bf16[512,512]{1,0:T(8,128)(2,1)}, u32[]{:S(2)}) copy-start(bf16[512,512]{1,0:T(8,128)(2,1)} %refs_13_.1) | copy-start | bytes 1572868
  0.6 9.9 %collective-permute-start = (bf16[512,512]{1,0:T(8,128)(2,1)}, bf16[512,512]{1,0:T(8,128)(2,1)S(1)}, u32[]{:S(2)}, u32[]{:S(2)}) collective-permute-start(bf16[512,512]{1,0:T(8,128)(2,1)} %refs_8_.1), channel_id=1, source_target_pairs={{0,1},{1,0},{2,3},{3,2},{4,5},{5,4},{6,7},{7,6},{8,9},{9,8},{10,11... | collective-permute-start | bytes 1572872 | tf_op jit(solution)/shard_map/ppermute | solution.py:19
  1.2 15.6 %collective-permute-start.4 = (bf16[512,512]{1,0:T(8,128)(2,1)}, bf16[512,512]{1,0:T(8,128)(2,1)S(1)}, u32[]{:S(2)}, u32[]{:S(2)}) collective-permute-start(bf16[512,512]{1,0:T(8,128)(2,1)} %refs_8_.1), channel_id=1, source_target_pairs={{0,4},{4,0},{8,12},{12,8},{1,5},{5,1},{9,13},{13,9},{2,6},{6,2},{1... | collective-permute-start | bytes 1572872 | tf_op jit(solution)/shard_map/ppermute | solution.py:576
  3.8 13.7 %collective-permute-start.7 = (bf16[512,512]{1,0:T(8,128)(2,1)}, bf16[512,512]{1,0:T(8,128)(2,1)S(1)}, u32[]{:S(2)}, u32[]{:S(2)}) collective-permute-start(bf16[512,512]{1,0:T(8,128)(2,1)} %refs_13_.1), channel_id=1, source_target_pairs={{4,8},{8,4},{5,9},{9,5},{6,10},{10,6},{7,11},{11,7},{20,24},{24,20... | collective-permute-start | bytes 1572872 | tf_op jit(solution)/shard_map/ppermute | solution.py:576
  4.5 14.4 %collective-permute-start.10 = (bf16[512,512]{1,0:T(8,128)(2,1)}, bf16[512,512]{1,0:T(8,128)(2,1)S(1)}, u32[]{:S(2)}, u32[]{:S(2)}) collective-permute-start(bf16[512,512]{1,0:T(8,128)(2,1)} %refs_13_.1), channel_id=1, source_target_pairs={{0,2},{2,0},{1,3},{3,1},{4,6},{6,4},{5,7},{7,5},{8,10},{10,8},{9,1... | collective-permute-start | bytes 1572872 | tf_op jit(solution)/shard_map/ppermute | solution.py:19
  6.1 22.0 %collective-permute-start.1 = (bf16[512,512]{1,0:T(8,128)(2,1)}, bf16[512,512]{1,0:T(8,128)(2,1)S(1)}, u32[]{:S(2)}, u32[]{:S(2)}) collective-permute-start(bf16[512,512]{1,0:T(8,128)(2,1)} %refs_13_.1), channel_id=1, source_target_pairs={{0,4},{4,0},{8,12},{12,8},{1,5},{5,1},{9,13},{13,9},{2,6},{6,2},{1... | collective-permute-start | bytes 1572872 | tf_op jit(solution)/shard_map/ppermute | solution.py:576
  16.8 13.8 %collective-permute-start.5 = (bf16[512,512]{1,0:T(8,128)(2,1)}, bf16[512,512]{1,0:T(8,128)(2,1)S(1)}, u32[]{:S(2)}, u32[]{:S(2)}) collective-permute-start(bf16[512,512]{1,0:T(8,128)(2,1)} %refs_8_.1), channel_id=1, source_target_pairs={{4,8},{8,4},{5,9},{9,5},{6,10},{10,6},{7,11},{11,7},{20,24},{24,20... | collective-permute-start | bytes 1572872 | tf_op jit(solution)/shard_map/ppermute | solution.py:576
  17.5 21.8 %collective-permute-start.8 = (bf16[512,512]{1,0:T(8,128)(2,1)S(1)}, bf16[512,512]{1,0:T(8,128)(2,1)S(1)}, u32[]{:S(2)}, u32[]{:S(2)}) collective-permute-start(bf16[512,512]{1,0:T(8,128)(2,1)S(1)} %collective-permute-done.7.inner), channel_id=1, source_target_pairs={{4,0},{8,12},{5,1},{9,13},{6,2},{10,14},{7,3},{11,15},{20,16},{24,... | collective-permute-start | bytes 1572872 | tf_op jit(solution)/shard_map/ppermute | solution.py:576
  18.8 21.3 %collective-permute-start.12 = (bf16[512,512]{1,0:T(8,128)(2,1)S(1)}, bf16[512,512]{1,0:T(8,128)(2,1)S(1)}, u32[]{:S(2)}, u32[]{:S(2)}) collective-permute-start(bf16[512,512]{1,0:T(8,128)(2,1)S(1)} %collective-permute-done.4.refs_2_), channel_id=1, source_target_pairs={{0,1},{1,0},{2,3},{3,2},{4,5},{5,4},{6,7},{7,6},{8,9},{9,8},{10,11... | collective-permute-start | bytes 1572872 | tf_op jit(solution)/shard_map/ppermute | solution.py:19
  28.0 13.4 %collective-permute-start.11 = (bf16[512,512]{1,0:T(8,128)(2,1)S(1)}, bf16[512,512]{1,0:T(8,128)(2,1)S(1)}, u32[]{:S(2)}, u32[]{:S(2)}) collective-permute-start(bf16[512,512]{1,0:T(8,128)(2,1)S(1)} %collective-permute-done.1.second.refs_8_), channel_id=1, source_target_pairs={{0,2},{2,0},{1,3},{3,1},{4,6},{6,4},{5,7},{7,5},{8,10},{10,8},{9,1... | collective-permute-start | bytes 1572872 | tf_op jit(solution)/shard_map/ppermute | solution.py:19
  29.9 13.0 %collective-permute-start.2 = (bf16[512,512]{1,0:T(8,128)(2,1)S(1)}, bf16[512,512]{1,0:T(8,128)(2,1)S(1)}, u32[]{:S(2)}, u32[]{:S(2)}) collective-permute-start(bf16[512,512]{1,0:T(8,128)(2,1)S(1)} %collective-permute-done.1.second.refs_8_), channel_id=1, source_target_pairs={{4,8},{8,4},{5,9},{9,5},{6,10},{10,6},{7,11},{11,7},{20,24},{24,20... | collective-permute-start | bytes 1572872 | tf_op jit(solution)/shard_map/ppermute | solution.py:576
  30.6 19.9 %collective-permute-start.6 = (bf16[512,512]{1,0:T(8,128)(2,1)S(1)}, bf16[512,512]{1,0:T(8,128)(2,1)S(1)}, u32[]{:S(2)}, u32[]{:S(2)}) collective-permute-start(bf16[512,512]{1,0:T(8,128)(2,1)S(1)} %collective-permute-done.5.inner), channel_id=1, source_target_pairs={{4,0},{8,12},{5,1},{9,13},{6,2},{10,14},{7,3},{11,15},{20,16},{24,... | collective-permute-start | bytes 1572872 | tf_op jit(solution)/shard_map/ppermute | solution.py:576
  39.3 12.7 %collective-permute-start.18 = (bf16[512,512]{1,0:T(8,128)(2,1)S(1)}, bf16[512,512]{1,0:T(8,128)(2,1)S(1)}, u32[]{:S(2)}, u32[]{:S(2)}) collective-permute-start(bf16[512,512]{1,0:T(8,128)(2,1)S(1)} %collective-permute-done.4.refs_2_), channel_id=1, source_target_pairs={{4,8},{8,4},{5,9},{9,5},{6,10},{10,6},{7,11},{11,7},{20,24},{24,20... | collective-permute-start | bytes 1572872 | tf_op jit(solution)/shard_map/ppermute | solution.py:576
  41.5 22.4 %collective-permute-start.13 = (bf16[512,512]{1,0:T(8,128)(2,1)S(1)}, bf16[512,512]{1,0:T(8,128)(2,1)S(1)}, u32[]{:S(2)}, u32[]{:S(2)}) collective-permute-start(bf16[512,512]{1,0:T(8,128)(2,1)S(1)} %shard_map.59.third.refs_10_), channel_id=1, source_target_pairs={{0,2},{2,0},{1,3},{3,1},{4,6},{6,4},{5,7},{7,5},{8,10},{10,8},{9,1... | collective-permute-start | bytes 1572872 | tf_op jit(solution)/shard_map/ppermute | solution.py:19
  43.0 21.0 %copy-start.1 = (bf16[512,512]{1,0:T(8,128)(2,1)S(1)}, bf16[512,512]{1,0:T(8,128)(2,1)}, u32[]{:S(2)}) copy-start(bf16[512,512]{1,0:T(8,128)(2,1)} %refs_8_.1) | copy-start | bytes 1572868
  43.0 13.0 %collective-permute-start.3 = (bf16[256,512]{1,0:T(8,128)(2,1)S(1)}, bf16[256,512]{1,0:T(8,128)(2,1)S(1)}, u32[]{:S(2)}, u32[]{:S(2)}) collective-permute-start(bf16[256,512]{1,0:T(8,128)(2,1)S(1)} %get-tuple-element.51.inner), channel_id=1, source_target_pairs={{4,0},{8,12},{5,1},{9,13},{6,2},{10,14},{7,3},{11,15},{20,16},{24,... | collective-permute-start | bytes 786440 | tf_op jit(solution)/shard_map/ppermute | solution.py:576
  50.6 13.3 %collective-permute-start.15 = (bf16[512,512]{1,0:T(8,128)(2,1)S(1)}, bf16[512,512]{1,0:T(8,128)(2,1)S(1)}, u32[]{:S(2)}, u32[]{:S(2)}) collective-permute-start(bf16[512,512]{1,0:T(8,128)(2,1)S(1)} %shard_map.58.refs_4_), channel_id=1, source_target_pairs={{0,1},{1,0},{2,3},{3,2},{4,5},{5,4},{6,7},{7,6},{8,9},{9,8},{10,11... | collective-permute-start | bytes 1572872 | tf_op jit(solution)/shard_map/ppermute | solution.py:19
  50.7 11.1 %collective-permute-start.9 = (bf16[256,512]{1,0:T(8,128)(2,1)S(1)}, bf16[256,512]{1,0:T(8,128)(2,1)S(1)}, u32[]{:S(2)}, u32[]{:S(2)}) collective-permute-start(bf16[256,512]{1,0:T(8,128)(2,1)S(1)} %get-tuple-element.56.inner), channel_id=1, source_target_pairs={{4,0},{8,12},{5,1},{9,13},{6,2},{10,14},{7,3},{11,15},{20,16},{24,... | collective-permute-start | bytes 786440 | tf_op jit(solution)/shard_map/ppermute | solution.py:576
  52.0 20.7 %collective-permute-start.19 = (bf16[512,512]{1,0:T(8,128)(2,1)S(1)}, bf16[512,512]{1,0:T(8,128)(2,1)S(1)}, u32[]{:S(2)}, u32[]{:S(2)}) collective-permute-start(bf16[512,512]{1,0:T(8,128)(2,1)S(1)} %collective-permute-done.18.inner), channel_id=1, source_target_pairs={{4,0},{8,12},{5,1},{9,13},{6,2},{10,14},{7,3},{11,15},{20,16},{24,... | collective-permute-start | bytes 1572872 | tf_op jit(solution)/shard_map/ppermute | solution.py:576
  56.2 7.8 %collective-permute-start.14 = (bf16[512,256]{1,0:T(8,128)(2,1)S(1)}, bf16[512,256]{1,0:T(8,128)(2,1)S(1)}, u32[]{:S(2)}, u32[]{:S(2)}) collective-permute-start(bf16[512,256]{1,0:T(8,128)(2,1)S(1)} %get-tuple-element.55.refs_0_.late_b_0), channel_id=1, source_target_pairs={{0,2},{2,0},{1,3},{3,1},{4,6},{6,4},{5,7},{7,5},{8,10},{10,8},{9,1... | collective-permute-start | bytes 786440 | tf_op jit(solution)/shard_map/ppermute | solution.py:19
  62.0 8.1 %collective-permute-start.17 = (bf16[544,256]{1,0:T(8,128)(2,1)S(1)}, bf16[544,256]{1,0:T(8,128)(2,1)S(1)}, u32[]{:S(2)}, u32[]{:S(2)}) collective-permute-start(bf16[544,256]{1,0:T(8,128)(2,1)S(1)} %shard_map.62.refs_1_.late_b_1), channel_id=1, source_target_pairs={{0,2},{2,0},{1,3},{3,1},{4,6},{6,4},{5,7},{7,5},{8,10},{10,8},{9,1... | collective-permute-start | bytes 835592 | tf_op jit(solution)/shard_map/ppermute | solution.py:19
  68.0 2.1 %collective-permute-start.16 = (f32[8,512]{1,0:T(8,128)S(1)}, f32[8,512]{1,0:T(8,128)S(1)}, u32[]{:S(2)}, u32[]{:S(2)}) collective-permute-start(f32[8,512]{1,0:T(8,128)S(1)} %get-tuple-element.68), channel_id=1, source_target_pairs={{0,1},{1,0},{2,3},{3,2},{4,5},{5,4},{6,7},{7,6},{8,9},{9,8},{10,11... | collective-permute-start | bytes 49160 | tf_op jit(solution)/shard_map/ppermute | solution.py:19
  72.9 2.1 %collective-permute-start.21 = (bf16[512,512]{1,0:T(8,128)(2,1)S(1)}, bf16[512,512]{1,0:T(8,128)(2,1)S(1)}, u32[]{:S(2)}, u32[]{:S(2)}) collective-permute-start(bf16[512,512]{1,0:T(8,128)(2,1)S(1)} %shard_map.65.late.refs_6_), channel_id=1, source_target_pairs={{0,1},{1,0},{2,3},{3,2},{4,5},{5,4},{6,7},{7,6},{8,9},{9,8},{10,11... | collective-permute-start | bytes 1572872 | tf_op jit(solution)/shard_map/ppermute | solution.py:19
  73.3 1.7 %collective-permute-start.20 = (f32[8,512]{1,0:T(8,128)S(1)}, f32[8,512]{1,0:T(8,128)S(1)}, u32[]{:S(2)}, u32[]{:S(2)}) collective-permute-start(f32[8,512]{1,0:T(8,128)S(1)} %shard_map.64.stats.refs_4_), channel_id=1, source_target_pairs={{0,1},{1,0},{2,3},{3,2},{4,5},{5,4},{6,7},{7,6},{8,9},{9,8},{10,11... | collective-permute-start | bytes 49160 | tf_op jit(solution)/shard_map/ppermute | solution.py:19
  76.5 13.9 %collective-permute-start.24 = (bf16[512,512]{1,0:T(8,128)(2,1)S(1)}, bf16[512,512]{1,0:T(8,128)(2,1)S(1)}, u32[]{:S(2)}, u32[]{:S(2)}) collective-permute-start(bf16[512,512]{1,0:T(8,128)(2,1)S(1)} %get-tuple-element.89), channel_id=1, source_target_pairs={{0,2},{2,0},{1,3},{3,1},{4,6},{6,4},{5,7},{7,5},{8,10},{10,8},{9,1... | collective-permute-start | bytes 1572872 | tf_op jit(solution)/shard_map/ppermute | solution.py:19
  85.8 2.3 %collective-permute-start.22 = (bf16[256,512]{1,0:T(8,128)(2,1)S(1)}, bf16[256,512]{1,0:T(8,128)(2,1)S(1)}, u32[]{:S(2)}, u32[]{:S(2)}) collective-permute-start(bf16[256,512]{1,0:T(8,128)(2,1)S(1)} %get-tuple-element.85), channel_id=1, source_target_pairs={{0,1},{1,0},{2,3},{3,2},{4,5},{5,4},{6,7},{7,6},{8,9},{9,8},{10,11... | collective-permute-start | bytes 786440 | tf_op jit(solution)/shard_map/ppermute | solution.py:19
  85.8 2.3 %collective-permute-start.23 = (bf16[256,512]{1,0:T(8,128)(2,1)S(1)}, bf16[256,512]{1,0:T(8,128)(2,1)S(1)}, u32[]{:S(2)}, u32[]{:S(2)}) collective-permute-start(bf16[256,512]{1,0:T(8,128)(2,1)S(1)} %get-tuple-element.86), channel_id=1, source_target_pairs={{0,1},{1,0},{2,3},{3,2},{4,5},{5,4},{6,7},{7,6},{8,9},{9,8},{10,11... | collective-permute-start | bytes 786440 | tf_op jit(solution)/shard_map/ppermute | solution.py:19
  86.3 1.4 %collective-permute-start.25 = (f32[8,128]{1,0:T(8,128)S(1)}, f32[8,128]{1,0:T(8,128)S(1)}, u32[]{:S(2)}, u32[]{:S(2)}) collective-permute-start(f32[8,128]{1,0:T(8,128)S(1)} %get-tuple-element.90.one), channel_id=1, source_target_pairs={{0,1},{1,0},{2,3},{3,2},{4,5},{5,4},{6,7},{7,6},{8,9},{9,8},{10,11... | collective-permute-start | bytes 12296 | tf_op jit(solution)/shard_map/ppermute | solution.py:19
  87.8 3.6 %collective-permute-start.26 = (f32[8,128]{1,0:T(8,128)S(1)}, f32[8,128]{1,0:T(8,128)S(1)}, u32[]{:S(2)}, u32[]{:S(2)}) collective-permute-start(f32[8,128]{1,0:T(8,128)S(1)} %shard_map.71.one), channel_id=1, source_target_pairs={{0,2},{2,0},{1,3},{3,1},{4,6},{6,4},{5,7},{7,5},{8,10},{10,8},{9,1... | collective-permute-start | bytes 12296 | tf_op jit(solution)/shard_map/ppermute | solution.py:19

commit v19 on v18

--- a/solution.py
+++ b/solution.py
@@ -350,14 +350,18 @@
     return columns[:, 0:1], columns[:, 1:2]
 
 
-def partner_kernel(images, part, late, stats, zero, sums, late_b_0, late_b_1, *refs):
+def right_columns_kernel(images, late_b_0, late_b_1, columns, rows_b):
+    offset, rstd, gap, delta = right_stats((late_b_0, late_b_1))
+    columns[...] = jnp.transpose(rows_of([rstd / images, delta * rstd]))
+    rows_b[...] = rows_of([offset, rstd, gap, delta])
+
+
+def partner_kernel(images, part, late, stats, zero, sums, late_b_0, late_b_1, columns, rows_b, *refs):
     if part:
-        (terms_in, across_in, vec_in, columns, first_b) = refs[:5]
-        (partial_out, e_out, vec_out, left) = refs[5:]
+        (terms_in, across_in, vec_in, first_b) = refs[:4]
+        (partial_out, e_out, vec_out, left) = refs[4:]
     else:
-        (terms_out, across_out, e_out, vec_out, columns, left) = refs
-        _, rstd_b, _, delta_b = right_stats((late_b_0, late_b_1))
-        columns[...] = jnp.transpose(rows_of([rstd_b / images, delta_b * rstd_b]))
+        (terms_out, across_out, e_out, vec_out, left) = refs
     late_b = (late_b_0, late_b_1)
     rows, quart = zero.shape
     width = quart // 2
@@ -378,7 +382,7 @@
     if part:
         vec_out[...] = rows_of([second_a, second_a + vec_in[0:1, :]])
         second = off_weight * lanes_to_row(across)
-        offset_b, rstd_b, _, _ = right_stats(late_b)
+        offset_b, rstd_b, _, _ = stats_rows(rows_b)
     else:
         vec_out[...] = rows_of([second_a])
         across_out[...] = across
@@ -660,6 +664,12 @@
     )
     row_a, late_b_other_1 = after(core_swap(row_other), late_b_other_1)
     late_b_other = (late_b_other_0, late_b_other_1)
+    columns, rows_b = local_call(
+        functools.partial(right_columns_kernel, batch_images),
+        late_b_other,
+        (jax.ShapeDtypeStruct((quart, 8), jnp.float32), row_out),
+    )
+    row_a, columns = after(row_a, columns)
     operands = (mask, last_a, third_a, row_a)
     (late_a,) = local_call(late_left_kernel, operands, (quarter_bf16,), held=(0, 1, 2, 3))
     late_a_other = core_swap(late_a)
@@ -668,15 +678,14 @@
     )
     stats_a_other = core_swap(stats_a)
 
-    terms, across, e_left, vec_own, columns = local_call(
+    terms, across, e_left, vec_own = local_call(
         functools.partial(partner_kernel, batch_images, 0),
-        (late_a, stats_a, zero_own, partner_own, *late_b_other),
+        (late_a, stats_a, zero_own, partner_own, *late_b_other, columns, rows_b),
         (
             jax.ShapeDtypeStruct((rows + 16, quart), jnp.float32),
             across_shape,
             quarter_bf16,
             row_out,
-            jax.ShapeDtypeStruct((quart, 8), jnp.float32),
         ),
         [low(rows + 16, quart)],
         2 * gemm,
@@ -685,7 +694,7 @@
     partial_right, e_right, vec_other = local_call(
         functools.partial(partner_kernel, batch_images, 1),
         (late_a_other, stats_a_other, zero_other, partner_other, *late_b_other)
-        + (terms, across, vec_own, columns, other_b0),
+        + (columns, rows_b, terms, across, vec_own, other_b0),
         (quarter_bf16, quarter_bf16, row_out),
         [low(rows + 16, quart)],
         2 * gemm,

time: 92.4 us -> 92.3 us (level)
    pallas_call x16 -> x17, Pallas kernels: 18.9 us -> 19 us  [local_call(): pl.pallas_call(kernel, out_shape=list(outs), in_specs=[space(x) for x in...]
where the time goes in v19:
time: 92.3 us; the launch traced here: 92.1 us
  waiting for transfers between devices  43.2 us (47%)
  starting transfers between devices  28.7 us (31%)
  Pallas kernels  19 us (21%)
  between operations  1.05 us (1%)
    ppermute x11, waiting for transfers between devices, along(): return lax.ppermute(block, 'dp', route)  36.9 us
    pallas_call x17, Pallas kernels, local_call(): pl.pallas_call(kernel, out_shape=list(outs), in_specs=[space(x) for x in...  19 us
    ppermute x11, starting transfers between devices, along(): return lax.ppermute(block, 'dp', route)  16.3 us
    ppermute x16, starting transfers between devices, swapped(): return lax.ppermute(block, axis, route)  12.3 us
    ppermute x16, waiting for transfers between devices, swapped(): return lax.ppermute(block, axis, route)  6.35 us
  transfers between devices with their start and end apart: 27, of which 12 were waited for; matrix products, arithmetic and copies ran while one was open for 0% of the time, Pallas kernels for 18%

profile of v19, /device:TPU:0, one launch (start us, length us, event | category | flops | bytes accessed | tf_op | source)
XLA Modules:
  0.0 92.1 jit_solution(1003752024597546587)
XLA Ops:
  1.2 2.7 %collective-permute-start.4 = (bf16[512,512]{1,0:T(8,128)(2,1)}, bf16[512,512]{1,0:T(8,128)(2,1)S(1)}, u32[]{:S(2)}, u32[]{:S(2)}) collective-permute-start(bf16[512,512]{1,0:T(8,128)(2,1)} %refs_8_.1), channel_id=1, source_target_pairs={{0,4},{4,0},{8,12},{12,8},{1,5},{5,1},{9,13},{13,9},{2,6},{6,2},{1... | collective-permute-start | bytes 1572872 | tf_op jit(solution)/shard_map/ppermute | solution.py:580
  4.5 1.6 %collective-permute-start.10 = (bf16[512,512]{1,0:T(8,128)(2,1)}, bf16[512,512]{1,0:T(8,128)(2,1)S(1)}, u32[]{:S(2)}, u32[]{:S(2)}) collective-permute-start(bf16[512,512]{1,0:T(8,128)(2,1)} %refs_13_.1), channel_id=1, source_target_pairs={{0,2},{2,0},{1,3},{3,1},{4,6},{6,4},{5,7},{7,5},{8,10},{10,8},{9,1... | collective-permute-start | bytes 1572872 | tf_op jit(solution)/shard_map/ppermute | solution.py:19
  6.1 4.4 %collective-permute-start.1 = (bf16[512,512]{1,0:T(8,128)(2,1)}, bf16[512,512]{1,0:T(8,128)(2,1)S(1)}, u32[]{:S(2)}, u32[]{:S(2)}) collective-permute-start(bf16[512,512]{1,0:T(8,128)(2,1)} %refs_13_.1), channel_id=1, source_target_pairs={{0,4},{4,0},{8,12},{12,8},{1,5},{5,1},{9,13},{13,9},{2,6},{6,2},{1... | collective-permute-start | bytes 1572872 | tf_op jit(solution)/shard_map/ppermute | solution.py:580
  10.5 6.3 %collective-permute-done.4.refs_2_ = bf16[512,512]{1,0:T(8,128)(2,1)S(1)} collective-permute-done((bf16[512,512]{1,0:T(8,128)(2,1)}, bf16[512,512]{1,0:T(8,128)(2,1)S(1)}, u32[]{:S(2)}, u32[]{:S(2)}) %collective-permute-start.4) | collective-permute-done | bytes 524320 | tf_op jit(solution)/shard_map/ppermute | solution.py:580
  17.5 1.3 %collective-permute-start.8 = (bf16[512,512]{1,0:T(8,128)(2,1)S(1)}, bf16[512,512]{1,0:T(8,128)(2,1)S(1)}, u32[]{:S(2)}, u32[]{:S(2)}) collective-permute-start(bf16[512,512]{1,0:T(8,128)(2,1)S(1)} %collective-permute-done.7.inner), channel_id=1, source_target_pairs={{4,0},{8,12},{5,1},{9,13},{6,2},{10,14},{7,3},{11,15},{20,16},{24,... | collective-permute-start | bytes 1572872 | tf_op jit(solution)/shard_map/ppermute | solution.py:580
  18.9 9.1 %collective-permute-done.1.second.refs_8_ = bf16[512,512]{1,0:T(8,128)(2,1)S(1)} collective-permute-done((bf16[512,512]{1,0:T(8,128)(2,1)}, bf16[512,512]{1,0:T(8,128)(2,1)S(1)}, u32[]{:S(2)}, u32[]{:S(2)}) %collective-permute-start.1) | collective-permute-done | bytes 524320 | tf_op jit(solution)/shard_map/ppermute | solution.py:580
  28.0 1.9 %collective-permute-start.11 = (bf16[512,512]{1,0:T(8,128)(2,1)S(1)}, bf16[512,512]{1,0:T(8,128)(2,1)S(1)}, u32[]{:S(2)}, u32[]{:S(2)}) collective-permute-start(bf16[512,512]{1,0:T(8,128)(2,1)S(1)} %collective-permute-done.1.second.refs_8_), channel_id=1, source_target_pairs={{0,2},{2,0},{1,3},{3,1},{4,6},{6,4},{5,7},{7,5},{8,10},{10,8},{9,1... | collective-permute-start | bytes 1572872 | tf_op jit(solution)/shard_map/ppermute | solution.py:19
  30.6 1.3 %collective-permute-start.6 = (bf16[512,512]{1,0:T(8,128)(2,1)S(1)}, bf16[512,512]{1,0:T(8,128)(2,1)S(1)}, u32[]{:S(2)}, u32[]{:S(2)}) collective-permute-start(bf16[512,512]{1,0:T(8,128)(2,1)S(1)} %collective-permute-done.5.inner), channel_id=1, source_target_pairs={{4,0},{8,12},{5,1},{9,13},{6,2},{10,14},{7,3},{11,15},{20,16},{24,... | collective-permute-start | bytes 1572872 | tf_op jit(solution)/shard_map/ppermute | solution.py:580
  31.9 7.4 %collective-permute-done.8.outer = bf16[512,512]{1,0:T(8,128)(2,1)S(1)} collective-permute-done((bf16[512,512]{1,0:T(8,128)(2,1)S(1)}, bf16[512,512]{1,0:T(8,128)(2,1)S(1)}, u32[]{:S(2)}, u32[]{:S(2)}) %collective-permute-start.8) | collective-permute-done | bytes 524320 | tf_op jit(solution)/shard_map/ppermute | solution.py:580
  39.3 0.7 collective-permute-start.18
  40.1 1.4 %collective-permute-done.11.refs_9_ = bf16[512,512]{1,0:T(8,128)(2,1)S(1)} collective-permute-done((bf16[512,512]{1,0:T(8,128)(2,1)S(1)}, bf16[512,512]{1,0:T(8,128)(2,1)S(1)}, u32[]{:S(2)}, u32[]{:S(2)}) %collective-permute-start.11) | collective-permute-done | bytes 524320 | tf_op jit(solution)/shard_map/ppermute | solution.py:19
  41.5 1.5 %collective-permute-start.13 = (bf16[512,512]{1,0:T(8,128)(2,1)S(1)}, bf16[512,512]{1,0:T(8,128)(2,1)S(1)}, u32[]{:S(2)}, u32[]{:S(2)}) collective-permute-start(bf16[512,512]{1,0:T(8,128)(2,1)S(1)} %shard_map.59.third.refs_10_), channel_id=1, source_target_pairs={{0,2},{2,0},{1,3},{3,1},{4,6},{6,4},{5,7},{7,5},{8,10},{10,8},{9,1... | collective-permute-start | bytes 1572872 | tf_op jit(solution)/shard_map/ppermute | solution.py:19
  43.0 1.4 %collective-permute-start.3 = (bf16[256,512]{1,0:T(8,128)(2,1)S(1)}, bf16[256,512]{1,0:T(8,128)(2,1)S(1)}, u32[]{:S(2)}, u32[]{:S(2)}) collective-permute-start(bf16[256,512]{1,0:T(8,128)(2,1)S(1)} %get-tuple-element.54.inner), channel_id=1, source_target_pairs={{4,0},{8,12},{5,1},{9,13},{6,2},{10,14},{7,3},{11,15},{20,16},{24,... | collective-permute-start | bytes 786440 | tf_op jit(solution)/shard_map/ppermute | solution.py:580
  44.4 1.0 %shard_map.60.row = f32[8,512]{1,0:T(8,128)S(1)} custom-call(bf16[512,512]{1,0:T(8,128)(2,1)S(1)} %copy-done, bf16[512,512]{1,0:T(8,128)(2,1)S(1)} %collective-permute-done.1.second.refs_8_, bf16[512,512]{1,0:T(8,128)(2,1)S(1)} %shard_map.59.third.refs_10_), custom_call_target="tpu_custom_call" | custom-call | flops 1048576 | bytes 1589248 | tf_op jit(solution)/shard_map/pallas_call | solution.py:550
  45.4 5.1 %collective-permute-done.6.outer = bf16[512,512]{1,0:T(8,128)(2,1)S(1)} collective-permute-done((bf16[512,512]{1,0:T(8,128)(2,1)S(1)}, bf16[512,512]{1,0:T(8,128)(2,1)S(1)}, u32[]{:S(2)}, u32[]{:S(2)}) %collective-permute-start.6) | collective-permute-done | bytes 524320 | tf_op jit(solution)/shard_map/ppermute | solution.py:580
  50.7 1.3 %collective-permute-start.9 = (bf16[256,512]{1,0:T(8,128)(2,1)S(1)}, bf16[256,512]{1,0:T(8,128)(2,1)S(1)}, u32[]{:S(2)}, u32[]{:S(2)}) collective-permute-start(bf16[256,512]{1,0:T(8,128)(2,1)S(1)} %get-tuple-element.59.inner), channel_id=1, source_target_pairs={{4,0},{8,12},{5,1},{9,13},{6,2},{10,14},{7,3},{11,15},{20,16},{24,... | collective-permute-start | bytes 786440 | tf_op jit(solution)/shard_map/ppermute | solution.py:580
  52.0 1.3 %collective-permute-start.19 = (bf16[512,512]{1,0:T(8,128)(2,1)S(1)}, bf16[512,512]{1,0:T(8,128)(2,1)S(1)}, u32[]{:S(2)}, u32[]{:S(2)}) collective-permute-start(bf16[512,512]{1,0:T(8,128)(2,1)S(1)} %collective-permute-done.18.inner), channel_id=1, source_target_pairs={{4,0},{8,12},{5,1},{9,13},{6,2},{10,14},{7,3},{11,15},{20,16},{24,... | collective-permute-start | bytes 1572872 | tf_op jit(solution)/shard_map/ppermute | solution.py:580
  53.3 2.7 %collective-permute-done.3.outer = bf16[256,512]{1,0:T(8,128)(2,1)S(1)} collective-permute-done((bf16[256,512]{1,0:T(8,128)(2,1)S(1)}, bf16[256,512]{1,0:T(8,128)(2,1)S(1)}, u32[]{:S(2)}, u32[]{:S(2)}) %collective-permute-start.3) | collective-permute-done | bytes 262176 | tf_op jit(solution)/shard_map/ppermute | solution.py:580
  56.2 1.6 %collective-permute-start.14 = (bf16[512,256]{1,0:T(8,128)(2,1)S(1)}, bf16[512,256]{1,0:T(8,128)(2,1)S(1)}, u32[]{:S(2)}, u32[]{:S(2)}) collective-permute-start(bf16[512,256]{1,0:T(8,128)(2,1)S(1)} %get-tuple-element.58.refs_0_.late_b_0), channel_id=1, source_target_pairs={{0,2},{2,0},{1,3},{3,1},{4,6},{6,4},{5,7},{7,5},{8,10},{10,8},{9,1... | collective-permute-start | bytes 786440 | tf_op jit(solution)/shard_map/ppermute | solution.py:19
  57.8 4.0 %collective-permute-done.9.outer = bf16[256,512]{1,0:T(8,128)(2,1)S(1)} collective-permute-done((bf16[256,512]{1,0:T(8,128)(2,1)S(1)}, bf16[256,512]{1,0:T(8,128)(2,1)S(1)}, u32[]{:S(2)}, u32[]{:S(2)}) %collective-permute-start.9) | collective-permute-done | bytes 262176 | tf_op jit(solution)/shard_map/ppermute | solution.py:580
  62.0 1.9 %collective-permute-start.17 = (bf16[544,256]{1,0:T(8,128)(2,1)S(1)}, bf16[544,256]{1,0:T(8,128)(2,1)S(1)}, u32[]{:S(2)}, u32[]{:S(2)}) collective-permute-start(bf16[544,256]{1,0:T(8,128)(2,1)S(1)} %shard_map.62.refs_1_.late_b_1), channel_id=1, source_target_pairs={{0,2},{2,0},{1,3},{3,1},{4,6},{6,4},{5,7},{7,5},{8,10},{10,8},{9,1... | collective-permute-start | bytes 835592 | tf_op jit(solution)/shard_map/ppermute | solution.py:19
  64.0 4.1 %shard_map.63 = (f32[512,512]{1,0:T(8,128)S(1)}, f32[512,512]{1,0:T(8,128)S(1)}, f32[512,1024]{1,0:T(8,128)S(1)}, f32[8,512]{1,0:T(8,128)S(1)}, bf16[512,512]{1,...) custom-call(bf16[512,512]{1,0:T(8,128)(2,1)S(1)} %copy-done.1, bf16[512,512]{1,0:T(8,128)(2,1)S(1)} %collective-permute-done.refs_1_.refs_9_, ...), custom_call_target="tpu_custom_call" | custom-call | flops 1048576 | bytes 65536 | tf_op jit(solution)/shard_map/pallas_call | solution.py:550
  68.1 2.0 %collective-permute-done.17.late_b_1.refs_3_ = bf16[544,256]{1,0:T(8,128)(2,1)S(1)} collective-permute-done((bf16[544,256]{1,0:T(8,128)(2,1)S(1)}, bf16[544,256]{1,0:T(8,128)(2,1)S(1)}, u32[]{:S(2)}, u32[]{:S(2)}) %collective-permute-start.17) | collective-permute-done | bytes 278560 | tf_op jit(solution)/shard_map/ppermute | solution.py:19
  70.3 2.4 %collective-permute-done.19.outer = bf16[512,512]{1,0:T(8,128)(2,1)S(1)} collective-permute-done((bf16[512,512]{1,0:T(8,128)(2,1)S(1)}, bf16[512,512]{1,0:T(8,128)(2,1)S(1)}, u32[]{:S(2)}, u32[]{:S(2)}) %collective-permute-start.19) | collective-permute-done | bytes 524320 | tf_op jit(solution)/shard_map/ppermute | solution.py:580
  73.9 1.1 %shard_map.67 = (f32[528,512]{1,0:T(8,128)S(1)}, f32[512,128]{1,0:T(8,128)S(1)}, bf16[512,512]{1,0:T(8,128)(2,1)S(1)}, f32[8,512]{1,0:T(8,128)S(1)}) custom-call(bf16[512,512]{1,0:T(8,128)(2,1)S(1)} %shard_map.66.late.refs_6_, f32[8,512]{1,0:T(8,128)S(1)} %shard_map.65.stats.refs_4_, bf16[512,512]{1,0:T(8,128)(2,1)S(1)} %get-tuple-element.76.zero.refs_10_, ...), custom_call_target="tpu_custom_call" | custom-call | flops 536870912 | bytes 4571136 | tf_op jit(solution)/shard_map/pallas_call | solution.py:550
  75.0 1.4 %shard_map.68 = (bf16[512,512]{1,0:T(8,128)(2,1)S(1)}, bf16[512,512]{1,0:T(8,128)(2,1)S(1)}, f32[8,512]{1,0:T(8,128)S(1)}) custom-call(bf16[512,512]{1,0:T(8,128)(2,1)S(1)} %collective-permute-done.21.late.refs_7_, f32[8,512]{1,0:T(8,128)S(1)} %collective-permute-done.20.stats.refs_5_, bf16[512,512]{1,0:T(8,128)(2,1)S(1)} %get-tuple-element.77.zero.refs_11_, ...), custom_call_target="tpu_custom_call" | custom-call | flops 536870912 | bytes 5636096 | tf_op jit(solution)/shard_map/pallas_call | solution.py:550
  76.4 1.8 %collective-permute-start.24 = (bf16[512,512]{1,0:T(8,128)(2,1)S(1)}, bf16[512,512]{1,0:T(8,128)(2,1)S(1)}, u32[]{:S(2)}, u32[]{:S(2)}) collective-permute-start(bf16[512,512]{1,0:T(8,128)(2,1)S(1)} %get-tuple-element.95), channel_id=1, source_target_pairs={{0,2},{2,0},{1,3},{3,1},{4,6},{6,4},{5,7},{7,5},{8,10},{10,8},{9,1... | collective-permute-start | bytes 1572872 | tf_op jit(solution)/shard_map/ppermute | solution.py:19
  78.1 7.6 %shard_map.69 = (f32[512,512]{1,0:T(8,128)S(1)}, f32[512,512]{1,0:T(8,128)S(1)}, bf16[256,512]{1,0:T(8,128)(2,1)S(1)}, bf16[256,512]{1,0:T(8,128)(2,1)S(1)}, f32[256,1024]{1,0:T(8,128)}, /*index=5*/f32[8,128]{1,0:T(8,128)S(1)}) custom-call(s32[2]{0:T(128)S(1)} %pad_add_fusion.flags, bf16[512,256]{1,0:T(8,128)(2,1)S(1)} %get-tuple-element.58.refs_0_.late_b_0, ...), custom_call_target="tpu_custom_call" | custom-call | flops 2147483648 | bytes 14258184 | tf_op jit(solution)/shard_map/pallas_call | solution.py:550
  86.3 1.4 %collective-permute-done.25.other = f32[8,128]{1,0:T(8,128)S(1)} collective-permute-done((f32[8,128]{1,0:T(8,128)S(1)}, f32[8,128]{1,0:T(8,128)S(1)}, u32[]{:S(2)}, u32[]{:S(2)}) %collective-permute-start.25) | collective-permute-done | bytes 4128 | tf_op jit(solution)/shard_map/ppermute | solution.py:19
  88.0 0.9 shard_map.70
  88.9 1.5 %collective-permute-done.24.from_x = bf16[512,512]{1,0:T(8,128)(2,1)S(1)} collective-permute-done((bf16[512,512]{1,0:T(8,128)(2,1)S(1)}, bf16[512,512]{1,0:T(8,128)(2,1)S(1)}, u32[]{:S(2)}, u32[]{:S(2)}) %collective-permute-start.24) | collective-permute-done | bytes 524320 | tf_op jit(solution)/shard_map/ppermute | solution.py:19
  90.4 0.9 %shard_map.71 = bf16[512,512]{1,0:T(8,128)(2,1)} custom-call(f32[512,512]{1,0:T(8,128)S(1)} %get-tuple-element.94.right, bf16[512,512]{1,0:T(8,128)(2,1)S(1)} %collective-permute-done.24.from_x, bf16[512,256]{1,0:T(8,128)(2,1)S(1)} %get-tuple-element.58.refs_0_.late_b_0, bf16[544,256]{1,0:T(8,128)(2,1)S(1)} %shard_map.62.refs_1_.late_b_1), custom_call_target="tpu_custom_call" | custom-call | flops 1048576 | bytes 2637824 | tf_op jit(solution)/shard_map/pallas_call | solution.py:550
  (45 shorter events, 6.4 us)
Async XLA Ops:
  0.6 43.8 %copy-start = (bf16[512,512]{1,0:T(8,128)(2,1)S(1)}, bf16[512,512]{1,0:T(8,128)(2,1)}, u32[]{:S(2)}) copy-start(bf16[512,512]{1,0:T(8,128)(2,1)} %refs_13_.1) | copy-start | bytes 1572868
  0.6 9.9 %collective-permute-start = (bf16[512,512]{1,0:T(8,128)(2,1)}, bf16[512,512]{1,0:T(8,128)(2,1)S(1)}, u32[]{:S(2)}, u32[]{:S(2)}) collective-permute-start(bf16[512,512]{1,0:T(8,128)(2,1)} %refs_8_.1), channel_id=1, source_target_pairs={{0,1},{1,0},{2,3},{3,2},{4,5},{5,4},{6,7},{7,6},{8,9},{9,8},{10,11... | collective-permute-start | bytes 1572872 | tf_op jit(solution)/shard_map/ppermute | solution.py:19
  1.2 15.6 %collective-permute-start.4 = (bf16[512,512]{1,0:T(8,128)(2,1)}, bf16[512,512]{1,0:T(8,128)(2,1)S(1)}, u32[]{:S(2)}, u32[]{:S(2)}) collective-permute-start(bf16[512,512]{1,0:T(8,128)(2,1)} %refs_8_.1), channel_id=1, source_target_pairs={{0,4},{4,0},{8,12},{12,8},{1,5},{5,1},{9,13},{13,9},{2,6},{6,2},{1... | collective-permute-start | bytes 1572872 | tf_op jit(solution)/shard_map/ppermute | solution.py:580
  3.8 13.7 %collective-permute-start.7 = (bf16[512,512]{1,0:T(8,128)(2,1)}, bf16[512,512]{1,0:T(8,128)(2,1)S(1)}, u32[]{:S(2)}, u32[]{:S(2)}) collective-permute-start(bf16[512,512]{1,0:T(8,128)(2,1)} %refs_13_.1), channel_id=1, source_target_pairs={{4,8},{8,4},{5,9},{9,5},{6,10},{10,6},{7,11},{11,7},{20,24},{24,20... | collective-permute-start | bytes 1572872 | tf_op jit(solution)/shard_map/ppermute | solution.py:580
  4.5 14.4 %collective-permute-start.10 = (bf16[512,512]{1,0:T(8,128)(2,1)}, bf16[512,512]{1,0:T(8,128)(2,1)S(1)}, u32[]{:S(2)}, u32[]{:S(2)}) collective-permute-start(bf16[512,512]{1,0:T(8,128)(2,1)} %refs_13_.1), channel_id=1, source_target_pairs={{0,2},{2,0},{1,3},{3,1},{4,6},{6,4},{5,7},{7,5},{8,10},{10,8},{9,1... | collective-permute-start | bytes 1572872 | tf_op jit(solution)/shard_map/ppermute | solution.py:19
  6.1 22.0 %collective-permute-start.1 = (bf16[512,512]{1,0:T(8,128)(2,1)}, bf16[512,512]{1,0:T(8,128)(2,1)S(1)}, u32[]{:S(2)}, u32[]{:S(2)}) collective-permute-start(bf16[512,512]{1,0:T(8,128)(2,1)} %refs_13_.1), channel_id=1, source_target_pairs={{0,4},{4,0},{8,12},{12,8},{1,5},{5,1},{9,13},{13,9},{2,6},{6,2},{1... | collective-permute-start | bytes 1572872 | tf_op jit(solution)/shard_map/ppermute | solution.py:580
  16.8 13.8 %collective-permute-start.5 = (bf16[512,512]{1,0:T(8,128)(2,1)}, bf16[512,512]{1,0:T(8,128)(2,1)S(1)}, u32[]{:S(2)}, u32[]{:S(2)}) collective-permute-start(bf16[512,512]{1,0:T(8,128)(2,1)} %refs_8_.1), channel_id=1, source_target_pairs={{4,8},{8,4},{5,9},{9,5},{6,10},{10,6},{7,11},{11,7},{20,24},{24,20... | collective-permute-start | bytes 1572872 | tf_op jit(solution)/shard_map/ppermute | solution.py:580
  17.5 21.8 %collective-permute-start.8 = (bf16[512,512]{1,0:T(8,128)(2,1)S(1)}, bf16[512,512]{1,0:T(8,128)(2,1)S(1)}, u32[]{:S(2)}, u32[]{:S(2)}) collective-permute-start(bf16[512,512]{1,0:T(8,128)(2,1)S(1)} %collective-permute-done.7.inner), channel_id=1, source_target_pairs={{4,0},{8,12},{5,1},{9,13},{6,2},{10,14},{7,3},{11,15},{20,16},{24,... | collective-permute-start | bytes 1572872 | tf_op jit(solution)/shard_map/ppermute | solution.py:580
  18.8 21.3 %collective-permute-start.12 = (bf16[512,512]{1,0:T(8,128)(2,1)S(1)}, bf16[512,512]{1,0:T(8,128)(2,1)S(1)}, u32[]{:S(2)}, u32[]{:S(2)}) collective-permute-start(bf16[512,512]{1,0:T(8,128)(2,1)S(1)} %collective-permute-done.4.refs_2_), channel_id=1, source_target_pairs={{0,1},{1,0},{2,3},{3,2},{4,5},{5,4},{6,7},{7,6},{8,9},{9,8},{10,11... | collective-permute-start | bytes 1572872 | tf_op jit(solution)/shard_map/ppermute | solution.py:19
  28.0 13.4 %collective-permute-start.11 = (bf16[512,512]{1,0:T(8,128)(2,1)S(1)}, bf16[512,512]{1,0:T(8,128)(2,1)S(1)}, u32[]{:S(2)}, u32[]{:S(2)}) collective-permute-start(bf16[512,512]{1,0:T(8,128)(2,1)S(1)} %collective-permute-done.1.second.refs_8_), channel_id=1, source_target_pairs={{0,2},{2,0},{1,3},{3,1},{4,6},{6,4},{5,7},{7,5},{8,10},{10,8},{9,1... | collective-permute-start | bytes 1572872 | tf_op jit(solution)/shard_map/ppermute | solution.py:19
  29.9 13.0 %collective-permute-start.2 = (bf16[512,512]{1,0:T(8,128)(2,1)S(1)}, bf16[512,512]{1,0:T(8,128)(2,1)S(1)}, u32[]{:S(2)}, u32[]{:S(2)}) collective-permute-start(bf16[512,512]{1,0:T(8,128)(2,1)S(1)} %collective-permute-done.1.second.refs_8_), channel_id=1, source_target_pairs={{4,8},{8,4},{5,9},{9,5},{6,10},{10,6},{7,11},{11,7},{20,24},{24,20... | collective-permute-start | bytes 1572872 | tf_op jit(solution)/shard_map/ppermute | solution.py:580
  30.6 19.9 %collective-permute-start.6 = (bf16[512,512]{1,0:T(8,128)(2,1)S(1)}, bf16[512,512]{1,0:T(8,128)(2,1)S(1)}, u32[]{:S(2)}, u32[]{:S(2)}) collective-permute-start(bf16[512,512]{1,0:T(8,128)(2,1)S(1)} %collective-permute-done.5.inner), channel_id=1, source_target_pairs={{4,0},{8,12},{5,1},{9,13},{6,2},{10,14},{7,3},{11,15},{20,16},{24,... | collective-permute-start | bytes 1572872 | tf_op jit(solution)/shard_map/ppermute | solution.py:580
  39.3 12.7 %collective-permute-start.18 = (bf16[512,512]{1,0:T(8,128)(2,1)S(1)}, bf16[512,512]{1,0:T(8,128)(2,1)S(1)}, u32[]{:S(2)}, u32[]{:S(2)}) collective-permute-start(bf16[512,512]{1,0:T(8,128)(2,1)S(1)} %collective-permute-done.4.refs_2_), channel_id=1, source_target_pairs={{4,8},{8,4},{5,9},{9,5},{6,10},{10,6},{7,11},{11,7},{20,24},{24,20... | collective-permute-start | bytes 1572872 | tf_op jit(solution)/shard_map/ppermute | solution.py:580
  41.5 22.4 %collective-permute-start.13 = (bf16[512,512]{1,0:T(8,128)(2,1)S(1)}, bf16[512,512]{1,0:T(8,128)(2,1)S(1)}, u32[]{:S(2)}, u32[]{:S(2)}) collective-permute-start(bf16[512,512]{1,0:T(8,128)(2,1)S(1)} %shard_map.59.third.refs_10_), channel_id=1, source_target_pairs={{0,2},{2,0},{1,3},{3,1},{4,6},{6,4},{5,7},{7,5},{8,10},{10,8},{9,1... | collective-permute-start | bytes 1572872 | tf_op jit(solution)/shard_map/ppermute | solution.py:19
  43.0 21.0 %copy-start.1 = (bf16[512,512]{1,0:T(8,128)(2,1)S(1)}, bf16[512,512]{1,0:T(8,128)(2,1)}, u32[]{:S(2)}) copy-start(bf16[512,512]{1,0:T(8,128)(2,1)} %refs_8_.1) | copy-start | bytes 1572868
  43.0 13.0 %collective-permute-start.3 = (bf16[256,512]{1,0:T(8,128)(2,1)S(1)}, bf16[256,512]{1,0:T(8,128)(2,1)S(1)}, u32[]{:S(2)}, u32[]{:S(2)}) collective-permute-start(bf16[256,512]{1,0:T(8,128)(2,1)S(1)} %get-tuple-element.54.inner), channel_id=1, source_target_pairs={{4,0},{8,12},{5,1},{9,13},{6,2},{10,14},{7,3},{11,15},{20,16},{24,... | collective-permute-start | bytes 786440 | tf_op jit(solution)/shard_map/ppermute | solution.py:580
  50.6 13.3 %collective-permute-start.15 = (bf16[512,512]{1,0:T(8,128)(2,1)S(1)}, bf16[512,512]{1,0:T(8,128)(2,1)S(1)}, u32[]{:S(2)}, u32[]{:S(2)}) collective-permute-start(bf16[512,512]{1,0:T(8,128)(2,1)S(1)} %shard_map.58.refs_4_), channel_id=1, source_target_pairs={{0,1},{1,0},{2,3},{3,2},{4,5},{5,4},{6,7},{7,6},{8,9},{9,8},{10,11... | collective-permute-start | bytes 1572872 | tf_op jit(solution)/shard_map/ppermute | solution.py:19
  50.7 11.1 %collective-permute-start.9 = (bf16[256,512]{1,0:T(8,128)(2,1)S(1)}, bf16[256,512]{1,0:T(8,128)(2,1)S(1)}, u32[]{:S(2)}, u32[]{:S(2)}) collective-permute-start(bf16[256,512]{1,0:T(8,128)(2,1)S(1)} %get-tuple-element.59.inner), channel_id=1, source_target_pairs={{4,0},{8,12},{5,1},{9,13},{6,2},{10,14},{7,3},{11,15},{20,16},{24,... | collective-permute-start | bytes 786440 | tf_op jit(solution)/shard_map/ppermute | solution.py:580
  52.0 20.7 %collective-permute-start.19 = (bf16[512,512]{1,0:T(8,128)(2,1)S(1)}, bf16[512,512]{1,0:T(8,128)(2,1)S(1)}, u32[]{:S(2)}, u32[]{:S(2)}) collective-permute-start(bf16[512,512]{1,0:T(8,128)(2,1)S(1)} %collective-permute-done.18.inner), channel_id=1, source_target_pairs={{4,0},{8,12},{5,1},{9,13},{6,2},{10,14},{7,3},{11,15},{20,16},{24,... | collective-permute-start | bytes 1572872 | tf_op jit(solution)/shard_map/ppermute | solution.py:580
  56.2 7.8 %collective-permute-start.14 = (bf16[512,256]{1,0:T(8,128)(2,1)S(1)}, bf16[512,256]{1,0:T(8,128)(2,1)S(1)}, u32[]{:S(2)}, u32[]{:S(2)}) collective-permute-start(bf16[512,256]{1,0:T(8,128)(2,1)S(1)} %get-tuple-element.58.refs_0_.late_b_0), channel_id=1, source_target_pairs={{0,2},{2,0},{1,3},{3,1},{4,6},{6,4},{5,7},{7,5},{8,10},{10,8},{9,1... | collective-permute-start | bytes 786440 | tf_op jit(solution)/shard_map/ppermute | solution.py:19
  62.0 8.1 %collective-permute-start.17 = (bf16[544,256]{1,0:T(8,128)(2,1)S(1)}, bf16[544,256]{1,0:T(8,128)(2,1)S(1)}, u32[]{:S(2)}, u32[]{:S(2)}) collective-permute-start(bf16[544,256]{1,0:T(8,128)(2,1)S(1)} %shard_map.62.refs_1_.late_b_1), channel_id=1, source_target_pairs={{0,2},{2,0},{1,3},{3,1},{4,6},{6,4},{5,7},{7,5},{8,10},{10,8},{9,1... | collective-permute-start | bytes 835592 | tf_op jit(solution)/shard_map/ppermute | solution.py:19
  68.0 2.1 %collective-permute-start.16 = (f32[8,512]{1,0:T(8,128)S(1)}, f32[8,512]{1,0:T(8,128)S(1)}, u32[]{:S(2)}, u32[]{:S(2)}) collective-permute-start(f32[8,512]{1,0:T(8,128)S(1)} %get-tuple-element.71), channel_id=1, source_target_pairs={{0,1},{1,0},{2,3},{3,2},{4,5},{5,4},{6,7},{7,6},{8,9},{9,8},{10,11... | collective-permute-start | bytes 49160 | tf_op jit(solution)/shard_map/ppermute | solution.py:19
  72.9 2.1 %collective-permute-start.21 = (bf16[512,512]{1,0:T(8,128)(2,1)S(1)}, bf16[512,512]{1,0:T(8,128)(2,1)S(1)}, u32[]{:S(2)}, u32[]{:S(2)}) collective-permute-start(bf16[512,512]{1,0:T(8,128)(2,1)S(1)} %shard_map.66.late.refs_6_), channel_id=1, source_target_pairs={{0,1},{1,0},{2,3},{3,2},{4,5},{5,4},{6,7},{7,6},{8,9},{9,8},{10,11... | collective-permute-start | bytes 1572872 | tf_op jit(solution)/shard_map/ppermute | solution.py:19
  73.3 1.6 %collective-permute-start.20 = (f32[8,512]{1,0:T(8,128)S(1)}, f32[8,512]{1,0:T(8,128)S(1)}, u32[]{:S(2)}, u32[]{:S(2)}) collective-permute-start(f32[8,512]{1,0:T(8,128)S(1)} %shard_map.65.stats.refs_4_), channel_id=1, source_target_pairs={{0,1},{1,0},{2,3},{3,2},{4,5},{5,4},{6,7},{7,6},{8,9},{9,8},{10,11... | collective-permute-start | bytes 49160 | tf_op jit(solution)/shard_map/ppermute | solution.py:19
  76.4 14.0 %collective-permute-start.24 = (bf16[512,512]{1,0:T(8,128)(2,1)S(1)}, bf16[512,512]{1,0:T(8,128)(2,1)S(1)}, u32[]{:S(2)}, u32[]{:S(2)}) collective-permute-start(bf16[512,512]{1,0:T(8,128)(2,1)S(1)} %get-tuple-element.95), channel_id=1, source_target_pairs={{0,2},{2,0},{1,3},{3,1},{4,6},{6,4},{5,7},{7,5},{8,10},{10,8},{9,1... | collective-permute-start | bytes 1572872 | tf_op jit(solution)/shard_map/ppermute | solution.py:19
  85.8 2.3 %collective-permute-start.22 = (bf16[256,512]{1,0:T(8,128)(2,1)S(1)}, bf16[256,512]{1,0:T(8,128)(2,1)S(1)}, u32[]{:S(2)}, u32[]{:S(2)}) collective-permute-start(bf16[256,512]{1,0:T(8,128)(2,1)S(1)} %get-tuple-element.91), channel_id=1, source_target_pairs={{0,1},{1,0},{2,3},{3,2},{4,5},{5,4},{6,7},{7,6},{8,9},{9,8},{10,11... | collective-permute-start | bytes 786440 | tf_op jit(solution)/shard_map/ppermute | solution.py:19
  85.8 2.3 %collective-permute-start.23 = (bf16[256,512]{1,0:T(8,128)(2,1)S(1)}, bf16[256,512]{1,0:T(8,128)(2,1)S(1)}, u32[]{:S(2)}, u32[]{:S(2)}) collective-permute-start(bf16[256,512]{1,0:T(8,128)(2,1)S(1)} %get-tuple-element.92), channel_id=1, source_target_pairs={{0,1},{1,0},{2,3},{3,2},{4,5},{5,4},{6,7},{7,6},{8,9},{9,8},{10,11... | collective-permute-start | bytes 786440 | tf_op jit(solution)/shard_map/ppermute | solution.py:19
  86.3 1.4 %collective-permute-start.25 = (f32[8,128]{1,0:T(8,128)S(1)}, f32[8,128]{1,0:T(8,128)S(1)}, u32[]{:S(2)}, u32[]{:S(2)}) collective-permute-start(f32[8,128]{1,0:T(8,128)S(1)} %get-tuple-element.96.one), channel_id=1, source_target_pairs={{0,1},{1,0},{2,3},{3,2},{4,5},{5,4},{6,7},{7,6},{8,9},{9,8},{10,11... | collective-permute-start | bytes 12296 | tf_op jit(solution)/shard_map/ppermute | solution.py:19
  87.7 3.6 %collective-permute-start.26 = (f32[8,128]{1,0:T(8,128)S(1)}, f32[8,128]{1,0:T(8,128)S(1)}, u32[]{:S(2)}, u32[]{:S(2)}) collective-permute-start(f32[8,128]{1,0:T(8,128)S(1)} %shard_map.72.one), channel_id=1, source_target_pairs={{0,2},{2,0},{1,3},{3,1},{4,6},{6,4},{5,7},{7,5},{8,10},{10,8},{9,1... | collective-permute-start | bytes 12296 | tf_op jit(solution)/shard_map/ppermute | solution.py:19

commit v20 on v19

--- a/solution.py
+++ b/solution.py
@@ -350,15 +350,17 @@
     return columns[:, 0:1], columns[:, 1:2]
 
 
-def right_columns_kernel(images, late_b_0, late_b_1, columns, rows_b):
-    offset, rstd, gap, delta = right_stats((late_b_0, late_b_1))
+def right_columns_kernel(images, late_b_0, late_b_1, first_b, columns, xhat):
+    offset, rstd, _, delta = right_stats((late_b_0, late_b_1))
     columns[...] = jnp.transpose(rows_of([rstd / images, delta * rstd]))
-    rows_b[...] = rows_of([offset, rstd, gap, delta])
-
-
-def partner_kernel(images, part, late, stats, zero, sums, late_b_0, late_b_1, columns, rows_b, *refs):
+    for at in range(0, first_b.shape[0], 64):
+        piece = slice(at, at + 64)
+        xhat[piece, :] = (first_b[piece, :].astype(jnp.float32) - offset) * rstd
+
+
+def partner_kernel(images, part, late, stats, zero, sums, late_b_0, late_b_1, columns, *refs):
     if part:
-        (terms_in, across_in, vec_in, first_b) = refs[:4]
+        (terms_in, across_in, vec_in, xhat) = refs[:4]
         (partial_out, e_out, vec_out, left) = refs[4:]
     else:
         (terms_out, across_out, e_out, vec_out, left) = refs
@@ -382,7 +384,6 @@
     if part:
         vec_out[...] = rows_of([second_a, second_a + vec_in[0:1, :]])
         second = off_weight * lanes_to_row(across)
-        offset_b, rstd_b, _, _ = stats_rows(rows_b)
     else:
         vec_out[...] = rows_of([second_a])
         across_out[...] = across
@@ -390,9 +391,8 @@
         at = slice(tile * width, (tile + 1) * width)
         terms = dot_rows(left[...], e_out[at, :])
         if part:
-            xhat = (first_b[:, at].astype(jnp.float32) - offset_b[:, at]) * rstd_b[:, at]
             partial_out[:, at] = (
-                without_extra(terms + terms_in[:, at], rows) - xhat * second[:, at]
+                without_extra(terms + terms_in[:, at], rows) - xhat[:, at] * second[:, at]
             ).astype(jnp.bfloat16)
         else:
             terms_out[:, at] = terms
@@ -664,10 +664,10 @@
     )
     row_a, late_b_other_1 = after(core_swap(row_other), late_b_other_1)
     late_b_other = (late_b_other_0, late_b_other_1)
-    columns, rows_b = local_call(
+    columns, xhat_other = local_call(
         functools.partial(right_columns_kernel, batch_images),
-        late_b_other,
-        (jax.ShapeDtypeStruct((quart, 8), jnp.float32), row_out),
+        (*late_b_other, other_b0),
+        (jax.ShapeDtypeStruct((quart, 8), jnp.float32), quarter_f32),
     )
     row_a, columns = after(row_a, columns)
     operands = (mask, last_a, third_a, row_a)
@@ -680,7 +680,7 @@
 
     terms, across, e_left, vec_own = local_call(
         functools.partial(partner_kernel, batch_images, 0),
-        (late_a, stats_a, zero_own, partner_own, *late_b_other, columns, rows_b),
+        (late_a, stats_a, zero_own, partner_own, *late_b_other, columns),
         (
             jax.ShapeDtypeStruct((rows + 16, quart), jnp.float32),
             across_shape,
@@ -694,7 +694,7 @@
     partial_right, e_right, vec_other = local_call(
         functools.partial(partner_kernel, batch_images, 1),
         (late_a_other, stats_a_other, zero_other, partner_other, *late_b_other)
-        + (columns, rows_b, terms, across, vec_own, other_b0),
+        + (columns, terms, across, vec_own, xhat_other),
         (quarter_bf16, quarter_bf16, row_out),
         [low(rows + 16, quart)],
         2 * gemm,

time: 92.3 us -> 92.3 us (level)
  no operation moved by 1% of the time
where the time goes in v20:
time: 92.3 us; the launch traced here: 92 us
  waiting for transfers between devices  43.1 us (47%)
  starting transfers between devices  28.7 us (31%)
  Pallas kernels  19.1 us (21%)
  between operations  1.04 us (1%)
    ppermute x11, waiting for transfers between devices, along(): return lax.ppermute(block, 'dp', route)  36.8 us
    pallas_call x17, Pallas kernels, local_call(): pl.pallas_call(kernel, out_shape=list(outs), in_specs=[space(x) for x in...  19.1 us
    ppermute x11, starting transfers between devices, along(): return lax.ppermute(block, 'dp', route)  16.3 us
    ppermute x16, starting transfers between devices, swapped(): return lax.ppermute(block, axis, route)  12.3 us
    ppermute x16, waiting for transfers between devices, swapped(): return lax.ppermute(block, axis, route)  6.35 us
  transfers between devices with their start and end apart: 27, of which 12 were waited for; matrix products, arithmetic and copies ran while one was open for 0% of the time, Pallas kernels for 18%

profile of v20, /device:TPU:0, one launch (start us, length us, event | category | flops | bytes accessed | tf_op | source)
XLA Modules:
  0.0 92.0 jit_solution(10883442772634240438)
XLA Ops:
  1.2 2.7 %collective-permute-start.4 = (bf16[512,512]{1,0:T(8,128)(2,1)}, bf16[512,512]{1,0:T(8,128)(2,1)S(1)}, u32[]{:S(2)}, u32[]{:S(2)}) collective-permute-start(bf16[512,512]{1,0:T(8,128)(2,1)} %refs_8_.1), channel_id=1, source_target_pairs={{0,4},{4,0},{8,12},{12,8},{1,5},{5,1},{9,13},{13,9},{2,6},{6,2},{1... | collective-permute-start | bytes 1572872 | tf_op jit(solution)/shard_map/ppermute | solution.py:580
  4.5 1.6 %collective-permute-start.10 = (bf16[512,512]{1,0:T(8,128)(2,1)}, bf16[512,512]{1,0:T(8,128)(2,1)S(1)}, u32[]{:S(2)}, u32[]{:S(2)}) collective-permute-start(bf16[512,512]{1,0:T(8,128)(2,1)} %refs_13_.1), channel_id=1, source_target_pairs={{0,2},{2,0},{1,3},{3,1},{4,6},{6,4},{5,7},{7,5},{8,10},{10,8},{9,1... | collective-permute-start | bytes 1572872 | tf_op jit(solution)/shard_map/ppermute | solution.py:19
  6.1 4.4 %collective-permute-start.1 = (bf16[512,512]{1,0:T(8,128)(2,1)}, bf16[512,512]{1,0:T(8,128)(2,1)S(1)}, u32[]{:S(2)}, u32[]{:S(2)}) collective-permute-start(bf16[512,512]{1,0:T(8,128)(2,1)} %refs_13_.1), channel_id=1, source_target_pairs={{0,4},{4,0},{8,12},{12,8},{1,5},{5,1},{9,13},{13,9},{2,6},{6,2},{1... | collective-permute-start | bytes 1572872 | tf_op jit(solution)/shard_map/ppermute | solution.py:580
  10.5 6.3 %collective-permute-done.4.refs_2_ = bf16[512,512]{1,0:T(8,128)(2,1)S(1)} collective-permute-done((bf16[512,512]{1,0:T(8,128)(2,1)}, bf16[512,512]{1,0:T(8,128)(2,1)S(1)}, u32[]{:S(2)}, u32[]{:S(2)}) %collective-permute-start.4) | collective-permute-done | bytes 524320 | tf_op jit(solution)/shard_map/ppermute | solution.py:580
  17.5 1.3 %collective-permute-start.8 = (bf16[512,512]{1,0:T(8,128)(2,1)S(1)}, bf16[512,512]{1,0:T(8,128)(2,1)S(1)}, u32[]{:S(2)}, u32[]{:S(2)}) collective-permute-start(bf16[512,512]{1,0:T(8,128)(2,1)S(1)} %collective-permute-done.7.inner), channel_id=1, source_target_pairs={{4,0},{8,12},{5,1},{9,13},{6,2},{10,14},{7,3},{11,15},{20,16},{24,... | collective-permute-start | bytes 1572872 | tf_op jit(solution)/shard_map/ppermute | solution.py:580
  18.9 9.1 %collective-permute-done.1.second.refs_8_ = bf16[512,512]{1,0:T(8,128)(2,1)S(1)} collective-permute-done((bf16[512,512]{1,0:T(8,128)(2,1)}, bf16[512,512]{1,0:T(8,128)(2,1)S(1)}, u32[]{:S(2)}, u32[]{:S(2)}) %collective-permute-start.1) | collective-permute-done | bytes 524320 | tf_op jit(solution)/shard_map/ppermute | solution.py:580
  28.0 1.9 %collective-permute-start.11 = (bf16[512,512]{1,0:T(8,128)(2,1)S(1)}, bf16[512,512]{1,0:T(8,128)(2,1)S(1)}, u32[]{:S(2)}, u32[]{:S(2)}) collective-permute-start(bf16[512,512]{1,0:T(8,128)(2,1)S(1)} %collective-permute-done.1.second.refs_8_), channel_id=1, source_target_pairs={{0,2},{2,0},{1,3},{3,1},{4,6},{6,4},{5,7},{7,5},{8,10},{10,8},{9,1... | collective-permute-start | bytes 1572872 | tf_op jit(solution)/shard_map/ppermute | solution.py:19
  30.6 1.3 %collective-permute-start.6 = (bf16[512,512]{1,0:T(8,128)(2,1)S(1)}, bf16[512,512]{1,0:T(8,128)(2,1)S(1)}, u32[]{:S(2)}, u32[]{:S(2)}) collective-permute-start(bf16[512,512]{1,0:T(8,128)(2,1)S(1)} %collective-permute-done.5.inner), channel_id=1, source_target_pairs={{4,0},{8,12},{5,1},{9,13},{6,2},{10,14},{7,3},{11,15},{20,16},{24,... | collective-permute-start | bytes 1572872 | tf_op jit(solution)/shard_map/ppermute | solution.py:580
  31.9 7.4 %collective-permute-done.8.outer = bf16[512,512]{1,0:T(8,128)(2,1)S(1)} collective-permute-done((bf16[512,512]{1,0:T(8,128)(2,1)S(1)}, bf16[512,512]{1,0:T(8,128)(2,1)S(1)}, u32[]{:S(2)}, u32[]{:S(2)}) %collective-permute-start.8) | collective-permute-done | bytes 524320 | tf_op jit(solution)/shard_map/ppermute | solution.py:580
  39.3 0.7 collective-permute-start.18
  40.1 1.4 %collective-permute-done.11.refs_9_ = bf16[512,512]{1,0:T(8,128)(2,1)S(1)} collective-permute-done((bf16[512,512]{1,0:T(8,128)(2,1)S(1)}, bf16[512,512]{1,0:T(8,128)(2,1)S(1)}, u32[]{:S(2)}, u32[]{:S(2)}) %collective-permute-start.11) | collective-permute-done | bytes 524320 | tf_op jit(solution)/shard_map/ppermute | solution.py:19
  41.5 1.5 %collective-permute-start.13 = (bf16[512,512]{1,0:T(8,128)(2,1)S(1)}, bf16[512,512]{1,0:T(8,128)(2,1)S(1)}, u32[]{:S(2)}, u32[]{:S(2)}) collective-permute-start(bf16[512,512]{1,0:T(8,128)(2,1)S(1)} %shard_map.59.third.refs_10_), channel_id=1, source_target_pairs={{0,2},{2,0},{1,3},{3,1},{4,6},{6,4},{5,7},{7,5},{8,10},{10,8},{9,1... | collective-permute-start | bytes 1572872 | tf_op jit(solution)/shard_map/ppermute | solution.py:19
  43.0 1.4 %collective-permute-start.3 = (bf16[256,512]{1,0:T(8,128)(2,1)S(1)}, bf16[256,512]{1,0:T(8,128)(2,1)S(1)}, u32[]{:S(2)}, u32[]{:S(2)}) collective-permute-start(bf16[256,512]{1,0:T(8,128)(2,1)S(1)} %get-tuple-element.54.inner), channel_id=1, source_target_pairs={{4,0},{8,12},{5,1},{9,13},{6,2},{10,14},{7,3},{11,15},{20,16},{24,... | collective-permute-start | bytes 786440 | tf_op jit(solution)/shard_map/ppermute | solution.py:580
  44.4 1.0 %shard_map.60.row = f32[8,512]{1,0:T(8,128)S(1)} custom-call(bf16[512,512]{1,0:T(8,128)(2,1)S(1)} %copy-done, bf16[512,512]{1,0:T(8,128)(2,1)S(1)} %collective-permute-done.1.second.refs_8_, bf16[512,512]{1,0:T(8,128)(2,1)S(1)} %shard_map.59.third.refs_10_), custom_call_target="tpu_custom_call" | custom-call | flops 1048576 | bytes 1589248 | tf_op jit(solution)/shard_map/pallas_call | solution.py:550
  45.4 5.1 %collective-permute-done.6.outer = bf16[512,512]{1,0:T(8,128)(2,1)S(1)} collective-permute-done((bf16[512,512]{1,0:T(8,128)(2,1)S(1)}, bf16[512,512]{1,0:T(8,128)(2,1)S(1)}, u32[]{:S(2)}, u32[]{:S(2)}) %collective-permute-start.6) | collective-permute-done | bytes 524320 | tf_op jit(solution)/shard_map/ppermute | solution.py:580
  50.7 1.3 %collective-permute-start.9 = (bf16[256,512]{1,0:T(8,128)(2,1)S(1)}, bf16[256,512]{1,0:T(8,128)(2,1)S(1)}, u32[]{:S(2)}, u32[]{:S(2)}) collective-permute-start(bf16[256,512]{1,0:T(8,128)(2,1)S(1)} %get-tuple-element.59.inner), channel_id=1, source_target_pairs={{4,0},{8,12},{5,1},{9,13},{6,2},{10,14},{7,3},{11,15},{20,16},{24,... | collective-permute-start | bytes 786440 | tf_op jit(solution)/shard_map/ppermute | solution.py:580
  52.0 1.3 %collective-permute-start.19 = (bf16[512,512]{1,0:T(8,128)(2,1)S(1)}, bf16[512,512]{1,0:T(8,128)(2,1)S(1)}, u32[]{:S(2)}, u32[]{:S(2)}) collective-permute-start(bf16[512,512]{1,0:T(8,128)(2,1)S(1)} %collective-permute-done.18.inner), channel_id=1, source_target_pairs={{4,0},{8,12},{5,1},{9,13},{6,2},{10,14},{7,3},{11,15},{20,16},{24,... | collective-permute-start | bytes 1572872 | tf_op jit(solution)/shard_map/ppermute | solution.py:580
  53.3 2.7 %collective-permute-done.3.outer = bf16[256,512]{1,0:T(8,128)(2,1)S(1)} collective-permute-done((bf16[256,512]{1,0:T(8,128)(2,1)S(1)}, bf16[256,512]{1,0:T(8,128)(2,1)S(1)}, u32[]{:S(2)}, u32[]{:S(2)}) %collective-permute-start.3) | collective-permute-done | bytes 262176 | tf_op jit(solution)/shard_map/ppermute | solution.py:580
  56.2 1.6 %collective-permute-start.14 = (bf16[512,256]{1,0:T(8,128)(2,1)S(1)}, bf16[512,256]{1,0:T(8,128)(2,1)S(1)}, u32[]{:S(2)}, u32[]{:S(2)}) collective-permute-start(bf16[512,256]{1,0:T(8,128)(2,1)S(1)} %get-tuple-element.58.refs_0_.late_b_0), channel_id=1, source_target_pairs={{0,2},{2,0},{1,3},{3,1},{4,6},{6,4},{5,7},{7,5},{8,10},{10,8},{9,1... | collective-permute-start | bytes 786440 | tf_op jit(solution)/shard_map/ppermute | solution.py:19
  57.8 4.0 %collective-permute-done.9.outer = bf16[256,512]{1,0:T(8,128)(2,1)S(1)} collective-permute-done((bf16[256,512]{1,0:T(8,128)(2,1)S(1)}, bf16[256,512]{1,0:T(8,128)(2,1)S(1)}, u32[]{:S(2)}, u32[]{:S(2)}) %collective-permute-start.9) | collective-permute-done | bytes 262176 | tf_op jit(solution)/shard_map/ppermute | solution.py:580
  62.0 1.9 %collective-permute-start.17 = (bf16[544,256]{1,0:T(8,128)(2,1)S(1)}, bf16[544,256]{1,0:T(8,128)(2,1)S(1)}, u32[]{:S(2)}, u32[]{:S(2)}) collective-permute-start(bf16[544,256]{1,0:T(8,128)(2,1)S(1)} %shard_map.62.refs_1_.late_b_1), channel_id=1, source_target_pairs={{0,2},{2,0},{1,3},{3,1},{4,6},{6,4},{5,7},{7,5},{8,10},{10,8},{9,1... | collective-permute-start | bytes 835592 | tf_op jit(solution)/shard_map/ppermute | solution.py:19
  64.0 4.1 %shard_map.63 = (f32[512,512]{1,0:T(8,128)S(1)}, f32[512,512]{1,0:T(8,128)S(1)}, f32[512,1024]{1,0:T(8,128)S(1)}, f32[8,512]{1,0:T(8,128)S(1)}, bf16[512,512]{1,...) custom-call(bf16[512,512]{1,0:T(8,128)(2,1)S(1)} %copy-done.1, bf16[512,512]{1,0:T(8,128)(2,1)S(1)} %collective-permute-done.refs_1_.refs_9_, ...), custom_call_target="tpu_custom_call" | custom-call | flops 1048576 | bytes 65536 | tf_op jit(solution)/shard_map/pallas_call | solution.py:550
  68.1 2.0 %collective-permute-done.17.late_b_1.refs_3_ = bf16[544,256]{1,0:T(8,128)(2,1)S(1)} collective-permute-done((bf16[544,256]{1,0:T(8,128)(2,1)S(1)}, bf16[544,256]{1,0:T(8,128)(2,1)S(1)}, u32[]{:S(2)}, u32[]{:S(2)}) %collective-permute-start.17) | collective-permute-done | bytes 278560 | tf_op jit(solution)/shard_map/ppermute | solution.py:19
  70.4 2.3 %collective-permute-done.19.outer = bf16[512,512]{1,0:T(8,128)(2,1)S(1)} collective-permute-done((bf16[512,512]{1,0:T(8,128)(2,1)S(1)}, bf16[512,512]{1,0:T(8,128)(2,1)S(1)}, u32[]{:S(2)}, u32[]{:S(2)}) %collective-permute-start.19) | collective-permute-done | bytes 524320 | tf_op jit(solution)/shard_map/ppermute | solution.py:580
  73.9 1.1 %shard_map.67 = (f32[528,512]{1,0:T(8,128)S(1)}, f32[512,128]{1,0:T(8,128)S(1)}, bf16[512,512]{1,0:T(8,128)(2,1)S(1)}, f32[8,512]{1,0:T(8,128)S(1)}) custom-call(bf16[512,512]{1,0:T(8,128)(2,1)S(1)} %shard_map.66.late.refs_6_, f32[8,512]{1,0:T(8,128)S(1)} %shard_map.65.stats.refs_4_, bf16[512,512]{1,0:T(8,128)(2,1)S(1)} %get-tuple-element.76.zero.refs_10_, ...), custom_call_target="tpu_custom_call" | custom-call | flops 536870912 | bytes 4554752 | tf_op jit(solution)/shard_map/pallas_call | solution.py:550
  75.0 1.4 %shard_map.68 = (bf16[512,512]{1,0:T(8,128)(2,1)S(1)}, bf16[512,512]{1,0:T(8,128)(2,1)S(1)}, f32[8,512]{1,0:T(8,128)S(1)}) custom-call(bf16[512,512]{1,0:T(8,128)(2,1)S(1)} %collective-permute-done.21.late.refs_7_, f32[8,512]{1,0:T(8,128)S(1)} %collective-permute-done.20.stats.refs_5_, bf16[512,512]{1,0:T(8,128)(2,1)S(1)} %get-tuple-element.77.zero.refs_11_, ...), custom_call_target="tpu_custom_call" | custom-call | flops 536870912 | bytes 6144000 | tf_op jit(solution)/shard_map/pallas_call | solution.py:550
  76.4 1.8 %collective-permute-start.24 = (bf16[512,512]{1,0:T(8,128)(2,1)S(1)}, bf16[512,512]{1,0:T(8,128)(2,1)S(1)}, u32[]{:S(2)}, u32[]{:S(2)}) collective-permute-start(bf16[512,512]{1,0:T(8,128)(2,1)S(1)} %get-tuple-element.95), channel_id=1, source_target_pairs={{0,2},{2,0},{1,3},{3,1},{4,6},{6,4},{5,7},{7,5},{8,10},{10,8},{9,1... | collective-permute-start | bytes 1572872 | tf_op jit(solution)/shard_map/ppermute | solution.py:19
  78.1 7.6 %shard_map.69 = (f32[512,512]{1,0:T(8,128)S(1)}, f32[512,512]{1,0:T(8,128)S(1)}, bf16[256,512]{1,0:T(8,128)(2,1)S(1)}, bf16[256,512]{1,0:T(8,128)(2,1)S(1)}, f32[256,1024]{1,0:T(8,128)}, /*index=5*/f32[8,128]{1,0:T(8,128)S(1)}) custom-call(s32[2]{0:T(128)S(1)} %pad_add_fusion.flags, bf16[512,256]{1,0:T(8,128)(2,1)S(1)} %get-tuple-element.58.refs_0_.late_b_0, ...), custom_call_target="tpu_custom_call" | custom-call | flops 2147483648 | bytes 14258184 | tf_op jit(solution)/shard_map/pallas_call | solution.py:550
  86.3 1.4 %collective-permute-done.25.other = f32[8,128]{1,0:T(8,128)S(1)} collective-permute-done((f32[8,128]{1,0:T(8,128)S(1)}, f32[8,128]{1,0:T(8,128)S(1)}, u32[]{:S(2)}, u32[]{:S(2)}) %collective-permute-start.25) | collective-permute-done | bytes 4128 | tf_op jit(solution)/shard_map/ppermute | solution.py:19
  88.0 0.9 shard_map.70
  88.9 1.5 %collective-permute-done.24.from_x = bf16[512,512]{1,0:T(8,128)(2,1)S(1)} collective-permute-done((bf16[512,512]{1,0:T(8,128)(2,1)S(1)}, bf16[512,512]{1,0:T(8,128)(2,1)S(1)}, u32[]{:S(2)}, u32[]{:S(2)}) %collective-permute-start.24) | collective-permute-done | bytes 524320 | tf_op jit(solution)/shard_map/ppermute | solution.py:19
  90.4 0.9 %shard_map.71 = bf16[512,512]{1,0:T(8,128)(2,1)} custom-call(f32[512,512]{1,0:T(8,128)S(1)} %get-tuple-element.94.right, bf16[512,512]{1,0:T(8,128)(2,1)S(1)} %collective-permute-done.24.from_x, bf16[512,256]{1,0:T(8,128)(2,1)S(1)} %get-tuple-element.58.refs_0_.late_b_0, bf16[544,256]{1,0:T(8,128)(2,1)S(1)} %shard_map.62.refs_1_.late_b_1), custom_call_target="tpu_custom_call" | custom-call | flops 1048576 | bytes 2637824 | tf_op jit(solution)/shard_map/pallas_call | solution.py:550
  (45 shorter events, 6.5 us)
Async XLA Ops:
  0.6 43.8 %copy-start = (bf16[512,512]{1,0:T(8,128)(2,1)S(1)}, bf16[512,512]{1,0:T(8,128)(2,1)}, u32[]{:S(2)}) copy-start(bf16[512,512]{1,0:T(8,128)(2,1)} %refs_13_.1) | copy-start | bytes 1572868
  0.6 9.9 %collective-permute-start = (bf16[512,512]{1,0:T(8,128)(2,1)}, bf16[512,512]{1,0:T(8,128)(2,1)S(1)}, u32[]{:S(2)}, u32[]{:S(2)}) collective-permute-start(bf16[512,512]{1,0:T(8,128)(2,1)} %refs_8_.1), channel_id=1, source_target_pairs={{0,1},{1,0},{2,3},{3,2},{4,5},{5,4},{6,7},{7,6},{8,9},{9,8},{10,11... | collective-permute-start | bytes 1572872 | tf_op jit(solution)/shard_map/ppermute | solution.py:19
  1.2 15.6 %collective-permute-start.4 = (bf16[512,512]{1,0:T(8,128)(2,1)}, bf16[512,512]{1,0:T(8,128)(2,1)S(1)}, u32[]{:S(2)}, u32[]{:S(2)}) collective-permute-start(bf16[512,512]{1,0:T(8,128)(2,1)} %refs_8_.1), channel_id=1, source_target_pairs={{0,4},{4,0},{8,12},{12,8},{1,5},{5,1},{9,13},{13,9},{2,6},{6,2},{1... | collective-permute-start | bytes 1572872 | tf_op jit(solution)/shard_map/ppermute | solution.py:580
  3.8 13.7 %collective-permute-start.7 = (bf16[512,512]{1,0:T(8,128)(2,1)}, bf16[512,512]{1,0:T(8,128)(2,1)S(1)}, u32[]{:S(2)}, u32[]{:S(2)}) collective-permute-start(bf16[512,512]{1,0:T(8,128)(2,1)} %refs_13_.1), channel_id=1, source_target_pairs={{4,8},{8,4},{5,9},{9,5},{6,10},{10,6},{7,11},{11,7},{20,24},{24,20... | collective-permute-start | bytes 1572872 | tf_op jit(solution)/shard_map/ppermute | solution.py:580
  4.5 14.4 %collective-permute-start.10 = (bf16[512,512]{1,0:T(8,128)(2,1)}, bf16[512,512]{1,0:T(8,128)(2,1)S(1)}, u32[]{:S(2)}, u32[]{:S(2)}) collective-permute-start(bf16[512,512]{1,0:T(8,128)(2,1)} %refs_13_.1), channel_id=1, source_target_pairs={{0,2},{2,0},{1,3},{3,1},{4,6},{6,4},{5,7},{7,5},{8,10},{10,8},{9,1... | collective-permute-start | bytes 1572872 | tf_op jit(solution)/shard_map/ppermute | solution.py:19
  6.1 22.0 %collective-permute-start.1 = (bf16[512,512]{1,0:T(8,128)(2,1)}, bf16[512,512]{1,0:T(8,128)(2,1)S(1)}, u32[]{:S(2)}, u32[]{:S(2)}) collective-permute-start(bf16[512,512]{1,0:T(8,128)(2,1)} %refs_13_.1), channel_id=1, source_target_pairs={{0,4},{4,0},{8,12},{12,8},{1,5},{5,1},{9,13},{13,9},{2,6},{6,2},{1... | collective-permute-start | bytes 1572872 | tf_op jit(solution)/shard_map/ppermute | solution.py:580
  16.8 13.8 %collective-permute-start.5 = (bf16[512,512]{1,0:T(8,128)(2,1)}, bf16[512,512]{1,0:T(8,128)(2,1)S(1)}, u32[]{:S(2)}, u32[]{:S(2)}) collective-permute-start(bf16[512,512]{1,0:T(8,128)(2,1)} %refs_8_.1), channel_id=1, source_target_pairs={{4,8},{8,4},{5,9},{9,5},{6,10},{10,6},{7,11},{11,7},{20,24},{24,20... | collective-permute-start | bytes 1572872 | tf_op jit(solution)/shard_map/ppermute | solution.py:580
  17.5 21.8 %collective-permute-start.8 = (bf16[512,512]{1,0:T(8,128)(2,1)S(1)}, bf16[512,512]{1,0:T(8,128)(2,1)S(1)}, u32[]{:S(2)}, u32[]{:S(2)}) collective-permute-start(bf16[512,512]{1,0:T(8,128)(2,1)S(1)} %collective-permute-done.7.inner), channel_id=1, source_target_pairs={{4,0},{8,12},{5,1},{9,13},{6,2},{10,14},{7,3},{11,15},{20,16},{24,... | collective-permute-start | bytes 1572872 | tf_op jit(solution)/shard_map/ppermute | solution.py:580
  18.8 21.3 %collective-permute-start.12 = (bf16[512,512]{1,0:T(8,128)(2,1)S(1)}, bf16[512,512]{1,0:T(8,128)(2,1)S(1)}, u32[]{:S(2)}, u32[]{:S(2)}) collective-permute-start(bf16[512,512]{1,0:T(8,128)(2,1)S(1)} %collective-permute-done.4.refs_2_), channel_id=1, source_target_pairs={{0,1},{1,0},{2,3},{3,2},{4,5},{5,4},{6,7},{7,6},{8,9},{9,8},{10,11... | collective-permute-start | bytes 1572872 | tf_op jit(solution)/shard_map/ppermute | solution.py:19
  28.0 13.4 %collective-permute-start.11 = (bf16[512,512]{1,0:T(8,128)(2,1)S(1)}, bf16[512,512]{1,0:T(8,128)(2,1)S(1)}, u32[]{:S(2)}, u32[]{:S(2)}) collective-permute-start(bf16[512,512]{1,0:T(8,128)(2,1)S(1)} %collective-permute-done.1.second.refs_8_), channel_id=1, source_target_pairs={{0,2},{2,0},{1,3},{3,1},{4,6},{6,4},{5,7},{7,5},{8,10},{10,8},{9,1... | collective-permute-start | bytes 1572872 | tf_op jit(solution)/shard_map/ppermute | solution.py:19
  29.9 13.0 %collective-permute-start.2 = (bf16[512,512]{1,0:T(8,128)(2,1)S(1)}, bf16[512,512]{1,0:T(8,128)(2,1)S(1)}, u32[]{:S(2)}, u32[]{:S(2)}) collective-permute-start(bf16[512,512]{1,0:T(8,128)(2,1)S(1)} %collective-permute-done.1.second.refs_8_), channel_id=1, source_target_pairs={{4,8},{8,4},{5,9},{9,5},{6,10},{10,6},{7,11},{11,7},{20,24},{24,20... | collective-permute-start | bytes 1572872 | tf_op jit(solution)/shard_map/ppermute | solution.py:580
  30.6 19.9 %collective-permute-start.6 = (bf16[512,512]{1,0:T(8,128)(2,1)S(1)}, bf16[512,512]{1,0:T(8,128)(2,1)S(1)}, u32[]{:S(2)}, u32[]{:S(2)}) collective-permute-start(bf16[512,512]{1,0:T(8,128)(2,1)S(1)} %collective-permute-done.5.inner), channel_id=1, source_target_pairs={{4,0},{8,12},{5,1},{9,13},{6,2},{10,14},{7,3},{11,15},{20,16},{24,... | collective-permute-start | bytes 1572872 | tf_op jit(solution)/shard_map/ppermute | solution.py:580
  39.3 12.7 %collective-permute-start.18 = (bf16[512,512]{1,0:T(8,128)(2,1)S(1)}, bf16[512,512]{1,0:T(8,128)(2,1)S(1)}, u32[]{:S(2)}, u32[]{:S(2)}) collective-permute-start(bf16[512,512]{1,0:T(8,128)(2,1)S(1)} %collective-permute-done.4.refs_2_), channel_id=1, source_target_pairs={{4,8},{8,4},{5,9},{9,5},{6,10},{10,6},{7,11},{11,7},{20,24},{24,20... | collective-permute-start | bytes 1572872 | tf_op jit(solution)/shard_map/ppermute | solution.py:580
  41.5 22.4 %collective-permute-start.13 = (bf16[512,512]{1,0:T(8,128)(2,1)S(1)}, bf16[512,512]{1,0:T(8,128)(2,1)S(1)}, u32[]{:S(2)}, u32[]{:S(2)}) collective-permute-start(bf16[512,512]{1,0:T(8,128)(2,1)S(1)} %shard_map.59.third.refs_10_), channel_id=1, source_target_pairs={{0,2},{2,0},{1,3},{3,1},{4,6},{6,4},{5,7},{7,5},{8,10},{10,8},{9,1... | collective-permute-start | bytes 1572872 | tf_op jit(solution)/shard_map/ppermute | solution.py:19
  43.0 21.0 %copy-start.1 = (bf16[512,512]{1,0:T(8,128)(2,1)S(1)}, bf16[512,512]{1,0:T(8,128)(2,1)}, u32[]{:S(2)}) copy-start(bf16[512,512]{1,0:T(8,128)(2,1)} %refs_8_.1) | copy-start | bytes 1572868
  43.0 13.0 %collective-permute-start.3 = (bf16[256,512]{1,0:T(8,128)(2,1)S(1)}, bf16[256,512]{1,0:T(8,128)(2,1)S(1)}, u32[]{:S(2)}, u32[]{:S(2)}) collective-permute-start(bf16[256,512]{1,0:T(8,128)(2,1)S(1)} %get-tuple-element.54.inner), channel_id=1, source_target_pairs={{4,0},{8,12},{5,1},{9,13},{6,2},{10,14},{7,3},{11,15},{20,16},{24,... | collective-permute-start | bytes 786440 | tf_op jit(solution)/shard_map/ppermute | solution.py:580
  50.6 13.3 %collective-permute-start.15 = (bf16[512,512]{1,0:T(8,128)(2,1)S(1)}, bf16[512,512]{1,0:T(8,128)(2,1)S(1)}, u32[]{:S(2)}, u32[]{:S(2)}) collective-permute-start(bf16[512,512]{1,0:T(8,128)(2,1)S(1)} %shard_map.58.refs_4_), channel_id=1, source_target_pairs={{0,1},{1,0},{2,3},{3,2},{4,5},{5,4},{6,7},{7,6},{8,9},{9,8},{10,11... | collective-permute-start | bytes 1572872 | tf_op jit(solution)/shard_map/ppermute | solution.py:19
  50.7 11.1 %collective-permute-start.9 = (bf16[256,512]{1,0:T(8,128)(2,1)S(1)}, bf16[256,512]{1,0:T(8,128)(2,1)S(1)}, u32[]{:S(2)}, u32[]{:S(2)}) collective-permute-start(bf16[256,512]{1,0:T(8,128)(2,1)S(1)} %get-tuple-element.59.inner), channel_id=1, source_target_pairs={{4,0},{8,12},{5,1},{9,13},{6,2},{10,14},{7,3},{11,15},{20,16},{24,... | collective-permute-start | bytes 786440 | tf_op jit(solution)/shard_map/ppermute | solution.py:580
  52.0 20.7 %collective-permute-start.19 = (bf16[512,512]{1,0:T(8,128)(2,1)S(1)}, bf16[512,512]{1,0:T(8,128)(2,1)S(1)}, u32[]{:S(2)}, u32[]{:S(2)}) collective-permute-start(bf16[512,512]{1,0:T(8,128)(2,1)S(1)} %collective-permute-done.18.inner), channel_id=1, source_target_pairs={{4,0},{8,12},{5,1},{9,13},{6,2},{10,14},{7,3},{11,15},{20,16},{24,... | collective-permute-start | bytes 1572872 | tf_op jit(solution)/shard_map/ppermute | solution.py:580
  56.2 7.8 %collective-permute-start.14 = (bf16[512,256]{1,0:T(8,128)(2,1)S(1)}, bf16[512,256]{1,0:T(8,128)(2,1)S(1)}, u32[]{:S(2)}, u32[]{:S(2)}) collective-permute-start(bf16[512,256]{1,0:T(8,128)(2,1)S(1)} %get-tuple-element.58.refs_0_.late_b_0), channel_id=1, source_target_pairs={{0,2},{2,0},{1,3},{3,1},{4,6},{6,4},{5,7},{7,5},{8,10},{10,8},{9,1... | collective-permute-start | bytes 786440 | tf_op jit(solution)/shard_map/ppermute | solution.py:19
  62.0 8.1 %collective-permute-start.17 = (bf16[544,256]{1,0:T(8,128)(2,1)S(1)}, bf16[544,256]{1,0:T(8,128)(2,1)S(1)}, u32[]{:S(2)}, u32[]{:S(2)}) collective-permute-start(bf16[544,256]{1,0:T(8,128)(2,1)S(1)} %shard_map.62.refs_1_.late_b_1), channel_id=1, source_target_pairs={{0,2},{2,0},{1,3},{3,1},{4,6},{6,4},{5,7},{7,5},{8,10},{10,8},{9,1... | collective-permute-start | bytes 835592 | tf_op jit(solution)/shard_map/ppermute | solution.py:19
  68.0 2.1 %collective-permute-start.16 = (f32[8,512]{1,0:T(8,128)S(1)}, f32[8,512]{1,0:T(8,128)S(1)}, u32[]{:S(2)}, u32[]{:S(2)}) collective-permute-start(f32[8,512]{1,0:T(8,128)S(1)} %get-tuple-element.71), channel_id=1, source_target_pairs={{0,1},{1,0},{2,3},{3,2},{4,5},{5,4},{6,7},{7,6},{8,9},{9,8},{10,11... | collective-permute-start | bytes 49160 | tf_op jit(solution)/shard_map/ppermute | solution.py:19
  72.9 2.1 %collective-permute-start.21 = (bf16[512,512]{1,0:T(8,128)(2,1)S(1)}, bf16[512,512]{1,0:T(8,128)(2,1)S(1)}, u32[]{:S(2)}, u32[]{:S(2)}) collective-permute-start(bf16[512,512]{1,0:T(8,128)(2,1)S(1)} %shard_map.66.late.refs_6_), channel_id=1, source_target_pairs={{0,1},{1,0},{2,3},{3,2},{4,5},{5,4},{6,7},{7,6},{8,9},{9,8},{10,11... | collective-permute-start | bytes 1572872 | tf_op jit(solution)/shard_map/ppermute | solution.py:19
  73.3 1.6 %collective-permute-start.20 = (f32[8,512]{1,0:T(8,128)S(1)}, f32[8,512]{1,0:T(8,128)S(1)}, u32[]{:S(2)}, u32[]{:S(2)}) collective-permute-start(f32[8,512]{1,0:T(8,128)S(1)} %shard_map.65.stats.refs_4_), channel_id=1, source_target_pairs={{0,1},{1,0},{2,3},{3,2},{4,5},{5,4},{6,7},{7,6},{8,9},{9,8},{10,11... | collective-permute-start | bytes 49160 | tf_op jit(solution)/shard_map/ppermute | solution.py:19
  76.4 14.0 %collective-permute-start.24 = (bf16[512,512]{1,0:T(8,128)(2,1)S(1)}, bf16[512,512]{1,0:T(8,128)(2,1)S(1)}, u32[]{:S(2)}, u32[]{:S(2)}) collective-permute-start(bf16[512,512]{1,0:T(8,128)(2,1)S(1)} %get-tuple-element.95), channel_id=1, source_target_pairs={{0,2},{2,0},{1,3},{3,1},{4,6},{6,4},{5,7},{7,5},{8,10},{10,8},{9,1... | collective-permute-start | bytes 1572872 | tf_op jit(solution)/shard_map/ppermute | solution.py:19
  85.8 2.3 %collective-permute-start.22 = (bf16[256,512]{1,0:T(8,128)(2,1)S(1)}, bf16[256,512]{1,0:T(8,128)(2,1)S(1)}, u32[]{:S(2)}, u32[]{:S(2)}) collective-permute-start(bf16[256,512]{1,0:T(8,128)(2,1)S(1)} %get-tuple-element.91), channel_id=1, source_target_pairs={{0,1},{1,0},{2,3},{3,2},{4,5},{5,4},{6,7},{7,6},{8,9},{9,8},{10,11... | collective-permute-start | bytes 786440 | tf_op jit(solution)/shard_map/ppermute | solution.py:19
  85.8 2.3 %collective-permute-start.23 = (bf16[256,512]{1,0:T(8,128)(2,1)S(1)}, bf16[256,512]{1,0:T(8,128)(2,1)S(1)}, u32[]{:S(2)}, u32[]{:S(2)}) collective-permute-start(bf16[256,512]{1,0:T(8,128)(2,1)S(1)} %get-tuple-element.92), channel_id=1, source_target_pairs={{0,1},{1,0},{2,3},{3,2},{4,5},{5,4},{6,7},{7,6},{8,9},{9,8},{10,11... | collective-permute-start | bytes 786440 | tf_op jit(solution)/shard_map/ppermute | solution.py:19
  86.3 1.4 %collective-permute-start.25 = (f32[8,128]{1,0:T(8,128)S(1)}, f32[8,128]{1,0:T(8,128)S(1)}, u32[]{:S(2)}, u32[]{:S(2)}) collective-permute-start(f32[8,128]{1,0:T(8,128)S(1)} %get-tuple-element.96.one), channel_id=1, source_target_pairs={{0,1},{1,0},{2,3},{3,2},{4,5},{5,4},{6,7},{7,6},{8,9},{9,8},{10,11... | collective-permute-start | bytes 12296 | tf_op jit(solution)/shard_map/ppermute | solution.py:19
  87.7 3.7 %collective-permute-start.26 = (f32[8,128]{1,0:T(8,128)S(1)}, f32[8,128]{1,0:T(8,128)S(1)}, u32[]{:S(2)}, u32[]{:S(2)}) collective-permute-start(f32[8,128]{1,0:T(8,128)S(1)} %shard_map.72.one), channel_id=1, source_target_pairs={{0,2},{2,0},{1,3},{3,1},{4,6},{6,4},{5,7},{7,5},{8,10},{10,8},{9,1... | collective-permute-start | bytes 12296 | tf_op jit(solution)/shard_map/ppermute | solution.py:19

commit v21 on v20

--- a/solution.py
+++ b/solution.py
@@ -493,9 +493,8 @@
         xhat = (first_b[:, at].astype(jnp.float32) - own_b[0][:, at]) * own_b[1][:, at]
         norm_a = (first_own[:, at].astype(jnp.float32) - offset[:, at]) * rstd[:, at]
         norm_a = norm_a.astype(jnp.bfloat16).astype(jnp.float32)
-        right_out[:, at] = (
-            without_extra(terms, rows) - xhat * second_b[:, at] + norm_a * diagonal_row[:, at]
-        )
+        value = without_extra(terms, rows) - xhat * second_b[:, at] + norm_a * diagonal_row[:, at]
+        right_out[:, at] = own_b[1][:, at] * value
 
     own_columns = jnp.transpose(mine_own[...])
     partner_columns = jnp.transpose(mine_partner[...])
@@ -532,7 +531,7 @@
     rstd = right_stats((late_b_0, late_b_1))[1]
     for at in range(0, right.shape[0], 64):
         piece = slice(at, at + 64)
-        value = rstd * (right[piece, :] + from_x[piece, :].astype(jnp.float32))
+        value = right[piece, :] + rstd * from_x[piece, :].astype(jnp.float32)
         right_out[piece, :] = value.astype(jnp.bfloat16)
 
 

time: 92.3 us -> 92.3 us (level)
  no operation moved by 1% of the time
where the time goes in v21:
time: 92.3 us; the launch traced here: 92 us
  waiting for transfers between devices  43.1 us (47%)
  starting transfers between devices  28.7 us (31%)
  Pallas kernels  19.1 us (21%)
  between operations  1.04 us (1%)
    ppermute x11, waiting for transfers between devices, along(): return lax.ppermute(block, 'dp', route)  36.8 us
    pallas_call x17, Pallas kernels, local_call(): pl.pallas_call(kernel, out_shape=list(outs), in_specs=[space(x) for x in...  19.1 us
    ppermute x11, starting transfers between devices, along(): return lax.ppermute(block, 'dp', route)  16.3 us
    ppermute x16, starting transfers between devices, swapped(): return lax.ppermute(block, axis, route)  12.3 us
    ppermute x16, waiting for transfers between devices, swapped(): return lax.ppermute(block, axis, route)  6.33 us
  transfers between devices with their start and end apart: 27, of which 12 were waited for; matrix products, arithmetic and copies ran while one was open for 0% of the time, Pallas kernels for 18%

profile of v21, /device:TPU:0, one launch (start us, length us, event | category | flops | bytes accessed | tf_op | source)
XLA Modules:
  0.0 92.0 jit_solution(9724318257019984142)
XLA Ops:
  1.2 2.7 %collective-permute-start.4 = (bf16[512,512]{1,0:T(8,128)(2,1)}, bf16[512,512]{1,0:T(8,128)(2,1)S(1)}, u32[]{:S(2)}, u32[]{:S(2)}) collective-permute-start(bf16[512,512]{1,0:T(8,128)(2,1)} %refs_8_.1), channel_id=1, source_target_pairs={{0,4},{4,0},{8,12},{12,8},{1,5},{5,1},{9,13},{13,9},{2,6},{6,2},{1... | collective-permute-start | bytes 1572872 | tf_op jit(solution)/shard_map/ppermute | solution.py:579
  4.5 1.6 %collective-permute-start.10 = (bf16[512,512]{1,0:T(8,128)(2,1)}, bf16[512,512]{1,0:T(8,128)(2,1)S(1)}, u32[]{:S(2)}, u32[]{:S(2)}) collective-permute-start(bf16[512,512]{1,0:T(8,128)(2,1)} %refs_13_.1), channel_id=1, source_target_pairs={{0,2},{2,0},{1,3},{3,1},{4,6},{6,4},{5,7},{7,5},{8,10},{10,8},{9,1... | collective-permute-start | bytes 1572872 | tf_op jit(solution)/shard_map/ppermute | solution.py:19
  6.1 4.4 %collective-permute-start.1 = (bf16[512,512]{1,0:T(8,128)(2,1)}, bf16[512,512]{1,0:T(8,128)(2,1)S(1)}, u32[]{:S(2)}, u32[]{:S(2)}) collective-permute-start(bf16[512,512]{1,0:T(8,128)(2,1)} %refs_13_.1), channel_id=1, source_target_pairs={{0,4},{4,0},{8,12},{12,8},{1,5},{5,1},{9,13},{13,9},{2,6},{6,2},{1... | collective-permute-start | bytes 1572872 | tf_op jit(solution)/shard_map/ppermute | solution.py:579
  10.5 6.3 %collective-permute-done.4.refs_2_ = bf16[512,512]{1,0:T(8,128)(2,1)S(1)} collective-permute-done((bf16[512,512]{1,0:T(8,128)(2,1)}, bf16[512,512]{1,0:T(8,128)(2,1)S(1)}, u32[]{:S(2)}, u32[]{:S(2)}) %collective-permute-start.4) | collective-permute-done | bytes 524320 | tf_op jit(solution)/shard_map/ppermute | solution.py:579
  17.5 1.3 %collective-permute-start.8 = (bf16[512,512]{1,0:T(8,128)(2,1)S(1)}, bf16[512,512]{1,0:T(8,128)(2,1)S(1)}, u32[]{:S(2)}, u32[]{:S(2)}) collective-permute-start(bf16[512,512]{1,0:T(8,128)(2,1)S(1)} %collective-permute-done.7.inner), channel_id=1, source_target_pairs={{4,0},{8,12},{5,1},{9,13},{6,2},{10,14},{7,3},{11,15},{20,16},{24,... | collective-permute-start | bytes 1572872 | tf_op jit(solution)/shard_map/ppermute | solution.py:579
  18.9 9.1 %collective-permute-done.1.second.refs_8_ = bf16[512,512]{1,0:T(8,128)(2,1)S(1)} collective-permute-done((bf16[512,512]{1,0:T(8,128)(2,1)}, bf16[512,512]{1,0:T(8,128)(2,1)S(1)}, u32[]{:S(2)}, u32[]{:S(2)}) %collective-permute-start.1) | collective-permute-done | bytes 524320 | tf_op jit(solution)/shard_map/ppermute | solution.py:579
  28.0 1.9 %collective-permute-start.11 = (bf16[512,512]{1,0:T(8,128)(2,1)S(1)}, bf16[512,512]{1,0:T(8,128)(2,1)S(1)}, u32[]{:S(2)}, u32[]{:S(2)}) collective-permute-start(bf16[512,512]{1,0:T(8,128)(2,1)S(1)} %collective-permute-done.1.second.refs_8_), channel_id=1, source_target_pairs={{0,2},{2,0},{1,3},{3,1},{4,6},{6,4},{5,7},{7,5},{8,10},{10,8},{9,1... | collective-permute-start | bytes 1572872 | tf_op jit(solution)/shard_map/ppermute | solution.py:19
  30.6 1.3 %collective-permute-start.6 = (bf16[512,512]{1,0:T(8,128)(2,1)S(1)}, bf16[512,512]{1,0:T(8,128)(2,1)S(1)}, u32[]{:S(2)}, u32[]{:S(2)}) collective-permute-start(bf16[512,512]{1,0:T(8,128)(2,1)S(1)} %collective-permute-done.5.inner), channel_id=1, source_target_pairs={{4,0},{8,12},{5,1},{9,13},{6,2},{10,14},{7,3},{11,15},{20,16},{24,... | collective-permute-start | bytes 1572872 | tf_op jit(solution)/shard_map/ppermute | solution.py:579
  31.9 7.4 %collective-permute-done.8.outer = bf16[512,512]{1,0:T(8,128)(2,1)S(1)} collective-permute-done((bf16[512,512]{1,0:T(8,128)(2,1)S(1)}, bf16[512,512]{1,0:T(8,128)(2,1)S(1)}, u32[]{:S(2)}, u32[]{:S(2)}) %collective-permute-start.8) | collective-permute-done | bytes 524320 | tf_op jit(solution)/shard_map/ppermute | solution.py:579
  39.3 0.7 collective-permute-start.18
  40.1 1.4 %collective-permute-done.11.refs_9_ = bf16[512,512]{1,0:T(8,128)(2,1)S(1)} collective-permute-done((bf16[512,512]{1,0:T(8,128)(2,1)S(1)}, bf16[512,512]{1,0:T(8,128)(2,1)S(1)}, u32[]{:S(2)}, u32[]{:S(2)}) %collective-permute-start.11) | collective-permute-done | bytes 524320 | tf_op jit(solution)/shard_map/ppermute | solution.py:19
  41.5 1.5 %collective-permute-start.13 = (bf16[512,512]{1,0:T(8,128)(2,1)S(1)}, bf16[512,512]{1,0:T(8,128)(2,1)S(1)}, u32[]{:S(2)}, u32[]{:S(2)}) collective-permute-start(bf16[512,512]{1,0:T(8,128)(2,1)S(1)} %shard_map.59.third.refs_10_), channel_id=1, source_target_pairs={{0,2},{2,0},{1,3},{3,1},{4,6},{6,4},{5,7},{7,5},{8,10},{10,8},{9,1... | collective-permute-start | bytes 1572872 | tf_op jit(solution)/shard_map/ppermute | solution.py:19
  43.0 1.4 %collective-permute-start.3 = (bf16[256,512]{1,0:T(8,128)(2,1)S(1)}, bf16[256,512]{1,0:T(8,128)(2,1)S(1)}, u32[]{:S(2)}, u32[]{:S(2)}) collective-permute-start(bf16[256,512]{1,0:T(8,128)(2,1)S(1)} %get-tuple-element.54.inner), channel_id=1, source_target_pairs={{4,0},{8,12},{5,1},{9,13},{6,2},{10,14},{7,3},{11,15},{20,16},{24,... | collective-permute-start | bytes 786440 | tf_op jit(solution)/shard_map/ppermute | solution.py:579
  44.4 1.0 %shard_map.60.row = f32[8,512]{1,0:T(8,128)S(1)} custom-call(bf16[512,512]{1,0:T(8,128)(2,1)S(1)} %copy-done, bf16[512,512]{1,0:T(8,128)(2,1)S(1)} %collective-permute-done.1.second.refs_8_, bf16[512,512]{1,0:T(8,128)(2,1)S(1)} %shard_map.59.third.refs_10_), custom_call_target="tpu_custom_call" | custom-call | flops 1048576 | bytes 1589248 | tf_op jit(solution)/shard_map/pallas_call | solution.py:549
  45.4 5.1 %collective-permute-done.6.outer = bf16[512,512]{1,0:T(8,128)(2,1)S(1)} collective-permute-done((bf16[512,512]{1,0:T(8,128)(2,1)S(1)}, bf16[512,512]{1,0:T(8,128)(2,1)S(1)}, u32[]{:S(2)}, u32[]{:S(2)}) %collective-permute-start.6) | collective-permute-done | bytes 524320 | tf_op jit(solution)/shard_map/ppermute | solution.py:579
  50.7 1.3 %collective-permute-start.9 = (bf16[256,512]{1,0:T(8,128)(2,1)S(1)}, bf16[256,512]{1,0:T(8,128)(2,1)S(1)}, u32[]{:S(2)}, u32[]{:S(2)}) collective-permute-start(bf16[256,512]{1,0:T(8,128)(2,1)S(1)} %get-tuple-element.59.inner), channel_id=1, source_target_pairs={{4,0},{8,12},{5,1},{9,13},{6,2},{10,14},{7,3},{11,15},{20,16},{24,... | collective-permute-start | bytes 786440 | tf_op jit(solution)/shard_map/ppermute | solution.py:579
  52.0 1.3 %collective-permute-start.19 = (bf16[512,512]{1,0:T(8,128)(2,1)S(1)}, bf16[512,512]{1,0:T(8,128)(2,1)S(1)}, u32[]{:S(2)}, u32[]{:S(2)}) collective-permute-start(bf16[512,512]{1,0:T(8,128)(2,1)S(1)} %collective-permute-done.18.inner), channel_id=1, source_target_pairs={{4,0},{8,12},{5,1},{9,13},{6,2},{10,14},{7,3},{11,15},{20,16},{24,... | collective-permute-start | bytes 1572872 | tf_op jit(solution)/shard_map/ppermute | solution.py:579
  53.3 2.7 %collective-permute-done.3.outer = bf16[256,512]{1,0:T(8,128)(2,1)S(1)} collective-permute-done((bf16[256,512]{1,0:T(8,128)(2,1)S(1)}, bf16[256,512]{1,0:T(8,128)(2,1)S(1)}, u32[]{:S(2)}, u32[]{:S(2)}) %collective-permute-start.3) | collective-permute-done | bytes 262176 | tf_op jit(solution)/shard_map/ppermute | solution.py:579
  56.2 1.6 %collective-permute-start.14 = (bf16[512,256]{1,0:T(8,128)(2,1)S(1)}, bf16[512,256]{1,0:T(8,128)(2,1)S(1)}, u32[]{:S(2)}, u32[]{:S(2)}) collective-permute-start(bf16[512,256]{1,0:T(8,128)(2,1)S(1)} %get-tuple-element.58.refs_0_.late_b_0), channel_id=1, source_target_pairs={{0,2},{2,0},{1,3},{3,1},{4,6},{6,4},{5,7},{7,5},{8,10},{10,8},{9,1... | collective-permute-start | bytes 786440 | tf_op jit(solution)/shard_map/ppermute | solution.py:19
  57.8 4.0 %collective-permute-done.9.outer = bf16[256,512]{1,0:T(8,128)(2,1)S(1)} collective-permute-done((bf16[256,512]{1,0:T(8,128)(2,1)S(1)}, bf16[256,512]{1,0:T(8,128)(2,1)S(1)}, u32[]{:S(2)}, u32[]{:S(2)}) %collective-permute-start.9) | collective-permute-done | bytes 262176 | tf_op jit(solution)/shard_map/ppermute | solution.py:579
  62.0 1.9 %collective-permute-start.17 = (bf16[544,256]{1,0:T(8,128)(2,1)S(1)}, bf16[544,256]{1,0:T(8,128)(2,1)S(1)}, u32[]{:S(2)}, u32[]{:S(2)}) collective-permute-start(bf16[544,256]{1,0:T(8,128)(2,1)S(1)} %shard_map.62.refs_1_.late_b_1), channel_id=1, source_target_pairs={{0,2},{2,0},{1,3},{3,1},{4,6},{6,4},{5,7},{7,5},{8,10},{10,8},{9,1... | collective-permute-start | bytes 835592 | tf_op jit(solution)/shard_map/ppermute | solution.py:19
  64.0 4.1 %shard_map.63 = (f32[512,512]{1,0:T(8,128)S(1)}, f32[512,512]{1,0:T(8,128)S(1)}, f32[512,1024]{1,0:T(8,128)S(1)}, f32[8,512]{1,0:T(8,128)S(1)}, bf16[512,512]{1,...) custom-call(bf16[512,512]{1,0:T(8,128)(2,1)S(1)} %copy-done.1, bf16[512,512]{1,0:T(8,128)(2,1)S(1)} %collective-permute-done.refs_1_.refs_9_, ...), custom_call_target="tpu_custom_call" | custom-call | flops 1048576 | bytes 65536 | tf_op jit(solution)/shard_map/pallas_call | solution.py:549
  68.1 2.0 %collective-permute-done.17.late_b_1.refs_3_ = bf16[544,256]{1,0:T(8,128)(2,1)S(1)} collective-permute-done((bf16[544,256]{1,0:T(8,128)(2,1)S(1)}, bf16[544,256]{1,0:T(8,128)(2,1)S(1)}, u32[]{:S(2)}, u32[]{:S(2)}) %collective-permute-start.17) | collective-permute-done | bytes 278560 | tf_op jit(solution)/shard_map/ppermute | solution.py:19
  70.4 2.3 %collective-permute-done.19.outer = bf16[512,512]{1,0:T(8,128)(2,1)S(1)} collective-permute-done((bf16[512,512]{1,0:T(8,128)(2,1)S(1)}, bf16[512,512]{1,0:T(8,128)(2,1)S(1)}, u32[]{:S(2)}, u32[]{:S(2)}) %collective-permute-start.19) | collective-permute-done | bytes 524320 | tf_op jit(solution)/shard_map/ppermute | solution.py:579
  73.9 1.1 %shard_map.67 = (f32[528,512]{1,0:T(8,128)S(1)}, f32[512,128]{1,0:T(8,128)S(1)}, bf16[512,512]{1,0:T(8,128)(2,1)S(1)}, f32[8,512]{1,0:T(8,128)S(1)}) custom-call(bf16[512,512]{1,0:T(8,128)(2,1)S(1)} %shard_map.66.late.refs_6_, f32[8,512]{1,0:T(8,128)S(1)} %shard_map.65.stats.refs_4_, bf16[512,512]{1,0:T(8,128)(2,1)S(1)} %get-tuple-element.76.zero.refs_10_, ...), custom_call_target="tpu_custom_call" | custom-call | flops 536870912 | bytes 4554752 | tf_op jit(solution)/shard_map/pallas_call | solution.py:549
  75.0 1.4 %shard_map.68 = (bf16[512,512]{1,0:T(8,128)(2,1)S(1)}, bf16[512,512]{1,0:T(8,128)(2,1)S(1)}, f32[8,512]{1,0:T(8,128)S(1)}) custom-call(bf16[512,512]{1,0:T(8,128)(2,1)S(1)} %collective-permute-done.21.late.refs_7_, f32[8,512]{1,0:T(8,128)S(1)} %collective-permute-done.20.stats.refs_5_, bf16[512,512]{1,0:T(8,128)(2,1)S(1)} %get-tuple-element.77.zero.refs_11_, ...), custom_call_target="tpu_custom_call" | custom-call | flops 536870912 | bytes 6144000 | tf_op jit(solution)/shard_map/pallas_call | solution.py:549
  76.4 1.8 %collective-permute-start.24 = (bf16[512,512]{1,0:T(8,128)(2,1)S(1)}, bf16[512,512]{1,0:T(8,128)(2,1)S(1)}, u32[]{:S(2)}, u32[]{:S(2)}) collective-permute-start(bf16[512,512]{1,0:T(8,128)(2,1)S(1)} %get-tuple-element.95), channel_id=1, source_target_pairs={{0,2},{2,0},{1,3},{3,1},{4,6},{6,4},{5,7},{7,5},{8,10},{10,8},{9,1... | collective-permute-start | bytes 1572872 | tf_op jit(solution)/shard_map/ppermute | solution.py:19
  78.1 7.6 %shard_map.69 = (f32[512,512]{1,0:T(8,128)S(1)}, f32[512,512]{1,0:T(8,128)S(1)}, bf16[256,512]{1,0:T(8,128)(2,1)S(1)}, bf16[256,512]{1,0:T(8,128)(2,1)S(1)}, f32[256,1024]{1,0:T(8,128)}, /*index=5*/f32[8,128]{1,0:T(8,128)S(1)}) custom-call(s32[2]{0:T(128)S(1)} %pad_add_fusion.flags, bf16[512,256]{1,0:T(8,128)(2,1)S(1)} %get-tuple-element.58.refs_0_.late_b_0, ...), custom_call_target="tpu_custom_call" | custom-call | flops 2147483648 | bytes 14258184 | tf_op jit(solution)/shard_map/pallas_call | solution.py:549
  86.3 1.4 %collective-permute-done.25.other = f32[8,128]{1,0:T(8,128)S(1)} collective-permute-done((f32[8,128]{1,0:T(8,128)S(1)}, f32[8,128]{1,0:T(8,128)S(1)}, u32[]{:S(2)}, u32[]{:S(2)}) %collective-permute-start.25) | collective-permute-done | bytes 4128 | tf_op jit(solution)/shard_map/ppermute | solution.py:19
  88.0 0.9 shard_map.70
  89.0 1.4 %collective-permute-done.24.from_x = bf16[512,512]{1,0:T(8,128)(2,1)S(1)} collective-permute-done((bf16[512,512]{1,0:T(8,128)(2,1)S(1)}, bf16[512,512]{1,0:T(8,128)(2,1)S(1)}, u32[]{:S(2)}, u32[]{:S(2)}) %collective-permute-start.24) | collective-permute-done | bytes 524320 | tf_op jit(solution)/shard_map/ppermute | solution.py:19
  90.4 0.9 %shard_map.71 = bf16[512,512]{1,0:T(8,128)(2,1)} custom-call(f32[512,512]{1,0:T(8,128)S(1)} %get-tuple-element.94.right, bf16[512,512]{1,0:T(8,128)(2,1)S(1)} %collective-permute-done.24.from_x, bf16[512,256]{1,0:T(8,128)(2,1)S(1)} %get-tuple-element.58.refs_0_.late_b_0, bf16[544,256]{1,0:T(8,128)(2,1)S(1)} %shard_map.62.refs_1_.late_b_1), custom_call_target="tpu_custom_call" | custom-call | flops 1048576 | bytes 2637824 | tf_op jit(solution)/shard_map/pallas_call | solution.py:549
  (45 shorter events, 6.5 us)
Async XLA Ops:
  0.6 43.8 %copy-start = (bf16[512,512]{1,0:T(8,128)(2,1)S(1)}, bf16[512,512]{1,0:T(8,128)(2,1)}, u32[]{:S(2)}) copy-start(bf16[512,512]{1,0:T(8,128)(2,1)} %refs_13_.1) | copy-start | bytes 1572868
  0.6 9.9 %collective-permute-start = (bf16[512,512]{1,0:T(8,128)(2,1)}, bf16[512,512]{1,0:T(8,128)(2,1)S(1)}, u32[]{:S(2)}, u32[]{:S(2)}) collective-permute-start(bf16[512,512]{1,0:T(8,128)(2,1)} %refs_8_.1), channel_id=1, source_target_pairs={{0,1},{1,0},{2,3},{3,2},{4,5},{5,4},{6,7},{7,6},{8,9},{9,8},{10,11... | collective-permute-start | bytes 1572872 | tf_op jit(solution)/shard_map/ppermute | solution.py:19
  1.2 15.6 %collective-permute-start.4 = (bf16[512,512]{1,0:T(8,128)(2,1)}, bf16[512,512]{1,0:T(8,128)(2,1)S(1)}, u32[]{:S(2)}, u32[]{:S(2)}) collective-permute-start(bf16[512,512]{1,0:T(8,128)(2,1)} %refs_8_.1), channel_id=1, source_target_pairs={{0,4},{4,0},{8,12},{12,8},{1,5},{5,1},{9,13},{13,9},{2,6},{6,2},{1... | collective-permute-start | bytes 1572872 | tf_op jit(solution)/shard_map/ppermute | solution.py:579
  3.8 13.7 %collective-permute-start.7 = (bf16[512,512]{1,0:T(8,128)(2,1)}, bf16[512,512]{1,0:T(8,128)(2,1)S(1)}, u32[]{:S(2)}, u32[]{:S(2)}) collective-permute-start(bf16[512,512]{1,0:T(8,128)(2,1)} %refs_13_.1), channel_id=1, source_target_pairs={{4,8},{8,4},{5,9},{9,5},{6,10},{10,6},{7,11},{11,7},{20,24},{24,20... | collective-permute-start | bytes 1572872 | tf_op jit(solution)/shard_map/ppermute | solution.py:579
  4.5 14.4 %collective-permute-start.10 = (bf16[512,512]{1,0:T(8,128)(2,1)}, bf16[512,512]{1,0:T(8,128)(2,1)S(1)}, u32[]{:S(2)}, u32[]{:S(2)}) collective-permute-start(bf16[512,512]{1,0:T(8,128)(2,1)} %refs_13_.1), channel_id=1, source_target_pairs={{0,2},{2,0},{1,3},{3,1},{4,6},{6,4},{5,7},{7,5},{8,10},{10,8},{9,1... | collective-permute-start | bytes 1572872 | tf_op jit(solution)/shard_map/ppermute | solution.py:19
  6.1 22.0 %collective-permute-start.1 = (bf16[512,512]{1,0:T(8,128)(2,1)}, bf16[512,512]{1,0:T(8,128)(2,1)S(1)}, u32[]{:S(2)}, u32[]{:S(2)}) collective-permute-start(bf16[512,512]{1,0:T(8,128)(2,1)} %refs_13_.1), channel_id=1, source_target_pairs={{0,4},{4,0},{8,12},{12,8},{1,5},{5,1},{9,13},{13,9},{2,6},{6,2},{1... | collective-permute-start | bytes 1572872 | tf_op jit(solution)/shard_map/ppermute | solution.py:579
  16.8 13.8 %collective-permute-start.5 = (bf16[512,512]{1,0:T(8,128)(2,1)}, bf16[512,512]{1,0:T(8,128)(2,1)S(1)}, u32[]{:S(2)}, u32[]{:S(2)}) collective-permute-start(bf16[512,512]{1,0:T(8,128)(2,1)} %refs_8_.1), channel_id=1, source_target_pairs={{4,8},{8,4},{5,9},{9,5},{6,10},{10,6},{7,11},{11,7},{20,24},{24,20... | collective-permute-start | bytes 1572872 | tf_op jit(solution)/shard_map/ppermute | solution.py:579
  17.5 21.8 %collective-permute-start.8 = (bf16[512,512]{1,0:T(8,128)(2,1)S(1)}, bf16[512,512]{1,0:T(8,128)(2,1)S(1)}, u32[]{:S(2)}, u32[]{:S(2)}) collective-permute-start(bf16[512,512]{1,0:T(8,128)(2,1)S(1)} %collective-permute-done.7.inner), channel_id=1, source_target_pairs={{4,0},{8,12},{5,1},{9,13},{6,2},{10,14},{7,3},{11,15},{20,16},{24,... | collective-permute-start | bytes 1572872 | tf_op jit(solution)/shard_map/ppermute | solution.py:579
  18.8 21.3 %collective-permute-start.12 = (bf16[512,512]{1,0:T(8,128)(2,1)S(1)}, bf16[512,512]{1,0:T(8,128)(2,1)S(1)}, u32[]{:S(2)}, u32[]{:S(2)}) collective-permute-start(bf16[512,512]{1,0:T(8,128)(2,1)S(1)} %collective-permute-done.4.refs_2_), channel_id=1, source_target_pairs={{0,1},{1,0},{2,3},{3,2},{4,5},{5,4},{6,7},{7,6},{8,9},{9,8},{10,11... | collective-permute-start | bytes 1572872 | tf_op jit(solution)/shard_map/ppermute | solution.py:19
  28.0 13.4 %collective-permute-start.11 = (bf16[512,512]{1,0:T(8,128)(2,1)S(1)}, bf16[512,512]{1,0:T(8,128)(2,1)S(1)}, u32[]{:S(2)}, u32[]{:S(2)}) collective-permute-start(bf16[512,512]{1,0:T(8,128)(2,1)S(1)} %collective-permute-done.1.second.refs_8_), channel_id=1, source_target_pairs={{0,2},{2,0},{1,3},{3,1},{4,6},{6,4},{5,7},{7,5},{8,10},{10,8},{9,1... | collective-permute-start | bytes 1572872 | tf_op jit(solution)/shard_map/ppermute | solution.py:19
  29.9 13.0 %collective-permute-start.2 = (bf16[512,512]{1,0:T(8,128)(2,1)S(1)}, bf16[512,512]{1,0:T(8,128)(2,1)S(1)}, u32[]{:S(2)}, u32[]{:S(2)}) collective-permute-start(bf16[512,512]{1,0:T(8,128)(2,1)S(1)} %collective-permute-done.1.second.refs_8_), channel_id=1, source_target_pairs={{4,8},{8,4},{5,9},{9,5},{6,10},{10,6},{7,11},{11,7},{20,24},{24,20... | collective-permute-start | bytes 1572872 | tf_op jit(solution)/shard_map/ppermute | solution.py:579
  30.6 19.9 %collective-permute-start.6 = (bf16[512,512]{1,0:T(8,128)(2,1)S(1)}, bf16[512,512]{1,0:T(8,128)(2,1)S(1)}, u32[]{:S(2)}, u32[]{:S(2)}) collective-permute-start(bf16[512,512]{1,0:T(8,128)(2,1)S(1)} %collective-permute-done.5.inner), channel_id=1, source_target_pairs={{4,0},{8,12},{5,1},{9,13},{6,2},{10,14},{7,3},{11,15},{20,16},{24,... | collective-permute-start | bytes 1572872 | tf_op jit(solution)/shard_map/ppermute | solution.py:579
  39.3 12.7 %collective-permute-start.18 = (bf16[512,512]{1,0:T(8,128)(2,1)S(1)}, bf16[512,512]{1,0:T(8,128)(2,1)S(1)}, u32[]{:S(2)}, u32[]{:S(2)}) collective-permute-start(bf16[512,512]{1,0:T(8,128)(2,1)S(1)} %collective-permute-done.4.refs_2_), channel_id=1, source_target_pairs={{4,8},{8,4},{5,9},{9,5},{6,10},{10,6},{7,11},{11,7},{20,24},{24,20... | collective-permute-start | bytes 1572872 | tf_op jit(solution)/shard_map/ppermute | solution.py:579
  41.5 22.4 %collective-permute-start.13 = (bf16[512,512]{1,0:T(8,128)(2,1)S(1)}, bf16[512,512]{1,0:T(8,128)(2,1)S(1)}, u32[]{:S(2)}, u32[]{:S(2)}) collective-permute-start(bf16[512,512]{1,0:T(8,128)(2,1)S(1)} %shard_map.59.third.refs_10_), channel_id=1, source_target_pairs={{0,2},{2,0},{1,3},{3,1},{4,6},{6,4},{5,7},{7,5},{8,10},{10,8},{9,1... | collective-permute-start | bytes 1572872 | tf_op jit(solution)/shard_map/ppermute | solution.py:19
  43.0 21.0 %copy-start.1 = (bf16[512,512]{1,0:T(8,128)(2,1)S(1)}, bf16[512,512]{1,0:T(8,128)(2,1)}, u32[]{:S(2)}) copy-start(bf16[512,512]{1,0:T(8,128)(2,1)} %refs_8_.1) | copy-start | bytes 1572868
  43.0 13.0 %collective-permute-start.3 = (bf16[256,512]{1,0:T(8,128)(2,1)S(1)}, bf16[256,512]{1,0:T(8,128)(2,1)S(1)}, u32[]{:S(2)}, u32[]{:S(2)}) collective-permute-start(bf16[256,512]{1,0:T(8,128)(2,1)S(1)} %get-tuple-element.54.inner), channel_id=1, source_target_pairs={{4,0},{8,12},{5,1},{9,13},{6,2},{10,14},{7,3},{11,15},{20,16},{24,... | collective-permute-start | bytes 786440 | tf_op jit(solution)/shard_map/ppermute | solution.py:579
  50.6 13.3 %collective-permute-start.15 = (bf16[512,512]{1,0:T(8,128)(2,1)S(1)}, bf16[512,512]{1,0:T(8,128)(2,1)S(1)}, u32[]{:S(2)}, u32[]{:S(2)}) collective-permute-start(bf16[512,512]{1,0:T(8,128)(2,1)S(1)} %shard_map.58.refs_4_), channel_id=1, source_target_pairs={{0,1},{1,0},{2,3},{3,2},{4,5},{5,4},{6,7},{7,6},{8,9},{9,8},{10,11... | collective-permute-start | bytes 1572872 | tf_op jit(solution)/shard_map/ppermute | solution.py:19
  50.7 11.1 %collective-permute-start.9 = (bf16[256,512]{1,0:T(8,128)(2,1)S(1)}, bf16[256,512]{1,0:T(8,128)(2,1)S(1)}, u32[]{:S(2)}, u32[]{:S(2)}) collective-permute-start(bf16[256,512]{1,0:T(8,128)(2,1)S(1)} %get-tuple-element.59.inner), channel_id=1, source_target_pairs={{4,0},{8,12},{5,1},{9,13},{6,2},{10,14},{7,3},{11,15},{20,16},{24,... | collective-permute-start | bytes 786440 | tf_op jit(solution)/shard_map/ppermute | solution.py:579
  52.0 20.7 %collective-permute-start.19 = (bf16[512,512]{1,0:T(8,128)(2,1)S(1)}, bf16[512,512]{1,0:T(8,128)(2,1)S(1)}, u32[]{:S(2)}, u32[]{:S(2)}) collective-permute-start(bf16[512,512]{1,0:T(8,128)(2,1)S(1)} %collective-permute-done.18.inner), channel_id=1, source_target_pairs={{4,0},{8,12},{5,1},{9,13},{6,2},{10,14},{7,3},{11,15},{20,16},{24,... | collective-permute-start | bytes 1572872 | tf_op jit(solution)/shard_map/ppermute | solution.py:579
  56.2 7.8 %collective-permute-start.14 = (bf16[512,256]{1,0:T(8,128)(2,1)S(1)}, bf16[512,256]{1,0:T(8,128)(2,1)S(1)}, u32[]{:S(2)}, u32[]{:S(2)}) collective-permute-start(bf16[512,256]{1,0:T(8,128)(2,1)S(1)} %get-tuple-element.58.refs_0_.late_b_0), channel_id=1, source_target_pairs={{0,2},{2,0},{1,3},{3,1},{4,6},{6,4},{5,7},{7,5},{8,10},{10,8},{9,1... | collective-permute-start | bytes 786440 | tf_op jit(solution)/shard_map/ppermute | solution.py:19
  62.0 8.1 %collective-permute-start.17 = (bf16[544,256]{1,0:T(8,128)(2,1)S(1)}, bf16[544,256]{1,0:T(8,128)(2,1)S(1)}, u32[]{:S(2)}, u32[]{:S(2)}) collective-permute-start(bf16[544,256]{1,0:T(8,128)(2,1)S(1)} %shard_map.62.refs_1_.late_b_1), channel_id=1, source_target_pairs={{0,2},{2,0},{1,3},{3,1},{4,6},{6,4},{5,7},{7,5},{8,10},{10,8},{9,1... | collective-permute-start | bytes 835592 | tf_op jit(solution)/shard_map/ppermute | solution.py:19
  68.0 2.1 %collective-permute-start.16 = (f32[8,512]{1,0:T(8,128)S(1)}, f32[8,512]{1,0:T(8,128)S(1)}, u32[]{:S(2)}, u32[]{:S(2)}) collective-permute-start(f32[8,512]{1,0:T(8,128)S(1)} %get-tuple-element.71), channel_id=1, source_target_pairs={{0,1},{1,0},{2,3},{3,2},{4,5},{5,4},{6,7},{7,6},{8,9},{9,8},{10,11... | collective-permute-start | bytes 49160 | tf_op jit(solution)/shard_map/ppermute | solution.py:19
  72.9 2.1 %collective-permute-start.21 = (bf16[512,512]{1,0:T(8,128)(2,1)S(1)}, bf16[512,512]{1,0:T(8,128)(2,1)S(1)}, u32[]{:S(2)}, u32[]{:S(2)}) collective-permute-start(bf16[512,512]{1,0:T(8,128)(2,1)S(1)} %shard_map.66.late.refs_6_), channel_id=1, source_target_pairs={{0,1},{1,0},{2,3},{3,2},{4,5},{5,4},{6,7},{7,6},{8,9},{9,8},{10,11... | collective-permute-start | bytes 1572872 | tf_op jit(solution)/shard_map/ppermute | solution.py:19
  73.3 1.6 %collective-permute-start.20 = (f32[8,512]{1,0:T(8,128)S(1)}, f32[8,512]{1,0:T(8,128)S(1)}, u32[]{:S(2)}, u32[]{:S(2)}) collective-permute-start(f32[8,512]{1,0:T(8,128)S(1)} %shard_map.65.stats.refs_4_), channel_id=1, source_target_pairs={{0,1},{1,0},{2,3},{3,2},{4,5},{5,4},{6,7},{7,6},{8,9},{9,8},{10,11... | collective-permute-start | bytes 49160 | tf_op jit(solution)/shard_map/ppermute | solution.py:19
  76.4 14.0 %collective-permute-start.24 = (bf16[512,512]{1,0:T(8,128)(2,1)S(1)}, bf16[512,512]{1,0:T(8,128)(2,1)S(1)}, u32[]{:S(2)}, u32[]{:S(2)}) collective-permute-start(bf16[512,512]{1,0:T(8,128)(2,1)S(1)} %get-tuple-element.95), channel_id=1, source_target_pairs={{0,2},{2,0},{1,3},{3,1},{4,6},{6,4},{5,7},{7,5},{8,10},{10,8},{9,1... | collective-permute-start | bytes 1572872 | tf_op jit(solution)/shard_map/ppermute | solution.py:19
  85.8 2.3 %collective-permute-start.22 = (bf16[256,512]{1,0:T(8,128)(2,1)S(1)}, bf16[256,512]{1,0:T(8,128)(2,1)S(1)}, u32[]{:S(2)}, u32[]{:S(2)}) collective-permute-start(bf16[256,512]{1,0:T(8,128)(2,1)S(1)} %get-tuple-element.91), channel_id=1, source_target_pairs={{0,1},{1,0},{2,3},{3,2},{4,5},{5,4},{6,7},{7,6},{8,9},{9,8},{10,11... | collective-permute-start | bytes 786440 | tf_op jit(solution)/shard_map/ppermute | solution.py:19
  85.8 2.3 %collective-permute-start.23 = (bf16[256,512]{1,0:T(8,128)(2,1)S(1)}, bf16[256,512]{1,0:T(8,128)(2,1)S(1)}, u32[]{:S(2)}, u32[]{:S(2)}) collective-permute-start(bf16[256,512]{1,0:T(8,128)(2,1)S(1)} %get-tuple-element.92), channel_id=1, source_target_pairs={{0,1},{1,0},{2,3},{3,2},{4,5},{5,4},{6,7},{7,6},{8,9},{9,8},{10,11... | collective-permute-start | bytes 786440 | tf_op jit(solution)/shard_map/ppermute | solution.py:19
  86.3 1.4 %collective-permute-start.25 = (f32[8,128]{1,0:T(8,128)S(1)}, f32[8,128]{1,0:T(8,128)S(1)}, u32[]{:S(2)}, u32[]{:S(2)}) collective-permute-start(f32[8,128]{1,0:T(8,128)S(1)} %get-tuple-element.96.one), channel_id=1, source_target_pairs={{0,1},{1,0},{2,3},{3,2},{4,5},{5,4},{6,7},{7,6},{8,9},{9,8},{10,11... | collective-permute-start | bytes 12296 | tf_op jit(solution)/shard_map/ppermute | solution.py:19
  87.7 3.6 %collective-permute-start.26 = (f32[8,128]{1,0:T(8,128)S(1)}, f32[8,128]{1,0:T(8,128)S(1)}, u32[]{:S(2)}, u32[]{:S(2)}) collective-permute-start(f32[8,128]{1,0:T(8,128)S(1)} %shard_map.72.one), channel_id=1, source_target_pairs={{0,2},{2,0},{1,3},{3,1},{4,6},{6,4},{5,7},{7,5},{8,10},{10,8},{9,1... | collective-permute-start | bytes 12296 | tf_op jit(solution)/shard_map/ppermute | solution.py:19
